TPU v7x, 32 devices: a whole 2x2x4 slice. The times are simulated.
32 devices in a mesh: groups: 2 (over x), row: 8 (over z, y), chan: 2 (over core).
Axes of the slice: x: 2, y: 2, z: 4, core: 2. Of those that a mesh axis runs over, the one named last changes fastest.
Arguments:
- pair: bfloat16 [512, 256, 128], P(('groups', 'row'), 'chan'), parts along dimension 0, may hold values from -6 to 6
- pair_mask: int32 [512, 256], P(('groups', 'row'), 'chan'), parts along dimension 0, may hold values 0 or 1
- in_gain: float32 [128], replicated, may hold values from 0.1 to 1.9
- proj_weight: bfloat16 [128, 512], replicated, may hold values from -0.5 to 0.5
- gate_weight: bfloat16 [128, 128], replicated, may hold values from -0.5 to 0.5
- out_gain: float32 [128], replicated, may hold values from 0.1 to 1.9
- out_weight: bfloat16 [128, 128], replicated, may hold values from -0.5 to 0.5
Outputs:
- update: bfloat16 [512, 256, 128], P(('groups', 'row'), 'chan'), parts along dimension 0
There are 2 independent parts, one for each index of `groups`. A program takes and returns all parts, laid end to end along the dimension named above; an argument that names none is the same for every part. Nothing has to cross between parts.
All inputs are finite; a program needn't handle non-finite values. No bound on the sum of `pair_mask` on one device may be relied on, other than what follows from the above.
Results may differ from a plain program's by a relative error of at most 0.0083.
Values may be sent and summed in bfloat16 or wider, within the bound.
No kernel may reach another device: no remote copies, remote signals or barrier semaphores. Data moves between devices by JAX's collectives and lax.ppermute only.
A program may use at most 64 MiB of HBM per device.

v0:
```python
import jax
import jax.numpy as jnp
from jax import lax
from jax.sharding import PartitionSpec as P


def local(pair, pair_mask, in_gain, proj_weight, gate_weight, out_gain, out_weight):
    values = pair.astype(jnp.float32)
    mean = jnp.mean(values, axis=-1, keepdims=True)
    centered = values - mean
    var = jnp.mean(centered * centered, axis=-1, keepdims=True)
    normed = (centered * lax.rsqrt(var + 1e-05) * in_gain).astype(jnp.bfloat16)
    hidden = proj_weight.shape[1] // 4
    proj = jnp.einsum("ijc,cf->fij", normed, proj_weight, preferred_element_type=jnp.float32)
    valid = pair_mask.astype(jnp.float32)
    left = (valid * jax.nn.sigmoid(proj[:hidden]) * proj[hidden : 2 * hidden]).astype(jnp.bfloat16)
    right = (valid * jax.nn.sigmoid(proj[2 * hidden : 3 * hidden]) * proj[3 * hidden :]).astype(
        jnp.bfloat16
    )
    gate = jax.nn.sigmoid(
        jnp.einsum("ijc,cf->ijf", normed, gate_weight, preferred_element_type=jnp.float32)
    )
    left_planes, right_planes = (
        lax.all_to_all(
            lax.all_to_all(left, "row", split_axis=0, concat_axis=1, tiled=True),
            "chan",
            split_axis=0,
            concat_axis=2,
            tiled=True,
        ),
        lax.all_to_all(
            lax.all_to_all(right, "row", split_axis=0, concat_axis=1, tiled=True),
            "chan",
            split_axis=0,
            concat_axis=2,
            tiled=True,
        ),
    )
    product = jnp.einsum(
        "cik,cjk->cij", left_planes, right_planes, preferred_element_type=jnp.float32
    ).astype(jnp.bfloat16)
    product = lax.all_to_all(
        lax.all_to_all(product, "chan", split_axis=2, concat_axis=0, tiled=True),
        "row",
        split_axis=1,
        concat_axis=0,
        tiled=True,
    )
    prod_vals = product.astype(jnp.float32)
    pmean = jnp.mean(prod_vals, axis=0, keepdims=True)
    pcentered = prod_vals - pmean
    pvar = jnp.mean(pcentered * pcentered, axis=0, keepdims=True)
    pnorm = (pcentered * lax.rsqrt(pvar + 1e-05) * out_gain[:, None, None]).astype(jnp.bfloat16)
    mapped = jnp.einsum("hij,hc->ijc", pnorm, out_weight, preferred_element_type=jnp.float32)
    return (gate * mapped).astype(jnp.bfloat16)


def solution(mesh):
    placed = (
        P(("groups", "row"), "chan", None),
        P(("groups", "row"), "chan"),
        P(),
        P(),
        P(),
        P(),
        P(),
    )
    return jax.shard_map(
        local,
        mesh=mesh,
        in_specs=placed,
        out_specs=P(("groups", "row"), "chan", None),
        check_vma=False,
    )
```

profile of v0, /device:TPU:1, one launch (start us, length us, event | category | flops | bytes accessed | tf_op | source)
XLA Modules:
  0.0 125.8 jit_solution(5957080225341533951)
XLA Ops:
  0.0 0.0 copy-start
  0.0 0.0 copy-start.1
  0.0 0.0 copy-start.4
  0.0 0.0 copy-start.5
  0.0 1.7 %convert_reduce_fusion = f32[32,128]{1,0:T(8,128)S(1)} fusion(bf16[32,128,128]{2,1,0:T(8,128)(2,1)} %param.7), kind=kLoop, calls=%fused_computation.2 | loop fusion | flops 1044480 | bytes 1064960 | tf_op jit(solution)/shard_map/reduce_sum | solution.py:9
  1.7 2.3 %fusion.2 = f32[32,128]{1,0:T(8,128)S(1)} fusion(bf16[32,128,128]{2,1,0:T(8,128)(2,1)} %param.7, f32[32,128]{1,0:T(8,128)S(1)} %broadcast_multiply_fusion.1), kind=kLoop, calls=%fused_computation.5 | loop fusion | flops 2093056 | bytes 1081344 | tf_op jit(solution)/shard_map/reduce_sum | solution.py:11
  4.1 0.0 copy-done.4
  4.1 0.0 copy-done
  4.1 0.0 copy-done.1
  4.1 0.0 copy-done.5
  4.1 1.3 %convolution_bitcast_fusion = f32[512,32,128]{0,2,1:T(8,128)S(1)} fusion(bf16[32,128,128]{2,1,0:T(8,128)(2,1)S(1)} %copy-done.1, f32[128]{0:T(128)S(1)} %copy-done.5, f32[32,128]{1,0:T(8,128)S(1)} %add_rsqrt_fusion.1, f32[32,128]{1,0:T(8,128)S(1)} %broadcast_multiply_fusion.1, bf16[128,512]{1,0:T(8,128)(2,1)S(1)} %copy-done), kind=kOutput, calls=%fused_computation | convolution fusion | flops 539492352 | bytes 9601536 | tf_op jit(solution)/shard_map/ijc,cf->fij/dot_general | solution.py:14
  5.4 1.3 %fusion.10 = (bf16[128,32,128]{0,2,1:T(8,128)(2,1)S(1)}, bf16[128,32,128]{0,2,1:T(8,128)(2,1)S(1)}) fusion(f32[512,32,128]{0,2,1:T(8,128)S(1)} %convolution_bitcast_fusion, f32[32,128]{1,0:T(8,128)S(1)} %convert_element_type.44), kind=kLoop, calls=%fused_computation.16 | loop fusion | flops 6291456 | bytes 10502144 | tf_op jit(solution)/shard_map/convert_element_type | solution.py:16
  6.7 1.7 %copy.28 = bf16[128,32,128]{2,1,0:T(8,128)(2,1)} copy(bf16[128,32,128]{0,2,1:T(8,128)(2,1)S(1)} %get-tuple-element.5) | data formatting | bytes 2097152 | tf_op jit(solution)/shard_map/convert_element_type | solution.py:16
  8.4 6.4 %all-to-all-start = ((bf16[128,32,128]{2,1,0:T(8,128)(2,1)}), bf16[128,32,128]{2,1,0:T(8,128)(2,1)S(1)}, u32[]{:S(2)}, u32[]{:S(2)}) async-start(bf16[128,32,128]{2,1,0:T(8,128)(2,1)} %copy.28), calls=%async_computation | async-start | bytes 2097152 | tf_op jit(solution)/shard_map/all_to_all | solution.py:25
  14.8 1.7 %copy.31 = bf16[128,32,128]{2,1,0:T(8,128)(2,1)} copy(bf16[128,32,128]{0,2,1:T(8,128)(2,1)S(1)} %get-tuple-element.6) | data formatting | bytes 2097152 | tf_op jit(solution)/shard_map/convert_element_type | solution.py:17
  16.4 22.9 %all-to-all-done = bf16[128,32,128]{2,1,0:T(8,128)(2,1)S(1)} async-done(((bf16[128,32,128]{2,1,0:T(8,128)(2,1)}), bf16[128,32,128]{2,1,0:T(8,128)(2,1)S(1)}, u32[]{:S(2)}, u32[]{:S(2)}) %all-to-all-start) | async-done | bytes 1048608 | tf_op jit(solution)/shard_map/all_to_all | solution.py:25
  39.4 4.9 %all-to-all-start.2 = ((bf16[128,32,128]{2,1,0:T(8,128)(2,1)}), bf16[128,32,128]{2,1,0:T(8,128)(2,1)S(1)}, u32[]{:S(2)}, u32[]{:S(2)}) async-start(bf16[128,32,128]{2,1,0:T(8,128)(2,1)} %copy.31), calls=%async_computation.2 | async-start | bytes 2097152 | tf_op jit(solution)/shard_map/all_to_all | solution.py:32
  44.3 1.2 copy.29
  45.5 24.0 %all-to-all-done.2 = bf16[128,32,128]{2,1,0:T(8,128)(2,1)S(1)} async-done(((bf16[128,32,128]{2,1,0:T(8,128)(2,1)}), bf16[128,32,128]{2,1,0:T(8,128)(2,1)S(1)}, u32[]{:S(2)}, u32[]{:S(2)}) %all-to-all-start.2) | async-done | bytes 1048608 | tf_op jit(solution)/shard_map/all_to_all | solution.py:32
  69.4 6.0 %all-to-all-start.1 = ((bf16[16,256,128]{2,1,0:T(8,128)(2,1)}), bf16[16,256,128]{2,1,0:T(8,128)(2,1)}, u32[]{:S(2)}, u32[]{:S(2)}) async-start(bf16[16,256,128]{2,1,0:T(8,128)(2,1)} %bitcast.58), calls=%async_computation.1 | async-start | bytes 2097152 | tf_op jit(solution)/shard_map/all_to_all | solution.py:24
  75.4 0.1 copy.32
  75.5 1.8 %all-to-all-done.1 = bf16[16,256,128]{2,1,0:T(8,128)(2,1)} async-done(((bf16[16,256,128]{2,1,0:T(8,128)(2,1)}), bf16[16,256,128]{2,1,0:T(8,128)(2,1)}, u32[]{:S(2)}, u32[]{:S(2)}) %all-to-all-start.1) | async-done | bytes 1048608 | tf_op jit(solution)/shard_map/all_to_all | solution.py:24
  77.3 4.6 %all_to_all.99 = bf16[16,256,128]{2,1,0:T(8,128)(2,1)S(1)} all-to-all(bf16[16,256,128]{2,1,0:T(8,128)(2,1)S(1)} %bitcast.59), channel_id=1, replica_groups=mesh['groups'=2,'row'=8,'chan'=2] {'chan'}, dimensions={0} | all-to-all | bytes 2097152 | tf_op jit(solution)/shard_map/all_to_all | solution.py:31
  81.9 1.7 %convolution_convert_fusion = bf16[8,256,256]{2,1,0:T(8,128)(2,1)S(1)} fusion(bf16[2,8,32,8,128]{4,3,2,1,0:T(8,128)(2,1)S(1)} %bitcast.62, bf16[2,8,32,8,128]{4,3,2,1,0:T(8,128)(2,1)} %bitcast.26), kind=kOutput, calls=%fused_computation.29 | convolution fusion | flops 268959744 | bytes 3145728 | tf_op jit(solution)/shard_map/cik,cjk->cij/dot_general | solution.py:39
  83.6 1.0 copy.34
  84.6 4.6 %all_to_all.100 = bf16[8,256,256]{1,0,2:T(8,128)(2,1)S(1)} all-to-all(bf16[8,256,256]{1,0,2:T(8,128)(2,1)S(1)} %copy.34), channel_id=1, replica_groups=mesh['groups'=2,'row'=8,'chan'=2] {'chan'}, dimensions={2} | all-to-all | bytes 2097152 | tf_op jit(solution)/shard_map/all_to_all | solution.py:43
  89.2 1.0 copy.36
  90.2 0.0 copy-start.3
  90.2 1.6 %copy.37 = bf16[16,256,128]{2,0,1:T(8,128)(2,1)} copy(bf16[16,256,128]{2,1,0:T(8,128)(2,1)S(1)} %bitcast.61) | data formatting | bytes 2097152 | tf_op jit(solution)/shard_map/all_to_all | solution.py:43
  91.8 3.6 %all-to-all-start.5 = ((bf16[16,256,128]{2,0,1:T(8,128)(2,1)}), bf16[16,256,128]{2,0,1:T(8,128)(2,1)S(1)}, u32[]{:S(2)}, u32[]{:S(2)}) async-start(bf16[16,256,128]{2,0,1:T(8,128)(2,1)} %copy.37), calls=%async_computation.5 | async-start | bytes 2097152 | tf_op jit(solution)/shard_map/all_to_all | solution.py:42
  95.4 0.0 copy-done.3
  95.4 2.5 %fusion.25 = f32[32,128,128]{2,1,0:T(8,128)} fusion(bf16[32,128,128]{2,1,0:T(8,128)(2,1)S(1)} %copy-done.1, f32[128]{0:T(128)S(1)} %copy-done.5, f32[32,128]{1,0:T(8,128)S(1)} %add_rsqrt_fusion.1, f32[32,128]{1,0:T(8,128)S(1)} %broadcast_multiply_fusion.1, bf16[128,128]{1,0:T(8,128)(2,1)S(1)} %copy-done.3), kind=kOutput, calls=%fused_computation.36 | convolution fusion | flops 136839168 | bytes 3211776 | tf_op jit(solution)/shard_map/ijc,cf->ijf/dot_general | solution.py:21
  97.9 22.7 %all-to-all-done.5 = bf16[16,256,128]{2,0,1:T(8,128)(2,1)S(1)} async-done(((bf16[16,256,128]{2,0,1:T(8,128)(2,1)}), bf16[16,256,128]{2,0,1:T(8,128)(2,1)S(1)}, u32[]{:S(2)}, u32[]{:S(2)}) %all-to-all-start.5) | async-done | bytes 1048608 | tf_op jit(solution)/shard_map/all_to_all | solution.py:42
  120.7 0.3 fusion.30
  121.0 0.2 fusion.18
  121.2 0.3 multiply_reduce_fusion
  121.6 0.0 copy-start.6
  121.6 0.2 copy.39
  121.8 0.4 copy-done.6
  122.2 0.0 copy-start.2
  122.2 0.0 copy-start.7
  122.2 0.3 fusion.17
  122.5 1.3 %copy-done.2 = f32[32,128,128]{2,1,0:T(8,128)S(1)} copy-done((f32[32,128,128]{2,1,0:T(8,128)S(1)}, f32[32,128,128]{2,1,0:T(8,128)}, u32[]{:S(2)}) %copy-start.2) | copy-done | bytes 2097176
  123.8 0.0 copy-done.7
  123.8 2.0 %multiply_convert_fusion = bf16[32,128,128]{2,1,0:T(8,128)(2,1)} fusion(f32[32,128,128]{2,1,0:T(8,128)S(1)} %copy-done.2, bf16[128,32,128]{2,1,0:T(8,128)(2,1)S(1)} %fusion.17, bf16[128,128]{1,0:T(8,128)(2,1)S(1)} %copy-done.7), kind=kOutput, calls=%fused_computation.27 | convolution fusion | flops 136839168 | bytes 4227072 | tf_op jit(solution)/shard_map/hij,hc->ijc/dot_general | solution.py:54
  (5 shorter events, 0.0 us)
Async XLA Ops:
  0.0 4.1 %copy-start = (bf16[128,512]{1,0:T(8,128)(2,1)S(1)}, bf16[128,512]{1,0:T(8,128)(2,1)}, u32[]{:S(2)}) copy-start(bf16[128,512]{1,0:T(8,128)(2,1)} %param.10) | copy-start | bytes 393220
  0.0 4.1 %copy-start.1 = (bf16[32,128,128]{2,1,0:T(8,128)(2,1)S(1)}, bf16[32,128,128]{2,1,0:T(8,128)(2,1)}, u32[]{:S(2)}) copy-start(bf16[32,128,128]{2,1,0:T(8,128)(2,1)} %param.7) | copy-start | bytes 3145732
  0.0 4.1 %copy-start.4 = (s32[32,128]{1,0:T(8,128)S(1)}, s32[32,128]{1,0:T(8,128)}, u32[]{:S(2)}) copy-start(s32[32,128]{1,0:T(8,128)} %param.8) | copy-start | bytes 49156
  0.0 4.1 %copy-start.5 = (f32[128]{0:T(128)S(1)}, f32[128]{0:T(128)}, u32[]{:S(2)}) copy-start(f32[128]{0:T(128)} %param.9) | copy-start | bytes 1540
  8.4 31.0 %all-to-all-start = ((bf16[128,32,128]{2,1,0:T(8,128)(2,1)}), bf16[128,32,128]{2,1,0:T(8,128)(2,1)S(1)}, u32[]{:S(2)}, u32[]{:S(2)}) async-start(bf16[128,32,128]{2,1,0:T(8,128)(2,1)} %copy.28), calls=%async_computation | async-start | bytes 2097152 | tf_op jit(solution)/shard_map/all_to_all | solution.py:25
  39.4 30.0 %all-to-all-start.2 = ((bf16[128,32,128]{2,1,0:T(8,128)(2,1)}), bf16[128,32,128]{2,1,0:T(8,128)(2,1)S(1)}, u32[]{:S(2)}, u32[]{:S(2)}) async-start(bf16[128,32,128]{2,1,0:T(8,128)(2,1)} %copy.31), calls=%async_computation.2 | async-start | bytes 2097152 | tf_op jit(solution)/shard_map/all_to_all | solution.py:32
  69.4 7.9 %all-to-all-start.1 = ((bf16[16,256,128]{2,1,0:T(8,128)(2,1)}), bf16[16,256,128]{2,1,0:T(8,128)(2,1)}, u32[]{:S(2)}, u32[]{:S(2)}) async-start(bf16[16,256,128]{2,1,0:T(8,128)(2,1)} %bitcast.58), calls=%async_computation.1 | async-start | bytes 2097152 | tf_op jit(solution)/shard_map/all_to_all | solution.py:24
  90.2 5.2 %copy-start.3 = (bf16[128,128]{1,0:T(8,128)(2,1)S(1)}, bf16[128,128]{1,0:T(8,128)(2,1)}, u32[]{:S(2)}) copy-start(bf16[128,128]{1,0:T(8,128)(2,1)} %param.11) | copy-start | bytes 98308
  91.8 28.9 %all-to-all-start.5 = ((bf16[16,256,128]{2,0,1:T(8,128)(2,1)}), bf16[16,256,128]{2,0,1:T(8,128)(2,1)S(1)}, u32[]{:S(2)}, u32[]{:S(2)}) async-start(bf16[16,256,128]{2,0,1:T(8,128)(2,1)} %copy.37), calls=%async_computation.5 | async-start | bytes 2097152 | tf_op jit(solution)/shard_map/all_to_all | solution.py:42
  121.6 0.7 copy-start.6
  122.2 1.6 %copy-start.2 = (f32[32,128,128]{2,1,0:T(8,128)S(1)}, f32[32,128,128]{2,1,0:T(8,128)}, u32[]{:S(2)}) copy-start(f32[32,128,128]{2,1,0:T(8,128)} %fusion.25) | copy-start | bytes 6291460
  122.2 1.6 %copy-start.7 = (bf16[128,128]{1,0:T(8,128)(2,1)S(1)}, bf16[128,128]{1,0:T(8,128)(2,1)}, u32[]{:S(2)}) copy-start(bf16[128,128]{1,0:T(8,128)(2,1)} %param.13) | copy-start | bytes 98308
where the time goes:
time: 128 us; the launch traced here: 126 us
  waiting for transfers between devices  71.4 us (56%)
  starting transfers between devices  20.9 us (16%)
  local copies, waits for them, and re-layouts  10.2 us (8%)
  blocking collectives  9.14 us (7%)
  matrix products  7.49 us (6%)
  other arithmetic  6.48 us (5%)
    all_to_all x1, waiting for transfers between devices, local(): lax.all_to_all(right, 'row', split_axis=0, concat_axis=1, tiled=True)  24 us
    all_to_all x1, waiting for transfers between devices, local(): lax.all_to_all(left, 'row', split_axis=0, concat_axis=1, tiled=True)  22.9 us
    all_to_all x1, waiting for transfers between devices, local(): lax.all_to_all(lax.all_to_all(product, 'chan', split_axis=2, concat_axis=...  22.7 us
    all_to_all x1, starting transfers between devices, local(): lax.all_to_all(left, 'row', split_axis=0, concat_axis=1, tiled=True)  6.38 us
    all_to_all x1, starting transfers between devices, local(): lax.all_to_all(lax.all_to_all(left, 'row', split_axis=0, concat_axis=1, t...  6.01 us
    all_to_all x1, starting transfers between devices, local(): lax.all_to_all(right, 'row', split_axis=0, concat_axis=1, tiled=True)  4.93 us
    all_to_all x1, blocking collectives, local(): lax.all_to_all(product, 'chan', split_axis=2, concat_axis=0, tiled=True)  4.58 us
    all_to_all x1, blocking collectives, local(): lax.all_to_all(lax.all_to_all(right, 'row', split_axis=0, concat_axis=1,...  4.56 us
  transfers between devices with their start and end apart: 4, of which 4 were waited for; matrix products, arithmetic and copies ran while one was open for 4% of the time, Pallas kernels for 0%

commit v1 on v0

v1 whole, which is shorter than its diff:
```python
import functools

import jax
import jax.numpy as jnp
from jax import lax
from jax.experimental import pallas as pl
from jax.experimental.pallas import tpu as pltpu
from jax.sharding import PartitionSpec as P

F32, BF16 = jnp.float32, jnp.bfloat16
PIECES = 4
LANES = 128
LIMIT = 40 * 1024 * 1024


def sigmoid(x):
    return 0.5 * jnp.tanh(0.5 * x) + 0.5


def normalise(x, gain):
    mean = jnp.mean(x, axis=-1, keepdims=True)
    centered = x - mean
    var = jnp.mean(centered * centered, axis=-1, keepdims=True)
    return (centered * lax.rsqrt(var + 1e-05) * gain).astype(BF16)


def operands_kernel(where, pair, mask, gain, weight, *rest):
    lefts, rights = rest[:PIECES], rest[PIECES : 2 * PIECES]
    left_all, right_all, turned = rest[2 * PIECES :]
    rows, toks, _ = pair.shape
    hidden = weight.shape[1] // 4
    part = hidden // PIECES
    turned[...] = weight[...].T
    group = 4

    @pl.loop(0, rows // group)
    def _(at):
        first = at * group
        x = pair[pl.ds(first, group)].astype(F32).reshape(group * toks, -1)
        normed = normalise(x, gain[...])
        proj = lax.dot_general(
            turned[...], normed, (((1,), (1,)), ((), ())), preferred_element_type=F32
        )
        for g in range(group):
            valid = mask[pl.ds(first + g, 1), :].astype(F32)
            mine = proj[:, g * toks : (g + 1) * toks]
            blocks = [mine[n * hidden : (n + 1) * hidden] for n in range(4)]
            spot = pl.ds(first + g, hidden, stride=rows)
            left = valid * sigmoid(blocks[0]) * blocks[1]
            right = valid * sigmoid(blocks[2]) * blocks[3]
            for n in range(toks // LANES):
                left_all[n, spot, :] = left[:, n * LANES : (n + 1) * LANES]
                right_all[n, spot, :] = right[:, n * LANES : (n + 1) * LANES]

    for r in range(PIECES):
        span = part * rows
        spot = pl.ds(pl.multiple_of((where[0] ^ r) * span, span), span)
        for n in range(toks // LANES):
            lanes = slice(n * LANES, (n + 1) * LANES)
            rights[r][:, :, lanes] = right_all[n, spot, :].astype(BF16).reshape(part, rows, LANES)
            lefts[r][:, :, lanes] = left_all[n, spot, :].astype(BF16).reshape(part, rows, LANES)


def gate_kernel(pair, gain, weight, out):
    rows, toks, _ = pair.shape
    group = 4

    @pl.loop(0, rows // group)
    def _(at):
        spot = pl.ds(at * group, group)
        x = pair[spot].astype(F32).reshape(group * toks, -1)
        logits = jnp.dot(normalise(x, gain[...]), weight[...], preferred_element_type=F32)
        out[spot] = sigmoid(logits).reshape(group, toks, -1)


def product_kernel(n_left, n_right, places, *rest):
    lefts = [rest[n * PIECES : (n + 1) * PIECES] for n in range(n_left)]
    rest = rest[n_left * PIECES :]
    rights = [rest[n * PIECES : (n + 1) * PIECES] for n in range(n_right)]
    rest = rest[n_right * PIECES :]
    outs, held = rest[: 2 * n_left], rest[2 * n_left]
    part, rows, toks = lefts[0][0].shape
    flip = places[0]
    for s in range(n_right):
        for r in range(PIECES):
            start = places[1 + s] * (2 * rows) + ((r // 2) ^ flip) * rows
            spot = pl.ds(pl.multiple_of(start, rows), rows)
            held[:, spot, (r % 2) * toks : (r % 2 + 1) * toks] = rights[s][r][...]
    for c in range(part):
        left = jnp.concatenate(
            [
                jnp.concatenate([lefts[n][2 * ry][c], lefts[n][2 * ry + 1][c]], axis=1)
                for n in range(n_left)
                for ry in range(2)
            ],
            axis=0,
        )
        out = lax.dot_general(
            left, held[c], (((1,), (1,)), ((), ())), preferred_element_type=F32
        ).astype(BF16)
        for n in range(2 * n_left):
            outs[n][c] = out[n * rows : (n + 1) * rows]


def update_kernel(where, gain, weight, gate, *rest):
    sets = [rest[n * PIECES : (n + 1) * PIECES] for n in range(3)]
    out, pieces, turned, sems = rest[3 * PIECES :]
    part, rows, toks = sets[0][0].shape
    hidden = part * PIECES
    for n in range(3):

        @pl.when(where[1] == n)
        def _():
            copies = [
                pltpu.make_async_copy(sets[n][r], pieces.at[r], sems.at[r]) for r in range(PIECES)
            ]
            for copy in copies:
                copy.start()
            for copy in copies:
                copy.wait()

    for r in range(PIECES):
        base = (where[0] ^ r) * part
        for c in range(part):
            piece = pieces[r, c].astype(F32)
            for n in range(toks // LANES):
                lanes = slice(n * LANES, (n + 1) * LANES)
                turned[n, pl.ds(base + c, rows, stride=hidden), :] = piece[:, lanes]
    scale = jnp.broadcast_to(gain[...], (hidden, toks))

    @pl.loop(0, rows)
    def _(i):
        spot = pl.ds(pl.multiple_of(i * hidden, hidden), hidden)
        x = jnp.concatenate([turned[n, spot, :] for n in range(toks // LANES)], axis=1)
        mean = jnp.mean(x, axis=0, keepdims=True)
        centered = x - mean
        var = jnp.mean(centered * centered, axis=0, keepdims=True)
        pnorm = (centered * lax.rsqrt(var + 1e-05) * scale).astype(BF16)
        mapped = lax.dot_general(
            pnorm, weight[...], (((0,), (0,)), ((), ())), preferred_element_type=F32
        )
        out[i] = (gate[i] * mapped).astype(BF16)


SMEM = pl.BlockSpec(memory_space=pltpu.SMEM)
VMEM = pl.BlockSpec(memory_space=pltpu.VMEM)
ANY = pl.BlockSpec(memory_space=pl.ANY)
PARAMS = pltpu.CompilerParams(vmem_limit_bytes=LIMIT)


def local(pair, pair_mask, in_gain, proj_weight, gate_weight, out_gain, out_weight, *, n_row):
    rows, toks, channels = pair.shape
    hidden = proj_weight.shape[1] // 4
    part = hidden // PIECES
    planes = n_row // 2
    half = planes // 2
    row, core = lax.axis_index("row"), lax.axis_index("chan")
    z, y = row // 2, row % 2
    quarter = 2 * y + core
    own_half = z // half
    at_end = (z == 0) | (z == planes - 1)
    mode = jnp.where(core == own_half, 0, jnp.where(at_end, 2, 1))
    where = jnp.stack([quarter, mode]).astype(jnp.int32)

    def send(x, target):
        pairs = []
        for source in range(2 * n_row):
            to = target(source // 4, source // 2 % 2, source % 2)
            if to is not None:
                pairs.append((source, 4 * to[0] + 2 * to[1] + to[2]))
        return lax.ppermute(x, ("row", "chan"), pairs)

    def is_end(p):
        return p == 0 or p == planes - 1

    def inward(p):
        return 1 if p == 0 else planes - 2

    def outward(p):
        return p - 1 if p < half else p + 1

    def in_plane(r):
        return lambda p, b, k: (p, b ^ (r // 2), k ^ (r % 2))

    def shifted(s):
        def target(p, b, k):
            base = p // half * half
            return (base + (p - base + s) % half, b, k)

        return target

    def mirrored(p, b, k):
        return None if is_end(p) else (planes - 1 - p, b, k)

    def to_inner(p, b, k):
        return (inward(p), b, k) if is_end(p) else None

    def back_own(r):
        def target(p, b, k):
            return (p, b ^ (r // 2), k ^ (r % 2)) if k ^ (r % 2) == p // half else None

        return target

    def back_other(r):
        def target(p, b, k):
            if is_end(p) or k ^ (r % 2) == p // half:
                return None
            return (p, b ^ (r // 2), k ^ (r % 2))

        return target

    def back_end(r):
        def target(p, b, k):
            if is_end(p) or not is_end(outward(p)) or k ^ (r % 2) == p // half:
                return None
            return (outward(p), b ^ (r // 2), k ^ (r % 2))

        return target

    piece = jax.ShapeDtypeStruct((part, rows, toks), BF16)
    made = pl.pallas_call(
        operands_kernel,
        out_shape=[piece] * (2 * PIECES),
        in_specs=[SMEM, VMEM, VMEM, VMEM, VMEM],
        out_specs=[VMEM] * (2 * PIECES),
        scratch_shapes=[
            pltpu.VMEM((toks // LANES, hidden * rows, LANES), F32),
            pltpu.VMEM((toks // LANES, hidden * rows, LANES), F32),
            pltpu.VMEM((4 * hidden, channels), BF16),
        ],
        compiler_params=PARAMS,
        name="operands",
    )(where, pair, pair_mask, in_gain.reshape(1, -1), proj_weight)
    lefts, rights = made[:PIECES], made[PIECES:]
    rights = [rights[0]] + [send(rights[r], in_plane(r)) for r in range(1, PIECES)]
    lefts = [lefts[0]] + [send(lefts[r], in_plane(r)) for r in range(1, PIECES)]
    own = [rights] + [[send(x, shifted(s)) for x in rights] for s in range(1, half)]
    other = [[send(x, mirrored) for x in own[s]] for s in range(half)]
    outer = [send(x, to_inner) for x in lefts]

    gate = pl.pallas_call(
        gate_kernel,
        out_shape=jax.ShapeDtypeStruct((rows, toks, channels), F32),
        in_specs=[VMEM] * 3,
        out_specs=VMEM,
        compiler_params=PARAMS,
        name="gate",
    )(pair, in_gain.reshape(1, -1), gate_weight)

    def products(sides, planes_right, places, name):
        count, depth = len(sides), len(planes_right)
        return pl.pallas_call(
            functools.partial(product_kernel, count, depth),
            out_shape=[jax.ShapeDtypeStruct((part, rows, 2 * rows * depth), BF16)] * (2 * count),
            in_specs=[SMEM] + [VMEM] * (PIECES * (count + depth)),
            out_specs=[VMEM] * (2 * count),
            scratch_shapes=[pltpu.VMEM((part, 2 * rows * depth, 2 * toks), BF16)],
            compiler_params=PARAMS,
            name=name,
        )(places, *[x for side in sides for x in side], *[x for side in planes_right for x in side])

    inner = z - own_half * half
    far = planes - 1 - z
    far_inner = far - far // half * half
    steps = jnp.arange(half)
    places_own = jnp.concatenate([y[None], (inner - steps) % half]).astype(jnp.int32)
    places_far = jnp.concatenate([y[None], (far_inner - steps) % half]).astype(jnp.int32)
    near = products([lefts], own, places_own, "near")
    away = products([lefts, outer], other, places_far, "away")

    own_set = [near[0]] + [send(near[r // 2], back_own(r)) for r in range(1, PIECES)]
    end_set = [send(away[2 + r // 2], back_end(r)) for r in range(PIECES)]
    far_set = [away[0]] + [send(away[r // 2], back_other(r)) for r in range(1, PIECES)]

    return pl.pallas_call(
        update_kernel,
        out_shape=jax.ShapeDtypeStruct((rows, toks, channels), BF16),
        in_specs=[SMEM, VMEM, VMEM, VMEM] + [ANY] * (3 * PIECES),
        out_specs=VMEM,
        scratch_shapes=[
            pltpu.VMEM((PIECES, part, rows, toks), BF16),
            pltpu.VMEM((toks // LANES, rows * hidden, LANES), F32),
            pltpu.SemaphoreType.DMA((PIECES,)),
        ],
        compiler_params=PARAMS,
        name="update",
    )(where, out_gain.reshape(-1, 1), out_weight, gate, *own_set, *far_set, *end_set)


def solution(mesh):
    placed = (
        P(("groups", "row"), "chan", None),
        P(("groups", "row"), "chan"),
        P(),
        P(),
        P(),
        P(),
        P(),
    )
    return jax.shard_map(
        functools.partial(local, n_row=mesh.shape["row"]),
        mesh=mesh,
        in_specs=placed,
        out_specs=P(("groups", "row"), "chan", None),
        check_vma=False,
    )
```

time: 128 us -> 134 us (1.047)
  Pallas kernels: 0 us -> 27.8 us
  starting transfers between devices: 20.9 us -> 39.7 us
  waiting for transfers between devices: 71.4 us -> 54 us
  blocking collectives: 9.14 us -> 0 us
  matrix products: 7.49 us -> 0 us
  other arithmetic: 6.48 us -> 0.25 us
    all_to_all x4 -> x0, waiting for transfers between devices: 71.4 us -> none  [the longest x1 24 us: local(): lax.all_to_all(right, 'row', split_axis=0, concat_axis=1, tiled=True)]
    ppermute x0 -> x32, waiting for transfers between devices: none -> 54 us  [send(): return lax.ppermute(x, ('row', 'chan'), pairs)]
    ppermute x0 -> x32, starting transfers between devices: none -> 39.7 us  [send(): return lax.ppermute(x, ('row', 'chan'), pairs)]
    pallas_call x0 -> x5, Pallas kernels: none -> 27.8 us  [the longest x1 12.6 us: local(): pl.pallas_call(update_kernel, out_shape=jax.ShapeDtypeStruct((rows, toks,...]
    all_to_all x4 -> x0, starting transfers between devices: 20.9 us -> none  [the longest x1 6.38 us: local(): lax.all_to_all(left, 'row', split_axis=0, concat_axis=1, tiled=True)]
    all_to_all x2 -> x0, blocking collectives: 9.14 us -> none  [the longest x1 4.58 us: local(): lax.all_to_all(product, 'chan', split_axis=2, concat_axis=0, tiled=True)]
    unnamed x16 -> x42, local copies, waits for them, and re-layouts: 1.71 us -> 10.6 us
    dot_general x4 -> x0, matrix products: 7.49 us -> none  [the longest x1 2.55 us: local(): jnp.einsum('ijc,cf->ijf', normed, gate_weight, preferred_element_type=jnp...]
  transfers between devices with their start and end apart: 4 -> 32, of which waited for: 4 -> 13; matrix products, arithmetic and copies ran while one was open for 4% -> 0% of each run, Pallas kernels for 0% -> 6%
where the time goes in v1:
time: 134 us; the launch traced here: 133 us
  waiting for transfers between devices  54 us (40%)
  starting transfers between devices  39.7 us (30%)
  Pallas kernels  27.8 us (21%)
  local copies, waits for them, and re-layouts  10.8 us (8%)
    ppermute x32, waiting for transfers between devices, send(): return lax.ppermute(x, ('row', 'chan'), pairs)  54 us
    ppermute x32, starting transfers between devices, send(): return lax.ppermute(x, ('row', 'chan'), pairs)  39.7 us
    pallas_call x1, Pallas kernels, local(): pl.pallas_call(update_kernel, out_shape=jax.ShapeDtypeStruct((rows, toks,...  12.6 us
    unnamed x42, local copies, waits for them, and re-layouts  10.6 us
    pallas_call x1, Pallas kernels, local(): pl.pallas_call(operands_kernel, out_shape=[piece] * (2 * PIECES), in_spec...  7.1 us
    pallas_call x2, Pallas kernels, products(): pl.pallas_call(functools.partial(product_kernel, count, depth), out_shape...  5.15 us
    pallas_call x1, Pallas kernels, local(): pl.pallas_call(gate_kernel, out_shape=jax.ShapeDtypeStruct((rows, toks, c...  2.9 us
  transfers between devices with their start and end apart: 32, of which 13 were waited for; matrix products, arithmetic and copies ran while one was open for 0% of the time, Pallas kernels for 6%

profile of v1, /device:TPU:1, one launch (start us, length us, event | category | flops | bytes accessed | tf_op | source)
XLA Modules:
  0.0 133.0 jit_solution(16313850165361344878)
XLA Ops:
  0.0 0.1 pad_add_fusion.where
  0.1 1.2 copy-done
  1.3 0.9 copy-done.14
  2.2 0.7 copy-done.17
  2.9 0.7 copy-done.18
  3.6 7.1 %operands.1 = (bf16[32,32,128]{2,1,0:T(8,128)(2,1)S(1)}, bf16[32,32,128]{2,1,0:T(8,128)(2,1)S(1)}, bf16[32,32,128]{2,1,0:T(8,128)(2,1)S(1)}, bf16[32,32,128]{2,1...) custom-call(s32[2]{0:T(128)S(1)} %pad_add_fusion.where, ...), custom_call_target="tpu_custom_call" | custom-call | tf_op jit(solution)/shard_map/operands/pallas_call | solution.py:221
  10.7 0.1 collective-permute-start.3
  10.8 2.7 %collective-permute-start.4 = (bf16[32,32,128]{2,1,0:T(8,128)(2,1)S(1)}, bf16[32,32,128]{2,1,0:T(8,128)(2,1)}, u32[]{:S(2)}, u32[]{:S(2)}) collective-permute-start(bf16[32,32,128]{2,1,0:T(8,128)(2,1)S(1)} %get-tuple-element.25), channel_id=1, source_target_pairs={{0,2},{1,3},{2,0},{3,1},{4,6},{5,7},{6,4},{7,5},{8,10},{9,11},{10,... | collective-permute-start | bytes 786440 | tf_op jit(solution)/shard_map/ppermute | solution.py:171
  13.6 0.4 collective-permute-start
  13.9 1.4 %collective-permute-start.1 = (bf16[32,32,128]{2,1,0:T(8,128)(2,1)S(1)}, bf16[32,32,128]{2,1,0:T(8,128)(2,1)S(1)}, u32[]{:S(2)}, u32[]{:S(2)}) collective-permute-start(bf16[32,32,128]{2,1,0:T(8,128)(2,1)S(1)} %get-tuple-element.21), channel_id=1, source_target_pairs={{0,2},{1,3},{2,0},{3,1},{4,6},{5,7},{6,4},{7,5},{8,10},{9,11},{10,... | collective-permute-start | bytes 786440 | tf_op jit(solution)/shard_map/ppermute | solution.py:171
  15.4 0.3 collective-permute-start.2
  15.7 4.5 %collective-permute-done.4.rest_6_ = bf16[32,32,128]{2,1,0:T(8,128)(2,1)} collective-permute-done((bf16[32,32,128]{2,1,0:T(8,128)(2,1)S(1)}, bf16[32,32,128]{2,1,0:T(8,128)(2,1)}, u32[]{:S(2)}, u32[]{:S(2)}) %collective-permute-start.4) | collective-permute-done | bytes 262176 | tf_op jit(solution)/shard_map/ppermute | solution.py:171
  20.2 1.3 %collective-permute-start.6 = (bf16[32,32,128]{2,1,0:T(8,128)(2,1)S(1)}, bf16[32,32,128]{2,1,0:T(8,128)(2,1)}, u32[]{:S(2)}, u32[]{:S(2)}) collective-permute-start(bf16[32,32,128]{2,1,0:T(8,128)(2,1)S(1)} %get-tuple-element.23.rest_4_), channel_id=1, source_target_pairs={{0,4},{1,5},{2,6},{3,7},{4,0},{5,1},{6,2},{7,3},{8,12},{9,13},{10,... | collective-permute-start | bytes 786440 | tf_op jit(solution)/shard_map/ppermute | solution.py:171
  21.6 4.8 %collective-permute-done.5.rest_7_ = bf16[32,32,128]{2,1,0:T(8,128)(2,1)} collective-permute-done((bf16[32,32,128]{2,1,0:T(8,128)(2,1)S(1)}, bf16[32,32,128]{2,1,0:T(8,128)(2,1)}, u32[]{:S(2)}, u32[]{:S(2)}) %collective-permute-start.5) | collective-permute-done | bytes 262176 | tf_op jit(solution)/shard_map/ppermute | solution.py:171
  26.3 3.6 %collective-permute-start.13 = (bf16[32,32,128]{2,1,0:T(8,128)(2,1)S(1)}, bf16[32,32,128]{2,1,0:T(8,128)(2,1)S(1)}, u32[]{:S(2)}, u32[]{:S(2)}) collective-permute-start(bf16[32,32,128]{2,1,0:T(8,128)(2,1)S(1)} %get-tuple-element.19.rest_0_), channel_id=1, source_target_pairs={{0,4},{1,5},{2,6},{3,7},{12,8},{13,9},{14,10},{15,11},{16,20},{17,... | collective-permute-start | bytes 786440 | tf_op jit(solution)/shard_map/ppermute | solution.py:171
  30.0 0.7 collective-permute-start.17
  30.7 0.7 collective-permute-done.1.rest_2_
  31.3 1.3 %collective-permute-start.7 = (bf16[32,32,128]{2,1,0:T(8,128)(2,1)S(1)}, bf16[32,32,128]{2,1,0:T(8,128)(2,1)}, u32[]{:S(2)}, u32[]{:S(2)}) collective-permute-start(bf16[32,32,128]{2,1,0:T(8,128)(2,1)S(1)} %collective-permute-done.3.rest_5_), channel_id=1, source_target_pairs={{0,4},{1,5},{2,6},{3,7},{4,0},{5,1},{6,2},{7,3},{8,12},{9,13},{10,... | collective-permute-start | bytes 786440 | tf_op jit(solution)/shard_map/ppermute | solution.py:171
  32.7 4.6 %collective-permute-done.2.rest_3_ = bf16[32,32,128]{2,1,0:T(8,128)(2,1)S(1)} collective-permute-done((bf16[32,32,128]{2,1,0:T(8,128)(2,1)S(1)}, bf16[32,32,128]{2,1,0:T(8,128)(2,1)S(1)}, u32[]{:S(2)}, u32[]{:S(2)}) %collective-permute-start.2) | collective-permute-done | bytes 262176 | tf_op jit(solution)/shard_map/ppermute | solution.py:171
  37.3 1.5 %collective-permute-start.8 = (bf16[32,32,128]{2,1,0:T(8,128)(2,1)}, bf16[32,32,128]{2,1,0:T(8,128)(2,1)}, u32[]{:S(2)}, u32[]{:S(2)}) collective-permute-start(bf16[32,32,128]{2,1,0:T(8,128)(2,1)} %collective-permute-done.4.rest_6_), channel_id=1, source_target_pairs={{0,4},{1,5},{2,6},{3,7},{4,0},{5,1},{6,2},{7,3},{8,12},{9,13},{10,... | collective-permute-start | bytes 786440 | tf_op jit(solution)/shard_map/ppermute | solution.py:171
  38.9 3.4 %collective-permute-start.14 = (bf16[32,32,128]{2,1,0:T(8,128)(2,1)S(1)}, bf16[32,32,128]{2,1,0:T(8,128)(2,1)S(1)}, u32[]{:S(2)}, u32[]{:S(2)}) collective-permute-start(bf16[32,32,128]{2,1,0:T(8,128)(2,1)S(1)} %collective-permute-done.rest_1_), channel_id=1, source_target_pairs={{0,4},{1,5},{2,6},{3,7},{12,8},{13,9},{14,10},{15,11},{16,20},{17,... | collective-permute-start | bytes 786440 | tf_op jit(solution)/shard_map/ppermute | solution.py:171
  42.3 1.3 collective-permute-start.15
  43.6 2.3 %collective-permute-start.16 = (bf16[32,32,128]{2,1,0:T(8,128)(2,1)S(1)}, bf16[32,32,128]{2,1,0:T(8,128)(2,1)S(1)}, u32[]{:S(2)}, u32[]{:S(2)}) collective-permute-start(bf16[32,32,128]{2,1,0:T(8,128)(2,1)S(1)} %collective-permute-done.2.rest_3_), channel_id=1, source_target_pairs={{0,4},{1,5},{2,6},{3,7},{12,8},{13,9},{14,10},{15,11},{16,20},{17,... | collective-permute-start | bytes 786440 | tf_op jit(solution)/shard_map/ppermute | solution.py:171
  45.9 1.5 %collective-permute-done.8.rest_10_ = bf16[32,32,128]{2,1,0:T(8,128)(2,1)} collective-permute-done((bf16[32,32,128]{2,1,0:T(8,128)(2,1)}, bf16[32,32,128]{2,1,0:T(8,128)(2,1)}, u32[]{:S(2)}, u32[]{:S(2)}) %collective-permute-start.8) | collective-permute-done | bytes 262176 | tf_op jit(solution)/shard_map/ppermute | solution.py:171
  47.4 0.7 collective-permute-start.18
  48.1 0.7 copy-done.12
  48.8 4.2 %collective-permute-done.9.rest_11_ = bf16[32,32,128]{2,1,0:T(8,128)(2,1)} collective-permute-done((bf16[32,32,128]{2,1,0:T(8,128)(2,1)}, bf16[32,32,128]{2,1,0:T(8,128)(2,1)}, u32[]{:S(2)}, u32[]{:S(2)}) %collective-permute-start.9) | collective-permute-done | bytes 262176 | tf_op jit(solution)/shard_map/ppermute | solution.py:171
  53.0 0.7 collective-permute-start.19
  53.8 4.8 %collective-permute-done.14.rest_5_ = bf16[32,32,128]{2,1,0:T(8,128)(2,1)S(1)} collective-permute-done((bf16[32,32,128]{2,1,0:T(8,128)(2,1)S(1)}, bf16[32,32,128]{2,1,0:T(8,128)(2,1)S(1)}, u32[]{:S(2)}, u32[]{:S(2)}) %collective-permute-start.14) | collective-permute-done | bytes 262176 | tf_op jit(solution)/shard_map/ppermute | solution.py:171
  58.6 0.7 collective-permute-start.20
  59.2 4.9 %collective-permute-done.15.rest_6_ = bf16[32,32,128]{2,1,0:T(8,128)(2,1)S(1)} collective-permute-done((bf16[32,32,128]{2,1,0:T(8,128)(2,1)S(1)}, bf16[32,32,128]{2,1,0:T(8,128)(2,1)S(1)}, u32[]{:S(2)}, u32[]{:S(2)}) %collective-permute-start.15) | collective-permute-done | bytes 262176 | tf_op jit(solution)/shard_map/ppermute | solution.py:171
  64.2 0.7 collective-permute-start.21
  64.8 4.9 %collective-permute-done.16.rest_7_ = bf16[32,32,128]{2,1,0:T(8,128)(2,1)S(1)} collective-permute-done((bf16[32,32,128]{2,1,0:T(8,128)(2,1)S(1)}, bf16[32,32,128]{2,1,0:T(8,128)(2,1)S(1)}, u32[]{:S(2)}, u32[]{:S(2)}) %collective-permute-start.16) | collective-permute-done | bytes 262176 | tf_op jit(solution)/shard_map/ppermute | solution.py:171
  69.8 0.7 collective-permute-start.22
  70.5 0.7 collective-permute-start.23
  71.2 0.7 collective-permute-start.24
  71.9 0.1 pad_add_fusion.2.places
  71.9 0.1 pad_add_fusion.1.places
  72.0 0.9 copy-done.13
  73.0 2.6 %near.1 = (bf16[32,32,128]{2,1,0:T(8,128)(2,1)S(1)}, bf16[32,32,128]{2,1,0:T(8,128)(2,1)S(1)}) custom-call(s32[3]{0:T(128)S(1)} %pad_add_fusion.1.places, bf16[32,32,128]{2,1,0:T(8,128)(2,1)S(1)} %get-tuple-element.19.rest_0_, bf16[32,32,128]{2,1,0:T(8,128)(2,1)S(1)} %collective-permute-done.rest_1_, ...), custom_call_target="tpu_custom_call" | custom-call | tf_op jit(solution)/shard_map/near/pallas_call | solution.py:252
  75.6 2.2 %collective-permute-start.10 = (bf16[32,32,128]{2,1,0:T(8,128)(2,1)S(1)}, bf16[32,32,128]{2,1,0:T(8,128)(2,1)S(1)}, u32[]{:S(2)}, u32[]{:S(2)}) collective-permute-start(bf16[32,32,128]{2,1,0:T(8,128)(2,1)S(1)} %get-tuple-element.27.rest_0_), channel_id=1, source_target_pairs={{1,0},{3,2},{5,4},{7,6},{8,9},{10,11},{12,13},{14,15},{17,16},{19,... | collective-permute-start | bytes 786440 | tf_op jit(solution)/shard_map/ppermute | solution.py:171
  77.9 0.8 collective-permute-start.11
  78.7 4.2 %collective-permute-start.12 = (bf16[32,32,128]{2,1,0:T(8,128)(2,1)S(1)}, bf16[32,32,128]{2,1,0:T(8,128)(2,1)S(1)}, u32[]{:S(2)}, u32[]{:S(2)}) collective-permute-start(bf16[32,32,128]{2,1,0:T(8,128)(2,1)S(1)} %get-tuple-element.28), channel_id=1, source_target_pairs={{1,2},{3,0},{5,6},{7,4},{8,11},{10,9},{12,15},{14,13},{17,18},{19,... | collective-permute-start | bytes 786440 | tf_op jit(solution)/shard_map/ppermute | solution.py:171
  82.9 2.5 %away.1 = (bf16[32,32,128]{2,1,0:T(8,128)(2,1)S(1)}, bf16[32,32,128]{2,1,0:T(8,128)(2,1)}, bf16[32,32,128]{2,1,0:T(8,128)(2,1)}, bf16[32,32,128]{2,1,0:T(8,128)(2,1)}) custom-call(s32[3]{0:T(128)S(1)} %pad_add_fusion.2.places, bf16[32,32,128]{2,1,0:T(8,128)(2,1)S(1)} %get-tuple-element.19.rest_0_, bf16[32,32,128]{2,1,0:T(8,128)(2,1)S(1)} %collective-permute-done.rest_1_, ...), custom_call_target="tpu_custom_call" | custom-call | tf_op jit(solution)/shard_map/away/pallas_call | solution.py:252
  85.4 0.8 collective-permute-start.25
  86.2 0.7 collective-permute-start.26
  86.9 0.7 collective-permute-start.27
  87.6 1.3 collective-permute-start.28
  88.9 1.3 collective-permute-start.29
  90.3 1.3 collective-permute-start.30
  91.6 1.3 collective-permute-start.31
  92.9 2.9 %gate.1 = f32[32,128,128]{2,1,0:T(8,128)S(1)} custom-call(bf16[32,128,128]{2,1,0:T(8,128)(2,1)S(1)} %copy-done.1, f32[1,128]{1,0:T(1,128)S(1)} %bitcast.6, bf16[128,128]{1,0:T(8,128)(2,1)S(1)} %copy-done.15), custom_call_target="tpu_custom_call" | custom-call | tf_op jit(solution)/shard_map/gate/pallas_call | solution.py:241
  95.9 0.1 copy.8.gain
  96.0 0.7 copy-done.10
  96.7 10.0 %collective-permute-done.28.rest_8_ = bf16[32,32,128]{2,1,0:T(8,128)(2,1)} collective-permute-done((bf16[32,32,128]{2,1,0:T(8,128)(2,1)}, bf16[32,32,128]{2,1,0:T(8,128)(2,1)}, u32[]{:S(2)}, u32[]{:S(2)}) %collective-permute-start.28) | collective-permute-done | bytes 262176 | tf_op jit(solution)/shard_map/ppermute | solution.py:171
  106.7 5.1 %collective-permute-done.29.rest_9_ = bf16[32,32,128]{2,1,0:T(8,128)(2,1)} collective-permute-done((bf16[32,32,128]{2,1,0:T(8,128)(2,1)}, bf16[32,32,128]{2,1,0:T(8,128)(2,1)}, u32[]{:S(2)}, u32[]{:S(2)}) %collective-permute-start.29) | collective-permute-done | bytes 262176 | tf_op jit(solution)/shard_map/ppermute | solution.py:171
  111.9 0.6 collective-permute-done.30.rest_10_
  112.4 3.2 %collective-permute-done.31.rest_11_ = bf16[32,32,128]{2,1,0:T(8,128)(2,1)} collective-permute-done((bf16[32,32,128]{2,1,0:T(8,128)(2,1)}, bf16[32,32,128]{2,1,0:T(8,128)(2,1)}, u32[]{:S(2)}, u32[]{:S(2)}) %collective-permute-start.31) | collective-permute-done | bytes 262176 | tf_op jit(solution)/shard_map/ppermute | solution.py:171
  115.6 0.9 copy-done.3
  116.6 0.9 copy-done.5
  117.5 0.9 copy-done.7
  118.5 0.9 copy-done.9
  119.4 0.9 copy-done.11
  120.4 12.6 %update.1 = bf16[32,128,128]{2,1,0:T(8,128)(2,1)} custom-call(s32[2]{0:T(128)S(1)} %pad_add_fusion.where, f32[128,1]{1,0:T(8,128)S(1)} %copy.8.gain, bf16[128,128]{1,0:T(8,128)(2,1)S(1)} %copy-done.16, f32[32,128,128]{2,1,0:T(8,128)S(1)} %gate.1, bf16[32,32,128]{2,1,0:T(8,128)(2,1)S(1)} %get-tuple-element.27.rest_0_, ...), custom_call_target="tpu_custom_call" | custom-call | tf_op jit(solution)/shard_map/update/pallas_call | solution.py:275
  (53 shorter events, 0.2 us)
Async XLA Ops:
  0.1 1.2 copy-start
  1.3 0.9 copy-start.14
  2.2 0.7 copy-start.17
  2.9 0.7 copy-start.18
  10.7 4.7 %collective-permute-start.3 = (bf16[32,32,128]{2,1,0:T(8,128)(2,1)S(1)}, bf16[32,32,128]{2,1,0:T(8,128)(2,1)S(1)}, u32[]{:S(2)}, u32[]{:S(2)}) collective-permute-start(bf16[32,32,128]{2,1,0:T(8,128)(2,1)S(1)} %get-tuple-element.24), channel_id=1, source_target_pairs={{0,1},{1,0},{2,3},{3,2},{4,5},{5,4},{6,7},{7,6},{8,9},{9,8},{10,11... | collective-permute-start | bytes 786440 | tf_op jit(solution)/shard_map/ppermute | solution.py:171
  10.8 9.4 %collective-permute-start.4 = (bf16[32,32,128]{2,1,0:T(8,128)(2,1)S(1)}, bf16[32,32,128]{2,1,0:T(8,128)(2,1)}, u32[]{:S(2)}, u32[]{:S(2)}) collective-permute-start(bf16[32,32,128]{2,1,0:T(8,128)(2,1)S(1)} %get-tuple-element.25), channel_id=1, source_target_pairs={{0,2},{1,3},{2,0},{3,1},{4,6},{5,7},{6,4},{7,5},{8,10},{9,11},{10,... | collective-permute-start | bytes 786440 | tf_op jit(solution)/shard_map/ppermute | solution.py:171
  13.5 12.8 %collective-permute-start.5 = (bf16[32,32,128]{2,1,0:T(8,128)(2,1)S(1)}, bf16[32,32,128]{2,1,0:T(8,128)(2,1)}, u32[]{:S(2)}, u32[]{:S(2)}) collective-permute-start(bf16[32,32,128]{2,1,0:T(8,128)(2,1)S(1)} %get-tuple-element.26), channel_id=1, source_target_pairs={{0,3},{1,2},{2,1},{3,0},{4,7},{5,6},{6,5},{7,4},{8,11},{9,10},{10,... | collective-permute-start | bytes 786440 | tf_op jit(solution)/shard_map/ppermute | solution.py:171
  13.6 16.4 %collective-permute-start = (bf16[32,32,128]{2,1,0:T(8,128)(2,1)S(1)}, bf16[32,32,128]{2,1,0:T(8,128)(2,1)S(1)}, u32[]{:S(2)}, u32[]{:S(2)}) collective-permute-start(bf16[32,32,128]{2,1,0:T(8,128)(2,1)S(1)} %get-tuple-element.20), channel_id=1, source_target_pairs={{0,1},{1,0},{2,3},{3,2},{4,5},{5,4},{6,7},{7,6},{8,9},{9,8},{10,11... | collective-permute-start | bytes 786440 | tf_op jit(solution)/shard_map/ppermute | solution.py:171
  13.9 17.4 %collective-permute-start.1 = (bf16[32,32,128]{2,1,0:T(8,128)(2,1)S(1)}, bf16[32,32,128]{2,1,0:T(8,128)(2,1)S(1)}, u32[]{:S(2)}, u32[]{:S(2)}) collective-permute-start(bf16[32,32,128]{2,1,0:T(8,128)(2,1)S(1)} %get-tuple-element.21), channel_id=1, source_target_pairs={{0,2},{1,3},{2,0},{3,1},{4,6},{5,7},{6,4},{7,5},{8,10},{9,11},{10,... | collective-permute-start | bytes 786440 | tf_op jit(solution)/shard_map/ppermute | solution.py:171
  15.4 21.9 %collective-permute-start.2 = (bf16[32,32,128]{2,1,0:T(8,128)(2,1)S(1)}, bf16[32,32,128]{2,1,0:T(8,128)(2,1)S(1)}, u32[]{:S(2)}, u32[]{:S(2)}) collective-permute-start(bf16[32,32,128]{2,1,0:T(8,128)(2,1)S(1)} %get-tuple-element.22), channel_id=1, source_target_pairs={{0,3},{1,2},{2,1},{3,0},{4,7},{5,6},{6,5},{7,4},{8,11},{9,10},{10,... | collective-permute-start | bytes 786440 | tf_op jit(solution)/shard_map/ppermute | solution.py:171
  20.2 18.7 %collective-permute-start.6 = (bf16[32,32,128]{2,1,0:T(8,128)(2,1)S(1)}, bf16[32,32,128]{2,1,0:T(8,128)(2,1)}, u32[]{:S(2)}, u32[]{:S(2)}) collective-permute-start(bf16[32,32,128]{2,1,0:T(8,128)(2,1)S(1)} %get-tuple-element.23.rest_4_), channel_id=1, source_target_pairs={{0,4},{1,5},{2,6},{3,7},{4,0},{5,1},{6,2},{7,3},{8,12},{9,13},{10,... | collective-permute-start | bytes 786440 | tf_op jit(solution)/shard_map/ppermute | solution.py:171
  26.3 12.6 %collective-permute-start.13 = (bf16[32,32,128]{2,1,0:T(8,128)(2,1)S(1)}, bf16[32,32,128]{2,1,0:T(8,128)(2,1)S(1)}, u32[]{:S(2)}, u32[]{:S(2)}) collective-permute-start(bf16[32,32,128]{2,1,0:T(8,128)(2,1)S(1)} %get-tuple-element.19.rest_0_), channel_id=1, source_target_pairs={{0,4},{1,5},{2,6},{3,7},{12,8},{13,9},{14,10},{15,11},{16,20},{17,... | collective-permute-start | bytes 786440 | tf_op jit(solution)/shard_map/ppermute | solution.py:171
  30.0 12.3 %collective-permute-start.17 = (bf16[32,32,128]{2,1,0:T(8,128)(2,1)S(1)}, bf16[32,32,128]{2,1,0:T(8,128)(2,1)S(1)}, u32[]{:S(2)}, u32[]{:S(2)}) collective-permute-start(bf16[32,32,128]{2,1,0:T(8,128)(2,1)S(1)} %get-tuple-element.23.rest_4_), channel_id=1, source_target_pairs={{4,8},{5,9},{6,10},{7,11},{8,4},{9,5},{10,6},{11,7},{20,24},{21,25... | collective-permute-start | bytes 786440 | tf_op jit(solution)/shard_map/ppermute | solution.py:171
  31.3 12.3 %collective-permute-start.7 = (bf16[32,32,128]{2,1,0:T(8,128)(2,1)S(1)}, bf16[32,32,128]{2,1,0:T(8,128)(2,1)}, u32[]{:S(2)}, u32[]{:S(2)}) collective-permute-start(bf16[32,32,128]{2,1,0:T(8,128)(2,1)S(1)} %collective-permute-done.3.rest_5_), channel_id=1, source_target_pairs={{0,4},{1,5},{2,6},{3,7},{4,0},{5,1},{6,2},{7,3},{8,12},{9,13},{10,... | collective-permute-start | bytes 786440 | tf_op jit(solution)/shard_map/ppermute | solution.py:171
  37.3 10.1 %collective-permute-start.8 = (bf16[32,32,128]{2,1,0:T(8,128)(2,1)}, bf16[32,32,128]{2,1,0:T(8,128)(2,1)}, u32[]{:S(2)}, u32[]{:S(2)}) collective-permute-start(bf16[32,32,128]{2,1,0:T(8,128)(2,1)} %collective-permute-done.4.rest_6_), channel_id=1, source_target_pairs={{0,4},{1,5},{2,6},{3,7},{4,0},{5,1},{6,2},{7,3},{8,12},{9,13},{10,... | collective-permute-start | bytes 786440 | tf_op jit(solution)/shard_map/ppermute | solution.py:171
  38.9 14.2 %collective-permute-start.9 = (bf16[32,32,128]{2,1,0:T(8,128)(2,1)}, bf16[32,32,128]{2,1,0:T(8,128)(2,1)}, u32[]{:S(2)}, u32[]{:S(2)}) collective-permute-start(bf16[32,32,128]{2,1,0:T(8,128)(2,1)} %collective-permute-done.5.rest_7_), channel_id=1, source_target_pairs={{0,4},{1,5},{2,6},{3,7},{4,0},{5,1},{6,2},{7,3},{8,12},{9,13},{10,... | collective-permute-start | bytes 786440 | tf_op jit(solution)/shard_map/ppermute | solution.py:171
  38.9 19.7 %collective-permute-start.14 = (bf16[32,32,128]{2,1,0:T(8,128)(2,1)S(1)}, bf16[32,32,128]{2,1,0:T(8,128)(2,1)S(1)}, u32[]{:S(2)}, u32[]{:S(2)}) collective-permute-start(bf16[32,32,128]{2,1,0:T(8,128)(2,1)S(1)} %collective-permute-done.rest_1_), channel_id=1, source_target_pairs={{0,4},{1,5},{2,6},{3,7},{12,8},{13,9},{14,10},{15,11},{16,20},{17,... | collective-permute-start | bytes 786440 | tf_op jit(solution)/shard_map/ppermute | solution.py:171
  42.3 21.9 %collective-permute-start.15 = (bf16[32,32,128]{2,1,0:T(8,128)(2,1)S(1)}, bf16[32,32,128]{2,1,0:T(8,128)(2,1)S(1)}, u32[]{:S(2)}, u32[]{:S(2)}) collective-permute-start(bf16[32,32,128]{2,1,0:T(8,128)(2,1)S(1)} %collective-permute-done.1.rest_2_), channel_id=1, source_target_pairs={{0,4},{1,5},{2,6},{3,7},{12,8},{13,9},{14,10},{15,11},{16,20},{17,... | collective-permute-start | bytes 786440 | tf_op jit(solution)/shard_map/ppermute | solution.py:171
  43.6 26.2 %collective-permute-start.16 = (bf16[32,32,128]{2,1,0:T(8,128)(2,1)S(1)}, bf16[32,32,128]{2,1,0:T(8,128)(2,1)S(1)}, u32[]{:S(2)}, u32[]{:S(2)}) collective-permute-start(bf16[32,32,128]{2,1,0:T(8,128)(2,1)S(1)} %collective-permute-done.2.rest_3_), channel_id=1, source_target_pairs={{0,4},{1,5},{2,6},{3,7},{12,8},{13,9},{14,10},{15,11},{16,20},{17,... | collective-permute-start | bytes 786440 | tf_op jit(solution)/shard_map/ppermute | solution.py:171
  47.4 23.0 %collective-permute-start.18 = (bf16[32,32,128]{2,1,0:T(8,128)(2,1)S(1)}, bf16[32,32,128]{2,1,0:T(8,128)(2,1)S(1)}, u32[]{:S(2)}, u32[]{:S(2)}) collective-permute-start(bf16[32,32,128]{2,1,0:T(8,128)(2,1)S(1)} %collective-permute-done.3.rest_5_), channel_id=1, source_target_pairs={{4,8},{5,9},{6,10},{7,11},{8,4},{9,5},{10,6},{11,7},{20,24},{21,25... | collective-permute-start | bytes 786440 | tf_op jit(solution)/shard_map/ppermute | solution.py:171
  48.1 0.7 copy-start.12
  53.0 18.1 %collective-permute-start.19 = (bf16[32,32,128]{2,1,0:T(8,128)(2,1)}, bf16[32,32,128]{2,1,0:T(8,128)(2,1)S(1)}, u32[]{:S(2)}, u32[]{:S(2)}) collective-permute-start(bf16[32,32,128]{2,1,0:T(8,128)(2,1)} %collective-permute-done.4.rest_6_), channel_id=1, source_target_pairs={{4,8},{5,9},{6,10},{7,11},{8,4},{9,5},{10,6},{11,7},{20,24},{21,25... | collective-permute-start | bytes 786440 | tf_op jit(solution)/shard_map/ppermute | solution.py:171
  58.6 17.0 %collective-permute-start.20 = (bf16[32,32,128]{2,1,0:T(8,128)(2,1)}, bf16[32,32,128]{2,1,0:T(8,128)(2,1)S(1)}, u32[]{:S(2)}, u32[]{:S(2)}) collective-permute-start(bf16[32,32,128]{2,1,0:T(8,128)(2,1)} %collective-permute-done.5.rest_7_), channel_id=1, source_target_pairs={{4,8},{5,9},{6,10},{7,11},{8,4},{9,5},{10,6},{11,7},{20,24},{21,25... | collective-permute-start | bytes 786440 | tf_op jit(solution)/shard_map/ppermute | solution.py:171
  64.2 13.6 %collective-permute-start.21 = (bf16[32,32,128]{2,1,0:T(8,128)(2,1)}, bf16[32,32,128]{2,1,0:T(8,128)(2,1)S(1)}, u32[]{:S(2)}, u32[]{:S(2)}) collective-permute-start(bf16[32,32,128]{2,1,0:T(8,128)(2,1)} %collective-permute-done.6.rest_8_), channel_id=1, source_target_pairs={{4,8},{5,9},{6,10},{7,11},{8,4},{9,5},{10,6},{11,7},{20,24},{21,25... | collective-permute-start | bytes 786440 | tf_op jit(solution)/shard_map/ppermute | solution.py:171
  69.8 8.9 %collective-permute-start.22 = (bf16[32,32,128]{2,1,0:T(8,128)(2,1)}, bf16[32,32,128]{2,1,0:T(8,128)(2,1)S(1)}, u32[]{:S(2)}, u32[]{:S(2)}) collective-permute-start(bf16[32,32,128]{2,1,0:T(8,128)(2,1)} %collective-permute-done.7.rest_9_), channel_id=1, source_target_pairs={{4,8},{5,9},{6,10},{7,11},{8,4},{9,5},{10,6},{11,7},{20,24},{21,25... | collective-permute-start | bytes 786440 | tf_op jit(solution)/shard_map/ppermute | solution.py:171
  70.5 12.4 %collective-permute-start.23 = (bf16[32,32,128]{2,1,0:T(8,128)(2,1)}, bf16[32,32,128]{2,1,0:T(8,128)(2,1)S(1)}, u32[]{:S(2)}, u32[]{:S(2)}) collective-permute-start(bf16[32,32,128]{2,1,0:T(8,128)(2,1)} %collective-permute-done.8.rest_10_), channel_id=1, source_target_pairs={{4,8},{5,9},{6,10},{7,11},{8,4},{9,5},{10,6},{11,7},{20,24},{21,25... | collective-permute-start | bytes 786440 | tf_op jit(solution)/shard_map/ppermute | solution.py:171
  71.2 11.7 %collective-permute-start.24 = (bf16[32,32,128]{2,1,0:T(8,128)(2,1)}, bf16[32,32,128]{2,1,0:T(8,128)(2,1)S(1)}, u32[]{:S(2)}, u32[]{:S(2)}) collective-permute-start(bf16[32,32,128]{2,1,0:T(8,128)(2,1)} %collective-permute-done.9.rest_11_), channel_id=1, source_target_pairs={{4,8},{5,9},{6,10},{7,11},{8,4},{9,5},{10,6},{11,7},{20,24},{21,25... | collective-permute-start | bytes 786440 | tf_op jit(solution)/shard_map/ppermute | solution.py:171
  72.0 1.0 copy-start.13
  75.6 11.3 %collective-permute-start.10 = (bf16[32,32,128]{2,1,0:T(8,128)(2,1)S(1)}, bf16[32,32,128]{2,1,0:T(8,128)(2,1)S(1)}, u32[]{:S(2)}, u32[]{:S(2)}) collective-permute-start(bf16[32,32,128]{2,1,0:T(8,128)(2,1)S(1)} %get-tuple-element.27.rest_0_), channel_id=1, source_target_pairs={{1,0},{3,2},{5,4},{7,6},{8,9},{10,11},{12,13},{14,15},{17,16},{19,... | collective-permute-start | bytes 786440 | tf_op jit(solution)/shard_map/ppermute | solution.py:171
  77.8 15.1 %copy-start.1 = (bf16[32,128,128]{2,1,0:T(8,128)(2,1)S(1)}, bf16[32,128,128]{2,1,0:T(8,128)(2,1)}, u32[]{:S(2)}) copy-start(bf16[32,128,128]{2,1,0:T(8,128)(2,1)} %pair.3) | copy-start | bytes 3145732
  77.8 15.1 %copy-start.15 = (bf16[128,128]{1,0:T(8,128)(2,1)S(1)}, bf16[128,128]{1,0:T(8,128)(2,1)}, u32[]{:S(2)}) copy-start(bf16[128,128]{1,0:T(8,128)(2,1)} %weight.3) | copy-start | bytes 98308
  77.8 15.1 %copy-start.19 = (f32[128]{0:T(128)S(1)}, f32[128]{0:T(128)}, u32[]{:S(2)}) copy-start(f32[128]{0:T(128)} %param.9) | copy-start | bytes 1540
  77.9 9.8 %collective-permute-start.11 = (bf16[32,32,128]{2,1,0:T(8,128)(2,1)S(1)}, bf16[32,32,128]{2,1,0:T(8,128)(2,1)S(1)}, u32[]{:S(2)}, u32[]{:S(2)}) collective-permute-start(bf16[32,32,128]{2,1,0:T(8,128)(2,1)S(1)} %get-tuple-element.28), channel_id=1, source_target_pairs={{0,2},{2,0},{4,6},{6,4},{9,11},{11,9},{13,15},{15,13},{16,18},{18,... | collective-permute-start | bytes 786440 | tf_op jit(solution)/shard_map/ppermute | solution.py:171
  78.7 10.2 %collective-permute-start.12 = (bf16[32,32,128]{2,1,0:T(8,128)(2,1)S(1)}, bf16[32,32,128]{2,1,0:T(8,128)(2,1)S(1)}, u32[]{:S(2)}, u32[]{:S(2)}) collective-permute-start(bf16[32,32,128]{2,1,0:T(8,128)(2,1)S(1)} %get-tuple-element.28), channel_id=1, source_target_pairs={{1,2},{3,0},{5,6},{7,4},{8,11},{10,9},{12,15},{14,13},{17,18},{19,... | collective-permute-start | bytes 786440 | tf_op jit(solution)/shard_map/ppermute | solution.py:171
  85.4 10.4 %copy-start.6 = (bf16[32,32,128]{2,1,0:T(8,128)(2,1)}, bf16[32,32,128]{2,1,0:T(8,128)(2,1)S(1)}, u32[]{:S(2)}) copy-start(bf16[32,32,128]{2,1,0:T(8,128)(2,1)S(1)} %get-tuple-element.29.rest_4_) | copy-start | bytes 786436
  85.4 10.4 %copy-start.20 = (f32[128]{0:T(128)S(1)}, f32[128]{0:T(128)}, u32[]{:S(2)}) copy-start(f32[128]{0:T(128)} %param.12) | copy-start | bytes 1540
  85.4 30.2 %copy-start.16 = (bf16[128,128]{1,0:T(8,128)(2,1)S(1)}, bf16[128,128]{1,0:T(8,128)(2,1)}, u32[]{:S(2)}) copy-start(bf16[128,128]{1,0:T(8,128)(2,1)} %weight.5) | copy-start | bytes 98308
  85.4 4.8 %collective-permute-start.25 = (bf16[32,32,128]{2,1,0:T(8,128)(2,1)S(1)}, bf16[32,32,128]{2,1,0:T(8,128)(2,1)S(1)}, u32[]{:S(2)}, u32[]{:S(2)}) collective-permute-start(bf16[32,32,128]{2,1,0:T(8,128)(2,1)S(1)} %get-tuple-element.29.rest_4_), channel_id=1, source_target_pairs={{4,5},{6,7},{9,8},{11,10},{20,21},{22,23},{25,24},{27,26}} | collective-permute-start | bytes 786440 | tf_op jit(solution)/shard_map/ppermute | solution.py:171
  86.2 5.3 %collective-permute-start.26 = (bf16[32,32,128]{2,1,0:T(8,128)(2,1)}, bf16[32,32,128]{2,1,0:T(8,128)(2,1)S(1)}, u32[]{:S(2)}, u32[]{:S(2)}) collective-permute-start(bf16[32,32,128]{2,1,0:T(8,128)(2,1)} %get-tuple-element.30), channel_id=1, source_target_pairs={{5,7},{7,5},{8,10},{10,8},{21,23},{23,21},{24,26},{26,24}} | collective-permute-start | bytes 786440 | tf_op jit(solution)/shard_map/ppermute | solution.py:171
  86.9 9.1 %collective-permute-start.27 = (bf16[32,32,128]{2,1,0:T(8,128)(2,1)}, bf16[32,32,128]{2,1,0:T(8,128)(2,1)S(1)}, u32[]{:S(2)}, u32[]{:S(2)}) collective-permute-start(bf16[32,32,128]{2,1,0:T(8,128)(2,1)} %get-tuple-element.30), channel_id=1, source_target_pairs={{4,7},{6,5},{9,10},{11,8},{20,23},{22,21},{25,26},{27,24}} | collective-permute-start | bytes 786440 | tf_op jit(solution)/shard_map/ppermute | solution.py:171
  87.6 8.2 %copy-start.2 = (bf16[32,32,128]{2,1,0:T(8,128)(2,1)}, bf16[32,32,128]{2,1,0:T(8,128)(2,1)S(1)}, u32[]{:S(2)}) copy-start(bf16[32,32,128]{2,1,0:T(8,128)(2,1)S(1)} %collective-permute-done.11.rest_2_) | copy-start | bytes 786436
  87.6 19.1 %collective-permute-start.28 = (bf16[32,32,128]{2,1,0:T(8,128)(2,1)}, bf16[32,32,128]{2,1,0:T(8,128)(2,1)}, u32[]{:S(2)}, u32[]{:S(2)}) collective-permute-start(bf16[32,32,128]{2,1,0:T(8,128)(2,1)} %get-tuple-element.31), channel_id=1, source_target_pairs={{5,1},{7,3},{8,12},{10,14},{21,17},{23,19},{24,28},{26,30}} | collective-permute-start | bytes 786440 | tf_op jit(solution)/shard_map/ppermute | solution.py:171
  88.9 6.9 %copy-start.4 = (bf16[32,32,128]{2,1,0:T(8,128)(2,1)}, bf16[32,32,128]{2,1,0:T(8,128)(2,1)S(1)}, u32[]{:S(2)}) copy-start(bf16[32,32,128]{2,1,0:T(8,128)(2,1)S(1)} %collective-permute-done.12.rest_3_) | copy-start | bytes 786436
  88.9 22.9 %collective-permute-start.29 = (bf16[32,32,128]{2,1,0:T(8,128)(2,1)}, bf16[32,32,128]{2,1,0:T(8,128)(2,1)}, u32[]{:S(2)}, u32[]{:S(2)}) collective-permute-start(bf16[32,32,128]{2,1,0:T(8,128)(2,1)} %get-tuple-element.31), channel_id=1, source_target_pairs={{4,1},{6,3},{9,12},{11,14},{20,17},{22,19},{25,28},{27,30}} | collective-permute-start | bytes 786440 | tf_op jit(solution)/shard_map/ppermute | solution.py:171
  90.3 22.2 %collective-permute-start.30 = (bf16[32,32,128]{2,1,0:T(8,128)(2,1)}, bf16[32,32,128]{2,1,0:T(8,128)(2,1)}, u32[]{:S(2)}, u32[]{:S(2)}) collective-permute-start(bf16[32,32,128]{2,1,0:T(8,128)(2,1)} %get-tuple-element.32), channel_id=1, source_target_pairs={{5,3},{7,1},{8,14},{10,12},{21,19},{23,17},{24,30},{26,28}} | collective-permute-start | bytes 786440 | tf_op jit(solution)/shard_map/ppermute | solution.py:171
  91.6 4.3 %copy-start.8 = (bf16[32,32,128]{2,1,0:T(8,128)(2,1)}, bf16[32,32,128]{2,1,0:T(8,128)(2,1)S(1)}, u32[]{:S(2)}) copy-start(bf16[32,32,128]{2,1,0:T(8,128)(2,1)S(1)} %collective-permute-done.26.rest_6_) | copy-start | bytes 786436
  91.6 24.1 %collective-permute-start.31 = (bf16[32,32,128]{2,1,0:T(8,128)(2,1)}, bf16[32,32,128]{2,1,0:T(8,128)(2,1)}, u32[]{:S(2)}, u32[]{:S(2)}) collective-permute-start(bf16[32,32,128]{2,1,0:T(8,128)(2,1)} %get-tuple-element.32), channel_id=1, source_target_pairs={{4,3},{6,1},{9,14},{11,12},{20,19},{22,17},{25,30},{27,28}} | collective-permute-start | bytes 786440 | tf_op jit(solution)/shard_map/ppermute | solution.py:171
  96.0 0.7 copy-start.10
  115.6 1.0 copy-start.3
  116.6 0.9 copy-start.5
  117.5 0.9 copy-start.7
  118.5 0.9 copy-start.9
  119.4 0.9 copy-start.11

commit v2 on v0

v2 whole, which is shorter than its diff:
```python
import functools

import jax
import jax.numpy as jnp
from jax import lax
from jax.experimental import pallas as pl
from jax.experimental.pallas import tpu as pltpu
from jax.sharding import PartitionSpec as P

F32, BF16 = jnp.float32, jnp.bfloat16
LANES = 128
LIMIT = 40 * 1024 * 1024
NT = (((1,), (1,)), ((), ()))
TN = (((0,), (0,)), ((), ()))
SMEM = pl.BlockSpec(memory_space=pltpu.SMEM)
VMEM = pl.BlockSpec(memory_space=pltpu.VMEM)
PARAMS = pltpu.CompilerParams(vmem_limit_bytes=LIMIT)


def normalise(x, gain):
    mean = jnp.mean(x, axis=-1, keepdims=True)
    centered = x - mean
    var = jnp.mean(centered * centered, axis=-1, keepdims=True)
    return (centered * lax.rsqrt(var + 1e-05) * gain).astype(BF16)


def operands_kernel(merge, where, pair, mask, gain, weight, *rest):
    before = rest[:4] if merge else ()
    rest = rest[len(before) :]
    outs, held, turned, chosen = rest[:4], rest[4:6], rest[6], rest[7]
    rows, toks, _ = pair.shape
    hidden = weight.shape[1] // 4
    part = hidden // 4
    pitch = rows + 1
    turned[...] = weight[...].T
    for n in range(4):
        for p in range(2):
            start = pl.multiple_of(n * hidden + (where[0] ^ (2 * p)) * part, part)
            half = 0.5 if n % 2 == 0 else 1.0
            chosen[(2 * n + p) * part : (2 * n + p + 1) * part, :] = turned[pl.ds(start, part), :] * half
    group = 4

    @pl.loop(0, rows // group)
    def _(at):
        first = at * group
        x = pair[pl.ds(first, group)].astype(F32).reshape(group * toks, -1)
        normed = normalise(x, gain[...])
        proj = lax.dot_general(chosen[...], normed, NT, preferred_element_type=F32)
        for g in range(group):
            valid = mask[pl.ds(first + g, 1), :].astype(F32) * 0.5
            mine = proj[:, g * toks : (g + 1) * toks]
            blocks = [mine[n * 2 * part : (n + 1) * 2 * part] for n in range(4)]
            spot = pl.ds(first + g, 2 * part, stride=pitch)
            for n in range(2):
                value = (jnp.tanh(blocks[2 * n]) + 1.0) * (valid * blocks[2 * n + 1])
                for m in range(toks // LANES):
                    held[n][m, spot, :] = value[:, m * LANES : (m + 1) * LANES]

    base = toks if merge else 0
    for n in range(2):
        for p in range(2):
            out = outs[2 * n + p]
            if merge:
                out[:, :, :toks] = before[2 * n + p][...]
            for m in range(toks // LANES):
                lanes = slice(base + m * LANES, base + (m + 1) * LANES)
                for c in range(part):
                    row = (p * part + c) * pitch
                    out[c, :, lanes] = held[n][m, row : row + rows, :].astype(BF16)


def gate_kernel(pair, gain, weight, out):
    rows, toks, _ = pair.shape
    group = 4

    @pl.loop(0, rows // group)
    def _(at):
        spot = pl.ds(at * group, group)
        x = pair[spot].astype(F32).reshape(group * toks, -1)
        logits = jnp.dot(normalise(x, gain[...]), weight[...], preferred_element_type=F32)
        out[spot] = (0.5 * jnp.tanh(0.5 * logits) + 0.5).reshape(group, toks, -1)


def product_kernel(n_left, n_right, places, *rest):
    lefts = [rest[2 * n : 2 * n + 2] for n in range(n_left)]
    rest = rest[2 * n_left :]
    rights = [rest[2 * n : 2 * n + 2] for n in range(n_right)]
    rest = rest[2 * n_right :]
    outs, held = rest[: 2 * n_left], rest[2 * n_left]
    part, rows, _ = outs[0].shape
    for s in range(n_right):
        for p in range(2):
            start = places[1 + s] * (2 * rows) + (places[0] ^ p) * rows
            held[:, pl.ds(pl.multiple_of(start, rows), rows), :] = rights[s][p][...]
    for c in range(part):
        left = jnp.concatenate([x[c] for side in lefts for x in side], axis=0)
        out = lax.dot_general(left, held[c], NT, preferred_element_type=F32).astype(BF16)
        for n in range(2 * n_left):
            outs[n][c] = out[n * rows : (n + 1) * rows]


def hand_out_kernel(where, near0, near1, far0, far1, end0, end1, *outs):
    near, far, end = (near0, near1), (far0, far1), (end0, end1)
    for r in range(4):
        source = where[2] ^ (r % 2)

        @pl.when(source == 0)
        def _():
            outs[r][...] = near[r // 2][...]

        @pl.when((source == 1) & (where[1] == 0))
        def _():
            outs[r][...] = far[r // 2][...]

        @pl.when((source == 1) & (where[1] == 1))
        def _():
            outs[r][...] = end[r // 2][...]


def update_kernel(where, gain, weight, gate, *rest):
    pieces, out, turned = rest[:-2], rest[-2], rest[-1]
    part = sum(x.shape[0] for x in pieces[::4])
    _, rows, toks = pieces[0].shape
    hidden = 4 * part
    pitch = hidden + 1
    for r in range(4):
        base = (where[0] ^ r) * part
        for piece in pieces[r::4]:
            for c in range(piece.shape[0]):
                value = piece[c].astype(F32)
                for m in range(toks // LANES):
                    turned[m, pl.ds(base + c, rows, stride=pitch), :] = value[
                        :, m * LANES : (m + 1) * LANES
                    ]
            base = base + piece.shape[0]
    scale = jnp.broadcast_to(gain[...], (hidden, toks))

    @pl.loop(0, rows, unroll=8)
    def _(i):
        x = jnp.concatenate(
            [turned[m, pl.ds(i * pitch, hidden), :] for m in range(toks // LANES)], axis=1
        )
        mean = jnp.mean(x, axis=0, keepdims=True)
        centered = x - mean
        var = jnp.mean(centered * centered, axis=0, keepdims=True)
        pnorm = (centered * lax.rsqrt(var + 1e-05) * scale).astype(BF16)
        mapped = lax.dot_general(pnorm, weight[...], TN, preferred_element_type=F32)
        out[i] = (gate[i] * mapped).astype(BF16)


def local(pair, pair_mask, in_gain, proj_weight, gate_weight, out_gain, out_weight, *, n_row):
    rows, toks, channels = pair.shape
    hidden = proj_weight.shape[1] // 4
    part = hidden // 4
    planes = n_row // 2
    half = planes // 2
    row, core = lax.axis_index("row"), lax.axis_index("chan")
    z, y = row // 2, row % 2
    own_half = z // half
    at_end = (z == 0) | (z == planes - 1)
    where = jnp.stack([2 * y + core, at_end, core ^ own_half]).astype(jnp.int32)

    def send(x, target):
        pairs = []
        for source in range(2 * n_row):
            to = target(source // 4, source // 2 % 2, source % 2)
            pairs.append((source, 4 * to[0] + 2 * to[1] + to[2]))
        return lax.ppermute(x, ("row", "chan"), pairs)

    def after(x, *earlier):
        return lax.optimization_barrier((x, *earlier))[0]

    def in_plane(r):
        return lambda p, b, k: (p, b ^ (r // 2), k ^ (r % 2))

    def shifted(s):
        return lambda p, b, k: (p // half * half + (p + s) % half, b, k)

    def mirrored(p, b, k):
        return (p if p in (0, planes - 1) else planes - 1 - p, b, k)

    def edge(p, b, k):
        swap = {0: 1, 1: 0, planes - 1: planes - 2, planes - 2: planes - 1}
        return (swap.get(p, p), b, k)

    gains = in_gain.reshape(1, -1)
    twin, twin_mask = send(pair, in_plane(1)), send(pair_mask, in_plane(1))

    def operands(x, mask, before):
        depth = toks * (2 if before else 1)
        return pl.pallas_call(
            functools.partial(operands_kernel, bool(before)),
            out_shape=[jax.ShapeDtypeStruct((part, rows, depth), BF16)] * 4,
            in_specs=[SMEM] + [VMEM] * (4 + len(before)),
            out_specs=[VMEM] * 4,
            scratch_shapes=[pltpu.VMEM((toks // LANES, 2 * part * (rows + 1), LANES), F32)] * 2
            + [pltpu.VMEM((4 * hidden, channels), BF16), pltpu.VMEM((8 * part, channels), BF16)],
            compiler_params=PARAMS,
            name="operands_b" if before else "operands_a",
        )(where, x, mask, gains, proj_weight, *before)

    mine = operands(pair, pair_mask, [])
    left0, left1, right0, right1 = operands(twin, twin_mask, mine)

    shifts = range(1, half)
    near0 = [right0] + [send(right0, shifted(s)) for s in shifts]
    right1 = send(right1, in_plane(2))
    far0 = [send(right0, mirrored)]
    left1 = send(after(left1, right1), in_plane(2))
    far0 += [send(x, mirrored) for x in near0[1:]]
    outer0 = send(after(left0, near0[-1]), edge)
    near1 = [right1] + [send(right1, shifted(s)) for s in shifts]
    far1 = [send(x, mirrored) for x in near1]
    outer1 = send(left1, edge)

    gate = pl.pallas_call(
        gate_kernel,
        out_shape=jax.ShapeDtypeStruct((rows, toks, channels), F32),
        in_specs=[VMEM] * 3,
        out_specs=VMEM,
        compiler_params=PARAMS,
        name="gate",
    )(pair, gains, gate_weight)

    def products(lefts, rights, places, name):
        span = 2 * rows * len(rights)
        return pl.pallas_call(
            functools.partial(product_kernel, len(lefts), len(rights)),
            out_shape=[jax.ShapeDtypeStruct((part, rows, span), BF16)] * (2 * len(lefts)),
            in_specs=[SMEM] + [VMEM] * (2 * (len(lefts) + len(rights))),
            out_specs=[VMEM] * (2 * len(lefts)),
            scratch_shapes=[pltpu.VMEM((part, span, 2 * toks), BF16)],
            compiler_params=PARAMS,
            name=name,
        )(places, *[x for side in (*lefts, *rights) for x in side])

    steps = jnp.arange(half)
    inner = z % half
    far_inner = (planes - 1 - z) % half
    places_near = jnp.concatenate([y[None], (inner - steps) % half]).astype(jnp.int32)
    places_far = jnp.concatenate([y[None], (far_inner - steps) % half]).astype(jnp.int32)
    near = products([(left0, left1)], list(zip(near0, near1)), places_near, "near")
    away = products(
        [(after(left0, near[0], gate), left1), (outer0, outer1)], list(zip(far0, far1)), places_far, "away"
    )
    ends = [send(x, edge) for x in away[2:]]
    handed = pl.pallas_call(
        hand_out_kernel,
        out_shape=[jax.ShapeDtypeStruct((part, rows, toks), BF16)] * 4,
        in_specs=[SMEM] + [VMEM] * 6,
        out_specs=[VMEM] * 4,
        compiler_params=PARAMS,
        name="hand_out",
    )(where, *near, *away[:2], *ends)
    pieces = [handed[0]] + [send(handed[r], in_plane(r)) for r in range(1, 4)]

    return pl.pallas_call(
        update_kernel,
        out_shape=jax.ShapeDtypeStruct((rows, toks, channels), BF16),
        in_specs=[SMEM] + [VMEM] * (3 + len(pieces)),
        out_specs=VMEM,
        scratch_shapes=[pltpu.VMEM((toks // LANES, rows * (hidden + 1), LANES), F32)],
        compiler_params=PARAMS,
        name="update",
    )(where, out_gain.reshape(-1, 1), out_weight, gate, *pieces)


def solution(mesh):
    placed = (
        P(("groups", "row"), "chan", None),
        P(("groups", "row"), "chan"),
        P(),
        P(),
        P(),
        P(),
        P(),
    )
    return jax.shard_map(
        functools.partial(local, n_row=mesh.shape["row"]),
        mesh=mesh,
        in_specs=placed,
        out_specs=P(("groups", "row"), "chan", None),
        check_vma=False,
    )
```

time: 128 us -> 104 us (0.81)
  waiting for transfers between devices: 71.4 us -> 39.9 us
  Pallas kernels: 0 us -> 22.2 us
  starting transfers between devices: 20.9 us -> 33 us
  blocking collectives: 9.14 us -> 0 us
  matrix products: 7.49 us -> 0 us
  other arithmetic: 6.48 us -> 0.25 us
  local copies, waits for them, and re-layouts: 10.2 us -> 7.18 us
    all_to_all x4 -> x0, waiting for transfers between devices: 71.4 us -> none  [the longest x1 24 us: local(): lax.all_to_all(right, 'row', split_axis=0, concat_axis=1, tiled=True)]
    ppermute x0 -> x17, waiting for transfers between devices: none -> 39.9 us  [send(): return lax.ppermute(x, ('row', 'chan'), pairs)]
    ppermute x0 -> x17, starting transfers between devices: none -> 33 us  [send(): return lax.ppermute(x, ('row', 'chan'), pairs)]
    pallas_call x0 -> x7, Pallas kernels: none -> 22.2 us  [the longest x2 9.23 us: operands(): pl.pallas_call(functools.partial(operands_kernel, bool(before)), out_shap...]
    all_to_all x4 -> x0, starting transfers between devices: 20.9 us -> none  [the longest x1 6.38 us: local(): lax.all_to_all(left, 'row', split_axis=0, concat_axis=1, tiled=True)]
    all_to_all x2 -> x0, blocking collectives: 9.14 us -> none  [the longest x1 4.58 us: local(): lax.all_to_all(product, 'chan', split_axis=2, concat_axis=0, tiled=True)]
    dot_general x4 -> x0, matrix products: 7.49 us -> none  [the longest x1 2.55 us: local(): jnp.einsum('ijc,cf->ijf', normed, gate_weight, preferred_element_type=jnp...]
    unnamed x16 -> x28, local copies, waits for them, and re-layouts: 1.71 us -> 7.07 us
  transfers between devices with their start and end apart: 4 -> 17, of which waited for: 4 -> 6; matrix products, arithmetic and copies ran while one was open for 4% -> 0% of each run, Pallas kernels for 0% -> 10%
where the time goes in v2:
time: 104 us; the launch traced here: 103 us
  waiting for transfers between devices  39.9 us (38%)
  starting transfers between devices  33 us (32%)
  Pallas kernels  22.2 us (21%)
  local copies, waits for them, and re-layouts  7.18 us (7%)
    ppermute x17, waiting for transfers between devices, send(): return lax.ppermute(x, ('row', 'chan'), pairs)  39.9 us
    ppermute x17, starting transfers between devices, send(): return lax.ppermute(x, ('row', 'chan'), pairs)  33 us
    pallas_call x2, Pallas kernels, operands(): pl.pallas_call(functools.partial(operands_kernel, bool(before)), out_shap...  9.23 us
    unnamed x28, local copies, waits for them, and re-layouts  7.07 us
    pallas_call x2, Pallas kernels, products(): pl.pallas_call(functools.partial(product_kernel, len(lefts), len(rights))...  5.5 us
    pallas_call x1, Pallas kernels, local(): pl.pallas_call(update_kernel, out_shape=jax.ShapeDtypeStruct((rows, toks,...  3.06 us
    pallas_call x1, Pallas kernels, local(): pl.pallas_call(gate_kernel, out_shape=jax.ShapeDtypeStruct((rows, toks, c...  2.9 us
  transfers between devices with their start and end apart: 17, of which 6 were waited for; matrix products, arithmetic and copies ran while one was open for 0% of the time, Pallas kernels for 10%

profile of v2, /device:TPU:1, one launch (start us, length us, event | category | flops | bytes accessed | tf_op | source)
XLA Modules:
  0.0 102.7 jit_solution(7886163587093593215)
XLA Ops:
  0.0 0.1 collective-permute-start
  0.1 0.5 collective-permute-start.1
  0.5 0.1 pad_add_fusion.where
  0.6 1.2 %copy-done = bf16[32,128,128]{2,1,0:T(8,128)(2,1)S(1)} copy-done((bf16[32,128,128]{2,1,0:T(8,128)(2,1)S(1)}, bf16[32,128,128]{2,1,0:T(8,128)(2,1)}, u32[]{:S(2)}) %copy-start) | copy-done | bytes 1048600
  1.8 0.9 copy-done.6
  2.7 0.7 copy-done.10
  3.4 0.7 copy-done.11
  4.1 4.2 %operands_a.1 = (bf16[32,32,128]{2,1,0:T(8,128)(2,1)S(1)}, bf16[32,32,128]{2,1,0:T(8,128)(2,1)S(1)}, bf16[32,32,128]{2,1,0:T(8,128)(2,1)S(1)}, bf16[32,32,128]{2,1,0:T(8,128)(2,1)S(1)}) custom-call(s32[3]{0:T(128)S(1)} %pad_add_fusion.where, bf16[32,128,128]{2,1,0:T(8,128)(2,1)S(1)} %copy-done, s32[32,128]{1,0:T(8,128)S(1)} %copy-done.10, ...), custom_call_target="tpu_custom_call" | custom-call | tf_op jit(solution)/shard_map/operands_a/pallas_call | solution.py:191
  8.3 0.0 collective-permute-done.1.mask
  8.3 0.0 collective-permute-done.pair
  8.3 0.0 copy-start.7
  8.3 0.9 copy-done.7
  9.2 5.0 %operands_b.1 = (bf16[32,32,256]{2,1,0:T(8,128)(2,1)}, bf16[32,32,256]{2,1,0:T(8,128)(2,1)S(1)}, bf16[32,32,256]{2,1,0:T(8,128)(2,1)S(1)}, bf16[32,32,256]{2,1,0:T(8,128)(2,1)S(1)}) custom-call(s32[3]{0:T(128)S(1)} %pad_add_fusion.where, bf16[32,128,128]{2,1,0:T(8,128)(2,1)S(1)} %collective-permute-done.pair, s32[32,128]{1,0:T(8,128)S(1)} %collective-permute-done.1.mask, ...), custom_call_target="tpu_custom_call" | custom-call | tf_op jit(solution)/shard_map/operands_b/pallas_call | solution.py:191
  14.3 2.3 %collective-permute-start.2 = (bf16[32,32,256]{2,1,0:T(8,128)(2,1)S(1)}, bf16[32,32,256]{2,1,0:T(8,128)(2,1)}, u32[]{:S(2)}, u32[]{:S(2)}) collective-permute-start(bf16[32,32,256]{2,1,0:T(8,128)(2,1)S(1)} %get-tuple-element.32), channel_id=1, source_target_pairs={{0,2},{1,3},{2,0},{3,1},{4,6},{5,7},{6,4},{7,5},{8,10},{9,11},{10,... | collective-permute-start | bytes 1572872 | tf_op jit(solution)/shard_map/ppermute | solution.py:168
  16.6 1.3 %collective-permute-start.4 = (bf16[32,32,256]{2,1,0:T(8,128)(2,1)S(1)}, bf16[32,32,256]{2,1,0:T(8,128)(2,1)}, u32[]{:S(2)}, u32[]{:S(2)}) collective-permute-start(bf16[32,32,256]{2,1,0:T(8,128)(2,1)S(1)} %get-tuple-element.34.rest_2_), channel_id=1, source_target_pairs={{0,4},{1,5},{2,6},{3,7},{4,0},{5,1},{6,2},{7,3},{8,12},{9,13},{10,... | collective-permute-start | bytes 1572872 | tf_op jit(solution)/shard_map/ppermute | solution.py:168
  17.9 0.7 collective-permute-start.8
  18.6 0.0 copy-start.4
  18.6 0.8 copy-done.4
  19.4 9.2 %collective-permute-done.2.rest_3_ = bf16[32,32,256]{2,1,0:T(8,128)(2,1)} collective-permute-done((bf16[32,32,256]{2,1,0:T(8,128)(2,1)S(1)}, bf16[32,32,256]{2,1,0:T(8,128)(2,1)}, u32[]{:S(2)}, u32[]{:S(2)}) %collective-permute-start.2) | collective-permute-done | bytes 524320 | tf_op jit(solution)/shard_map/ppermute | solution.py:168
  28.6 1.1 %collective-permute-start.3 = (bf16[32,32,256]{2,1,0:T(8,128)(2,1)S(1)}, bf16[32,32,256]{2,1,0:T(8,128)(2,1)}, u32[]{:S(2)}, u32[]{:S(2)}) collective-permute-start(bf16[32,32,256]{2,1,0:T(8,128)(2,1)S(1)} %get-tuple-element.33), channel_id=1, source_target_pairs={{0,2},{1,3},{2,0},{3,1},{4,6},{5,7},{6,4},{7,5},{8,10},{9,11},{10,... | collective-permute-start | bytes 1572872 | tf_op jit(solution)/shard_map/ppermute | solution.py:168
  29.7 1.3 %collective-permute-start.5 = (bf16[32,32,256]{2,1,0:T(8,128)(2,1)}, bf16[32,32,256]{2,1,0:T(8,128)(2,1)}, u32[]{:S(2)}, u32[]{:S(2)}) collective-permute-start(bf16[32,32,256]{2,1,0:T(8,128)(2,1)} %collective-permute-done.2.rest_3_), channel_id=1, source_target_pairs={{0,4},{1,5},{2,6},{3,7},{4,0},{5,1},{6,2},{7,3},{8,12},{9,13},{10,... | collective-permute-start | bytes 1572872 | tf_op jit(solution)/shard_map/ppermute | solution.py:168
  31.0 0.0 collective-permute-done.4.rest_4_
  31.0 0.2 collective-permute-start.6
  31.2 5.3 %collective-permute-start.10 = (bf16[32,32,256]{2,1,0:T(8,128)(2,1)}, bf16[32,32,256]{2,1,0:T(8,128)(2,1)}, u32[]{:S(2)}, u32[]{:S(2)}) collective-permute-start(bf16[32,32,256]{2,1,0:T(8,128)(2,1)} %collective-permute-done.4.rest_4_), channel_id=1, source_target_pairs={{0,0},{1,1},{2,2},{3,3},{4,8},{5,9},{6,10},{7,11},{8,4},{9,5},{10,... | collective-permute-start | bytes 1572872 | tf_op jit(solution)/shard_map/ppermute | solution.py:168
  36.6 0.0 collective-permute-done.8.rest_4_
  36.6 0.8 copy-done.2
  37.3 5.4 %collective-permute-start.9 = (bf16[32,32,256]{2,1,0:T(8,128)(2,1)}, bf16[32,32,256]{2,1,0:T(8,128)(2,1)}, u32[]{:S(2)}, u32[]{:S(2)}) collective-permute-start(bf16[32,32,256]{2,1,0:T(8,128)(2,1)} %collective-permute-done.2.rest_3_), channel_id=1, source_target_pairs={{0,0},{1,1},{2,2},{3,3},{4,8},{5,9},{6,10},{7,11},{8,4},{9,5},{10,... | collective-permute-start | bytes 1572872 | tf_op jit(solution)/shard_map/ppermute | solution.py:168
  42.7 0.0 collective-permute-done.3.rest_1_
  42.7 0.0 collective-permute-start.7
  42.7 0.0 collective-permute-done.5.rest_5_
  42.7 5.4 %collective-permute-start.11 = (bf16[32,32,256]{2,1,0:T(8,128)(2,1)}, bf16[32,32,256]{2,1,0:T(8,128)(2,1)}, u32[]{:S(2)}, u32[]{:S(2)}) collective-permute-start(bf16[32,32,256]{2,1,0:T(8,128)(2,1)} %collective-permute-done.5.rest_5_), channel_id=1, source_target_pairs={{0,0},{1,1},{2,2},{3,3},{4,8},{5,9},{6,10},{7,11},{8,4},{9,5},{10,... | collective-permute-start | bytes 1572872 | tf_op jit(solution)/shard_map/ppermute | solution.py:168
  48.1 0.0 copy-done.12
  48.1 0.0 copy-done.8
  48.1 0.0 copy-done.1
  48.1 2.9 %gate.1 = f32[32,128,128]{2,1,0:T(8,128)S(1)} custom-call(bf16[32,128,128]{2,1,0:T(8,128)(2,1)S(1)} %copy-done.1, f32[1,128]{1,0:T(1,128)S(1)} %bitcast.8, bf16[128,128]{1,0:T(8,128)(2,1)S(1)} %copy-done.8), custom_call_target="tpu_custom_call" | custom-call | tf_op jit(solution)/shard_map/gate/pallas_call | solution.py:216
  51.0 0.0 copy-start.3
  51.1 0.1 pad_add_fusion.1.places
  51.1 0.1 pad_add_fusion.2.places
  51.2 1.0 %copy-done.5 = bf16[32,32,256]{2,1,0:T(8,128)(2,1)S(1)} copy-done((bf16[32,32,256]{2,1,0:T(8,128)(2,1)S(1)}, bf16[32,32,256]{2,1,0:T(8,128)(2,1)}, u32[]{:S(2)}) %copy-start.5) | copy-done | bytes 524312
  52.2 2.7 %near.1 = (bf16[32,32,128]{2,1,0:T(8,128)(2,1)S(1)}, bf16[32,32,128]{2,1,0:T(8,128)(2,1)S(1)}) custom-call(s32[3]{0:T(128)S(1)} %pad_add_fusion.1.places, bf16[32,32,256]{2,1,0:T(8,128)(2,1)} %get-tuple-element.38.rest_0_, bf16[32,32,256]{2,1,0:T(8,128)(2,1)} %collective-permute-done.3.rest_1_, bf16[32,32,256]{2,1,0:T(8,128)(2,1)S(1)} %copy-done.5, ...), custom_call_target="tpu_custom_call" | custom-call | tf_op jit(solution)/shard_map/near/pallas_call | solution.py:227
  54.9 0.0 copy-start.13
  54.9 0.0 copy-start.9
  54.9 0.0 collective-permute-done.6.rest_2_
  54.9 0.0 collective-permute-done.10.rest_6_
  55.0 0.0 collective-permute-done.9.rest_5_
  55.0 9.4 %collective-permute-done.7.rest_3_ = bf16[32,32,256]{2,1,0:T(8,128)(2,1)} collective-permute-done((bf16[32,32,256]{2,1,0:T(8,128)(2,1)}, bf16[32,32,256]{2,1,0:T(8,128)(2,1)}, u32[]{:S(2)}, u32[]{:S(2)}) %collective-permute-start.7) | collective-permute-done | bytes 524320 | tf_op jit(solution)/shard_map/ppermute | solution.py:168
  64.4 0.0 collective-permute-done.11.rest_7_
  64.4 0.0 copy-done.3
  64.4 2.8 %away.1 = (bf16[32,32,128]{2,1,0:T(8,128)(2,1)S(1)}, bf16[32,32,128]{2,1,0:T(8,128)(2,1)S(1)}, bf16[32,32,128]{2,1,0:T(8,128)(2,1)S(1)}, bf16[32,32,128]{2,1,0:T(8,128)(2,1)S(1)}) custom-call(s32[3]{0:T(128)S(1)} %pad_add_fusion.2.places, bf16[32,32,256]{2,1,0:T(8,128)(2,1)} %get-tuple-element.38.rest_0_, ...), custom_call_target="tpu_custom_call" | custom-call | tf_op jit(solution)/shard_map/away/pallas_call | solution.py:227
  67.2 4.1 %collective-permute-start.12 = (bf16[32,32,128]{2,1,0:T(8,128)(2,1)S(1)}, bf16[32,32,128]{2,1,0:T(8,128)(2,1)S(1)}, u32[]{:S(2)}, u32[]{:S(2)}) collective-permute-start(bf16[32,32,128]{2,1,0:T(8,128)(2,1)S(1)} %get-tuple-element.41), channel_id=1, source_target_pairs={{0,4},{1,5},{2,6},{3,7},{4,0},{5,1},{6,2},{7,3},{8,12},{9,13},{10,... | collective-permute-start | bytes 786440 | tf_op jit(solution)/shard_map/ppermute | solution.py:168
  71.4 0.1 collective-permute-start.13
  71.5 3.7 %collective-permute-done.12.end0 = bf16[32,32,128]{2,1,0:T(8,128)(2,1)S(1)} collective-permute-done((bf16[32,32,128]{2,1,0:T(8,128)(2,1)S(1)}, bf16[32,32,128]{2,1,0:T(8,128)(2,1)S(1)}, u32[]{:S(2)}, u32[]{:S(2)}) %collective-permute-start.12) | collective-permute-done | bytes 262176 | tf_op jit(solution)/shard_map/ppermute | solution.py:168
  75.2 5.4 %collective-permute-done.13.end1 = bf16[32,32,128]{2,1,0:T(8,128)(2,1)S(1)} collective-permute-done((bf16[32,32,128]{2,1,0:T(8,128)(2,1)S(1)}, bf16[32,32,128]{2,1,0:T(8,128)(2,1)S(1)}, u32[]{:S(2)}, u32[]{:S(2)}) %collective-permute-start.13) | collective-permute-done | bytes 262176 | tf_op jit(solution)/shard_map/ppermute | solution.py:168
  80.6 1.5 %hand_out.1 = (bf16[32,32,128]{2,1,0:T(8,128)(2,1)S(1)}, bf16[32,32,128]{2,1,0:T(8,128)(2,1)}, bf16[32,32,128]{2,1,0:T(8,128)(2,1)}, bf16[32,32,128]{2,1,0:T(8,128)(2,1)S(1)}) custom-call(s32[3]{0:T(128)S(1)} %pad_add_fusion.where, bf16[32,32,128]{2,1,0:T(8,128)(2,1)S(1)} %get-tuple-element.35.near0, bf16[32,32,128]{2,1,0:T(8,128)(2,1)S(1)} %get-tuple-element.36.near1, ...), custom_call_target="tpu_custom_call" | custom-call | tf_op jit(solution)/shard_map/hand_out/pallas_call | solution.py:247
  82.1 3.7 %collective-permute-start.14 = (bf16[32,32,128]{2,1,0:T(8,128)(2,1)}, bf16[32,32,128]{2,1,0:T(8,128)(2,1)S(1)}, u32[]{:S(2)}, u32[]{:S(2)}) collective-permute-start(bf16[32,32,128]{2,1,0:T(8,128)(2,1)} %get-tuple-element.44), channel_id=1, source_target_pairs={{0,1},{1,0},{2,3},{3,2},{4,5},{5,4},{6,7},{7,6},{8,9},{9,8},{10,11... | collective-permute-start | bytes 786440 | tf_op jit(solution)/shard_map/ppermute | solution.py:168
  85.7 0.2 collective-permute-start.15
  86.0 1.4 %collective-permute-start.16 = (bf16[32,32,128]{2,1,0:T(8,128)(2,1)S(1)}, bf16[32,32,128]{2,1,0:T(8,128)(2,1)S(1)}, u32[]{:S(2)}, u32[]{:S(2)}) collective-permute-start(bf16[32,32,128]{2,1,0:T(8,128)(2,1)S(1)} %get-tuple-element.46), channel_id=1, source_target_pairs={{0,3},{1,2},{2,1},{3,0},{4,7},{5,6},{6,5},{7,4},{8,11},{9,10},{10,... | collective-permute-start | bytes 786440 | tf_op jit(solution)/shard_map/ppermute | solution.py:168
  87.4 0.0 copy-done.13
  87.4 0.1 copy.8.gain
  87.5 0.0 collective-permute-done.14.rest_1_
  87.5 6.4 %collective-permute-done.15.rest_2_ = bf16[32,32,128]{2,1,0:T(8,128)(2,1)S(1)} collective-permute-done((bf16[32,32,128]{2,1,0:T(8,128)(2,1)}, bf16[32,32,128]{2,1,0:T(8,128)(2,1)S(1)}, u32[]{:S(2)}, u32[]{:S(2)}) %collective-permute-start.15) | collective-permute-done | bytes 262176 | tf_op jit(solution)/shard_map/ppermute | solution.py:168
  93.9 5.7 %collective-permute-done.16.rest_3_ = bf16[32,32,128]{2,1,0:T(8,128)(2,1)S(1)} collective-permute-done((bf16[32,32,128]{2,1,0:T(8,128)(2,1)S(1)}, bf16[32,32,128]{2,1,0:T(8,128)(2,1)S(1)}, u32[]{:S(2)}, u32[]{:S(2)}) %collective-permute-start.16) | collective-permute-done | bytes 262176 | tf_op jit(solution)/shard_map/ppermute | solution.py:168
  99.6 0.0 copy-done.9
  99.6 3.1 %update.1 = bf16[32,128,128]{2,1,0:T(8,128)(2,1)} custom-call(s32[3]{0:T(128)S(1)} %pad_add_fusion.where, f32[128,1]{1,0:T(8,128)S(1)} %copy.8.gain, bf16[128,128]{1,0:T(8,128)(2,1)S(1)} %copy-done.9, f32[32,128,128]{2,1,0:T(8,128)S(1)} %gate.1, bf16[32,32,128]{2,1,0:T(8,128)(2,1)S(1)} %get-tuple-element.43.rest_0_, ...), custom_call_target="tpu_custom_call" | custom-call | tf_op jit(solution)/shard_map/update/pallas_call | solution.py:257
  (11 shorter events, 0.0 us)
Async XLA Ops:
  0.0 48.1 %copy-start.12 = (f32[128]{0:T(128)S(1)}, f32[128]{0:T(128)}, u32[]{:S(2)}) copy-start(f32[128]{0:T(128)} %param.9) | copy-start | bytes 1540
  0.0 48.1 %copy-start.8 = (bf16[128,128]{1,0:T(8,128)(2,1)S(1)}, bf16[128,128]{1,0:T(8,128)(2,1)}, u32[]{:S(2)}) copy-start(bf16[128,128]{1,0:T(8,128)(2,1)} %weight.4) | copy-start | bytes 98308
  0.0 8.3 %collective-permute-start = (bf16[32,128,128]{2,1,0:T(8,128)(2,1)}, bf16[32,128,128]{2,1,0:T(8,128)(2,1)S(1)}, u32[]{:S(2)}, u32[]{:S(2)}) collective-permute-start(bf16[32,128,128]{2,1,0:T(8,128)(2,1)} %pair.3), channel_id=1, source_target_pairs={{0,1},{1,0},{2,3},{3,2},{4,5},{5,4},{6,7},{7,6},{8,9},{9,8},{10,11... | collective-permute-start | bytes 3145736 | tf_op jit(solution)/shard_map/ppermute | solution.py:168
  0.1 8.2 %collective-permute-start.1 = (s32[32,128]{1,0:T(8,128)}, s32[32,128]{1,0:T(8,128)S(1)}, u32[]{:S(2)}, u32[]{:S(2)}) collective-permute-start(s32[32,128]{1,0:T(8,128)} %mask.1), channel_id=1, source_target_pairs={{0,1},{1,0},{2,3},{3,2},{4,5},{5,4},{6,7},{7,6},{8,9},{9,8},{10,11... | collective-permute-start | bytes 49160 | tf_op jit(solution)/shard_map/ppermute | solution.py:168
  0.6 1.2 %copy-start = (bf16[32,128,128]{2,1,0:T(8,128)(2,1)S(1)}, bf16[32,128,128]{2,1,0:T(8,128)(2,1)}, u32[]{:S(2)}) copy-start(bf16[32,128,128]{2,1,0:T(8,128)(2,1)} %pair.3) | copy-start | bytes 3145732
  1.8 0.9 copy-start.6
  2.7 0.7 copy-start.10
  3.4 0.7 copy-start.11
  4.1 44.0 %copy-start.1 = (bf16[32,128,128]{2,1,0:T(8,128)(2,1)S(1)}, bf16[32,128,128]{2,1,0:T(8,128)(2,1)}, u32[]{:S(2)}) copy-start(bf16[32,128,128]{2,1,0:T(8,128)(2,1)} %pair.3) | copy-start | bytes 3145732
  8.3 0.9 copy-start.7
  14.3 14.3 %collective-permute-start.2 = (bf16[32,32,256]{2,1,0:T(8,128)(2,1)S(1)}, bf16[32,32,256]{2,1,0:T(8,128)(2,1)}, u32[]{:S(2)}, u32[]{:S(2)}) collective-permute-start(bf16[32,32,256]{2,1,0:T(8,128)(2,1)S(1)} %get-tuple-element.32), channel_id=1, source_target_pairs={{0,2},{1,3},{2,0},{3,1},{4,6},{5,7},{6,4},{7,5},{8,10},{9,11},{10,... | collective-permute-start | bytes 1572872 | tf_op jit(solution)/shard_map/ppermute | solution.py:168
  16.6 14.5 %collective-permute-start.4 = (bf16[32,32,256]{2,1,0:T(8,128)(2,1)S(1)}, bf16[32,32,256]{2,1,0:T(8,128)(2,1)}, u32[]{:S(2)}, u32[]{:S(2)}) collective-permute-start(bf16[32,32,256]{2,1,0:T(8,128)(2,1)S(1)} %get-tuple-element.34.rest_2_), channel_id=1, source_target_pairs={{0,4},{1,5},{2,6},{3,7},{4,0},{5,1},{6,2},{7,3},{8,12},{9,13},{10,... | collective-permute-start | bytes 1572872 | tf_op jit(solution)/shard_map/ppermute | solution.py:168
  17.9 18.7 %collective-permute-start.8 = (bf16[32,32,256]{2,1,0:T(8,128)(2,1)S(1)}, bf16[32,32,256]{2,1,0:T(8,128)(2,1)S(1)}, u32[]{:S(2)}, u32[]{:S(2)}) collective-permute-start(bf16[32,32,256]{2,1,0:T(8,128)(2,1)S(1)} %get-tuple-element.34.rest_2_), channel_id=1, source_target_pairs={{0,0},{1,1},{2,2},{3,3},{4,8},{5,9},{6,10},{7,11},{8,4},{9,5},{10,... | collective-permute-start | bytes 1572872 | tf_op jit(solution)/shard_map/ppermute | solution.py:168
  18.6 0.8 copy-start.4
  28.6 14.1 %collective-permute-start.3 = (bf16[32,32,256]{2,1,0:T(8,128)(2,1)S(1)}, bf16[32,32,256]{2,1,0:T(8,128)(2,1)}, u32[]{:S(2)}, u32[]{:S(2)}) collective-permute-start(bf16[32,32,256]{2,1,0:T(8,128)(2,1)S(1)} %get-tuple-element.33), channel_id=1, source_target_pairs={{0,2},{1,3},{2,0},{3,1},{4,6},{5,7},{6,4},{7,5},{8,10},{9,11},{10,... | collective-permute-start | bytes 1572872 | tf_op jit(solution)/shard_map/ppermute | solution.py:168
  29.7 13.0 %collective-permute-start.5 = (bf16[32,32,256]{2,1,0:T(8,128)(2,1)}, bf16[32,32,256]{2,1,0:T(8,128)(2,1)}, u32[]{:S(2)}, u32[]{:S(2)}) collective-permute-start(bf16[32,32,256]{2,1,0:T(8,128)(2,1)} %collective-permute-done.2.rest_3_), channel_id=1, source_target_pairs={{0,4},{1,5},{2,6},{3,7},{4,0},{5,1},{6,2},{7,3},{8,12},{9,13},{10,... | collective-permute-start | bytes 1572872 | tf_op jit(solution)/shard_map/ppermute | solution.py:168
  31.0 23.9 %collective-permute-start.6 = (bf16[32,32,256]{2,1,0:T(8,128)(2,1)}, bf16[32,32,256]{2,1,0:T(8,128)(2,1)}, u32[]{:S(2)}, u32[]{:S(2)}) collective-permute-start(bf16[32,32,256]{2,1,0:T(8,128)(2,1)} %get-tuple-element.38.rest_0_), channel_id=1, source_target_pairs={{0,4},{1,5},{2,6},{3,7},{4,0},{5,1},{6,2},{7,3},{8,12},{9,13},{10,... | collective-permute-start | bytes 1572872 | tf_op jit(solution)/shard_map/ppermute | solution.py:168
  31.2 23.7 %collective-permute-start.10 = (bf16[32,32,256]{2,1,0:T(8,128)(2,1)}, bf16[32,32,256]{2,1,0:T(8,128)(2,1)}, u32[]{:S(2)}, u32[]{:S(2)}) collective-permute-start(bf16[32,32,256]{2,1,0:T(8,128)(2,1)} %collective-permute-done.4.rest_4_), channel_id=1, source_target_pairs={{0,0},{1,1},{2,2},{3,3},{4,8},{5,9},{6,10},{7,11},{8,4},{9,5},{10,... | collective-permute-start | bytes 1572872 | tf_op jit(solution)/shard_map/ppermute | solution.py:168
  36.6 0.8 copy-start.2
  37.3 17.6 %collective-permute-start.9 = (bf16[32,32,256]{2,1,0:T(8,128)(2,1)}, bf16[32,32,256]{2,1,0:T(8,128)(2,1)}, u32[]{:S(2)}, u32[]{:S(2)}) collective-permute-start(bf16[32,32,256]{2,1,0:T(8,128)(2,1)} %collective-permute-done.2.rest_3_), channel_id=1, source_target_pairs={{0,0},{1,1},{2,2},{3,3},{4,8},{5,9},{6,10},{7,11},{8,4},{9,5},{10,... | collective-permute-start | bytes 1572872 | tf_op jit(solution)/shard_map/ppermute | solution.py:168
  42.7 21.7 %collective-permute-start.7 = (bf16[32,32,256]{2,1,0:T(8,128)(2,1)}, bf16[32,32,256]{2,1,0:T(8,128)(2,1)}, u32[]{:S(2)}, u32[]{:S(2)}) collective-permute-start(bf16[32,32,256]{2,1,0:T(8,128)(2,1)} %collective-permute-done.3.rest_1_), channel_id=1, source_target_pairs={{0,4},{1,5},{2,6},{3,7},{4,0},{5,1},{6,2},{7,3},{8,12},{9,13},{10,... | collective-permute-start | bytes 1572872 | tf_op jit(solution)/shard_map/ppermute | solution.py:168
  42.7 21.7 %collective-permute-start.11 = (bf16[32,32,256]{2,1,0:T(8,128)(2,1)}, bf16[32,32,256]{2,1,0:T(8,128)(2,1)}, u32[]{:S(2)}, u32[]{:S(2)}) collective-permute-start(bf16[32,32,256]{2,1,0:T(8,128)(2,1)} %collective-permute-done.5.rest_5_), channel_id=1, source_target_pairs={{0,0},{1,1},{2,2},{3,3},{4,8},{5,9},{6,10},{7,11},{8,4},{9,5},{10,... | collective-permute-start | bytes 1572872 | tf_op jit(solution)/shard_map/ppermute | solution.py:168
  51.0 13.4 %copy-start.3 = (bf16[32,32,256]{2,1,0:T(8,128)(2,1)S(1)}, bf16[32,32,256]{2,1,0:T(8,128)(2,1)}, u32[]{:S(2)}) copy-start(bf16[32,32,256]{2,1,0:T(8,128)(2,1)} %copy-done.2) | copy-start | bytes 1572868
  51.2 1.0 %copy-start.5 = (bf16[32,32,256]{2,1,0:T(8,128)(2,1)S(1)}, bf16[32,32,256]{2,1,0:T(8,128)(2,1)}, u32[]{:S(2)}) copy-start(bf16[32,32,256]{2,1,0:T(8,128)(2,1)} %copy-done.4) | copy-start | bytes 1572868
  54.9 32.5 %copy-start.13 = (f32[128]{0:T(128)S(1)}, f32[128]{0:T(128)}, u32[]{:S(2)}) copy-start(f32[128]{0:T(128)} %param.12) | copy-start | bytes 1540
  54.9 44.7 %copy-start.9 = (bf16[128,128]{1,0:T(8,128)(2,1)S(1)}, bf16[128,128]{1,0:T(8,128)(2,1)}, u32[]{:S(2)}) copy-start(bf16[128,128]{1,0:T(8,128)(2,1)} %weight.7) | copy-start | bytes 98308
  67.2 7.9 %collective-permute-start.12 = (bf16[32,32,128]{2,1,0:T(8,128)(2,1)S(1)}, bf16[32,32,128]{2,1,0:T(8,128)(2,1)S(1)}, u32[]{:S(2)}, u32[]{:S(2)}) collective-permute-start(bf16[32,32,128]{2,1,0:T(8,128)(2,1)S(1)} %get-tuple-element.41), channel_id=1, source_target_pairs={{0,4},{1,5},{2,6},{3,7},{4,0},{5,1},{6,2},{7,3},{8,12},{9,13},{10,... | collective-permute-start | bytes 786440 | tf_op jit(solution)/shard_map/ppermute | solution.py:168
  71.4 9.2 %collective-permute-start.13 = (bf16[32,32,128]{2,1,0:T(8,128)(2,1)S(1)}, bf16[32,32,128]{2,1,0:T(8,128)(2,1)S(1)}, u32[]{:S(2)}, u32[]{:S(2)}) collective-permute-start(bf16[32,32,128]{2,1,0:T(8,128)(2,1)S(1)} %get-tuple-element.42), channel_id=1, source_target_pairs={{0,4},{1,5},{2,6},{3,7},{4,0},{5,1},{6,2},{7,3},{8,12},{9,13},{10,... | collective-permute-start | bytes 786440 | tf_op jit(solution)/shard_map/ppermute | solution.py:168
  82.1 5.4 %collective-permute-start.14 = (bf16[32,32,128]{2,1,0:T(8,128)(2,1)}, bf16[32,32,128]{2,1,0:T(8,128)(2,1)S(1)}, u32[]{:S(2)}, u32[]{:S(2)}) collective-permute-start(bf16[32,32,128]{2,1,0:T(8,128)(2,1)} %get-tuple-element.44), channel_id=1, source_target_pairs={{0,1},{1,0},{2,3},{3,2},{4,5},{5,4},{6,7},{7,6},{8,9},{9,8},{10,11... | collective-permute-start | bytes 786440 | tf_op jit(solution)/shard_map/ppermute | solution.py:168
  85.7 8.1 %collective-permute-start.15 = (bf16[32,32,128]{2,1,0:T(8,128)(2,1)}, bf16[32,32,128]{2,1,0:T(8,128)(2,1)S(1)}, u32[]{:S(2)}, u32[]{:S(2)}) collective-permute-start(bf16[32,32,128]{2,1,0:T(8,128)(2,1)} %get-tuple-element.45), channel_id=1, source_target_pairs={{0,2},{1,3},{2,0},{3,1},{4,6},{5,7},{6,4},{7,5},{8,10},{9,11},{10,... | collective-permute-start | bytes 786440 | tf_op jit(solution)/shard_map/ppermute | solution.py:168
  86.0 13.6 %collective-permute-start.16 = (bf16[32,32,128]{2,1,0:T(8,128)(2,1)S(1)}, bf16[32,32,128]{2,1,0:T(8,128)(2,1)S(1)}, u32[]{:S(2)}, u32[]{:S(2)}) collective-permute-start(bf16[32,32,128]{2,1,0:T(8,128)(2,1)S(1)} %get-tuple-element.46), channel_id=1, source_target_pairs={{0,3},{1,2},{2,1},{3,0},{4,7},{5,6},{6,5},{7,4},{8,11},{9,10},{10,... | collective-permute-start | bytes 786440 | tf_op jit(solution)/shard_map/ppermute | solution.py:168

commit v3 on v2

v3 whole, which is shorter than its diff:
```python
import functools

import jax
import jax.numpy as jnp
from jax import lax
from jax.experimental import pallas as pl
from jax.experimental.pallas import tpu as pltpu
from jax.sharding import PartitionSpec as P

F32, BF16 = jnp.float32, jnp.bfloat16
LANES = 128
LIMIT = 40 * 1024 * 1024
SHARES = (2, 2)
NT = (((1,), (1,)), ((), ()))
TN = (((0,), (0,)), ((), ()))
SMEM = pl.BlockSpec(memory_space=pltpu.SMEM)
VMEM = pl.BlockSpec(memory_space=pltpu.VMEM)
HBM = pl.BlockSpec(memory_space=pltpu.HBM)
PARAMS = pltpu.CompilerParams(vmem_limit_bytes=LIMIT)
GROUP = 4


def normalise(x, gain):
    mean = jnp.mean(x, axis=-1, keepdims=True)
    centered = x - mean
    var = jnp.mean(centered * centered, axis=-1, keepdims=True)
    return (centered * lax.rsqrt(var + 1e-05) * gain).astype(BF16)


def gated(normed, chosen, mask, first, held):
    toks = mask.shape[1]
    wide = chosen.shape[0] // 2
    rows = mask.shape[0]
    proj = lax.dot_general(chosen[...], normed, NT, preferred_element_type=F32)
    for g in range(normed.shape[0] // toks):
        valid = mask[pl.ds(first + g, 1), :].astype(F32) * 0.5
        mine = proj[:, g * toks : (g + 1) * toks]
        value = (jnp.tanh(mine[:wide]) + 1.0) * (valid * mine[wide:])
        for m in range(toks // LANES):
            spot = pl.ds(first + g, wide, stride=rows + 1)
            held[m, spot, :] = value[:, m * LANES : (m + 1) * LANES]


def write_pieces(outs, held, base):
    row = 0
    for out in outs:
        count, rows, _ = out.shape
        for c in range(count):
            for m in range(held.shape[0]):
                lanes = slice(base + m * LANES, base + (m + 1) * LANES)
                out[c, :, lanes] = held[m, row : row + rows, :].astype(BF16)
            row += rows + 1


def right_own_kernel(where, pair, mask, gain, weight, *rest):
    outs, (normed_out, chosen_right, chosen_left) = rest[:-11], rest[-11:-8]
    pair_v, mask_v, gain_v, weight_v, turned, held, sem, pair_sem = rest[-8:]
    rows, toks, _ = pair_v.shape
    hidden = weight_v.shape[1] // 4
    part = hidden // 4
    parts = pair_sem.shape[0]
    each = rows // parts
    small = [
        pltpu.make_async_copy(a, b, sem.at[n])
        for n, (a, b) in enumerate(((weight, weight_v), (mask, mask_v), (gain, gain_v)))
    ]
    large = [
        pltpu.make_async_copy(
            pair.at[pl.ds(n * each, each)], pair_v.at[pl.ds(n * each, each)], pair_sem.at[n]
        )
        for n in range(parts)
    ]
    for copy in small + large:
        copy.start()
    for copy in small:
        copy.wait()
    turned[...] = weight_v[...].T
    for n in range(4):
        chosen = chosen_left if n < 2 else chosen_right
        half = 0.5 if n % 2 == 0 else 1.0
        for p in range(2):
            start = pl.multiple_of(n * hidden + (where[0] ^ (2 * p)) * part, part)
            at = (2 * (n % 2) + p) * part
            chosen[at : at + part, :] = turned[pl.ds(start, part), :] * half
    for n in range(parts):
        large[n].wait()

        @pl.loop(0, each // GROUP)
        def _(at):
            first = n * each + at * GROUP
            x = pair_v[pl.ds(first, GROUP)].astype(F32).reshape(GROUP * toks, -1)
            normed = normalise(x, gain_v[...])
            normed_out[pl.ds(first * toks, GROUP * toks), :] = normed
            gated(normed, chosen_right, mask_v, first, held)

    write_pieces(outs, held, 0)


def right_twin_kernel(pair, mask, gain, chosen, *rest):
    count = (len(rest) - 2) // 2
    before, outs, normed_out, held = rest[:count], rest[count:-2], rest[-2], rest[-1]
    rows, toks, _ = pair.shape
    for x, out in zip(before, outs):
        out[:, :, :toks] = x[...]

    @pl.loop(0, rows // GROUP)
    def _(at):
        first = at * GROUP
        x = pair[pl.ds(first, GROUP)].astype(F32).reshape(GROUP * toks, -1)
        normed = normalise(x, gain[...])
        normed_out[pl.ds(first * toks, GROUP * toks), :] = normed
        gated(normed, chosen, mask, first, held)

    write_pieces(outs, held, toks)


def left_kernel(normed0, normed1, mask0, mask1, chosen, *rest):
    outs, held = rest[:-1], rest[-1]
    rows, toks = mask0.shape
    for n, (normed, mask) in enumerate(((normed0, mask0), (normed1, mask1))):

        @pl.loop(0, rows // GROUP)
        def _(at):
            first = at * GROUP
            gated(normed[pl.ds(first * toks, GROUP * toks), :], chosen, mask, first, held)

        write_pieces(outs, held, n * toks)


def gate_kernel(normed, weight, out):
    rows, toks, _ = out.shape

    @pl.loop(0, rows // GROUP)
    def _(at):
        x = normed[pl.ds(at * GROUP * toks, GROUP * toks), :]
        logits = jnp.dot(x, weight[...], preferred_element_type=F32)
        out[pl.ds(at * GROUP, GROUP)] = (0.5 * jnp.tanh(0.5 * logits) + 0.5).reshape(GROUP, toks, -1)


def merge_kernel(start, own, neighbour, out):
    rows = own.shape[1]
    own_at = pl.multiple_of(start[0] * rows, rows)
    out[:, pl.ds(own_at, rows), :] = own[...]
    out[:, pl.ds(rows - own_at, rows), :] = neighbour[...]


def product_kernel(n_left, n_right, places, *rest):
    lefts, rights = rest[:n_left], rest[n_left : n_left + n_right]
    outs, held = rest[n_left + n_right : -1], rest[-1]
    count, span, _ = lefts[0].shape
    for s in range(n_right):
        held[:, pl.ds(pl.multiple_of(places[s] * span, span), span), :] = rights[s][...]
    for c in range(count):
        left = jnp.concatenate([x[c] for x in lefts], axis=0)
        out = lax.dot_general(left, held[c], NT, preferred_element_type=F32).astype(BF16)
        for n in range(n_left):
            outs[n][c] = out[n * span : (n + 1) * span]


def hand_out_kernel(where, near, far, end, *outs):
    rows = outs[0].shape[1]
    for r in range(4):
        source = where[2] ^ (r % 2)
        span = slice((r // 2) * rows, (r // 2 + 1) * rows)

        @pl.when(source == 0)
        def _():
            outs[r][...] = near[:, span, :]

        @pl.when((source == 1) & (where[1] == 0))
        def _():
            outs[r][...] = far[:, span, :]

        @pl.when((source == 1) & (where[1] == 1))
        def _():
            outs[r][...] = end[:, span, :]


def update_kernel(where, gain, weight, gate, *rest):
    pieces, out, turned = rest[:-2], rest[-2], rest[-1]
    part = sum(x.shape[0] for x in pieces[::4])
    _, rows, toks = pieces[0].shape
    hidden = 4 * part
    pitch = hidden + 1
    for r in range(4):
        base = (where[0] ^ r) * part
        for piece in pieces[r::4]:
            for c in range(piece.shape[0]):
                value = piece[c].astype(F32)
                for m in range(toks // LANES):
                    turned[m, pl.ds(base + c, rows, stride=pitch), :] = value[
                        :, m * LANES : (m + 1) * LANES
                    ]
            base = base + piece.shape[0]
    scale = jnp.broadcast_to(gain[...], (hidden, toks))

    @pl.loop(0, rows, unroll=8)
    def _(i):
        x = jnp.concatenate(
            [turned[m, pl.ds(i * pitch, hidden), :] for m in range(toks // LANES)], axis=1
        )
        mean = jnp.mean(x, axis=0, keepdims=True)
        centered = x - mean
        var = jnp.mean(centered * centered, axis=0, keepdims=True)
        pnorm = (centered * lax.rsqrt(var + 1e-05) * scale).astype(BF16)
        mapped = lax.dot_general(pnorm, weight[...], TN, preferred_element_type=F32)
        out[i] = (gate[i] * mapped).astype(BF16)


def kernel(body, name, out_shape, in_specs, scratch=()):
    outs = jax.tree.map(lambda _: VMEM, out_shape)
    return pl.pallas_call(
        body,
        out_shape=out_shape,
        in_specs=in_specs,
        out_specs=outs,
        scratch_shapes=list(scratch),
        compiler_params=PARAMS,
        name=name,
    )


def local(pair, pair_mask, in_gain, proj_weight, gate_weight, out_gain, out_weight, *, n_row):
    rows, toks, channels = pair.shape
    hidden = proj_weight.shape[1] // 4
    part = hidden // 4
    planes = n_row // 2
    half = planes // 2
    counts = [part * share // sum(SHARES) for share in SHARES]
    groups = range(len(counts))
    row, core = lax.axis_index("row"), lax.axis_index("chan")
    z, y = row // 2, row % 2
    own_half = z // half
    at_end = (z == 0) | (z == planes - 1)
    where = jnp.stack([2 * y + core, at_end, core ^ own_half]).astype(jnp.int32)
    start = y[None].astype(jnp.int32)
    zero = jnp.zeros((1,), jnp.int32)

    def send(x, target):
        pairs = []
        for source in range(2 * n_row):
            to = target(source // 4, source // 2 % 2, source % 2)
            pairs.append((source, 4 * to[0] + 2 * to[1] + to[2]))
        return lax.ppermute(x, ("row", "chan"), pairs)

    def after(x, *earlier):
        return lax.optimization_barrier((x, *earlier))[0]

    def in_plane(r):
        return lambda p, b, k: (p, b ^ (r // 2), k ^ (r % 2))

    def shifted(s):
        return lambda p, b, k: (p // half * half + (p + s) % half, b, k)

    def mirrored(p, b, k):
        return (p if p in (0, planes - 1) else planes - 1 - p, b, k)

    def edge(p, b, k):
        swap = {0: 1, 1: 0, planes - 1: planes - 2, planes - 2: planes - 1}
        return (swap.get(p, p), b, k)

    gains = in_gain.reshape(1, -1)
    twin, twin_mask = send(pair, in_plane(1)), send(pair_mask, in_plane(1))

    def piece(count, height, depth):
        return jax.ShapeDtypeStruct((count, height, depth), BF16)

    held = pltpu.VMEM((toks // LANES, 2 * part * (rows + 1), LANES), F32)
    rows_all = jax.ShapeDtypeStruct((rows * toks, channels), BF16)
    weights = jax.ShapeDtypeStruct((4 * part, channels), BF16)
    copies = 4
    *mine, normed0, chosen_right, chosen_left = kernel(
        right_own_kernel,
        "right_own",
        [piece(count, rows, toks) for _ in range(2) for count in counts] + [rows_all, weights, weights],
        [SMEM] + [HBM] * 4,
        [
            pltpu.VMEM(pair.shape, BF16),
            pltpu.VMEM(pair_mask.shape, pair_mask.dtype),
            pltpu.VMEM(gains.shape, F32),
            pltpu.VMEM(proj_weight.shape, BF16),
            pltpu.VMEM((4 * hidden, channels), BF16),
            held,
            pltpu.SemaphoreType.DMA((3,)),
            pltpu.SemaphoreType.DMA((copies,)),
        ],
    )(where, pair, pair_mask, gains, proj_weight)
    whole = [piece(count, rows, 2 * toks) for _ in range(2) for count in counts]
    *right, normed1 = kernel(
        right_twin_kernel, "right_twin", whole + [rows_all], [VMEM] * (4 + len(mine)), [held]
    )(twin, twin_mask, gains, chosen_right, *mine)
    right0, right1 = list(right[: len(counts)]), list(right[len(counts) :])
    right1[0] = send(right1[0], in_plane(2))
    left = kernel(left_kernel, "left", whole, [VMEM] * 5, [held])(
        normed0, normed1, pair_mask, twin_mask, chosen_left
    )
    left0, left1 = list(left[: len(counts)]), list(left[len(counts) :])
    gate = kernel(
        gate_kernel, "gate", jax.ShapeDtypeStruct((rows, toks, channels), F32), [VMEM] * 2
    )(normed0, gate_weight)

    def merge(own, neighbour, at, name):
        shape = piece(own.shape[0], 2 * rows, 2 * toks)
        return kernel(merge_kernel, name, shape, [SMEM, VMEM, VMEM])(at, own, neighbour)

    def products(lefts, rights, places, name):
        span = 2 * rows * len(rights)
        count = lefts[0].shape[0]
        return kernel(
            functools.partial(product_kernel, len(lefts), len(rights)),
            name,
            [piece(count, 2 * rows, span)] * len(lefts),
            [SMEM] + [VMEM] * (len(lefts) + len(rights)),
            [pltpu.VMEM((count, span, 2 * toks), BF16)],
        )(places, *lefts, *rights)

    steps = jnp.arange(half)
    places_near = ((z - steps) % half).astype(jnp.int32)
    places_far = ((planes - 1 - z - steps) % half).astype(jnp.int32)
    done_y, done_z, done = [right1[0]], [], [gate]
    pieces = []
    for g in groups:
        if g:
            right1[g] = send(after(right1[g], *done_y), in_plane(2))
            done_y = [right1[g]]
        left1[g] = send(after(left1[g], *done_y), in_plane(2))
        done_y = [left1[g]]
        own = merge(right0[g], right1[g], start, "merge_right")
        own = after(own, *done_z)
        far = [send(own, mirrored)]
        near = [own] + [send(own, shifted(s)) for s in range(1, half)]
        far += [send(x, mirrored) for x in near[1:]]
        left = merge(left0[g], left1[g], zero, "merge_left")
        done_z = [far[0], near[-1], left]
        outer = send(after(left, near[-1]), edge)
        (close,) = products([left], near, places_near, "near")
        away, ends = products([after(left, close, *done), outer], far, places_far, "away")
        ends = send(ends, edge)
        handed = kernel(
            hand_out_kernel,
            "hand_out",
            [piece(counts[g], rows, toks)] * 4,
            [SMEM] + [VMEM] * 3,
        )(where, close, away, ends)
        done = [handed[0]] + [send(handed[r], in_plane(r)) for r in range(1, 4)]
        pieces += done

    return kernel(
        update_kernel,
        "update",
        jax.ShapeDtypeStruct((rows, toks, channels), BF16),
        [SMEM] + [VMEM] * (3 + len(pieces)),
        [pltpu.VMEM((toks // LANES, rows * (hidden + 1), LANES), F32)],
    )(where, out_gain.reshape(-1, 1), out_weight, gate, *pieces)


def solution(mesh):
    placed = (
        P(("groups", "row"), "chan", None),
        P(("groups", "row"), "chan"),
        P(),
        P(),
        P(),
        P(),
        P(),
    )
    return jax.shard_map(
        functools.partial(local, n_row=mesh.shape["row"]),
        mesh=mesh,
        in_specs=placed,
        out_specs=P(("groups", "row"), "chan", None),
        check_vma=False,
    )
```

time: 104 us -> 99.8 us (0.960)
  waiting for transfers between devices: 39.9 us -> 33.8 us
  Pallas kernels: 22.2 us -> 24.3 us
    ppermute x17 -> x22, waiting for transfers between devices: 39.9 us -> 33.8 us  [send(): return lax.ppermute(x, ('row', 'chan'), pairs)]
    pallas_call x7 -> x15, Pallas kernels: 22.2 us -> 24.3 us  [the longest x4 5.96 us: products(): kernel(functools.partial(product_kernel, len(lefts), len(rights)), name,...]
    unnamed x28 -> x32, local copies, waits for them, and re-layouts: 7.07 us -> 7.23 us
    ppermute x17 -> x22, starting transfers between devices: 33 us -> 32.9 us  [send(): return lax.ppermute(x, ('row', 'chan'), pairs)]
  transfers between devices with their start and end apart: 17 -> 22, of which waited for: 6 -> 10; matrix products, arithmetic and copies ran while one was open for 0% -> 0% of each run, Pallas kernels for 10% -> 16%
where the time goes in v3:
time: 99.8 us; the launch traced here: 98.7 us
  waiting for transfers between devices  33.8 us (34%)
  starting transfers between devices  32.9 us (33%)
  Pallas kernels  24.3 us (24%)
  local copies, waits for them, and re-layouts  7.34 us (7%)
    ppermute x22, waiting for transfers between devices, send(): return lax.ppermute(x, ('row', 'chan'), pairs)  33.8 us
    ppermute x22, starting transfers between devices, send(): return lax.ppermute(x, ('row', 'chan'), pairs)  32.9 us
    unnamed x32, local copies, waits for them, and re-layouts  7.23 us
    pallas_call x4, Pallas kernels, products(): kernel(functools.partial(product_kernel, len(lefts), len(rights)), name,...  5.96 us
    pallas_call x1, Pallas kernels, local(): kernel(right_own_kernel, 'right_own', [piece(count, rows, toks) for _ in...  4.17 us
    pallas_call x1, Pallas kernels, local(): kernel(left_kernel, 'left', whole, [VMEM] * 5, [held])  3.93 us
    pallas_call x1, Pallas kernels, local(): kernel(right_twin_kernel, 'right_twin', whole + [rows_all], [VMEM] * (4 +...  3.31 us
    pallas_call x1, Pallas kernels, local(): kernel(update_kernel, 'update', jax.ShapeDtypeStruct((rows, toks, channel...  3.06 us
  transfers between devices with their start and end apart: 22, of which 10 were waited for; matrix products, arithmetic and copies ran while one was open for 0% of the time, Pallas kernels for 16%

profile of v3, /device:TPU:1, one launch (start us, length us, event | category | flops | bytes accessed | tf_op | source)
XLA Modules:
  0.0 98.7 jit_solution(4941177255482176966)
XLA Ops:
  0.0 0.1 collective-permute-start
  0.1 0.5 collective-permute-start.1
  0.5 0.1 pad_add_fusion.where
  0.6 1.2 %copy-done.4 = bf16[32,128,128]{2,1,0:T(8,128)(2,1)S(1)} copy-done((bf16[32,128,128]{2,1,0:T(8,128)(2,1)S(1)}, bf16[32,128,128]{2,1,0:T(8,128)(2,1)}, u32[]{:S(2)}) %copy-start.4) | copy-done | bytes 1048600
  1.8 0.9 copy-done.9
  2.7 0.7 copy-done.10
  3.4 0.7 copy-done.14
  4.1 4.2 %right_own.1 = (bf16[16,32,128]{2,1,0:T(8,128)(2,1)S(1)}, bf16[16,32,128]{2,1,0:T(8,128)(2,1)S(1)}, bf16[16,32,128]{2,1,0:T(8,128)(2,1)S(1)}, bf16[16,32,128]{2,...) custom-call(s32[3]{0:T(128)S(1)} %pad_add_fusion.where, ...), custom_call_target="tpu_custom_call" | custom-call | tf_op jit(solution)/shard_map/right_own/pallas_call | solution.py:272
  8.3 0.0 copy-start
  8.3 0.0 collective-permute-done.1.mask.mask1
  8.3 0.0 collective-permute-done.pair
  8.3 3.3 %right_twin.1 = (bf16[16,32,256]{2,1,0:T(8,128)(2,1)S(1)}, bf16[16,32,256]{2,1,0:T(8,128)(2,1)S(1)}, bf16[16,32,256]{2,1,0:T(8,128)(2,1)S(1)}, bf16[16,32,256]{2,1,0:T(8,128)(2,1)S(1)}, bf16[4096,128]{1,0:T(8,128)(2,1)S(1)}) custom-call(bf16[32,128,128]{2,1,0:T(8,128)(2,1)S(1)} %collective-permute-done.pair, ...), custom_call_target="tpu_custom_call" | custom-call | tf_op jit(solution)/shard_map/right_twin/pallas_call | solution.py:289
  11.6 2.4 %collective-permute-start.2 = (bf16[16,32,256]{2,1,0:T(8,128)(2,1)S(1)}, bf16[16,32,256]{2,1,0:T(8,128)(2,1)S(1)}, u32[]{:S(2)}, u32[]{:S(2)}) collective-permute-start(bf16[16,32,256]{2,1,0:T(8,128)(2,1)S(1)} %get-tuple-element.51), channel_id=1, source_target_pairs={{0,2},{1,3},{2,0},{3,1},{4,6},{5,7},{6,4},{7,5},{8,10},{9,11},{10,... | collective-permute-start | bytes 786440 | tf_op jit(solution)/shard_map/ppermute | solution.py:244
  14.0 3.9 %left.1 = (bf16[16,32,256]{2,1,0:T(8,128)(2,1)S(1)}, bf16[16,32,256]{2,1,0:T(8,128)(2,1)S(1)}, bf16[16,32,256]{2,1,0:T(8,128)(2,1)S(1)}, bf16[16,32,256]{2,1,0:T(8,128)(2,1)}) custom-call(bf16[4096,128]{1,0:T(8,128)(2,1)S(1)} %get-tuple-element.41.normed.normed0, bf16[4096,128]{1,0:T(8,128)(2,1)S(1)} %get-tuple-element.47.normed1, s32[32,128]{1,0:T(8,128)S(1)} %copy-done.11, ...), custom_call_target="tpu_custom_call" | custom-call | tf_op jit(solution)/shard_map/left/pallas_call | solution.py:294
  17.9 2.4 %collective-permute-done.2.neighbour = bf16[16,32,256]{2,1,0:T(8,128)(2,1)S(1)} collective-permute-done((bf16[16,32,256]{2,1,0:T(8,128)(2,1)S(1)}, bf16[16,32,256]{2,1,0:T(8,128)(2,1)S(1)}, u32[]{:S(2)}, u32[]{:S(2)}) %collective-permute-start.2) | collective-permute-done | bytes 262176 | tf_op jit(solution)/shard_map/ppermute | solution.py:244
  20.3 1.3 %collective-permute-start.4 = (bf16[16,64,256]{2,1,0:T(8,128)(2,1)S(1)}, bf16[16,64,256]{2,1,0:T(8,128)(2,1)}, u32[]{:S(2)}, u32[]{:S(2)}) collective-permute-start(bf16[16,64,256]{2,1,0:T(8,128)(2,1)S(1)} %merge_right.2.rest_1_), channel_id=1, source_target_pairs={{0,4},{1,5},{2,6},{3,7},{4,0},{5,1},{6,2},{7,3},{8,12},{9,13},{10,... | collective-permute-start | bytes 1572872 | tf_op jit(solution)/shard_map/ppermute | solution.py:244
  21.6 1.2 %collective-permute-start.3 = (bf16[16,32,256]{2,1,0:T(8,128)(2,1)S(1)}, bf16[16,32,256]{2,1,0:T(8,128)(2,1)S(1)}, u32[]{:S(2)}, u32[]{:S(2)}) collective-permute-start(bf16[16,32,256]{2,1,0:T(8,128)(2,1)S(1)} %get-tuple-element.52), channel_id=1, source_target_pairs={{0,2},{1,3},{2,0},{3,1},{4,6},{5,7},{6,4},{7,5},{8,10},{9,11},{10,... | collective-permute-start | bytes 786440 | tf_op jit(solution)/shard_map/ppermute | solution.py:244
  22.8 0.7 collective-permute-start.6
  23.5 4.4 %collective-permute-done.3.neighbour = bf16[16,32,256]{2,1,0:T(8,128)(2,1)S(1)} collective-permute-done((bf16[16,32,256]{2,1,0:T(8,128)(2,1)S(1)}, bf16[16,32,256]{2,1,0:T(8,128)(2,1)S(1)}, u32[]{:S(2)}, u32[]{:S(2)}) %collective-permute-start.3) | collective-permute-done | bytes 262176 | tf_op jit(solution)/shard_map/ppermute | solution.py:244
  27.9 1.2 %collective-permute-start.12 = (bf16[16,32,256]{2,1,0:T(8,128)(2,1)S(1)}, bf16[16,32,256]{2,1,0:T(8,128)(2,1)S(1)}, u32[]{:S(2)}, u32[]{:S(2)}) collective-permute-start(bf16[16,32,256]{2,1,0:T(8,128)(2,1)S(1)} %get-tuple-element.65), channel_id=1, source_target_pairs={{0,2},{1,3},{2,0},{3,1},{4,6},{5,7},{6,4},{7,5},{8,10},{9,11},{10,... | collective-permute-start | bytes 786440 | tf_op jit(solution)/shard_map/ppermute | solution.py:244
  29.2 3.7 %collective-permute-done.4.rest_2_ = bf16[16,64,256]{2,1,0:T(8,128)(2,1)} collective-permute-done((bf16[16,64,256]{2,1,0:T(8,128)(2,1)S(1)}, bf16[16,64,256]{2,1,0:T(8,128)(2,1)}, u32[]{:S(2)}, u32[]{:S(2)}) %collective-permute-start.4) | collective-permute-done | bytes 524320 | tf_op jit(solution)/shard_map/ppermute | solution.py:244
  33.0 0.9 collective-permute-start.5
  33.8 5.4 %collective-permute-start.7 = (bf16[16,64,256]{2,1,0:T(8,128)(2,1)}, bf16[16,64,256]{2,1,0:T(8,128)(2,1)}, u32[]{:S(2)}, u32[]{:S(2)}) collective-permute-start(bf16[16,64,256]{2,1,0:T(8,128)(2,1)} %collective-permute-done.4.rest_2_), channel_id=1, source_target_pairs={{0,0},{1,1},{2,2},{3,3},{4,8},{5,9},{6,10},{7,11},{8,4},{9,5},{10,... | collective-permute-start | bytes 1572872 | tf_op jit(solution)/shard_map/ppermute | solution.py:244
  39.2 0.0 collective-permute-done.12.neighbour
  39.3 0.8 copy-done.5
  40.1 0.0 collective-permute-start.14
  40.1 1.2 %collective-permute-start.13 = (bf16[16,32,256]{2,1,0:T(8,128)(2,1)}, bf16[16,32,256]{2,1,0:T(8,128)(2,1)}, u32[]{:S(2)}, u32[]{:S(2)}) collective-permute-start(bf16[16,32,256]{2,1,0:T(8,128)(2,1)} %get-tuple-element.66), channel_id=1, source_target_pairs={{0,2},{1,3},{2,0},{3,1},{4,6},{5,7},{6,4},{7,5},{8,10},{9,11},{10,... | collective-permute-start | bytes 786440 | tf_op jit(solution)/shard_map/ppermute | solution.py:244
  41.3 1.2 %copy-done.1 = bf16[4096,128]{1,0:T(8,128)(2,1)S(1)} copy-done((bf16[4096,128]{1,0:T(8,128)(2,1)S(1)}, bf16[4096,128]{1,0:T(8,128)(2,1)}, u32[]{:S(2)}) %copy-start.1) | copy-done | bytes 1048600
  42.6 1.5 %gate.1 = f32[32,128,128]{2,1,0:T(8,128)S(1)} custom-call(bf16[4096,128]{1,0:T(8,128)(2,1)S(1)} %copy-done.1, bf16[128,128]{1,0:T(8,128)(2,1)S(1)} %copy-done.12), custom_call_target="tpu_custom_call" | custom-call | tf_op jit(solution)/shard_map/gate/pallas_call | solution.py:298
  44.1 1.6 %near.2 = bf16[16,64,128]{2,1,0:T(8,128)(2,1)S(1)} custom-call(s32[2]{0:T(128)S(1)} %and_select_fusion.1.places, bf16[16,64,256]{2,1,0:T(8,128)(2,1)S(1)} %merge_left.2.rest_0_, bf16[16,64,256]{2,1,0:T(8,128)(2,1)S(1)} %copy-done.3, bf16[16,64,256]{2,1,0:T(8,128)(2,1)} %collective-permute-done.4.rest_2_), custom_call_target="tpu_custom_call" | custom-call | tf_op jit(solution)/shard_map/near/pallas_call | solution.py:309
  45.7 0.0 collective-permute-done.5.rest_1_
  45.7 1.7 %away.2 = (bf16[16,64,128]{2,1,0:T(8,128)(2,1)S(1)}, bf16[16,64,128]{2,1,0:T(8,128)(2,1)S(1)}) custom-call(s32[2]{0:T(128)S(1)} %and_select_fusion.places, bf16[16,64,256]{2,1,0:T(8,128)(2,1)S(1)} %merge_left.2.rest_0_, bf16[16,64,256]{2,1,0:T(8,128)(2,1)} %collective-permute-done.5.rest_1_, bf16[16,64,256]{2,1,0:T(8,128)(2,1)S(1)} %copy-done.6, ...), custom_call_target="tpu_custom_call" | custom-call | tf_op jit(solution)/shard_map/away/pallas_call | solution.py:309
  47.4 2.8 %collective-permute-start.8 = (bf16[16,64,128]{2,1,0:T(8,128)(2,1)S(1)}, bf16[16,64,128]{2,1,0:T(8,128)(2,1)S(1)}, u32[]{:S(2)}, u32[]{:S(2)}) collective-permute-start(bf16[16,64,128]{2,1,0:T(8,128)(2,1)S(1)} %get-tuple-element.57), channel_id=1, source_target_pairs={{0,4},{1,5},{2,6},{3,7},{4,0},{5,1},{6,2},{7,3},{8,12},{9,13},{10,... | collective-permute-start | bytes 786440 | tf_op jit(solution)/shard_map/ppermute | solution.py:244
  50.2 0.7 collective-permute-start.16
  50.9 0.0 collective-permute-done.13.neighbour
  50.9 1.0 merge_left.3.rest_0_
  51.9 3.9 %collective-permute-done.14.rest_2_ = bf16[16,64,256]{2,1,0:T(8,128)(2,1)} collective-permute-done((bf16[16,64,256]{2,1,0:T(8,128)(2,1)S(1)}, bf16[16,64,256]{2,1,0:T(8,128)(2,1)}, u32[]{:S(2)}, u32[]{:S(2)}) %collective-permute-start.14) | collective-permute-done | bytes 524320 | tf_op jit(solution)/shard_map/ppermute | solution.py:244
  55.8 0.5 collective-permute-start.15
  56.4 1.7 %collective-permute-start.17 = (bf16[16,64,256]{2,1,0:T(8,128)(2,1)}, bf16[16,64,256]{2,1,0:T(8,128)(2,1)S(1)}, u32[]{:S(2)}, u32[]{:S(2)}) collective-permute-start(bf16[16,64,256]{2,1,0:T(8,128)(2,1)} %collective-permute-done.14.rest_2_), channel_id=1, source_target_pairs={{0,0},{1,1},{2,2},{3,3},{4,8},{5,9},{6,10},{7,11},{8,4},{9,5},{10,... | collective-permute-start | bytes 1572872 | tf_op jit(solution)/shard_map/ppermute | solution.py:244
  58.1 3.3 %collective-permute-done.8.end = bf16[16,64,128]{2,1,0:T(8,128)(2,1)S(1)} collective-permute-done((bf16[16,64,128]{2,1,0:T(8,128)(2,1)S(1)}, bf16[16,64,128]{2,1,0:T(8,128)(2,1)S(1)}, u32[]{:S(2)}, u32[]{:S(2)}) %collective-permute-start.8) | collective-permute-done | bytes 262176 | tf_op jit(solution)/shard_map/ppermute | solution.py:244
  61.4 0.7 hand_out.2
  62.0 5.3 %collective-permute-start.9 = (bf16[16,32,128]{2,1,0:T(8,128)(2,1)S(1)}, bf16[16,32,128]{2,1,0:T(8,128)(2,1)S(1)}, u32[]{:S(2)}, u32[]{:S(2)}) collective-permute-start(bf16[16,32,128]{2,1,0:T(8,128)(2,1)S(1)} %get-tuple-element.59), channel_id=1, source_target_pairs={{0,1},{1,0},{2,3},{3,2},{4,5},{5,4},{6,7},{7,6},{8,9},{9,8},{10,11... | collective-permute-start | bytes 393224 | tf_op jit(solution)/shard_map/ppermute | solution.py:244
  67.3 1.2 %collective-permute-start.10 = (bf16[16,32,128]{2,1,0:T(8,128)(2,1)S(1)}, bf16[16,32,128]{2,1,0:T(8,128)(2,1)S(1)}, u32[]{:S(2)}, u32[]{:S(2)}) collective-permute-start(bf16[16,32,128]{2,1,0:T(8,128)(2,1)S(1)} %get-tuple-element.60), channel_id=1, source_target_pairs={{0,2},{1,3},{2,0},{3,1},{4,6},{5,7},{6,4},{7,5},{8,10},{9,11},{10,... | collective-permute-start | bytes 393224 | tf_op jit(solution)/shard_map/ppermute | solution.py:244
  68.5 0.0 collective-permute-done.9.rest_1_
  68.5 1.2 %collective-permute-start.11 = (bf16[16,32,128]{2,1,0:T(8,128)(2,1)S(1)}, bf16[16,32,128]{2,1,0:T(8,128)(2,1)S(1)}, u32[]{:S(2)}, u32[]{:S(2)}) collective-permute-start(bf16[16,32,128]{2,1,0:T(8,128)(2,1)S(1)} %get-tuple-element.61), channel_id=1, source_target_pairs={{0,3},{1,2},{2,1},{3,0},{4,7},{5,6},{6,5},{7,4},{8,11},{9,10},{10,... | collective-permute-start | bytes 393224 | tf_op jit(solution)/shard_map/ppermute | solution.py:244
  69.7 1.6 %near.3 = bf16[16,64,128]{2,1,0:T(8,128)(2,1)S(1)} custom-call(s32[2]{0:T(128)S(1)} %and_select_fusion.1.places, bf16[16,64,256]{2,1,0:T(8,128)(2,1)S(1)} %merge_left.3.rest_0_, bf16[16,64,256]{2,1,0:T(8,128)(2,1)S(1)} %merge_right.3.rest_1_, bf16[16,64,256]{2,1,0:T(8,128)(2,1)} %collective-permute-done.14.rest_2_), custom_call_target="tpu_custom_call" | custom-call | tf_op jit(solution)/shard_map/near/pallas_call | solution.py:309
  71.3 1.1 %collective-permute-done.10.rest_2_ = bf16[16,32,128]{2,1,0:T(8,128)(2,1)S(1)} collective-permute-done((bf16[16,32,128]{2,1,0:T(8,128)(2,1)S(1)}, bf16[16,32,128]{2,1,0:T(8,128)(2,1)S(1)}, u32[]{:S(2)}, u32[]{:S(2)}) %collective-permute-start.10) | collective-permute-done | bytes 131104 | tf_op jit(solution)/shard_map/ppermute | solution.py:244
  72.4 3.0 %collective-permute-done.11.rest_3_ = bf16[16,32,128]{2,1,0:T(8,128)(2,1)S(1)} collective-permute-done((bf16[16,32,128]{2,1,0:T(8,128)(2,1)S(1)}, bf16[16,32,128]{2,1,0:T(8,128)(2,1)S(1)}, u32[]{:S(2)}, u32[]{:S(2)}) %collective-permute-start.11) | collective-permute-done | bytes 131104 | tf_op jit(solution)/shard_map/ppermute | solution.py:244
  75.3 0.0 collective-permute-done.16.rest_2_
  75.4 0.0 collective-permute-done.15.rest_1_
  75.4 1.0 %away.3 = (bf16[16,64,128]{2,1,0:T(8,128)(2,1)S(1)}, bf16[16,64,128]{2,1,0:T(8,128)(2,1)S(1)}) custom-call(s32[2]{0:T(128)S(1)} %and_select_fusion.places, bf16[16,64,256]{2,1,0:T(8,128)(2,1)S(1)} %merge_left.3.rest_0_, bf16[16,64,256]{2,1,0:T(8,128)(2,1)S(1)} %collective-permute-done.15.rest_1_, bf16[16,64,256]{2,1,0:T(8,128)(2,1)S(1)} %collective-permute-done.16.rest_2_, ...), custom_call_target="tpu_custom_call" | custom-call | tf_op jit(solution)/shard_map/away/pallas_call | solution.py:309
  76.4 1.6 %collective-permute-start.18 = (bf16[16,64,128]{2,1,0:T(8,128)(2,1)S(1)}, bf16[16,64,128]{2,1,0:T(8,128)(2,1)S(1)}, u32[]{:S(2)}, u32[]{:S(2)}) collective-permute-start(bf16[16,64,128]{2,1,0:T(8,128)(2,1)S(1)} %get-tuple-element.72), channel_id=1, source_target_pairs={{0,4},{1,5},{2,6},{3,7},{4,0},{5,1},{6,2},{7,3},{8,12},{9,13},{10,... | collective-permute-start | bytes 786440 | tf_op jit(solution)/shard_map/ppermute | solution.py:244
  78.0 5.8 %collective-permute-done.18.end = bf16[16,64,128]{2,1,0:T(8,128)(2,1)S(1)} collective-permute-done((bf16[16,64,128]{2,1,0:T(8,128)(2,1)S(1)}, bf16[16,64,128]{2,1,0:T(8,128)(2,1)S(1)}, u32[]{:S(2)}, u32[]{:S(2)}) %collective-permute-start.18) | collective-permute-done | bytes 262176 | tf_op jit(solution)/shard_map/ppermute | solution.py:244
  83.8 0.7 hand_out.3
  84.5 1.5 %collective-permute-start.19 = (bf16[16,32,128]{2,1,0:T(8,128)(2,1)S(1)}, bf16[16,32,128]{2,1,0:T(8,128)(2,1)S(1)}, u32[]{:S(2)}, u32[]{:S(2)}) collective-permute-start(bf16[16,32,128]{2,1,0:T(8,128)(2,1)S(1)} %get-tuple-element.74), channel_id=1, source_target_pairs={{0,1},{1,0},{2,3},{3,2},{4,5},{5,4},{6,7},{7,6},{8,9},{9,8},{10,11... | collective-permute-start | bytes 393224 | tf_op jit(solution)/shard_map/ppermute | solution.py:244
  86.0 1.3 %collective-permute-start.20 = (bf16[16,32,128]{2,1,0:T(8,128)(2,1)S(1)}, bf16[16,32,128]{2,1,0:T(8,128)(2,1)S(1)}, u32[]{:S(2)}, u32[]{:S(2)}) collective-permute-start(bf16[16,32,128]{2,1,0:T(8,128)(2,1)S(1)} %get-tuple-element.75), channel_id=1, source_target_pairs={{0,2},{1,3},{2,0},{3,1},{4,6},{5,7},{6,4},{7,5},{8,10},{9,11},{10,... | collective-permute-start | bytes 393224 | tf_op jit(solution)/shard_map/ppermute | solution.py:244
  87.2 0.5 collective-permute-start.21
  87.7 0.1 copy.8.gain
  87.8 0.0 collective-permute-done.19.rest_5_
  87.8 3.2 %collective-permute-done.20.rest_6_ = bf16[16,32,128]{2,1,0:T(8,128)(2,1)S(1)} collective-permute-done((bf16[16,32,128]{2,1,0:T(8,128)(2,1)S(1)}, bf16[16,32,128]{2,1,0:T(8,128)(2,1)S(1)}, u32[]{:S(2)}, u32[]{:S(2)}) %collective-permute-start.20) | collective-permute-done | bytes 131104 | tf_op jit(solution)/shard_map/ppermute | solution.py:244
  91.0 3.0 %collective-permute-done.21.rest_7_ = bf16[16,32,128]{2,1,0:T(8,128)(2,1)S(1)} collective-permute-done((bf16[16,32,128]{2,1,0:T(8,128)(2,1)S(1)}, bf16[16,32,128]{2,1,0:T(8,128)(2,1)S(1)}, u32[]{:S(2)}, u32[]{:S(2)}) %collective-permute-start.21) | collective-permute-done | bytes 131104 | tf_op jit(solution)/shard_map/ppermute | solution.py:244
  94.0 0.9 copy-done.8
  94.9 0.8 copy-done.13
  95.7 3.1 %update.1 = bf16[32,128,128]{2,1,0:T(8,128)(2,1)} custom-call(s32[3]{0:T(128)S(1)} %pad_add_fusion.where, f32[128,1]{1,0:T(8,128)S(1)} %copy.8.gain, bf16[128,128]{1,0:T(8,128)(2,1)S(1)} %copy-done.13, f32[32,128,128]{2,1,0:T(8,128)S(1)} %gate.1, bf16[16,32,128]{2,1,0:T(8,128)(2,1)S(1)} %get-tuple-element.58.rest_0_, ...), custom_call_target="tpu_custom_call" | custom-call | tf_op jit(solution)/shard_map/update/pallas_call | solution.py:348
  (31 shorter events, 0.2 us)
Async XLA Ops:
  0.0 14.0 %copy-start.11 = (s32[32,128]{1,0:T(8,128)S(1)}, s32[32,128]{1,0:T(8,128)}, u32[]{:S(2)}) copy-start(s32[32,128]{1,0:T(8,128)} %mask0.1) | copy-start | bytes 49156
  0.0 8.3 %collective-permute-start = (bf16[32,128,128]{2,1,0:T(8,128)(2,1)}, bf16[32,128,128]{2,1,0:T(8,128)(2,1)S(1)}, u32[]{:S(2)}, u32[]{:S(2)}) collective-permute-start(bf16[32,128,128]{2,1,0:T(8,128)(2,1)} %pair.1), channel_id=1, source_target_pairs={{0,1},{1,0},{2,3},{3,2},{4,5},{5,4},{6,7},{7,6},{8,9},{9,8},{10,11... | collective-permute-start | bytes 3145736 | tf_op jit(solution)/shard_map/ppermute | solution.py:244
  0.1 8.2 %collective-permute-start.1 = (s32[32,128]{1,0:T(8,128)}, s32[32,128]{1,0:T(8,128)S(1)}, u32[]{:S(2)}, u32[]{:S(2)}) collective-permute-start(s32[32,128]{1,0:T(8,128)} %mask0.1), channel_id=1, source_target_pairs={{0,1},{1,0},{2,3},{3,2},{4,5},{5,4},{6,7},{7,6},{8,9},{9,8},{10,11... | collective-permute-start | bytes 49160 | tf_op jit(solution)/shard_map/ppermute | solution.py:244
  0.6 1.2 %copy-start.4 = (bf16[32,128,128]{2,1,0:T(8,128)(2,1)S(1)}, bf16[32,128,128]{2,1,0:T(8,128)(2,1)}, u32[]{:S(2)}) copy-start(bf16[32,128,128]{2,1,0:T(8,128)(2,1)} %pair.1) | copy-start | bytes 3145732
  1.8 0.9 copy-start.9
  2.7 0.7 copy-start.10
  3.4 0.7 copy-start.14
  8.3 12.0 %copy-start = (bf16[4096,128]{1,0:T(8,128)(2,1)}, bf16[4096,128]{1,0:T(8,128)(2,1)S(1)}, u32[]{:S(2)}) copy-start(bf16[4096,128]{1,0:T(8,128)(2,1)S(1)} %get-tuple-element.41.normed.normed0) | copy-start | bytes 3145732
  11.6 8.7 %collective-permute-start.2 = (bf16[16,32,256]{2,1,0:T(8,128)(2,1)S(1)}, bf16[16,32,256]{2,1,0:T(8,128)(2,1)S(1)}, u32[]{:S(2)}, u32[]{:S(2)}) collective-permute-start(bf16[16,32,256]{2,1,0:T(8,128)(2,1)S(1)} %get-tuple-element.51), channel_id=1, source_target_pairs={{0,2},{1,3},{2,0},{3,1},{4,6},{5,7},{6,4},{7,5},{8,10},{9,11},{10,... | collective-permute-start | bytes 786440 | tf_op jit(solution)/shard_map/ppermute | solution.py:244
  17.9 23.4 %copy-start.12 = (bf16[128,128]{1,0:T(8,128)(2,1)S(1)}, bf16[128,128]{1,0:T(8,128)(2,1)}, u32[]{:S(2)}) copy-start(bf16[128,128]{1,0:T(8,128)(2,1)} %weight.4) | copy-start | bytes 98308
  20.3 18.9 %copy-start.2 = (bf16[16,64,256]{2,1,0:T(8,128)(2,1)}, bf16[16,64,256]{2,1,0:T(8,128)(2,1)S(1)}, u32[]{:S(2)}) copy-start(bf16[16,64,256]{2,1,0:T(8,128)(2,1)S(1)} %merge_right.2.rest_1_) | copy-start | bytes 1572868
  20.3 12.6 %collective-permute-start.4 = (bf16[16,64,256]{2,1,0:T(8,128)(2,1)S(1)}, bf16[16,64,256]{2,1,0:T(8,128)(2,1)}, u32[]{:S(2)}, u32[]{:S(2)}) collective-permute-start(bf16[16,64,256]{2,1,0:T(8,128)(2,1)S(1)} %merge_right.2.rest_1_), channel_id=1, source_target_pairs={{0,4},{1,5},{2,6},{3,7},{4,0},{5,1},{6,2},{7,3},{8,12},{9,13},{10,... | collective-permute-start | bytes 1572872 | tf_op jit(solution)/shard_map/ppermute | solution.py:244
  21.6 6.3 %collective-permute-start.3 = (bf16[16,32,256]{2,1,0:T(8,128)(2,1)S(1)}, bf16[16,32,256]{2,1,0:T(8,128)(2,1)S(1)}, u32[]{:S(2)}, u32[]{:S(2)}) collective-permute-start(bf16[16,32,256]{2,1,0:T(8,128)(2,1)S(1)} %get-tuple-element.52), channel_id=1, source_target_pairs={{0,2},{1,3},{2,0},{3,1},{4,6},{5,7},{6,4},{7,5},{8,10},{9,11},{10,... | collective-permute-start | bytes 786440 | tf_op jit(solution)/shard_map/ppermute | solution.py:244
  22.8 16.4 %collective-permute-start.6 = (bf16[16,64,256]{2,1,0:T(8,128)(2,1)S(1)}, bf16[16,64,256]{2,1,0:T(8,128)(2,1)S(1)}, u32[]{:S(2)}, u32[]{:S(2)}) collective-permute-start(bf16[16,64,256]{2,1,0:T(8,128)(2,1)S(1)} %merge_right.2.rest_1_), channel_id=1, source_target_pairs={{0,0},{1,1},{2,2},{3,3},{4,8},{5,9},{6,10},{7,11},{8,4},{9,5},{10,... | collective-permute-start | bytes 1572872 | tf_op jit(solution)/shard_map/ppermute | solution.py:244
  27.9 11.3 %collective-permute-start.12 = (bf16[16,32,256]{2,1,0:T(8,128)(2,1)S(1)}, bf16[16,32,256]{2,1,0:T(8,128)(2,1)S(1)}, u32[]{:S(2)}, u32[]{:S(2)}) collective-permute-start(bf16[16,32,256]{2,1,0:T(8,128)(2,1)S(1)} %get-tuple-element.65), channel_id=1, source_target_pairs={{0,2},{1,3},{2,0},{3,1},{4,6},{5,7},{6,4},{7,5},{8,10},{9,11},{10,... | collective-permute-start | bytes 786440 | tf_op jit(solution)/shard_map/ppermute | solution.py:244
  33.0 12.7 %collective-permute-start.5 = (bf16[16,64,256]{2,1,0:T(8,128)(2,1)S(1)}, bf16[16,64,256]{2,1,0:T(8,128)(2,1)}, u32[]{:S(2)}, u32[]{:S(2)}) collective-permute-start(bf16[16,64,256]{2,1,0:T(8,128)(2,1)S(1)} %merge_left.2.rest_0_), channel_id=1, source_target_pairs={{0,4},{1,5},{2,6},{3,7},{4,0},{5,1},{6,2},{7,3},{8,12},{9,13},{10,... | collective-permute-start | bytes 1572872 | tf_op jit(solution)/shard_map/ppermute | solution.py:244
  33.8 11.9 %collective-permute-start.7 = (bf16[16,64,256]{2,1,0:T(8,128)(2,1)}, bf16[16,64,256]{2,1,0:T(8,128)(2,1)}, u32[]{:S(2)}, u32[]{:S(2)}) collective-permute-start(bf16[16,64,256]{2,1,0:T(8,128)(2,1)} %collective-permute-done.4.rest_2_), channel_id=1, source_target_pairs={{0,0},{1,1},{2,2},{3,3},{4,8},{5,9},{6,10},{7,11},{8,4},{9,5},{10,... | collective-permute-start | bytes 1572872 | tf_op jit(solution)/shard_map/ppermute | solution.py:244
  39.3 0.8 copy-start.5
  40.1 15.8 %collective-permute-start.14 = (bf16[16,64,256]{2,1,0:T(8,128)(2,1)S(1)}, bf16[16,64,256]{2,1,0:T(8,128)(2,1)}, u32[]{:S(2)}, u32[]{:S(2)}) collective-permute-start(bf16[16,64,256]{2,1,0:T(8,128)(2,1)S(1)} %merge_right.3.rest_1_), channel_id=1, source_target_pairs={{0,4},{1,5},{2,6},{3,7},{4,0},{5,1},{6,2},{7,3},{8,12},{9,13},{10,... | collective-permute-start | bytes 1572872 | tf_op jit(solution)/shard_map/ppermute | solution.py:244
  40.1 10.8 %collective-permute-start.13 = (bf16[16,32,256]{2,1,0:T(8,128)(2,1)}, bf16[16,32,256]{2,1,0:T(8,128)(2,1)}, u32[]{:S(2)}, u32[]{:S(2)}) collective-permute-start(bf16[16,32,256]{2,1,0:T(8,128)(2,1)} %get-tuple-element.66), channel_id=1, source_target_pairs={{0,2},{1,3},{2,0},{3,1},{4,6},{5,7},{6,4},{7,5},{8,10},{9,11},{10,... | collective-permute-start | bytes 786440 | tf_op jit(solution)/shard_map/ppermute | solution.py:244
  41.3 1.2 %copy-start.1 = (bf16[4096,128]{1,0:T(8,128)(2,1)S(1)}, bf16[4096,128]{1,0:T(8,128)(2,1)}, u32[]{:S(2)}) copy-start(bf16[4096,128]{1,0:T(8,128)(2,1)} %copy-done) | copy-start | bytes 3145732
  42.6 1.5 %copy-start.3 = (bf16[16,64,256]{2,1,0:T(8,128)(2,1)S(1)}, bf16[16,64,256]{2,1,0:T(8,128)(2,1)}, u32[]{:S(2)}) copy-start(bf16[16,64,256]{2,1,0:T(8,128)(2,1)} %copy-done.2) | copy-start | bytes 1572868
  42.6 3.1 %copy-start.6 = (bf16[16,64,256]{2,1,0:T(8,128)(2,1)S(1)}, bf16[16,64,256]{2,1,0:T(8,128)(2,1)}, u32[]{:S(2)}) copy-start(bf16[16,64,256]{2,1,0:T(8,128)(2,1)} %copy-done.5) | copy-start | bytes 1572868
  47.4 13.9 %collective-permute-start.8 = (bf16[16,64,128]{2,1,0:T(8,128)(2,1)S(1)}, bf16[16,64,128]{2,1,0:T(8,128)(2,1)S(1)}, u32[]{:S(2)}, u32[]{:S(2)}) collective-permute-start(bf16[16,64,128]{2,1,0:T(8,128)(2,1)S(1)} %get-tuple-element.57), channel_id=1, source_target_pairs={{0,4},{1,5},{2,6},{3,7},{4,0},{5,1},{6,2},{7,3},{8,12},{9,13},{10,... | collective-permute-start | bytes 786440 | tf_op jit(solution)/shard_map/ppermute | solution.py:244
  50.2 25.1 %collective-permute-start.16 = (bf16[16,64,256]{2,1,0:T(8,128)(2,1)S(1)}, bf16[16,64,256]{2,1,0:T(8,128)(2,1)S(1)}, u32[]{:S(2)}, u32[]{:S(2)}) collective-permute-start(bf16[16,64,256]{2,1,0:T(8,128)(2,1)S(1)} %merge_right.3.rest_1_), channel_id=1, source_target_pairs={{0,0},{1,1},{2,2},{3,3},{4,8},{5,9},{6,10},{7,11},{8,4},{9,5},{10,... | collective-permute-start | bytes 1572872 | tf_op jit(solution)/shard_map/ppermute | solution.py:244
  55.8 19.5 %collective-permute-start.15 = (bf16[16,64,256]{2,1,0:T(8,128)(2,1)S(1)}, bf16[16,64,256]{2,1,0:T(8,128)(2,1)S(1)}, u32[]{:S(2)}, u32[]{:S(2)}) collective-permute-start(bf16[16,64,256]{2,1,0:T(8,128)(2,1)S(1)} %merge_left.3.rest_0_), channel_id=1, source_target_pairs={{0,4},{1,5},{2,6},{3,7},{4,0},{5,1},{6,2},{7,3},{8,12},{9,13},{10,... | collective-permute-start | bytes 1572872 | tf_op jit(solution)/shard_map/ppermute | solution.py:244
  56.4 19.0 %collective-permute-start.17 = (bf16[16,64,256]{2,1,0:T(8,128)(2,1)}, bf16[16,64,256]{2,1,0:T(8,128)(2,1)S(1)}, u32[]{:S(2)}, u32[]{:S(2)}) collective-permute-start(bf16[16,64,256]{2,1,0:T(8,128)(2,1)} %collective-permute-done.14.rest_2_), channel_id=1, source_target_pairs={{0,0},{1,1},{2,2},{3,3},{4,8},{5,9},{6,10},{7,11},{8,4},{9,5},{10,... | collective-permute-start | bytes 1572872 | tf_op jit(solution)/shard_map/ppermute | solution.py:244
  62.0 6.4 %collective-permute-start.9 = (bf16[16,32,128]{2,1,0:T(8,128)(2,1)S(1)}, bf16[16,32,128]{2,1,0:T(8,128)(2,1)S(1)}, u32[]{:S(2)}, u32[]{:S(2)}) collective-permute-start(bf16[16,32,128]{2,1,0:T(8,128)(2,1)S(1)} %get-tuple-element.59), channel_id=1, source_target_pairs={{0,1},{1,0},{2,3},{3,2},{4,5},{5,4},{6,7},{7,6},{8,9},{9,8},{10,11... | collective-permute-start | bytes 393224 | tf_op jit(solution)/shard_map/ppermute | solution.py:244
  67.3 5.1 %collective-permute-start.10 = (bf16[16,32,128]{2,1,0:T(8,128)(2,1)S(1)}, bf16[16,32,128]{2,1,0:T(8,128)(2,1)S(1)}, u32[]{:S(2)}, u32[]{:S(2)}) collective-permute-start(bf16[16,32,128]{2,1,0:T(8,128)(2,1)S(1)} %get-tuple-element.60), channel_id=1, source_target_pairs={{0,2},{1,3},{2,0},{3,1},{4,6},{5,7},{6,4},{7,5},{8,10},{9,11},{10,... | collective-permute-start | bytes 393224 | tf_op jit(solution)/shard_map/ppermute | solution.py:244
  68.5 19.2 %copy-start.15 = (f32[128]{0:T(128)S(1)}, f32[128]{0:T(128)}, u32[]{:S(2)}) copy-start(f32[128]{0:T(128)} %param.12) | copy-start | bytes 1540
  68.5 6.9 %collective-permute-start.11 = (bf16[16,32,128]{2,1,0:T(8,128)(2,1)S(1)}, bf16[16,32,128]{2,1,0:T(8,128)(2,1)S(1)}, u32[]{:S(2)}, u32[]{:S(2)}) collective-permute-start(bf16[16,32,128]{2,1,0:T(8,128)(2,1)S(1)} %get-tuple-element.61), channel_id=1, source_target_pairs={{0,3},{1,2},{2,1},{3,0},{4,7},{5,6},{6,5},{7,4},{8,11},{9,10},{10,... | collective-permute-start | bytes 393224 | tf_op jit(solution)/shard_map/ppermute | solution.py:244
  75.3 12.3 %copy-start.7 = (bf16[16,32,128]{2,1,0:T(8,128)(2,1)}, bf16[16,32,128]{2,1,0:T(8,128)(2,1)S(1)}, u32[]{:S(2)}) copy-start(bf16[16,32,128]{2,1,0:T(8,128)(2,1)S(1)} %collective-permute-done.11.rest_3_) | copy-start | bytes 393220
  76.4 7.4 %collective-permute-start.18 = (bf16[16,64,128]{2,1,0:T(8,128)(2,1)S(1)}, bf16[16,64,128]{2,1,0:T(8,128)(2,1)S(1)}, u32[]{:S(2)}, u32[]{:S(2)}) collective-permute-start(bf16[16,64,128]{2,1,0:T(8,128)(2,1)S(1)} %get-tuple-element.72), channel_id=1, source_target_pairs={{0,4},{1,5},{2,6},{3,7},{4,0},{5,1},{6,2},{7,3},{8,12},{9,13},{10,... | collective-permute-start | bytes 786440 | tf_op jit(solution)/shard_map/ppermute | solution.py:244
  84.5 3.3 %collective-permute-start.19 = (bf16[16,32,128]{2,1,0:T(8,128)(2,1)S(1)}, bf16[16,32,128]{2,1,0:T(8,128)(2,1)S(1)}, u32[]{:S(2)}, u32[]{:S(2)}) collective-permute-start(bf16[16,32,128]{2,1,0:T(8,128)(2,1)S(1)} %get-tuple-element.74), channel_id=1, source_target_pairs={{0,1},{1,0},{2,3},{3,2},{4,5},{5,4},{6,7},{7,6},{8,9},{9,8},{10,11... | collective-permute-start | bytes 393224 | tf_op jit(solution)/shard_map/ppermute | solution.py:244
  86.0 5.1 %collective-permute-start.20 = (bf16[16,32,128]{2,1,0:T(8,128)(2,1)S(1)}, bf16[16,32,128]{2,1,0:T(8,128)(2,1)S(1)}, u32[]{:S(2)}, u32[]{:S(2)}) collective-permute-start(bf16[16,32,128]{2,1,0:T(8,128)(2,1)S(1)} %get-tuple-element.75), channel_id=1, source_target_pairs={{0,2},{1,3},{2,0},{3,1},{4,6},{5,7},{6,4},{7,5},{8,10},{9,11},{10,... | collective-permute-start | bytes 393224 | tf_op jit(solution)/shard_map/ppermute | solution.py:244
  87.2 6.8 %collective-permute-start.21 = (bf16[16,32,128]{2,1,0:T(8,128)(2,1)S(1)}, bf16[16,32,128]{2,1,0:T(8,128)(2,1)S(1)}, u32[]{:S(2)}, u32[]{:S(2)}) collective-permute-start(bf16[16,32,128]{2,1,0:T(8,128)(2,1)S(1)} %get-tuple-element.76), channel_id=1, source_target_pairs={{0,3},{1,2},{2,1},{3,0},{4,7},{5,6},{6,5},{7,4},{8,11},{9,10},{10,... | collective-permute-start | bytes 393224 | tf_op jit(solution)/shard_map/ppermute | solution.py:244
  94.0 0.9 copy-start.8
  94.9 0.8 copy-start.13

commit v4 on v3

--- a/solution.py
+++ b/solution.py
@@ -10,7 +10,7 @@
 F32, BF16 = jnp.float32, jnp.bfloat16
 LANES = 128
 LIMIT = 40 * 1024 * 1024
-SHARES = (2, 2)
+SHARES = (5, 3)
 NT = (((1,), (1,)), ((), ()))
 TN = (((0,), (0,)), ((), ()))
 SMEM = pl.BlockSpec(memory_space=pltpu.SMEM)
@@ -137,21 +137,20 @@
         out[pl.ds(at * GROUP, GROUP)] = (0.5 * jnp.tanh(0.5 * logits) + 0.5).reshape(GROUP, toks, -1)
 
 
-def merge_kernel(start, own, neighbour, out):
-    rows = own.shape[1]
-    own_at = pl.multiple_of(start[0] * rows, rows)
-    out[:, pl.ds(own_at, rows), :] = own[...]
-    out[:, pl.ds(rows - own_at, rows), :] = neighbour[...]
-
-
-def product_kernel(n_left, n_right, places, *rest):
-    lefts, rights = rest[:n_left], rest[n_left : n_left + n_right]
-    outs, held = rest[n_left + n_right : -1], rest[-1]
-    count, span, _ = lefts[0].shape
+def product_kernel(first, n_left, n_right, places, *rest):
+    lefts = [rest[2 * n : 2 * n + 2] for n in range(n_left)]
+    rest = rest[2 * n_left :]
+    rights = [rest[2 * n : 2 * n + 2] for n in range(n_right)]
+    outs, held = rest[2 * n_right : -1], rest[-1]
+    count, span, _ = outs[0].shape
+    rows = span // 2
     for s in range(n_right):
-        held[:, pl.ds(pl.multiple_of(places[s] * span, span), span), :] = rights[s][...]
+        for p in range(2):
+            start = pl.multiple_of(places[1 + s] * span + (places[0] ^ p) * rows, rows)
+            part = rights[s][p][...] if p else rights[s][p][first : first + count]
+            held[:, pl.ds(start, rows), :] = part
     for c in range(count):
-        left = jnp.concatenate([x[c] for x in lefts], axis=0)
+        left = jnp.concatenate([x for own, other in lefts for x in (own[first + c], other[c])], axis=0)
         out = lax.dot_general(left, held[c], NT, preferred_element_type=F32).astype(BF16)
         for n in range(n_left):
             outs[n][c] = out[n * span : (n + 1) * span]
@@ -233,8 +232,6 @@
     own_half = z // half
     at_end = (z == 0) | (z == planes - 1)
     where = jnp.stack([2 * y + core, at_end, core ^ own_half]).astype(jnp.int32)
-    start = y[None].astype(jnp.int32)
-    zero = jnp.zeros((1,), jnp.int32)
 
     def send(x, target):
         pairs = []
@@ -253,11 +250,11 @@
         return lambda p, b, k: (p // half * half + (p + s) % half, b, k)
 
     def mirrored(p, b, k):
-        return (p if p in (0, planes - 1) else planes - 1 - p, b, k)
+        return (p, b, 1 - k) if p in (0, planes - 1) else (planes - 1 - p, b, k)
 
     def edge(p, b, k):
         swap = {0: 1, 1: 0, planes - 1: planes - 2, planes - 2: planes - 1}
-        return (swap.get(p, p), b, k)
+        return (swap[p], b, k) if p in swap else (p, b, 1 - k)
 
     gains = in_gain.reshape(1, -1)
     twin, twin_mask = send(pair, in_plane(1)), send(pair_mask, in_plane(1))
@@ -272,7 +269,7 @@
     *mine, normed0, chosen_right, chosen_left = kernel(
         right_own_kernel,
         "right_own",
-        [piece(count, rows, toks) for _ in range(2) for count in counts] + [rows_all, weights, weights],
+        [piece(count, rows, toks) for count in (part, *counts)] + [rows_all, weights, weights],
         [SMEM] + [HBM] * 4,
         [
             pltpu.VMEM(pair.shape, BF16),
@@ -285,57 +282,70 @@
             pltpu.SemaphoreType.DMA((copies,)),
         ],
     )(where, pair, pair_mask, gains, proj_weight)
-    whole = [piece(count, rows, 2 * toks) for _ in range(2) for count in counts]
+    whole = [piece(count, rows, 2 * toks) for count in (part, *counts)]
     *right, normed1 = kernel(
         right_twin_kernel, "right_twin", whole + [rows_all], [VMEM] * (4 + len(mine)), [held]
     )(twin, twin_mask, gains, chosen_right, *mine)
-    right0, right1 = list(right[: len(counts)]), list(right[len(counts) :])
-    right1[0] = send(right1[0], in_plane(2))
+    right0, right1 = right[0], list(right[1:])
+    queues = {"y": [], "end": [], "mid": []}
+
+    def queued(link, x, target, window=2, also=()):
+        done = queues[link]
+        early = done[len(done) - window :][:1] if len(done) >= window else []
+        done.append(send(after(x, *early, *also), target))
+        return done[-1]
+
+    def shift_all(x, link, target):
+        return [x] + [queued(link, x, target(s)) for s in range(1, half)]
+
+    far0 = [queued("mid", right0, mirrored)]
+    near0 = shift_all(right0, "end", shifted)
+    right1[0] = queued("y", right1[0], in_plane(2), 1)
     left = kernel(left_kernel, "left", whole, [VMEM] * 5, [held])(
         normed0, normed1, pair_mask, twin_mask, chosen_left
     )
-    left0, left1 = list(left[: len(counts)]), list(left[len(counts) :])
+    left0, left1 = left[0], list(left[1:])
+    far0 += [queued("mid", x, mirrored) for x in near0[1:]]
+    outer0 = queued("end", left0, edge)
+    left1[0] = queued("y", left1[0], in_plane(2), 1)
+    for g in groups[1:]:
+        right1[g] = queued("y", right1[g], in_plane(2), 1)
+        left1[g] = queued("y", left1[g], in_plane(2), 1)
     gate = kernel(
         gate_kernel, "gate", jax.ShapeDtypeStruct((rows, toks, channels), F32), [VMEM] * 2
     )(normed0, gate_weight)
 
-    def merge(own, neighbour, at, name):
-        shape = piece(own.shape[0], 2 * rows, 2 * toks)
-        return kernel(merge_kernel, name, shape, [SMEM, VMEM, VMEM])(at, own, neighbour)
-
-    def products(lefts, rights, places, name):
+    def products(first, lefts, rights, places, name):
         span = 2 * rows * len(rights)
-        count = lefts[0].shape[0]
+        count = lefts[0][1].shape[0]
         return kernel(
-            functools.partial(product_kernel, len(lefts), len(rights)),
+            functools.partial(product_kernel, first, len(lefts), len(rights)),
             name,
             [piece(count, 2 * rows, span)] * len(lefts),
-            [SMEM] + [VMEM] * (len(lefts) + len(rights)),
+            [SMEM] + [VMEM] * (2 * (len(lefts) + len(rights))),
             [pltpu.VMEM((count, span, 2 * toks), BF16)],
-        )(places, *lefts, *rights)
+        )(places, *[x for pairs in (*lefts, *rights) for x in pairs])
 
     steps = jnp.arange(half)
-    places_near = ((z - steps) % half).astype(jnp.int32)
-    places_far = ((planes - 1 - z - steps) % half).astype(jnp.int32)
-    done_y, done_z, done = [right1[0]], [], [gate]
-    pieces = []
+    places_near = jnp.concatenate([y[None], (z - steps) % half]).astype(jnp.int32)
+    places_far = jnp.concatenate([y[None], (planes - 1 - z - steps) % half]).astype(jnp.int32)
+    near1, far1, outer1 = [], [], []
     for g in groups:
-        if g:
-            right1[g] = send(after(right1[g], *done_y), in_plane(2))
-            done_y = [right1[g]]
-        left1[g] = send(after(left1[g], *done_y), in_plane(2))
-        done_y = [left1[g]]
-        own = merge(right0[g], right1[g], start, "merge_right")
-        own = after(own, *done_z)
-        far = [send(own, mirrored)]
-        near = [own] + [send(own, shifted(s)) for s in range(1, half)]
-        far += [send(x, mirrored) for x in near[1:]]
-        left = merge(left0[g], left1[g], zero, "merge_left")
-        done_z = [far[0], near[-1], left]
-        outer = send(after(left, near[-1]), edge)
-        (close,) = products([left], near, places_near, "near")
-        away, ends = products([after(left, close, *done), outer], far, places_far, "away")
-        ends = send(ends, edge)
+        far = [queued("mid", right1[g], mirrored)]
+        near1.append(shift_all(right1[g], "end", shifted))
+        far1.append(far + [queued("mid", x, mirrored) for x in near1[g][1:]])
+        outer1.append(queued("end", left1[g], edge))
+    done, pieces, first = [gate], [], 0
+    for g in groups:
+        crossed = [x[g + 1] for x in (right1, left1) if g < groups[-1]]
+        moved = [x[g + 1][n] for x, n in ((far1, 0), (near1, -1)) if g < groups[-1]]
+        mine = (left0, after(left1[g], *crossed))
+        (close,) = products(first, [mine], list(zip(near0, near1[g])), places_near, "near")
+        mine = (left0, after(left1[g], close, *done))
+        away, ends = products(
+            first, [mine, (outer0, outer1[g])], list(zip(far0, far1[g])), places_far, "away"
+        )
+        ends = after(send(ends, edge), *moved)
         handed = kernel(
             hand_out_kernel,
             "hand_out",
@@ -344,6 +354,7 @@
         )(where, close, away, ends)
         done = [handed[0]] + [send(handed[r], in_plane(r)) for r in range(1, 4)]
         pieces += done
+        first += counts[g]
 
     return kernel(
         update_kernel,

time: 99.8 us -> 105 us (1.052)
  waiting for transfers between devices: 33.8 us -> 42.2 us
  starting transfers between devices: 32.9 us -> 30.1 us
    ppermute x22 -> x26, waiting for transfers between devices: 33.8 us -> 42.2 us  [send(): return lax.ppermute(x, ('row', 'chan'), pairs)]
    ppermute x22 -> x26, starting transfers between devices: 32.9 us -> 30.1 us  [send(): return lax.ppermute(x, ('row', 'chan'), pairs)]
    unnamed x32 -> x36, local copies, waits for them, and re-layouts: 7.23 us -> 7.02 us
    pallas_call x9 -> x5, Pallas kernels: 11.2 us -> 11.4 us  [the longest x4 7.22 us: products(): kernel(functools.partial(product_kernel, first, len(lefts), len(rights)),...]
  transfers between devices with their start and end apart: 22 -> 26, of which waited for: 10 -> 10; matrix products, arithmetic and copies ran while one was open for 0% -> 0% of each run, Pallas kernels for 16% -> 13%
where the time goes in v4:
time: 105 us; the launch traced here: 104 us
  waiting for transfers between devices  42.2 us (40%)
  starting transfers between devices  30.1 us (29%)
  Pallas kernels  24.5 us (23%)
  local copies, waits for them, and re-layouts  7.14 us (7%)
    ppermute x26, waiting for transfers between devices, send(): return lax.ppermute(x, ('row', 'chan'), pairs)  42.2 us
    ppermute x26, starting transfers between devices, send(): return lax.ppermute(x, ('row', 'chan'), pairs)  30.1 us
    pallas_call x4, Pallas kernels, products(): kernel(functools.partial(product_kernel, first, len(lefts), len(rights)),...  7.22 us
    unnamed x36, local copies, waits for them, and re-layouts  7.02 us
    pallas_call x1, Pallas kernels, local(): kernel(right_own_kernel, 'right_own', [piece(count, rows, toks) for count...  4.18 us
    pallas_call x1, Pallas kernels, local(): kernel(left_kernel, 'left', whole, [VMEM] * 5, [held])  3.91 us
    pallas_call x1, Pallas kernels, local(): kernel(right_twin_kernel, 'right_twin', whole + [rows_all], [VMEM] * (4 +...  3.31 us
    pallas_call x1, Pallas kernels, local(): kernel(update_kernel, 'update', jax.ShapeDtypeStruct((rows, toks, channel...  3.06 us
  transfers between devices with their start and end apart: 26, of which 10 were waited for; matrix products, arithmetic and copies ran while one was open for 0% of the time, Pallas kernels for 13%

profile of v4, /device:TPU:1, one launch (start us, length us, event | category | flops | bytes accessed | tf_op | source)
XLA Modules:
  0.0 104.4 jit_solution(3506871145633277332)
XLA Ops:
  0.0 0.1 collective-permute-start
  0.1 0.5 collective-permute-start.1
  0.5 0.1 pad_add_fusion.where
  0.6 1.2 %copy-done.2 = bf16[32,128,128]{2,1,0:T(8,128)(2,1)S(1)} copy-done((bf16[32,128,128]{2,1,0:T(8,128)(2,1)S(1)}, bf16[32,128,128]{2,1,0:T(8,128)(2,1)}, u32[]{:S(2)}) %copy-start.2) | copy-done | bytes 1048600
  1.8 0.9 copy-done.7
  2.7 0.7 copy-done.8
  3.4 0.7 copy-done.12
  4.1 4.2 %right_own.1 = (bf16[32,32,128]{2,1,0:T(8,128)(2,1)S(1)}, bf16[20,32,128]{2,1,0:T(8,128)(2,1)S(1)}, bf16[12,32,128]{2,1,0:T(8,128)(2,1)S(1)}, bf16[4096,128]{1,0...) custom-call(s32[3]{0:T(128)S(1)} %pad_add_fusion.where, ...), custom_call_target="tpu_custom_call" | custom-call | tf_op jit(solution)/shard_map/right_own/pallas_call | solution.py:269
  8.3 0.0 copy-start
  8.3 0.0 copy-start.10
  8.3 0.0 collective-permute-done.1.mask.mask1
  8.3 3.3 %right_twin.1 = (bf16[32,32,256]{2,1,0:T(8,128)(2,1)S(1)}, bf16[20,32,256]{2,1,0:T(8,128)(2,1)S(1)}, bf16[12,32,256]{2,1,0:T(8,128)(2,1)S(1)}, bf16[4096,128]{1,0:T(8,128)(2,1)S(1)}) custom-call(bf16[32,128,128]{2,1,0:T(8,128)(2,1)S(1)} %collective-permute-done.pair, s32[32,128]{1,0:T(8,128)S(1)} %collective-permute-done.1.mask.mask1, f32[1,128]{1,0:T(1,128)S(1)} %bitcast.7, ...), custom_call_target="tpu_custom_call" | custom-call | tf_op jit(solution)/shard_map/right_twin/pallas_call | solution.py:286
  11.7 2.4 %collective-permute-start.6 = (bf16[32,32,256]{2,1,0:T(8,128)(2,1)S(1)}, bf16[32,32,256]{2,1,0:T(8,128)(2,1)}, u32[]{:S(2)}, u32[]{:S(2)}) collective-permute-start(bf16[32,32,256]{2,1,0:T(8,128)(2,1)S(1)} %get-tuple-element.61.rest_2_), channel_id=1, source_target_pairs={{0,4},{1,5},{2,6},{3,7},{4,0},{5,1},{6,2},{7,3},{8,12},{9,13},{10,... | collective-permute-start | bytes 1572872 | tf_op jit(solution)/shard_map/ppermute | solution.py:241
  14.1 1.2 %collective-permute-start.2 = (bf16[20,32,256]{2,1,0:T(8,128)(2,1)S(1)}, bf16[20,32,256]{2,1,0:T(8,128)(2,1)}, u32[]{:S(2)}, u32[]{:S(2)}) collective-permute-start(bf16[20,32,256]{2,1,0:T(8,128)(2,1)S(1)} %get-tuple-element.54), channel_id=1, source_target_pairs={{0,2},{1,3},{2,0},{3,1},{4,6},{5,7},{6,4},{7,5},{8,10},{9,11},{10,... | collective-permute-start | bytes 983048 | tf_op jit(solution)/shard_map/ppermute | solution.py:241
  15.3 1.0 collective-permute-start.10
  16.3 3.9 %left.1 = (bf16[32,32,256]{2,1,0:T(8,128)(2,1)S(1)}, bf16[20,32,256]{2,1,0:T(8,128)(2,1)}, bf16[12,32,256]{2,1,0:T(8,128)(2,1)S(1)}) custom-call(bf16[4096,128]{1,0:T(8,128)(2,1)S(1)} %get-tuple-element.45.normed.normed0, bf16[4096,128]{1,0:T(8,128)(2,1)S(1)} %get-tuple-element.50.normed1, s32[32,128]{1,0:T(8,128)S(1)} %copy-done.9, ...), custom_call_target="tpu_custom_call" | custom-call | tf_op jit(solution)/shard_map/left/pallas_call | solution.py:304
  20.2 0.7 copy-done.15
  20.9 1.6 %collective-permute-start.8 = (bf16[32,32,256]{2,1,0:T(8,128)(2,1)S(1)}, bf16[32,32,256]{2,1,0:T(8,128)(2,1)}, u32[]{:S(2)}, u32[]{:S(2)}) collective-permute-start(bf16[32,32,256]{2,1,0:T(8,128)(2,1)S(1)} %get-tuple-element.52.rest_0_), channel_id=1, source_target_pairs={{0,4},{1,5},{2,6},{3,7},{4,0},{5,1},{6,2},{7,3},{8,12},{9,13},{10,... | collective-permute-start | bytes 1572872 | tf_op jit(solution)/shard_map/ppermute | solution.py:241
  22.5 3.6 %collective-permute-done.6.rest_4_ = bf16[32,32,256]{2,1,0:T(8,128)(2,1)} collective-permute-done((bf16[32,32,256]{2,1,0:T(8,128)(2,1)S(1)}, bf16[32,32,256]{2,1,0:T(8,128)(2,1)}, u32[]{:S(2)}, u32[]{:S(2)}) %collective-permute-start.6) | collective-permute-done | bytes 524320 | tf_op jit(solution)/shard_map/ppermute | solution.py:241
  26.1 1.5 %collective-permute-start.12 = (bf16[32,32,256]{2,1,0:T(8,128)(2,1)}, bf16[32,32,256]{2,1,0:T(8,128)(2,1)}, u32[]{:S(2)}, u32[]{:S(2)}) collective-permute-start(bf16[32,32,256]{2,1,0:T(8,128)(2,1)} %collective-permute-done.6.rest_4_), channel_id=1, source_target_pairs={{0,1},{1,0},{2,3},{3,2},{4,8},{5,9},{6,10},{7,11},{8,4},{9,5},{10,... | collective-permute-start | bytes 1572872 | tf_op jit(solution)/shard_map/ppermute | solution.py:241
  27.6 0.0 collective-permute-done.2.rest_3_
  27.6 1.7 %collective-permute-start.3 = (bf16[20,32,256]{2,1,0:T(8,128)(2,1)}, bf16[20,32,256]{2,1,0:T(8,128)(2,1)S(1)}, u32[]{:S(2)}, u32[]{:S(2)}) collective-permute-start(bf16[20,32,256]{2,1,0:T(8,128)(2,1)} %get-tuple-element.55), channel_id=1, source_target_pairs={{0,2},{1,3},{2,0},{3,1},{4,6},{5,7},{6,4},{7,5},{8,10},{9,11},{10,... | collective-permute-start | bytes 983048 | tf_op jit(solution)/shard_map/ppermute | solution.py:241
  29.4 0.4 collective-permute-start.7
  29.8 1.2 %copy-done.1 = bf16[4096,128]{1,0:T(8,128)(2,1)S(1)} copy-done((bf16[4096,128]{1,0:T(8,128)(2,1)S(1)}, bf16[4096,128]{1,0:T(8,128)(2,1)}, u32[]{:S(2)}) %copy-start.1) | copy-done | bytes 1048600
  31.0 1.5 %gate.1 = f32[32,128,128]{2,1,0:T(8,128)S(1)} custom-call(bf16[4096,128]{1,0:T(8,128)(2,1)S(1)} %copy-done.1, bf16[128,128]{1,0:T(8,128)(2,1)S(1)} %copy-done.10), custom_call_target="tpu_custom_call" | custom-call | tf_op jit(solution)/shard_map/gate/pallas_call | solution.py:314
  32.5 5.2 %collective-permute-done.3.rest_1_ = bf16[20,32,256]{2,1,0:T(8,128)(2,1)S(1)} collective-permute-done((bf16[20,32,256]{2,1,0:T(8,128)(2,1)}, bf16[20,32,256]{2,1,0:T(8,128)(2,1)S(1)}, u32[]{:S(2)}, u32[]{:S(2)}) %collective-permute-start.3) | collective-permute-done | bytes 327712 | tf_op jit(solution)/shard_map/ppermute | solution.py:241
  37.7 1.3 %collective-permute-start.4 = (bf16[12,32,256]{2,1,0:T(8,128)(2,1)S(1)}, bf16[12,32,256]{2,1,0:T(8,128)(2,1)S(1)}, u32[]{:S(2)}, u32[]{:S(2)}) collective-permute-start(bf16[12,32,256]{2,1,0:T(8,128)(2,1)S(1)} %copy-done.14), channel_id=1, source_target_pairs={{0,2},{1,3},{2,0},{3,1},{4,6},{5,7},{6,4},{7,5},{8,10},{9,11},{10,... | collective-permute-start | bytes 589832 | tf_op jit(solution)/shard_map/ppermute | solution.py:241
  39.0 1.1 %collective-permute-start.11 = (bf16[20,32,256]{2,1,0:T(8,128)(2,1)}, bf16[20,32,256]{2,1,0:T(8,128)(2,1)S(1)}, u32[]{:S(2)}, u32[]{:S(2)}) collective-permute-start(bf16[20,32,256]{2,1,0:T(8,128)(2,1)} %collective-permute-done.2.rest_3_), channel_id=1, source_target_pairs={{0,1},{1,0},{2,3},{3,2},{4,8},{5,9},{6,10},{7,11},{8,4},{9,5},{10,... | collective-permute-start | bytes 983048 | tf_op jit(solution)/shard_map/ppermute | solution.py:241
  40.1 4.3 %collective-permute-done.7.rest_5_ = bf16[20,32,256]{2,1,0:T(8,128)(2,1)} collective-permute-done((bf16[20,32,256]{2,1,0:T(8,128)(2,1)}, bf16[20,32,256]{2,1,0:T(8,128)(2,1)}, u32[]{:S(2)}, u32[]{:S(2)}) %collective-permute-start.7) | collective-permute-done | bytes 327712 | tf_op jit(solution)/shard_map/ppermute | solution.py:241
  44.4 1.5 %collective-permute-start.13 = (bf16[20,32,256]{2,1,0:T(8,128)(2,1)}, bf16[20,32,256]{2,1,0:T(8,128)(2,1)S(1)}, u32[]{:S(2)}, u32[]{:S(2)}) collective-permute-start(bf16[20,32,256]{2,1,0:T(8,128)(2,1)} %collective-permute-done.7.rest_5_), channel_id=1, source_target_pairs={{0,1},{1,0},{2,3},{3,2},{4,8},{5,9},{6,10},{7,11},{8,4},{9,5},{10,... | collective-permute-start | bytes 983048 | tf_op jit(solution)/shard_map/ppermute | solution.py:241
  45.9 1.8 %collective-permute-start.5 = (bf16[12,32,256]{2,1,0:T(8,128)(2,1)S(1)}, bf16[12,32,256]{2,1,0:T(8,128)(2,1)S(1)}, u32[]{:S(2)}, u32[]{:S(2)}) collective-permute-start(bf16[12,32,256]{2,1,0:T(8,128)(2,1)S(1)} %copy-done.16), channel_id=1, source_target_pairs={{0,2},{1,3},{2,0},{3,1},{4,6},{5,7},{6,4},{7,5},{8,10},{9,11},{10,... | collective-permute-start | bytes 589832 | tf_op jit(solution)/shard_map/ppermute | solution.py:241
  47.7 0.1 pad_add_fusion.1.places
  47.8 0.1 pad_add_fusion.2.places
  47.9 5.1 %collective-permute-done.5.rest_1_ = bf16[12,32,256]{2,1,0:T(8,128)(2,1)S(1)} collective-permute-done((bf16[12,32,256]{2,1,0:T(8,128)(2,1)S(1)}, bf16[12,32,256]{2,1,0:T(8,128)(2,1)S(1)}, u32[]{:S(2)}, u32[]{:S(2)}) %collective-permute-start.5) | collective-permute-done | bytes 196640 | tf_op jit(solution)/shard_map/ppermute | solution.py:241
  52.9 1.9 %near.2 = bf16[20,64,128]{2,1,0:T(8,128)(2,1)S(1)} custom-call(s32[3]{0:T(128)S(1)} %pad_add_fusion.1.places, bf16[32,32,256]{2,1,0:T(8,128)(2,1)S(1)} %get-tuple-element.52.rest_0_, bf16[20,32,256]{2,1,0:T(8,128)(2,1)S(1)} %collective-permute-done.3.rest_1_, bf16[32,32,256]{2,1,0:T(8,128)(2,1)S(1)} %get-tuple-element.61.rest_2_, ...), custom_call_target="tpu_custom_call" | custom-call | tf_op jit(solution)/shard_map/near/pallas_call | solution.py:321
  54.9 2.0 %away.2 = (bf16[20,64,128]{2,1,0:T(8,128)(2,1)S(1)}, bf16[20,64,128]{2,1,0:T(8,128)(2,1)S(1)}) custom-call(s32[3]{0:T(128)S(1)} %pad_add_fusion.2.places, bf16[32,32,256]{2,1,0:T(8,128)(2,1)S(1)} %get-tuple-element.52.rest_0_, bf16[20,32,256]{2,1,0:T(8,128)(2,1)S(1)} %collective-permute-done.3.rest_1_, bf16[32,32,256]{2,1,0:T(8,128)(2,1)} %collective-permute-done.8.rest_2_, ...), custom_call_target="tpu_custom_call" | custom-call | tf_op jit(solution)/shard_map/away/pallas_call | solution.py:321
  56.8 0.1 collective-permute-start.14
  56.9 1.5 %collective-permute-start.16 = (bf16[12,32,256]{2,1,0:T(8,128)(2,1)S(1)}, bf16[12,32,256]{2,1,0:T(8,128)(2,1)S(1)}, u32[]{:S(2)}, u32[]{:S(2)}) collective-permute-start(bf16[12,32,256]{2,1,0:T(8,128)(2,1)S(1)} %collective-permute-done.4.rest_3_), channel_id=1, source_target_pairs={{0,4},{1,5},{2,6},{3,7},{4,0},{5,1},{6,2},{7,3},{8,12},{9,13},{10,... | collective-permute-start | bytes 589832 | tf_op jit(solution)/shard_map/ppermute | solution.py:241
  58.4 1.2 %collective-permute-start.15 = (bf16[12,32,256]{2,1,0:T(8,128)(2,1)S(1)}, bf16[12,32,256]{2,1,0:T(8,128)(2,1)S(1)}, u32[]{:S(2)}, u32[]{:S(2)}) collective-permute-start(bf16[12,32,256]{2,1,0:T(8,128)(2,1)S(1)} %collective-permute-done.4.rest_3_), channel_id=1, source_target_pairs={{0,1},{1,0},{2,3},{3,2},{4,8},{5,9},{6,10},{7,11},{8,4},{9,5},{10,... | collective-permute-start | bytes 589832 | tf_op jit(solution)/shard_map/ppermute | solution.py:241
  59.5 1.4 %collective-permute-start.20 = (bf16[12,32,256]{2,1,0:T(8,128)(2,1)S(1)}, bf16[12,32,256]{2,1,0:T(8,128)(2,1)S(1)}, u32[]{:S(2)}, u32[]{:S(2)}) collective-permute-start(bf16[12,32,256]{2,1,0:T(8,128)(2,1)S(1)} %collective-permute-done.5.rest_1_), channel_id=1, source_target_pairs={{0,4},{1,5},{2,6},{3,7},{4,0},{5,1},{6,2},{7,3},{8,12},{9,13},{10,... | collective-permute-start | bytes 589832 | tf_op jit(solution)/shard_map/ppermute | solution.py:241
  60.9 8.8 %collective-permute-done.16.rest_5_ = bf16[12,32,256]{2,1,0:T(8,128)(2,1)S(1)} collective-permute-done((bf16[12,32,256]{2,1,0:T(8,128)(2,1)S(1)}, bf16[12,32,256]{2,1,0:T(8,128)(2,1)S(1)}, u32[]{:S(2)}, u32[]{:S(2)}) %collective-permute-start.16) | collective-permute-done | bytes 196640 | tf_op jit(solution)/shard_map/ppermute | solution.py:241
  69.8 2.6 %collective-permute-start.21 = (bf16[12,32,256]{2,1,0:T(8,128)(2,1)S(1)}, bf16[12,32,256]{2,1,0:T(8,128)(2,1)S(1)}, u32[]{:S(2)}, u32[]{:S(2)}) collective-permute-start(bf16[12,32,256]{2,1,0:T(8,128)(2,1)S(1)} %collective-permute-done.16.rest_5_), channel_id=1, source_target_pairs={{0,1},{1,0},{2,3},{3,2},{4,8},{5,9},{6,10},{7,11},{8,4},{9,5},{10,... | collective-permute-start | bytes 589832 | tf_op jit(solution)/shard_map/ppermute | solution.py:241
  72.3 0.7 hand_out.2
  73.0 0.1 collective-permute-start.17
  73.1 1.6 %collective-permute-start.18 = (bf16[20,32,128]{2,1,0:T(8,128)(2,1)S(1)}, bf16[20,32,128]{2,1,0:T(8,128)(2,1)S(1)}, u32[]{:S(2)}, u32[]{:S(2)}) collective-permute-start(bf16[20,32,128]{2,1,0:T(8,128)(2,1)S(1)} %get-tuple-element.74), channel_id=1, source_target_pairs={{0,2},{1,3},{2,0},{3,1},{4,6},{5,7},{6,4},{7,5},{8,10},{9,11},{10,... | collective-permute-start | bytes 491528 | tf_op jit(solution)/shard_map/ppermute | solution.py:241
  74.6 0.6 collective-permute-start.19
  75.2 1.5 %near.3 = bf16[12,64,128]{2,1,0:T(8,128)(2,1)S(1)} custom-call(s32[3]{0:T(128)S(1)} %pad_add_fusion.1.places, bf16[32,32,256]{2,1,0:T(8,128)(2,1)S(1)} %get-tuple-element.52.rest_0_, bf16[12,32,256]{2,1,0:T(8,128)(2,1)S(1)} %collective-permute-done.5.rest_1_, bf16[32,32,256]{2,1,0:T(8,128)(2,1)S(1)} %get-tuple-element.61.rest_2_, ...), custom_call_target="tpu_custom_call" | custom-call | tf_op jit(solution)/shard_map/near/pallas_call | solution.py:321
  76.7 0.0 copy-start.17
  76.7 0.0 copy-start.11
  76.7 1.8 %collective-permute-done.18.rest_2_ = bf16[20,32,128]{2,1,0:T(8,128)(2,1)S(1)} collective-permute-done((bf16[20,32,128]{2,1,0:T(8,128)(2,1)S(1)}, bf16[20,32,128]{2,1,0:T(8,128)(2,1)S(1)}, u32[]{:S(2)}, u32[]{:S(2)}) %collective-permute-start.18) | collective-permute-done | bytes 163872 | tf_op jit(solution)/shard_map/ppermute | solution.py:241
  78.6 0.7 copy-done.3
  79.2 3.4 %collective-permute-done.19.rest_3_ = bf16[20,32,128]{2,1,0:T(8,128)(2,1)S(1)} collective-permute-done((bf16[20,32,128]{2,1,0:T(8,128)(2,1)S(1)}, bf16[20,32,128]{2,1,0:T(8,128)(2,1)S(1)}, u32[]{:S(2)}, u32[]{:S(2)}) %collective-permute-start.19) | collective-permute-done | bytes 163872 | tf_op jit(solution)/shard_map/ppermute | solution.py:241
  82.6 1.9 %away.3 = (bf16[12,64,128]{2,1,0:T(8,128)(2,1)S(1)}, bf16[12,64,128]{2,1,0:T(8,128)(2,1)S(1)}) custom-call(s32[3]{0:T(128)S(1)} %pad_add_fusion.2.places, bf16[32,32,256]{2,1,0:T(8,128)(2,1)S(1)} %get-tuple-element.52.rest_0_, bf16[12,32,256]{2,1,0:T(8,128)(2,1)S(1)} %collective-permute-done.5.rest_1_, bf16[32,32,256]{2,1,0:T(8,128)(2,1)} %collective-permute-done.8.rest_2_, ...), custom_call_target="tpu_custom_call" | custom-call | tf_op jit(solution)/shard_map/away/pallas_call | solution.py:321
  84.5 2.6 %collective-permute-start.22 = (bf16[12,64,128]{2,1,0:T(8,128)(2,1)S(1)}, bf16[12,64,128]{2,1,0:T(8,128)(2,1)S(1)}, u32[]{:S(2)}, u32[]{:S(2)}) collective-permute-start(bf16[12,64,128]{2,1,0:T(8,128)(2,1)S(1)} %get-tuple-element.80), channel_id=1, source_target_pairs={{0,4},{1,5},{2,6},{3,7},{4,0},{5,1},{6,2},{7,3},{8,12},{9,13},{10,... | collective-permute-start | bytes 589832 | tf_op jit(solution)/shard_map/ppermute | solution.py:241
  87.1 5.1 %collective-permute-done.22.end = bf16[12,64,128]{2,1,0:T(8,128)(2,1)S(1)} collective-permute-done((bf16[12,64,128]{2,1,0:T(8,128)(2,1)S(1)}, bf16[12,64,128]{2,1,0:T(8,128)(2,1)S(1)}, u32[]{:S(2)}, u32[]{:S(2)}) %collective-permute-start.22) | collective-permute-done | bytes 196640 | tf_op jit(solution)/shard_map/ppermute | solution.py:241
  92.3 0.7 hand_out.3
  92.9 0.8 collective-permute-start.23
  93.7 1.3 %collective-permute-start.24 = (bf16[12,32,128]{2,1,0:T(8,128)(2,1)S(1)}, bf16[12,32,128]{2,1,0:T(8,128)(2,1)S(1)}, u32[]{:S(2)}, u32[]{:S(2)}) collective-permute-start(bf16[12,32,128]{2,1,0:T(8,128)(2,1)S(1)} %get-tuple-element.83), channel_id=1, source_target_pairs={{0,2},{1,3},{2,0},{3,1},{4,6},{5,7},{6,4},{7,5},{8,10},{9,11},{10,... | collective-permute-start | bytes 294920 | tf_op jit(solution)/shard_map/ppermute | solution.py:241
  95.0 0.5 collective-permute-start.25
  95.4 0.1 copy.8.gain
  95.6 2.5 %collective-permute-done.24.rest_6_ = bf16[12,32,128]{2,1,0:T(8,128)(2,1)S(1)} collective-permute-done((bf16[12,32,128]{2,1,0:T(8,128)(2,1)S(1)}, bf16[12,32,128]{2,1,0:T(8,128)(2,1)S(1)}, u32[]{:S(2)}, u32[]{:S(2)}) %collective-permute-start.24) | collective-permute-done | bytes 98336 | tf_op jit(solution)/shard_map/ppermute | solution.py:241
  98.1 2.3 %collective-permute-done.25.rest_7_ = bf16[12,32,128]{2,1,0:T(8,128)(2,1)S(1)} collective-permute-done((bf16[12,32,128]{2,1,0:T(8,128)(2,1)S(1)}, bf16[12,32,128]{2,1,0:T(8,128)(2,1)S(1)}, u32[]{:S(2)}, u32[]{:S(2)}) %collective-permute-start.25) | collective-permute-done | bytes 98336 | tf_op jit(solution)/shard_map/ppermute | solution.py:241
  100.4 0.9 copy-done.6
  101.3 3.1 %update.1 = bf16[32,128,128]{2,1,0:T(8,128)(2,1)} custom-call(s32[3]{0:T(128)S(1)} %pad_add_fusion.where, f32[128,1]{1,0:T(8,128)S(1)} %copy.8.gain, bf16[128,128]{1,0:T(8,128)(2,1)S(1)} %copy-done.11, f32[32,128,128]{2,1,0:T(8,128)S(1)} %gate.1, bf16[20,32,128]{2,1,0:T(8,128)(2,1)S(1)} %get-tuple-element.72.rest_0_, ...), custom_call_target="tpu_custom_call" | custom-call | tf_op jit(solution)/shard_map/update/pallas_call | solution.py:359
  (41 shorter events, 0.1 us)
Async XLA Ops:
  0.0 16.3 %copy-start.9 = (s32[32,128]{1,0:T(8,128)S(1)}, s32[32,128]{1,0:T(8,128)}, u32[]{:S(2)}) copy-start(s32[32,128]{1,0:T(8,128)} %mask0.1) | copy-start | bytes 49156
  0.0 8.3 %collective-permute-start = (bf16[32,128,128]{2,1,0:T(8,128)(2,1)}, bf16[32,128,128]{2,1,0:T(8,128)(2,1)S(1)}, u32[]{:S(2)}, u32[]{:S(2)}) collective-permute-start(bf16[32,128,128]{2,1,0:T(8,128)(2,1)} %pair.1), channel_id=1, source_target_pairs={{0,1},{1,0},{2,3},{3,2},{4,5},{5,4},{6,7},{7,6},{8,9},{9,8},{10,11... | collective-permute-start | bytes 3145736 | tf_op jit(solution)/shard_map/ppermute | solution.py:241
  0.1 8.2 %collective-permute-start.1 = (s32[32,128]{1,0:T(8,128)}, s32[32,128]{1,0:T(8,128)S(1)}, u32[]{:S(2)}, u32[]{:S(2)}) collective-permute-start(s32[32,128]{1,0:T(8,128)} %mask0.1), channel_id=1, source_target_pairs={{0,1},{1,0},{2,3},{3,2},{4,5},{5,4},{6,7},{7,6},{8,9},{9,8},{10,11... | collective-permute-start | bytes 49160 | tf_op jit(solution)/shard_map/ppermute | solution.py:241
  0.6 1.2 %copy-start.2 = (bf16[32,128,128]{2,1,0:T(8,128)(2,1)S(1)}, bf16[32,128,128]{2,1,0:T(8,128)(2,1)}, u32[]{:S(2)}) copy-start(bf16[32,128,128]{2,1,0:T(8,128)(2,1)} %pair.1) | copy-start | bytes 3145732
  1.8 0.9 copy-start.7
  2.7 0.7 copy-start.8
  3.4 0.7 copy-start.12
  8.3 12.0 %copy-start = (bf16[4096,128]{1,0:T(8,128)(2,1)}, bf16[4096,128]{1,0:T(8,128)(2,1)S(1)}, u32[]{:S(2)}) copy-start(bf16[4096,128]{1,0:T(8,128)(2,1)S(1)} %get-tuple-element.45.normed.normed0) | copy-start | bytes 3145732
  8.3 21.5 %copy-start.10 = (bf16[128,128]{1,0:T(8,128)(2,1)S(1)}, bf16[128,128]{1,0:T(8,128)(2,1)}, u32[]{:S(2)}) copy-start(bf16[128,128]{1,0:T(8,128)(2,1)} %weight.4) | copy-start | bytes 98308
  11.6 16.0 %copy-start.13 = (bf16[12,32,256]{2,1,0:T(8,128)(2,1)}, bf16[12,32,256]{2,1,0:T(8,128)(2,1)S(1)}, u32[]{:S(2)}) copy-start(bf16[12,32,256]{2,1,0:T(8,128)(2,1)S(1)} %get-tuple-element.57) | copy-start | bytes 589828
  11.7 14.4 %collective-permute-start.6 = (bf16[32,32,256]{2,1,0:T(8,128)(2,1)S(1)}, bf16[32,32,256]{2,1,0:T(8,128)(2,1)}, u32[]{:S(2)}, u32[]{:S(2)}) collective-permute-start(bf16[32,32,256]{2,1,0:T(8,128)(2,1)S(1)} %get-tuple-element.61.rest_2_), channel_id=1, source_target_pairs={{0,4},{1,5},{2,6},{3,7},{4,0},{5,1},{6,2},{7,3},{8,12},{9,13},{10,... | collective-permute-start | bytes 1572872 | tf_op jit(solution)/shard_map/ppermute | solution.py:241
  14.1 13.6 %collective-permute-start.2 = (bf16[20,32,256]{2,1,0:T(8,128)(2,1)S(1)}, bf16[20,32,256]{2,1,0:T(8,128)(2,1)}, u32[]{:S(2)}, u32[]{:S(2)}) collective-permute-start(bf16[20,32,256]{2,1,0:T(8,128)(2,1)S(1)} %get-tuple-element.54), channel_id=1, source_target_pairs={{0,2},{1,3},{2,0},{3,1},{4,6},{5,7},{6,4},{7,5},{8,10},{9,11},{10,... | collective-permute-start | bytes 983048 | tf_op jit(solution)/shard_map/ppermute | solution.py:241
  15.3 23.6 %collective-permute-start.10 = (bf16[32,32,256]{2,1,0:T(8,128)(2,1)S(1)}, bf16[32,32,256]{2,1,0:T(8,128)(2,1)}, u32[]{:S(2)}, u32[]{:S(2)}) collective-permute-start(bf16[32,32,256]{2,1,0:T(8,128)(2,1)S(1)} %get-tuple-element.61.rest_2_), channel_id=1, source_target_pairs={{0,1},{1,0},{2,3},{3,2},{4,8},{5,9},{6,10},{7,11},{8,4},{9,5},{10,... | collective-permute-start | bytes 1572872 | tf_op jit(solution)/shard_map/ppermute | solution.py:241
  20.2 0.7 copy-start.15
  20.9 19.1 %collective-permute-start.8 = (bf16[32,32,256]{2,1,0:T(8,128)(2,1)S(1)}, bf16[32,32,256]{2,1,0:T(8,128)(2,1)}, u32[]{:S(2)}, u32[]{:S(2)}) collective-permute-start(bf16[32,32,256]{2,1,0:T(8,128)(2,1)S(1)} %get-tuple-element.52.rest_0_), channel_id=1, source_target_pairs={{0,4},{1,5},{2,6},{3,7},{4,0},{5,1},{6,2},{7,3},{8,12},{9,13},{10,... | collective-permute-start | bytes 1572872 | tf_op jit(solution)/shard_map/ppermute | solution.py:241
  26.1 18.3 %collective-permute-start.12 = (bf16[32,32,256]{2,1,0:T(8,128)(2,1)}, bf16[32,32,256]{2,1,0:T(8,128)(2,1)}, u32[]{:S(2)}, u32[]{:S(2)}) collective-permute-start(bf16[32,32,256]{2,1,0:T(8,128)(2,1)} %collective-permute-done.6.rest_4_), channel_id=1, source_target_pairs={{0,1},{1,0},{2,3},{3,2},{4,8},{5,9},{6,10},{7,11},{8,4},{9,5},{10,... | collective-permute-start | bytes 1572872 | tf_op jit(solution)/shard_map/ppermute | solution.py:241
  27.6 10.0 %collective-permute-start.3 = (bf16[20,32,256]{2,1,0:T(8,128)(2,1)}, bf16[20,32,256]{2,1,0:T(8,128)(2,1)S(1)}, u32[]{:S(2)}, u32[]{:S(2)}) collective-permute-start(bf16[20,32,256]{2,1,0:T(8,128)(2,1)} %get-tuple-element.55), channel_id=1, source_target_pairs={{0,2},{1,3},{2,0},{3,1},{4,6},{5,7},{6,4},{7,5},{8,10},{9,11},{10,... | collective-permute-start | bytes 983048 | tf_op jit(solution)/shard_map/ppermute | solution.py:241
  29.4 15.0 %collective-permute-start.7 = (bf16[20,32,256]{2,1,0:T(8,128)(2,1)}, bf16[20,32,256]{2,1,0:T(8,128)(2,1)}, u32[]{:S(2)}, u32[]{:S(2)}) collective-permute-start(bf16[20,32,256]{2,1,0:T(8,128)(2,1)} %collective-permute-done.2.rest_3_), channel_id=1, source_target_pairs={{0,4},{1,5},{2,6},{3,7},{4,0},{5,1},{6,2},{7,3},{8,12},{9,13},{10,... | collective-permute-start | bytes 983048 | tf_op jit(solution)/shard_map/ppermute | solution.py:241
  29.8 1.2 %copy-start.1 = (bf16[4096,128]{1,0:T(8,128)(2,1)S(1)}, bf16[4096,128]{1,0:T(8,128)(2,1)}, u32[]{:S(2)}) copy-start(bf16[4096,128]{1,0:T(8,128)(2,1)} %copy-done) | copy-start | bytes 3145732
  31.0 6.7 %copy-start.14 = (bf16[12,32,256]{2,1,0:T(8,128)(2,1)S(1)}, bf16[12,32,256]{2,1,0:T(8,128)(2,1)}, u32[]{:S(2)}) copy-start(bf16[12,32,256]{2,1,0:T(8,128)(2,1)} %copy-done.13) | copy-start | bytes 589828
  31.0 14.9 %copy-start.16 = (bf16[12,32,256]{2,1,0:T(8,128)(2,1)S(1)}, bf16[12,32,256]{2,1,0:T(8,128)(2,1)}, u32[]{:S(2)}) copy-start(bf16[12,32,256]{2,1,0:T(8,128)(2,1)} %copy-done.15) | copy-start | bytes 589828
  37.7 8.2 %collective-permute-start.4 = (bf16[12,32,256]{2,1,0:T(8,128)(2,1)S(1)}, bf16[12,32,256]{2,1,0:T(8,128)(2,1)S(1)}, u32[]{:S(2)}, u32[]{:S(2)}) collective-permute-start(bf16[12,32,256]{2,1,0:T(8,128)(2,1)S(1)} %copy-done.14), channel_id=1, source_target_pairs={{0,2},{1,3},{2,0},{3,1},{4,6},{5,7},{6,4},{7,5},{8,10},{9,11},{10,... | collective-permute-start | bytes 589832 | tf_op jit(solution)/shard_map/ppermute | solution.py:241
  39.0 15.9 %collective-permute-start.11 = (bf16[20,32,256]{2,1,0:T(8,128)(2,1)}, bf16[20,32,256]{2,1,0:T(8,128)(2,1)S(1)}, u32[]{:S(2)}, u32[]{:S(2)}) collective-permute-start(bf16[20,32,256]{2,1,0:T(8,128)(2,1)} %collective-permute-done.2.rest_3_), channel_id=1, source_target_pairs={{0,1},{1,0},{2,3},{3,2},{4,8},{5,9},{6,10},{7,11},{8,4},{9,5},{10,... | collective-permute-start | bytes 983048 | tf_op jit(solution)/shard_map/ppermute | solution.py:241
  40.1 14.8 %collective-permute-start.9 = (bf16[20,32,256]{2,1,0:T(8,128)(2,1)S(1)}, bf16[20,32,256]{2,1,0:T(8,128)(2,1)S(1)}, u32[]{:S(2)}, u32[]{:S(2)}) collective-permute-start(bf16[20,32,256]{2,1,0:T(8,128)(2,1)S(1)} %collective-permute-done.3.rest_1_), channel_id=1, source_target_pairs={{0,4},{1,5},{2,6},{3,7},{4,0},{5,1},{6,2},{7,3},{8,12},{9,13},{10,... | collective-permute-start | bytes 983048 | tf_op jit(solution)/shard_map/ppermute | solution.py:241
  44.4 10.5 %collective-permute-start.13 = (bf16[20,32,256]{2,1,0:T(8,128)(2,1)}, bf16[20,32,256]{2,1,0:T(8,128)(2,1)S(1)}, u32[]{:S(2)}, u32[]{:S(2)}) collective-permute-start(bf16[20,32,256]{2,1,0:T(8,128)(2,1)} %collective-permute-done.7.rest_5_), channel_id=1, source_target_pairs={{0,1},{1,0},{2,3},{3,2},{4,8},{5,9},{6,10},{7,11},{8,4},{9,5},{10,... | collective-permute-start | bytes 983048 | tf_op jit(solution)/shard_map/ppermute | solution.py:241
  45.9 7.0 %collective-permute-start.5 = (bf16[12,32,256]{2,1,0:T(8,128)(2,1)S(1)}, bf16[12,32,256]{2,1,0:T(8,128)(2,1)S(1)}, u32[]{:S(2)}, u32[]{:S(2)}) collective-permute-start(bf16[12,32,256]{2,1,0:T(8,128)(2,1)S(1)} %copy-done.16), channel_id=1, source_target_pairs={{0,2},{1,3},{2,0},{3,1},{4,6},{5,7},{6,4},{7,5},{8,10},{9,11},{10,... | collective-permute-start | bytes 589832 | tf_op jit(solution)/shard_map/ppermute | solution.py:241
  56.8 15.5 %collective-permute-start.14 = (bf16[20,64,128]{2,1,0:T(8,128)(2,1)S(1)}, bf16[20,64,128]{2,1,0:T(8,128)(2,1)S(1)}, u32[]{:S(2)}, u32[]{:S(2)}) collective-permute-start(bf16[20,64,128]{2,1,0:T(8,128)(2,1)S(1)} %get-tuple-element.68), channel_id=1, source_target_pairs={{0,4},{1,5},{2,6},{3,7},{4,0},{5,1},{6,2},{7,3},{8,12},{9,13},{10,... | collective-permute-start | bytes 983048 | tf_op jit(solution)/shard_map/ppermute | solution.py:241
  56.9 12.8 %collective-permute-start.16 = (bf16[12,32,256]{2,1,0:T(8,128)(2,1)S(1)}, bf16[12,32,256]{2,1,0:T(8,128)(2,1)S(1)}, u32[]{:S(2)}, u32[]{:S(2)}) collective-permute-start(bf16[12,32,256]{2,1,0:T(8,128)(2,1)S(1)} %collective-permute-done.4.rest_3_), channel_id=1, source_target_pairs={{0,4},{1,5},{2,6},{3,7},{4,0},{5,1},{6,2},{7,3},{8,12},{9,13},{10,... | collective-permute-start | bytes 589832 | tf_op jit(solution)/shard_map/ppermute | solution.py:241
  58.4 14.0 %collective-permute-start.15 = (bf16[12,32,256]{2,1,0:T(8,128)(2,1)S(1)}, bf16[12,32,256]{2,1,0:T(8,128)(2,1)S(1)}, u32[]{:S(2)}, u32[]{:S(2)}) collective-permute-start(bf16[12,32,256]{2,1,0:T(8,128)(2,1)S(1)} %collective-permute-done.4.rest_3_), channel_id=1, source_target_pairs={{0,1},{1,0},{2,3},{3,2},{4,8},{5,9},{6,10},{7,11},{8,4},{9,5},{10,... | collective-permute-start | bytes 589832 | tf_op jit(solution)/shard_map/ppermute | solution.py:241
  59.5 23.1 %collective-permute-start.20 = (bf16[12,32,256]{2,1,0:T(8,128)(2,1)S(1)}, bf16[12,32,256]{2,1,0:T(8,128)(2,1)S(1)}, u32[]{:S(2)}, u32[]{:S(2)}) collective-permute-start(bf16[12,32,256]{2,1,0:T(8,128)(2,1)S(1)} %collective-permute-done.5.rest_1_), channel_id=1, source_target_pairs={{0,4},{1,5},{2,6},{3,7},{4,0},{5,1},{6,2},{7,3},{8,12},{9,13},{10,... | collective-permute-start | bytes 589832 | tf_op jit(solution)/shard_map/ppermute | solution.py:241
  69.8 12.9 %collective-permute-start.21 = (bf16[12,32,256]{2,1,0:T(8,128)(2,1)S(1)}, bf16[12,32,256]{2,1,0:T(8,128)(2,1)S(1)}, u32[]{:S(2)}, u32[]{:S(2)}) collective-permute-start(bf16[12,32,256]{2,1,0:T(8,128)(2,1)S(1)} %collective-permute-done.16.rest_5_), channel_id=1, source_target_pairs={{0,1},{1,0},{2,3},{3,2},{4,8},{5,9},{6,10},{7,11},{8,4},{9,5},{10,... | collective-permute-start | bytes 589832 | tf_op jit(solution)/shard_map/ppermute | solution.py:241
  73.0 3.7 %collective-permute-start.17 = (bf16[20,32,128]{2,1,0:T(8,128)(2,1)S(1)}, bf16[20,32,128]{2,1,0:T(8,128)(2,1)S(1)}, u32[]{:S(2)}, u32[]{:S(2)}) collective-permute-start(bf16[20,32,128]{2,1,0:T(8,128)(2,1)S(1)} %get-tuple-element.73), channel_id=1, source_target_pairs={{0,1},{1,0},{2,3},{3,2},{4,5},{5,4},{6,7},{7,6},{8,9},{9,8},{10,11... | collective-permute-start | bytes 491528 | tf_op jit(solution)/shard_map/ppermute | solution.py:241
  73.1 5.5 %collective-permute-start.18 = (bf16[20,32,128]{2,1,0:T(8,128)(2,1)S(1)}, bf16[20,32,128]{2,1,0:T(8,128)(2,1)S(1)}, u32[]{:S(2)}, u32[]{:S(2)}) collective-permute-start(bf16[20,32,128]{2,1,0:T(8,128)(2,1)S(1)} %get-tuple-element.74), channel_id=1, source_target_pairs={{0,2},{1,3},{2,0},{3,1},{4,6},{5,7},{6,4},{7,5},{8,10},{9,11},{10,... | collective-permute-start | bytes 491528 | tf_op jit(solution)/shard_map/ppermute | solution.py:241
  74.6 8.0 %collective-permute-start.19 = (bf16[20,32,128]{2,1,0:T(8,128)(2,1)S(1)}, bf16[20,32,128]{2,1,0:T(8,128)(2,1)S(1)}, u32[]{:S(2)}, u32[]{:S(2)}) collective-permute-start(bf16[20,32,128]{2,1,0:T(8,128)(2,1)S(1)} %get-tuple-element.75), channel_id=1, source_target_pairs={{0,3},{1,2},{2,1},{3,0},{4,7},{5,6},{6,5},{7,4},{8,11},{9,10},{10,... | collective-permute-start | bytes 491528 | tf_op jit(solution)/shard_map/ppermute | solution.py:241
  76.7 18.7 %copy-start.17 = (f32[128]{0:T(128)S(1)}, f32[128]{0:T(128)}, u32[]{:S(2)}) copy-start(f32[128]{0:T(128)} %param.12) | copy-start | bytes 1540
  76.7 23.6 %copy-start.11 = (bf16[128,128]{1,0:T(8,128)(2,1)S(1)}, bf16[128,128]{1,0:T(8,128)(2,1)}, u32[]{:S(2)}) copy-start(bf16[128,128]{1,0:T(8,128)(2,1)} %weight.5) | copy-start | bytes 98308
  78.6 0.7 copy-start.3
  82.6 12.8 %copy-start.5 = (bf16[20,32,128]{2,1,0:T(8,128)(2,1)}, bf16[20,32,128]{2,1,0:T(8,128)(2,1)S(1)}, u32[]{:S(2)}) copy-start(bf16[20,32,128]{2,1,0:T(8,128)(2,1)S(1)} %collective-permute-done.19.rest_3_) | copy-start | bytes 491524
  82.6 17.8 %copy-start.4 = (bf16[20,32,128]{2,1,0:T(8,128)(2,1)S(1)}, bf16[20,32,128]{2,1,0:T(8,128)(2,1)}, u32[]{:S(2)}) copy-start(bf16[20,32,128]{2,1,0:T(8,128)(2,1)} %copy-done.3) | copy-start | bytes 491524
  84.5 7.8 %collective-permute-start.22 = (bf16[12,64,128]{2,1,0:T(8,128)(2,1)S(1)}, bf16[12,64,128]{2,1,0:T(8,128)(2,1)S(1)}, u32[]{:S(2)}, u32[]{:S(2)}) collective-permute-start(bf16[12,64,128]{2,1,0:T(8,128)(2,1)S(1)} %get-tuple-element.80), channel_id=1, source_target_pairs={{0,4},{1,5},{2,6},{3,7},{4,0},{5,1},{6,2},{7,3},{8,12},{9,13},{10,... | collective-permute-start | bytes 589832 | tf_op jit(solution)/shard_map/ppermute | solution.py:241
  92.9 2.6 %collective-permute-start.23 = (bf16[12,32,128]{2,1,0:T(8,128)(2,1)S(1)}, bf16[12,32,128]{2,1,0:T(8,128)(2,1)S(1)}, u32[]{:S(2)}, u32[]{:S(2)}) collective-permute-start(bf16[12,32,128]{2,1,0:T(8,128)(2,1)S(1)} %get-tuple-element.82), channel_id=1, source_target_pairs={{0,1},{1,0},{2,3},{3,2},{4,5},{5,4},{6,7},{7,6},{8,9},{9,8},{10,11... | collective-permute-start | bytes 294920 | tf_op jit(solution)/shard_map/ppermute | solution.py:241
  93.7 4.4 %collective-permute-start.24 = (bf16[12,32,128]{2,1,0:T(8,128)(2,1)S(1)}, bf16[12,32,128]{2,1,0:T(8,128)(2,1)S(1)}, u32[]{:S(2)}, u32[]{:S(2)}) collective-permute-start(bf16[12,32,128]{2,1,0:T(8,128)(2,1)S(1)} %get-tuple-element.83), channel_id=1, source_target_pairs={{0,2},{1,3},{2,0},{3,1},{4,6},{5,7},{6,4},{7,5},{8,10},{9,11},{10,... | collective-permute-start | bytes 294920 | tf_op jit(solution)/shard_map/ppermute | solution.py:241
  95.0 5.4 %collective-permute-start.25 = (bf16[12,32,128]{2,1,0:T(8,128)(2,1)S(1)}, bf16[12,32,128]{2,1,0:T(8,128)(2,1)S(1)}, u32[]{:S(2)}, u32[]{:S(2)}) collective-permute-start(bf16[12,32,128]{2,1,0:T(8,128)(2,1)S(1)} %get-tuple-element.84), channel_id=1, source_target_pairs={{0,3},{1,2},{2,1},{3,0},{4,7},{5,6},{6,5},{7,4},{8,11},{9,10},{10,... | collective-permute-start | bytes 294920 | tf_op jit(solution)/shard_map/ppermute | solution.py:241
  100.4 0.9 copy-start.6

commit v5 on v4

v5 whole, which is shorter than its diff:
```python
import functools
import math

import jax
import jax.numpy as jnp
from jax import lax
from jax.experimental import pallas as pl
from jax.experimental.pallas import tpu as pltpu
from jax.sharding import PartitionSpec as P

F32, BF16 = jnp.float32, jnp.bfloat16
LANES = 128
SPARE = 6 * 1024 * 1024
SHARES = (4, 4)
NT = (((1,), (1,)), ((), ()))
TN = (((0,), (0,)), ((), ()))
SMEM = pl.BlockSpec(memory_space=pltpu.SMEM)
VMEM = pl.BlockSpec(memory_space=pltpu.VMEM)
GROUP = 4
UNROLL = 2


def normalise(x, gain):
    mean = jnp.mean(x, axis=-1, keepdims=True)
    centered = x - mean
    var = jnp.mean(centered * centered, axis=-1, keepdims=True)
    return (centered * lax.rsqrt(var + 1e-05) * gain).astype(BF16)


def gated(normed, chosen, valid, first, held):
    toks = valid.shape[1]
    wide = chosen.shape[0] // 2
    rows = valid.shape[0]
    proj = lax.dot_general(chosen[...], normed, NT, preferred_element_type=F32)
    for g in range(normed.shape[0] // toks):
        mine = proj[:, g * toks : (g + 1) * toks]
        value = (jnp.tanh(mine[:wide]) + 1.0) * (valid[pl.ds(first + g, 1), :] * mine[wide:])
        for m in range(toks // LANES):
            spot = pl.ds(first + g, wide, stride=rows + 1)
            held[m, spot, :] = value[:, m * LANES : (m + 1) * LANES]


def write_pieces(outs, held, base):
    row = 0
    for out in outs:
        count, rows, _ = out.shape
        for c in range(count):
            for m in range(held.shape[0]):
                lanes = slice(base + m * LANES, base + (m + 1) * LANES)
                out[c, :, lanes] = held[m, row : row + rows, :].astype(BF16)
            row += rows + 1


def right_rows(pair, valid, gain, chosen, normed_out, held):
    rows, toks, _ = pair.shape

    @pl.loop(0, rows // GROUP, unroll=UNROLL)
    def _(at):
        first = at * GROUP
        x = pair[pl.ds(first, GROUP)].astype(F32).reshape(GROUP * toks, -1)
        normed = normalise(x, gain[0:1, :])
        normed_out[pl.ds(first * toks, GROUP * toks), :] = normed
        gated(normed, chosen, valid, first, held)


def right_own_kernel(where, pair, valid, gain, weight, *rest):
    *outs, normed_out, chosen_right, chosen_left, turned, held = rest
    hidden = weight.shape[1] // 4
    part = hidden // 4
    turned[...] = weight[...].T
    for n in range(4):
        chosen = chosen_left if n < 2 else chosen_right
        for p in range(2):
            start = pl.multiple_of(n * hidden + (where[0] ^ (2 * p)) * part, part)
            at = (2 * (n % 2) + p) * part
            chosen[at : at + part, :] = turned[pl.ds(start, part), :]
    right_rows(pair, valid, gain, chosen_right, normed_out, held)
    write_pieces(outs, held, 0)


def right_twin_kernel(pair, valid, gain, chosen, *rest):
    count = (len(rest) - 2) // 2
    before, outs, normed_out, held = rest[:count], rest[count:-2], rest[-2], rest[-1]
    for x, out in zip(before, outs):
        out[:, :, : x.shape[2]] = x[...]
    right_rows(pair, valid, gain, chosen, normed_out, held)
    write_pieces(outs, held, pair.shape[1])


def left_kernel(normed0, normed1, valid0, valid1, chosen, *rest):
    outs, held = rest[:-1], rest[-1]
    rows, toks = valid0.shape
    for n, (normed, valid) in enumerate(((normed0, valid0), (normed1, valid1))):

        @pl.loop(0, rows // GROUP, unroll=UNROLL)
        def _(at):
            first = at * GROUP
            gated(normed[pl.ds(first * toks, GROUP * toks), :], chosen, valid, first, held)

        write_pieces(outs, held, n * toks)


def gate_kernel(normed, weight, out):
    rows, toks, _ = out.shape

    @pl.loop(0, rows // GROUP, unroll=UNROLL)
    def _(at):
        x = normed[pl.ds(at * GROUP * toks, GROUP * toks), :]
        logits = jnp.dot(x, weight[...], preferred_element_type=F32)
        out[pl.ds(at * GROUP, GROUP)] = (0.5 * jnp.tanh(0.5 * logits) + 0.5).reshape(GROUP, toks, -1)


def product_kernel(first, n_left, n_right, places, *rest):
    lefts = [rest[2 * n : 2 * n + 2] for n in range(n_left)]
    rest = rest[2 * n_left :]
    rights = [rest[2 * n : 2 * n + 2] for n in range(n_right)]
    outs, held = rest[2 * n_right : -1], rest[-1]
    count, span, _ = outs[0].shape
    rows = span // 2
    for s in range(n_right):
        for p in range(2):
            start = pl.multiple_of(places[1 + s] * span + (places[0] ^ p) * rows, rows)
            held[:, pl.ds(start, rows), :] = rights[s][p][first : first + count]
    for c in range(count):
        left = jnp.concatenate([x[first + c] for side in lefts for x in side], axis=0)
        out = lax.dot_general(left, held[c], NT, preferred_element_type=F32).astype(BF16)
        for n in range(n_left):
            outs[n][c] = out[n * span : (n + 1) * span]


def hand_out_kernel(first, where, near, far, end, *outs):
    count, rows, _ = outs[0].shape
    for r in range(4):
        source = where[2] ^ (r % 2)
        span = slice((r // 2) * rows, (r // 2 + 1) * rows)

        @pl.when(source == 0)
        def _():
            outs[r][...] = near[first : first + count, span, :]

        @pl.when((source == 1) & (where[1] == 0))
        def _():
            outs[r][...] = far[:, span, :]

        @pl.when((source == 1) & (where[1] == 1))
        def _():
            outs[r][...] = end[:, span, :]


def update_kernel(where, scale, weight, gate, *rest):
    pieces, out, turned = rest[:-2], rest[-2], rest[-1]
    part = sum(x.shape[0] for x in pieces[::4])
    _, rows, toks = pieces[0].shape
    hidden = 4 * part
    pitch = hidden + 1
    for r in range(4):
        base = (where[0] ^ r) * part
        for piece in pieces[r::4]:
            for c in range(piece.shape[0]):
                value = piece[c].astype(F32)
                for m in range(toks // LANES):
                    turned[m, pl.ds(base + c, rows, stride=pitch), :] = value[
                        :, m * LANES : (m + 1) * LANES
                    ]
            base = base + piece.shape[0]

    @pl.loop(0, rows, unroll=8)
    def _(i):
        x = jnp.concatenate(
            [turned[m, pl.ds(i * pitch, hidden), :] for m in range(toks // LANES)], axis=1
        )
        mean = jnp.mean(x, axis=0, keepdims=True)
        centered = x - mean
        var = jnp.mean(centered * centered, axis=0, keepdims=True)
        pnorm = (centered * lax.rsqrt(var + 1e-05) * scale[...]).astype(BF16)
        mapped = lax.dot_general(pnorm, weight[...], TN, preferred_element_type=F32)
        out[i] = (gate[i] * mapped).astype(BF16)


def kernel(body, name, out_shape, in_specs, scratch=()):
    outs = jax.tree.map(lambda _: VMEM, out_shape)

    def call(*args):
        arrays = [*args, *jax.tree.leaves(out_shape), *scratch]
        size = sum(x.dtype.itemsize * math.prod(x.shape) for x in arrays)
        return pl.pallas_call(
            body,
            out_shape=out_shape,
            in_specs=in_specs,
            out_specs=outs,
            scratch_shapes=list(scratch),
            compiler_params=pltpu.CompilerParams(vmem_limit_bytes=size + SPARE),
            name=name,
        )(*args)

    return call


def local(pair, pair_mask, in_gain, proj_weight, gate_weight, out_gain, out_weight, *, n_row):
    rows, toks, channels = pair.shape
    hidden = proj_weight.shape[1] // 4
    part = hidden // 4
    planes = n_row // 2
    half = planes // 2
    counts = [part * share // sum(SHARES) for share in SHARES]
    groups = range(len(counts))
    row, core = lax.axis_index("row"), lax.axis_index("chan")
    z, y = row // 2, row % 2
    own_half = z // half
    at_end = (z == 0) | (z == planes - 1)
    where = jnp.stack([2 * y + core, at_end, core ^ own_half]).astype(jnp.int32)

    def send(x, target, name):
        pairs = []
        for source in range(2 * n_row):
            to = target(source // 4, source // 2 % 2, source % 2)
            pairs.append((source, 4 * to[0] + 2 * to[1] + to[2]))
        with jax.named_scope(name):
            return lax.ppermute(x, ("row", "chan"), pairs)

    def after(x, *earlier):
        return lax.optimization_barrier((x, *earlier))[0]

    def in_plane(r):
        return lambda p, b, k: (p, b ^ (r // 2), k ^ (r % 2))

    def shifted(s):
        return lambda p, b, k: (p // half * half + (p + s) % half, b, k)

    def mirrored(p, b, k):
        return (p, b, 1 - k) if p in (0, planes - 1) else (planes - 1 - p, b, k)

    def edge(p, b, k):
        swap = {0: 1, 1: 0, planes - 1: planes - 2, planes - 2: planes - 1}
        return (swap[p], b, k) if p in swap else (p, b, 1 - k)

    gains = jnp.broadcast_to(in_gain, (8, channels))
    scales = jnp.broadcast_to(out_gain[:, None], (hidden, toks))
    halves = jnp.where(jnp.arange(4 * hidden) // hidden % 2 == 0, 0.5, 1.0).astype(BF16)
    weight = proj_weight * halves
    valid = pair_mask.astype(F32) * 0.5
    twin, twin_valid = send(pair, in_plane(1), "pair"), send(valid, in_plane(1), "valid")

    def piece(count, height, depth):
        return jax.ShapeDtypeStruct((count, height, depth), BF16)

    held = pltpu.VMEM((toks // LANES, 2 * part * (rows + 1), LANES), F32)
    rows_all = jax.ShapeDtypeStruct((rows * toks, channels), BF16)
    weights = jax.ShapeDtypeStruct((4 * part, channels), BF16)
    *mine, normed0, chosen_right, chosen_left = kernel(
        right_own_kernel,
        "right_own",
        [piece(part, rows, toks) for _ in range(2)] + [rows_all, weights, weights],
        [SMEM] + [VMEM] * 4,
        [pltpu.VMEM((4 * hidden, channels), BF16), held],
    )(where, pair, valid, gains, weight)
    whole = [piece(part, rows, 2 * toks) for _ in range(2)]
    *right, normed1 = kernel(
        right_twin_kernel, "right_twin", whole + [rows_all], [VMEM] * (4 + len(mine)), [held]
    )(twin, twin_valid, gains, chosen_right, *mine)
    queues = {"mid": [], "end": []}

    def queued(link, name, x, target):
        done = queues[link]
        done.append(send(after(x, *done[:-1][-1:]), target, name))
        return done[-1]

    def near_far(x, name):
        near = [x] + [queued("end", f"end_{name}", x, shifted(s)) for s in range(1, half)]
        return near, [queued("mid", f"mid_{name}", x, mirrored)]

    right0, right1 = right
    near0, far0 = near_far(right0, "right_0")
    right1 = send(right1, in_plane(2), "cross_right")
    left0, left1 = kernel(left_kernel, "left", whole, [VMEM] * 5, [held])(
        normed0, normed1, valid, twin_valid, chosen_left
    )
    near1, far1 = near_far(after(right1, left0), "right_1")
    left1 = send(after(left1, right1), in_plane(2), "cross_left")
    gate = kernel(
        gate_kernel, "gate", jax.ShapeDtypeStruct((rows, toks, channels), F32), [VMEM] * 2
    )(normed0, gate_weight)
    far0 += [queued("mid", "mid_next_0", x, mirrored) for x in near0[1:]]
    outer0 = queued("end", "end_left_0", after(left0, gate), edge)
    far1 += [queued("mid", "mid_next_1", x, mirrored) for x in near1[1:]]
    outer1 = queued("end", "end_left_1", left1, edge)

    def products(first, count, lefts, rights, places, name):
        span = 2 * rows * len(rights)
        return kernel(
            functools.partial(product_kernel, first, len(lefts), len(rights)),
            name,
            [piece(count, 2 * rows, span)] * len(lefts),
            [SMEM] + [VMEM] * (2 * (len(lefts) + len(rights))),
            [pltpu.VMEM((count, span, 2 * toks), BF16)],
        )(places, *[x for pairs in (*lefts, *rights) for x in pairs])

    steps = jnp.arange(half)
    places_near = jnp.concatenate([y[None], (z - steps) % half]).astype(jnp.int32)
    places_far = jnp.concatenate([y[None], (planes - 1 - z - steps) % half]).astype(jnp.int32)
    (near,) = products(0, part, [(left0, left1)], list(zip(near0, near1)), places_near, "near")
    starts = [sum(counts[:g]) for g in groups]
    done, far, ends = [near], [], []
    for g in groups:
        sides = [(after(left0, *done), left1), (outer0, outer1)]
        away, end = products(starts[g], counts[g], sides, list(zip(far0, far1)), places_far, "away")
        ends.append(send(end, edge, f"products_back_{g}"))
        far.append(away)
        done = [away]
    pieces = []
    for g in groups:
        handed = kernel(
            functools.partial(hand_out_kernel, starts[g]),
            "hand_out",
            [piece(counts[g], rows, toks)] * 4,
            [SMEM] + [VMEM] * 3,
        )(where, near, far[g], ends[g])
        pieces += [handed[0]] + [
            send(handed[r], in_plane(r), f"return_{g}{r}") for r in range(1, 4)
        ]

    return kernel(
        update_kernel,
        "update",
        jax.ShapeDtypeStruct((rows, toks, channels), BF16),
        [SMEM] + [VMEM] * (3 + len(pieces)),
        [pltpu.VMEM((toks // LANES, rows * (hidden + 1), LANES), F32)],
    )(where, scales, out_weight, gate, *pieces)


def solution(mesh):
    placed = (
        P(("groups", "row"), "chan", None),
        P(("groups", "row"), "chan"),
        P(),
        P(),
        P(),
        P(),
        P(),
    )
    return jax.shard_map(
        functools.partial(local, n_row=mesh.shape["row"]),
        mesh=mesh,
        in_specs=placed,
        out_specs=P(("groups", "row"), "chan", None),
        check_vma=False,
    )
```

time: 105 us -> 93 us (0.89)
  Pallas kernels: 24.5 us -> 18.6 us
  waiting for transfers between devices: 42.2 us -> 37.9 us
  starting transfers between devices: 30.1 us -> 28.1 us
  other arithmetic: 0.24 us -> 1.9 us
  local copies, waits for them, and re-layouts: 7.14 us -> 5.75 us
    pallas_call x11 -> x10, Pallas kernels: 24.5 us -> 18.6 us  [call(): pl.pallas_call(body, out_shape=out_shape, in_specs=in_specs, out_specs=ou...]
    ppermute x26 -> x20, waiting for transfers between devices: 42.2 us -> 37.9 us  [send(): return lax.ppermute(x, ('row', 'chan'), pairs)]
    unnamed x36 -> x24, local copies, waits for them, and re-layouts: 7.02 us -> 5.02 us
    ppermute x26 -> x20, starting transfers between devices: 30.1 us -> 28.1 us  [send(): return lax.ppermute(x, ('row', 'chan'), pairs)]
    mul x0 -> x2, other arithmetic: none -> 1.64 us  [the longest x1 0.92 us: local(): weight = proj_weight * halves]
  transfers between devices with their start and end apart: 26 -> 20, of which waited for: 10 -> 10; matrix products, arithmetic and copies ran while one was open for 0% -> 3% of each run, Pallas kernels for 13% -> 10%
where the time goes in v5:
time: 93 us; the launch traced here: 92.5 us
  waiting for transfers between devices  37.9 us (41%)
  starting transfers between devices  28.1 us (30%)
  Pallas kernels  18.6 us (20%)
  local copies, waits for them, and re-layouts  5.75 us (6%)
  other arithmetic  1.9 us (2%)
    ppermute x20, waiting for transfers between devices, send(): return lax.ppermute(x, ('row', 'chan'), pairs)  37.9 us
    ppermute x20, starting transfers between devices, send(): return lax.ppermute(x, ('row', 'chan'), pairs)  28.1 us
    pallas_call x10, Pallas kernels, call(): pl.pallas_call(body, out_shape=out_shape, in_specs=in_specs, out_specs=ou...  18.6 us
    unnamed x24, local copies, waits for them, and re-layouts  5.02 us
  transfers between devices with their start and end apart: 20, of which 10 were waited for; matrix products, arithmetic and copies ran while one was open for 3% of the time, Pallas kernels for 10%

profile of v5, /device:TPU:1, one launch (start us, length us, event | category | flops | bytes accessed | tf_op | source)
XLA Modules:
  0.0 92.5 jit_solution(11325461012689867794)
XLA Ops:
  0.0 0.1 collective-permute-start
  0.1 0.7 convert_multiply_fusion.valid.valid0
  0.8 0.5 collective-permute-start.1
  1.2 0.9 broadcast_multiply_fusion.weight
  2.2 0.1 pad_add_fusion.where
  2.2 0.7 broadcast_in_dim.23.gain
  2.9 1.2 %copy-done.4 = bf16[32,128,128]{2,1,0:T(8,128)(2,1)S(1)} copy-done((bf16[32,128,128]{2,1,0:T(8,128)(2,1)S(1)}, bf16[32,128,128]{2,1,0:T(8,128)(2,1)}, u32[]{:S(2)}) %copy-start.4) | copy-done | bytes 1048600
  4.1 2.8 %right_own.1 = (bf16[32,32,128]{2,1,0:T(8,128)(2,1)S(1)}, bf16[32,32,128]{2,1,0:T(8,128)(2,1)S(1)}, bf16[4096,128]{1,0:T(8,128)(2,1)S(1)}, bf16[128,128]{1,0:T(8,128)(2,1)S(1)}, bf16[128,128]{1,0:T(8,128)(2,1)S(1)}) custom-call(s32[3]{0:T(128)S(1)} %pad_add_fusion.where, bf16[32,128,128]{2,1,0:T(8,128)(2,1)S(1)} %copy-done.4, ...), custom_call_target="tpu_custom_call" | custom-call | tf_op jit(solution)/shard_map/right_own/pallas_call | solution.py:186
  7.0 0.0 copy-start.9
  7.0 0.0 collective-permute-done.1.valid.valid1
  7.0 0.0 collective-permute-done.pair
  7.0 2.3 %right_twin.1 = (bf16[32,32,256]{2,1,0:T(8,128)(2,1)S(1)}, bf16[32,32,256]{2,1,0:T(8,128)(2,1)S(1)}, bf16[4096,128]{1,0:T(8,128)(2,1)S(1)}) custom-call(bf16[32,128,128]{2,1,0:T(8,128)(2,1)S(1)} %collective-permute-done.pair, f32[32,128]{1,0:T(8,128)S(1)} %collective-permute-done.1.valid.valid1, f32[8,128]{1,0:T(8,128)S(1)} %broadcast_in_dim.23.gain, ...), custom_call_target="tpu_custom_call" | custom-call | tf_op jit(solution)/shard_map/right_twin/pallas_call | solution.py:186
  9.3 0.0 copy-start.5
  9.3 2.3 %collective-permute-start.2 = (bf16[32,32,256]{2,1,0:T(8,128)(2,1)S(1)}, bf16[32,32,256]{2,1,0:T(8,128)(2,1)S(1)}, u32[]{:S(2)}, u32[]{:S(2)}) collective-permute-start(bf16[32,32,256]{2,1,0:T(8,128)(2,1)S(1)} %get-tuple-element.44), channel_id=1, source_target_pairs={{0,2},{1,3},{2,0},{3,1},{4,6},{5,7},{6,4},{7,5},{8,10},{9,11},{10,... | collective-permute-start | bytes 1572872 | tf_op jit(solution)/shard_map/cross_right/ppermute | solution.py:219
  11.6 0.8 collective-permute-start.8
  12.4 1.8 %collective-permute-start.4 = (bf16[32,32,256]{2,1,0:T(8,128)(2,1)S(1)}, bf16[32,32,256]{2,1,0:T(8,128)(2,1)}, u32[]{:S(2)}, u32[]{:S(2)}) collective-permute-start(bf16[32,32,256]{2,1,0:T(8,128)(2,1)S(1)} %get-tuple-element.46.rest_2_), channel_id=1, source_target_pairs={{0,4},{1,5},{2,6},{3,7},{4,0},{5,1},{6,2},{7,3},{8,12},{9,13},{10,... | collective-permute-start | bytes 1572872 | tf_op jit(solution)/shard_map/end_right_0/ppermute | solution.py:219
  14.2 2.0 %left.1 = (bf16[32,32,256]{2,1,0:T(8,128)(2,1)S(1)}, bf16[32,32,256]{2,1,0:T(8,128)(2,1)S(1)}) custom-call(bf16[4096,128]{1,0:T(8,128)(2,1)S(1)} %get-tuple-element.36.normed.normed0, bf16[4096,128]{1,0:T(8,128)(2,1)S(1)} %get-tuple-element.40.normed1, f32[32,128]{1,0:T(8,128)S(1)} %convert_multiply_fusion.valid.valid0, ...), custom_call_target="tpu_custom_call" | custom-call | tf_op jit(solution)/shard_map/left/pallas_call | solution.py:186
  16.2 7.4 %collective-permute-done.2.rest_3_ = bf16[32,32,256]{2,1,0:T(8,128)(2,1)S(1)} collective-permute-done((bf16[32,32,256]{2,1,0:T(8,128)(2,1)S(1)}, bf16[32,32,256]{2,1,0:T(8,128)(2,1)S(1)}, u32[]{:S(2)}, u32[]{:S(2)}) %collective-permute-start.2) | collective-permute-done | bytes 524320 | tf_op jit(solution)/shard_map/cross_right/ppermute | solution.py:219
  23.6 0.9 collective-permute-start.9
  24.5 1.6 %collective-permute-start.5 = (bf16[32,32,256]{2,1,0:T(8,128)(2,1)S(1)}, bf16[32,32,256]{2,1,0:T(8,128)(2,1)}, u32[]{:S(2)}, u32[]{:S(2)}) collective-permute-start(bf16[32,32,256]{2,1,0:T(8,128)(2,1)S(1)} %collective-permute-done.2.rest_3_), channel_id=1, source_target_pairs={{0,4},{1,5},{2,6},{3,7},{4,0},{5,1},{6,2},{7,3},{8,12},{9,13},{10,... | collective-permute-start | bytes 1572872 | tf_op jit(solution)/shard_map/end_right_1/ppermute | solution.py:219
  26.1 1.2 %collective-permute-start.3 = (bf16[32,32,256]{2,1,0:T(8,128)(2,1)S(1)}, bf16[32,32,256]{2,1,0:T(8,128)(2,1)S(1)}, u32[]{:S(2)}, u32[]{:S(2)}) collective-permute-start(bf16[32,32,256]{2,1,0:T(8,128)(2,1)S(1)} %get-tuple-element.45), channel_id=1, source_target_pairs={{0,2},{1,3},{2,0},{3,1},{4,6},{5,7},{6,4},{7,5},{8,10},{9,11},{10,... | collective-permute-start | bytes 1572872 | tf_op jit(solution)/shard_map/cross_left/ppermute | solution.py:219
  27.3 0.9 gate.1
  28.2 0.0 collective-permute-done.8.rest_4_
  28.2 0.8 copy-done
  29.0 0.0 collective-permute-done.4.rest_4_
  29.0 2.1 %collective-permute-start.10 = (bf16[32,32,256]{2,1,0:T(8,128)(2,1)}, bf16[32,32,256]{2,1,0:T(8,128)(2,1)}, u32[]{:S(2)}, u32[]{:S(2)}) collective-permute-start(bf16[32,32,256]{2,1,0:T(8,128)(2,1)} %collective-permute-done.4.rest_4_), channel_id=1, source_target_pairs={{0,1},{1,0},{2,3},{3,2},{4,8},{5,9},{6,10},{7,11},{8,4},{9,5},{10,... | collective-permute-start | bytes 1572872 | tf_op jit(solution)/shard_map/mid_next_0/ppermute | solution.py:219
  31.1 0.5 collective-permute-start.6
  31.6 0.0 collective-permute-done.9.rest_5_
  31.6 0.8 copy-done.2
  32.4 4.5 %collective-permute-done.5.rest_5_ = bf16[32,32,256]{2,1,0:T(8,128)(2,1)} collective-permute-done((bf16[32,32,256]{2,1,0:T(8,128)(2,1)S(1)}, bf16[32,32,256]{2,1,0:T(8,128)(2,1)}, u32[]{:S(2)}, u32[]{:S(2)}) %collective-permute-start.5) | collective-permute-done | bytes 524320 | tf_op jit(solution)/shard_map/end_right_1/ppermute | solution.py:219
  36.9 0.9 collective-permute-done.3.rest_1_
  37.8 0.3 collective-permute-start.7
  38.1 4.8 %collective-permute-start.11 = (bf16[32,32,256]{2,1,0:T(8,128)(2,1)}, bf16[32,32,256]{2,1,0:T(8,128)(2,1)}, u32[]{:S(2)}, u32[]{:S(2)}) collective-permute-start(bf16[32,32,256]{2,1,0:T(8,128)(2,1)} %collective-permute-done.5.rest_5_), channel_id=1, source_target_pairs={{0,1},{1,0},{2,3},{3,2},{4,8},{5,9},{6,10},{7,11},{8,4},{9,5},{10,... | collective-permute-start | bytes 1572872 | tf_op jit(solution)/shard_map/mid_next_1/ppermute | solution.py:219
  42.9 0.1 pad_add_fusion.1.places
  43.0 0.1 pad_add_fusion.2.places
  43.0 1.1 %copy-done.6 = bf16[32,32,256]{2,1,0:T(8,128)(2,1)S(1)} copy-done((bf16[32,32,256]{2,1,0:T(8,128)(2,1)S(1)}, bf16[32,32,256]{2,1,0:T(8,128)(2,1)}, u32[]{:S(2)}) %copy-start.6) | copy-done | bytes 524312
  44.2 1.0 %copy-done.8 = bf16[32,32,256]{2,1,0:T(8,128)(2,1)S(1)} copy-done((bf16[32,32,256]{2,1,0:T(8,128)(2,1)S(1)}, bf16[32,32,256]{2,1,0:T(8,128)(2,1)}, u32[]{:S(2)}) %copy-start.8) | copy-done | bytes 524312
  45.2 2.2 %near.1 = bf16[32,64,128]{2,1,0:T(8,128)(2,1)S(1)} custom-call(s32[3]{0:T(128)S(1)} %pad_add_fusion.1.places, bf16[32,32,256]{2,1,0:T(8,128)(2,1)S(1)} %get-tuple-element.60.rest_0_, bf16[32,32,256]{2,1,0:T(8,128)(2,1)S(1)} %collective-permute-done.3.rest_1_, bf16[32,32,256]{2,1,0:T(8,128)(2,1)S(1)} %copy-done.6, bf16[32,32,256]{2,1,0:T(8,128)(2,1)S(1)} %copy-done.8, ...), custom_call_target="tpu_custom_call" | custom-call | tf_op jit(solution)/shard_map/near/pallas_call | solution.py:186
  47.4 0.7 collective-permute-done.6.rest_2_
  48.1 11.2 %collective-permute-done.7.rest_3_ = bf16[32,32,256]{2,1,0:T(8,128)(2,1)} collective-permute-done((bf16[32,32,256]{2,1,0:T(8,128)(2,1)S(1)}, bf16[32,32,256]{2,1,0:T(8,128)(2,1)}, u32[]{:S(2)}, u32[]{:S(2)}) %collective-permute-start.7) | collective-permute-done | bytes 524320 | tf_op jit(solution)/shard_map/end_left_1/ppermute | solution.py:219
  59.3 0.0 collective-permute-done.11.rest_7_
  59.4 2.0 %away.2 = (bf16[16,64,128]{2,1,0:T(8,128)(2,1)S(1)}, bf16[16,64,128]{2,1,0:T(8,128)(2,1)S(1)}) custom-call(s32[3]{0:T(128)S(1)} %pad_add_fusion.2.places, bf16[32,32,256]{2,1,0:T(8,128)(2,1)S(1)} %get-tuple-element.60.rest_0_, bf16[32,32,256]{2,1,0:T(8,128)(2,1)S(1)} %collective-permute-done.3.rest_1_, bf16[32,32,256]{2,1,0:T(8,128)(2,1)} %collective-permute-done.6.rest_2_, ...), custom_call_target="tpu_custom_call" | custom-call | tf_op jit(solution)/shard_map/away/pallas_call | solution.py:186
  61.4 2.0 %away.3 = (bf16[16,64,128]{2,1,0:T(8,128)(2,1)S(1)}, bf16[16,64,128]{2,1,0:T(8,128)(2,1)S(1)}) custom-call(s32[3]{0:T(128)S(1)} %pad_add_fusion.2.places, bf16[32,32,256]{2,1,0:T(8,128)(2,1)S(1)} %get-tuple-element.60.rest_0_, bf16[32,32,256]{2,1,0:T(8,128)(2,1)S(1)} %collective-permute-done.3.rest_1_, bf16[32,32,256]{2,1,0:T(8,128)(2,1)} %collective-permute-done.6.rest_2_, ...), custom_call_target="tpu_custom_call" | custom-call | tf_op jit(solution)/shard_map/away/pallas_call | solution.py:186
  63.4 0.0 copy-start.11
  63.4 0.0 copy-start.10
  63.5 1.3 %collective-permute-start.16 = (bf16[16,64,128]{2,1,0:T(8,128)(2,1)S(1)}, bf16[16,64,128]{2,1,0:T(8,128)(2,1)S(1)}, u32[]{:S(2)}, u32[]{:S(2)}) collective-permute-start(bf16[16,64,128]{2,1,0:T(8,128)(2,1)S(1)} %get-tuple-element.62), channel_id=1, source_target_pairs={{0,4},{1,5},{2,6},{3,7},{4,0},{5,1},{6,2},{7,3},{8,12},{9,13},{10,... | collective-permute-start | bytes 786440 | tf_op jit(solution)/shard_map/products_back_1/ppermute | solution.py:219
  64.7 0.3 collective-permute-start.12
  65.0 4.2 %collective-permute-done.16.end = bf16[16,64,128]{2,1,0:T(8,128)(2,1)S(1)} collective-permute-done((bf16[16,64,128]{2,1,0:T(8,128)(2,1)S(1)}, bf16[16,64,128]{2,1,0:T(8,128)(2,1)S(1)}, u32[]{:S(2)}, u32[]{:S(2)}) %collective-permute-start.16) | collective-permute-done | bytes 262176 | tf_op jit(solution)/shard_map/products_back_1/ppermute | solution.py:219
  69.1 0.7 hand_out.3
  69.8 5.9 %collective-permute-start.17 = (bf16[16,32,128]{2,1,0:T(8,128)(2,1)S(1)}, bf16[16,32,128]{2,1,0:T(8,128)(2,1)S(1)}, u32[]{:S(2)}, u32[]{:S(2)}) collective-permute-start(bf16[16,32,128]{2,1,0:T(8,128)(2,1)S(1)} %get-tuple-element.64), channel_id=1, source_target_pairs={{0,1},{1,0},{2,3},{3,2},{4,5},{5,4},{6,7},{7,6},{8,9},{9,8},{10,11... | collective-permute-start | bytes 393224 | tf_op jit(solution)/shard_map/return_11/ppermute | solution.py:219
  75.7 1.4 %collective-permute-start.18 = (bf16[16,32,128]{2,1,0:T(8,128)(2,1)S(1)}, bf16[16,32,128]{2,1,0:T(8,128)(2,1)S(1)}, u32[]{:S(2)}, u32[]{:S(2)}) collective-permute-start(bf16[16,32,128]{2,1,0:T(8,128)(2,1)S(1)} %get-tuple-element.65), channel_id=1, source_target_pairs={{0,2},{1,3},{2,0},{3,1},{4,6},{5,7},{6,4},{7,5},{8,10},{9,11},{10,... | collective-permute-start | bytes 393224 | tf_op jit(solution)/shard_map/return_12/ppermute | solution.py:219
  77.1 0.3 collective-permute-start.19
  77.4 0.7 hand_out.2
  78.1 0.5 collective-permute-start.13
  78.6 1.5 %collective-permute-start.14 = (bf16[16,32,128]{2,1,0:T(8,128)(2,1)S(1)}, bf16[16,32,128]{2,1,0:T(8,128)(2,1)S(1)}, u32[]{:S(2)}, u32[]{:S(2)}) collective-permute-start(bf16[16,32,128]{2,1,0:T(8,128)(2,1)S(1)} %get-tuple-element.58), channel_id=1, source_target_pairs={{0,2},{1,3},{2,0},{3,1},{4,6},{5,7},{6,4},{7,5},{8,10},{9,11},{10,... | collective-permute-start | bytes 393224 | tf_op jit(solution)/shard_map/return_02/ppermute | solution.py:219
  80.1 0.2 collective-permute-start.15
  80.3 0.4 collective-permute-done.18.rest_6_
  80.8 3.4 %collective-permute-done.19.rest_7_ = bf16[16,32,128]{2,1,0:T(8,128)(2,1)S(1)} collective-permute-done((bf16[16,32,128]{2,1,0:T(8,128)(2,1)S(1)}, bf16[16,32,128]{2,1,0:T(8,128)(2,1)S(1)}, u32[]{:S(2)}, u32[]{:S(2)}) %collective-permute-start.19) | collective-permute-done | bytes 131104 | tf_op jit(solution)/shard_map/return_13/ppermute | solution.py:219
  84.2 0.0 collective-permute-done.13.rest_1_
  84.2 2.2 %collective-permute-done.14.rest_2_ = bf16[16,32,128]{2,1,0:T(8,128)(2,1)S(1)} collective-permute-done((bf16[16,32,128]{2,1,0:T(8,128)(2,1)S(1)}, bf16[16,32,128]{2,1,0:T(8,128)(2,1)S(1)}, u32[]{:S(2)}, u32[]{:S(2)}) %collective-permute-start.14) | collective-permute-done | bytes 131104 | tf_op jit(solution)/shard_map/return_02/ppermute | solution.py:219
  86.4 3.0 %collective-permute-done.15.rest_3_ = bf16[16,32,128]{2,1,0:T(8,128)(2,1)S(1)} collective-permute-done((bf16[16,32,128]{2,1,0:T(8,128)(2,1)S(1)}, bf16[16,32,128]{2,1,0:T(8,128)(2,1)S(1)}, u32[]{:S(2)}, u32[]{:S(2)}) %collective-permute-start.15) | collective-permute-done | bytes 131104 | tf_op jit(solution)/shard_map/return_03/ppermute | solution.py:219
  89.3 0.1 broadcast_in_dim.22.scale
  89.4 0.0 copy-done.10
  89.4 3.1 %update.1 = bf16[32,128,128]{2,1,0:T(8,128)(2,1)} custom-call(s32[3]{0:T(128)S(1)} %pad_add_fusion.where, f32[128,128]{1,0:T(8,128)S(1)} %broadcast_in_dim.22.scale, bf16[128,128]{1,0:T(8,128)(2,1)S(1)} %copy-done.10, f32[32,128,128]{2,1,0:T(8,128)S(1)} %gate.1, bf16[16,32,128]{2,1,0:T(8,128)(2,1)S(1)} %get-tuple-element.56.rest_0_, ...), custom_call_target="tpu_custom_call" | custom-call | tf_op jit(solution)/shard_map/update/pallas_call | solution.py:186
  (20 shorter events, 0.1 us)
Async XLA Ops:
  0.0 7.0 %collective-permute-start = (bf16[32,128,128]{2,1,0:T(8,128)(2,1)}, bf16[32,128,128]{2,1,0:T(8,128)(2,1)S(1)}, u32[]{:S(2)}, u32[]{:S(2)}) collective-permute-start(bf16[32,128,128]{2,1,0:T(8,128)(2,1)} %pair.1), channel_id=1, source_target_pairs={{0,1},{1,0},{2,3},{3,2},{4,5},{5,4},{6,7},{7,6},{8,9},{9,8},{10,11... | collective-permute-start | bytes 3145736 | tf_op jit(solution)/shard_map/pair/ppermute | solution.py:219
  0.8 6.2 %collective-permute-start.1 = (f32[32,128]{1,0:T(8,128)S(1)}, f32[32,128]{1,0:T(8,128)S(1)}, u32[]{:S(2)}, u32[]{:S(2)}) collective-permute-start(f32[32,128]{1,0:T(8,128)S(1)} %convert_multiply_fusion.valid.valid0), channel_id=1, source_target_pairs={{0,1},{1,0},{2,3},{3,2},{4,5},{5,4},{6,7},{7,6},{8,9},{9,8},{10,11... | collective-permute-start | bytes 49160 | tf_op jit(solution)/shard_map/valid/ppermute | solution.py:219
  2.9 1.2 %copy-start.4 = (bf16[32,128,128]{2,1,0:T(8,128)(2,1)S(1)}, bf16[32,128,128]{2,1,0:T(8,128)(2,1)}, u32[]{:S(2)}) copy-start(bf16[32,128,128]{2,1,0:T(8,128)(2,1)} %pair.1) | copy-start | bytes 3145732
  7.0 20.4 %copy-start.9 = (bf16[128,128]{1,0:T(8,128)(2,1)S(1)}, bf16[128,128]{1,0:T(8,128)(2,1)}, u32[]{:S(2)}) copy-start(bf16[128,128]{1,0:T(8,128)(2,1)} %weight.2) | copy-start | bytes 98308
  9.3 18.9 %copy-start.5 = (bf16[32,32,256]{2,1,0:T(8,128)(2,1)}, bf16[32,32,256]{2,1,0:T(8,128)(2,1)S(1)}, u32[]{:S(2)}) copy-start(bf16[32,32,256]{2,1,0:T(8,128)(2,1)S(1)} %get-tuple-element.46.rest_2_) | copy-start | bytes 1572868
  9.3 14.3 %collective-permute-start.2 = (bf16[32,32,256]{2,1,0:T(8,128)(2,1)S(1)}, bf16[32,32,256]{2,1,0:T(8,128)(2,1)S(1)}, u32[]{:S(2)}, u32[]{:S(2)}) collective-permute-start(bf16[32,32,256]{2,1,0:T(8,128)(2,1)S(1)} %get-tuple-element.44), channel_id=1, source_target_pairs={{0,2},{1,3},{2,0},{3,1},{4,6},{5,7},{6,4},{7,5},{8,10},{9,11},{10,... | collective-permute-start | bytes 1572872 | tf_op jit(solution)/shard_map/cross_right/ppermute | solution.py:219
  11.6 16.6 %collective-permute-start.8 = (bf16[32,32,256]{2,1,0:T(8,128)(2,1)S(1)}, bf16[32,32,256]{2,1,0:T(8,128)(2,1)S(1)}, u32[]{:S(2)}, u32[]{:S(2)}) collective-permute-start(bf16[32,32,256]{2,1,0:T(8,128)(2,1)S(1)} %get-tuple-element.46.rest_2_), channel_id=1, source_target_pairs={{0,1},{1,0},{2,3},{3,2},{4,8},{5,9},{6,10},{7,11},{8,4},{9,5},{10,... | collective-permute-start | bytes 1572872 | tf_op jit(solution)/shard_map/mid_right_0/ppermute | solution.py:219
  12.4 16.6 %collective-permute-start.4 = (bf16[32,32,256]{2,1,0:T(8,128)(2,1)S(1)}, bf16[32,32,256]{2,1,0:T(8,128)(2,1)}, u32[]{:S(2)}, u32[]{:S(2)}) collective-permute-start(bf16[32,32,256]{2,1,0:T(8,128)(2,1)S(1)} %get-tuple-element.46.rest_2_), channel_id=1, source_target_pairs={{0,4},{1,5},{2,6},{3,7},{4,0},{5,1},{6,2},{7,3},{8,12},{9,13},{10,... | collective-permute-start | bytes 1572872 | tf_op jit(solution)/shard_map/end_right_0/ppermute | solution.py:219
  23.6 14.2 %copy-start.7 = (bf16[32,32,256]{2,1,0:T(8,128)(2,1)}, bf16[32,32,256]{2,1,0:T(8,128)(2,1)S(1)}, u32[]{:S(2)}) copy-start(bf16[32,32,256]{2,1,0:T(8,128)(2,1)S(1)} %collective-permute-done.2.rest_3_) | copy-start | bytes 1572868
  23.6 8.0 %collective-permute-start.9 = (bf16[32,32,256]{2,1,0:T(8,128)(2,1)S(1)}, bf16[32,32,256]{2,1,0:T(8,128)(2,1)S(1)}, u32[]{:S(2)}, u32[]{:S(2)}) collective-permute-start(bf16[32,32,256]{2,1,0:T(8,128)(2,1)S(1)} %collective-permute-done.2.rest_3_), channel_id=1, source_target_pairs={{0,1},{1,0},{2,3},{3,2},{4,8},{5,9},{6,10},{7,11},{8,4},{9,5},{10,... | collective-permute-start | bytes 1572872 | tf_op jit(solution)/shard_map/mid_right_1/ppermute | solution.py:219
  24.5 12.4 %collective-permute-start.5 = (bf16[32,32,256]{2,1,0:T(8,128)(2,1)S(1)}, bf16[32,32,256]{2,1,0:T(8,128)(2,1)}, u32[]{:S(2)}, u32[]{:S(2)}) collective-permute-start(bf16[32,32,256]{2,1,0:T(8,128)(2,1)S(1)} %collective-permute-done.2.rest_3_), channel_id=1, source_target_pairs={{0,4},{1,5},{2,6},{3,7},{4,0},{5,1},{6,2},{7,3},{8,12},{9,13},{10,... | collective-permute-start | bytes 1572872 | tf_op jit(solution)/shard_map/end_right_1/ppermute | solution.py:219
  26.1 11.7 %collective-permute-start.3 = (bf16[32,32,256]{2,1,0:T(8,128)(2,1)S(1)}, bf16[32,32,256]{2,1,0:T(8,128)(2,1)S(1)}, u32[]{:S(2)}, u32[]{:S(2)}) collective-permute-start(bf16[32,32,256]{2,1,0:T(8,128)(2,1)S(1)} %get-tuple-element.45), channel_id=1, source_target_pairs={{0,2},{1,3},{2,0},{3,1},{4,6},{5,7},{6,4},{7,5},{8,10},{9,11},{10,... | collective-permute-start | bytes 1572872 | tf_op jit(solution)/shard_map/cross_left/ppermute | solution.py:219
  28.2 0.8 copy-start
  29.0 18.4 %collective-permute-start.10 = (bf16[32,32,256]{2,1,0:T(8,128)(2,1)}, bf16[32,32,256]{2,1,0:T(8,128)(2,1)}, u32[]{:S(2)}, u32[]{:S(2)}) collective-permute-start(bf16[32,32,256]{2,1,0:T(8,128)(2,1)} %collective-permute-done.4.rest_4_), channel_id=1, source_target_pairs={{0,1},{1,0},{2,3},{3,2},{4,8},{5,9},{6,10},{7,11},{8,4},{9,5},{10,... | collective-permute-start | bytes 1572872 | tf_op jit(solution)/shard_map/mid_next_0/ppermute | solution.py:219
  31.1 17.0 %collective-permute-start.6 = (bf16[32,32,256]{2,1,0:T(8,128)(2,1)S(1)}, bf16[32,32,256]{2,1,0:T(8,128)(2,1)}, u32[]{:S(2)}, u32[]{:S(2)}) collective-permute-start(bf16[32,32,256]{2,1,0:T(8,128)(2,1)S(1)} %get-tuple-element.60.rest_0_), channel_id=1, source_target_pairs={{0,4},{1,5},{2,6},{3,7},{4,0},{5,1},{6,2},{7,3},{8,12},{9,13},{10,... | collective-permute-start | bytes 1572872 | tf_op jit(solution)/shard_map/end_left_0/ppermute | solution.py:219
  31.6 0.8 copy-start.2
  37.8 21.6 %collective-permute-start.7 = (bf16[32,32,256]{2,1,0:T(8,128)(2,1)S(1)}, bf16[32,32,256]{2,1,0:T(8,128)(2,1)}, u32[]{:S(2)}, u32[]{:S(2)}) collective-permute-start(bf16[32,32,256]{2,1,0:T(8,128)(2,1)S(1)} %collective-permute-done.3.rest_1_), channel_id=1, source_target_pairs={{0,4},{1,5},{2,6},{3,7},{4,0},{5,1},{6,2},{7,3},{8,12},{9,13},{10,... | collective-permute-start | bytes 1572872 | tf_op jit(solution)/shard_map/end_left_1/ppermute | solution.py:219
  38.1 21.3 %collective-permute-start.11 = (bf16[32,32,256]{2,1,0:T(8,128)(2,1)}, bf16[32,32,256]{2,1,0:T(8,128)(2,1)}, u32[]{:S(2)}, u32[]{:S(2)}) collective-permute-start(bf16[32,32,256]{2,1,0:T(8,128)(2,1)} %collective-permute-done.5.rest_5_), channel_id=1, source_target_pairs={{0,1},{1,0},{2,3},{3,2},{4,8},{5,9},{6,10},{7,11},{8,4},{9,5},{10,... | collective-permute-start | bytes 1572872 | tf_op jit(solution)/shard_map/mid_next_1/ppermute | solution.py:219
  42.8 16.5 %copy-start.1 = (bf16[32,32,256]{2,1,0:T(8,128)(2,1)S(1)}, bf16[32,32,256]{2,1,0:T(8,128)(2,1)}, u32[]{:S(2)}) copy-start(bf16[32,32,256]{2,1,0:T(8,128)(2,1)} %copy-done) | copy-start | bytes 1572868
  42.8 16.5 %copy-start.3 = (bf16[32,32,256]{2,1,0:T(8,128)(2,1)S(1)}, bf16[32,32,256]{2,1,0:T(8,128)(2,1)}, u32[]{:S(2)}) copy-start(bf16[32,32,256]{2,1,0:T(8,128)(2,1)} %copy-done.2) | copy-start | bytes 1572868
  43.0 1.1 %copy-start.6 = (bf16[32,32,256]{2,1,0:T(8,128)(2,1)S(1)}, bf16[32,32,256]{2,1,0:T(8,128)(2,1)}, u32[]{:S(2)}) copy-start(bf16[32,32,256]{2,1,0:T(8,128)(2,1)} %copy-done.5) | copy-start | bytes 1572868
  44.2 1.0 %copy-start.8 = (bf16[32,32,256]{2,1,0:T(8,128)(2,1)S(1)}, bf16[32,32,256]{2,1,0:T(8,128)(2,1)}, u32[]{:S(2)}) copy-start(bf16[32,32,256]{2,1,0:T(8,128)(2,1)} %copy-done.7) | copy-start | bytes 1572868
  63.4 25.9 %copy-start.11 = (f32[128]{0:T(128)S(1)}, f32[128]{0:T(128)}, u32[]{:S(2)}) copy-start(f32[128]{0:T(128)} %param.12) | copy-start | bytes 1540
  63.4 26.0 %copy-start.10 = (bf16[128,128]{1,0:T(8,128)(2,1)S(1)}, bf16[128,128]{1,0:T(8,128)(2,1)}, u32[]{:S(2)}) copy-start(bf16[128,128]{1,0:T(8,128)(2,1)} %weight.3) | copy-start | bytes 98308
  63.5 5.7 %collective-permute-start.16 = (bf16[16,64,128]{2,1,0:T(8,128)(2,1)S(1)}, bf16[16,64,128]{2,1,0:T(8,128)(2,1)S(1)}, u32[]{:S(2)}, u32[]{:S(2)}) collective-permute-start(bf16[16,64,128]{2,1,0:T(8,128)(2,1)S(1)} %get-tuple-element.62), channel_id=1, source_target_pairs={{0,4},{1,5},{2,6},{3,7},{4,0},{5,1},{6,2},{7,3},{8,12},{9,13},{10,... | collective-permute-start | bytes 786440 | tf_op jit(solution)/shard_map/products_back_1/ppermute | solution.py:219
  64.7 12.7 %collective-permute-start.12 = (bf16[16,64,128]{2,1,0:T(8,128)(2,1)S(1)}, bf16[16,64,128]{2,1,0:T(8,128)(2,1)S(1)}, u32[]{:S(2)}, u32[]{:S(2)}) collective-permute-start(bf16[16,64,128]{2,1,0:T(8,128)(2,1)S(1)} %get-tuple-element.55), channel_id=1, source_target_pairs={{0,4},{1,5},{2,6},{3,7},{4,0},{5,1},{6,2},{7,3},{8,12},{9,13},{10,... | collective-permute-start | bytes 786440 | tf_op jit(solution)/shard_map/products_back_0/ppermute | solution.py:219
  69.8 10.3 %collective-permute-start.17 = (bf16[16,32,128]{2,1,0:T(8,128)(2,1)S(1)}, bf16[16,32,128]{2,1,0:T(8,128)(2,1)S(1)}, u32[]{:S(2)}, u32[]{:S(2)}) collective-permute-start(bf16[16,32,128]{2,1,0:T(8,128)(2,1)S(1)} %get-tuple-element.64), channel_id=1, source_target_pairs={{0,1},{1,0},{2,3},{3,2},{4,5},{5,4},{6,7},{7,6},{8,9},{9,8},{10,11... | collective-permute-start | bytes 393224 | tf_op jit(solution)/shard_map/return_11/ppermute | solution.py:219
  75.7 5.1 %collective-permute-start.18 = (bf16[16,32,128]{2,1,0:T(8,128)(2,1)S(1)}, bf16[16,32,128]{2,1,0:T(8,128)(2,1)S(1)}, u32[]{:S(2)}, u32[]{:S(2)}) collective-permute-start(bf16[16,32,128]{2,1,0:T(8,128)(2,1)S(1)} %get-tuple-element.65), channel_id=1, source_target_pairs={{0,2},{1,3},{2,0},{3,1},{4,6},{5,7},{6,4},{7,5},{8,10},{9,11},{10,... | collective-permute-start | bytes 393224 | tf_op jit(solution)/shard_map/return_12/ppermute | solution.py:219
  77.1 7.1 %collective-permute-start.19 = (bf16[16,32,128]{2,1,0:T(8,128)(2,1)S(1)}, bf16[16,32,128]{2,1,0:T(8,128)(2,1)S(1)}, u32[]{:S(2)}, u32[]{:S(2)}) collective-permute-start(bf16[16,32,128]{2,1,0:T(8,128)(2,1)S(1)} %get-tuple-element.66), channel_id=1, source_target_pairs={{0,3},{1,2},{2,1},{3,0},{4,7},{5,6},{6,5},{7,4},{8,11},{9,10},{10,... | collective-permute-start | bytes 393224 | tf_op jit(solution)/shard_map/return_13/ppermute | solution.py:219
  78.1 6.1 %collective-permute-start.13 = (bf16[16,32,128]{2,1,0:T(8,128)(2,1)S(1)}, bf16[16,32,128]{2,1,0:T(8,128)(2,1)S(1)}, u32[]{:S(2)}, u32[]{:S(2)}) collective-permute-start(bf16[16,32,128]{2,1,0:T(8,128)(2,1)S(1)} %get-tuple-element.57), channel_id=1, source_target_pairs={{0,1},{1,0},{2,3},{3,2},{4,5},{5,4},{6,7},{7,6},{8,9},{9,8},{10,11... | collective-permute-start | bytes 393224 | tf_op jit(solution)/shard_map/return_01/ppermute | solution.py:219
  78.6 7.8 %collective-permute-start.14 = (bf16[16,32,128]{2,1,0:T(8,128)(2,1)S(1)}, bf16[16,32,128]{2,1,0:T(8,128)(2,1)S(1)}, u32[]{:S(2)}, u32[]{:S(2)}) collective-permute-start(bf16[16,32,128]{2,1,0:T(8,128)(2,1)S(1)} %get-tuple-element.58), channel_id=1, source_target_pairs={{0,2},{1,3},{2,0},{3,1},{4,6},{5,7},{6,4},{7,5},{8,10},{9,11},{10,... | collective-permute-start | bytes 393224 | tf_op jit(solution)/shard_map/return_02/ppermute | solution.py:219
  80.1 9.2 %collective-permute-start.15 = (bf16[16,32,128]{2,1,0:T(8,128)(2,1)S(1)}, bf16[16,32,128]{2,1,0:T(8,128)(2,1)S(1)}, u32[]{:S(2)}, u32[]{:S(2)}) collective-permute-start(bf16[16,32,128]{2,1,0:T(8,128)(2,1)S(1)} %get-tuple-element.59), channel_id=1, source_target_pairs={{0,3},{1,2},{2,1},{3,0},{4,7},{5,6},{6,5},{7,4},{8,11},{9,10},{10,... | collective-permute-start | bytes 393224 | tf_op jit(solution)/shard_map/return_03/ppermute | solution.py:219

commit v6 on v5

--- a/solution.py
+++ b/solution.py
@@ -28,13 +28,12 @@
 
 
 def gated(normed, chosen, valid, first, held):
-    toks = valid.shape[1]
+    _, rows, toks = valid.shape
     wide = chosen.shape[0] // 2
-    rows = valid.shape[0]
     proj = lax.dot_general(chosen[...], normed, NT, preferred_element_type=F32)
     for g in range(normed.shape[0] // toks):
         mine = proj[:, g * toks : (g + 1) * toks]
-        value = (jnp.tanh(mine[:wide]) + 1.0) * (valid[pl.ds(first + g, 1), :] * mine[wide:])
+        value = (jnp.tanh(mine[:wide]) + 1.0) * (valid[0, pl.ds(first + g, 1), :] * mine[wide:])
         for m in range(toks // LANES):
             spot = pl.ds(first + g, wide, stride=rows + 1)
             held[m, spot, :] = value[:, m * LANES : (m + 1) * LANES]
@@ -63,33 +62,38 @@
         gated(normed, chosen, valid, first, held)
 
 
-def right_own_kernel(where, pair, valid, gain, weight, *rest):
-    *outs, normed_out, chosen_right, chosen_left, turned, held = rest
-    hidden = weight.shape[1] // 4
+def right_own_kernel(where, pair, packed, *rest):
+    *outs, normed_out, chosen_right, chosen_left, valid, gain, turned, held = rest
+    rows, toks, channels = pair.shape
+    hidden = packed.shape[1] // 4
     part = hidden // 4
-    turned[...] = weight[...].T
+    turned[...] = packed[:channels, :].astype(BF16).T
+    valid[0] = packed[channels : channels + rows, :toks] * 0.5
+    gain[...] = packed[channels + rows :, :channels]
     for n in range(4):
         chosen = chosen_left if n < 2 else chosen_right
+        half = 0.5 if n % 2 == 0 else 1.0
         for p in range(2):
             start = pl.multiple_of(n * hidden + (where[0] ^ (2 * p)) * part, part)
             at = (2 * (n % 2) + p) * part
-            chosen[at : at + part, :] = turned[pl.ds(start, part), :]
+            chosen[at : at + part, :] = turned[pl.ds(start, part), :] * half
     right_rows(pair, valid, gain, chosen_right, normed_out, held)
     write_pieces(outs, held, 0)
 
 
-def right_twin_kernel(pair, valid, gain, chosen, *rest):
-    count = (len(rest) - 2) // 2
-    before, outs, normed_out, held = rest[:count], rest[count:-2], rest[-2], rest[-1]
+def right_twin_kernel(pair, mask, gain, chosen, *rest):
+    count = (len(rest) - 3) // 2
+    before, (*outs, normed_out, valid, held) = rest[:count], rest[count:]
     for x, out in zip(before, outs):
         out[:, :, : x.shape[2]] = x[...]
+    valid[0] = mask[...].astype(F32) * 0.5
     right_rows(pair, valid, gain, chosen, normed_out, held)
     write_pieces(outs, held, pair.shape[1])
 
 
 def left_kernel(normed0, normed1, valid0, valid1, chosen, *rest):
     outs, held = rest[:-1], rest[-1]
-    rows, toks = valid0.shape
+    _, rows, toks = valid0.shape
     for n, (normed, valid) in enumerate(((normed0, valid0), (normed1, valid1))):
 
         @pl.loop(0, rows // GROUP, unroll=UNROLL)
@@ -120,23 +124,24 @@
     for s in range(n_right):
         for p in range(2):
             start = pl.multiple_of(places[1 + s] * span + (places[0] ^ p) * rows, rows)
-            held[:, pl.ds(start, rows), :] = rights[s][p][first : first + count]
+            part = rights[s][p][...] if p else rights[s][p][first : first + count]
+            held[:, pl.ds(start, rows), :] = part
     for c in range(count):
-        left = jnp.concatenate([x[first + c] for side in lefts for x in side], axis=0)
+        left = jnp.concatenate([x for own, other in lefts for x in (own[first + c], other[c])], axis=0)
         out = lax.dot_general(left, held[c], NT, preferred_element_type=F32).astype(BF16)
         for n in range(n_left):
             outs[n][c] = out[n * span : (n + 1) * span]
 
 
-def hand_out_kernel(first, where, near, far, end, *outs):
-    count, rows, _ = outs[0].shape
+def hand_out_kernel(where, near, far, end, *outs):
+    rows = outs[0].shape[1]
     for r in range(4):
         source = where[2] ^ (r % 2)
         span = slice((r // 2) * rows, (r // 2 + 1) * rows)
 
         @pl.when(source == 0)
         def _():
-            outs[r][...] = near[first : first + count, span, :]
+            outs[r][...] = near[:, span, :]
 
         @pl.when((source == 1) & (where[1] == 0))
         def _():
@@ -234,12 +239,14 @@
         swap = {0: 1, 1: 0, planes - 1: planes - 2, planes - 2: planes - 1}
         return (swap[p], b, k) if p in swap else (p, b, 1 - k)
 
-    gains = jnp.broadcast_to(in_gain, (8, channels))
     scales = jnp.broadcast_to(out_gain[:, None], (hidden, toks))
-    halves = jnp.where(jnp.arange(4 * hidden) // hidden % 2 == 0, 0.5, 1.0).astype(BF16)
-    weight = proj_weight * halves
-    valid = pair_mask.astype(F32) * 0.5
-    twin, twin_valid = send(pair, in_plane(1), "pair"), send(valid, in_plane(1), "valid")
+    wide = 4 * hidden
+    packed = (
+        jnp.pad(proj_weight.astype(F32), ((0, rows + 8), (0, 0)))
+        + jnp.pad(pair_mask.astype(F32), ((channels, 8), (0, wide - toks)))
+        + jnp.pad(in_gain[None], ((channels + rows, 7), (0, wide - channels)))
+    )
+    twin, twin_mask = send(pair, in_plane(1), "pair"), send(pair_mask, in_plane(1), "mask")
 
     def piece(count, height, depth):
         return jax.ShapeDtypeStruct((count, height, depth), BF16)
@@ -247,46 +254,59 @@
     held = pltpu.VMEM((toks // LANES, 2 * part * (rows + 1), LANES), F32)
     rows_all = jax.ShapeDtypeStruct((rows * toks, channels), BF16)
     weights = jax.ShapeDtypeStruct((4 * part, channels), BF16)
-    *mine, normed0, chosen_right, chosen_left = kernel(
+    valid_shape = jax.ShapeDtypeStruct((1, rows, toks), F32)
+    gain_shape = jax.ShapeDtypeStruct((8, channels), F32)
+    *mine, normed0, chosen_right, chosen_left, valid, gain = kernel(
         right_own_kernel,
         "right_own",
-        [piece(part, rows, toks) for _ in range(2)] + [rows_all, weights, weights],
-        [SMEM] + [VMEM] * 4,
+        [piece(count, rows, toks) for count in (part, *counts)]
+        + [rows_all, weights, weights, valid_shape, gain_shape],
+        [SMEM, VMEM, VMEM],
         [pltpu.VMEM((4 * hidden, channels), BF16), held],
-    )(where, pair, valid, gains, weight)
-    whole = [piece(part, rows, 2 * toks) for _ in range(2)]
-    *right, normed1 = kernel(
-        right_twin_kernel, "right_twin", whole + [rows_all], [VMEM] * (4 + len(mine)), [held]
-    )(twin, twin_valid, gains, chosen_right, *mine)
-    queues = {"mid": [], "end": []}
-
-    def queued(link, name, x, target):
+    )(where, pair, packed)
+    whole = [piece(count, rows, 2 * toks) for count in (part, *counts)]
+    *right, normed1, twin_valid = kernel(
+        right_twin_kernel,
+        "right_twin",
+        whole + [rows_all, valid_shape],
+        [VMEM] * (4 + len(mine)),
+        [held],
+    )(twin, twin_mask, gain, chosen_right, *mine)
+    right0, right1 = right[0], list(right[1:])
+    queues = {"y": [], "end": [], "mid": []}
+
+    def queued(link, name, x, target, window=3, also=()):
         done = queues[link]
-        done.append(send(after(x, *done[:-1][-1:]), target, name))
+        early = done[len(done) - window :][:1] if len(done) >= window else []
+        done.append(send(after(x, *early, *also), target, name))
         return done[-1]
 
-    def near_far(x, name):
-        near = [x] + [queued("end", f"end_{name}", x, shifted(s)) for s in range(1, half)]
-        return near, [queued("mid", f"mid_{name}", x, mirrored)]
-
-    right0, right1 = right
-    near0, far0 = near_far(right0, "right_0")
-    right1 = send(right1, in_plane(2), "cross_right")
-    left0, left1 = kernel(left_kernel, "left", whole, [VMEM] * 5, [held])(
+    def shift_all(x, name):
+        return [x] + [queued("end", name, x, shifted(s)) for s in range(1, half)]
+
+    far0 = [queued("mid", "mid_own_0", right0, mirrored)]
+    near0 = shift_all(right0, "end_right_0")
+    right1[0] = queued("y", "cross_right_0", right1[0], in_plane(2), 1)
+    left = kernel(left_kernel, "left", whole, [VMEM] * 5, [held])(
         normed0, normed1, valid, twin_valid, chosen_left
     )
-    near1, far1 = near_far(after(right1, left0), "right_1")
-    left1 = send(after(left1, right1), in_plane(2), "cross_left")
+    left0, left1 = left[0], list(left[1:])
+    for g in groups[1:]:
+        right1[g] = queued("y", f"cross_right_{g}", after(right1[g], left0), in_plane(2), 1)
+    for g in groups:
+        left1[g] = queued("y", f"cross_left_{g}", left1[g], in_plane(2), 1)
+    far1, near1 = [], []
+    for g in groups:
+        far1.append([queued("mid", f"mid_own_1{g}", right1[g], mirrored)])
+        near1.append(shift_all(right1[g], f"end_right_1{g}"))
+    far0 += [queued("mid", "mid_next_0", x, mirrored) for x in near0[1:]]
+    outer0 = queued("end", "end_left_0", left0, edge)
     gate = kernel(
         gate_kernel, "gate", jax.ShapeDtypeStruct((rows, toks, channels), F32), [VMEM] * 2
     )(normed0, gate_weight)
-    far0 += [queued("mid", "mid_next_0", x, mirrored) for x in near0[1:]]
-    outer0 = queued("end", "end_left_0", after(left0, gate), edge)
-    far1 += [queued("mid", "mid_next_1", x, mirrored) for x in near1[1:]]
-    outer1 = queued("end", "end_left_1", left1, edge)
-
-    def products(first, count, lefts, rights, places, name):
+    def products(first, lefts, rights, places, name):
         span = 2 * rows * len(rights)
+        count = lefts[0][1].shape[0]
         return kernel(
             functools.partial(product_kernel, first, len(lefts), len(rights)),
             name,
@@ -298,26 +318,36 @@
     steps = jnp.arange(half)
     places_near = jnp.concatenate([y[None], (z - steps) % half]).astype(jnp.int32)
     places_far = jnp.concatenate([y[None], (planes - 1 - z - steps) % half]).astype(jnp.int32)
-    (near,) = products(0, part, [(left0, left1)], list(zip(near0, near1)), places_near, "near")
-    starts = [sum(counts[:g]) for g in groups]
-    done, far, ends = [near], [], []
+    outer1, close, first = [], [], 0
     for g in groups:
-        sides = [(after(left0, *done), left1), (outer0, outer1)]
-        away, end = products(starts[g], counts[g], sides, list(zip(far0, far1)), places_far, "away")
-        ends.append(send(end, edge, f"products_back_{g}"))
-        far.append(away)
-        done = [away]
-    pieces = []
+        far1[g] += [queued("mid", f"mid_next_1{g}", x, mirrored) for x in near1[g][1:]]
+        outer1.append(queued("end", f"end_left_1{g}", left1[g], edge))
+        close += products(
+            first,
+            [(after(left0, gate), left1[g])],
+            list(zip(near0, near1[g])),
+            places_near,
+            "near",
+        )
+        first += counts[g]
+    done, pieces, first = close, [], 0
     for g in groups:
+        mine = (left0, after(left1[g], *done))
+        away, ends = products(
+            first, [mine, (outer0, outer1[g])], list(zip(far0, far1[g])), places_far, "away"
+        )
+        ends = send(ends, edge, f"products_back_{g}")
         handed = kernel(
-            functools.partial(hand_out_kernel, starts[g]),
+            hand_out_kernel,
             "hand_out",
             [piece(counts[g], rows, toks)] * 4,
             [SMEM] + [VMEM] * 3,
-        )(where, near, far[g], ends[g])
+        )(where, close[g], away, ends)
+        done = [away]
         pieces += [handed[0]] + [
             send(handed[r], in_plane(r), f"return_{g}{r}") for r in range(1, 4)
         ]
+        first += counts[g]
 
     return kernel(
         update_kernel,

time: 93 us -> 94.2 us (1.013)
  starting transfers between devices: 28.1 us -> 46.4 us
  waiting for transfers between devices: 37.9 us -> 20.2 us
  Pallas kernels: 18.6 us -> 19.9 us
    ppermute x20 -> x26, starting transfers between devices: 28.1 us -> 46.4 us  [send(): return lax.ppermute(x, ('row', 'chan'), pairs)]
    ppermute x20 -> x26, waiting for transfers between devices: 37.9 us -> 20.2 us  [send(): return lax.ppermute(x, ('row', 'chan'), pairs)]
    mul x2 -> x0, other arithmetic: 1.64 us -> none  [the longest x1 0.92 us: local(): weight = proj_weight * halves]
    pallas_call x10 -> x11, Pallas kernels: 18.6 us -> 19.9 us  [call(): pl.pallas_call(body, out_shape=out_shape, in_specs=in_specs, out_specs=ou...]
    add x0 -> x1, other arithmetic: none -> 0.94 us  [local(): jnp.pad(proj_weight.astype(F32), ((0, rows + 8), (0, 0)))]
    unnamed x24 -> x20, local copies, waits for them, and re-layouts: 5.02 us -> 4.84 us
  transfers between devices with their start and end apart: 20 -> 26, of which waited for: 10 -> 9; matrix products, arithmetic and copies ran while one was open for 3% -> 2% of each run, Pallas kernels for 10% -> 16%
where the time goes in v6:
time: 94.2 us; the launch traced here: 93.6 us
  starting transfers between devices  46.4 us (49%)
  waiting for transfers between devices  20.2 us (21%)
  Pallas kernels  19.9 us (21%)
  local copies, waits for them, and re-layouts  4.92 us (5%)
  other arithmetic  1.91 us (2%)
    ppermute x26, starting transfers between devices, send(): return lax.ppermute(x, ('row', 'chan'), pairs)  46.4 us
    ppermute x26, waiting for transfers between devices, send(): return lax.ppermute(x, ('row', 'chan'), pairs)  20.2 us
    pallas_call x11, Pallas kernels, call(): pl.pallas_call(body, out_shape=out_shape, in_specs=in_specs, out_specs=ou...  19.9 us
    unnamed x20, local copies, waits for them, and re-layouts  4.84 us
  transfers between devices with their start and end apart: 26, of which 9 were waited for; matrix products, arithmetic and copies ran while one was open for 2% of the time, Pallas kernels for 16%

profile of v6, /device:TPU:1, one launch (start us, length us, event | category | flops | bytes accessed | tf_op | source)
XLA Modules:
  0.0 93.6 jit_solution(7902332472593736043)
XLA Ops:
  0.0 0.1 collective-permute-start
  0.1 0.5 collective-permute-start.1
  0.5 0.7 convert_element_type.7
  1.2 0.9 %pad_add_fusion.packed = f32[168,512]{1,0:T(8,128)S(1)} fusion(f32[1,128]{1,0:T(1,128)} %bitcast.5, f32[32,128]{1,0:T(8,128)S(1)} %convert_element_type.7, bf16[128,512]{1,0:T(8,128)(2,1)} %param.10), kind=kLoop, calls=%fused_computation | loop fusion | flops 258048 | bytes 492032 | tf_op jit(solution)/shard_map/add | solution.py:245
  2.2 0.1 pad_add_fusion.1.where
  2.3 1.2 %copy-done = bf16[32,128,128]{2,1,0:T(8,128)(2,1)S(1)} copy-done((bf16[32,128,128]{2,1,0:T(8,128)(2,1)S(1)}, bf16[32,128,128]{2,1,0:T(8,128)(2,1)}, u32[]{:S(2)}) %copy-start) | copy-done | bytes 1048600
  3.5 2.8 %right_own.1 = (bf16[32,32,128]{2,1,0:T(8,128)(2,1)S(1)}, bf16[16,32,128]{2,1,0:T(8,128)(2,1)S(1)}, bf16[16,32,128]{2,1,0:T(8,128)(2,1)S(1)}, bf16[4096,128]{1,0...) custom-call(s32[3]{0:T(128)S(1)} %pad_add_fusion.1.where, ...), custom_call_target="tpu_custom_call" | custom-call | tf_op jit(solution)/shard_map/right_own/pallas_call | solution.py:191
  6.3 0.0 collective-permute-done.pair
  6.3 0.0 copy-start.1
  6.4 1.0 %copy-done.1 = bf16[32,128,128]{2,1,0:T(8,128)(2,1)} copy-done((bf16[32,128,128]{2,1,0:T(8,128)(2,1)}, bf16[32,128,128]{2,1,0:T(8,128)(2,1)S(1)}, u32[]{:S(2)}) %copy-start.1) | copy-done | bytes 1048600
  7.3 1.2 %copy-done.2 = bf16[32,128,128]{2,1,0:T(8,128)(2,1)S(1)} copy-done((bf16[32,128,128]{2,1,0:T(8,128)(2,1)S(1)}, bf16[32,128,128]{2,1,0:T(8,128)(2,1)}, u32[]{:S(2)}) %copy-start.2) | copy-done | bytes 1048600
  8.5 2.3 %right_twin.1 = (bf16[32,32,256]{2,1,0:T(8,128)(2,1)S(1)}, bf16[16,32,256]{2,1,0:T(8,128)(2,1)S(1)}, bf16[16,32,256]{2,1,0:T(8,128)(2,1)S(1)}, bf16[4096,128]{1,0:T(8,128)(2,1)S(1)}, f32[1,32,128]{2,1,0:T(8,128)S(1)}) custom-call(bf16[32,128,128]{2,1,0:T(8,128)(2,1)S(1)} %copy-done.2, s32[32,128]{1,0:T(8,128)S(1)} %collective-permute-done.1.mask, ...), custom_call_target="tpu_custom_call" | custom-call | tf_op jit(solution)/shard_map/right_twin/pallas_call | solution.py:191
  10.9 2.3 %collective-permute-start.2 = (bf16[16,32,256]{2,1,0:T(8,128)(2,1)S(1)}, bf16[16,32,256]{2,1,0:T(8,128)(2,1)S(1)}, u32[]{:S(2)}, u32[]{:S(2)}) collective-permute-start(bf16[16,32,256]{2,1,0:T(8,128)(2,1)S(1)} %get-tuple-element.61), channel_id=1, source_target_pairs={{0,2},{1,3},{2,0},{3,1},{4,6},{5,7},{6,4},{7,5},{8,10},{9,11},{10,... | collective-permute-start | bytes 786440 | tf_op jit(solution)/shard_map/cross_right_0/ppermute | solution.py:224
  13.2 1.3 %collective-permute-start.5 = (bf16[32,32,256]{2,1,0:T(8,128)(2,1)S(1)}, bf16[32,32,256]{2,1,0:T(8,128)(2,1)S(1)}, u32[]{:S(2)}, u32[]{:S(2)}) collective-permute-start(bf16[32,32,256]{2,1,0:T(8,128)(2,1)S(1)} %get-tuple-element.64.rest_2_), channel_id=1, source_target_pairs={{0,4},{1,5},{2,6},{3,7},{4,0},{5,1},{6,2},{7,3},{8,12},{9,13},{10,... | collective-permute-start | bytes 1572872 | tf_op jit(solution)/shard_map/end_right_0/ppermute | solution.py:224
  14.5 1.1 %collective-permute-start.11 = (bf16[32,32,256]{2,1,0:T(8,128)(2,1)S(1)}, bf16[32,32,256]{2,1,0:T(8,128)(2,1)S(1)}, u32[]{:S(2)}, u32[]{:S(2)}) collective-permute-start(bf16[32,32,256]{2,1,0:T(8,128)(2,1)S(1)} %get-tuple-element.64.rest_2_), channel_id=1, source_target_pairs={{0,1},{1,0},{2,3},{3,2},{4,8},{5,9},{6,10},{7,11},{8,4},{9,5},{10,... | collective-permute-start | bytes 1572872 | tf_op jit(solution)/shard_map/mid_own_0/ppermute | solution.py:224
  15.5 2.7 %left.1 = (bf16[32,32,256]{2,1,0:T(8,128)(2,1)S(1)}, bf16[16,32,256]{2,1,0:T(8,128)(2,1)S(1)}, bf16[16,32,256]{2,1,0:T(8,128)(2,1)}) custom-call(bf16[4096,128]{1,0:T(8,128)(2,1)S(1)} %get-tuple-element.46.normed.normed0, bf16[4096,128]{1,0:T(8,128)(2,1)S(1)} %get-tuple-element.52.normed1, f32[1,32,128]{2,1,0:T(8,128)S(1)} %get-tuple-element.53.valid0, ...), custom_call_target="tpu_custom_call" | custom-call | tf_op jit(solution)/shard_map/left/pallas_call | solution.py:191
  18.2 1.2 %collective-permute-done.2.rest_3_ = bf16[16,32,256]{2,1,0:T(8,128)(2,1)S(1)} collective-permute-done((bf16[16,32,256]{2,1,0:T(8,128)(2,1)S(1)}, bf16[16,32,256]{2,1,0:T(8,128)(2,1)S(1)}, u32[]{:S(2)}, u32[]{:S(2)}) %collective-permute-start.2) | collective-permute-done | bytes 262176 | tf_op jit(solution)/shard_map/cross_right_0/ppermute | solution.py:224
  19.4 1.1 %collective-permute-start.3 = (bf16[16,32,256]{2,1,0:T(8,128)(2,1)S(1)}, bf16[16,32,256]{2,1,0:T(8,128)(2,1)}, u32[]{:S(2)}, u32[]{:S(2)}) collective-permute-start(bf16[16,32,256]{2,1,0:T(8,128)(2,1)S(1)} %get-tuple-element.62), channel_id=1, source_target_pairs={{0,2},{1,3},{2,0},{3,1},{4,6},{5,7},{6,4},{7,5},{8,10},{9,11},{10,... | collective-permute-start | bytes 786440 | tf_op jit(solution)/shard_map/cross_right_1/ppermute | solution.py:224
  20.5 1.3 %collective-permute-start.6 = (bf16[16,32,256]{2,1,0:T(8,128)(2,1)S(1)}, bf16[16,32,256]{2,1,0:T(8,128)(2,1)}, u32[]{:S(2)}, u32[]{:S(2)}) collective-permute-start(bf16[16,32,256]{2,1,0:T(8,128)(2,1)S(1)} %collective-permute-done.2.rest_3_), channel_id=1, source_target_pairs={{0,4},{1,5},{2,6},{3,7},{4,0},{5,1},{6,2},{7,3},{8,12},{9,13},{10,... | collective-permute-start | bytes 786440 | tf_op jit(solution)/shard_map/end_right_10/ppermute | solution.py:224
  21.8 4.4 %collective-permute-done.3.rest_3_ = bf16[16,32,256]{2,1,0:T(8,128)(2,1)} collective-permute-done((bf16[16,32,256]{2,1,0:T(8,128)(2,1)S(1)}, bf16[16,32,256]{2,1,0:T(8,128)(2,1)}, u32[]{:S(2)}, u32[]{:S(2)}) %collective-permute-start.3) | collective-permute-done | bytes 262176 | tf_op jit(solution)/shard_map/cross_right_1/ppermute | solution.py:224
  26.3 0.8 collective-permute-start.4
  27.1 2.6 %collective-permute-start.12 = (bf16[16,32,256]{2,1,0:T(8,128)(2,1)S(1)}, bf16[16,32,256]{2,1,0:T(8,128)(2,1)S(1)}, u32[]{:S(2)}, u32[]{:S(2)}) collective-permute-start(bf16[16,32,256]{2,1,0:T(8,128)(2,1)S(1)} %collective-permute-done.2.rest_3_), channel_id=1, source_target_pairs={{0,1},{1,0},{2,3},{3,2},{4,8},{5,9},{6,10},{7,11},{8,4},{9,5},{10,... | collective-permute-start | bytes 786440 | tf_op jit(solution)/shard_map/mid_own_10/ppermute | solution.py:224
  29.6 0.7 copy-done.3
  30.3 0.0 collective-permute-done.5.rest_4_
  30.3 0.0 collective-permute-start.8
  30.4 0.0 collective-permute-done.11.rest_4_
  30.4 3.1 %collective-permute-start.20 = (bf16[16,32,256]{2,1,0:T(8,128)(2,1)}, bf16[16,32,256]{2,1,0:T(8,128)(2,1)}, u32[]{:S(2)}, u32[]{:S(2)}) collective-permute-start(bf16[16,32,256]{2,1,0:T(8,128)(2,1)} %collective-permute-done.3.rest_3_), channel_id=1, source_target_pairs={{0,1},{1,0},{2,3},{3,2},{4,8},{5,9},{6,10},{7,11},{8,4},{9,5},{10,... | collective-permute-start | bytes 786440 | tf_op jit(solution)/shard_map/mid_own_11/ppermute | solution.py:224
  33.5 0.7 collective-permute-start.9
  34.2 1.2 %collective-permute-start.13 = (bf16[32,32,256]{2,1,0:T(8,128)(2,1)S(1)}, bf16[32,32,256]{2,1,0:T(8,128)(2,1)}, u32[]{:S(2)}, u32[]{:S(2)}) collective-permute-start(bf16[32,32,256]{2,1,0:T(8,128)(2,1)S(1)} %collective-permute-done.5.rest_4_), channel_id=1, source_target_pairs={{0,1},{1,0},{2,3},{3,2},{4,8},{5,9},{6,10},{7,11},{8,4},{9,5},{10,... | collective-permute-start | bytes 1572872 | tf_op jit(solution)/shard_map/mid_next_0/ppermute | solution.py:224
  35.5 0.7 copy-done.5
  36.2 0.3 collective-permute-start.7
  36.5 0.8 collective-permute-done.8.rest_5_
  37.3 3.7 %collective-permute-start.14 = (bf16[16,32,256]{2,1,0:T(8,128)(2,1)}, bf16[16,32,256]{2,1,0:T(8,128)(2,1)}, u32[]{:S(2)}, u32[]{:S(2)}) collective-permute-start(bf16[16,32,256]{2,1,0:T(8,128)(2,1)} %collective-permute-done.6.rest_5_), channel_id=1, source_target_pairs={{0,1},{1,0},{2,3},{3,2},{4,8},{5,9},{6,10},{7,11},{8,4},{9,5},{10,... | collective-permute-start | bytes 786440 | tf_op jit(solution)/shard_map/mid_next_10/ppermute | solution.py:224
  41.1 0.5 collective-permute-start.10
  41.5 2.9 %collective-permute-done.7.rest_1_ = bf16[16,32,256]{2,1,0:T(8,128)(2,1)} collective-permute-done((bf16[16,32,256]{2,1,0:T(8,128)(2,1)}, bf16[16,32,256]{2,1,0:T(8,128)(2,1)}, u32[]{:S(2)}, u32[]{:S(2)}) %collective-permute-start.7) | collective-permute-done | bytes 262176 | tf_op jit(solution)/shard_map/cross_left_1/ppermute | solution.py:224
  44.4 0.8 collective-permute-start.21
  45.2 13.2 %collective-permute-start.19 = (bf16[16,32,256]{2,1,0:T(8,128)(2,1)}, bf16[16,32,256]{2,1,0:T(8,128)(2,1)S(1)}, u32[]{:S(2)}, u32[]{:S(2)}) collective-permute-start(bf16[16,32,256]{2,1,0:T(8,128)(2,1)} %collective-permute-done.7.rest_1_), channel_id=1, source_target_pairs={{0,4},{1,5},{2,6},{3,7},{4,0},{5,1},{6,2},{7,3},{8,12},{9,13},{10,... | collective-permute-start | bytes 786440 | tf_op jit(solution)/shard_map/end_left_11/ppermute | solution.py:224
  58.4 0.1 pad_add_fusion.2.places
  58.4 0.9 gate.1
  59.3 0.1 pad_add_fusion.3.places
  59.4 1.5 %near.2 = bf16[16,64,128]{2,1,0:T(8,128)(2,1)S(1)} custom-call(s32[3]{0:T(128)S(1)} %pad_add_fusion.2.places, bf16[32,32,256]{2,1,0:T(8,128)(2,1)S(1)} %get-tuple-element.68.rest_0_, bf16[16,32,256]{2,1,0:T(8,128)(2,1)S(1)} %collective-permute-done.4.rest_1_, bf16[32,32,256]{2,1,0:T(8,128)(2,1)S(1)} %get-tuple-element.64.rest_2_, ...), custom_call_target="tpu_custom_call" | custom-call | tf_op jit(solution)/shard_map/near/pallas_call | solution.py:191
  61.0 1.7 %near.3 = bf16[16,64,128]{2,1,0:T(8,128)(2,1)S(1)} custom-call(s32[3]{0:T(128)S(1)} %pad_add_fusion.2.places, bf16[32,32,256]{2,1,0:T(8,128)(2,1)S(1)} %get-tuple-element.68.rest_0_, bf16[16,32,256]{2,1,0:T(8,128)(2,1)} %collective-permute-done.7.rest_1_, bf16[32,32,256]{2,1,0:T(8,128)(2,1)S(1)} %get-tuple-element.64.rest_2_, ...), custom_call_target="tpu_custom_call" | custom-call | tf_op jit(solution)/shard_map/near/pallas_call | solution.py:191
  62.7 1.8 %away.2 = (bf16[16,64,128]{2,1,0:T(8,128)(2,1)S(1)}, bf16[16,64,128]{2,1,0:T(8,128)(2,1)S(1)}) custom-call(s32[3]{0:T(128)S(1)} %pad_add_fusion.3.places, bf16[32,32,256]{2,1,0:T(8,128)(2,1)S(1)} %get-tuple-element.68.rest_0_, bf16[16,32,256]{2,1,0:T(8,128)(2,1)S(1)} %collective-permute-done.4.rest_1_, bf16[32,32,256]{2,1,0:T(8,128)(2,1)} %collective-permute-done.9.rest_2_, ...), custom_call_target="tpu_custom_call" | custom-call | tf_op jit(solution)/shard_map/away/pallas_call | solution.py:191
  64.5 0.1 collective-permute-start.15
  64.6 0.0 copy-start.9
  64.6 0.0 copy-start.8
  64.6 1.9 %away.3 = (bf16[16,64,128]{2,1,0:T(8,128)(2,1)S(1)}, bf16[16,64,128]{2,1,0:T(8,128)(2,1)S(1)}) custom-call(s32[3]{0:T(128)S(1)} %pad_add_fusion.3.places, bf16[32,32,256]{2,1,0:T(8,128)(2,1)S(1)} %get-tuple-element.68.rest_0_, bf16[16,32,256]{2,1,0:T(8,128)(2,1)} %collective-permute-done.7.rest_1_, bf16[32,32,256]{2,1,0:T(8,128)(2,1)} %collective-permute-done.9.rest_2_, ...), custom_call_target="tpu_custom_call" | custom-call | tf_op jit(solution)/shard_map/away/pallas_call | solution.py:191
  66.5 1.5 %collective-permute-start.22 = (bf16[16,64,128]{2,1,0:T(8,128)(2,1)S(1)}, bf16[16,64,128]{2,1,0:T(8,128)(2,1)S(1)}, u32[]{:S(2)}, u32[]{:S(2)}) collective-permute-start(bf16[16,64,128]{2,1,0:T(8,128)(2,1)S(1)} %get-tuple-element.82), channel_id=1, source_target_pairs={{0,4},{1,5},{2,6},{3,7},{4,0},{5,1},{6,2},{7,3},{8,12},{9,13},{10,... | collective-permute-start | bytes 786440 | tf_op jit(solution)/shard_map/products_back_1/ppermute | solution.py:224
  68.0 1.8 %collective-permute-done.15.end = bf16[16,64,128]{2,1,0:T(8,128)(2,1)S(1)} collective-permute-done((bf16[16,64,128]{2,1,0:T(8,128)(2,1)S(1)}, bf16[16,64,128]{2,1,0:T(8,128)(2,1)S(1)}, u32[]{:S(2)}, u32[]{:S(2)}) %collective-permute-start.15) | collective-permute-done | bytes 262176 | tf_op jit(solution)/shard_map/products_back_0/ppermute | solution.py:224
  69.8 0.7 hand_out.2
  70.4 6.4 %collective-permute-start.16 = (bf16[16,32,128]{2,1,0:T(8,128)(2,1)S(1)}, bf16[16,32,128]{2,1,0:T(8,128)(2,1)S(1)}, u32[]{:S(2)}, u32[]{:S(2)}) collective-permute-start(bf16[16,32,128]{2,1,0:T(8,128)(2,1)S(1)} %get-tuple-element.75), channel_id=1, source_target_pairs={{0,1},{1,0},{2,3},{3,2},{4,5},{5,4},{6,7},{7,6},{8,9},{9,8},{10,11... | collective-permute-start | bytes 393224 | tf_op jit(solution)/shard_map/return_01/ppermute | solution.py:224
  76.8 0.2 collective-permute-start.17
  77.1 1.5 %collective-permute-start.18 = (bf16[16,32,128]{2,1,0:T(8,128)(2,1)S(1)}, bf16[16,32,128]{2,1,0:T(8,128)(2,1)S(1)}, u32[]{:S(2)}, u32[]{:S(2)}) collective-permute-start(bf16[16,32,128]{2,1,0:T(8,128)(2,1)S(1)} %get-tuple-element.77), channel_id=1, source_target_pairs={{0,3},{1,2},{2,1},{3,0},{4,7},{5,6},{6,5},{7,4},{8,11},{9,10},{10,... | collective-permute-start | bytes 393224 | tf_op jit(solution)/shard_map/return_03/ppermute | solution.py:224
  78.5 0.7 hand_out.3
  79.2 0.4 collective-permute-start.23
  79.6 0.2 collective-permute-start.24
  79.8 1.6 %collective-permute-start.25 = (bf16[16,32,128]{2,1,0:T(8,128)(2,1)S(1)}, bf16[16,32,128]{2,1,0:T(8,128)(2,1)S(1)}, u32[]{:S(2)}, u32[]{:S(2)}) collective-permute-start(bf16[16,32,128]{2,1,0:T(8,128)(2,1)S(1)} %get-tuple-element.86), channel_id=1, source_target_pairs={{0,3},{1,2},{2,1},{3,0},{4,7},{5,6},{6,5},{7,4},{8,11},{9,10},{10,... | collective-permute-start | bytes 393224 | tf_op jit(solution)/shard_map/return_13/ppermute | solution.py:224
  81.4 0.5 collective-permute-done.17.rest_2_
  81.9 3.4 %collective-permute-done.18.rest_3_ = bf16[16,32,128]{2,1,0:T(8,128)(2,1)S(1)} collective-permute-done((bf16[16,32,128]{2,1,0:T(8,128)(2,1)S(1)}, bf16[16,32,128]{2,1,0:T(8,128)(2,1)S(1)}, u32[]{:S(2)}, u32[]{:S(2)}) %collective-permute-start.18) | collective-permute-done | bytes 131104 | tf_op jit(solution)/shard_map/return_03/ppermute | solution.py:224
  85.3 2.2 %collective-permute-done.24.rest_6_ = bf16[16,32,128]{2,1,0:T(8,128)(2,1)S(1)} collective-permute-done((bf16[16,32,128]{2,1,0:T(8,128)(2,1)S(1)}, bf16[16,32,128]{2,1,0:T(8,128)(2,1)S(1)}, u32[]{:S(2)}, u32[]{:S(2)}) %collective-permute-start.24) | collective-permute-done | bytes 131104 | tf_op jit(solution)/shard_map/return_12/ppermute | solution.py:224
  87.5 3.0 %collective-permute-done.25.rest_7_ = bf16[16,32,128]{2,1,0:T(8,128)(2,1)S(1)} collective-permute-done((bf16[16,32,128]{2,1,0:T(8,128)(2,1)S(1)}, bf16[16,32,128]{2,1,0:T(8,128)(2,1)S(1)}, u32[]{:S(2)}, u32[]{:S(2)}) %collective-permute-start.25) | collective-permute-done | bytes 131104 | tf_op jit(solution)/shard_map/return_13/ppermute | solution.py:224
  90.5 0.1 broadcast_in_dim.6.scale
  90.6 0.0 copy-done.8
  90.6 3.1 %update.1 = bf16[32,128,128]{2,1,0:T(8,128)(2,1)} custom-call(s32[3]{0:T(128)S(1)} %pad_add_fusion.1.where, f32[128,128]{1,0:T(8,128)S(1)} %broadcast_in_dim.6.scale, bf16[128,128]{1,0:T(8,128)(2,1)S(1)} %copy-done.8, f32[32,128,128]{2,1,0:T(8,128)S(1)} %gate.1, bf16[16,32,128]{2,1,0:T(8,128)(2,1)S(1)} %get-tuple-element.74.rest_0_, ...), custom_call_target="tpu_custom_call" | custom-call | tf_op jit(solution)/shard_map/update/pallas_call | solution.py:191
  (27 shorter events, 0.1 us)
Async XLA Ops:
  0.0 6.3 %collective-permute-start = (bf16[32,128,128]{2,1,0:T(8,128)(2,1)}, bf16[32,128,128]{2,1,0:T(8,128)(2,1)S(1)}, u32[]{:S(2)}, u32[]{:S(2)}) collective-permute-start(bf16[32,128,128]{2,1,0:T(8,128)(2,1)} %pair.1), channel_id=1, source_target_pairs={{0,1},{1,0},{2,3},{3,2},{4,5},{5,4},{6,7},{7,6},{8,9},{9,8},{10,11... | collective-permute-start | bytes 3145736 | tf_op jit(solution)/shard_map/pair/ppermute | solution.py:224
  0.1 6.3 %collective-permute-start.1 = (s32[32,128]{1,0:T(8,128)}, s32[32,128]{1,0:T(8,128)S(1)}, u32[]{:S(2)}, u32[]{:S(2)}) collective-permute-start(s32[32,128]{1,0:T(8,128)} %param.8), channel_id=1, source_target_pairs={{0,1},{1,0},{2,3},{3,2},{4,5},{5,4},{6,7},{7,6},{8,9},{9,8},{10,11... | collective-permute-start | bytes 49160 | tf_op jit(solution)/shard_map/mask/ppermute | solution.py:224
  2.3 1.2 %copy-start = (bf16[32,128,128]{2,1,0:T(8,128)(2,1)S(1)}, bf16[32,128,128]{2,1,0:T(8,128)(2,1)}, u32[]{:S(2)}) copy-start(bf16[32,128,128]{2,1,0:T(8,128)(2,1)} %pair.1) | copy-start | bytes 3145732
  3.5 54.9 %copy-start.7 = (bf16[128,128]{1,0:T(8,128)(2,1)S(1)}, bf16[128,128]{1,0:T(8,128)(2,1)}, u32[]{:S(2)}) copy-start(bf16[128,128]{1,0:T(8,128)(2,1)} %weight.2) | copy-start | bytes 98308
  6.3 1.0 %copy-start.1 = (bf16[32,128,128]{2,1,0:T(8,128)(2,1)}, bf16[32,128,128]{2,1,0:T(8,128)(2,1)S(1)}, u32[]{:S(2)}) copy-start(bf16[32,128,128]{2,1,0:T(8,128)(2,1)S(1)} %collective-permute-done.pair) | copy-start | bytes 3145732
  7.3 1.2 %copy-start.2 = (bf16[32,128,128]{2,1,0:T(8,128)(2,1)S(1)}, bf16[32,128,128]{2,1,0:T(8,128)(2,1)}, u32[]{:S(2)}) copy-start(bf16[32,128,128]{2,1,0:T(8,128)(2,1)} %copy-done.1) | copy-start | bytes 3145732
  10.9 8.5 %collective-permute-start.2 = (bf16[16,32,256]{2,1,0:T(8,128)(2,1)S(1)}, bf16[16,32,256]{2,1,0:T(8,128)(2,1)S(1)}, u32[]{:S(2)}, u32[]{:S(2)}) collective-permute-start(bf16[16,32,256]{2,1,0:T(8,128)(2,1)S(1)} %get-tuple-element.61), channel_id=1, source_target_pairs={{0,2},{1,3},{2,0},{3,1},{4,6},{5,7},{6,4},{7,5},{8,10},{9,11},{10,... | collective-permute-start | bytes 786440 | tf_op jit(solution)/shard_map/cross_right_0/ppermute | solution.py:224
  13.2 17.2 %collective-permute-start.5 = (bf16[32,32,256]{2,1,0:T(8,128)(2,1)S(1)}, bf16[32,32,256]{2,1,0:T(8,128)(2,1)S(1)}, u32[]{:S(2)}, u32[]{:S(2)}) collective-permute-start(bf16[32,32,256]{2,1,0:T(8,128)(2,1)S(1)} %get-tuple-element.64.rest_2_), channel_id=1, source_target_pairs={{0,4},{1,5},{2,6},{3,7},{4,0},{5,1},{6,2},{7,3},{8,12},{9,13},{10,... | collective-permute-start | bytes 1572872 | tf_op jit(solution)/shard_map/end_right_0/ppermute | solution.py:224
  14.5 15.9 %collective-permute-start.11 = (bf16[32,32,256]{2,1,0:T(8,128)(2,1)S(1)}, bf16[32,32,256]{2,1,0:T(8,128)(2,1)S(1)}, u32[]{:S(2)}, u32[]{:S(2)}) collective-permute-start(bf16[32,32,256]{2,1,0:T(8,128)(2,1)S(1)} %get-tuple-element.64.rest_2_), channel_id=1, source_target_pairs={{0,1},{1,0},{2,3},{3,2},{4,8},{5,9},{6,10},{7,11},{8,4},{9,5},{10,... | collective-permute-start | bytes 1572872 | tf_op jit(solution)/shard_map/mid_own_0/ppermute | solution.py:224
  19.4 6.9 %collective-permute-start.3 = (bf16[16,32,256]{2,1,0:T(8,128)(2,1)S(1)}, bf16[16,32,256]{2,1,0:T(8,128)(2,1)}, u32[]{:S(2)}, u32[]{:S(2)}) collective-permute-start(bf16[16,32,256]{2,1,0:T(8,128)(2,1)S(1)} %get-tuple-element.62), channel_id=1, source_target_pairs={{0,2},{1,3},{2,0},{3,1},{4,6},{5,7},{6,4},{7,5},{8,10},{9,11},{10,... | collective-permute-start | bytes 786440 | tf_op jit(solution)/shard_map/cross_right_1/ppermute | solution.py:224
  20.5 13.0 %collective-permute-start.6 = (bf16[16,32,256]{2,1,0:T(8,128)(2,1)S(1)}, bf16[16,32,256]{2,1,0:T(8,128)(2,1)}, u32[]{:S(2)}, u32[]{:S(2)}) collective-permute-start(bf16[16,32,256]{2,1,0:T(8,128)(2,1)S(1)} %collective-permute-done.2.rest_3_), channel_id=1, source_target_pairs={{0,4},{1,5},{2,6},{3,7},{4,0},{5,1},{6,2},{7,3},{8,12},{9,13},{10,... | collective-permute-start | bytes 786440 | tf_op jit(solution)/shard_map/end_right_10/ppermute | solution.py:224
  26.3 8.0 %collective-permute-start.4 = (bf16[16,32,256]{2,1,0:T(8,128)(2,1)S(1)}, bf16[16,32,256]{2,1,0:T(8,128)(2,1)S(1)}, u32[]{:S(2)}, u32[]{:S(2)}) collective-permute-start(bf16[16,32,256]{2,1,0:T(8,128)(2,1)S(1)} %get-tuple-element.63), channel_id=1, source_target_pairs={{0,2},{1,3},{2,0},{3,1},{4,6},{5,7},{6,4},{7,5},{8,10},{9,11},{10,... | collective-permute-start | bytes 786440 | tf_op jit(solution)/shard_map/cross_left_0/ppermute | solution.py:224
  27.1 8.4 %collective-permute-start.12 = (bf16[16,32,256]{2,1,0:T(8,128)(2,1)S(1)}, bf16[16,32,256]{2,1,0:T(8,128)(2,1)S(1)}, u32[]{:S(2)}, u32[]{:S(2)}) collective-permute-start(bf16[16,32,256]{2,1,0:T(8,128)(2,1)S(1)} %collective-permute-done.2.rest_3_), channel_id=1, source_target_pairs={{0,1},{1,0},{2,3},{3,2},{4,8},{5,9},{6,10},{7,11},{8,4},{9,5},{10,... | collective-permute-start | bytes 786440 | tf_op jit(solution)/shard_map/mid_own_10/ppermute | solution.py:224
  29.6 0.7 copy-start.3
  30.3 7.0 %collective-permute-start.8 = (bf16[16,32,256]{2,1,0:T(8,128)(2,1)}, bf16[16,32,256]{2,1,0:T(8,128)(2,1)}, u32[]{:S(2)}, u32[]{:S(2)}) collective-permute-start(bf16[16,32,256]{2,1,0:T(8,128)(2,1)} %collective-permute-done.3.rest_3_), channel_id=1, source_target_pairs={{0,4},{1,5},{2,6},{3,7},{4,0},{5,1},{6,2},{7,3},{8,12},{9,13},{10,... | collective-permute-start | bytes 786440 | tf_op jit(solution)/shard_map/end_right_11/ppermute | solution.py:224
  30.4 10.7 %collective-permute-start.20 = (bf16[16,32,256]{2,1,0:T(8,128)(2,1)}, bf16[16,32,256]{2,1,0:T(8,128)(2,1)}, u32[]{:S(2)}, u32[]{:S(2)}) collective-permute-start(bf16[16,32,256]{2,1,0:T(8,128)(2,1)} %collective-permute-done.3.rest_3_), channel_id=1, source_target_pairs={{0,1},{1,0},{2,3},{3,2},{4,8},{5,9},{6,10},{7,11},{8,4},{9,5},{10,... | collective-permute-start | bytes 786440 | tf_op jit(solution)/shard_map/mid_own_11/ppermute | solution.py:224
  33.5 29.2 %collective-permute-start.9 = (bf16[32,32,256]{2,1,0:T(8,128)(2,1)S(1)}, bf16[32,32,256]{2,1,0:T(8,128)(2,1)}, u32[]{:S(2)}, u32[]{:S(2)}) collective-permute-start(bf16[32,32,256]{2,1,0:T(8,128)(2,1)S(1)} %get-tuple-element.68.rest_0_), channel_id=1, source_target_pairs={{0,4},{1,5},{2,6},{3,7},{4,0},{5,1},{6,2},{7,3},{8,12},{9,13},{10,... | collective-permute-start | bytes 1572872 | tf_op jit(solution)/shard_map/end_left_0/ppermute | solution.py:224
  34.2 28.4 %collective-permute-start.13 = (bf16[32,32,256]{2,1,0:T(8,128)(2,1)S(1)}, bf16[32,32,256]{2,1,0:T(8,128)(2,1)}, u32[]{:S(2)}, u32[]{:S(2)}) collective-permute-start(bf16[32,32,256]{2,1,0:T(8,128)(2,1)S(1)} %collective-permute-done.5.rest_4_), channel_id=1, source_target_pairs={{0,1},{1,0},{2,3},{3,2},{4,8},{5,9},{6,10},{7,11},{8,4},{9,5},{10,... | collective-permute-start | bytes 1572872 | tf_op jit(solution)/shard_map/mid_next_0/ppermute | solution.py:224
  35.5 0.7 copy-start.5
  36.2 8.3 %collective-permute-start.7 = (bf16[16,32,256]{2,1,0:T(8,128)(2,1)}, bf16[16,32,256]{2,1,0:T(8,128)(2,1)}, u32[]{:S(2)}, u32[]{:S(2)}) collective-permute-start(bf16[16,32,256]{2,1,0:T(8,128)(2,1)} %get-tuple-element.66), channel_id=1, source_target_pairs={{0,2},{1,3},{2,0},{3,1},{4,6},{5,7},{6,4},{7,5},{8,10},{9,11},{10,... | collective-permute-start | bytes 786440 | tf_op jit(solution)/shard_map/cross_left_1/ppermute | solution.py:224
  37.3 7.9 %collective-permute-start.14 = (bf16[16,32,256]{2,1,0:T(8,128)(2,1)}, bf16[16,32,256]{2,1,0:T(8,128)(2,1)}, u32[]{:S(2)}, u32[]{:S(2)}) collective-permute-start(bf16[16,32,256]{2,1,0:T(8,128)(2,1)} %collective-permute-done.6.rest_5_), channel_id=1, source_target_pairs={{0,1},{1,0},{2,3},{3,2},{4,8},{5,9},{6,10},{7,11},{8,4},{9,5},{10,... | collective-permute-start | bytes 786440 | tf_op jit(solution)/shard_map/mid_next_10/ppermute | solution.py:224
  41.0 18.4 %copy-start.4 = (bf16[16,32,256]{2,1,0:T(8,128)(2,1)S(1)}, bf16[16,32,256]{2,1,0:T(8,128)(2,1)}, u32[]{:S(2)}) copy-start(bf16[16,32,256]{2,1,0:T(8,128)(2,1)} %copy-done.3) | copy-start | bytes 786436
  41.1 21.6 %collective-permute-start.10 = (bf16[16,32,256]{2,1,0:T(8,128)(2,1)S(1)}, bf16[16,32,256]{2,1,0:T(8,128)(2,1)S(1)}, u32[]{:S(2)}, u32[]{:S(2)}) collective-permute-start(bf16[16,32,256]{2,1,0:T(8,128)(2,1)S(1)} %collective-permute-done.4.rest_1_), channel_id=1, source_target_pairs={{0,4},{1,5},{2,6},{3,7},{4,0},{5,1},{6,2},{7,3},{8,12},{9,13},{10,... | collective-permute-start | bytes 786440 | tf_op jit(solution)/shard_map/end_left_10/ppermute | solution.py:224
  44.4 20.2 %collective-permute-start.21 = (bf16[16,32,256]{2,1,0:T(8,128)(2,1)}, bf16[16,32,256]{2,1,0:T(8,128)(2,1)S(1)}, u32[]{:S(2)}, u32[]{:S(2)}) collective-permute-start(bf16[16,32,256]{2,1,0:T(8,128)(2,1)} %collective-permute-done.8.rest_5_), channel_id=1, source_target_pairs={{0,1},{1,0},{2,3},{3,2},{4,8},{5,9},{6,10},{7,11},{8,4},{9,5},{10,... | collective-permute-start | bytes 786440 | tf_op jit(solution)/shard_map/mid_next_11/ppermute | solution.py:224
  45.2 19.4 %collective-permute-start.19 = (bf16[16,32,256]{2,1,0:T(8,128)(2,1)}, bf16[16,32,256]{2,1,0:T(8,128)(2,1)S(1)}, u32[]{:S(2)}, u32[]{:S(2)}) collective-permute-start(bf16[16,32,256]{2,1,0:T(8,128)(2,1)} %collective-permute-done.7.rest_1_), channel_id=1, source_target_pairs={{0,4},{1,5},{2,6},{3,7},{4,0},{5,1},{6,2},{7,3},{8,12},{9,13},{10,... | collective-permute-start | bytes 786440 | tf_op jit(solution)/shard_map/end_left_11/ppermute | solution.py:224
  59.4 3.3 %copy-start.6 = (bf16[16,32,256]{2,1,0:T(8,128)(2,1)S(1)}, bf16[16,32,256]{2,1,0:T(8,128)(2,1)}, u32[]{:S(2)}) copy-start(bf16[16,32,256]{2,1,0:T(8,128)(2,1)} %copy-done.5) | copy-start | bytes 786436
  64.5 5.3 %collective-permute-start.15 = (bf16[16,64,128]{2,1,0:T(8,128)(2,1)S(1)}, bf16[16,64,128]{2,1,0:T(8,128)(2,1)S(1)}, u32[]{:S(2)}, u32[]{:S(2)}) collective-permute-start(bf16[16,64,128]{2,1,0:T(8,128)(2,1)S(1)} %get-tuple-element.73), channel_id=1, source_target_pairs={{0,4},{1,5},{2,6},{3,7},{4,0},{5,1},{6,2},{7,3},{8,12},{9,13},{10,... | collective-permute-start | bytes 786440 | tf_op jit(solution)/shard_map/products_back_0/ppermute | solution.py:224
  64.6 25.9 %copy-start.9 = (f32[128]{0:T(128)S(1)}, f32[128]{0:T(128)}, u32[]{:S(2)}) copy-start(f32[128]{0:T(128)} %param.12) | copy-start | bytes 1540
  64.6 26.0 %copy-start.8 = (bf16[128,128]{1,0:T(8,128)(2,1)S(1)}, bf16[128,128]{1,0:T(8,128)(2,1)}, u32[]{:S(2)}) copy-start(bf16[128,128]{1,0:T(8,128)(2,1)} %weight.3) | copy-start | bytes 98308
  66.5 12.0 %collective-permute-start.22 = (bf16[16,64,128]{2,1,0:T(8,128)(2,1)S(1)}, bf16[16,64,128]{2,1,0:T(8,128)(2,1)S(1)}, u32[]{:S(2)}, u32[]{:S(2)}) collective-permute-start(bf16[16,64,128]{2,1,0:T(8,128)(2,1)S(1)} %get-tuple-element.82), channel_id=1, source_target_pairs={{0,4},{1,5},{2,6},{3,7},{4,0},{5,1},{6,2},{7,3},{8,12},{9,13},{10,... | collective-permute-start | bytes 786440 | tf_op jit(solution)/shard_map/products_back_1/ppermute | solution.py:224
  70.4 9.4 %collective-permute-start.16 = (bf16[16,32,128]{2,1,0:T(8,128)(2,1)S(1)}, bf16[16,32,128]{2,1,0:T(8,128)(2,1)S(1)}, u32[]{:S(2)}, u32[]{:S(2)}) collective-permute-start(bf16[16,32,128]{2,1,0:T(8,128)(2,1)S(1)} %get-tuple-element.75), channel_id=1, source_target_pairs={{0,1},{1,0},{2,3},{3,2},{4,5},{5,4},{6,7},{7,6},{8,9},{9,8},{10,11... | collective-permute-start | bytes 393224 | tf_op jit(solution)/shard_map/return_01/ppermute | solution.py:224
  76.8 5.1 %collective-permute-start.17 = (bf16[16,32,128]{2,1,0:T(8,128)(2,1)S(1)}, bf16[16,32,128]{2,1,0:T(8,128)(2,1)S(1)}, u32[]{:S(2)}, u32[]{:S(2)}) collective-permute-start(bf16[16,32,128]{2,1,0:T(8,128)(2,1)S(1)} %get-tuple-element.76), channel_id=1, source_target_pairs={{0,2},{1,3},{2,0},{3,1},{4,6},{5,7},{6,4},{7,5},{8,10},{9,11},{10,... | collective-permute-start | bytes 393224 | tf_op jit(solution)/shard_map/return_02/ppermute | solution.py:224
  77.1 8.3 %collective-permute-start.18 = (bf16[16,32,128]{2,1,0:T(8,128)(2,1)S(1)}, bf16[16,32,128]{2,1,0:T(8,128)(2,1)S(1)}, u32[]{:S(2)}, u32[]{:S(2)}) collective-permute-start(bf16[16,32,128]{2,1,0:T(8,128)(2,1)S(1)} %get-tuple-element.77), channel_id=1, source_target_pairs={{0,3},{1,2},{2,1},{3,0},{4,7},{5,6},{6,5},{7,4},{8,11},{9,10},{10,... | collective-permute-start | bytes 393224 | tf_op jit(solution)/shard_map/return_03/ppermute | solution.py:224
  79.2 6.1 %collective-permute-start.23 = (bf16[16,32,128]{2,1,0:T(8,128)(2,1)S(1)}, bf16[16,32,128]{2,1,0:T(8,128)(2,1)S(1)}, u32[]{:S(2)}, u32[]{:S(2)}) collective-permute-start(bf16[16,32,128]{2,1,0:T(8,128)(2,1)S(1)} %get-tuple-element.84), channel_id=1, source_target_pairs={{0,1},{1,0},{2,3},{3,2},{4,5},{5,4},{6,7},{7,6},{8,9},{9,8},{10,11... | collective-permute-start | bytes 393224 | tf_op jit(solution)/shard_map/return_11/ppermute | solution.py:224
  79.6 7.9 %collective-permute-start.24 = (bf16[16,32,128]{2,1,0:T(8,128)(2,1)S(1)}, bf16[16,32,128]{2,1,0:T(8,128)(2,1)S(1)}, u32[]{:S(2)}, u32[]{:S(2)}) collective-permute-start(bf16[16,32,128]{2,1,0:T(8,128)(2,1)S(1)} %get-tuple-element.85), channel_id=1, source_target_pairs={{0,2},{1,3},{2,0},{3,1},{4,6},{5,7},{6,4},{7,5},{8,10},{9,11},{10,... | collective-permute-start | bytes 393224 | tf_op jit(solution)/shard_map/return_12/ppermute | solution.py:224
  79.8 10.6 %collective-permute-start.25 = (bf16[16,32,128]{2,1,0:T(8,128)(2,1)S(1)}, bf16[16,32,128]{2,1,0:T(8,128)(2,1)S(1)}, u32[]{:S(2)}, u32[]{:S(2)}) collective-permute-start(bf16[16,32,128]{2,1,0:T(8,128)(2,1)S(1)} %get-tuple-element.86), channel_id=1, source_target_pairs={{0,3},{1,2},{2,1},{3,0},{4,7},{5,6},{6,5},{7,4},{8,11},{9,10},{10,... | collective-permute-start | bytes 393224 | tf_op jit(solution)/shard_map/return_13/ppermute | solution.py:224

commit v7 on v6

v7 whole, which is shorter than its diff:
```python
import functools
import math

import jax
import jax.numpy as jnp
from jax import lax
from jax.experimental import pallas as pl
from jax.experimental.pallas import tpu as pltpu
from jax.sharding import PartitionSpec as P

F32, BF16 = jnp.float32, jnp.bfloat16
LANES = 128
SPARE = 6 * 1024 * 1024
SHARES = (5, 3)
NT = (((1,), (1,)), ((), ()))
TN = (((0,), (0,)), ((), ()))
VMEM = pl.BlockSpec(memory_space=pltpu.VMEM)
GROUP = 4
UNROLL = 2


def place():
    row = lax.axis_index("row")
    return row // 2, row % 2, lax.axis_index("chan")


def normalise(x, gain):
    mean = jnp.mean(x, axis=-1, keepdims=True)
    centered = x - mean
    var = jnp.mean(centered * centered, axis=-1, keepdims=True)
    return (centered * lax.rsqrt(var + 1e-05) * gain).astype(BF16)


def gated(normed, chosen, valid, first, held):
    _, rows, toks = valid.shape
    wide = chosen.shape[0] // 2
    proj = lax.dot_general(chosen[...], normed, NT, preferred_element_type=F32)
    for g in range(normed.shape[0] // toks):
        mine = proj[:, g * toks : (g + 1) * toks]
        value = (jnp.tanh(mine[:wide]) + 1.0) * (valid[0, pl.ds(first + g, 1), :] * mine[wide:])
        for m in range(toks // LANES):
            spot = pl.ds(first + g, wide, stride=rows + 1)
            held[m, spot, :] = value[:, m * LANES : (m + 1) * LANES]


def write_pieces(outs, held, base):
    row = 0
    for out in outs:
        count, rows, _ = out.shape
        for c in range(count):
            for m in range(held.shape[0]):
                lanes = slice(base + m * LANES, base + (m + 1) * LANES)
                out[c, :, lanes] = held[m, row : row + rows, :].astype(BF16)
            row += rows + 1


def right_rows(pair, valid, gain, chosen, normed_out, held):
    rows, toks, _ = pair.shape

    @pl.loop(0, rows // GROUP, unroll=UNROLL)
    def _(at):
        first = at * GROUP
        x = pair[pl.ds(first, GROUP)].astype(F32).reshape(GROUP * toks, -1)
        normed = normalise(x, gain[...])
        normed_out[pl.ds(first * toks, GROUP * toks), :] = normed
        gated(normed, chosen, valid, first, held)


def right_own_kernel(pair, mask, gain, weight, *rest):
    *outs, normed_out, chosen_right, chosen_left, valid, turned, held = rest
    hidden = weight.shape[1] // 4
    part = hidden // 4
    _, y, core = place()
    turned[...] = weight[...].T
    valid[0] = mask[...].astype(F32) * 0.5
    for n in range(4):
        chosen = chosen_left if n < 2 else chosen_right
        half = 0.5 if n % 2 == 0 else 1.0
        for p in range(2):
            start = pl.multiple_of(n * hidden + ((2 * y + core) ^ (2 * p)) * part, part)
            at = (2 * (n % 2) + p) * part
            chosen[at : at + part, :] = turned[pl.ds(start, part), :] * half
    right_rows(pair, valid, gain, chosen_right, normed_out, held)
    write_pieces(outs, held, 0)


def right_twin_kernel(pair, mask, gain, chosen, *rest):
    count = (len(rest) - 3) // 2
    before, (*outs, normed_out, valid, held) = rest[:count], rest[count:]
    for x, out in zip(before, outs):
        out[:, :, : x.shape[2]] = x[...]
    valid[0] = mask[...].astype(F32) * 0.5
    right_rows(pair, valid, gain, chosen, normed_out, held)
    write_pieces(outs, held, pair.shape[1])


def left_kernel(normed0, normed1, valid0, valid1, chosen, *rest):
    outs, held = rest[:-1], rest[-1]
    _, rows, toks = valid0.shape
    for n, (normed, valid) in enumerate(((normed0, valid0), (normed1, valid1))):

        @pl.loop(0, rows // GROUP, unroll=UNROLL)
        def _(at):
            first = at * GROUP
            gated(normed[pl.ds(first * toks, GROUP * toks), :], chosen, valid, first, held)

        write_pieces(outs, held, n * toks)


def gate_kernel(normed, weight, out):
    rows, toks, _ = out.shape

    @pl.loop(0, rows // GROUP, unroll=UNROLL)
    def _(at):
        x = normed[pl.ds(at * GROUP * toks, GROUP * toks), :]
        logits = jnp.dot(x, weight[...], preferred_element_type=F32)
        out[pl.ds(at * GROUP, GROUP)] = (0.5 * jnp.tanh(0.5 * logits) + 0.5).reshape(GROUP, toks, -1)


def merge_kernel(own, neighbour, out):
    rows = own.shape[1]
    out[:, :rows, :] = own[...]
    out[:, rows:, :] = neighbour[...]


def product_kernel(mirror, lefts, rights, *rest):
    count, span, width = rest[sum(lefts) + sum(rights)].shape
    rows = span // 2
    refs = iter(rest)

    def plane(arrays):
        if arrays == 1:
            both = next(refs)
            return [both.at[:, :rows, :], both.at[:, rows:, :]]
        return [next(refs), next(refs)]

    lefts, rights = [plane(n) for n in lefts], [plane(n) for n in rights]
    *outs, held = refs
    half = len(rights)
    z, y, _ = place()
    z = 2 * half - 1 - z if mirror else z
    for s in range(half):
        for p in range(2):
            start = pl.multiple_of((z + half - s) % half * span + (y ^ p) * rows, rows)
            held[:, pl.ds(start, rows), :] = rights[s][p][...]
    for c in range(count):
        left = jnp.concatenate([x[c] for side in lefts for x in side], axis=0)
        out = lax.dot_general(left, held[c], NT, preferred_element_type=F32).astype(BF16)
        for n in range(len(lefts)):
            outs[n][c] = out[n * span : (n + 1) * span]


def hand_out_kernel(planes, near, far, end, *outs):
    _, rows, _ = outs[0].shape
    z, _, core = place()
    at_end = (z == 0) | (z == planes - 1)
    for r in range(4):
        is_near = (core ^ (r % 2)) == z // (planes // 2)
        span = slice((r // 2) * rows, (r // 2 + 1) * rows)

        @pl.when(is_near)
        def _():
            outs[r][...] = near[:, span, :]

        @pl.when(jnp.logical_not(is_near | at_end))
        def _():
            outs[r][...] = far[:, span, :]

        @pl.when(jnp.logical_not(is_near) & at_end)
        def _():
            outs[r][...] = end[:, span, :]


def update_kernel(gain, weight, gate, *rest):
    pieces, out, turned = rest[:-2], rest[-2], rest[-1]
    part = sum(x.shape[0] for x in pieces[::4])
    _, rows, toks = pieces[0].shape
    hidden = 4 * part
    pitch = hidden + 1
    _, y, core = place()
    scale = jnp.broadcast_to(gain[...], (toks, hidden)).T
    for r in range(4):
        base = ((2 * y + core) ^ r) * part
        for piece in pieces[r::4]:
            for c in range(piece.shape[0]):
                value = piece[c].astype(F32)
                for m in range(toks // LANES):
                    turned[m, pl.ds(base + c, rows, stride=pitch), :] = value[
                        :, m * LANES : (m + 1) * LANES
                    ]
            base = base + piece.shape[0]

    @pl.loop(0, rows, unroll=8)
    def _(i):
        x = jnp.concatenate(
            [turned[m, pl.ds(i * pitch, hidden), :] for m in range(toks // LANES)], axis=1
        )
        mean = jnp.mean(x, axis=0, keepdims=True)
        centered = x - mean
        var = jnp.mean(centered * centered, axis=0, keepdims=True)
        pnorm = (centered * lax.rsqrt(var + 1e-05) * scale).astype(BF16)
        mapped = lax.dot_general(pnorm, weight[...], TN, preferred_element_type=F32)
        out[i] = (gate[i] * mapped).astype(BF16)


def kernel(body, name, out_shape, in_specs, scratch=()):
    outs = jax.tree.map(lambda _: VMEM, out_shape)

    def call(*args):
        arrays = [*args, *jax.tree.leaves(out_shape), *scratch]
        size = sum(x.dtype.itemsize * math.prod(x.shape) for x in arrays)
        return pl.pallas_call(
            body,
            out_shape=out_shape,
            in_specs=in_specs,
            out_specs=outs,
            scratch_shapes=list(scratch),
            compiler_params=pltpu.CompilerParams(vmem_limit_bytes=size + SPARE),
            name=name,
        )(*args)

    return call


def local(pair, pair_mask, in_gain, proj_weight, gate_weight, out_gain, out_weight, *, n_row):
    rows, toks, channels = pair.shape
    hidden = proj_weight.shape[1] // 4
    part = hidden // 4
    planes = n_row // 2
    half = planes // 2
    counts = [part * share // sum(SHARES) for share in SHARES]
    groups = range(len(counts))
    def send(x, target, name):
        pairs = []
        for source in range(2 * n_row):
            to = target(source // 4, source // 2 % 2, source % 2)
            if to is not None:
                pairs.append((source, 4 * to[0] + 2 * to[1] + to[2]))
        with jax.named_scope(name):
            return lax.ppermute(x, ("row", "chan"), pairs)

    def after(x, *earlier):
        return lax.optimization_barrier((x, *earlier))[0]

    def in_plane(r):
        return lambda p, b, k: (p, b ^ (r // 2), k ^ (r % 2))

    def shifted(s):
        return lambda p, b, k: (p // half * half + (p + s) % half, b, k)

    def mirrored(p, b, k):
        return (p, b, 1 - k) if p in (0, planes - 1) else (planes - 1 - p, b, k)

    def edge(p, b, k):
        swap = {0: 1, 1: 0, planes - 1: planes - 2, planes - 2: planes - 1}
        return (swap[p], b, k) if p in swap else (p, b, 1 - k)

    def outward(p, b, k):
        return {1: (0, b, k), planes - 2: (planes - 1, b, k)}.get(p)

    gains = in_gain.reshape(1, -1)
    twin, twin_mask = send(pair, in_plane(1), "pair"), send(pair_mask, in_plane(1), "mask")

    def piece(count, height, depth):
        return jax.ShapeDtypeStruct((count, height, depth), BF16)

    held = pltpu.VMEM((toks // LANES, 2 * part * (rows + 1), LANES), F32)
    rows_all = jax.ShapeDtypeStruct((rows * toks, channels), BF16)
    weights = jax.ShapeDtypeStruct((4 * part, channels), BF16)
    valid_shape = jax.ShapeDtypeStruct((1, rows, toks), F32)
    *mine, normed0, chosen_right, chosen_left, valid = kernel(
        right_own_kernel,
        "right_own",
        [piece(count, rows, toks) for count in (*counts, *counts)]
        + [rows_all, weights, weights, valid_shape],
        [VMEM] * 4,
        [pltpu.VMEM((4 * hidden, channels), BF16), held],
    )(pair, pair_mask, gains, proj_weight)
    whole = [piece(count, rows, 2 * toks) for count in (*counts, *counts)]
    *right, normed1, twin_valid = kernel(
        right_twin_kernel,
        "right_twin",
        whole + [rows_all, valid_shape],
        [VMEM] * (4 + len(mine)),
        [held],
    )(twin, twin_mask, gains, chosen_right, *mine)
    right0, right1 = list(right[: len(counts)]), list(right[len(counts) :])
    queues = {"y": [], "end": [], "mid": []}

    def queued(link, name, x, target, window=2, also=()):
        done = queues[link]
        early = done[len(done) - window :][:1] if len(done) >= window else []
        done.append(send(after(x, *early, *also), target, name))
        return done[-1]

    def hops(name, right, left):
        far = [queued("mid", f"mid_own_{name}", right, mirrored)]
        near = [right] + [
            queued("end", f"end_right_{name}", right, shifted(s)) for s in range(1, half)
        ]
        return near, far, left

    def last_hops(name, near, far, left):
        far = far + [queued("mid", f"mid_next_{name}", x, mirrored) for x in near[1:]]
        return near, far, left, queued("end", f"end_left_{name}", left, edge)

    def cross(name, x):
        return queued("y", f"cross_{name}", x, in_plane(2), 1)

    def merge(own, neighbour, name):
        shape = piece(own.shape[0], 2 * rows, 2 * toks)
        return kernel(merge_kernel, name, shape, [VMEM, VMEM])(own, neighbour)

    first0 = hops("00", right0[0], None)
    right1[0] = cross("right_0", right1[0])
    left = kernel(left_kernel, "left", whole, [VMEM] * 5, [held])(
        normed0, normed1, valid, twin_valid, chosen_left
    )
    left0, left1 = list(left[: len(counts)]), list(left[len(counts) :])
    first1 = hops("01", after(right1[0], left0[0]), None)
    left1[0] = cross("left_0", after(left1[0], first0[0][-1], first0[1][0]))
    begun = [[("00", *first0[:2], left0[0]), ("01", *first1[:2], left1[0])]]
    moved = [[last_hops(*begun[0][0])]]
    for g in groups[1:]:
        right1[g] = cross(f"right_{g}", right1[g])
        left1[g] = cross(f"left_{g}", left1[g])
        right = merge(right0[g], right1[g], "merge_right")
        left = merge(left0[g], left1[g], "merge_left")
        begun.append([(f"{g}", *hops(f"{g}", right, left))])
    moved[0].append(last_hops(*begun[0][1]))
    moved += [[last_hops(*x) for x in begun[g]] for g in groups[1:]]
    gate = kernel(
        gate_kernel, "gate", jax.ShapeDtypeStruct((rows, toks, channels), F32), [VMEM] * 2
    )(normed0, gate_weight)

    def products(mirror, lefts, rights, name):
        span = 2 * rows * len(rights)
        count = lefts[0][0].shape[0]
        args = [x for arrays in (*lefts, *rights) for x in arrays]
        return kernel(
            functools.partial(
                product_kernel, mirror, [len(x) for x in lefts], [len(x) for x in rights]
            ),
            name,
            [piece(count, 2 * rows, span)] * len(lefts),
            [VMEM] * len(args),
            [pltpu.VMEM((count, span, 2 * toks), BF16)],
        )(*args)

    done, pieces = [], []
    for g in groups:
        near, far, left, outer = zip(*moved[g])
        (close,) = products(False, [left], list(zip(*near)), "near")
        left = (after(left[0], *done), *left[1:])
        away, ends = products(True, [left, outer], list(zip(*far)), "away")
        ends = send(ends, edge if g == groups[-1] else outward, f"products_back_{g}")
        handed = kernel(
            functools.partial(hand_out_kernel, planes),
            "hand_out",
            [piece(counts[g], rows, toks)] * 4,
            [VMEM] * 3,
        )(close, away, ends)
        got = [handed[0]] + [send(handed[r], in_plane(r), f"return_{g}{r}") for r in range(1, 4)]
        done = got[:2]
        pieces += got

    return kernel(
        update_kernel,
        "update",
        jax.ShapeDtypeStruct((rows, toks, channels), BF16),
        [VMEM] * (3 + len(pieces)),
        [pltpu.VMEM((toks // LANES, rows * (hidden + 1), LANES), F32)],
    )(out_gain.reshape(1, -1), out_weight, gate, *pieces)


def solution(mesh):
    placed = (
        P(("groups", "row"), "chan", None),
        P(("groups", "row"), "chan"),
        P(),
        P(),
        P(),
        P(),
        P(),
    )
    return jax.shard_map(
        functools.partial(local, n_row=mesh.shape["row"]),
        mesh=mesh,
        in_specs=placed,
        out_specs=P(("groups", "row"), "chan", None),
        check_vma=False,
    )
```

time: 94.2 us -> 86.3 us (0.916)
  waiting for transfers between devices: 20.2 us -> 33.1 us
  starting transfers between devices: 46.4 us -> 36 us
  Pallas kernels: 19.9 us -> 12.4 us
  other arithmetic: 1.91 us -> 0 us
    ppermute x26, waiting for transfers between devices: 20.2 us -> 33.1 us  [send(): return lax.ppermute(x, ('row', 'chan'), pairs)]
    ppermute x26, starting transfers between devices: 46.4 us -> 36 us  [send(): return lax.ppermute(x, ('row', 'chan'), pairs)]
    pallas_call x11 -> x13, Pallas kernels: 19.9 us -> 12.4 us  [call(): pl.pallas_call(body, out_shape=out_shape, in_specs=in_specs, out_specs=ou...]
    add x1 -> x0, other arithmetic: 0.94 us -> none  [local(): jnp.pad(proj_weight.astype(F32), ((0, rows + 8), (0, 0)))]
    unnamed x20 -> x16, local copies, waits for them, and re-layouts: 4.84 us -> 4.17 us
  transfers between devices with their start and end apart: 26 -> 26, of which waited for: 9 -> 12; matrix products, arithmetic and copies ran while one was open for 2% -> 0% of each run, Pallas kernels for 16% -> 8%
where the time goes in v7:
time: 86.3 us; the launch traced here: 85.9 us
  starting transfers between devices  36 us (42%)
  waiting for transfers between devices  33.1 us (38%)
  Pallas kernels  12.4 us (14%)
  local copies, waits for them, and re-layouts  4.17 us (5%)
    ppermute x26, starting transfers between devices, send(): return lax.ppermute(x, ('row', 'chan'), pairs)  36 us
    ppermute x26, waiting for transfers between devices, send(): return lax.ppermute(x, ('row', 'chan'), pairs)  33.1 us
    pallas_call x13, Pallas kernels, call(): pl.pallas_call(body, out_shape=out_shape, in_specs=in_specs, out_specs=ou...  12.4 us
    unnamed x16, local copies, waits for them, and re-layouts  4.17 us
  transfers between devices with their start and end apart: 26, of which 12 were waited for; matrix products, arithmetic and copies ran while one was open for 0% of the time, Pallas kernels for 8%

profile of v7, /device:TPU:1, one launch (start us, length us, event | category | flops | bytes accessed | tf_op | source)
XLA Modules:
  0.0 85.9 jit_solution(10097043841206683934)
XLA Ops:
  0.0 0.1 collective-permute-start
  0.1 0.5 collective-permute-start.1
  0.5 1.2 %copy-done = bf16[32,128,128]{2,1,0:T(8,128)(2,1)S(1)} copy-done((bf16[32,128,128]{2,1,0:T(8,128)(2,1)S(1)}, bf16[32,128,128]{2,1,0:T(8,128)(2,1)}, u32[]{:S(2)}) %copy-start) | copy-done | bytes 1048600
  1.7 0.9 %copy-done.1 = bf16[128,512]{1,0:T(8,128)(2,1)S(1)} copy-done((bf16[128,512]{1,0:T(8,128)(2,1)S(1)}, bf16[128,512]{1,0:T(8,128)(2,1)}, u32[]{:S(2)}) %copy-start.1) | copy-done | bytes 131096
  2.6 0.7 copy-done.4
  3.4 0.7 copy-done.5
  4.0 2.3 %right_own.1 = (bf16[20,32,128]{2,1,0:T(8,128)(2,1)S(1)}, bf16[12,32,128]{2,1,0:T(8,128)(2,1)S(1)}, bf16[20,32,128]{2,1,0:T(8,128)(2,1)S(1)}, bf16[12,32,128]{2,...) custom-call(bf16[32,128,128]{2,1,0:T(8,128)(2,1)S(1)} %copy-done, ...), custom_call_target="tpu_custom_call" | custom-call | tf_op jit(solution)/shard_map/right_own/pallas_call | solution.py:212
  6.3 0.0 collective-permute-done.1.mask
  6.3 0.0 collective-permute-done.pair
  6.3 0.0 copy-start.6
  6.3 0.6 copy-done.6
  7.0 2.3 %right_twin.1 = (bf16[20,32,256]{2,1,0:T(8,128)(2,1)S(1)}, bf16[12,32,256]{2,1,0:T(8,128)(2,1)S(1)}, bf16[20,32,256]{2,1,0:T(8,128)(2,1)S(1)}, bf16[12,32,256]{2...) custom-call(bf16[32,128,128]{2,1,0:T(8,128)(2,1)S(1)} %collective-permute-done.pair, ...), custom_call_target="tpu_custom_call" | custom-call | tf_op jit(solution)/shard_map/right_twin/pallas_call | solution.py:212
  9.3 0.1 collective-permute-start.3
  9.4 3.5 %collective-permute-start.2 = (bf16[20,32,256]{2,1,0:T(8,128)(2,1)S(1)}, bf16[20,32,256]{2,1,0:T(8,128)(2,1)S(1)}, u32[]{:S(2)}, u32[]{:S(2)}) collective-permute-start(bf16[20,32,256]{2,1,0:T(8,128)(2,1)S(1)} %get-tuple-element.61.rest_2_), channel_id=1, source_target_pairs={{0,4},{1,5},{2,6},{3,7},{4,0},{5,1},{6,2},{7,3},{8,12},{9,13},{10,... | collective-permute-start | bytes 983048 | tf_op jit(solution)/shard_map/end_right_00/ppermute | solution.py:240
  13.0 1.2 %collective-permute-start.4 = (bf16[20,32,256]{2,1,0:T(8,128)(2,1)S(1)}, bf16[20,32,256]{2,1,0:T(8,128)(2,1)S(1)}, u32[]{:S(2)}, u32[]{:S(2)}) collective-permute-start(bf16[20,32,256]{2,1,0:T(8,128)(2,1)S(1)} %get-tuple-element.63), channel_id=1, source_target_pairs={{0,2},{1,3},{2,0},{3,1},{4,6},{5,7},{6,4},{7,5},{8,10},{9,11},{10,... | collective-permute-start | bytes 983048 | tf_op jit(solution)/shard_map/cross_right_0/ppermute | solution.py:240
  14.2 2.0 %left.1 = (bf16[20,32,256]{2,1,0:T(8,128)(2,1)S(1)}, bf16[12,32,256]{2,1,0:T(8,128)(2,1)S(1)}, bf16[20,32,256]{2,1,0:T(8,128)(2,1)S(1)}, bf16[12,32,256]{2,1,0:T(8,128)(2,1)S(1)}) custom-call(bf16[4096,128]{1,0:T(8,128)(2,1)S(1)} %get-tuple-element.49.normed.normed0, bf16[4096,128]{1,0:T(8,128)(2,1)S(1)} %get-tuple-element.55.normed1, ...), custom_call_target="tpu_custom_call" | custom-call | tf_op jit(solution)/shard_map/left/pallas_call | solution.py:212
  16.2 0.0 collective-permute-done.3.rest_4_
  16.2 4.0 %collective-permute-done.2.rest_4_ = bf16[20,32,256]{2,1,0:T(8,128)(2,1)S(1)} collective-permute-done((bf16[20,32,256]{2,1,0:T(8,128)(2,1)S(1)}, bf16[20,32,256]{2,1,0:T(8,128)(2,1)S(1)}, u32[]{:S(2)}, u32[]{:S(2)}) %collective-permute-start.2) | collective-permute-done | bytes 327712 | tf_op jit(solution)/shard_map/end_right_00/ppermute | solution.py:240
  20.3 0.8 collective-permute-done.4.rest_3_
  21.1 1.3 %collective-permute-start.5 = (bf16[20,32,256]{2,1,0:T(8,128)(2,1)S(1)}, bf16[20,32,256]{2,1,0:T(8,128)(2,1)S(1)}, u32[]{:S(2)}, u32[]{:S(2)}) collective-permute-start(bf16[20,32,256]{2,1,0:T(8,128)(2,1)S(1)} %get-tuple-element.64), channel_id=1, source_target_pairs={{0,2},{1,3},{2,0},{3,1},{4,6},{5,7},{6,4},{7,5},{8,10},{9,11},{10,... | collective-permute-start | bytes 983048 | tf_op jit(solution)/shard_map/cross_left_0/ppermute | solution.py:240
  22.3 0.3 collective-permute-start.7
  22.7 1.1 %collective-permute-start.6 = (bf16[20,32,256]{2,1,0:T(8,128)(2,1)S(1)}, bf16[20,32,256]{2,1,0:T(8,128)(2,1)S(1)}, u32[]{:S(2)}, u32[]{:S(2)}) collective-permute-start(bf16[20,32,256]{2,1,0:T(8,128)(2,1)S(1)} %collective-permute-done.4.rest_3_), channel_id=1, source_target_pairs={{0,4},{1,5},{2,6},{3,7},{4,0},{5,1},{6,2},{7,3},{8,12},{9,13},{10,... | collective-permute-start | bytes 983048 | tf_op jit(solution)/shard_map/end_right_01/ppermute | solution.py:240
  23.8 2.8 %collective-permute-start.10 = (bf16[20,32,256]{2,1,0:T(8,128)(2,1)S(1)}, bf16[20,32,256]{2,1,0:T(8,128)(2,1)S(1)}, u32[]{:S(2)}, u32[]{:S(2)}) collective-permute-start(bf16[20,32,256]{2,1,0:T(8,128)(2,1)S(1)} %collective-permute-done.2.rest_4_), channel_id=1, source_target_pairs={{0,1},{1,0},{2,3},{3,2},{4,8},{5,9},{6,10},{7,11},{8,4},{9,5},{10,... | collective-permute-start | bytes 983048 | tf_op jit(solution)/shard_map/mid_next_00/ppermute | solution.py:240
  26.6 1.7 %collective-permute-done.5.rest_1_ = bf16[20,32,256]{2,1,0:T(8,128)(2,1)S(1)} collective-permute-done((bf16[20,32,256]{2,1,0:T(8,128)(2,1)S(1)}, bf16[20,32,256]{2,1,0:T(8,128)(2,1)S(1)}, u32[]{:S(2)}, u32[]{:S(2)}) %collective-permute-start.5) | collective-permute-done | bytes 327712 | tf_op jit(solution)/shard_map/cross_left_0/ppermute | solution.py:240
  28.3 1.3 %collective-permute-start.16 = (bf16[12,32,256]{2,1,0:T(8,128)(2,1)S(1)}, bf16[12,32,256]{2,1,0:T(8,128)(2,1)S(1)}, u32[]{:S(2)}, u32[]{:S(2)}) collective-permute-start(bf16[12,32,256]{2,1,0:T(8,128)(2,1)S(1)} %get-tuple-element.79), channel_id=1, source_target_pairs={{0,2},{1,3},{2,0},{3,1},{4,6},{5,7},{6,4},{7,5},{8,10},{9,11},{10,... | collective-permute-start | bytes 589832 | tf_op jit(solution)/shard_map/cross_right_1/ppermute | solution.py:240
  29.6 0.0 collective-permute-done.7.rest_2_
  29.6 0.6 collective-permute-start.8
  30.2 6.1 %collective-permute-done.6.rest_5_ = bf16[20,32,256]{2,1,0:T(8,128)(2,1)S(1)} collective-permute-done((bf16[20,32,256]{2,1,0:T(8,128)(2,1)S(1)}, bf16[20,32,256]{2,1,0:T(8,128)(2,1)S(1)}, u32[]{:S(2)}, u32[]{:S(2)}) %collective-permute-start.6) | collective-permute-done | bytes 327712 | tf_op jit(solution)/shard_map/end_right_01/ppermute | solution.py:240
  36.3 6.0 %collective-permute-start.11 = (bf16[20,32,256]{2,1,0:T(8,128)(2,1)S(1)}, bf16[20,32,256]{2,1,0:T(8,128)(2,1)S(1)}, u32[]{:S(2)}, u32[]{:S(2)}) collective-permute-start(bf16[20,32,256]{2,1,0:T(8,128)(2,1)S(1)} %collective-permute-done.6.rest_5_), channel_id=1, source_target_pairs={{0,1},{1,0},{2,3},{3,2},{4,8},{5,9},{6,10},{7,11},{8,4},{9,5},{10,... | collective-permute-start | bytes 983048 | tf_op jit(solution)/shard_map/mid_next_01/ppermute | solution.py:240
  42.3 0.0 collective-permute-done.16.neighbour
  42.3 0.1 collective-permute-start.18
  42.4 0.0 collective-permute-done.9.rest_5_
  42.4 2.4 %collective-permute-start.20 = (bf16[12,64,256]{2,1,0:T(8,128)(2,1)S(1)}, bf16[12,64,256]{2,1,0:T(8,128)(2,1)S(1)}, u32[]{:S(2)}, u32[]{:S(2)}) collective-permute-start(bf16[12,64,256]{2,1,0:T(8,128)(2,1)S(1)} %merge_right.1.rest_1_), channel_id=1, source_target_pairs={{0,1},{1,0},{2,3},{3,2},{4,8},{5,9},{6,10},{7,11},{8,4},{9,5},{10,... | collective-permute-start | bytes 1179656 | tf_op jit(solution)/shard_map/mid_own_1/ppermute | solution.py:240
  44.8 0.2 collective-permute-start.17
  45.0 0.0 collective-permute-done.8.rest_3_
  45.0 0.0 collective-permute-done.11.rest_7_
  45.0 0.6 away.2
  45.6 1.3 %collective-permute-start.12 = (bf16[20,64,128]{2,1,0:T(8,128)(2,1)S(1)}, bf16[20,64,128]{2,1,0:T(8,128)(2,1)S(1)}, u32[]{:S(2)}, u32[]{:S(2)}) collective-permute-start(bf16[20,64,128]{2,1,0:T(8,128)(2,1)S(1)} %get-tuple-element.71), channel_id=1, source_target_pairs={{4,0},{5,1},{6,2},{7,3},{8,12},{9,13},{10,14},{11,15},{20,16},{21,... | collective-permute-start | bytes 983048 | tf_op jit(solution)/shard_map/products_back_0/ppermute | solution.py:240
  46.9 4.4 %collective-permute-done.17.neighbour = bf16[12,32,256]{2,1,0:T(8,128)(2,1)S(1)} collective-permute-done((bf16[12,32,256]{2,1,0:T(8,128)(2,1)S(1)}, bf16[12,32,256]{2,1,0:T(8,128)(2,1)S(1)}, u32[]{:S(2)}, u32[]{:S(2)}) %collective-permute-start.17) | collective-permute-done | bytes 196640 | tf_op jit(solution)/shard_map/cross_left_1/ppermute | solution.py:240
  51.3 2.3 %collective-permute-done.18.rest_2_ = bf16[12,64,256]{2,1,0:T(8,128)(2,1)S(1)} collective-permute-done((bf16[12,64,256]{2,1,0:T(8,128)(2,1)S(1)}, bf16[12,64,256]{2,1,0:T(8,128)(2,1)S(1)}, u32[]{:S(2)}, u32[]{:S(2)}) %collective-permute-start.18) | collective-permute-done | bytes 393248 | tf_op jit(solution)/shard_map/end_right_1/ppermute | solution.py:240
  53.6 0.0 collective-permute-start.19
  53.6 0.0 collective-permute-done.20.rest_2_
  53.6 2.3 %collective-permute-start.21 = (bf16[12,64,256]{2,1,0:T(8,128)(2,1)S(1)}, bf16[12,64,256]{2,1,0:T(8,128)(2,1)S(1)}, u32[]{:S(2)}, u32[]{:S(2)}) collective-permute-start(bf16[12,64,256]{2,1,0:T(8,128)(2,1)S(1)} %collective-permute-done.18.rest_2_), channel_id=1, source_target_pairs={{0,1},{1,0},{2,3},{3,2},{4,8},{5,9},{6,10},{7,11},{8,4},{9,5},{10,... | collective-permute-start | bytes 1179656 | tf_op jit(solution)/shard_map/mid_next_1/ppermute | solution.py:240
  55.9 0.7 near.2
  56.6 3.7 %collective-permute-done.12.end = bf16[20,64,128]{2,1,0:T(8,128)(2,1)S(1)} collective-permute-done((bf16[20,64,128]{2,1,0:T(8,128)(2,1)S(1)}, bf16[20,64,128]{2,1,0:T(8,128)(2,1)S(1)}, u32[]{:S(2)}, u32[]{:S(2)}) %collective-permute-start.12) | collective-permute-done | bytes 327712 | tf_op jit(solution)/shard_map/products_back_0/ppermute | solution.py:240
  60.3 0.1 hand_out.2
  60.4 3.0 %collective-permute-start.13 = (bf16[20,32,128]{2,1,0:T(8,128)(2,1)S(1)}, bf16[20,32,128]{2,1,0:T(8,128)(2,1)S(1)}, u32[]{:S(2)}, u32[]{:S(2)}) collective-permute-start(bf16[20,32,128]{2,1,0:T(8,128)(2,1)S(1)} %get-tuple-element.73), channel_id=1, source_target_pairs={{0,1},{1,0},{2,3},{3,2},{4,5},{5,4},{6,7},{7,6},{8,9},{9,8},{10,11... | collective-permute-start | bytes 491528 | tf_op jit(solution)/shard_map/return_01/ppermute | solution.py:240
  63.4 1.0 %collective-permute-done.13.rest_1_ = bf16[20,32,128]{2,1,0:T(8,128)(2,1)S(1)} collective-permute-done((bf16[20,32,128]{2,1,0:T(8,128)(2,1)S(1)}, bf16[20,32,128]{2,1,0:T(8,128)(2,1)S(1)}, u32[]{:S(2)}, u32[]{:S(2)}) %collective-permute-start.13) | collective-permute-done | bytes 163872 | tf_op jit(solution)/shard_map/return_01/ppermute | solution.py:240
  64.4 4.4 %collective-permute-done.19.rest_1_ = bf16[12,64,256]{2,1,0:T(8,128)(2,1)S(1)} collective-permute-done((bf16[12,64,256]{2,1,0:T(8,128)(2,1)S(1)}, bf16[12,64,256]{2,1,0:T(8,128)(2,1)S(1)}, u32[]{:S(2)}, u32[]{:S(2)}) %collective-permute-start.19) | collective-permute-done | bytes 393248 | tf_op jit(solution)/shard_map/end_left_1/ppermute | solution.py:240
  68.7 0.4 away.3
  69.2 0.1 collective-permute-start.22
  69.3 0.3 collective-permute-start.14
  69.6 3.1 %collective-permute-start.15 = (bf16[20,32,128]{2,1,0:T(8,128)(2,1)S(1)}, bf16[20,32,128]{2,1,0:T(8,128)(2,1)S(1)}, u32[]{:S(2)}, u32[]{:S(2)}) collective-permute-start(bf16[20,32,128]{2,1,0:T(8,128)(2,1)S(1)} %get-tuple-element.75), channel_id=1, source_target_pairs={{0,3},{1,2},{2,1},{3,0},{4,7},{5,6},{6,5},{7,4},{8,11},{9,10},{10,... | collective-permute-start | bytes 491528 | tf_op jit(solution)/shard_map/return_03/ppermute | solution.py:240
  72.6 0.5 near.3
  73.1 0.0 copy-start.3
  73.1 0.0 copy-start.7
  73.1 0.7 collective-permute-done.22.end
  73.8 2.9 %collective-permute-start.23 = (bf16[12,32,128]{2,1,0:T(8,128)(2,1)S(1)}, bf16[12,32,128]{2,1,0:T(8,128)(2,1)S(1)}, u32[]{:S(2)}, u32[]{:S(2)}) collective-permute-start(bf16[12,32,128]{2,1,0:T(8,128)(2,1)S(1)} %get-tuple-element.90), channel_id=1, source_target_pairs={{0,1},{1,0},{2,3},{3,2},{4,5},{5,4},{6,7},{7,6},{8,9},{9,8},{10,11... | collective-permute-start | bytes 294920 | tf_op jit(solution)/shard_map/return_11/ppermute | solution.py:240
  76.7 0.2 collective-permute-start.24
  76.9 1.5 %collective-permute-start.25 = (bf16[12,32,128]{2,1,0:T(8,128)(2,1)S(1)}, bf16[12,32,128]{2,1,0:T(8,128)(2,1)S(1)}, u32[]{:S(2)}, u32[]{:S(2)}) collective-permute-start(bf16[12,32,128]{2,1,0:T(8,128)(2,1)S(1)} %get-tuple-element.92), channel_id=1, source_target_pairs={{0,3},{1,2},{2,1},{3,0},{4,7},{5,6},{6,5},{7,4},{8,11},{9,10},{10,... | collective-permute-start | bytes 294920 | tf_op jit(solution)/shard_map/return_13/ppermute | solution.py:240
  78.4 0.9 %gate.1 = f32[32,128,128]{2,1,0:T(8,128)S(1)} custom-call(bf16[4096,128]{1,0:T(8,128)(2,1)S(1)} %get-tuple-element.49.normed.normed0, bf16[128,128]{1,0:T(8,128)(2,1)S(1)} %copy-done.2), custom_call_target="tpu_custom_call" | custom-call | tf_op jit(solution)/shard_map/gate/pallas_call | solution.py:212
  79.3 1.7 %collective-permute-done.24.rest_6_ = bf16[12,32,128]{2,1,0:T(8,128)(2,1)S(1)} collective-permute-done((bf16[12,32,128]{2,1,0:T(8,128)(2,1)S(1)}, bf16[12,32,128]{2,1,0:T(8,128)(2,1)S(1)}, u32[]{:S(2)}, u32[]{:S(2)}) %collective-permute-start.24) | collective-permute-done | bytes 98336 | tf_op jit(solution)/shard_map/return_12/ppermute | solution.py:240
  81.1 2.3 %collective-permute-done.25.rest_7_ = bf16[12,32,128]{2,1,0:T(8,128)(2,1)S(1)} collective-permute-done((bf16[12,32,128]{2,1,0:T(8,128)(2,1)S(1)}, bf16[12,32,128]{2,1,0:T(8,128)(2,1)S(1)}, u32[]{:S(2)}, u32[]{:S(2)}) %collective-permute-start.25) | collective-permute-done | bytes 98336 | tf_op jit(solution)/shard_map/return_13/ppermute | solution.py:240
  83.3 2.5 %update.1 = bf16[32,128,128]{2,1,0:T(8,128)(2,1)} custom-call(f32[1,128]{1,0:T(1,128)S(1)} %bitcast.4, bf16[128,128]{1,0:T(8,128)(2,1)S(1)} %copy-done.3, f32[32,128,128]{2,1,0:T(8,128)S(1)} %gate.1, bf16[20,32,128]{2,1,0:T(8,128)(2,1)S(1)} %get-tuple-element.72.rest_0_, bf16[20,32,128]{2,1,0:T(8,128)(2,1)S(1)} %collective-permute-done.13.rest_1_, ...), custom_call_target="tpu_custom_call" | custom-call | tf_op jit(solution)/shard_map/update/pallas_call | solution.py:212
  (17 shorter events, 0.1 us)
Async XLA Ops:
  0.0 6.3 %collective-permute-start = (bf16[32,128,128]{2,1,0:T(8,128)(2,1)}, bf16[32,128,128]{2,1,0:T(8,128)(2,1)S(1)}, u32[]{:S(2)}, u32[]{:S(2)}) collective-permute-start(bf16[32,128,128]{2,1,0:T(8,128)(2,1)} %pair.1), channel_id=1, source_target_pairs={{0,1},{1,0},{2,3},{3,2},{4,5},{5,4},{6,7},{7,6},{8,9},{9,8},{10,11... | collective-permute-start | bytes 3145736 | tf_op jit(solution)/shard_map/pair/ppermute | solution.py:240
  0.1 6.3 %collective-permute-start.1 = (s32[32,128]{1,0:T(8,128)}, s32[32,128]{1,0:T(8,128)S(1)}, u32[]{:S(2)}, u32[]{:S(2)}) collective-permute-start(s32[32,128]{1,0:T(8,128)} %mask.1), channel_id=1, source_target_pairs={{0,1},{1,0},{2,3},{3,2},{4,5},{5,4},{6,7},{7,6},{8,9},{9,8},{10,11... | collective-permute-start | bytes 49160 | tf_op jit(solution)/shard_map/mask/ppermute | solution.py:240
  0.5 1.2 %copy-start = (bf16[32,128,128]{2,1,0:T(8,128)(2,1)S(1)}, bf16[32,128,128]{2,1,0:T(8,128)(2,1)}, u32[]{:S(2)}) copy-start(bf16[32,128,128]{2,1,0:T(8,128)(2,1)} %pair.1) | copy-start | bytes 3145732
  1.7 0.9 %copy-start.1 = (bf16[128,512]{1,0:T(8,128)(2,1)S(1)}, bf16[128,512]{1,0:T(8,128)(2,1)}, u32[]{:S(2)}) copy-start(bf16[128,512]{1,0:T(8,128)(2,1)} %weight.3) | copy-start | bytes 393220
  2.6 0.7 copy-start.4
  3.4 0.7 copy-start.5
  6.3 0.7 copy-start.6
  9.3 6.9 %collective-permute-start.3 = (bf16[20,32,256]{2,1,0:T(8,128)(2,1)S(1)}, bf16[20,32,256]{2,1,0:T(8,128)(2,1)S(1)}, u32[]{:S(2)}, u32[]{:S(2)}) collective-permute-start(bf16[20,32,256]{2,1,0:T(8,128)(2,1)S(1)} %get-tuple-element.61.rest_2_), channel_id=1, source_target_pairs={{0,1},{1,0},{2,3},{3,2},{4,8},{5,9},{6,10},{7,11},{8,4},{9,5},{10,... | collective-permute-start | bytes 983048 | tf_op jit(solution)/shard_map/mid_own_00/ppermute | solution.py:240
  9.4 10.8 %collective-permute-start.2 = (bf16[20,32,256]{2,1,0:T(8,128)(2,1)S(1)}, bf16[20,32,256]{2,1,0:T(8,128)(2,1)S(1)}, u32[]{:S(2)}, u32[]{:S(2)}) collective-permute-start(bf16[20,32,256]{2,1,0:T(8,128)(2,1)S(1)} %get-tuple-element.61.rest_2_), channel_id=1, source_target_pairs={{0,4},{1,5},{2,6},{3,7},{4,0},{5,1},{6,2},{7,3},{8,12},{9,13},{10,... | collective-permute-start | bytes 983048 | tf_op jit(solution)/shard_map/end_right_00/ppermute | solution.py:240
  13.0 8.1 %collective-permute-start.4 = (bf16[20,32,256]{2,1,0:T(8,128)(2,1)S(1)}, bf16[20,32,256]{2,1,0:T(8,128)(2,1)S(1)}, u32[]{:S(2)}, u32[]{:S(2)}) collective-permute-start(bf16[20,32,256]{2,1,0:T(8,128)(2,1)S(1)} %get-tuple-element.63), channel_id=1, source_target_pairs={{0,2},{1,3},{2,0},{3,1},{4,6},{5,7},{6,4},{7,5},{8,10},{9,11},{10,... | collective-permute-start | bytes 983048 | tf_op jit(solution)/shard_map/cross_right_0/ppermute | solution.py:240
  21.1 7.2 %collective-permute-start.5 = (bf16[20,32,256]{2,1,0:T(8,128)(2,1)S(1)}, bf16[20,32,256]{2,1,0:T(8,128)(2,1)S(1)}, u32[]{:S(2)}, u32[]{:S(2)}) collective-permute-start(bf16[20,32,256]{2,1,0:T(8,128)(2,1)S(1)} %get-tuple-element.64), channel_id=1, source_target_pairs={{0,2},{1,3},{2,0},{3,1},{4,6},{5,7},{6,4},{7,5},{8,10},{9,11},{10,... | collective-permute-start | bytes 983048 | tf_op jit(solution)/shard_map/cross_left_0/ppermute | solution.py:240
  22.3 7.2 %collective-permute-start.7 = (bf16[20,32,256]{2,1,0:T(8,128)(2,1)S(1)}, bf16[20,32,256]{2,1,0:T(8,128)(2,1)S(1)}, u32[]{:S(2)}, u32[]{:S(2)}) collective-permute-start(bf16[20,32,256]{2,1,0:T(8,128)(2,1)S(1)} %get-tuple-element.66.rest_0_), channel_id=1, source_target_pairs={{0,4},{1,5},{2,6},{3,7},{4,0},{5,1},{6,2},{7,3},{8,12},{9,13},{10,... | collective-permute-start | bytes 983048 | tf_op jit(solution)/shard_map/end_left_00/ppermute | solution.py:240
  22.7 13.6 %collective-permute-start.6 = (bf16[20,32,256]{2,1,0:T(8,128)(2,1)S(1)}, bf16[20,32,256]{2,1,0:T(8,128)(2,1)S(1)}, u32[]{:S(2)}, u32[]{:S(2)}) collective-permute-start(bf16[20,32,256]{2,1,0:T(8,128)(2,1)S(1)} %collective-permute-done.4.rest_3_), channel_id=1, source_target_pairs={{0,4},{1,5},{2,6},{3,7},{4,0},{5,1},{6,2},{7,3},{8,12},{9,13},{10,... | collective-permute-start | bytes 983048 | tf_op jit(solution)/shard_map/end_right_01/ppermute | solution.py:240
  23.8 12.5 %collective-permute-start.10 = (bf16[20,32,256]{2,1,0:T(8,128)(2,1)S(1)}, bf16[20,32,256]{2,1,0:T(8,128)(2,1)S(1)}, u32[]{:S(2)}, u32[]{:S(2)}) collective-permute-start(bf16[20,32,256]{2,1,0:T(8,128)(2,1)S(1)} %collective-permute-done.2.rest_4_), channel_id=1, source_target_pairs={{0,1},{1,0},{2,3},{3,2},{4,8},{5,9},{6,10},{7,11},{8,4},{9,5},{10,... | collective-permute-start | bytes 983048 | tf_op jit(solution)/shard_map/mid_next_00/ppermute | solution.py:240
  26.6 15.8 %collective-permute-start.9 = (bf16[20,32,256]{2,1,0:T(8,128)(2,1)S(1)}, bf16[20,32,256]{2,1,0:T(8,128)(2,1)S(1)}, u32[]{:S(2)}, u32[]{:S(2)}) collective-permute-start(bf16[20,32,256]{2,1,0:T(8,128)(2,1)S(1)} %collective-permute-done.4.rest_3_), channel_id=1, source_target_pairs={{0,1},{1,0},{2,3},{3,2},{4,8},{5,9},{6,10},{7,11},{8,4},{9,5},{10,... | collective-permute-start | bytes 983048 | tf_op jit(solution)/shard_map/mid_own_01/ppermute | solution.py:240
  28.3 14.0 %collective-permute-start.16 = (bf16[12,32,256]{2,1,0:T(8,128)(2,1)S(1)}, bf16[12,32,256]{2,1,0:T(8,128)(2,1)S(1)}, u32[]{:S(2)}, u32[]{:S(2)}) collective-permute-start(bf16[12,32,256]{2,1,0:T(8,128)(2,1)S(1)} %get-tuple-element.79), channel_id=1, source_target_pairs={{0,2},{1,3},{2,0},{3,1},{4,6},{5,7},{6,4},{7,5},{8,10},{9,11},{10,... | collective-permute-start | bytes 589832 | tf_op jit(solution)/shard_map/cross_right_1/ppermute | solution.py:240
  29.6 15.4 %collective-permute-start.8 = (bf16[20,32,256]{2,1,0:T(8,128)(2,1)S(1)}, bf16[20,32,256]{2,1,0:T(8,128)(2,1)S(1)}, u32[]{:S(2)}, u32[]{:S(2)}) collective-permute-start(bf16[20,32,256]{2,1,0:T(8,128)(2,1)S(1)} %collective-permute-done.5.rest_1_), channel_id=1, source_target_pairs={{0,4},{1,5},{2,6},{3,7},{4,0},{5,1},{6,2},{7,3},{8,12},{9,13},{10,... | collective-permute-start | bytes 983048 | tf_op jit(solution)/shard_map/end_left_01/ppermute | solution.py:240
  36.3 8.7 %collective-permute-start.11 = (bf16[20,32,256]{2,1,0:T(8,128)(2,1)S(1)}, bf16[20,32,256]{2,1,0:T(8,128)(2,1)S(1)}, u32[]{:S(2)}, u32[]{:S(2)}) collective-permute-start(bf16[20,32,256]{2,1,0:T(8,128)(2,1)S(1)} %collective-permute-done.6.rest_5_), channel_id=1, source_target_pairs={{0,1},{1,0},{2,3},{3,2},{4,8},{5,9},{6,10},{7,11},{8,4},{9,5},{10,... | collective-permute-start | bytes 983048 | tf_op jit(solution)/shard_map/mid_next_01/ppermute | solution.py:240
  42.3 11.3 %collective-permute-start.18 = (bf16[12,64,256]{2,1,0:T(8,128)(2,1)S(1)}, bf16[12,64,256]{2,1,0:T(8,128)(2,1)S(1)}, u32[]{:S(2)}, u32[]{:S(2)}) collective-permute-start(bf16[12,64,256]{2,1,0:T(8,128)(2,1)S(1)} %merge_right.1.rest_1_), channel_id=1, source_target_pairs={{0,4},{1,5},{2,6},{3,7},{4,0},{5,1},{6,2},{7,3},{8,12},{9,13},{10,... | collective-permute-start | bytes 1179656 | tf_op jit(solution)/shard_map/end_right_1/ppermute | solution.py:240
  42.4 11.2 %collective-permute-start.20 = (bf16[12,64,256]{2,1,0:T(8,128)(2,1)S(1)}, bf16[12,64,256]{2,1,0:T(8,128)(2,1)S(1)}, u32[]{:S(2)}, u32[]{:S(2)}) collective-permute-start(bf16[12,64,256]{2,1,0:T(8,128)(2,1)S(1)} %merge_right.1.rest_1_), channel_id=1, source_target_pairs={{0,1},{1,0},{2,3},{3,2},{4,8},{5,9},{6,10},{7,11},{8,4},{9,5},{10,... | collective-permute-start | bytes 1179656 | tf_op jit(solution)/shard_map/mid_own_1/ppermute | solution.py:240
  44.8 6.5 %collective-permute-start.17 = (bf16[12,32,256]{2,1,0:T(8,128)(2,1)S(1)}, bf16[12,32,256]{2,1,0:T(8,128)(2,1)S(1)}, u32[]{:S(2)}, u32[]{:S(2)}) collective-permute-start(bf16[12,32,256]{2,1,0:T(8,128)(2,1)S(1)} %get-tuple-element.80), channel_id=1, source_target_pairs={{0,2},{1,3},{2,0},{3,1},{4,6},{5,7},{6,4},{7,5},{8,10},{9,11},{10,... | collective-permute-start | bytes 589832 | tf_op jit(solution)/shard_map/cross_left_1/ppermute | solution.py:240
  45.6 14.7 %collective-permute-start.12 = (bf16[20,64,128]{2,1,0:T(8,128)(2,1)S(1)}, bf16[20,64,128]{2,1,0:T(8,128)(2,1)S(1)}, u32[]{:S(2)}, u32[]{:S(2)}) collective-permute-start(bf16[20,64,128]{2,1,0:T(8,128)(2,1)S(1)} %get-tuple-element.71), channel_id=1, source_target_pairs={{4,0},{5,1},{6,2},{7,3},{8,12},{9,13},{10,14},{11,15},{20,16},{21,... | collective-permute-start | bytes 983048 | tf_op jit(solution)/shard_map/products_back_0/ppermute | solution.py:240
  53.6 15.2 %collective-permute-start.19 = (bf16[12,64,256]{2,1,0:T(8,128)(2,1)S(1)}, bf16[12,64,256]{2,1,0:T(8,128)(2,1)S(1)}, u32[]{:S(2)}, u32[]{:S(2)}) collective-permute-start(bf16[12,64,256]{2,1,0:T(8,128)(2,1)S(1)} %merge_left.1.rest_0_), channel_id=1, source_target_pairs={{0,4},{1,5},{2,6},{3,7},{4,0},{5,1},{6,2},{7,3},{8,12},{9,13},{10,... | collective-permute-start | bytes 1179656 | tf_op jit(solution)/shard_map/end_left_1/ppermute | solution.py:240
  53.6 15.1 %collective-permute-start.21 = (bf16[12,64,256]{2,1,0:T(8,128)(2,1)S(1)}, bf16[12,64,256]{2,1,0:T(8,128)(2,1)S(1)}, u32[]{:S(2)}, u32[]{:S(2)}) collective-permute-start(bf16[12,64,256]{2,1,0:T(8,128)(2,1)S(1)} %collective-permute-done.18.rest_2_), channel_id=1, source_target_pairs={{0,1},{1,0},{2,3},{3,2},{4,8},{5,9},{6,10},{7,11},{8,4},{9,5},{10,... | collective-permute-start | bytes 1179656 | tf_op jit(solution)/shard_map/mid_next_1/ppermute | solution.py:240
  60.3 18.1 %copy-start.2 = (bf16[128,128]{1,0:T(8,128)(2,1)S(1)}, bf16[128,128]{1,0:T(8,128)(2,1)}, u32[]{:S(2)}) copy-start(bf16[128,128]{1,0:T(8,128)(2,1)} %weight.4) | copy-start | bytes 98308
  60.4 4.0 %collective-permute-start.13 = (bf16[20,32,128]{2,1,0:T(8,128)(2,1)S(1)}, bf16[20,32,128]{2,1,0:T(8,128)(2,1)S(1)}, u32[]{:S(2)}, u32[]{:S(2)}) collective-permute-start(bf16[20,32,128]{2,1,0:T(8,128)(2,1)S(1)} %get-tuple-element.73), channel_id=1, source_target_pairs={{0,1},{1,0},{2,3},{3,2},{4,5},{5,4},{6,7},{7,6},{8,9},{9,8},{10,11... | collective-permute-start | bytes 491528 | tf_op jit(solution)/shard_map/return_01/ppermute | solution.py:240
  69.2 4.6 %collective-permute-start.22 = (bf16[12,64,128]{2,1,0:T(8,128)(2,1)S(1)}, bf16[12,64,128]{2,1,0:T(8,128)(2,1)S(1)}, u32[]{:S(2)}, u32[]{:S(2)}) collective-permute-start(bf16[12,64,128]{2,1,0:T(8,128)(2,1)S(1)} %get-tuple-element.88), channel_id=1, source_target_pairs={{0,4},{1,5},{2,6},{3,7},{4,0},{5,1},{6,2},{7,3},{8,12},{9,13},{10,... | collective-permute-start | bytes 589832 | tf_op jit(solution)/shard_map/products_back_1/ppermute | solution.py:240
  69.3 10.0 %collective-permute-start.14 = (bf16[20,32,128]{2,1,0:T(8,128)(2,1)S(1)}, bf16[20,32,128]{2,1,0:T(8,128)(2,1)S(1)}, u32[]{:S(2)}, u32[]{:S(2)}) collective-permute-start(bf16[20,32,128]{2,1,0:T(8,128)(2,1)S(1)} %get-tuple-element.74), channel_id=1, source_target_pairs={{0,2},{1,3},{2,0},{3,1},{4,6},{5,7},{6,4},{7,5},{8,10},{9,11},{10,... | collective-permute-start | bytes 491528 | tf_op jit(solution)/shard_map/return_02/ppermute | solution.py:240
  69.6 9.8 %collective-permute-start.15 = (bf16[20,32,128]{2,1,0:T(8,128)(2,1)S(1)}, bf16[20,32,128]{2,1,0:T(8,128)(2,1)S(1)}, u32[]{:S(2)}, u32[]{:S(2)}) collective-permute-start(bf16[20,32,128]{2,1,0:T(8,128)(2,1)S(1)} %get-tuple-element.75), channel_id=1, source_target_pairs={{0,3},{1,2},{2,1},{3,0},{4,7},{5,6},{6,5},{7,4},{8,11},{9,10},{10,... | collective-permute-start | bytes 491528 | tf_op jit(solution)/shard_map/return_03/ppermute | solution.py:240
  73.1 10.3 %copy-start.3 = (bf16[128,128]{1,0:T(8,128)(2,1)S(1)}, bf16[128,128]{1,0:T(8,128)(2,1)}, u32[]{:S(2)}) copy-start(bf16[128,128]{1,0:T(8,128)(2,1)} %weight.5) | copy-start | bytes 98308
  73.1 10.2 %copy-start.7 = (f32[128]{0:T(128)S(1)}, f32[128]{0:T(128)}, u32[]{:S(2)}) copy-start(f32[128]{0:T(128)} %param.12) | copy-start | bytes 1540
  73.8 5.5 %collective-permute-start.23 = (bf16[12,32,128]{2,1,0:T(8,128)(2,1)S(1)}, bf16[12,32,128]{2,1,0:T(8,128)(2,1)S(1)}, u32[]{:S(2)}, u32[]{:S(2)}) collective-permute-start(bf16[12,32,128]{2,1,0:T(8,128)(2,1)S(1)} %get-tuple-element.90), channel_id=1, source_target_pairs={{0,1},{1,0},{2,3},{3,2},{4,5},{5,4},{6,7},{7,6},{8,9},{9,8},{10,11... | collective-permute-start | bytes 294920 | tf_op jit(solution)/shard_map/return_11/ppermute | solution.py:240
  76.7 4.4 %collective-permute-start.24 = (bf16[12,32,128]{2,1,0:T(8,128)(2,1)S(1)}, bf16[12,32,128]{2,1,0:T(8,128)(2,1)S(1)}, u32[]{:S(2)}, u32[]{:S(2)}) collective-permute-start(bf16[12,32,128]{2,1,0:T(8,128)(2,1)S(1)} %get-tuple-element.91), channel_id=1, source_target_pairs={{0,2},{1,3},{2,0},{3,1},{4,6},{5,7},{6,4},{7,5},{8,10},{9,11},{10,... | collective-permute-start | bytes 294920 | tf_op jit(solution)/shard_map/return_12/ppermute | solution.py:240
  76.9 6.4 %collective-permute-start.25 = (bf16[12,32,128]{2,1,0:T(8,128)(2,1)S(1)}, bf16[12,32,128]{2,1,0:T(8,128)(2,1)S(1)}, u32[]{:S(2)}, u32[]{:S(2)}) collective-permute-start(bf16[12,32,128]{2,1,0:T(8,128)(2,1)S(1)} %get-tuple-element.92), channel_id=1, source_target_pairs={{0,3},{1,2},{2,1},{3,0},{4,7},{5,6},{6,5},{7,4},{8,11},{9,10},{10,... | collective-permute-start | bytes 294920 | tf_op jit(solution)/shard_map/return_13/ppermute | solution.py:240

commit v8 on v7

--- a/solution.py
+++ b/solution.py
@@ -67,7 +67,8 @@
 
 
 def right_own_kernel(pair, mask, gain, weight, *rest):
-    *outs, normed_out, chosen_right, chosen_left, valid, turned, held = rest
+    *outs, normed_out, chosen_right, chosen_left, valid, gain_out, turned, held = rest
+    gain_out[...] = gain[...]
     hidden = weight.shape[1] // 4
     part = hidden // 4
     _, y, core = place()
@@ -268,11 +269,11 @@
     rows_all = jax.ShapeDtypeStruct((rows * toks, channels), BF16)
     weights = jax.ShapeDtypeStruct((4 * part, channels), BF16)
     valid_shape = jax.ShapeDtypeStruct((1, rows, toks), F32)
-    *mine, normed0, chosen_right, chosen_left, valid = kernel(
+    *mine, normed0, chosen_right, chosen_left, valid, gains = kernel(
         right_own_kernel,
         "right_own",
         [piece(count, rows, toks) for count in (*counts, *counts)]
-        + [rows_all, weights, weights, valid_shape],
+        + [rows_all, weights, weights, valid_shape, gains],
         [VMEM] * 4,
         [pltpu.VMEM((4 * hidden, channels), BF16), held],
     )(pair, pair_mask, gains, proj_weight)
@@ -285,50 +286,54 @@
         [held],
     )(twin, twin_mask, gains, chosen_right, *mine)
     right0, right1 = list(right[: len(counts)]), list(right[len(counts) :])
-    queues = {"y": [], "end": [], "mid": []}
-
-    def queued(link, name, x, target, window=2, also=()):
-        done = queues[link]
-        early = done[len(done) - window :][:1] if len(done) >= window else []
-        done.append(send(after(x, *early, *also), target, name))
-        return done[-1]
-
-    def hops(name, right, left):
-        far = [queued("mid", f"mid_own_{name}", right, mirrored)]
-        near = [right] + [
-            queued("end", f"end_right_{name}", right, shifted(s)) for s in range(1, half)
-        ]
-        return near, far, left
-
-    def last_hops(name, near, far, left):
-        far = far + [queued("mid", f"mid_next_{name}", x, mirrored) for x in near[1:]]
-        return near, far, left, queued("end", f"end_left_{name}", left, edge)
-
-    def cross(name, x):
-        return queued("y", f"cross_{name}", x, in_plane(2), 1)
+
+    def mid(name, x, *earlier):
+        return send(after(x, *earlier), mirrored, f"mid_{name}")
+
+    def end_right(name, x, *earlier):
+        x = after(x, *earlier)
+        return [send(x, shifted(s), f"end_right_{name}") for s in range(1, half)]
+
+    def end_left(name, x, *earlier):
+        return send(after(x, *earlier), edge, f"end_left_{name}")
+
+    def cross(name, x, *earlier):
+        return send(after(x, *earlier), in_plane(2), f"cross_{name}")
 
     def merge(own, neighbour, name):
         shape = piece(own.shape[0], 2 * rows, 2 * toks)
         return kernel(merge_kernel, name, shape, [VMEM, VMEM])(own, neighbour)
 
-    first0 = hops("00", right0[0], None)
-    right1[0] = cross("right_0", right1[0])
+    crossed = cross("right_0", right1[0])
+    own0 = mid("own_00", right0[0])
+    near0 = end_right("00", right0[0])
     left = kernel(left_kernel, "left", whole, [VMEM] * 5, [held])(
         normed0, normed1, valid, twin_valid, chosen_left
     )
     left0, left1 = list(left[: len(counts)]), list(left[len(counts) :])
-    first1 = hops("01", after(right1[0], left0[0]), None)
-    left1[0] = cross("left_0", after(left1[0], first0[0][-1], first0[1][0]))
-    begun = [[("00", *first0[:2], left0[0]), ("01", *first1[:2], left1[0])]]
-    moved = [[last_hops(*begun[0][0])]]
-    for g in groups[1:]:
-        right1[g] = cross(f"right_{g}", right1[g])
-        left1[g] = cross(f"left_{g}", left1[g])
-        right = merge(right0[g], right1[g], "merge_right")
-        left = merge(left0[g], left1[g], "merge_left")
-        begun.append([(f"{g}", *hops(f"{g}", right, left))])
-    moved[0].append(last_hops(*begun[0][1]))
-    moved += [[last_hops(*x) for x in begun[g]] for g in groups[1:]]
+    right1[0] = after(crossed, left0[0])
+    own1 = mid("own_01", right1[0])
+    near1 = end_right("01", right1[0])
+    left1[0] = cross("left_0", left1[0], crossed, own0)
+    next0 = [mid("next_00", x, own0) for x in near0]
+    outer0 = end_left("00", left0[0], near0[-1])
+    right1[1] = cross("right_1", right1[1], left1[0], own1)
+    next1 = [mid("next_01", x, own1) for x in near1]
+    outer1 = end_left("01", left1[0], near1[-1])
+    left1[1] = cross("left_1", left1[1], right1[1], next0[-1])
+    right = merge(right0[1], right1[1], "merge_right")
+    own2 = mid("own_1", right, own1)
+    near2 = end_right("1", right, near1[-1])
+    left = merge(left0[1], left1[1], "merge_left")
+    next2 = [mid("next_1", x, next1[-1]) for x in near2]
+    outer2 = end_left("1", left, outer1, own2)
+    moved = [
+        [
+            ([right0[0], *near0], [own0, *next0], left0[0], outer0),
+            ([right1[0], *near1], [own1, *next1], left1[0], outer1),
+        ],
+        [([right, *near2], [own2, *next2], left, outer2)],
+    ]
     gate = kernel(
         gate_kernel, "gate", jax.ShapeDtypeStruct((rows, toks, channels), F32), [VMEM] * 2
     )(normed0, gate_weight)
@@ -360,8 +365,10 @@
             [piece(counts[g], rows, toks)] * 4,
             [VMEM] * 3,
         )(close, away, ends)
-        got = [handed[0]] + [send(handed[r], in_plane(r), f"return_{g}{r}") for r in range(1, 4)]
-        done = got[:2]
+        got = [handed[0]] + [
+            send(handed[r], in_plane(r), f"return_{g}{r}") for r in range(1, 4)
+        ]
+        done = got
         pieces += got
 
     return kernel(

time: 86.3 us -> 91.9 us (1.065)
  waiting for transfers between devices: 33.1 us -> 41.4 us
  starting transfers between devices: 36 us -> 33.9 us
    ppermute x26, waiting for transfers between devices: 33.1 us -> 41.4 us  [send(): return lax.ppermute(x, ('row', 'chan'), pairs)]
    ppermute x26, starting transfers between devices: 36 us -> 33.9 us  [send(): return lax.ppermute(x, ('row', 'chan'), pairs)]
    unnamed x16 -> x14, local copies, waits for them, and re-layouts: 4.17 us -> 3.52 us
where the time goes in v8:
time: 91.9 us; the launch traced here: 91.4 us
  waiting for transfers between devices  41.4 us (45%)
  starting transfers between devices  33.9 us (37%)
  Pallas kernels  12.4 us (13%)
  local copies, waits for them, and re-layouts  3.52 us (4%)
    ppermute x26, waiting for transfers between devices, send(): return lax.ppermute(x, ('row', 'chan'), pairs)  41.4 us
    ppermute x26, starting transfers between devices, send(): return lax.ppermute(x, ('row', 'chan'), pairs)  33.9 us
    pallas_call x13, Pallas kernels, call(): pl.pallas_call(body, out_shape=out_shape, in_specs=in_specs, out_specs=ou...  12.4 us
    unnamed x14, local copies, waits for them, and re-layouts  3.52 us
  transfers between devices with their start and end apart: 26, of which 12 were waited for; matrix products, arithmetic and copies ran while one was open for 0% of the time, Pallas kernels for 8%

profile of v8, /device:TPU:1, one launch (start us, length us, event | category | flops | bytes accessed | tf_op | source)
XLA Modules:
  0.0 91.4 jit_solution(7986764301322268569)
XLA Ops:
  0.0 0.1 collective-permute-start
  0.1 0.5 collective-permute-start.1
  0.5 1.2 %copy-done = bf16[32,128,128]{2,1,0:T(8,128)(2,1)S(1)} copy-done((bf16[32,128,128]{2,1,0:T(8,128)(2,1)S(1)}, bf16[32,128,128]{2,1,0:T(8,128)(2,1)}, u32[]{:S(2)}) %copy-start) | copy-done | bytes 1048600
  1.7 0.9 copy-done.1
  2.6 0.7 copy-done.4
  3.4 0.7 copy-done.5
  4.0 2.3 %right_own.1 = (bf16[20,32,128]{2,1,0:T(8,128)(2,1)S(1)}, bf16[12,32,128]{2,1,0:T(8,128)(2,1)S(1)}, bf16[20,32,128]{2,1,0:T(8,128)(2,1)S(1)}, bf16[12,32,128]{2,...) custom-call(bf16[32,128,128]{2,1,0:T(8,128)(2,1)S(1)} %copy-done, ...), custom_call_target="tpu_custom_call" | custom-call | tf_op jit(solution)/shard_map/right_own/pallas_call | solution.py:213
  6.3 0.0 collective-permute-done.1.mask
  6.3 0.0 collective-permute-done.pair
  6.3 2.3 %right_twin.1 = (bf16[20,32,256]{2,1,0:T(8,128)(2,1)S(1)}, bf16[12,32,256]{2,1,0:T(8,128)(2,1)S(1)}, bf16[20,32,256]{2,1,0:T(8,128)(2,1)S(1)}, bf16[12,32,256]{2...) custom-call(bf16[32,128,128]{2,1,0:T(8,128)(2,1)S(1)} %collective-permute-done.pair, ...), custom_call_target="tpu_custom_call" | custom-call | tf_op jit(solution)/shard_map/right_twin/pallas_call | solution.py:213
  8.7 2.3 %collective-permute-start.2 = (bf16[20,32,256]{2,1,0:T(8,128)(2,1)S(1)}, bf16[20,32,256]{2,1,0:T(8,128)(2,1)S(1)}, u32[]{:S(2)}, u32[]{:S(2)}) collective-permute-start(bf16[20,32,256]{2,1,0:T(8,128)(2,1)S(1)} %get-tuple-element.62), channel_id=1, source_target_pairs={{0,2},{1,3},{2,0},{3,1},{4,6},{5,7},{6,4},{7,5},{8,10},{9,11},{10,... | collective-permute-start | bytes 983048 | tf_op jit(solution)/shard_map/cross_right_0/ppermute | solution.py:241
  11.0 0.8 collective-permute-start.3
  11.7 1.8 %collective-permute-start.5 = (bf16[20,32,256]{2,1,0:T(8,128)(2,1)S(1)}, bf16[20,32,256]{2,1,0:T(8,128)(2,1)S(1)}, u32[]{:S(2)}, u32[]{:S(2)}) collective-permute-start(bf16[20,32,256]{2,1,0:T(8,128)(2,1)S(1)} %get-tuple-element.63.rest_2_), channel_id=1, source_target_pairs={{0,4},{1,5},{2,6},{3,7},{4,0},{5,1},{6,2},{7,3},{8,12},{9,13},{10,... | collective-permute-start | bytes 983048 | tf_op jit(solution)/shard_map/end_right_00/ppermute | solution.py:241
  13.5 2.0 %left.1 = (bf16[20,32,256]{2,1,0:T(8,128)(2,1)S(1)}, bf16[12,32,256]{2,1,0:T(8,128)(2,1)S(1)}, bf16[20,32,256]{2,1,0:T(8,128)(2,1)S(1)}, bf16[12,32,256]{2,1,0:T(8,128)(2,1)S(1)}) custom-call(bf16[4096,128]{1,0:T(8,128)(2,1)S(1)} %get-tuple-element.49.normed.normed0, bf16[4096,128]{1,0:T(8,128)(2,1)S(1)} %get-tuple-element.56.normed1, ...), custom_call_target="tpu_custom_call" | custom-call | tf_op jit(solution)/shard_map/left/pallas_call | solution.py:213
  15.6 3.0 %collective-permute-done.2.rest_3_ = bf16[20,32,256]{2,1,0:T(8,128)(2,1)S(1)} collective-permute-done((bf16[20,32,256]{2,1,0:T(8,128)(2,1)S(1)}, bf16[20,32,256]{2,1,0:T(8,128)(2,1)S(1)}, u32[]{:S(2)}, u32[]{:S(2)}) %collective-permute-start.2) | collective-permute-done | bytes 327712 | tf_op jit(solution)/shard_map/cross_right_0/ppermute | solution.py:241
  18.6 1.0 %collective-permute-start.9 = (bf16[20,32,256]{2,1,0:T(8,128)(2,1)S(1)}, bf16[20,32,256]{2,1,0:T(8,128)(2,1)S(1)}, u32[]{:S(2)}, u32[]{:S(2)}) collective-permute-start(bf16[20,32,256]{2,1,0:T(8,128)(2,1)S(1)} %collective-permute-done.2.rest_3_), channel_id=1, source_target_pairs={{0,1},{1,0},{2,3},{3,2},{4,8},{5,9},{6,10},{7,11},{8,4},{9,5},{10,... | collective-permute-start | bytes 983048 | tf_op jit(solution)/shard_map/mid_own_01/ppermute | solution.py:241
  19.6 0.0 collective-permute-done.3.rest_4_
  19.6 1.5 %collective-permute-start.4 = (bf16[20,32,256]{2,1,0:T(8,128)(2,1)S(1)}, bf16[20,32,256]{2,1,0:T(8,128)(2,1)S(1)}, u32[]{:S(2)}, u32[]{:S(2)}) collective-permute-start(bf16[20,32,256]{2,1,0:T(8,128)(2,1)S(1)} %get-tuple-element.64), channel_id=1, source_target_pairs={{0,2},{1,3},{2,0},{3,1},{4,6},{5,7},{6,4},{7,5},{8,10},{9,11},{10,... | collective-permute-start | bytes 983048 | tf_op jit(solution)/shard_map/cross_left_0/ppermute | solution.py:241
  21.1 1.2 %collective-permute-start.6 = (bf16[20,32,256]{2,1,0:T(8,128)(2,1)S(1)}, bf16[20,32,256]{2,1,0:T(8,128)(2,1)S(1)}, u32[]{:S(2)}, u32[]{:S(2)}) collective-permute-start(bf16[20,32,256]{2,1,0:T(8,128)(2,1)S(1)} %collective-permute-done.2.rest_3_), channel_id=1, source_target_pairs={{0,4},{1,5},{2,6},{3,7},{4,0},{5,1},{6,2},{7,3},{8,12},{9,13},{10,... | collective-permute-start | bytes 983048 | tf_op jit(solution)/shard_map/end_right_01/ppermute | solution.py:241
  22.3 0.0 collective-permute-done.5.rest_4_
  22.3 2.2 %collective-permute-start.10 = (bf16[20,32,256]{2,1,0:T(8,128)(2,1)S(1)}, bf16[20,32,256]{2,1,0:T(8,128)(2,1)S(1)}, u32[]{:S(2)}, u32[]{:S(2)}) collective-permute-start(bf16[20,32,256]{2,1,0:T(8,128)(2,1)S(1)} %collective-permute-done.5.rest_4_), channel_id=1, source_target_pairs={{0,1},{1,0},{2,3},{3,2},{4,8},{5,9},{6,10},{7,11},{8,4},{9,5},{10,... | collective-permute-start | bytes 983048 | tf_op jit(solution)/shard_map/mid_next_00/ppermute | solution.py:241
  24.5 0.0 collective-permute-done.9.rest_5_
  24.5 4.4 %collective-permute-done.4.rest_1_ = bf16[20,32,256]{2,1,0:T(8,128)(2,1)S(1)} collective-permute-done((bf16[20,32,256]{2,1,0:T(8,128)(2,1)S(1)}, bf16[20,32,256]{2,1,0:T(8,128)(2,1)S(1)}, u32[]{:S(2)}, u32[]{:S(2)}) %collective-permute-start.4) | collective-permute-done | bytes 327712 | tf_op jit(solution)/shard_map/cross_left_0/ppermute | solution.py:241
  29.0 1.5 %collective-permute-start.16 = (bf16[12,32,256]{2,1,0:T(8,128)(2,1)S(1)}, bf16[12,32,256]{2,1,0:T(8,128)(2,1)S(1)}, u32[]{:S(2)}, u32[]{:S(2)}) collective-permute-start(bf16[12,32,256]{2,1,0:T(8,128)(2,1)S(1)} %get-tuple-element.79), channel_id=1, source_target_pairs={{0,2},{1,3},{2,0},{3,1},{4,6},{5,7},{6,4},{7,5},{8,10},{9,11},{10,... | collective-permute-start | bytes 589832 | tf_op jit(solution)/shard_map/cross_right_1/ppermute | solution.py:241
  30.4 0.0 collective-permute-start.7
  30.4 0.0 collective-permute-done.6.rest_5_
  30.4 3.2 %collective-permute-start.11 = (bf16[20,32,256]{2,1,0:T(8,128)(2,1)S(1)}, bf16[20,32,256]{2,1,0:T(8,128)(2,1)S(1)}, u32[]{:S(2)}, u32[]{:S(2)}) collective-permute-start(bf16[20,32,256]{2,1,0:T(8,128)(2,1)S(1)} %collective-permute-done.6.rest_5_), channel_id=1, source_target_pairs={{0,1},{1,0},{2,3},{3,2},{4,8},{5,9},{6,10},{7,11},{8,4},{9,5},{10,... | collective-permute-start | bytes 983048 | tf_op jit(solution)/shard_map/mid_next_01/ppermute | solution.py:241
  33.6 0.7 collective-permute-start.8
  34.3 0.3 collective-permute-done.16.neighbour
  34.6 0.5 collective-permute-start.18
  35.2 0.0 collective-permute-done.10.rest_6_
  35.2 2.7 %collective-permute-start.19 = (bf16[12,64,256]{2,1,0:T(8,128)(2,1)S(1)}, bf16[12,64,256]{2,1,0:T(8,128)(2,1)S(1)}, u32[]{:S(2)}, u32[]{:S(2)}) collective-permute-start(bf16[12,64,256]{2,1,0:T(8,128)(2,1)S(1)} %merge_right.1.rest_1_), channel_id=1, source_target_pairs={{0,1},{1,0},{2,3},{3,2},{4,8},{5,9},{6,10},{7,11},{8,4},{9,5},{10,... | collective-permute-start | bytes 1179656 | tf_op jit(solution)/shard_map/mid_own_1/ppermute | solution.py:241
  37.8 0.6 collective-permute-done.7.rest_2_
  38.5 0.6 collective-permute-start.17
  39.1 6.4 %collective-permute-done.8.rest_3_ = bf16[20,32,256]{2,1,0:T(8,128)(2,1)S(1)} collective-permute-done((bf16[20,32,256]{2,1,0:T(8,128)(2,1)S(1)}, bf16[20,32,256]{2,1,0:T(8,128)(2,1)S(1)}, u32[]{:S(2)}, u32[]{:S(2)}) %collective-permute-start.8) | collective-permute-done | bytes 327712 | tf_op jit(solution)/shard_map/end_left_01/ppermute | solution.py:241
  45.5 0.6 away.2
  46.1 1.3 %collective-permute-start.12 = (bf16[20,64,128]{2,1,0:T(8,128)(2,1)S(1)}, bf16[20,64,128]{2,1,0:T(8,128)(2,1)S(1)}, u32[]{:S(2)}, u32[]{:S(2)}) collective-permute-start(bf16[20,64,128]{2,1,0:T(8,128)(2,1)S(1)} %get-tuple-element.71), channel_id=1, source_target_pairs={{4,0},{5,1},{6,2},{7,3},{8,12},{9,13},{10,14},{11,15},{20,16},{21,... | collective-permute-start | bytes 983048 | tf_op jit(solution)/shard_map/products_back_0/ppermute | solution.py:241
  47.4 0.0 collective-permute-done.17.neighbour
  47.5 6.5 %collective-permute-done.18.rest_2_ = bf16[12,64,256]{2,1,0:T(8,128)(2,1)S(1)} collective-permute-done((bf16[12,64,256]{2,1,0:T(8,128)(2,1)S(1)}, bf16[12,64,256]{2,1,0:T(8,128)(2,1)S(1)}, u32[]{:S(2)}, u32[]{:S(2)}) %collective-permute-start.18) | collective-permute-done | bytes 393248 | tf_op jit(solution)/shard_map/end_right_1/ppermute | solution.py:241
  53.9 3.7 %collective-permute-start.21 = (bf16[12,64,256]{2,1,0:T(8,128)(2,1)S(1)}, bf16[12,64,256]{2,1,0:T(8,128)(2,1)S(1)}, u32[]{:S(2)}, u32[]{:S(2)}) collective-permute-start(bf16[12,64,256]{2,1,0:T(8,128)(2,1)S(1)} %collective-permute-done.18.rest_2_), channel_id=1, source_target_pairs={{0,1},{1,0},{2,3},{3,2},{4,8},{5,9},{6,10},{7,11},{8,4},{9,5},{10,... | collective-permute-start | bytes 1179656 | tf_op jit(solution)/shard_map/mid_next_1/ppermute | solution.py:241
  57.7 0.0 collective-permute-done.19.rest_2_
  57.7 0.0 collective-permute-start.20
  57.7 0.7 near.2
  58.4 2.6 %collective-permute-done.12.end = bf16[20,64,128]{2,1,0:T(8,128)(2,1)S(1)} collective-permute-done((bf16[20,64,128]{2,1,0:T(8,128)(2,1)S(1)}, bf16[20,64,128]{2,1,0:T(8,128)(2,1)S(1)}, u32[]{:S(2)}, u32[]{:S(2)}) %collective-permute-start.12) | collective-permute-done | bytes 327712 | tf_op jit(solution)/shard_map/products_back_0/ppermute | solution.py:241
  61.0 0.1 hand_out.2
  61.0 3.8 %collective-permute-start.13 = (bf16[20,32,128]{2,1,0:T(8,128)(2,1)S(1)}, bf16[20,32,128]{2,1,0:T(8,128)(2,1)S(1)}, u32[]{:S(2)}, u32[]{:S(2)}) collective-permute-start(bf16[20,32,128]{2,1,0:T(8,128)(2,1)S(1)} %get-tuple-element.73), channel_id=1, source_target_pairs={{0,1},{1,0},{2,3},{3,2},{4,5},{5,4},{6,7},{7,6},{8,9},{9,8},{10,11... | collective-permute-start | bytes 491528 | tf_op jit(solution)/shard_map/return_01/ppermute | solution.py:241
  64.8 0.2 collective-permute-start.14
  65.1 1.5 %collective-permute-start.15 = (bf16[20,32,128]{2,1,0:T(8,128)(2,1)S(1)}, bf16[20,32,128]{2,1,0:T(8,128)(2,1)S(1)}, u32[]{:S(2)}, u32[]{:S(2)}) collective-permute-start(bf16[20,32,128]{2,1,0:T(8,128)(2,1)S(1)} %get-tuple-element.75), channel_id=1, source_target_pairs={{0,3},{1,2},{2,1},{3,0},{4,7},{5,6},{6,5},{7,4},{8,11},{9,10},{10,... | collective-permute-start | bytes 491528 | tf_op jit(solution)/shard_map/return_03/ppermute | solution.py:241
  66.6 0.0 collective-permute-done.13.rest_1_
  66.6 4.1 %collective-permute-done.14.rest_2_ = bf16[20,32,128]{2,1,0:T(8,128)(2,1)S(1)} collective-permute-done((bf16[20,32,128]{2,1,0:T(8,128)(2,1)S(1)}, bf16[20,32,128]{2,1,0:T(8,128)(2,1)S(1)}, u32[]{:S(2)}, u32[]{:S(2)}) %collective-permute-start.14) | collective-permute-done | bytes 163872 | tf_op jit(solution)/shard_map/return_02/ppermute | solution.py:241
  70.6 3.7 %collective-permute-done.15.rest_3_ = bf16[20,32,128]{2,1,0:T(8,128)(2,1)S(1)} collective-permute-done((bf16[20,32,128]{2,1,0:T(8,128)(2,1)S(1)}, bf16[20,32,128]{2,1,0:T(8,128)(2,1)S(1)}, u32[]{:S(2)}, u32[]{:S(2)}) %collective-permute-start.15) | collective-permute-done | bytes 163872 | tf_op jit(solution)/shard_map/return_03/ppermute | solution.py:241
  74.3 0.4 away.3
  74.8 0.1 collective-permute-start.22
  74.8 0.5 near.3
  75.3 0.0 copy-start.3
  75.3 0.0 copy-start.6
  75.3 5.8 %collective-permute-done.22.end = bf16[12,64,128]{2,1,0:T(8,128)(2,1)S(1)} collective-permute-done((bf16[12,64,128]{2,1,0:T(8,128)(2,1)S(1)}, bf16[12,64,128]{2,1,0:T(8,128)(2,1)S(1)}, u32[]{:S(2)}, u32[]{:S(2)}) %collective-permute-start.22) | collective-permute-done | bytes 196640 | tf_op jit(solution)/shard_map/products_back_1/ppermute | solution.py:241
  81.1 1.1 %collective-permute-start.23 = (bf16[12,32,128]{2,1,0:T(8,128)(2,1)S(1)}, bf16[12,32,128]{2,1,0:T(8,128)(2,1)S(1)}, u32[]{:S(2)}, u32[]{:S(2)}) collective-permute-start(bf16[12,32,128]{2,1,0:T(8,128)(2,1)S(1)} %get-tuple-element.90), channel_id=1, source_target_pairs={{0,1},{1,0},{2,3},{3,2},{4,5},{5,4},{6,7},{7,6},{8,9},{9,8},{10,11... | collective-permute-start | bytes 294920 | tf_op jit(solution)/shard_map/return_11/ppermute | solution.py:241
  82.2 0.2 collective-permute-start.24
  82.5 1.5 %collective-permute-start.25 = (bf16[12,32,128]{2,1,0:T(8,128)(2,1)S(1)}, bf16[12,32,128]{2,1,0:T(8,128)(2,1)S(1)}, u32[]{:S(2)}, u32[]{:S(2)}) collective-permute-start(bf16[12,32,128]{2,1,0:T(8,128)(2,1)S(1)} %get-tuple-element.92), channel_id=1, source_target_pairs={{0,3},{1,2},{2,1},{3,0},{4,7},{5,6},{6,5},{7,4},{8,11},{9,10},{10,... | collective-permute-start | bytes 294920 | tf_op jit(solution)/shard_map/return_13/ppermute | solution.py:241
  84.0 0.9 gate.1
  84.9 1.8 %collective-permute-done.24.rest_6_ = bf16[12,32,128]{2,1,0:T(8,128)(2,1)S(1)} collective-permute-done((bf16[12,32,128]{2,1,0:T(8,128)(2,1)S(1)}, bf16[12,32,128]{2,1,0:T(8,128)(2,1)S(1)}, u32[]{:S(2)}, u32[]{:S(2)}) %collective-permute-start.24) | collective-permute-done | bytes 98336 | tf_op jit(solution)/shard_map/return_12/ppermute | solution.py:241
  86.6 2.3 %collective-permute-done.25.rest_7_ = bf16[12,32,128]{2,1,0:T(8,128)(2,1)S(1)} collective-permute-done((bf16[12,32,128]{2,1,0:T(8,128)(2,1)S(1)}, bf16[12,32,128]{2,1,0:T(8,128)(2,1)S(1)}, u32[]{:S(2)}, u32[]{:S(2)}) %collective-permute-start.25) | collective-permute-done | bytes 98336 | tf_op jit(solution)/shard_map/return_13/ppermute | solution.py:241
  88.9 2.5 %update.1 = bf16[32,128,128]{2,1,0:T(8,128)(2,1)} custom-call(f32[1,128]{1,0:T(1,128)S(1)} %bitcast.3, bf16[128,128]{1,0:T(8,128)(2,1)S(1)} %copy-done.3, f32[32,128,128]{2,1,0:T(8,128)S(1)} %gate.1, bf16[20,32,128]{2,1,0:T(8,128)(2,1)S(1)} %get-tuple-element.72.rest_0_, bf16[20,32,128]{2,1,0:T(8,128)(2,1)S(1)} %collective-permute-done.13.rest_1_, ...), custom_call_target="tpu_custom_call" | custom-call | tf_op jit(solution)/shard_map/update/pallas_call | solution.py:213
  (15 shorter events, 0.1 us)
Async XLA Ops:
  0.0 6.3 %collective-permute-start = (bf16[32,128,128]{2,1,0:T(8,128)(2,1)}, bf16[32,128,128]{2,1,0:T(8,128)(2,1)S(1)}, u32[]{:S(2)}, u32[]{:S(2)}) collective-permute-start(bf16[32,128,128]{2,1,0:T(8,128)(2,1)} %pair.1), channel_id=1, source_target_pairs={{0,1},{1,0},{2,3},{3,2},{4,5},{5,4},{6,7},{7,6},{8,9},{9,8},{10,11... | collective-permute-start | bytes 3145736 | tf_op jit(solution)/shard_map/pair/ppermute | solution.py:241
  0.1 6.3 %collective-permute-start.1 = (s32[32,128]{1,0:T(8,128)}, s32[32,128]{1,0:T(8,128)S(1)}, u32[]{:S(2)}, u32[]{:S(2)}) collective-permute-start(s32[32,128]{1,0:T(8,128)} %mask.1), channel_id=1, source_target_pairs={{0,1},{1,0},{2,3},{3,2},{4,5},{5,4},{6,7},{7,6},{8,9},{9,8},{10,11... | collective-permute-start | bytes 49160 | tf_op jit(solution)/shard_map/mask/ppermute | solution.py:241
  0.5 1.2 %copy-start = (bf16[32,128,128]{2,1,0:T(8,128)(2,1)S(1)}, bf16[32,128,128]{2,1,0:T(8,128)(2,1)}, u32[]{:S(2)}) copy-start(bf16[32,128,128]{2,1,0:T(8,128)(2,1)} %pair.1) | copy-start | bytes 3145732
  1.7 0.9 copy-start.1
  2.6 0.7 copy-start.4
  3.4 0.7 copy-start.5
  8.7 9.9 %collective-permute-start.2 = (bf16[20,32,256]{2,1,0:T(8,128)(2,1)S(1)}, bf16[20,32,256]{2,1,0:T(8,128)(2,1)S(1)}, u32[]{:S(2)}, u32[]{:S(2)}) collective-permute-start(bf16[20,32,256]{2,1,0:T(8,128)(2,1)S(1)} %get-tuple-element.62), channel_id=1, source_target_pairs={{0,2},{1,3},{2,0},{3,1},{4,6},{5,7},{6,4},{7,5},{8,10},{9,11},{10,... | collective-permute-start | bytes 983048 | tf_op jit(solution)/shard_map/cross_right_0/ppermute | solution.py:241
  11.0 8.7 %collective-permute-start.3 = (bf16[20,32,256]{2,1,0:T(8,128)(2,1)S(1)}, bf16[20,32,256]{2,1,0:T(8,128)(2,1)S(1)}, u32[]{:S(2)}, u32[]{:S(2)}) collective-permute-start(bf16[20,32,256]{2,1,0:T(8,128)(2,1)S(1)} %get-tuple-element.63.rest_2_), channel_id=1, source_target_pairs={{0,1},{1,0},{2,3},{3,2},{4,8},{5,9},{6,10},{7,11},{8,4},{9,5},{10,... | collective-permute-start | bytes 983048 | tf_op jit(solution)/shard_map/mid_own_00/ppermute | solution.py:241
  11.7 10.6 %collective-permute-start.5 = (bf16[20,32,256]{2,1,0:T(8,128)(2,1)S(1)}, bf16[20,32,256]{2,1,0:T(8,128)(2,1)S(1)}, u32[]{:S(2)}, u32[]{:S(2)}) collective-permute-start(bf16[20,32,256]{2,1,0:T(8,128)(2,1)S(1)} %get-tuple-element.63.rest_2_), channel_id=1, source_target_pairs={{0,4},{1,5},{2,6},{3,7},{4,0},{5,1},{6,2},{7,3},{8,12},{9,13},{10,... | collective-permute-start | bytes 983048 | tf_op jit(solution)/shard_map/end_right_00/ppermute | solution.py:241
  18.6 5.9 %collective-permute-start.9 = (bf16[20,32,256]{2,1,0:T(8,128)(2,1)S(1)}, bf16[20,32,256]{2,1,0:T(8,128)(2,1)S(1)}, u32[]{:S(2)}, u32[]{:S(2)}) collective-permute-start(bf16[20,32,256]{2,1,0:T(8,128)(2,1)S(1)} %collective-permute-done.2.rest_3_), channel_id=1, source_target_pairs={{0,1},{1,0},{2,3},{3,2},{4,8},{5,9},{6,10},{7,11},{8,4},{9,5},{10,... | collective-permute-start | bytes 983048 | tf_op jit(solution)/shard_map/mid_own_01/ppermute | solution.py:241
  19.6 9.3 %collective-permute-start.4 = (bf16[20,32,256]{2,1,0:T(8,128)(2,1)S(1)}, bf16[20,32,256]{2,1,0:T(8,128)(2,1)S(1)}, u32[]{:S(2)}, u32[]{:S(2)}) collective-permute-start(bf16[20,32,256]{2,1,0:T(8,128)(2,1)S(1)} %get-tuple-element.64), channel_id=1, source_target_pairs={{0,2},{1,3},{2,0},{3,1},{4,6},{5,7},{6,4},{7,5},{8,10},{9,11},{10,... | collective-permute-start | bytes 983048 | tf_op jit(solution)/shard_map/cross_left_0/ppermute | solution.py:241
  21.1 9.3 %collective-permute-start.6 = (bf16[20,32,256]{2,1,0:T(8,128)(2,1)S(1)}, bf16[20,32,256]{2,1,0:T(8,128)(2,1)S(1)}, u32[]{:S(2)}, u32[]{:S(2)}) collective-permute-start(bf16[20,32,256]{2,1,0:T(8,128)(2,1)S(1)} %collective-permute-done.2.rest_3_), channel_id=1, source_target_pairs={{0,4},{1,5},{2,6},{3,7},{4,0},{5,1},{6,2},{7,3},{8,12},{9,13},{10,... | collective-permute-start | bytes 983048 | tf_op jit(solution)/shard_map/end_right_01/ppermute | solution.py:241
  22.3 12.8 %collective-permute-start.10 = (bf16[20,32,256]{2,1,0:T(8,128)(2,1)S(1)}, bf16[20,32,256]{2,1,0:T(8,128)(2,1)S(1)}, u32[]{:S(2)}, u32[]{:S(2)}) collective-permute-start(bf16[20,32,256]{2,1,0:T(8,128)(2,1)S(1)} %collective-permute-done.5.rest_4_), channel_id=1, source_target_pairs={{0,1},{1,0},{2,3},{3,2},{4,8},{5,9},{6,10},{7,11},{8,4},{9,5},{10,... | collective-permute-start | bytes 983048 | tf_op jit(solution)/shard_map/mid_next_00/ppermute | solution.py:241
  29.0 5.6 %collective-permute-start.16 = (bf16[12,32,256]{2,1,0:T(8,128)(2,1)S(1)}, bf16[12,32,256]{2,1,0:T(8,128)(2,1)S(1)}, u32[]{:S(2)}, u32[]{:S(2)}) collective-permute-start(bf16[12,32,256]{2,1,0:T(8,128)(2,1)S(1)} %get-tuple-element.79), channel_id=1, source_target_pairs={{0,2},{1,3},{2,0},{3,1},{4,6},{5,7},{6,4},{7,5},{8,10},{9,11},{10,... | collective-permute-start | bytes 589832 | tf_op jit(solution)/shard_map/cross_right_1/ppermute | solution.py:241
  30.4 8.1 %collective-permute-start.7 = (bf16[20,32,256]{2,1,0:T(8,128)(2,1)S(1)}, bf16[20,32,256]{2,1,0:T(8,128)(2,1)S(1)}, u32[]{:S(2)}, u32[]{:S(2)}) collective-permute-start(bf16[20,32,256]{2,1,0:T(8,128)(2,1)S(1)} %get-tuple-element.66.rest_0_), channel_id=1, source_target_pairs={{0,4},{1,5},{2,6},{3,7},{4,0},{5,1},{6,2},{7,3},{8,12},{9,13},{10,... | collective-permute-start | bytes 983048 | tf_op jit(solution)/shard_map/end_left_00/ppermute | solution.py:241
  30.4 8.7 %collective-permute-start.11 = (bf16[20,32,256]{2,1,0:T(8,128)(2,1)S(1)}, bf16[20,32,256]{2,1,0:T(8,128)(2,1)S(1)}, u32[]{:S(2)}, u32[]{:S(2)}) collective-permute-start(bf16[20,32,256]{2,1,0:T(8,128)(2,1)S(1)} %collective-permute-done.6.rest_5_), channel_id=1, source_target_pairs={{0,1},{1,0},{2,3},{3,2},{4,8},{5,9},{6,10},{7,11},{8,4},{9,5},{10,... | collective-permute-start | bytes 983048 | tf_op jit(solution)/shard_map/mid_next_01/ppermute | solution.py:241
  33.6 11.9 %collective-permute-start.8 = (bf16[20,32,256]{2,1,0:T(8,128)(2,1)S(1)}, bf16[20,32,256]{2,1,0:T(8,128)(2,1)S(1)}, u32[]{:S(2)}, u32[]{:S(2)}) collective-permute-start(bf16[20,32,256]{2,1,0:T(8,128)(2,1)S(1)} %collective-permute-done.4.rest_1_), channel_id=1, source_target_pairs={{0,4},{1,5},{2,6},{3,7},{4,0},{5,1},{6,2},{7,3},{8,12},{9,13},{10,... | collective-permute-start | bytes 983048 | tf_op jit(solution)/shard_map/end_left_01/ppermute | solution.py:241
  34.6 19.3 %collective-permute-start.18 = (bf16[12,64,256]{2,1,0:T(8,128)(2,1)S(1)}, bf16[12,64,256]{2,1,0:T(8,128)(2,1)S(1)}, u32[]{:S(2)}, u32[]{:S(2)}) collective-permute-start(bf16[12,64,256]{2,1,0:T(8,128)(2,1)S(1)} %merge_right.1.rest_1_), channel_id=1, source_target_pairs={{0,4},{1,5},{2,6},{3,7},{4,0},{5,1},{6,2},{7,3},{8,12},{9,13},{10,... | collective-permute-start | bytes 1179656 | tf_op jit(solution)/shard_map/end_right_1/ppermute | solution.py:241
  35.2 22.5 %collective-permute-start.19 = (bf16[12,64,256]{2,1,0:T(8,128)(2,1)S(1)}, bf16[12,64,256]{2,1,0:T(8,128)(2,1)S(1)}, u32[]{:S(2)}, u32[]{:S(2)}) collective-permute-start(bf16[12,64,256]{2,1,0:T(8,128)(2,1)S(1)} %merge_right.1.rest_1_), channel_id=1, source_target_pairs={{0,1},{1,0},{2,3},{3,2},{4,8},{5,9},{6,10},{7,11},{8,4},{9,5},{10,... | collective-permute-start | bytes 1179656 | tf_op jit(solution)/shard_map/mid_own_1/ppermute | solution.py:241
  38.5 8.9 %collective-permute-start.17 = (bf16[12,32,256]{2,1,0:T(8,128)(2,1)S(1)}, bf16[12,32,256]{2,1,0:T(8,128)(2,1)S(1)}, u32[]{:S(2)}, u32[]{:S(2)}) collective-permute-start(bf16[12,32,256]{2,1,0:T(8,128)(2,1)S(1)} %get-tuple-element.80), channel_id=1, source_target_pairs={{0,2},{1,3},{2,0},{3,1},{4,6},{5,7},{6,4},{7,5},{8,10},{9,11},{10,... | collective-permute-start | bytes 589832 | tf_op jit(solution)/shard_map/cross_left_1/ppermute | solution.py:241
  46.1 14.8 %collective-permute-start.12 = (bf16[20,64,128]{2,1,0:T(8,128)(2,1)S(1)}, bf16[20,64,128]{2,1,0:T(8,128)(2,1)S(1)}, u32[]{:S(2)}, u32[]{:S(2)}) collective-permute-start(bf16[20,64,128]{2,1,0:T(8,128)(2,1)S(1)} %get-tuple-element.71), channel_id=1, source_target_pairs={{4,0},{5,1},{6,2},{7,3},{8,12},{9,13},{10,14},{11,15},{20,16},{21,... | collective-permute-start | bytes 983048 | tf_op jit(solution)/shard_map/products_back_0/ppermute | solution.py:241
  53.9 20.4 %collective-permute-start.21 = (bf16[12,64,256]{2,1,0:T(8,128)(2,1)S(1)}, bf16[12,64,256]{2,1,0:T(8,128)(2,1)S(1)}, u32[]{:S(2)}, u32[]{:S(2)}) collective-permute-start(bf16[12,64,256]{2,1,0:T(8,128)(2,1)S(1)} %collective-permute-done.18.rest_2_), channel_id=1, source_target_pairs={{0,1},{1,0},{2,3},{3,2},{4,8},{5,9},{6,10},{7,11},{8,4},{9,5},{10,... | collective-permute-start | bytes 1179656 | tf_op jit(solution)/shard_map/mid_next_1/ppermute | solution.py:241
  57.7 16.6 %collective-permute-start.20 = (bf16[12,64,256]{2,1,0:T(8,128)(2,1)S(1)}, bf16[12,64,256]{2,1,0:T(8,128)(2,1)S(1)}, u32[]{:S(2)}, u32[]{:S(2)}) collective-permute-start(bf16[12,64,256]{2,1,0:T(8,128)(2,1)S(1)} %merge_left.1.rest_0_), channel_id=1, source_target_pairs={{0,4},{1,5},{2,6},{3,7},{4,0},{5,1},{6,2},{7,3},{8,12},{9,13},{10,... | collective-permute-start | bytes 1179656 | tf_op jit(solution)/shard_map/end_left_1/ppermute | solution.py:241
  61.0 23.0 %copy-start.2 = (bf16[128,128]{1,0:T(8,128)(2,1)S(1)}, bf16[128,128]{1,0:T(8,128)(2,1)}, u32[]{:S(2)}) copy-start(bf16[128,128]{1,0:T(8,128)(2,1)} %weight.4) | copy-start | bytes 98308
  61.0 5.5 %collective-permute-start.13 = (bf16[20,32,128]{2,1,0:T(8,128)(2,1)S(1)}, bf16[20,32,128]{2,1,0:T(8,128)(2,1)S(1)}, u32[]{:S(2)}, u32[]{:S(2)}) collective-permute-start(bf16[20,32,128]{2,1,0:T(8,128)(2,1)S(1)} %get-tuple-element.73), channel_id=1, source_target_pairs={{0,1},{1,0},{2,3},{3,2},{4,5},{5,4},{6,7},{7,6},{8,9},{9,8},{10,11... | collective-permute-start | bytes 491528 | tf_op jit(solution)/shard_map/return_01/ppermute | solution.py:241
  64.8 5.8 %collective-permute-start.14 = (bf16[20,32,128]{2,1,0:T(8,128)(2,1)S(1)}, bf16[20,32,128]{2,1,0:T(8,128)(2,1)S(1)}, u32[]{:S(2)}, u32[]{:S(2)}) collective-permute-start(bf16[20,32,128]{2,1,0:T(8,128)(2,1)S(1)} %get-tuple-element.74), channel_id=1, source_target_pairs={{0,2},{1,3},{2,0},{3,1},{4,6},{5,7},{6,4},{7,5},{8,10},{9,11},{10,... | collective-permute-start | bytes 491528 | tf_op jit(solution)/shard_map/return_02/ppermute | solution.py:241
  65.1 9.2 %collective-permute-start.15 = (bf16[20,32,128]{2,1,0:T(8,128)(2,1)S(1)}, bf16[20,32,128]{2,1,0:T(8,128)(2,1)S(1)}, u32[]{:S(2)}, u32[]{:S(2)}) collective-permute-start(bf16[20,32,128]{2,1,0:T(8,128)(2,1)S(1)} %get-tuple-element.75), channel_id=1, source_target_pairs={{0,3},{1,2},{2,1},{3,0},{4,7},{5,6},{6,5},{7,4},{8,11},{9,10},{10,... | collective-permute-start | bytes 491528 | tf_op jit(solution)/shard_map/return_03/ppermute | solution.py:241
  74.8 6.3 %collective-permute-start.22 = (bf16[12,64,128]{2,1,0:T(8,128)(2,1)S(1)}, bf16[12,64,128]{2,1,0:T(8,128)(2,1)S(1)}, u32[]{:S(2)}, u32[]{:S(2)}) collective-permute-start(bf16[12,64,128]{2,1,0:T(8,128)(2,1)S(1)} %get-tuple-element.88), channel_id=1, source_target_pairs={{0,4},{1,5},{2,6},{3,7},{4,0},{5,1},{6,2},{7,3},{8,12},{9,13},{10,... | collective-permute-start | bytes 589832 | tf_op jit(solution)/shard_map/products_back_1/ppermute | solution.py:241
  75.3 13.6 %copy-start.3 = (bf16[128,128]{1,0:T(8,128)(2,1)S(1)}, bf16[128,128]{1,0:T(8,128)(2,1)}, u32[]{:S(2)}) copy-start(bf16[128,128]{1,0:T(8,128)(2,1)} %weight.5) | copy-start | bytes 98308
  75.3 13.6 %copy-start.6 = (f32[128]{0:T(128)S(1)}, f32[128]{0:T(128)}, u32[]{:S(2)}) copy-start(f32[128]{0:T(128)} %param.12) | copy-start | bytes 1540
  81.1 3.7 %collective-permute-start.23 = (bf16[12,32,128]{2,1,0:T(8,128)(2,1)S(1)}, bf16[12,32,128]{2,1,0:T(8,128)(2,1)S(1)}, u32[]{:S(2)}, u32[]{:S(2)}) collective-permute-start(bf16[12,32,128]{2,1,0:T(8,128)(2,1)S(1)} %get-tuple-element.90), channel_id=1, source_target_pairs={{0,1},{1,0},{2,3},{3,2},{4,5},{5,4},{6,7},{7,6},{8,9},{9,8},{10,11... | collective-permute-start | bytes 294920 | tf_op jit(solution)/shard_map/return_11/ppermute | solution.py:241
  82.2 4.4 %collective-permute-start.24 = (bf16[12,32,128]{2,1,0:T(8,128)(2,1)S(1)}, bf16[12,32,128]{2,1,0:T(8,128)(2,1)S(1)}, u32[]{:S(2)}, u32[]{:S(2)}) collective-permute-start(bf16[12,32,128]{2,1,0:T(8,128)(2,1)S(1)} %get-tuple-element.91), channel_id=1, source_target_pairs={{0,2},{1,3},{2,0},{3,1},{4,6},{5,7},{6,4},{7,5},{8,10},{9,11},{10,... | collective-permute-start | bytes 294920 | tf_op jit(solution)/shard_map/return_12/ppermute | solution.py:241
  82.5 6.4 %collective-permute-start.25 = (bf16[12,32,128]{2,1,0:T(8,128)(2,1)S(1)}, bf16[12,32,128]{2,1,0:T(8,128)(2,1)S(1)}, u32[]{:S(2)}, u32[]{:S(2)}) collective-permute-start(bf16[12,32,128]{2,1,0:T(8,128)(2,1)S(1)} %get-tuple-element.92), channel_id=1, source_target_pairs={{0,3},{1,2},{2,1},{3,0},{4,7},{5,6},{6,5},{7,4},{8,11},{9,10},{10,... | collective-permute-start | bytes 294920 | tf_op jit(solution)/shard_map/return_13/ppermute | solution.py:241

commit v9 on v8

--- a/solution.py
+++ b/solution.py
@@ -11,7 +11,7 @@
 F32, BF16 = jnp.float32, jnp.bfloat16
 LANES = 128
 SPARE = 6 * 1024 * 1024
-SHARES = (5, 3)
+SHARES = (4, 4)
 NT = (((1,), (1,)), ((), ()))
 TN = (((0,), (0,)), ((), ()))
 VMEM = pl.BlockSpec(memory_space=pltpu.VMEM)
@@ -118,36 +118,24 @@
         out[pl.ds(at * GROUP, GROUP)] = (0.5 * jnp.tanh(0.5 * logits) + 0.5).reshape(GROUP, toks, -1)
 
 
-def merge_kernel(own, neighbour, out):
-    rows = own.shape[1]
-    out[:, :rows, :] = own[...]
-    out[:, rows:, :] = neighbour[...]
-
-
-def product_kernel(mirror, lefts, rights, *rest):
-    count, span, width = rest[sum(lefts) + sum(rights)].shape
+def product_kernel(mirror, first, n_left, n_right, *rest):
+    *refs, held = rest
+    planes = [refs[2 * n : 2 * n + 2] for n in range(n_left + n_right)]
+    lefts, rights = planes[:n_left], planes[n_left:]
+    outs = refs[2 * (n_left + n_right) :]
+    count, span, _ = outs[0].shape
     rows = span // 2
-    refs = iter(rest)
-
-    def plane(arrays):
-        if arrays == 1:
-            both = next(refs)
-            return [both.at[:, :rows, :], both.at[:, rows:, :]]
-        return [next(refs), next(refs)]
-
-    lefts, rights = [plane(n) for n in lefts], [plane(n) for n in rights]
-    *outs, held = refs
-    half = len(rights)
     z, y, _ = place()
-    z = 2 * half - 1 - z if mirror else z
-    for s in range(half):
+    z = 2 * n_right - 1 - z if mirror else z
+    for s in range(n_right):
         for p in range(2):
-            start = pl.multiple_of((z + half - s) % half * span + (y ^ p) * rows, rows)
-            held[:, pl.ds(start, rows), :] = rights[s][p][...]
+            start = pl.multiple_of((z + n_right - s) % n_right * span + (y ^ p) * rows, rows)
+            at = 0 if p else first
+            held[:, pl.ds(start, rows), :] = rights[s][p][at : at + count]
     for c in range(count):
-        left = jnp.concatenate([x[c] for side in lefts for x in side], axis=0)
+        left = jnp.concatenate([x for own, other in lefts for x in (own[first + c], other[c])], axis=0)
         out = lax.dot_general(left, held[c], NT, preferred_element_type=F32).astype(BF16)
-        for n in range(len(lefts)):
+        for n in range(n_left):
             outs[n][c] = out[n * span : (n + 1) * span]
 
 
@@ -272,12 +260,12 @@
     *mine, normed0, chosen_right, chosen_left, valid, gains = kernel(
         right_own_kernel,
         "right_own",
-        [piece(count, rows, toks) for count in (*counts, *counts)]
+        [piece(count, rows, toks) for count in (part, *counts)]
         + [rows_all, weights, weights, valid_shape, gains],
         [VMEM] * 4,
         [pltpu.VMEM((4 * hidden, channels), BF16), held],
     )(pair, pair_mask, gains, proj_weight)
-    whole = [piece(count, rows, 2 * toks) for count in (*counts, *counts)]
+    whole = [piece(count, rows, 2 * toks) for count in (part, *counts)]
     *right, normed1, twin_valid = kernel(
         right_twin_kernel,
         "right_twin",
@@ -285,7 +273,7 @@
         [VMEM] * (4 + len(mine)),
         [held],
     )(twin, twin_mask, gains, chosen_right, *mine)
-    right0, right1 = list(right[: len(counts)]), list(right[len(counts) :])
+    right0, right1 = right[0], list(right[1:])
 
     def mid(name, x, *earlier):
         return send(after(x, *earlier), mirrored, f"mid_{name}")
@@ -300,64 +288,49 @@
     def cross(name, x, *earlier):
         return send(after(x, *earlier), in_plane(2), f"cross_{name}")
 
-    def merge(own, neighbour, name):
-        shape = piece(own.shape[0], 2 * rows, 2 * toks)
-        return kernel(merge_kernel, name, shape, [VMEM, VMEM])(own, neighbour)
-
+    own0 = mid("own_0", right0)
     crossed = cross("right_0", right1[0])
-    own0 = mid("own_00", right0[0])
-    near0 = end_right("00", right0[0])
+    near0 = end_right("0", right0)
     left = kernel(left_kernel, "left", whole, [VMEM] * 5, [held])(
         normed0, normed1, valid, twin_valid, chosen_left
     )
-    left0, left1 = list(left[: len(counts)]), list(left[len(counts) :])
-    right1[0] = after(crossed, left0[0])
-    own1 = mid("own_01", right1[0])
-    near1 = end_right("01", right1[0])
-    left1[0] = cross("left_0", left1[0], crossed, own0)
-    next0 = [mid("next_00", x, own0) for x in near0]
-    outer0 = end_left("00", left0[0], near0[-1])
-    right1[1] = cross("right_1", right1[1], left1[0], own1)
-    next1 = [mid("next_01", x, own1) for x in near1]
-    outer1 = end_left("01", left1[0], near1[-1])
-    left1[1] = cross("left_1", left1[1], right1[1], next0[-1])
-    right = merge(right0[1], right1[1], "merge_right")
-    own2 = mid("own_1", right, own1)
-    near2 = end_right("1", right, near1[-1])
-    left = merge(left0[1], left1[1], "merge_left")
-    next2 = [mid("next_1", x, next1[-1]) for x in near2]
-    outer2 = end_left("1", left, outer1, own2)
-    moved = [
-        [
-            ([right0[0], *near0], [own0, *next0], left0[0], outer0),
-            ([right1[0], *near1], [own1, *next1], left1[0], outer1),
-        ],
-        [([right, *near2], [own2, *next2], left, outer2)],
-    ]
+    left0, left1 = left[0], list(left[1:])
     gate = kernel(
         gate_kernel, "gate", jax.ShapeDtypeStruct((rows, toks, channels), F32), [VMEM] * 2
     )(normed0, gate_weight)
-
-    def products(mirror, lefts, rights, name):
+    right1[0] = after(crossed, left0)
+    right1[1] = cross("right_1", right1[1], right1[0])
+    own1 = [mid(f"own_1{g}", right1[g]) for g in groups]
+    near1 = [end_right(f"1{g}", right1[g]) for g in groups]
+    left1[0] = cross("left_0", left1[0], right1[1])
+    next0 = [mid("next_0", x, own0) for x in near0]
+    outer0 = end_left("0", left0, own0, crossed)
+    left1[1] = cross("left_1", left1[1], left1[0], own1[0])
+    next1 = [[mid("next_10", x, own1[0], gate) for x in near1[0]]]
+    outer1 = [end_left("10", left1[0], near1[0][-1])]
+    next1.append([mid("next_11", x, own1[1], next0[-1]) for x in near1[1]])
+    outer1.append(end_left("11", left1[1], near1[1][-1], outer0))
+
+    def products(mirror, first, lefts, rights, name):
         span = 2 * rows * len(rights)
-        count = lefts[0][0].shape[0]
+        count = lefts[0][1].shape[0]
         args = [x for arrays in (*lefts, *rights) for x in arrays]
         return kernel(
-            functools.partial(
-                product_kernel, mirror, [len(x) for x in lefts], [len(x) for x in rights]
-            ),
+            functools.partial(product_kernel, mirror, first, len(lefts), len(rights)),
             name,
             [piece(count, 2 * rows, span)] * len(lefts),
             [VMEM] * len(args),
             [pltpu.VMEM((count, span, 2 * toks), BF16)],
         )(*args)
 
-    done, pieces = [], []
+    done, pieces, first = [], [], 0
     for g in groups:
-        near, far, left, outer = zip(*moved[g])
-        (close,) = products(False, [left], list(zip(*near)), "near")
-        left = (after(left[0], *done), *left[1:])
-        away, ends = products(True, [left, outer], list(zip(*far)), "away")
+        mine = (left0, left1[g])
+        near = list(zip([right0, *near0], [right1[g], *near1[g]]))
+        far = list(zip([own0, *next0], [own1[g], *next1[g]]))
+        (close,) = products(False, first, [mine], near, "near")
+        mine = (after(left0, *done), left1[g])
+        away, ends = products(True, first, [mine, (outer0, outer1[g])], far, "away")
         ends = send(ends, edge if g == groups[-1] else outward, f"products_back_{g}")
         handed = kernel(
             functools.partial(hand_out_kernel, planes),
@@ -365,11 +338,11 @@
             [piece(counts[g], rows, toks)] * 4,
             [VMEM] * 3,
         )(close, away, ends)
-        got = [handed[0]] + [
+        done = [away]
+        pieces += [handed[0]] + [
             send(handed[r], in_plane(r), f"return_{g}{r}") for r in range(1, 4)
         ]
-        done = got
-        pieces += got
+        first += counts[g]
 
     return kernel(
         update_kernel,

time: 91.9 us -> 87.8 us (0.955)
  waiting for transfers between devices: 41.4 us -> 35.4 us
  starting transfers between devices: 33.9 us -> 35.8 us
    ppermute x26, waiting for transfers between devices: 41.4 us -> 35.4 us  [send(): return lax.ppermute(x, ('row', 'chan'), pairs)]
    ppermute x26, starting transfers between devices: 33.9 us -> 35.8 us  [send(): return lax.ppermute(x, ('row', 'chan'), pairs)]
    pallas_call x13 -> x11, Pallas kernels: 12.4 us -> 12.3 us  [call(): pl.pallas_call(body, out_shape=out_shape, in_specs=in_specs, out_specs=ou...]
  transfers between devices with their start and end apart: 26 -> 26, of which waited for: 12 -> 11; matrix products, arithmetic and copies ran while one was open for 0% -> 0% of each run, Pallas kernels for 8% -> 9%
where the time goes in v9:
time: 87.8 us; the launch traced here: 87.3 us
  starting transfers between devices  35.8 us (41%)
  waiting for transfers between devices  35.4 us (40%)
  Pallas kernels  12.3 us (14%)
  local copies, waits for them, and re-layouts  3.52 us (4%)
    ppermute x26, starting transfers between devices, send(): return lax.ppermute(x, ('row', 'chan'), pairs)  35.8 us
    ppermute x26, waiting for transfers between devices, send(): return lax.ppermute(x, ('row', 'chan'), pairs)  35.4 us
    pallas_call x11, Pallas kernels, call(): pl.pallas_call(body, out_shape=out_shape, in_specs=in_specs, out_specs=ou...  12.3 us
    unnamed x14, local copies, waits for them, and re-layouts  3.52 us
  transfers between devices with their start and end apart: 26, of which 11 were waited for; matrix products, arithmetic and copies ran while one was open for 0% of the time, Pallas kernels for 9%

profile of v9, /device:TPU:1, one launch (start us, length us, event | category | flops | bytes accessed | tf_op | source)
XLA Modules:
  0.0 87.3 jit_solution(7457548807581184254)
XLA Ops:
  0.0 0.1 collective-permute-start
  0.1 0.5 collective-permute-start.1
  0.5 1.2 %copy-done = bf16[32,128,128]{2,1,0:T(8,128)(2,1)S(1)} copy-done((bf16[32,128,128]{2,1,0:T(8,128)(2,1)S(1)}, bf16[32,128,128]{2,1,0:T(8,128)(2,1)}, u32[]{:S(2)}) %copy-start) | copy-done | bytes 1048600
  1.7 0.9 %copy-done.1 = bf16[128,512]{1,0:T(8,128)(2,1)S(1)} copy-done((bf16[128,512]{1,0:T(8,128)(2,1)S(1)}, bf16[128,512]{1,0:T(8,128)(2,1)}, u32[]{:S(2)}) %copy-start.1) | copy-done | bytes 131096
  2.6 0.7 copy-done.4
  3.4 0.7 copy-done.5
  4.0 2.3 %right_own.1 = (bf16[32,32,128]{2,1,0:T(8,128)(2,1)S(1)}, bf16[16,32,128]{2,1,0:T(8,128)(2,1)S(1)}, bf16[16,32,128]{2,1,0:T(8,128)(2,1)S(1)}, bf16[4096,128]{1,0...) custom-call(bf16[32,128,128]{2,1,0:T(8,128)(2,1)S(1)} %copy-done, ...), custom_call_target="tpu_custom_call" | custom-call | tf_op jit(solution)/shard_map/right_own/pallas_call | solution.py:201
  6.3 0.0 copy-start.2
  6.3 0.0 collective-permute-done.1.mask
  6.3 0.0 collective-permute-done.pair
  6.3 2.3 %right_twin.1 = (bf16[32,32,256]{2,1,0:T(8,128)(2,1)S(1)}, bf16[16,32,256]{2,1,0:T(8,128)(2,1)S(1)}, bf16[16,32,256]{2,1,0:T(8,128)(2,1)S(1)}, bf16[4096,128]{1,0:T(8,128)(2,1)S(1)}, f32[1,32,128]{2,1,0:T(8,128)S(1)}) custom-call(bf16[32,128,128]{2,1,0:T(8,128)(2,1)S(1)} %collective-permute-done.pair, s32[32,128]{1,0:T(8,128)S(1)} %collective-permute-done.1.mask, ...), custom_call_target="tpu_custom_call" | custom-call | tf_op jit(solution)/shard_map/right_twin/pallas_call | solution.py:201
  8.7 0.1 collective-permute-start.7
  8.8 2.7 %collective-permute-start.2 = (bf16[16,32,256]{2,1,0:T(8,128)(2,1)S(1)}, bf16[16,32,256]{2,1,0:T(8,128)(2,1)S(1)}, u32[]{:S(2)}, u32[]{:S(2)}) collective-permute-start(bf16[16,32,256]{2,1,0:T(8,128)(2,1)S(1)} %get-tuple-element.57), channel_id=1, source_target_pairs={{0,2},{1,3},{2,0},{3,1},{4,6},{5,7},{6,4},{7,5},{8,10},{9,11},{10,... | collective-permute-start | bytes 786440 | tf_op jit(solution)/shard_map/cross_right_0/ppermute | solution.py:229
  11.5 2.1 %collective-permute-start.5 = (bf16[32,32,256]{2,1,0:T(8,128)(2,1)S(1)}, bf16[32,32,256]{2,1,0:T(8,128)(2,1)S(1)}, u32[]{:S(2)}, u32[]{:S(2)}) collective-permute-start(bf16[32,32,256]{2,1,0:T(8,128)(2,1)S(1)} %get-tuple-element.61.rest_2_), channel_id=1, source_target_pairs={{0,4},{1,5},{2,6},{3,7},{4,0},{5,1},{6,2},{7,3},{8,12},{9,13},{10,... | collective-permute-start | bytes 1572872 | tf_op jit(solution)/shard_map/end_right_0/ppermute | solution.py:229
  13.6 2.0 %left.1 = (bf16[32,32,256]{2,1,0:T(8,128)(2,1)S(1)}, bf16[16,32,256]{2,1,0:T(8,128)(2,1)S(1)}, bf16[16,32,256]{2,1,0:T(8,128)(2,1)S(1)}) custom-call(bf16[4096,128]{1,0:T(8,128)(2,1)S(1)} %get-tuple-element.44.normed.normed0, bf16[4096,128]{1,0:T(8,128)(2,1)S(1)} %get-tuple-element.50.normed1, f32[1,32,128]{2,1,0:T(8,128)S(1)} %get-tuple-element.51.valid0, ...), custom_call_target="tpu_custom_call" | custom-call | tf_op jit(solution)/shard_map/left/pallas_call | solution.py:201
  15.6 2.5 %collective-permute-done.2.rest_3_ = bf16[16,32,256]{2,1,0:T(8,128)(2,1)S(1)} collective-permute-done((bf16[16,32,256]{2,1,0:T(8,128)(2,1)S(1)}, bf16[16,32,256]{2,1,0:T(8,128)(2,1)S(1)}, u32[]{:S(2)}, u32[]{:S(2)}) %collective-permute-start.2) | collective-permute-done | bytes 262176 | tf_op jit(solution)/shard_map/cross_right_0/ppermute | solution.py:229
  18.1 1.3 %collective-permute-start.3 = (bf16[16,32,256]{2,1,0:T(8,128)(2,1)S(1)}, bf16[16,32,256]{2,1,0:T(8,128)(2,1)S(1)}, u32[]{:S(2)}, u32[]{:S(2)}) collective-permute-start(bf16[16,32,256]{2,1,0:T(8,128)(2,1)S(1)} %get-tuple-element.59), channel_id=1, source_target_pairs={{0,2},{1,3},{2,0},{3,1},{4,6},{5,7},{6,4},{7,5},{8,10},{9,11},{10,... | collective-permute-start | bytes 786440 | tf_op jit(solution)/shard_map/cross_right_1/ppermute | solution.py:229
  19.4 1.1 %collective-permute-start.10 = (bf16[16,32,256]{2,1,0:T(8,128)(2,1)S(1)}, bf16[16,32,256]{2,1,0:T(8,128)(2,1)S(1)}, u32[]{:S(2)}, u32[]{:S(2)}) collective-permute-start(bf16[16,32,256]{2,1,0:T(8,128)(2,1)S(1)} %collective-permute-done.2.rest_3_), channel_id=1, source_target_pairs={{0,1},{1,0},{2,3},{3,2},{4,8},{5,9},{6,10},{7,11},{8,4},{9,5},{10,... | collective-permute-start | bytes 786440 | tf_op jit(solution)/shard_map/mid_own_10/ppermute | solution.py:229
  20.5 0.0 collective-permute-done.7.rest_4_
  20.5 3.5 %collective-permute-start.8 = (bf16[32,32,256]{2,1,0:T(8,128)(2,1)S(1)}, bf16[32,32,256]{2,1,0:T(8,128)(2,1)S(1)}, u32[]{:S(2)}, u32[]{:S(2)}) collective-permute-start(bf16[32,32,256]{2,1,0:T(8,128)(2,1)S(1)} %get-tuple-element.74.rest_0_), channel_id=1, source_target_pairs={{0,4},{1,5},{2,6},{3,7},{4,0},{5,1},{6,2},{7,3},{8,12},{9,13},{10,... | collective-permute-start | bytes 1572872 | tf_op jit(solution)/shard_map/end_left_0/ppermute | solution.py:229
  24.0 1.3 %collective-permute-done.3.rest_3_ = bf16[16,32,256]{2,1,0:T(8,128)(2,1)S(1)} collective-permute-done((bf16[16,32,256]{2,1,0:T(8,128)(2,1)S(1)}, bf16[16,32,256]{2,1,0:T(8,128)(2,1)S(1)}, u32[]{:S(2)}, u32[]{:S(2)}) %collective-permute-start.3) | collective-permute-done | bytes 262176 | tf_op jit(solution)/shard_map/cross_right_1/ppermute | solution.py:229
  25.3 1.1 %collective-permute-start.4 = (bf16[16,32,256]{2,1,0:T(8,128)(2,1)S(1)}, bf16[16,32,256]{2,1,0:T(8,128)(2,1)S(1)}, u32[]{:S(2)}, u32[]{:S(2)}) collective-permute-start(bf16[16,32,256]{2,1,0:T(8,128)(2,1)S(1)} %get-tuple-element.60), channel_id=1, source_target_pairs={{0,2},{1,3},{2,0},{3,1},{4,6},{5,7},{6,4},{7,5},{8,10},{9,11},{10,... | collective-permute-start | bytes 786440 | tf_op jit(solution)/shard_map/cross_left_0/ppermute | solution.py:229
  26.3 0.4 collective-permute-start.6
  26.7 3.2 %collective-permute-start.11 = (bf16[32,32,256]{2,1,0:T(8,128)(2,1)S(1)}, bf16[32,32,256]{2,1,0:T(8,128)(2,1)S(1)}, u32[]{:S(2)}, u32[]{:S(2)}) collective-permute-start(bf16[32,32,256]{2,1,0:T(8,128)(2,1)S(1)} %collective-permute-done.5.rest_4_), channel_id=1, source_target_pairs={{0,1},{1,0},{2,3},{3,2},{4,8},{5,9},{6,10},{7,11},{8,4},{9,5},{10,... | collective-permute-start | bytes 1572872 | tf_op jit(solution)/shard_map/mid_next_0/ppermute | solution.py:229
  29.9 0.0 collective-permute-done.10.rest_5_
  29.9 0.3 collective-permute-start.18
  30.2 1.3 %collective-permute-done.4.rest_1_ = bf16[16,32,256]{2,1,0:T(8,128)(2,1)S(1)} collective-permute-done((bf16[16,32,256]{2,1,0:T(8,128)(2,1)S(1)}, bf16[16,32,256]{2,1,0:T(8,128)(2,1)S(1)}, u32[]{:S(2)}, u32[]{:S(2)}) %collective-permute-start.4) | collective-permute-done | bytes 262176 | tf_op jit(solution)/shard_map/cross_left_0/ppermute | solution.py:229
  31.5 0.9 collective-permute-start.17
  32.4 8.7 %collective-permute-done.6.rest_5_ = bf16[16,32,256]{2,1,0:T(8,128)(2,1)S(1)} collective-permute-done((bf16[16,32,256]{2,1,0:T(8,128)(2,1)S(1)}, bf16[16,32,256]{2,1,0:T(8,128)(2,1)S(1)}, u32[]{:S(2)}, u32[]{:S(2)}) %collective-permute-start.6) | collective-permute-done | bytes 262176 | tf_op jit(solution)/shard_map/end_right_10/ppermute | solution.py:229
  41.1 3.9 %collective-permute-start.20 = (bf16[16,32,256]{2,1,0:T(8,128)(2,1)S(1)}, bf16[16,32,256]{2,1,0:T(8,128)(2,1)S(1)}, u32[]{:S(2)}, u32[]{:S(2)}) collective-permute-start(bf16[16,32,256]{2,1,0:T(8,128)(2,1)S(1)} %collective-permute-done.3.rest_3_), channel_id=1, source_target_pairs={{0,1},{1,0},{2,3},{3,2},{4,8},{5,9},{6,10},{7,11},{8,4},{9,5},{10,... | collective-permute-start | bytes 786440 | tf_op jit(solution)/shard_map/mid_own_11/ppermute | solution.py:229
  45.1 0.9 %gate.1 = f32[32,128,128]{2,1,0:T(8,128)S(1)} custom-call(bf16[4096,128]{1,0:T(8,128)(2,1)S(1)} %get-tuple-element.44.normed.normed0, bf16[128,128]{1,0:T(8,128)(2,1)S(1)} %copy-done.2), custom_call_target="tpu_custom_call" | custom-call | tf_op jit(solution)/shard_map/gate/pallas_call | solution.py:201
  46.0 0.8 collective-permute-done.18.rest_5_
  46.7 2.2 %collective-permute-start.12 = (bf16[16,32,256]{2,1,0:T(8,128)(2,1)S(1)}, bf16[16,32,256]{2,1,0:T(8,128)(2,1)S(1)}, u32[]{:S(2)}, u32[]{:S(2)}) collective-permute-start(bf16[16,32,256]{2,1,0:T(8,128)(2,1)S(1)} %collective-permute-done.6.rest_5_), channel_id=1, source_target_pairs={{0,1},{1,0},{2,3},{3,2},{4,8},{5,9},{6,10},{7,11},{8,4},{9,5},{10,... | collective-permute-start | bytes 786440 | tf_op jit(solution)/shard_map/mid_next_10/ppermute | solution.py:229
  48.9 1.5 %collective-permute-start.19 = (bf16[16,32,256]{2,1,0:T(8,128)(2,1)S(1)}, bf16[16,32,256]{2,1,0:T(8,128)(2,1)S(1)}, u32[]{:S(2)}, u32[]{:S(2)}) collective-permute-start(bf16[16,32,256]{2,1,0:T(8,128)(2,1)S(1)} %collective-permute-done.17.rest_1_), channel_id=1, source_target_pairs={{0,4},{1,5},{2,6},{3,7},{4,0},{5,1},{6,2},{7,3},{8,12},{9,13},{10,... | collective-permute-start | bytes 786440 | tf_op jit(solution)/shard_map/end_left_11/ppermute | solution.py:229
  50.4 0.0 collective-permute-done.20.rest_5_
  50.4 0.0 collective-permute-done.11.rest_6_
  50.4 1.2 %collective-permute-start.21 = (bf16[16,32,256]{2,1,0:T(8,128)(2,1)S(1)}, bf16[16,32,256]{2,1,0:T(8,128)(2,1)S(1)}, u32[]{:S(2)}, u32[]{:S(2)}) collective-permute-start(bf16[16,32,256]{2,1,0:T(8,128)(2,1)S(1)} %collective-permute-done.18.rest_5_), channel_id=1, source_target_pairs={{0,1},{1,0},{2,3},{3,2},{4,8},{5,9},{6,10},{7,11},{8,4},{9,5},{10,... | collective-permute-start | bytes 786440 | tf_op jit(solution)/shard_map/mid_next_11/ppermute | solution.py:229
  51.5 4.7 %collective-permute-done.9.rest_3_ = bf16[16,32,256]{2,1,0:T(8,128)(2,1)S(1)} collective-permute-done((bf16[16,32,256]{2,1,0:T(8,128)(2,1)S(1)}, bf16[16,32,256]{2,1,0:T(8,128)(2,1)S(1)}, u32[]{:S(2)}, u32[]{:S(2)}) %collective-permute-start.9) | collective-permute-done | bytes 262176 | tf_op jit(solution)/shard_map/end_left_10/ppermute | solution.py:229
  56.3 0.5 away.2
  56.8 1.3 %collective-permute-start.13 = (bf16[16,64,128]{2,1,0:T(8,128)(2,1)S(1)}, bf16[16,64,128]{2,1,0:T(8,128)(2,1)S(1)}, u32[]{:S(2)}, u32[]{:S(2)}) collective-permute-start(bf16[16,64,128]{2,1,0:T(8,128)(2,1)S(1)} %get-tuple-element.67), channel_id=1, source_target_pairs={{4,0},{5,1},{6,2},{7,3},{8,12},{9,13},{10,14},{11,15},{20,16},{21,... | collective-permute-start | bytes 786440 | tf_op jit(solution)/shard_map/products_back_0/ppermute | solution.py:229
  58.1 3.8 %collective-permute-done.19.rest_3_ = bf16[16,32,256]{2,1,0:T(8,128)(2,1)S(1)} collective-permute-done((bf16[16,32,256]{2,1,0:T(8,128)(2,1)S(1)}, bf16[16,32,256]{2,1,0:T(8,128)(2,1)S(1)}, u32[]{:S(2)}, u32[]{:S(2)}) %collective-permute-start.19) | collective-permute-done | bytes 262176 | tf_op jit(solution)/shard_map/end_left_11/ppermute | solution.py:229
  61.9 0.0 collective-permute-done.21.rest_7_
  61.9 0.5 away.3
  62.4 0.1 collective-permute-start.22
  62.5 0.6 near.2
  63.1 0.0 copy-start.3
  63.1 0.0 copy-start.6
  63.1 3.9 %collective-permute-done.13.end = bf16[16,64,128]{2,1,0:T(8,128)(2,1)S(1)} collective-permute-done((bf16[16,64,128]{2,1,0:T(8,128)(2,1)S(1)}, bf16[16,64,128]{2,1,0:T(8,128)(2,1)S(1)}, u32[]{:S(2)}, u32[]{:S(2)}) %collective-permute-start.13) | collective-permute-done | bytes 262176 | tf_op jit(solution)/shard_map/products_back_0/ppermute | solution.py:229
  67.0 0.1 hand_out.2
  67.1 3.3 %collective-permute-start.14 = (bf16[16,32,128]{2,1,0:T(8,128)(2,1)S(1)}, bf16[16,32,128]{2,1,0:T(8,128)(2,1)S(1)}, u32[]{:S(2)}, u32[]{:S(2)}) collective-permute-start(bf16[16,32,128]{2,1,0:T(8,128)(2,1)S(1)} %get-tuple-element.69), channel_id=1, source_target_pairs={{0,1},{1,0},{2,3},{3,2},{4,5},{5,4},{6,7},{7,6},{8,9},{9,8},{10,11... | collective-permute-start | bytes 393224 | tf_op jit(solution)/shard_map/return_01/ppermute | solution.py:229
  70.4 0.6 near.3
  71.0 1.4 %collective-permute-start.15 = (bf16[16,32,128]{2,1,0:T(8,128)(2,1)S(1)}, bf16[16,32,128]{2,1,0:T(8,128)(2,1)S(1)}, u32[]{:S(2)}, u32[]{:S(2)}) collective-permute-start(bf16[16,32,128]{2,1,0:T(8,128)(2,1)S(1)} %get-tuple-element.70), channel_id=1, source_target_pairs={{0,2},{1,3},{2,0},{3,1},{4,6},{5,7},{6,4},{7,5},{8,10},{9,11},{10,... | collective-permute-start | bytes 393224 | tf_op jit(solution)/shard_map/return_02/ppermute | solution.py:229
  72.4 0.4 collective-permute-start.16
  72.7 0.0 collective-permute-done.22.end
  72.7 0.1 hand_out.3
  72.8 1.8 %collective-permute-start.23 = (bf16[16,32,128]{2,1,0:T(8,128)(2,1)S(1)}, bf16[16,32,128]{2,1,0:T(8,128)(2,1)S(1)}, u32[]{:S(2)}, u32[]{:S(2)}) collective-permute-start(bf16[16,32,128]{2,1,0:T(8,128)(2,1)S(1)} %get-tuple-element.80), channel_id=1, source_target_pairs={{0,1},{1,0},{2,3},{3,2},{4,5},{5,4},{6,7},{7,6},{8,9},{9,8},{10,11... | collective-permute-start | bytes 393224 | tf_op jit(solution)/shard_map/return_11/ppermute | solution.py:229
  74.6 0.5 collective-permute-start.24
  75.1 0.0 collective-permute-done.14.rest_1_
  75.1 1.2 %collective-permute-start.25 = (bf16[16,32,128]{2,1,0:T(8,128)(2,1)S(1)}, bf16[16,32,128]{2,1,0:T(8,128)(2,1)S(1)}, u32[]{:S(2)}, u32[]{:S(2)}) collective-permute-start(bf16[16,32,128]{2,1,0:T(8,128)(2,1)S(1)} %get-tuple-element.82), channel_id=1, source_target_pairs={{0,3},{1,2},{2,1},{3,0},{4,7},{5,6},{6,5},{7,4},{8,11},{9,10},{10,... | collective-permute-start | bytes 393224 | tf_op jit(solution)/shard_map/return_13/ppermute | solution.py:229
  76.3 0.0 collective-permute-done.15.rest_2_
  76.3 3.2 %collective-permute-done.16.rest_3_ = bf16[16,32,128]{2,1,0:T(8,128)(2,1)S(1)} collective-permute-done((bf16[16,32,128]{2,1,0:T(8,128)(2,1)S(1)}, bf16[16,32,128]{2,1,0:T(8,128)(2,1)S(1)}, u32[]{:S(2)}, u32[]{:S(2)}) %collective-permute-start.16) | collective-permute-done | bytes 131104 | tf_op jit(solution)/shard_map/return_03/ppermute | solution.py:229
  79.5 2.3 %collective-permute-done.24.rest_6_ = bf16[16,32,128]{2,1,0:T(8,128)(2,1)S(1)} collective-permute-done((bf16[16,32,128]{2,1,0:T(8,128)(2,1)S(1)}, bf16[16,32,128]{2,1,0:T(8,128)(2,1)S(1)}, u32[]{:S(2)}, u32[]{:S(2)}) %collective-permute-start.24) | collective-permute-done | bytes 131104 | tf_op jit(solution)/shard_map/return_12/ppermute | solution.py:229
  81.8 2.9 %collective-permute-done.25.rest_7_ = bf16[16,32,128]{2,1,0:T(8,128)(2,1)S(1)} collective-permute-done((bf16[16,32,128]{2,1,0:T(8,128)(2,1)S(1)}, bf16[16,32,128]{2,1,0:T(8,128)(2,1)S(1)}, u32[]{:S(2)}, u32[]{:S(2)}) %collective-permute-start.25) | collective-permute-done | bytes 131104 | tf_op jit(solution)/shard_map/return_13/ppermute | solution.py:229
  84.7 2.5 %update.1 = bf16[32,128,128]{2,1,0:T(8,128)(2,1)} custom-call(f32[1,128]{1,0:T(1,128)S(1)} %bitcast.3, bf16[128,128]{1,0:T(8,128)(2,1)S(1)} %copy-done.3, f32[32,128,128]{2,1,0:T(8,128)S(1)} %gate.1, bf16[16,32,128]{2,1,0:T(8,128)(2,1)S(1)} %get-tuple-element.68.rest_0_, bf16[16,32,128]{2,1,0:T(8,128)(2,1)S(1)} %collective-permute-done.14.rest_1_, ...), custom_call_target="tpu_custom_call" | custom-call | tf_op jit(solution)/shard_map/update/pallas_call | solution.py:201
  (13 shorter events, 0.0 us)
Async XLA Ops:
  0.0 6.3 %collective-permute-start = (bf16[32,128,128]{2,1,0:T(8,128)(2,1)}, bf16[32,128,128]{2,1,0:T(8,128)(2,1)S(1)}, u32[]{:S(2)}, u32[]{:S(2)}) collective-permute-start(bf16[32,128,128]{2,1,0:T(8,128)(2,1)} %pair.1), channel_id=1, source_target_pairs={{0,1},{1,0},{2,3},{3,2},{4,5},{5,4},{6,7},{7,6},{8,9},{9,8},{10,11... | collective-permute-start | bytes 3145736 | tf_op jit(solution)/shard_map/pair/ppermute | solution.py:229
  0.1 6.3 %collective-permute-start.1 = (s32[32,128]{1,0:T(8,128)}, s32[32,128]{1,0:T(8,128)S(1)}, u32[]{:S(2)}, u32[]{:S(2)}) collective-permute-start(s32[32,128]{1,0:T(8,128)} %mask.1), channel_id=1, source_target_pairs={{0,1},{1,0},{2,3},{3,2},{4,5},{5,4},{6,7},{7,6},{8,9},{9,8},{10,11... | collective-permute-start | bytes 49160 | tf_op jit(solution)/shard_map/mask/ppermute | solution.py:229
  0.5 1.2 %copy-start = (bf16[32,128,128]{2,1,0:T(8,128)(2,1)S(1)}, bf16[32,128,128]{2,1,0:T(8,128)(2,1)}, u32[]{:S(2)}) copy-start(bf16[32,128,128]{2,1,0:T(8,128)(2,1)} %pair.1) | copy-start | bytes 3145732
  1.7 0.9 %copy-start.1 = (bf16[128,512]{1,0:T(8,128)(2,1)S(1)}, bf16[128,512]{1,0:T(8,128)(2,1)}, u32[]{:S(2)}) copy-start(bf16[128,512]{1,0:T(8,128)(2,1)} %weight.3) | copy-start | bytes 393220
  2.6 0.7 copy-start.4
  3.4 0.7 copy-start.5
  6.3 38.7 %copy-start.2 = (bf16[128,128]{1,0:T(8,128)(2,1)S(1)}, bf16[128,128]{1,0:T(8,128)(2,1)}, u32[]{:S(2)}) copy-start(bf16[128,128]{1,0:T(8,128)(2,1)} %weight.4) | copy-start | bytes 98308
  8.7 11.8 %collective-permute-start.7 = (bf16[32,32,256]{2,1,0:T(8,128)(2,1)S(1)}, bf16[32,32,256]{2,1,0:T(8,128)(2,1)S(1)}, u32[]{:S(2)}, u32[]{:S(2)}) collective-permute-start(bf16[32,32,256]{2,1,0:T(8,128)(2,1)S(1)} %get-tuple-element.61.rest_2_), channel_id=1, source_target_pairs={{0,1},{1,0},{2,3},{3,2},{4,8},{5,9},{6,10},{7,11},{8,4},{9,5},{10,... | collective-permute-start | bytes 1572872 | tf_op jit(solution)/shard_map/mid_own_0/ppermute | solution.py:229
  8.8 9.3 %collective-permute-start.2 = (bf16[16,32,256]{2,1,0:T(8,128)(2,1)S(1)}, bf16[16,32,256]{2,1,0:T(8,128)(2,1)S(1)}, u32[]{:S(2)}, u32[]{:S(2)}) collective-permute-start(bf16[16,32,256]{2,1,0:T(8,128)(2,1)S(1)} %get-tuple-element.57), channel_id=1, source_target_pairs={{0,2},{1,3},{2,0},{3,1},{4,6},{5,7},{6,4},{7,5},{8,10},{9,11},{10,... | collective-permute-start | bytes 786440 | tf_op jit(solution)/shard_map/cross_right_0/ppermute | solution.py:229
  11.5 15.2 %collective-permute-start.5 = (bf16[32,32,256]{2,1,0:T(8,128)(2,1)S(1)}, bf16[32,32,256]{2,1,0:T(8,128)(2,1)S(1)}, u32[]{:S(2)}, u32[]{:S(2)}) collective-permute-start(bf16[32,32,256]{2,1,0:T(8,128)(2,1)S(1)} %get-tuple-element.61.rest_2_), channel_id=1, source_target_pairs={{0,4},{1,5},{2,6},{3,7},{4,0},{5,1},{6,2},{7,3},{8,12},{9,13},{10,... | collective-permute-start | bytes 1572872 | tf_op jit(solution)/shard_map/end_right_0/ppermute | solution.py:229
  18.1 7.2 %collective-permute-start.3 = (bf16[16,32,256]{2,1,0:T(8,128)(2,1)S(1)}, bf16[16,32,256]{2,1,0:T(8,128)(2,1)S(1)}, u32[]{:S(2)}, u32[]{:S(2)}) collective-permute-start(bf16[16,32,256]{2,1,0:T(8,128)(2,1)S(1)} %get-tuple-element.59), channel_id=1, source_target_pairs={{0,2},{1,3},{2,0},{3,1},{4,6},{5,7},{6,4},{7,5},{8,10},{9,11},{10,... | collective-permute-start | bytes 786440 | tf_op jit(solution)/shard_map/cross_right_1/ppermute | solution.py:229
  19.4 10.5 %collective-permute-start.10 = (bf16[16,32,256]{2,1,0:T(8,128)(2,1)S(1)}, bf16[16,32,256]{2,1,0:T(8,128)(2,1)S(1)}, u32[]{:S(2)}, u32[]{:S(2)}) collective-permute-start(bf16[16,32,256]{2,1,0:T(8,128)(2,1)S(1)} %collective-permute-done.2.rest_3_), channel_id=1, source_target_pairs={{0,1},{1,0},{2,3},{3,2},{4,8},{5,9},{6,10},{7,11},{8,4},{9,5},{10,... | collective-permute-start | bytes 786440 | tf_op jit(solution)/shard_map/mid_own_10/ppermute | solution.py:229
  20.5 28.4 %collective-permute-start.8 = (bf16[32,32,256]{2,1,0:T(8,128)(2,1)S(1)}, bf16[32,32,256]{2,1,0:T(8,128)(2,1)S(1)}, u32[]{:S(2)}, u32[]{:S(2)}) collective-permute-start(bf16[32,32,256]{2,1,0:T(8,128)(2,1)S(1)} %get-tuple-element.74.rest_0_), channel_id=1, source_target_pairs={{0,4},{1,5},{2,6},{3,7},{4,0},{5,1},{6,2},{7,3},{8,12},{9,13},{10,... | collective-permute-start | bytes 1572872 | tf_op jit(solution)/shard_map/end_left_0/ppermute | solution.py:229
  25.3 6.3 %collective-permute-start.4 = (bf16[16,32,256]{2,1,0:T(8,128)(2,1)S(1)}, bf16[16,32,256]{2,1,0:T(8,128)(2,1)S(1)}, u32[]{:S(2)}, u32[]{:S(2)}) collective-permute-start(bf16[16,32,256]{2,1,0:T(8,128)(2,1)S(1)} %get-tuple-element.60), channel_id=1, source_target_pairs={{0,2},{1,3},{2,0},{3,1},{4,6},{5,7},{6,4},{7,5},{8,10},{9,11},{10,... | collective-permute-start | bytes 786440 | tf_op jit(solution)/shard_map/cross_left_0/ppermute | solution.py:229
  26.3 14.8 %collective-permute-start.6 = (bf16[16,32,256]{2,1,0:T(8,128)(2,1)S(1)}, bf16[16,32,256]{2,1,0:T(8,128)(2,1)S(1)}, u32[]{:S(2)}, u32[]{:S(2)}) collective-permute-start(bf16[16,32,256]{2,1,0:T(8,128)(2,1)S(1)} %collective-permute-done.2.rest_3_), channel_id=1, source_target_pairs={{0,4},{1,5},{2,6},{3,7},{4,0},{5,1},{6,2},{7,3},{8,12},{9,13},{10,... | collective-permute-start | bytes 786440 | tf_op jit(solution)/shard_map/end_right_10/ppermute | solution.py:229
  26.7 23.6 %collective-permute-start.11 = (bf16[32,32,256]{2,1,0:T(8,128)(2,1)S(1)}, bf16[32,32,256]{2,1,0:T(8,128)(2,1)S(1)}, u32[]{:S(2)}, u32[]{:S(2)}) collective-permute-start(bf16[32,32,256]{2,1,0:T(8,128)(2,1)S(1)} %collective-permute-done.5.rest_4_), channel_id=1, source_target_pairs={{0,1},{1,0},{2,3},{3,2},{4,8},{5,9},{6,10},{7,11},{8,4},{9,5},{10,... | collective-permute-start | bytes 1572872 | tf_op jit(solution)/shard_map/mid_next_0/ppermute | solution.py:229
  29.9 16.8 %collective-permute-start.18 = (bf16[16,32,256]{2,1,0:T(8,128)(2,1)S(1)}, bf16[16,32,256]{2,1,0:T(8,128)(2,1)S(1)}, u32[]{:S(2)}, u32[]{:S(2)}) collective-permute-start(bf16[16,32,256]{2,1,0:T(8,128)(2,1)S(1)} %collective-permute-done.3.rest_3_), channel_id=1, source_target_pairs={{0,4},{1,5},{2,6},{3,7},{4,0},{5,1},{6,2},{7,3},{8,12},{9,13},{10,... | collective-permute-start | bytes 786440 | tf_op jit(solution)/shard_map/end_right_11/ppermute | solution.py:229
  31.5 17.4 %collective-permute-start.17 = (bf16[16,32,256]{2,1,0:T(8,128)(2,1)S(1)}, bf16[16,32,256]{2,1,0:T(8,128)(2,1)S(1)}, u32[]{:S(2)}, u32[]{:S(2)}) collective-permute-start(bf16[16,32,256]{2,1,0:T(8,128)(2,1)S(1)} %get-tuple-element.73), channel_id=1, source_target_pairs={{0,2},{1,3},{2,0},{3,1},{4,6},{5,7},{6,4},{7,5},{8,10},{9,11},{10,... | collective-permute-start | bytes 786440 | tf_op jit(solution)/shard_map/cross_left_1/ppermute | solution.py:229
  41.1 9.3 %collective-permute-start.20 = (bf16[16,32,256]{2,1,0:T(8,128)(2,1)S(1)}, bf16[16,32,256]{2,1,0:T(8,128)(2,1)S(1)}, u32[]{:S(2)}, u32[]{:S(2)}) collective-permute-start(bf16[16,32,256]{2,1,0:T(8,128)(2,1)S(1)} %collective-permute-done.3.rest_3_), channel_id=1, source_target_pairs={{0,1},{1,0},{2,3},{3,2},{4,8},{5,9},{6,10},{7,11},{8,4},{9,5},{10,... | collective-permute-start | bytes 786440 | tf_op jit(solution)/shard_map/mid_own_11/ppermute | solution.py:229
  46.7 4.8 %collective-permute-start.12 = (bf16[16,32,256]{2,1,0:T(8,128)(2,1)S(1)}, bf16[16,32,256]{2,1,0:T(8,128)(2,1)S(1)}, u32[]{:S(2)}, u32[]{:S(2)}) collective-permute-start(bf16[16,32,256]{2,1,0:T(8,128)(2,1)S(1)} %collective-permute-done.6.rest_5_), channel_id=1, source_target_pairs={{0,1},{1,0},{2,3},{3,2},{4,8},{5,9},{6,10},{7,11},{8,4},{9,5},{10,... | collective-permute-start | bytes 786440 | tf_op jit(solution)/shard_map/mid_next_10/ppermute | solution.py:229
  48.9 7.4 %collective-permute-start.9 = (bf16[16,32,256]{2,1,0:T(8,128)(2,1)S(1)}, bf16[16,32,256]{2,1,0:T(8,128)(2,1)S(1)}, u32[]{:S(2)}, u32[]{:S(2)}) collective-permute-start(bf16[16,32,256]{2,1,0:T(8,128)(2,1)S(1)} %collective-permute-done.4.rest_1_), channel_id=1, source_target_pairs={{0,4},{1,5},{2,6},{3,7},{4,0},{5,1},{6,2},{7,3},{8,12},{9,13},{10,... | collective-permute-start | bytes 786440 | tf_op jit(solution)/shard_map/end_left_10/ppermute | solution.py:229
  48.9 13.0 %collective-permute-start.19 = (bf16[16,32,256]{2,1,0:T(8,128)(2,1)S(1)}, bf16[16,32,256]{2,1,0:T(8,128)(2,1)S(1)}, u32[]{:S(2)}, u32[]{:S(2)}) collective-permute-start(bf16[16,32,256]{2,1,0:T(8,128)(2,1)S(1)} %collective-permute-done.17.rest_1_), channel_id=1, source_target_pairs={{0,4},{1,5},{2,6},{3,7},{4,0},{5,1},{6,2},{7,3},{8,12},{9,13},{10,... | collective-permute-start | bytes 786440 | tf_op jit(solution)/shard_map/end_left_11/ppermute | solution.py:229
  50.4 11.5 %collective-permute-start.21 = (bf16[16,32,256]{2,1,0:T(8,128)(2,1)S(1)}, bf16[16,32,256]{2,1,0:T(8,128)(2,1)S(1)}, u32[]{:S(2)}, u32[]{:S(2)}) collective-permute-start(bf16[16,32,256]{2,1,0:T(8,128)(2,1)S(1)} %collective-permute-done.18.rest_5_), channel_id=1, source_target_pairs={{0,1},{1,0},{2,3},{3,2},{4,8},{5,9},{6,10},{7,11},{8,4},{9,5},{10,... | collective-permute-start | bytes 786440 | tf_op jit(solution)/shard_map/mid_next_11/ppermute | solution.py:229
  56.8 10.2 %collective-permute-start.13 = (bf16[16,64,128]{2,1,0:T(8,128)(2,1)S(1)}, bf16[16,64,128]{2,1,0:T(8,128)(2,1)S(1)}, u32[]{:S(2)}, u32[]{:S(2)}) collective-permute-start(bf16[16,64,128]{2,1,0:T(8,128)(2,1)S(1)} %get-tuple-element.67), channel_id=1, source_target_pairs={{4,0},{5,1},{6,2},{7,3},{8,12},{9,13},{10,14},{11,15},{20,16},{21,... | collective-permute-start | bytes 786440 | tf_op jit(solution)/shard_map/products_back_0/ppermute | solution.py:229
  62.4 10.3 %collective-permute-start.22 = (bf16[16,64,128]{2,1,0:T(8,128)(2,1)S(1)}, bf16[16,64,128]{2,1,0:T(8,128)(2,1)S(1)}, u32[]{:S(2)}, u32[]{:S(2)}) collective-permute-start(bf16[16,64,128]{2,1,0:T(8,128)(2,1)S(1)} %get-tuple-element.78), channel_id=1, source_target_pairs={{0,4},{1,5},{2,6},{3,7},{4,0},{5,1},{6,2},{7,3},{8,12},{9,13},{10,... | collective-permute-start | bytes 786440 | tf_op jit(solution)/shard_map/products_back_1/ppermute | solution.py:229
  63.1 21.6 %copy-start.3 = (bf16[128,128]{1,0:T(8,128)(2,1)S(1)}, bf16[128,128]{1,0:T(8,128)(2,1)}, u32[]{:S(2)}) copy-start(bf16[128,128]{1,0:T(8,128)(2,1)} %weight.5) | copy-start | bytes 98308
  63.1 21.6 %copy-start.6 = (f32[128]{0:T(128)S(1)}, f32[128]{0:T(128)}, u32[]{:S(2)}) copy-start(f32[128]{0:T(128)} %param.12) | copy-start | bytes 1540
  67.1 8.0 %collective-permute-start.14 = (bf16[16,32,128]{2,1,0:T(8,128)(2,1)S(1)}, bf16[16,32,128]{2,1,0:T(8,128)(2,1)S(1)}, u32[]{:S(2)}, u32[]{:S(2)}) collective-permute-start(bf16[16,32,128]{2,1,0:T(8,128)(2,1)S(1)} %get-tuple-element.69), channel_id=1, source_target_pairs={{0,1},{1,0},{2,3},{3,2},{4,5},{5,4},{6,7},{7,6},{8,9},{9,8},{10,11... | collective-permute-start | bytes 393224 | tf_op jit(solution)/shard_map/return_01/ppermute | solution.py:229
  71.0 5.3 %collective-permute-start.15 = (bf16[16,32,128]{2,1,0:T(8,128)(2,1)S(1)}, bf16[16,32,128]{2,1,0:T(8,128)(2,1)S(1)}, u32[]{:S(2)}, u32[]{:S(2)}) collective-permute-start(bf16[16,32,128]{2,1,0:T(8,128)(2,1)S(1)} %get-tuple-element.70), channel_id=1, source_target_pairs={{0,2},{1,3},{2,0},{3,1},{4,6},{5,7},{6,4},{7,5},{8,10},{9,11},{10,... | collective-permute-start | bytes 393224 | tf_op jit(solution)/shard_map/return_02/ppermute | solution.py:229
  72.4 7.1 %collective-permute-start.16 = (bf16[16,32,128]{2,1,0:T(8,128)(2,1)S(1)}, bf16[16,32,128]{2,1,0:T(8,128)(2,1)S(1)}, u32[]{:S(2)}, u32[]{:S(2)}) collective-permute-start(bf16[16,32,128]{2,1,0:T(8,128)(2,1)S(1)} %get-tuple-element.71), channel_id=1, source_target_pairs={{0,3},{1,2},{2,1},{3,0},{4,7},{5,6},{6,5},{7,4},{8,11},{9,10},{10,... | collective-permute-start | bytes 393224 | tf_op jit(solution)/shard_map/return_03/ppermute | solution.py:229
  72.8 6.7 %collective-permute-start.23 = (bf16[16,32,128]{2,1,0:T(8,128)(2,1)S(1)}, bf16[16,32,128]{2,1,0:T(8,128)(2,1)S(1)}, u32[]{:S(2)}, u32[]{:S(2)}) collective-permute-start(bf16[16,32,128]{2,1,0:T(8,128)(2,1)S(1)} %get-tuple-element.80), channel_id=1, source_target_pairs={{0,1},{1,0},{2,3},{3,2},{4,5},{5,4},{6,7},{7,6},{8,9},{9,8},{10,11... | collective-permute-start | bytes 393224 | tf_op jit(solution)/shard_map/return_11/ppermute | solution.py:229
  74.6 7.2 %collective-permute-start.24 = (bf16[16,32,128]{2,1,0:T(8,128)(2,1)S(1)}, bf16[16,32,128]{2,1,0:T(8,128)(2,1)S(1)}, u32[]{:S(2)}, u32[]{:S(2)}) collective-permute-start(bf16[16,32,128]{2,1,0:T(8,128)(2,1)S(1)} %get-tuple-element.81), channel_id=1, source_target_pairs={{0,2},{1,3},{2,0},{3,1},{4,6},{5,7},{6,4},{7,5},{8,10},{9,11},{10,... | collective-permute-start | bytes 393224 | tf_op jit(solution)/shard_map/return_12/ppermute | solution.py:229
  75.1 9.6 %collective-permute-start.25 = (bf16[16,32,128]{2,1,0:T(8,128)(2,1)S(1)}, bf16[16,32,128]{2,1,0:T(8,128)(2,1)S(1)}, u32[]{:S(2)}, u32[]{:S(2)}) collective-permute-start(bf16[16,32,128]{2,1,0:T(8,128)(2,1)S(1)} %get-tuple-element.82), channel_id=1, source_target_pairs={{0,3},{1,2},{2,1},{3,0},{4,7},{5,6},{6,5},{7,4},{8,11},{9,10},{10,... | collective-permute-start | bytes 393224 | tf_op jit(solution)/shard_map/return_13/ppermute | solution.py:229

commit v10 on v9

--- a/solution.py
+++ b/solution.py
@@ -11,7 +11,7 @@
 F32, BF16 = jnp.float32, jnp.bfloat16
 LANES = 128
 SPARE = 6 * 1024 * 1024
-SHARES = (4, 4)
+SHARES = (5, 3)
 NT = (((1,), (1,)), ((), ()))
 TN = (((0,), (0,)), ((), ()))
 VMEM = pl.BlockSpec(memory_space=pltpu.VMEM)
@@ -299,17 +299,19 @@
         gate_kernel, "gate", jax.ShapeDtypeStruct((rows, toks, channels), F32), [VMEM] * 2
     )(normed0, gate_weight)
     right1[0] = after(crossed, left0)
-    right1[1] = cross("right_1", right1[1], right1[0])
-    own1 = [mid(f"own_1{g}", right1[g]) for g in groups]
-    near1 = [end_right(f"1{g}", right1[g]) for g in groups]
-    left1[0] = cross("left_0", left1[0], right1[1])
+    own1 = [mid("own_10", right1[0])]
+    near1 = [end_right("10", right1[0])]
+    left1[0] = cross("left_0", left1[0], crossed, own0)
     next0 = [mid("next_0", x, own0) for x in near0]
-    outer0 = end_left("0", left0, own0, crossed)
-    left1[1] = cross("left_1", left1[1], left1[0], own1[0])
+    outer0 = end_left("0", left0, own0)
+    right1[1] = cross("right_1", right1[1], left1[0], own1[0])
     next1 = [[mid("next_10", x, own1[0], gate) for x in near1[0]]]
     outer1 = [end_left("10", left1[0], near1[0][-1])]
-    next1.append([mid("next_11", x, own1[1], next0[-1]) for x in near1[1]])
-    outer1.append(end_left("11", left1[1], near1[1][-1], outer0))
+    left1[1] = cross("left_1", left1[1], right1[1], next0[-1])
+    own1.append(mid("own_11", right1[1], own1[0]))
+    near1.append(end_right("11", right1[1], outer0))
+    next1.append([mid("next_11", x, next1[0][-1], own1[1]) for x in near1[1]])
+    outer1.append(end_left("11", left1[1], outer1[0], own1[1]))
 
     def products(mirror, first, lefts, rights, name):
         span = 2 * rows * len(rights)

time: 87.8 us -> 84.6 us (0.964)
  waiting for transfers between devices: 35.4 us -> 33.1 us
  starting transfers between devices: 35.8 us -> 34.9 us
    ppermute x26, waiting for transfers between devices: 35.4 us -> 33.1 us  [send(): return lax.ppermute(x, ('row', 'chan'), pairs)]
    ppermute x26, starting transfers between devices: 35.8 us -> 34.9 us  [send(): return lax.ppermute(x, ('row', 'chan'), pairs)]
  transfers between devices with their start and end apart: 26 -> 26, of which waited for: 11 -> 10; matrix products, arithmetic and copies ran while one was open for 0% -> 0% of each run, Pallas kernels for 9% -> 9%
where the time goes in v10:
time: 84.6 us; the launch traced here: 84.1 us
  starting transfers between devices  34.9 us (41%)
  waiting for transfers between devices  33.1 us (39%)
  Pallas kernels  12.4 us (15%)
  local copies, waits for them, and re-layouts  3.52 us (4%)
    ppermute x26, starting transfers between devices, send(): return lax.ppermute(x, ('row', 'chan'), pairs)  34.9 us
    ppermute x26, waiting for transfers between devices, send(): return lax.ppermute(x, ('row', 'chan'), pairs)  33.1 us
    pallas_call x11, Pallas kernels, call(): pl.pallas_call(body, out_shape=out_shape, in_specs=in_specs, out_specs=ou...  12.4 us
    unnamed x14, local copies, waits for them, and re-layouts  3.52 us
  transfers between devices with their start and end apart: 26, of which 10 were waited for; matrix products, arithmetic and copies ran while one was open for 0% of the time, Pallas kernels for 9%

profile of v10, /device:TPU:1, one launch (start us, length us, event | category | flops | bytes accessed | tf_op | source)
XLA Modules:
  0.0 84.1 jit_solution(10406279417499747056)
XLA Ops:
  0.0 0.1 collective-permute-start
  0.1 0.5 collective-permute-start.1
  0.5 1.2 %copy-done = bf16[32,128,128]{2,1,0:T(8,128)(2,1)S(1)} copy-done((bf16[32,128,128]{2,1,0:T(8,128)(2,1)S(1)}, bf16[32,128,128]{2,1,0:T(8,128)(2,1)}, u32[]{:S(2)}) %copy-start) | copy-done | bytes 1048600
  1.7 0.9 %copy-done.1 = bf16[128,512]{1,0:T(8,128)(2,1)S(1)} copy-done((bf16[128,512]{1,0:T(8,128)(2,1)S(1)}, bf16[128,512]{1,0:T(8,128)(2,1)}, u32[]{:S(2)}) %copy-start.1) | copy-done | bytes 131096
  2.6 0.7 copy-done.4
  3.4 0.7 copy-done.5
  4.0 2.3 %right_own.1 = (bf16[32,32,128]{2,1,0:T(8,128)(2,1)S(1)}, bf16[20,32,128]{2,1,0:T(8,128)(2,1)S(1)}, bf16[12,32,128]{2,1,0:T(8,128)(2,1)S(1)}, bf16[4096,128]{1,0...) custom-call(bf16[32,128,128]{2,1,0:T(8,128)(2,1)S(1)} %copy-done, ...), custom_call_target="tpu_custom_call" | custom-call | tf_op jit(solution)/shard_map/right_own/pallas_call | solution.py:201
  6.3 0.0 copy-start.2
  6.3 0.0 collective-permute-done.1.mask
  6.3 0.0 collective-permute-done.pair
  6.3 2.3 %right_twin.1 = (bf16[32,32,256]{2,1,0:T(8,128)(2,1)S(1)}, bf16[20,32,256]{2,1,0:T(8,128)(2,1)S(1)}, bf16[12,32,256]{2,1,0:T(8,128)(2,1)S(1)}, bf16[4096,128]{1,0:T(8,128)(2,1)S(1)}, f32[1,32,128]{2,1,0:T(8,128)S(1)}) custom-call(bf16[32,128,128]{2,1,0:T(8,128)(2,1)S(1)} %collective-permute-done.pair, s32[32,128]{1,0:T(8,128)S(1)} %collective-permute-done.1.mask, ...), custom_call_target="tpu_custom_call" | custom-call | tf_op jit(solution)/shard_map/right_twin/pallas_call | solution.py:201
  8.7 0.1 collective-permute-start.3
  8.8 3.5 %collective-permute-start.5 = (bf16[32,32,256]{2,1,0:T(8,128)(2,1)S(1)}, bf16[32,32,256]{2,1,0:T(8,128)(2,1)S(1)}, u32[]{:S(2)}, u32[]{:S(2)}) collective-permute-start(bf16[32,32,256]{2,1,0:T(8,128)(2,1)S(1)} %get-tuple-element.59.rest_2_), channel_id=1, source_target_pairs={{0,4},{1,5},{2,6},{3,7},{4,0},{5,1},{6,2},{7,3},{8,12},{9,13},{10,... | collective-permute-start | bytes 1572872 | tf_op jit(solution)/shard_map/end_right_0/ppermute | solution.py:229
  12.3 1.2 %collective-permute-start.2 = (bf16[20,32,256]{2,1,0:T(8,128)(2,1)S(1)}, bf16[20,32,256]{2,1,0:T(8,128)(2,1)S(1)}, u32[]{:S(2)}, u32[]{:S(2)}) collective-permute-start(bf16[20,32,256]{2,1,0:T(8,128)(2,1)S(1)} %get-tuple-element.58), channel_id=1, source_target_pairs={{0,2},{1,3},{2,0},{3,1},{4,6},{5,7},{6,4},{7,5},{8,10},{9,11},{10,... | collective-permute-start | bytes 983048 | tf_op jit(solution)/shard_map/cross_right_0/ppermute | solution.py:229
  13.6 2.0 %left.1 = (bf16[32,32,256]{2,1,0:T(8,128)(2,1)S(1)}, bf16[20,32,256]{2,1,0:T(8,128)(2,1)S(1)}, bf16[12,32,256]{2,1,0:T(8,128)(2,1)S(1)}) custom-call(bf16[4096,128]{1,0:T(8,128)(2,1)S(1)} %get-tuple-element.46.normed.normed0, bf16[4096,128]{1,0:T(8,128)(2,1)S(1)} %get-tuple-element.52.normed1, f32[1,32,128]{2,1,0:T(8,128)S(1)} %get-tuple-element.53.valid0, ...), custom_call_target="tpu_custom_call" | custom-call | tf_op jit(solution)/shard_map/left/pallas_call | solution.py:201
  15.6 4.9 %collective-permute-done.2.rest_3_ = bf16[20,32,256]{2,1,0:T(8,128)(2,1)S(1)} collective-permute-done((bf16[20,32,256]{2,1,0:T(8,128)(2,1)S(1)}, bf16[20,32,256]{2,1,0:T(8,128)(2,1)S(1)}, u32[]{:S(2)}, u32[]{:S(2)}) %collective-permute-start.2) | collective-permute-done | bytes 327712 | tf_op jit(solution)/shard_map/cross_right_0/ppermute | solution.py:229
  20.5 2.0 %collective-permute-start.9 = (bf16[20,32,256]{2,1,0:T(8,128)(2,1)S(1)}, bf16[20,32,256]{2,1,0:T(8,128)(2,1)S(1)}, u32[]{:S(2)}, u32[]{:S(2)}) collective-permute-start(bf16[20,32,256]{2,1,0:T(8,128)(2,1)S(1)} %collective-permute-done.2.rest_3_), channel_id=1, source_target_pairs={{0,1},{1,0},{2,3},{3,2},{4,8},{5,9},{6,10},{7,11},{8,4},{9,5},{10,... | collective-permute-start | bytes 983048 | tf_op jit(solution)/shard_map/mid_own_10/ppermute | solution.py:229
  22.4 0.6 collective-permute-start.6
  23.1 1.2 %collective-permute-start.4 = (bf16[20,32,256]{2,1,0:T(8,128)(2,1)S(1)}, bf16[20,32,256]{2,1,0:T(8,128)(2,1)S(1)}, u32[]{:S(2)}, u32[]{:S(2)}) collective-permute-start(bf16[20,32,256]{2,1,0:T(8,128)(2,1)S(1)} %get-tuple-element.60), channel_id=1, source_target_pairs={{0,2},{1,3},{2,0},{3,1},{4,6},{5,7},{6,4},{7,5},{8,10},{9,11},{10,... | collective-permute-start | bytes 983048 | tf_op jit(solution)/shard_map/cross_left_0/ppermute | solution.py:229
  24.3 2.0 %collective-permute-start.10 = (bf16[32,32,256]{2,1,0:T(8,128)(2,1)S(1)}, bf16[32,32,256]{2,1,0:T(8,128)(2,1)S(1)}, u32[]{:S(2)}, u32[]{:S(2)}) collective-permute-start(bf16[32,32,256]{2,1,0:T(8,128)(2,1)S(1)} %collective-permute-done.5.rest_4_), channel_id=1, source_target_pairs={{0,1},{1,0},{2,3},{3,2},{4,8},{5,9},{6,10},{7,11},{8,4},{9,5},{10,... | collective-permute-start | bytes 1572872 | tf_op jit(solution)/shard_map/mid_next_0/ppermute | solution.py:229
  26.3 0.2 collective-permute-start.7
  26.5 0.9 %gate.1 = f32[32,128,128]{2,1,0:T(8,128)S(1)} custom-call(bf16[4096,128]{1,0:T(8,128)(2,1)S(1)} %get-tuple-element.46.normed.normed0, bf16[128,128]{1,0:T(8,128)(2,1)S(1)} %copy-done.2), custom_call_target="tpu_custom_call" | custom-call | tf_op jit(solution)/shard_map/gate/pallas_call | solution.py:201
  27.5 3.9 %collective-permute-done.6.rest_5_ = bf16[20,32,256]{2,1,0:T(8,128)(2,1)S(1)} collective-permute-done((bf16[20,32,256]{2,1,0:T(8,128)(2,1)S(1)}, bf16[20,32,256]{2,1,0:T(8,128)(2,1)S(1)}, u32[]{:S(2)}, u32[]{:S(2)}) %collective-permute-start.6) | collective-permute-done | bytes 327712 | tf_op jit(solution)/shard_map/end_right_10/ppermute | solution.py:229
  31.4 2.0 %collective-permute-start.11 = (bf16[20,32,256]{2,1,0:T(8,128)(2,1)S(1)}, bf16[20,32,256]{2,1,0:T(8,128)(2,1)S(1)}, u32[]{:S(2)}, u32[]{:S(2)}) collective-permute-start(bf16[20,32,256]{2,1,0:T(8,128)(2,1)S(1)} %collective-permute-done.6.rest_5_), channel_id=1, source_target_pairs={{0,1},{1,0},{2,3},{3,2},{4,8},{5,9},{6,10},{7,11},{8,4},{9,5},{10,... | collective-permute-start | bytes 983048 | tf_op jit(solution)/shard_map/mid_next_10/ppermute | solution.py:229
  33.4 0.0 collective-permute-done.4.rest_1_
  33.4 0.0 collective-permute-start.8
  33.4 1.2 %collective-permute-start.16 = (bf16[12,32,256]{2,1,0:T(8,128)(2,1)S(1)}, bf16[12,32,256]{2,1,0:T(8,128)(2,1)S(1)}, u32[]{:S(2)}, u32[]{:S(2)}) collective-permute-start(bf16[12,32,256]{2,1,0:T(8,128)(2,1)S(1)} %get-tuple-element.74), channel_id=1, source_target_pairs={{0,2},{1,3},{2,0},{3,1},{4,6},{5,7},{6,4},{7,5},{8,10},{9,11},{10,... | collective-permute-start | bytes 589832 | tf_op jit(solution)/shard_map/cross_right_1/ppermute | solution.py:229
  34.6 3.6 %collective-permute-done.16.rest_3_ = bf16[12,32,256]{2,1,0:T(8,128)(2,1)S(1)} collective-permute-done((bf16[12,32,256]{2,1,0:T(8,128)(2,1)S(1)}, bf16[12,32,256]{2,1,0:T(8,128)(2,1)S(1)}, u32[]{:S(2)}, u32[]{:S(2)}) %collective-permute-start.16) | collective-permute-done | bytes 196640 | tf_op jit(solution)/shard_map/cross_right_1/ppermute | solution.py:229
  38.2 3.0 %collective-permute-start.19 = (bf16[12,32,256]{2,1,0:T(8,128)(2,1)S(1)}, bf16[12,32,256]{2,1,0:T(8,128)(2,1)S(1)}, u32[]{:S(2)}, u32[]{:S(2)}) collective-permute-start(bf16[12,32,256]{2,1,0:T(8,128)(2,1)S(1)} %collective-permute-done.16.rest_3_), channel_id=1, source_target_pairs={{0,1},{1,0},{2,3},{3,2},{4,8},{5,9},{6,10},{7,11},{8,4},{9,5},{10,... | collective-permute-start | bytes 589832 | tf_op jit(solution)/shard_map/mid_own_11/ppermute | solution.py:229
  41.2 0.0 collective-permute-done.10.rest_6_
  41.2 1.2 %collective-permute-start.17 = (bf16[12,32,256]{2,1,0:T(8,128)(2,1)S(1)}, bf16[12,32,256]{2,1,0:T(8,128)(2,1)S(1)}, u32[]{:S(2)}, u32[]{:S(2)}) collective-permute-start(bf16[12,32,256]{2,1,0:T(8,128)(2,1)S(1)} %get-tuple-element.75), channel_id=1, source_target_pairs={{0,2},{1,3},{2,0},{3,1},{4,6},{5,7},{6,4},{7,5},{8,10},{9,11},{10,... | collective-permute-start | bytes 589832 | tf_op jit(solution)/shard_map/cross_left_1/ppermute | solution.py:229
  42.4 0.2 collective-permute-done.7.rest_2_
  42.6 1.1 %collective-permute-start.18 = (bf16[12,32,256]{2,1,0:T(8,128)(2,1)S(1)}, bf16[12,32,256]{2,1,0:T(8,128)(2,1)S(1)}, u32[]{:S(2)}, u32[]{:S(2)}) collective-permute-start(bf16[12,32,256]{2,1,0:T(8,128)(2,1)S(1)} %collective-permute-done.16.rest_3_), channel_id=1, source_target_pairs={{0,4},{1,5},{2,6},{3,7},{4,0},{5,1},{6,2},{7,3},{8,12},{9,13},{10,... | collective-permute-start | bytes 589832 | tf_op jit(solution)/shard_map/end_right_11/ppermute | solution.py:229
  43.7 0.0 collective-permute-done.11.rest_7_
  43.7 5.9 %collective-permute-done.8.rest_3_ = bf16[20,32,256]{2,1,0:T(8,128)(2,1)S(1)} collective-permute-done((bf16[20,32,256]{2,1,0:T(8,128)(2,1)S(1)}, bf16[20,32,256]{2,1,0:T(8,128)(2,1)S(1)}, u32[]{:S(2)}, u32[]{:S(2)}) %collective-permute-start.8) | collective-permute-done | bytes 327712 | tf_op jit(solution)/shard_map/end_left_10/ppermute | solution.py:229
  49.6 0.6 away.2
  50.3 1.3 %collective-permute-start.12 = (bf16[20,64,128]{2,1,0:T(8,128)(2,1)S(1)}, bf16[20,64,128]{2,1,0:T(8,128)(2,1)S(1)}, u32[]{:S(2)}, u32[]{:S(2)}) collective-permute-start(bf16[20,64,128]{2,1,0:T(8,128)(2,1)S(1)} %get-tuple-element.67), channel_id=1, source_target_pairs={{4,0},{5,1},{6,2},{7,3},{8,12},{9,13},{10,14},{11,15},{20,16},{21,... | collective-permute-start | bytes 983048 | tf_op jit(solution)/shard_map/products_back_0/ppermute | solution.py:229
  51.6 0.0 collective-permute-done.19.rest_5_
  51.6 2.2 %collective-permute-start.20 = (bf16[12,32,256]{2,1,0:T(8,128)(2,1)S(1)}, bf16[12,32,256]{2,1,0:T(8,128)(2,1)S(1)}, u32[]{:S(2)}, u32[]{:S(2)}) collective-permute-start(bf16[12,32,256]{2,1,0:T(8,128)(2,1)S(1)} %collective-permute-done.17.rest_1_), channel_id=1, source_target_pairs={{0,4},{1,5},{2,6},{3,7},{4,0},{5,1},{6,2},{7,3},{8,12},{9,13},{10,... | collective-permute-start | bytes 589832 | tf_op jit(solution)/shard_map/end_left_11/ppermute | solution.py:229
  53.8 0.1 collective-permute-done.18.rest_5_
  53.9 2.4 %collective-permute-start.21 = (bf16[12,32,256]{2,1,0:T(8,128)(2,1)S(1)}, bf16[12,32,256]{2,1,0:T(8,128)(2,1)S(1)}, u32[]{:S(2)}, u32[]{:S(2)}) collective-permute-start(bf16[12,32,256]{2,1,0:T(8,128)(2,1)S(1)} %collective-permute-done.18.rest_5_), channel_id=1, source_target_pairs={{0,1},{1,0},{2,3},{3,2},{4,8},{5,9},{6,10},{7,11},{8,4},{9,5},{10,... | collective-permute-start | bytes 589832 | tf_op jit(solution)/shard_map/mid_next_11/ppermute | solution.py:229
  56.3 7.3 %collective-permute-done.20.rest_3_ = bf16[12,32,256]{2,1,0:T(8,128)(2,1)S(1)} collective-permute-done((bf16[12,32,256]{2,1,0:T(8,128)(2,1)S(1)}, bf16[12,32,256]{2,1,0:T(8,128)(2,1)S(1)}, u32[]{:S(2)}, u32[]{:S(2)}) %collective-permute-start.20) | collective-permute-done | bytes 196640 | tf_op jit(solution)/shard_map/end_left_11/ppermute | solution.py:229
  63.6 0.4 away.3
  64.1 0.1 collective-permute-start.22
  64.1 0.7 near.2
  64.8 0.0 copy-start.3
  64.8 0.0 copy-start.6
  64.9 0.0 collective-permute-done.12.end
  64.9 0.1 hand_out.2
  65.0 3.0 %collective-permute-start.13 = (bf16[20,32,128]{2,1,0:T(8,128)(2,1)S(1)}, bf16[20,32,128]{2,1,0:T(8,128)(2,1)S(1)}, u32[]{:S(2)}, u32[]{:S(2)}) collective-permute-start(bf16[20,32,128]{2,1,0:T(8,128)(2,1)S(1)} %get-tuple-element.69), channel_id=1, source_target_pairs={{0,1},{1,0},{2,3},{3,2},{4,5},{5,4},{6,7},{7,6},{8,9},{9,8},{10,11... | collective-permute-start | bytes 491528 | tf_op jit(solution)/shard_map/return_01/ppermute | solution.py:229
  67.9 1.3 %collective-permute-start.14 = (bf16[20,32,128]{2,1,0:T(8,128)(2,1)S(1)}, bf16[20,32,128]{2,1,0:T(8,128)(2,1)S(1)}, u32[]{:S(2)}, u32[]{:S(2)}) collective-permute-start(bf16[20,32,128]{2,1,0:T(8,128)(2,1)S(1)} %get-tuple-element.70), channel_id=1, source_target_pairs={{0,2},{1,3},{2,0},{3,1},{4,6},{5,7},{6,4},{7,5},{8,10},{9,11},{10,... | collective-permute-start | bytes 491528 | tf_op jit(solution)/shard_map/return_02/ppermute | solution.py:229
  69.2 0.4 collective-permute-start.15
  69.6 0.5 near.3
  70.1 0.0 collective-permute-done.22.end
  70.1 0.1 hand_out.3
  70.2 2.6 %collective-permute-start.23 = (bf16[12,32,128]{2,1,0:T(8,128)(2,1)S(1)}, bf16[12,32,128]{2,1,0:T(8,128)(2,1)S(1)}, u32[]{:S(2)}, u32[]{:S(2)}) collective-permute-start(bf16[12,32,128]{2,1,0:T(8,128)(2,1)S(1)} %get-tuple-element.84), channel_id=1, source_target_pairs={{0,1},{1,0},{2,3},{3,2},{4,5},{5,4},{6,7},{7,6},{8,9},{9,8},{10,11... | collective-permute-start | bytes 294920 | tf_op jit(solution)/shard_map/return_11/ppermute | solution.py:229
  72.8 1.3 %collective-permute-start.24 = (bf16[12,32,128]{2,1,0:T(8,128)(2,1)S(1)}, bf16[12,32,128]{2,1,0:T(8,128)(2,1)S(1)}, u32[]{:S(2)}, u32[]{:S(2)}) collective-permute-start(bf16[12,32,128]{2,1,0:T(8,128)(2,1)S(1)} %get-tuple-element.85), channel_id=1, source_target_pairs={{0,2},{1,3},{2,0},{3,1},{4,6},{5,7},{6,4},{7,5},{8,10},{9,11},{10,... | collective-permute-start | bytes 294920 | tf_op jit(solution)/shard_map/return_12/ppermute | solution.py:229
  74.1 0.0 collective-permute-done.13.rest_1_
  74.1 0.4 collective-permute-start.25
  74.5 0.0 collective-permute-done.14.rest_2_
  74.5 3.3 %collective-permute-done.15.rest_3_ = bf16[20,32,128]{2,1,0:T(8,128)(2,1)S(1)} collective-permute-done((bf16[20,32,128]{2,1,0:T(8,128)(2,1)S(1)}, bf16[20,32,128]{2,1,0:T(8,128)(2,1)S(1)}, u32[]{:S(2)}, u32[]{:S(2)}) %collective-permute-start.15) | collective-permute-done | bytes 163872 | tf_op jit(solution)/shard_map/return_03/ppermute | solution.py:229
  77.8 1.5 %collective-permute-done.24.rest_6_ = bf16[12,32,128]{2,1,0:T(8,128)(2,1)S(1)} collective-permute-done((bf16[12,32,128]{2,1,0:T(8,128)(2,1)S(1)}, bf16[12,32,128]{2,1,0:T(8,128)(2,1)S(1)}, u32[]{:S(2)}, u32[]{:S(2)}) %collective-permute-start.24) | collective-permute-done | bytes 98336 | tf_op jit(solution)/shard_map/return_12/ppermute | solution.py:229
  79.3 2.3 %collective-permute-done.25.rest_7_ = bf16[12,32,128]{2,1,0:T(8,128)(2,1)S(1)} collective-permute-done((bf16[12,32,128]{2,1,0:T(8,128)(2,1)S(1)}, bf16[12,32,128]{2,1,0:T(8,128)(2,1)S(1)}, u32[]{:S(2)}, u32[]{:S(2)}) %collective-permute-start.25) | collective-permute-done | bytes 98336 | tf_op jit(solution)/shard_map/return_13/ppermute | solution.py:229
  81.6 2.5 %update.1 = bf16[32,128,128]{2,1,0:T(8,128)(2,1)} custom-call(f32[1,128]{1,0:T(1,128)S(1)} %bitcast.3, bf16[128,128]{1,0:T(8,128)(2,1)S(1)} %copy-done.3, f32[32,128,128]{2,1,0:T(8,128)S(1)} %gate.1, bf16[20,32,128]{2,1,0:T(8,128)(2,1)S(1)} %get-tuple-element.68.rest_0_, bf16[20,32,128]{2,1,0:T(8,128)(2,1)S(1)} %collective-permute-done.13.rest_1_, ...), custom_call_target="tpu_custom_call" | custom-call | tf_op jit(solution)/shard_map/update/pallas_call | solution.py:201
  (13 shorter events, 0.0 us)
Async XLA Ops:
  0.0 6.3 %collective-permute-start = (bf16[32,128,128]{2,1,0:T(8,128)(2,1)}, bf16[32,128,128]{2,1,0:T(8,128)(2,1)S(1)}, u32[]{:S(2)}, u32[]{:S(2)}) collective-permute-start(bf16[32,128,128]{2,1,0:T(8,128)(2,1)} %pair.1), channel_id=1, source_target_pairs={{0,1},{1,0},{2,3},{3,2},{4,5},{5,4},{6,7},{7,6},{8,9},{9,8},{10,11... | collective-permute-start | bytes 3145736 | tf_op jit(solution)/shard_map/pair/ppermute | solution.py:229
  0.1 6.3 %collective-permute-start.1 = (s32[32,128]{1,0:T(8,128)}, s32[32,128]{1,0:T(8,128)S(1)}, u32[]{:S(2)}, u32[]{:S(2)}) collective-permute-start(s32[32,128]{1,0:T(8,128)} %mask.1), channel_id=1, source_target_pairs={{0,1},{1,0},{2,3},{3,2},{4,5},{5,4},{6,7},{7,6},{8,9},{9,8},{10,11... | collective-permute-start | bytes 49160 | tf_op jit(solution)/shard_map/mask/ppermute | solution.py:229
  0.5 1.2 %copy-start = (bf16[32,128,128]{2,1,0:T(8,128)(2,1)S(1)}, bf16[32,128,128]{2,1,0:T(8,128)(2,1)}, u32[]{:S(2)}) copy-start(bf16[32,128,128]{2,1,0:T(8,128)(2,1)} %pair.1) | copy-start | bytes 3145732
  1.7 0.9 %copy-start.1 = (bf16[128,512]{1,0:T(8,128)(2,1)S(1)}, bf16[128,512]{1,0:T(8,128)(2,1)}, u32[]{:S(2)}) copy-start(bf16[128,512]{1,0:T(8,128)(2,1)} %weight.3) | copy-start | bytes 393220
  2.6 0.7 copy-start.4
  3.4 0.7 copy-start.5
  6.3 20.2 %copy-start.2 = (bf16[128,128]{1,0:T(8,128)(2,1)S(1)}, bf16[128,128]{1,0:T(8,128)(2,1)}, u32[]{:S(2)}) copy-start(bf16[128,128]{1,0:T(8,128)(2,1)} %weight.4) | copy-start | bytes 98308
  8.7 14.4 %collective-permute-start.3 = (bf16[32,32,256]{2,1,0:T(8,128)(2,1)S(1)}, bf16[32,32,256]{2,1,0:T(8,128)(2,1)S(1)}, u32[]{:S(2)}, u32[]{:S(2)}) collective-permute-start(bf16[32,32,256]{2,1,0:T(8,128)(2,1)S(1)} %get-tuple-element.59.rest_2_), channel_id=1, source_target_pairs={{0,1},{1,0},{2,3},{3,2},{4,8},{5,9},{6,10},{7,11},{8,4},{9,5},{10,... | collective-permute-start | bytes 1572872 | tf_op jit(solution)/shard_map/mid_own_0/ppermute | solution.py:229
  8.8 15.5 %collective-permute-start.5 = (bf16[32,32,256]{2,1,0:T(8,128)(2,1)S(1)}, bf16[32,32,256]{2,1,0:T(8,128)(2,1)S(1)}, u32[]{:S(2)}, u32[]{:S(2)}) collective-permute-start(bf16[32,32,256]{2,1,0:T(8,128)(2,1)S(1)} %get-tuple-element.59.rest_2_), channel_id=1, source_target_pairs={{0,4},{1,5},{2,6},{3,7},{4,0},{5,1},{6,2},{7,3},{8,12},{9,13},{10,... | collective-permute-start | bytes 1572872 | tf_op jit(solution)/shard_map/end_right_0/ppermute | solution.py:229
  12.3 8.1 %collective-permute-start.2 = (bf16[20,32,256]{2,1,0:T(8,128)(2,1)S(1)}, bf16[20,32,256]{2,1,0:T(8,128)(2,1)S(1)}, u32[]{:S(2)}, u32[]{:S(2)}) collective-permute-start(bf16[20,32,256]{2,1,0:T(8,128)(2,1)S(1)} %get-tuple-element.58), channel_id=1, source_target_pairs={{0,2},{1,3},{2,0},{3,1},{4,6},{5,7},{6,4},{7,5},{8,10},{9,11},{10,... | collective-permute-start | bytes 983048 | tf_op jit(solution)/shard_map/cross_right_0/ppermute | solution.py:229
  20.5 7.0 %collective-permute-start.9 = (bf16[20,32,256]{2,1,0:T(8,128)(2,1)S(1)}, bf16[20,32,256]{2,1,0:T(8,128)(2,1)S(1)}, u32[]{:S(2)}, u32[]{:S(2)}) collective-permute-start(bf16[20,32,256]{2,1,0:T(8,128)(2,1)S(1)} %collective-permute-done.2.rest_3_), channel_id=1, source_target_pairs={{0,1},{1,0},{2,3},{3,2},{4,8},{5,9},{6,10},{7,11},{8,4},{9,5},{10,... | collective-permute-start | bytes 983048 | tf_op jit(solution)/shard_map/mid_own_10/ppermute | solution.py:229
  22.4 8.9 %collective-permute-start.6 = (bf16[20,32,256]{2,1,0:T(8,128)(2,1)S(1)}, bf16[20,32,256]{2,1,0:T(8,128)(2,1)S(1)}, u32[]{:S(2)}, u32[]{:S(2)}) collective-permute-start(bf16[20,32,256]{2,1,0:T(8,128)(2,1)S(1)} %collective-permute-done.2.rest_3_), channel_id=1, source_target_pairs={{0,4},{1,5},{2,6},{3,7},{4,0},{5,1},{6,2},{7,3},{8,12},{9,13},{10,... | collective-permute-start | bytes 983048 | tf_op jit(solution)/shard_map/end_right_10/ppermute | solution.py:229
  23.1 10.3 %collective-permute-start.4 = (bf16[20,32,256]{2,1,0:T(8,128)(2,1)S(1)}, bf16[20,32,256]{2,1,0:T(8,128)(2,1)S(1)}, u32[]{:S(2)}, u32[]{:S(2)}) collective-permute-start(bf16[20,32,256]{2,1,0:T(8,128)(2,1)S(1)} %get-tuple-element.60), channel_id=1, source_target_pairs={{0,2},{1,3},{2,0},{3,1},{4,6},{5,7},{6,4},{7,5},{8,10},{9,11},{10,... | collective-permute-start | bytes 983048 | tf_op jit(solution)/shard_map/cross_left_0/ppermute | solution.py:229
  24.3 16.8 %collective-permute-start.10 = (bf16[32,32,256]{2,1,0:T(8,128)(2,1)S(1)}, bf16[32,32,256]{2,1,0:T(8,128)(2,1)S(1)}, u32[]{:S(2)}, u32[]{:S(2)}) collective-permute-start(bf16[32,32,256]{2,1,0:T(8,128)(2,1)S(1)} %collective-permute-done.5.rest_4_), channel_id=1, source_target_pairs={{0,1},{1,0},{2,3},{3,2},{4,8},{5,9},{6,10},{7,11},{8,4},{9,5},{10,... | collective-permute-start | bytes 1572872 | tf_op jit(solution)/shard_map/mid_next_0/ppermute | solution.py:229
  26.3 16.3 %collective-permute-start.7 = (bf16[32,32,256]{2,1,0:T(8,128)(2,1)S(1)}, bf16[32,32,256]{2,1,0:T(8,128)(2,1)S(1)}, u32[]{:S(2)}, u32[]{:S(2)}) collective-permute-start(bf16[32,32,256]{2,1,0:T(8,128)(2,1)S(1)} %get-tuple-element.77.rest_0_), channel_id=1, source_target_pairs={{0,4},{1,5},{2,6},{3,7},{4,0},{5,1},{6,2},{7,3},{8,12},{9,13},{10,... | collective-permute-start | bytes 1572872 | tf_op jit(solution)/shard_map/end_left_0/ppermute | solution.py:229
  31.4 12.3 %collective-permute-start.11 = (bf16[20,32,256]{2,1,0:T(8,128)(2,1)S(1)}, bf16[20,32,256]{2,1,0:T(8,128)(2,1)S(1)}, u32[]{:S(2)}, u32[]{:S(2)}) collective-permute-start(bf16[20,32,256]{2,1,0:T(8,128)(2,1)S(1)} %collective-permute-done.6.rest_5_), channel_id=1, source_target_pairs={{0,1},{1,0},{2,3},{3,2},{4,8},{5,9},{6,10},{7,11},{8,4},{9,5},{10,... | collective-permute-start | bytes 983048 | tf_op jit(solution)/shard_map/mid_next_10/ppermute | solution.py:229
  33.4 16.3 %collective-permute-start.8 = (bf16[20,32,256]{2,1,0:T(8,128)(2,1)S(1)}, bf16[20,32,256]{2,1,0:T(8,128)(2,1)S(1)}, u32[]{:S(2)}, u32[]{:S(2)}) collective-permute-start(bf16[20,32,256]{2,1,0:T(8,128)(2,1)S(1)} %collective-permute-done.4.rest_1_), channel_id=1, source_target_pairs={{0,4},{1,5},{2,6},{3,7},{4,0},{5,1},{6,2},{7,3},{8,12},{9,13},{10,... | collective-permute-start | bytes 983048 | tf_op jit(solution)/shard_map/end_left_10/ppermute | solution.py:229
  33.4 4.8 %collective-permute-start.16 = (bf16[12,32,256]{2,1,0:T(8,128)(2,1)S(1)}, bf16[12,32,256]{2,1,0:T(8,128)(2,1)S(1)}, u32[]{:S(2)}, u32[]{:S(2)}) collective-permute-start(bf16[12,32,256]{2,1,0:T(8,128)(2,1)S(1)} %get-tuple-element.74), channel_id=1, source_target_pairs={{0,2},{1,3},{2,0},{3,1},{4,6},{5,7},{6,4},{7,5},{8,10},{9,11},{10,... | collective-permute-start | bytes 589832 | tf_op jit(solution)/shard_map/cross_right_1/ppermute | solution.py:229
  38.2 13.4 %collective-permute-start.19 = (bf16[12,32,256]{2,1,0:T(8,128)(2,1)S(1)}, bf16[12,32,256]{2,1,0:T(8,128)(2,1)S(1)}, u32[]{:S(2)}, u32[]{:S(2)}) collective-permute-start(bf16[12,32,256]{2,1,0:T(8,128)(2,1)S(1)} %collective-permute-done.16.rest_3_), channel_id=1, source_target_pairs={{0,1},{1,0},{2,3},{3,2},{4,8},{5,9},{6,10},{7,11},{8,4},{9,5},{10,... | collective-permute-start | bytes 589832 | tf_op jit(solution)/shard_map/mid_own_11/ppermute | solution.py:229
  41.2 10.4 %collective-permute-start.17 = (bf16[12,32,256]{2,1,0:T(8,128)(2,1)S(1)}, bf16[12,32,256]{2,1,0:T(8,128)(2,1)S(1)}, u32[]{:S(2)}, u32[]{:S(2)}) collective-permute-start(bf16[12,32,256]{2,1,0:T(8,128)(2,1)S(1)} %get-tuple-element.75), channel_id=1, source_target_pairs={{0,2},{1,3},{2,0},{3,1},{4,6},{5,7},{6,4},{7,5},{8,10},{9,11},{10,... | collective-permute-start | bytes 589832 | tf_op jit(solution)/shard_map/cross_left_1/ppermute | solution.py:229
  42.6 11.2 %collective-permute-start.18 = (bf16[12,32,256]{2,1,0:T(8,128)(2,1)S(1)}, bf16[12,32,256]{2,1,0:T(8,128)(2,1)S(1)}, u32[]{:S(2)}, u32[]{:S(2)}) collective-permute-start(bf16[12,32,256]{2,1,0:T(8,128)(2,1)S(1)} %collective-permute-done.16.rest_3_), channel_id=1, source_target_pairs={{0,4},{1,5},{2,6},{3,7},{4,0},{5,1},{6,2},{7,3},{8,12},{9,13},{10,... | collective-permute-start | bytes 589832 | tf_op jit(solution)/shard_map/end_right_11/ppermute | solution.py:229
  50.3 14.6 %collective-permute-start.12 = (bf16[20,64,128]{2,1,0:T(8,128)(2,1)S(1)}, bf16[20,64,128]{2,1,0:T(8,128)(2,1)S(1)}, u32[]{:S(2)}, u32[]{:S(2)}) collective-permute-start(bf16[20,64,128]{2,1,0:T(8,128)(2,1)S(1)} %get-tuple-element.67), channel_id=1, source_target_pairs={{4,0},{5,1},{6,2},{7,3},{8,12},{9,13},{10,14},{11,15},{20,16},{21,... | collective-permute-start | bytes 983048 | tf_op jit(solution)/shard_map/products_back_0/ppermute | solution.py:229
  51.6 12.0 %collective-permute-start.20 = (bf16[12,32,256]{2,1,0:T(8,128)(2,1)S(1)}, bf16[12,32,256]{2,1,0:T(8,128)(2,1)S(1)}, u32[]{:S(2)}, u32[]{:S(2)}) collective-permute-start(bf16[12,32,256]{2,1,0:T(8,128)(2,1)S(1)} %collective-permute-done.17.rest_1_), channel_id=1, source_target_pairs={{0,4},{1,5},{2,6},{3,7},{4,0},{5,1},{6,2},{7,3},{8,12},{9,13},{10,... | collective-permute-start | bytes 589832 | tf_op jit(solution)/shard_map/end_left_11/ppermute | solution.py:229
  53.9 9.8 %collective-permute-start.21 = (bf16[12,32,256]{2,1,0:T(8,128)(2,1)S(1)}, bf16[12,32,256]{2,1,0:T(8,128)(2,1)S(1)}, u32[]{:S(2)}, u32[]{:S(2)}) collective-permute-start(bf16[12,32,256]{2,1,0:T(8,128)(2,1)S(1)} %collective-permute-done.18.rest_5_), channel_id=1, source_target_pairs={{0,1},{1,0},{2,3},{3,2},{4,8},{5,9},{6,10},{7,11},{8,4},{9,5},{10,... | collective-permute-start | bytes 589832 | tf_op jit(solution)/shard_map/mid_next_11/ppermute | solution.py:229
  64.1 6.1 %collective-permute-start.22 = (bf16[12,64,128]{2,1,0:T(8,128)(2,1)S(1)}, bf16[12,64,128]{2,1,0:T(8,128)(2,1)S(1)}, u32[]{:S(2)}, u32[]{:S(2)}) collective-permute-start(bf16[12,64,128]{2,1,0:T(8,128)(2,1)S(1)} %get-tuple-element.82), channel_id=1, source_target_pairs={{0,4},{1,5},{2,6},{3,7},{4,0},{5,1},{6,2},{7,3},{8,12},{9,13},{10,... | collective-permute-start | bytes 589832 | tf_op jit(solution)/shard_map/products_back_1/ppermute | solution.py:229
  64.8 16.8 %copy-start.3 = (bf16[128,128]{1,0:T(8,128)(2,1)S(1)}, bf16[128,128]{1,0:T(8,128)(2,1)}, u32[]{:S(2)}) copy-start(bf16[128,128]{1,0:T(8,128)(2,1)} %weight.5) | copy-start | bytes 98308
  64.8 16.8 %copy-start.6 = (f32[128]{0:T(128)S(1)}, f32[128]{0:T(128)}, u32[]{:S(2)}) copy-start(f32[128]{0:T(128)} %param.12) | copy-start | bytes 1540
  65.0 9.1 %collective-permute-start.13 = (bf16[20,32,128]{2,1,0:T(8,128)(2,1)S(1)}, bf16[20,32,128]{2,1,0:T(8,128)(2,1)S(1)}, u32[]{:S(2)}, u32[]{:S(2)}) collective-permute-start(bf16[20,32,128]{2,1,0:T(8,128)(2,1)S(1)} %get-tuple-element.69), channel_id=1, source_target_pairs={{0,1},{1,0},{2,3},{3,2},{4,5},{5,4},{6,7},{7,6},{8,9},{9,8},{10,11... | collective-permute-start | bytes 491528 | tf_op jit(solution)/shard_map/return_01/ppermute | solution.py:229
  67.9 6.6 %collective-permute-start.14 = (bf16[20,32,128]{2,1,0:T(8,128)(2,1)S(1)}, bf16[20,32,128]{2,1,0:T(8,128)(2,1)S(1)}, u32[]{:S(2)}, u32[]{:S(2)}) collective-permute-start(bf16[20,32,128]{2,1,0:T(8,128)(2,1)S(1)} %get-tuple-element.70), channel_id=1, source_target_pairs={{0,2},{1,3},{2,0},{3,1},{4,6},{5,7},{6,4},{7,5},{8,10},{9,11},{10,... | collective-permute-start | bytes 491528 | tf_op jit(solution)/shard_map/return_02/ppermute | solution.py:229
  69.2 8.6 %collective-permute-start.15 = (bf16[20,32,128]{2,1,0:T(8,128)(2,1)S(1)}, bf16[20,32,128]{2,1,0:T(8,128)(2,1)S(1)}, u32[]{:S(2)}, u32[]{:S(2)}) collective-permute-start(bf16[20,32,128]{2,1,0:T(8,128)(2,1)S(1)} %get-tuple-element.71), channel_id=1, source_target_pairs={{0,3},{1,2},{2,1},{3,0},{4,7},{5,6},{6,5},{7,4},{8,11},{9,10},{10,... | collective-permute-start | bytes 491528 | tf_op jit(solution)/shard_map/return_03/ppermute | solution.py:229
  70.2 7.6 %collective-permute-start.23 = (bf16[12,32,128]{2,1,0:T(8,128)(2,1)S(1)}, bf16[12,32,128]{2,1,0:T(8,128)(2,1)S(1)}, u32[]{:S(2)}, u32[]{:S(2)}) collective-permute-start(bf16[12,32,128]{2,1,0:T(8,128)(2,1)S(1)} %get-tuple-element.84), channel_id=1, source_target_pairs={{0,1},{1,0},{2,3},{3,2},{4,5},{5,4},{6,7},{7,6},{8,9},{9,8},{10,11... | collective-permute-start | bytes 294920 | tf_op jit(solution)/shard_map/return_11/ppermute | solution.py:229
  72.8 6.5 %collective-permute-start.24 = (bf16[12,32,128]{2,1,0:T(8,128)(2,1)S(1)}, bf16[12,32,128]{2,1,0:T(8,128)(2,1)S(1)}, u32[]{:S(2)}, u32[]{:S(2)}) collective-permute-start(bf16[12,32,128]{2,1,0:T(8,128)(2,1)S(1)} %get-tuple-element.85), channel_id=1, source_target_pairs={{0,2},{1,3},{2,0},{3,1},{4,6},{5,7},{6,4},{7,5},{8,10},{9,11},{10,... | collective-permute-start | bytes 294920 | tf_op jit(solution)/shard_map/return_12/ppermute | solution.py:229
  74.1 7.5 %collective-permute-start.25 = (bf16[12,32,128]{2,1,0:T(8,128)(2,1)S(1)}, bf16[12,32,128]{2,1,0:T(8,128)(2,1)S(1)}, u32[]{:S(2)}, u32[]{:S(2)}) collective-permute-start(bf16[12,32,128]{2,1,0:T(8,128)(2,1)S(1)} %get-tuple-element.86), channel_id=1, source_target_pairs={{0,3},{1,2},{2,1},{3,0},{4,7},{5,6},{6,5},{7,4},{8,11},{9,10},{10,... | collective-permute-start | bytes 294920 | tf_op jit(solution)/shard_map/return_13/ppermute | solution.py:229

commit v11 on v10

--- a/solution.py
+++ b/solution.py
@@ -11,7 +11,7 @@
 F32, BF16 = jnp.float32, jnp.bfloat16
 LANES = 128
 SPARE = 6 * 1024 * 1024
-SHARES = (5, 3)
+SHARES = (4, 4)
 NT = (((1,), (1,)), ((), ()))
 TN = (((0,), (0,)), ((), ()))
 VMEM = pl.BlockSpec(memory_space=pltpu.VMEM)
@@ -118,14 +118,16 @@
         out[pl.ds(at * GROUP, GROUP)] = (0.5 * jnp.tanh(0.5 * logits) + 0.5).reshape(GROUP, toks, -1)
 
 
-def product_kernel(mirror, first, n_left, n_right, *rest):
+def product_kernel(mirror, instead, first, n_left, n_right, *rest):
     *refs, held = rest
     planes = [refs[2 * n : 2 * n + 2] for n in range(n_left + n_right)]
     lefts, rights = planes[:n_left], planes[n_left:]
-    outs = refs[2 * (n_left + n_right) :]
-    count, span, _ = outs[0].shape
+    refs = refs[2 * (n_left + n_right) :]
+    other, outs = refs[0], refs[1 if instead else 0 :]
+    count, span, toks = outs[0].shape
     rows = span // 2
     z, y, _ = place()
+    at_end = (z == 0) | (z == 2 * n_right - 1)
     z = 2 * n_right - 1 - z if mirror else z
     for s in range(n_right):
         for p in range(2):
@@ -135,17 +137,25 @@
     for c in range(count):
         left = jnp.concatenate([x for own, other in lefts for x in (own[first + c], other[c])], axis=0)
         out = lax.dot_general(left, held[c], NT, preferred_element_type=F32).astype(BF16)
-        for n in range(n_left):
-            outs[n][c] = out[n * span : (n + 1) * span]
+        outs[0][c] = out[:span]
+        if n_left == 2:
+            outs[1][c, :, :toks] = out[span : span + rows]
+            outs[1][c, :, toks:] = out[span + rows :]
+    if instead:
+
+        @pl.when(at_end)
+        def _():
+            outs[1][...] = other[...]
 
 
 def hand_out_kernel(planes, near, far, end, *outs):
-    _, rows, _ = outs[0].shape
+    _, rows, toks = outs[0].shape
     z, _, core = place()
     at_end = (z == 0) | (z == planes - 1)
     for r in range(4):
         is_near = (core ^ (r % 2)) == z // (planes // 2)
         span = slice((r // 2) * rows, (r // 2 + 1) * rows)
+        lanes = slice((r // 2) * toks, (r // 2 + 1) * toks)
 
         @pl.when(is_near)
         def _():
@@ -157,7 +167,7 @@
 
         @pl.when(jnp.logical_not(is_near) & at_end)
         def _():
-            outs[r][...] = end[:, span, :]
+            outs[r][...] = end[:, :, lanes]
 
 
 def update_kernel(gain, weight, gate, *rest):
@@ -310,41 +320,50 @@
     left1[1] = cross("left_1", left1[1], right1[1], next0[-1])
     own1.append(mid("own_11", right1[1], own1[0]))
     near1.append(end_right("11", right1[1], outer0))
-    next1.append([mid("next_11", x, next1[0][-1], own1[1]) for x in near1[1]])
-    outer1.append(end_left("11", left1[1], outer1[0], own1[1]))
-
-    def products(mirror, first, lefts, rights, name):
+    def products(mirror, first, lefts, rights, name, instead=()):
         span = 2 * rows * len(rights)
         count = lefts[0][1].shape[0]
-        args = [x for arrays in (*lefts, *rights) for x in arrays]
+        args = [x for arrays in (*lefts, *rights) for x in arrays] + [*instead]
+        shapes = [piece(count, 2 * rows, span), piece(count, rows, 2 * span)]
         return kernel(
-            functools.partial(product_kernel, mirror, first, len(lefts), len(rights)),
+            functools.partial(
+                product_kernel, mirror, bool(instead), first, len(lefts), len(rights)
+            ),
             name,
-            [piece(count, 2 * rows, span)] * len(lefts),
+            shapes[: len(lefts)],
             [VMEM] * len(args),
             [pltpu.VMEM((count, span, 2 * toks), BF16)],
         )(*args)
 
-    done, pieces, first = [], [], 0
-    for g in groups:
-        mine = (left0, left1[g])
-        near = list(zip([right0, *near0], [right1[g], *near1[g]]))
-        far = list(zip([own0, *next0], [own1[g], *next1[g]]))
-        (close,) = products(False, first, [mine], near, "near")
-        mine = (after(left0, *done), left1[g])
-        away, ends = products(True, first, [mine, (outer0, outer1[g])], far, "away")
-        ends = send(ends, edge if g == groups[-1] else outward, f"products_back_{g}")
+    def near_planes(g):
+        return list(zip([right0, *near0], [right1[g], *near1[g]]))
+
+    def far_planes(g):
+        return list(zip([own0, *next0], [own1[g], *next1[g]]))
+
+    def hand_out(g, close, away, ends):
         handed = kernel(
             functools.partial(hand_out_kernel, planes),
             "hand_out",
             [piece(counts[g], rows, toks)] * 4,
             [VMEM] * 3,
         )(close, away, ends)
-        done = [away]
-        pieces += [handed[0]] + [
+        return [handed[0]] + [
             send(handed[r], in_plane(r), f"return_{g}{r}") for r in range(1, 4)
         ]
-        first += counts[g]
+
+    close, mine, first = [], [(left0, x) for x in left1], [0, counts[0]]
+    for g in groups:
+        close += products(False, first[g], [mine[g]], near_planes(g), "near")
+    sides = [mine[0], (outer0, outer1[0])]
+    away0, swapped = products(True, first[0], sides, far_planes(0), "away", [left1[1]])
+    next1.append([mid("next_11", x, next1[0][-1], own1[1], away0) for x in near1[1]])
+    swapped = send(swapped, edge, "left_11_and_products_back_0")
+    pieces = hand_out(0, close[0], away0, swapped)
+    sides = [(after(left0, pieces[0]), left1[1]), (outer0, swapped)]
+    away1, ends = products(True, first[1], sides, far_planes(1), "away")
+    ends = send(ends, edge, "products_back_1")
+    pieces += hand_out(1, close[1], away1, ends)
 
     return kernel(
         update_kernel,

time: 84.6 us -> 85.6 us (1.012)
  waiting for transfers between devices: 33.1 us -> 36.9 us
  starting transfers between devices: 34.9 us -> 32 us
    ppermute x26 -> x25, waiting for transfers between devices: 33.1 us -> 36.9 us  [send(): return lax.ppermute(x, ('row', 'chan'), pairs)]
    ppermute x26 -> x25, starting transfers between devices: 34.9 us -> 32 us  [send(): return lax.ppermute(x, ('row', 'chan'), pairs)]
  transfers between devices with their start and end apart: 26 -> 25, of which waited for: 10 -> 12; matrix products, arithmetic and copies ran while one was open for 0% -> 0% of each run, Pallas kernels for 9% -> 8%
where the time goes in v11:
time: 85.6 us; the launch traced here: 85 us
  waiting for transfers between devices  36.9 us (43%)
  starting transfers between devices  32 us (37%)
  Pallas kernels  12.4 us (14%)
  local copies, waits for them, and re-layouts  3.52 us (4%)
    ppermute x25, waiting for transfers between devices, send(): return lax.ppermute(x, ('row', 'chan'), pairs)  36.9 us
    ppermute x25, starting transfers between devices, send(): return lax.ppermute(x, ('row', 'chan'), pairs)  32 us
    pallas_call x11, Pallas kernels, call(): pl.pallas_call(body, out_shape=out_shape, in_specs=in_specs, out_specs=ou...  12.4 us
    unnamed x14, local copies, waits for them, and re-layouts  3.52 us
  transfers between devices with their start and end apart: 25, of which 12 were waited for; matrix products, arithmetic and copies ran while one was open for 0% of the time, Pallas kernels for 8%

profile of v11, /device:TPU:1, one launch (start us, length us, event | category | flops | bytes accessed | tf_op | source)
XLA Modules:
  0.0 85.0 jit_solution(11813891267298982406)
XLA Ops:
  0.0 0.1 collective-permute-start
  0.1 0.5 collective-permute-start.1
  0.5 1.2 %copy-done = bf16[32,128,128]{2,1,0:T(8,128)(2,1)S(1)} copy-done((bf16[32,128,128]{2,1,0:T(8,128)(2,1)S(1)}, bf16[32,128,128]{2,1,0:T(8,128)(2,1)}, u32[]{:S(2)}) %copy-start) | copy-done | bytes 1048600
  1.7 0.9 %copy-done.1 = bf16[128,512]{1,0:T(8,128)(2,1)S(1)} copy-done((bf16[128,512]{1,0:T(8,128)(2,1)S(1)}, bf16[128,512]{1,0:T(8,128)(2,1)}, u32[]{:S(2)}) %copy-start.1) | copy-done | bytes 131096
  2.6 0.7 copy-done.4
  3.4 0.7 copy-done.5
  4.0 2.3 %right_own.1 = (bf16[32,32,128]{2,1,0:T(8,128)(2,1)S(1)}, bf16[16,32,128]{2,1,0:T(8,128)(2,1)S(1)}, bf16[16,32,128]{2,1,0:T(8,128)(2,1)S(1)}, bf16[4096,128]{1,0...) custom-call(bf16[32,128,128]{2,1,0:T(8,128)(2,1)S(1)} %copy-done, ...), custom_call_target="tpu_custom_call" | custom-call | tf_op jit(solution)/shard_map/right_own/pallas_call | solution.py:211
  6.3 0.0 copy-start.2
  6.3 0.0 collective-permute-done.1.mask
  6.3 0.0 collective-permute-done.pair
  6.3 2.3 %right_twin.1 = (bf16[32,32,256]{2,1,0:T(8,128)(2,1)S(1)}, bf16[16,32,256]{2,1,0:T(8,128)(2,1)S(1)}, bf16[16,32,256]{2,1,0:T(8,128)(2,1)S(1)}, bf16[4096,128]{1,0:T(8,128)(2,1)S(1)}, f32[1,32,128]{2,1,0:T(8,128)S(1)}) custom-call(bf16[32,128,128]{2,1,0:T(8,128)(2,1)S(1)} %collective-permute-done.pair, s32[32,128]{1,0:T(8,128)S(1)} %collective-permute-done.1.mask, ...), custom_call_target="tpu_custom_call" | custom-call | tf_op jit(solution)/shard_map/right_twin/pallas_call | solution.py:211
  8.7 0.1 collective-permute-start.3
  8.8 3.5 %collective-permute-start.5 = (bf16[32,32,256]{2,1,0:T(8,128)(2,1)S(1)}, bf16[32,32,256]{2,1,0:T(8,128)(2,1)S(1)}, u32[]{:S(2)}, u32[]{:S(2)}) collective-permute-start(bf16[32,32,256]{2,1,0:T(8,128)(2,1)S(1)} %get-tuple-element.58.rest_2_), channel_id=1, source_target_pairs={{0,4},{1,5},{2,6},{3,7},{4,0},{5,1},{6,2},{7,3},{8,12},{9,13},{10,... | collective-permute-start | bytes 1572872 | tf_op jit(solution)/shard_map/end_right_0/ppermute | solution.py:239
  12.3 1.2 %collective-permute-start.2 = (bf16[16,32,256]{2,1,0:T(8,128)(2,1)S(1)}, bf16[16,32,256]{2,1,0:T(8,128)(2,1)S(1)}, u32[]{:S(2)}, u32[]{:S(2)}) collective-permute-start(bf16[16,32,256]{2,1,0:T(8,128)(2,1)S(1)} %get-tuple-element.57), channel_id=1, source_target_pairs={{0,2},{1,3},{2,0},{3,1},{4,6},{5,7},{6,4},{7,5},{8,10},{9,11},{10,... | collective-permute-start | bytes 786440 | tf_op jit(solution)/shard_map/cross_right_0/ppermute | solution.py:239
  13.6 2.0 %left.1 = (bf16[32,32,256]{2,1,0:T(8,128)(2,1)S(1)}, bf16[16,32,256]{2,1,0:T(8,128)(2,1)S(1)}, bf16[16,32,256]{2,1,0:T(8,128)(2,1)S(1)}) custom-call(bf16[4096,128]{1,0:T(8,128)(2,1)S(1)} %get-tuple-element.45.normed.normed0, bf16[4096,128]{1,0:T(8,128)(2,1)S(1)} %get-tuple-element.51.normed1, f32[1,32,128]{2,1,0:T(8,128)S(1)} %get-tuple-element.52.valid0, ...), custom_call_target="tpu_custom_call" | custom-call | tf_op jit(solution)/shard_map/left/pallas_call | solution.py:211
  15.6 3.5 %collective-permute-done.2.rest_3_ = bf16[16,32,256]{2,1,0:T(8,128)(2,1)S(1)} collective-permute-done((bf16[16,32,256]{2,1,0:T(8,128)(2,1)S(1)}, bf16[16,32,256]{2,1,0:T(8,128)(2,1)S(1)}, u32[]{:S(2)}, u32[]{:S(2)}) %collective-permute-start.2) | collective-permute-done | bytes 262176 | tf_op jit(solution)/shard_map/cross_right_0/ppermute | solution.py:239
  19.0 2.0 %collective-permute-start.9 = (bf16[16,32,256]{2,1,0:T(8,128)(2,1)S(1)}, bf16[16,32,256]{2,1,0:T(8,128)(2,1)S(1)}, u32[]{:S(2)}, u32[]{:S(2)}) collective-permute-start(bf16[16,32,256]{2,1,0:T(8,128)(2,1)S(1)} %collective-permute-done.2.rest_3_), channel_id=1, source_target_pairs={{0,1},{1,0},{2,3},{3,2},{4,8},{5,9},{6,10},{7,11},{8,4},{9,5},{10,... | collective-permute-start | bytes 786440 | tf_op jit(solution)/shard_map/mid_own_10/ppermute | solution.py:239
  21.0 0.0 collective-permute-done.3.rest_4_
  21.0 1.2 %collective-permute-start.4 = (bf16[16,32,256]{2,1,0:T(8,128)(2,1)S(1)}, bf16[16,32,256]{2,1,0:T(8,128)(2,1)S(1)}, u32[]{:S(2)}, u32[]{:S(2)}) collective-permute-start(bf16[16,32,256]{2,1,0:T(8,128)(2,1)S(1)} %get-tuple-element.59), channel_id=1, source_target_pairs={{0,2},{1,3},{2,0},{3,1},{4,6},{5,7},{6,4},{7,5},{8,10},{9,11},{10,... | collective-permute-start | bytes 786440 | tf_op jit(solution)/shard_map/cross_left_0/ppermute | solution.py:239
  22.3 1.5 %collective-permute-done.5.rest_4_ = bf16[32,32,256]{2,1,0:T(8,128)(2,1)S(1)} collective-permute-done((bf16[32,32,256]{2,1,0:T(8,128)(2,1)S(1)}, bf16[32,32,256]{2,1,0:T(8,128)(2,1)S(1)}, u32[]{:S(2)}, u32[]{:S(2)}) %collective-permute-start.5) | collective-permute-done | bytes 524320 | tf_op jit(solution)/shard_map/end_right_0/ppermute | solution.py:239
  23.8 1.4 %collective-permute-start.10 = (bf16[32,32,256]{2,1,0:T(8,128)(2,1)S(1)}, bf16[32,32,256]{2,1,0:T(8,128)(2,1)S(1)}, u32[]{:S(2)}, u32[]{:S(2)}) collective-permute-start(bf16[32,32,256]{2,1,0:T(8,128)(2,1)S(1)} %collective-permute-done.5.rest_4_), channel_id=1, source_target_pairs={{0,1},{1,0},{2,3},{3,2},{4,8},{5,9},{6,10},{7,11},{8,4},{9,5},{10,... | collective-permute-start | bytes 1572872 | tf_op jit(solution)/shard_map/mid_next_0/ppermute | solution.py:239
  25.2 1.4 %collective-permute-start.7 = (bf16[32,32,256]{2,1,0:T(8,128)(2,1)S(1)}, bf16[32,32,256]{2,1,0:T(8,128)(2,1)S(1)}, u32[]{:S(2)}, u32[]{:S(2)}) collective-permute-start(bf16[32,32,256]{2,1,0:T(8,128)(2,1)S(1)} %get-tuple-element.76.rest_0_), channel_id=1, source_target_pairs={{0,4},{1,5},{2,6},{3,7},{4,0},{5,1},{6,2},{7,3},{8,12},{9,13},{10,... | collective-permute-start | bytes 1572872 | tf_op jit(solution)/shard_map/end_left_0/ppermute | solution.py:239
  26.5 0.1 collective-permute-start.6
  26.7 0.0 collective-permute-done.9.rest_5_
  26.7 2.3 %collective-permute-done.4.rest_1_ = bf16[16,32,256]{2,1,0:T(8,128)(2,1)S(1)} collective-permute-done((bf16[16,32,256]{2,1,0:T(8,128)(2,1)S(1)}, bf16[16,32,256]{2,1,0:T(8,128)(2,1)S(1)}, u32[]{:S(2)}, u32[]{:S(2)}) %collective-permute-start.4) | collective-permute-done | bytes 262176 | tf_op jit(solution)/shard_map/cross_left_0/ppermute | solution.py:239
  29.0 1.2 %collective-permute-start.12 = (bf16[16,32,256]{2,1,0:T(8,128)(2,1)S(1)}, bf16[16,32,256]{2,1,0:T(8,128)(2,1)S(1)}, u32[]{:S(2)}, u32[]{:S(2)}) collective-permute-start(bf16[16,32,256]{2,1,0:T(8,128)(2,1)S(1)} %get-tuple-element.67), channel_id=1, source_target_pairs={{0,2},{1,3},{2,0},{3,1},{4,6},{5,7},{6,4},{7,5},{8,10},{9,11},{10,... | collective-permute-start | bytes 786440 | tf_op jit(solution)/shard_map/cross_right_1/ppermute | solution.py:239
  30.2 0.9 %gate.1 = f32[32,128,128]{2,1,0:T(8,128)S(1)} custom-call(bf16[4096,128]{1,0:T(8,128)(2,1)S(1)} %get-tuple-element.45.normed.normed0, bf16[128,128]{1,0:T(8,128)(2,1)S(1)} %copy-done.2), custom_call_target="tpu_custom_call" | custom-call | tf_op jit(solution)/shard_map/gate/pallas_call | solution.py:211
  31.1 10.6 %collective-permute-done.6.rest_5_ = bf16[16,32,256]{2,1,0:T(8,128)(2,1)S(1)} collective-permute-done((bf16[16,32,256]{2,1,0:T(8,128)(2,1)S(1)}, bf16[16,32,256]{2,1,0:T(8,128)(2,1)S(1)}, u32[]{:S(2)}, u32[]{:S(2)}) %collective-permute-start.6) | collective-permute-done | bytes 262176 | tf_op jit(solution)/shard_map/end_right_10/ppermute | solution.py:239
  41.7 3.4 %collective-permute-start.11 = (bf16[16,32,256]{2,1,0:T(8,128)(2,1)S(1)}, bf16[16,32,256]{2,1,0:T(8,128)(2,1)S(1)}, u32[]{:S(2)}, u32[]{:S(2)}) collective-permute-start(bf16[16,32,256]{2,1,0:T(8,128)(2,1)S(1)} %collective-permute-done.6.rest_5_), channel_id=1, source_target_pairs={{0,1},{1,0},{2,3},{3,2},{4,8},{5,9},{6,10},{7,11},{8,4},{9,5},{10,... | collective-permute-start | bytes 786440 | tf_op jit(solution)/shard_map/mid_next_10/ppermute | solution.py:239
  45.2 2.4 %collective-permute-start.19 = (bf16[16,32,256]{2,1,0:T(8,128)(2,1)S(1)}, bf16[16,32,256]{2,1,0:T(8,128)(2,1)S(1)}, u32[]{:S(2)}, u32[]{:S(2)}) collective-permute-start(bf16[16,32,256]{2,1,0:T(8,128)(2,1)S(1)} %collective-permute-done.12.rest_3_), channel_id=1, source_target_pairs={{0,1},{1,0},{2,3},{3,2},{4,8},{5,9},{6,10},{7,11},{8,4},{9,5},{10,... | collective-permute-start | bytes 786440 | tf_op jit(solution)/shard_map/mid_own_11/ppermute | solution.py:239
  47.5 1.2 %collective-permute-start.13 = (bf16[16,32,256]{2,1,0:T(8,128)(2,1)S(1)}, bf16[16,32,256]{2,1,0:T(8,128)(2,1)S(1)}, u32[]{:S(2)}, u32[]{:S(2)}) collective-permute-start(bf16[16,32,256]{2,1,0:T(8,128)(2,1)S(1)} %get-tuple-element.68), channel_id=1, source_target_pairs={{0,2},{1,3},{2,0},{3,1},{4,6},{5,7},{6,4},{7,5},{8,10},{9,11},{10,... | collective-permute-start | bytes 786440 | tf_op jit(solution)/shard_map/cross_left_1/ppermute | solution.py:239
  48.8 0.0 collective-permute-done.7.rest_2_
  48.8 0.9 %collective-permute-start.18 = (bf16[16,32,256]{2,1,0:T(8,128)(2,1)S(1)}, bf16[16,32,256]{2,1,0:T(8,128)(2,1)S(1)}, u32[]{:S(2)}, u32[]{:S(2)}) collective-permute-start(bf16[16,32,256]{2,1,0:T(8,128)(2,1)S(1)} %collective-permute-done.12.rest_3_), channel_id=1, source_target_pairs={{0,4},{1,5},{2,6},{3,7},{4,0},{5,1},{6,2},{7,3},{8,12},{9,13},{10,... | collective-permute-start | bytes 786440 | tf_op jit(solution)/shard_map/end_right_11/ppermute | solution.py:239
  49.7 0.0 collective-permute-done.11.rest_7_
  49.7 3.0 %collective-permute-done.8.rest_3_ = bf16[16,32,256]{2,1,0:T(8,128)(2,1)S(1)} collective-permute-done((bf16[16,32,256]{2,1,0:T(8,128)(2,1)S(1)}, bf16[16,32,256]{2,1,0:T(8,128)(2,1)S(1)}, u32[]{:S(2)}, u32[]{:S(2)}) %collective-permute-start.8) | collective-permute-done | bytes 262176 | tf_op jit(solution)/shard_map/end_left_10/ppermute | solution.py:239
  52.7 2.7 %collective-permute-done.13.rest_8_.rest_1_ = bf16[16,32,256]{2,1,0:T(8,128)(2,1)S(1)} collective-permute-done((bf16[16,32,256]{2,1,0:T(8,128)(2,1)S(1)}, bf16[16,32,256]{2,1,0:T(8,128)(2,1)S(1)}, u32[]{:S(2)}, u32[]{:S(2)}) %collective-permute-start.13) | collective-permute-done | bytes 262176 | tf_op jit(solution)/shard_map/cross_left_1/ppermute | solution.py:239
  55.4 0.5 away.2
  55.9 0.4 collective-permute-start.14
  56.3 0.0 collective-permute-done.19.rest_5_
  56.3 2.0 %collective-permute-done.18.rest_5_ = bf16[16,32,256]{2,1,0:T(8,128)(2,1)S(1)} collective-permute-done((bf16[16,32,256]{2,1,0:T(8,128)(2,1)S(1)}, bf16[16,32,256]{2,1,0:T(8,128)(2,1)S(1)}, u32[]{:S(2)}, u32[]{:S(2)}) %collective-permute-start.18) | collective-permute-done | bytes 262176 | tf_op jit(solution)/shard_map/end_right_11/ppermute | solution.py:239
  58.3 1.5 %collective-permute-start.20 = (bf16[16,32,256]{2,1,0:T(8,128)(2,1)S(1)}, bf16[16,32,256]{2,1,0:T(8,128)(2,1)S(1)}, u32[]{:S(2)}, u32[]{:S(2)}) collective-permute-start(bf16[16,32,256]{2,1,0:T(8,128)(2,1)S(1)} %collective-permute-done.18.rest_5_), channel_id=1, source_target_pairs={{0,1},{1,0},{2,3},{3,2},{4,8},{5,9},{6,10},{7,11},{8,4},{9,5},{10,... | collective-permute-start | bytes 786440 | tf_op jit(solution)/shard_map/mid_next_11/ppermute | solution.py:239
  59.8 0.6 near.2
  60.4 3.4 %collective-permute-done.14.end.rest_3_ = bf16[16,32,256]{2,1,0:T(8,128)(2,1)S(1)} collective-permute-done((bf16[16,32,256]{2,1,0:T(8,128)(2,1)S(1)}, bf16[16,32,256]{2,1,0:T(8,128)(2,1)S(1)}, u32[]{:S(2)}, u32[]{:S(2)}) %collective-permute-start.14) | collective-permute-done | bytes 262176 | tf_op jit(solution)/shard_map/left_11_and_products_back_0/ppermute | solution.py:239
  63.7 0.1 hand_out.2
  63.8 0.0 collective-permute-done.20.rest_7_
  63.8 0.5 away.3
  64.4 0.0 copy-start.3
  64.4 0.0 copy-start.6
  64.4 0.1 collective-permute-start.21
  64.5 3.5 %collective-permute-start.15 = (bf16[16,32,128]{2,1,0:T(8,128)(2,1)S(1)}, bf16[16,32,128]{2,1,0:T(8,128)(2,1)S(1)}, u32[]{:S(2)}, u32[]{:S(2)}) collective-permute-start(bf16[16,32,128]{2,1,0:T(8,128)(2,1)S(1)} %get-tuple-element.72), channel_id=1, source_target_pairs={{0,1},{1,0},{2,3},{3,2},{4,5},{5,4},{6,7},{7,6},{8,9},{9,8},{10,11... | collective-permute-start | bytes 393224 | tf_op jit(solution)/shard_map/return_01/ppermute | solution.py:239
  68.0 0.6 near.3
  68.5 1.7 %collective-permute-start.16 = (bf16[16,32,128]{2,1,0:T(8,128)(2,1)S(1)}, bf16[16,32,128]{2,1,0:T(8,128)(2,1)S(1)}, u32[]{:S(2)}, u32[]{:S(2)}) collective-permute-start(bf16[16,32,128]{2,1,0:T(8,128)(2,1)S(1)} %get-tuple-element.73), channel_id=1, source_target_pairs={{0,2},{1,3},{2,0},{3,1},{4,6},{5,7},{6,4},{7,5},{8,10},{9,11},{10,... | collective-permute-start | bytes 393224 | tf_op jit(solution)/shard_map/return_02/ppermute | solution.py:239
  70.3 0.5 collective-permute-done.21.end
  70.8 0.1 hand_out.3
  70.9 2.5 %collective-permute-start.22 = (bf16[16,32,128]{2,1,0:T(8,128)(2,1)S(1)}, bf16[16,32,128]{2,1,0:T(8,128)(2,1)S(1)}, u32[]{:S(2)}, u32[]{:S(2)}) collective-permute-start(bf16[16,32,128]{2,1,0:T(8,128)(2,1)S(1)} %get-tuple-element.82), channel_id=1, source_target_pairs={{0,1},{1,0},{2,3},{3,2},{4,5},{5,4},{6,7},{7,6},{8,9},{9,8},{10,11... | collective-permute-start | bytes 393224 | tf_op jit(solution)/shard_map/return_11/ppermute | solution.py:239
  73.4 1.3 %collective-permute-start.23 = (bf16[16,32,128]{2,1,0:T(8,128)(2,1)S(1)}, bf16[16,32,128]{2,1,0:T(8,128)(2,1)S(1)}, u32[]{:S(2)}, u32[]{:S(2)}) collective-permute-start(bf16[16,32,128]{2,1,0:T(8,128)(2,1)S(1)} %get-tuple-element.83), channel_id=1, source_target_pairs={{0,2},{1,3},{2,0},{3,1},{4,6},{5,7},{6,4},{7,5},{8,10},{9,11},{10,... | collective-permute-start | bytes 393224 | tf_op jit(solution)/shard_map/return_12/ppermute | solution.py:239
  74.6 0.0 collective-permute-done.15.rest_1_
  74.6 0.5 collective-permute-start.24
  75.1 0.0 collective-permute-done.16.rest_2_
  75.1 2.0 %collective-permute-done.17.rest_3_ = bf16[16,32,128]{2,1,0:T(8,128)(2,1)S(1)} collective-permute-done((bf16[16,32,128]{2,1,0:T(8,128)(2,1)S(1)}, bf16[16,32,128]{2,1,0:T(8,128)(2,1)S(1)}, u32[]{:S(2)}, u32[]{:S(2)}) %collective-permute-start.17) | collective-permute-done | bytes 131104 | tf_op jit(solution)/shard_map/return_03/ppermute | solution.py:239
  77.1 0.0 collective-permute-done.22.rest_5_
  77.1 2.6 %collective-permute-done.23.rest_6_ = bf16[16,32,128]{2,1,0:T(8,128)(2,1)S(1)} collective-permute-done((bf16[16,32,128]{2,1,0:T(8,128)(2,1)S(1)}, bf16[16,32,128]{2,1,0:T(8,128)(2,1)S(1)}, u32[]{:S(2)}, u32[]{:S(2)}) %collective-permute-start.23) | collective-permute-done | bytes 131104 | tf_op jit(solution)/shard_map/return_12/ppermute | solution.py:239
  79.7 2.8 %collective-permute-done.24.rest_7_ = bf16[16,32,128]{2,1,0:T(8,128)(2,1)S(1)} collective-permute-done((bf16[16,32,128]{2,1,0:T(8,128)(2,1)S(1)}, bf16[16,32,128]{2,1,0:T(8,128)(2,1)S(1)}, u32[]{:S(2)}, u32[]{:S(2)}) %collective-permute-start.24) | collective-permute-done | bytes 131104 | tf_op jit(solution)/shard_map/return_13/ppermute | solution.py:239
  82.5 2.5 %update.1 = bf16[32,128,128]{2,1,0:T(8,128)(2,1)} custom-call(f32[1,128]{1,0:T(1,128)S(1)} %bitcast.3, bf16[128,128]{1,0:T(8,128)(2,1)S(1)} %copy-done.3, f32[32,128,128]{2,1,0:T(8,128)S(1)} %gate.1, bf16[16,32,128]{2,1,0:T(8,128)(2,1)S(1)} %get-tuple-element.71.rest_0_, bf16[16,32,128]{2,1,0:T(8,128)(2,1)S(1)} %collective-permute-done.15.rest_1_, ...), custom_call_target="tpu_custom_call" | custom-call | tf_op jit(solution)/shard_map/update/pallas_call | solution.py:211
  (11 shorter events, 0.0 us)
Async XLA Ops:
  0.0 6.3 %collective-permute-start = (bf16[32,128,128]{2,1,0:T(8,128)(2,1)}, bf16[32,128,128]{2,1,0:T(8,128)(2,1)S(1)}, u32[]{:S(2)}, u32[]{:S(2)}) collective-permute-start(bf16[32,128,128]{2,1,0:T(8,128)(2,1)} %pair.1), channel_id=1, source_target_pairs={{0,1},{1,0},{2,3},{3,2},{4,5},{5,4},{6,7},{7,6},{8,9},{9,8},{10,11... | collective-permute-start | bytes 3145736 | tf_op jit(solution)/shard_map/pair/ppermute | solution.py:239
  0.1 6.3 %collective-permute-start.1 = (s32[32,128]{1,0:T(8,128)}, s32[32,128]{1,0:T(8,128)S(1)}, u32[]{:S(2)}, u32[]{:S(2)}) collective-permute-start(s32[32,128]{1,0:T(8,128)} %mask.1), channel_id=1, source_target_pairs={{0,1},{1,0},{2,3},{3,2},{4,5},{5,4},{6,7},{7,6},{8,9},{9,8},{10,11... | collective-permute-start | bytes 49160 | tf_op jit(solution)/shard_map/mask/ppermute | solution.py:239
  0.5 1.2 %copy-start = (bf16[32,128,128]{2,1,0:T(8,128)(2,1)S(1)}, bf16[32,128,128]{2,1,0:T(8,128)(2,1)}, u32[]{:S(2)}) copy-start(bf16[32,128,128]{2,1,0:T(8,128)(2,1)} %pair.1) | copy-start | bytes 3145732
  1.7 0.9 %copy-start.1 = (bf16[128,512]{1,0:T(8,128)(2,1)S(1)}, bf16[128,512]{1,0:T(8,128)(2,1)}, u32[]{:S(2)}) copy-start(bf16[128,512]{1,0:T(8,128)(2,1)} %weight.3) | copy-start | bytes 393220
  2.6 0.7 copy-start.4
  3.4 0.7 copy-start.5
  6.3 23.9 %copy-start.2 = (bf16[128,128]{1,0:T(8,128)(2,1)S(1)}, bf16[128,128]{1,0:T(8,128)(2,1)}, u32[]{:S(2)}) copy-start(bf16[128,128]{1,0:T(8,128)(2,1)} %weight.4) | copy-start | bytes 98308
  8.7 12.4 %collective-permute-start.3 = (bf16[32,32,256]{2,1,0:T(8,128)(2,1)S(1)}, bf16[32,32,256]{2,1,0:T(8,128)(2,1)S(1)}, u32[]{:S(2)}, u32[]{:S(2)}) collective-permute-start(bf16[32,32,256]{2,1,0:T(8,128)(2,1)S(1)} %get-tuple-element.58.rest_2_), channel_id=1, source_target_pairs={{0,1},{1,0},{2,3},{3,2},{4,8},{5,9},{6,10},{7,11},{8,4},{9,5},{10,... | collective-permute-start | bytes 1572872 | tf_op jit(solution)/shard_map/mid_own_0/ppermute | solution.py:239
  8.8 15.0 %collective-permute-start.5 = (bf16[32,32,256]{2,1,0:T(8,128)(2,1)S(1)}, bf16[32,32,256]{2,1,0:T(8,128)(2,1)S(1)}, u32[]{:S(2)}, u32[]{:S(2)}) collective-permute-start(bf16[32,32,256]{2,1,0:T(8,128)(2,1)S(1)} %get-tuple-element.58.rest_2_), channel_id=1, source_target_pairs={{0,4},{1,5},{2,6},{3,7},{4,0},{5,1},{6,2},{7,3},{8,12},{9,13},{10,... | collective-permute-start | bytes 1572872 | tf_op jit(solution)/shard_map/end_right_0/ppermute | solution.py:239
  12.3 6.7 %collective-permute-start.2 = (bf16[16,32,256]{2,1,0:T(8,128)(2,1)S(1)}, bf16[16,32,256]{2,1,0:T(8,128)(2,1)S(1)}, u32[]{:S(2)}, u32[]{:S(2)}) collective-permute-start(bf16[16,32,256]{2,1,0:T(8,128)(2,1)S(1)} %get-tuple-element.57), channel_id=1, source_target_pairs={{0,2},{1,3},{2,0},{3,1},{4,6},{5,7},{6,4},{7,5},{8,10},{9,11},{10,... | collective-permute-start | bytes 786440 | tf_op jit(solution)/shard_map/cross_right_0/ppermute | solution.py:239
  19.0 7.6 %collective-permute-start.9 = (bf16[16,32,256]{2,1,0:T(8,128)(2,1)S(1)}, bf16[16,32,256]{2,1,0:T(8,128)(2,1)S(1)}, u32[]{:S(2)}, u32[]{:S(2)}) collective-permute-start(bf16[16,32,256]{2,1,0:T(8,128)(2,1)S(1)} %collective-permute-done.2.rest_3_), channel_id=1, source_target_pairs={{0,1},{1,0},{2,3},{3,2},{4,8},{5,9},{6,10},{7,11},{8,4},{9,5},{10,... | collective-permute-start | bytes 786440 | tf_op jit(solution)/shard_map/mid_own_10/ppermute | solution.py:239
  21.0 7.9 %collective-permute-start.4 = (bf16[16,32,256]{2,1,0:T(8,128)(2,1)S(1)}, bf16[16,32,256]{2,1,0:T(8,128)(2,1)S(1)}, u32[]{:S(2)}, u32[]{:S(2)}) collective-permute-start(bf16[16,32,256]{2,1,0:T(8,128)(2,1)S(1)} %get-tuple-element.59), channel_id=1, source_target_pairs={{0,2},{1,3},{2,0},{3,1},{4,6},{5,7},{6,4},{7,5},{8,10},{9,11},{10,... | collective-permute-start | bytes 786440 | tf_op jit(solution)/shard_map/cross_left_0/ppermute | solution.py:239
  23.8 23.7 %collective-permute-start.10 = (bf16[32,32,256]{2,1,0:T(8,128)(2,1)S(1)}, bf16[32,32,256]{2,1,0:T(8,128)(2,1)S(1)}, u32[]{:S(2)}, u32[]{:S(2)}) collective-permute-start(bf16[32,32,256]{2,1,0:T(8,128)(2,1)S(1)} %collective-permute-done.5.rest_4_), channel_id=1, source_target_pairs={{0,1},{1,0},{2,3},{3,2},{4,8},{5,9},{6,10},{7,11},{8,4},{9,5},{10,... | collective-permute-start | bytes 1572872 | tf_op jit(solution)/shard_map/mid_next_0/ppermute | solution.py:239
  25.2 23.6 %collective-permute-start.7 = (bf16[32,32,256]{2,1,0:T(8,128)(2,1)S(1)}, bf16[32,32,256]{2,1,0:T(8,128)(2,1)S(1)}, u32[]{:S(2)}, u32[]{:S(2)}) collective-permute-start(bf16[32,32,256]{2,1,0:T(8,128)(2,1)S(1)} %get-tuple-element.76.rest_0_), channel_id=1, source_target_pairs={{0,4},{1,5},{2,6},{3,7},{4,0},{5,1},{6,2},{7,3},{8,12},{9,13},{10,... | collective-permute-start | bytes 1572872 | tf_op jit(solution)/shard_map/end_left_0/ppermute | solution.py:239
  26.5 15.2 %collective-permute-start.6 = (bf16[16,32,256]{2,1,0:T(8,128)(2,1)S(1)}, bf16[16,32,256]{2,1,0:T(8,128)(2,1)S(1)}, u32[]{:S(2)}, u32[]{:S(2)}) collective-permute-start(bf16[16,32,256]{2,1,0:T(8,128)(2,1)S(1)} %collective-permute-done.2.rest_3_), channel_id=1, source_target_pairs={{0,4},{1,5},{2,6},{3,7},{4,0},{5,1},{6,2},{7,3},{8,12},{9,13},{10,... | collective-permute-start | bytes 786440 | tf_op jit(solution)/shard_map/end_right_10/ppermute | solution.py:239
  29.0 16.2 %collective-permute-start.12 = (bf16[16,32,256]{2,1,0:T(8,128)(2,1)S(1)}, bf16[16,32,256]{2,1,0:T(8,128)(2,1)S(1)}, u32[]{:S(2)}, u32[]{:S(2)}) collective-permute-start(bf16[16,32,256]{2,1,0:T(8,128)(2,1)S(1)} %get-tuple-element.67), channel_id=1, source_target_pairs={{0,2},{1,3},{2,0},{3,1},{4,6},{5,7},{6,4},{7,5},{8,10},{9,11},{10,... | collective-permute-start | bytes 786440 | tf_op jit(solution)/shard_map/cross_right_1/ppermute | solution.py:239
  41.7 7.9 %collective-permute-start.11 = (bf16[16,32,256]{2,1,0:T(8,128)(2,1)S(1)}, bf16[16,32,256]{2,1,0:T(8,128)(2,1)S(1)}, u32[]{:S(2)}, u32[]{:S(2)}) collective-permute-start(bf16[16,32,256]{2,1,0:T(8,128)(2,1)S(1)} %collective-permute-done.6.rest_5_), channel_id=1, source_target_pairs={{0,1},{1,0},{2,3},{3,2},{4,8},{5,9},{6,10},{7,11},{8,4},{9,5},{10,... | collective-permute-start | bytes 786440 | tf_op jit(solution)/shard_map/mid_next_10/ppermute | solution.py:239
  45.2 7.5 %collective-permute-start.8 = (bf16[16,32,256]{2,1,0:T(8,128)(2,1)S(1)}, bf16[16,32,256]{2,1,0:T(8,128)(2,1)S(1)}, u32[]{:S(2)}, u32[]{:S(2)}) collective-permute-start(bf16[16,32,256]{2,1,0:T(8,128)(2,1)S(1)} %collective-permute-done.4.rest_1_), channel_id=1, source_target_pairs={{0,4},{1,5},{2,6},{3,7},{4,0},{5,1},{6,2},{7,3},{8,12},{9,13},{10,... | collective-permute-start | bytes 786440 | tf_op jit(solution)/shard_map/end_left_10/ppermute | solution.py:239
  45.2 11.2 %collective-permute-start.19 = (bf16[16,32,256]{2,1,0:T(8,128)(2,1)S(1)}, bf16[16,32,256]{2,1,0:T(8,128)(2,1)S(1)}, u32[]{:S(2)}, u32[]{:S(2)}) collective-permute-start(bf16[16,32,256]{2,1,0:T(8,128)(2,1)S(1)} %collective-permute-done.12.rest_3_), channel_id=1, source_target_pairs={{0,1},{1,0},{2,3},{3,2},{4,8},{5,9},{6,10},{7,11},{8,4},{9,5},{10,... | collective-permute-start | bytes 786440 | tf_op jit(solution)/shard_map/mid_own_11/ppermute | solution.py:239
  47.5 7.9 %collective-permute-start.13 = (bf16[16,32,256]{2,1,0:T(8,128)(2,1)S(1)}, bf16[16,32,256]{2,1,0:T(8,128)(2,1)S(1)}, u32[]{:S(2)}, u32[]{:S(2)}) collective-permute-start(bf16[16,32,256]{2,1,0:T(8,128)(2,1)S(1)} %get-tuple-element.68), channel_id=1, source_target_pairs={{0,2},{1,3},{2,0},{3,1},{4,6},{5,7},{6,4},{7,5},{8,10},{9,11},{10,... | collective-permute-start | bytes 786440 | tf_op jit(solution)/shard_map/cross_left_1/ppermute | solution.py:239
  48.8 9.5 %collective-permute-start.18 = (bf16[16,32,256]{2,1,0:T(8,128)(2,1)S(1)}, bf16[16,32,256]{2,1,0:T(8,128)(2,1)S(1)}, u32[]{:S(2)}, u32[]{:S(2)}) collective-permute-start(bf16[16,32,256]{2,1,0:T(8,128)(2,1)S(1)} %collective-permute-done.12.rest_3_), channel_id=1, source_target_pairs={{0,4},{1,5},{2,6},{3,7},{4,0},{5,1},{6,2},{7,3},{8,12},{9,13},{10,... | collective-permute-start | bytes 786440 | tf_op jit(solution)/shard_map/end_right_11/ppermute | solution.py:239
  55.9 7.8 %collective-permute-start.14 = (bf16[16,32,256]{2,1,0:T(8,128)(2,1)S(1)}, bf16[16,32,256]{2,1,0:T(8,128)(2,1)S(1)}, u32[]{:S(2)}, u32[]{:S(2)}) collective-permute-start(bf16[16,32,256]{2,1,0:T(8,128)(2,1)S(1)} %get-tuple-element.70), channel_id=1, source_target_pairs={{0,4},{1,5},{2,6},{3,7},{4,0},{5,1},{6,2},{7,3},{8,12},{9,13},{10,... | collective-permute-start | bytes 786440 | tf_op jit(solution)/shard_map/left_11_and_products_back_0/ppermute | solution.py:239
  58.3 5.5 %collective-permute-start.20 = (bf16[16,32,256]{2,1,0:T(8,128)(2,1)S(1)}, bf16[16,32,256]{2,1,0:T(8,128)(2,1)S(1)}, u32[]{:S(2)}, u32[]{:S(2)}) collective-permute-start(bf16[16,32,256]{2,1,0:T(8,128)(2,1)S(1)} %collective-permute-done.18.rest_5_), channel_id=1, source_target_pairs={{0,1},{1,0},{2,3},{3,2},{4,8},{5,9},{6,10},{7,11},{8,4},{9,5},{10,... | collective-permute-start | bytes 786440 | tf_op jit(solution)/shard_map/mid_next_11/ppermute | solution.py:239
  64.4 18.1 %copy-start.3 = (bf16[128,128]{1,0:T(8,128)(2,1)S(1)}, bf16[128,128]{1,0:T(8,128)(2,1)}, u32[]{:S(2)}) copy-start(bf16[128,128]{1,0:T(8,128)(2,1)} %weight.5) | copy-start | bytes 98308
  64.4 18.1 %copy-start.6 = (f32[128]{0:T(128)S(1)}, f32[128]{0:T(128)}, u32[]{:S(2)}) copy-start(f32[128]{0:T(128)} %param.12) | copy-start | bytes 1540
  64.4 6.4 %collective-permute-start.21 = (bf16[16,32,256]{2,1,0:T(8,128)(2,1)S(1)}, bf16[16,32,256]{2,1,0:T(8,128)(2,1)S(1)}, u32[]{:S(2)}, u32[]{:S(2)}) collective-permute-start(bf16[16,32,256]{2,1,0:T(8,128)(2,1)S(1)} %get-tuple-element.80), channel_id=1, source_target_pairs={{0,4},{1,5},{2,6},{3,7},{4,0},{5,1},{6,2},{7,3},{8,12},{9,13},{10,... | collective-permute-start | bytes 786440 | tf_op jit(solution)/shard_map/products_back_1/ppermute | solution.py:239
  64.5 10.1 %collective-permute-start.15 = (bf16[16,32,128]{2,1,0:T(8,128)(2,1)S(1)}, bf16[16,32,128]{2,1,0:T(8,128)(2,1)S(1)}, u32[]{:S(2)}, u32[]{:S(2)}) collective-permute-start(bf16[16,32,128]{2,1,0:T(8,128)(2,1)S(1)} %get-tuple-element.72), channel_id=1, source_target_pairs={{0,1},{1,0},{2,3},{3,2},{4,5},{5,4},{6,7},{7,6},{8,9},{9,8},{10,11... | collective-permute-start | bytes 393224 | tf_op jit(solution)/shard_map/return_01/ppermute | solution.py:239
  68.5 6.5 %collective-permute-start.16 = (bf16[16,32,128]{2,1,0:T(8,128)(2,1)S(1)}, bf16[16,32,128]{2,1,0:T(8,128)(2,1)S(1)}, u32[]{:S(2)}, u32[]{:S(2)}) collective-permute-start(bf16[16,32,128]{2,1,0:T(8,128)(2,1)S(1)} %get-tuple-element.73), channel_id=1, source_target_pairs={{0,2},{1,3},{2,0},{3,1},{4,6},{5,7},{6,4},{7,5},{8,10},{9,11},{10,... | collective-permute-start | bytes 393224 | tf_op jit(solution)/shard_map/return_02/ppermute | solution.py:239
  70.3 6.8 %collective-permute-start.17 = (bf16[16,32,128]{2,1,0:T(8,128)(2,1)S(1)}, bf16[16,32,128]{2,1,0:T(8,128)(2,1)S(1)}, u32[]{:S(2)}, u32[]{:S(2)}) collective-permute-start(bf16[16,32,128]{2,1,0:T(8,128)(2,1)S(1)} %get-tuple-element.74), channel_id=1, source_target_pairs={{0,3},{1,2},{2,1},{3,0},{4,7},{5,6},{6,5},{7,4},{8,11},{9,10},{10,... | collective-permute-start | bytes 393224 | tf_op jit(solution)/shard_map/return_03/ppermute | solution.py:239
  70.9 6.2 %collective-permute-start.22 = (bf16[16,32,128]{2,1,0:T(8,128)(2,1)S(1)}, bf16[16,32,128]{2,1,0:T(8,128)(2,1)S(1)}, u32[]{:S(2)}, u32[]{:S(2)}) collective-permute-start(bf16[16,32,128]{2,1,0:T(8,128)(2,1)S(1)} %get-tuple-element.82), channel_id=1, source_target_pairs={{0,1},{1,0},{2,3},{3,2},{4,5},{5,4},{6,7},{7,6},{8,9},{9,8},{10,11... | collective-permute-start | bytes 393224 | tf_op jit(solution)/shard_map/return_11/ppermute | solution.py:239
  73.4 6.3 %collective-permute-start.23 = (bf16[16,32,128]{2,1,0:T(8,128)(2,1)S(1)}, bf16[16,32,128]{2,1,0:T(8,128)(2,1)S(1)}, u32[]{:S(2)}, u32[]{:S(2)}) collective-permute-start(bf16[16,32,128]{2,1,0:T(8,128)(2,1)S(1)} %get-tuple-element.83), channel_id=1, source_target_pairs={{0,2},{1,3},{2,0},{3,1},{4,6},{5,7},{6,4},{7,5},{8,10},{9,11},{10,... | collective-permute-start | bytes 393224 | tf_op jit(solution)/shard_map/return_12/ppermute | solution.py:239
  74.6 7.9 %collective-permute-start.24 = (bf16[16,32,128]{2,1,0:T(8,128)(2,1)S(1)}, bf16[16,32,128]{2,1,0:T(8,128)(2,1)S(1)}, u32[]{:S(2)}, u32[]{:S(2)}) collective-permute-start(bf16[16,32,128]{2,1,0:T(8,128)(2,1)S(1)} %get-tuple-element.84), channel_id=1, source_target_pairs={{0,3},{1,2},{2,1},{3,0},{4,7},{5,6},{6,5},{7,4},{8,11},{9,10},{10,... | collective-permute-start | bytes 393224 | tf_op jit(solution)/shard_map/return_13/ppermute | solution.py:239

commit v12 on v11

--- a/solution.py
+++ b/solution.py
@@ -314,7 +314,7 @@
     left1[0] = cross("left_0", left1[0], crossed, own0)
     next0 = [mid("next_0", x, own0) for x in near0]
     outer0 = end_left("0", left0, own0)
-    right1[1] = cross("right_1", right1[1], left1[0], own1[0])
+    right1[1] = cross("right_1", right1[1], left1[0], own1[0], near1[0][-1])
     next1 = [[mid("next_10", x, own1[0], gate) for x in near1[0]]]
     outer1 = [end_left("10", left1[0], near1[0][-1])]
     left1[1] = cross("left_1", left1[1], right1[1], next0[-1])

time: 85.6 us -> 80.6 us (0.942)
  waiting for transfers between devices: 36.9 us -> 28.1 us
  starting transfers between devices: 32 us -> 36 us
    ppermute x25, waiting for transfers between devices: 36.9 us -> 28.1 us  [send(): return lax.ppermute(x, ('row', 'chan'), pairs)]
    ppermute x25, starting transfers between devices: 32 us -> 36 us  [send(): return lax.ppermute(x, ('row', 'chan'), pairs)]
  transfers between devices with their start and end apart: 25 -> 25, of which waited for: 12 -> 11; matrix products, arithmetic and copies ran while one was open for 0% -> 0% of each run, Pallas kernels for 8% -> 9%
where the time goes in v12:
time: 80.6 us; the launch traced here: 80.1 us
  starting transfers between devices  36 us (45%)
  waiting for transfers between devices  28.1 us (35%)
  Pallas kernels  12.4 us (15%)
  local copies, waits for them, and re-layouts  3.52 us (4%)
    ppermute x25, starting transfers between devices, send(): return lax.ppermute(x, ('row', 'chan'), pairs)  36 us
    ppermute x25, waiting for transfers between devices, send(): return lax.ppermute(x, ('row', 'chan'), pairs)  28.1 us
    pallas_call x11, Pallas kernels, call(): pl.pallas_call(body, out_shape=out_shape, in_specs=in_specs, out_specs=ou...  12.4 us
    unnamed x14, local copies, waits for them, and re-layouts  3.52 us
  transfers between devices with their start and end apart: 25, of which 11 were waited for; matrix products, arithmetic and copies ran while one was open for 0% of the time, Pallas kernels for 9%

profile of v12, /device:TPU:1, one launch (start us, length us, event | category | flops | bytes accessed | tf_op | source)
XLA Modules:
  0.0 80.1 jit_solution(16529018541387279222)
XLA Ops:
  0.0 0.1 collective-permute-start
  0.1 0.5 collective-permute-start.1
  0.5 1.2 %copy-done = bf16[32,128,128]{2,1,0:T(8,128)(2,1)S(1)} copy-done((bf16[32,128,128]{2,1,0:T(8,128)(2,1)S(1)}, bf16[32,128,128]{2,1,0:T(8,128)(2,1)}, u32[]{:S(2)}) %copy-start) | copy-done | bytes 1048600
  1.7 0.9 %copy-done.1 = bf16[128,512]{1,0:T(8,128)(2,1)S(1)} copy-done((bf16[128,512]{1,0:T(8,128)(2,1)S(1)}, bf16[128,512]{1,0:T(8,128)(2,1)}, u32[]{:S(2)}) %copy-start.1) | copy-done | bytes 131096
  2.6 0.7 copy-done.4
  3.4 0.7 copy-done.5
  4.0 2.3 %right_own.1 = (bf16[32,32,128]{2,1,0:T(8,128)(2,1)S(1)}, bf16[16,32,128]{2,1,0:T(8,128)(2,1)S(1)}, bf16[16,32,128]{2,1,0:T(8,128)(2,1)S(1)}, bf16[4096,128]{1,0...) custom-call(bf16[32,128,128]{2,1,0:T(8,128)(2,1)S(1)} %copy-done, ...), custom_call_target="tpu_custom_call" | custom-call | tf_op jit(solution)/shard_map/right_own/pallas_call | solution.py:211
  6.3 0.0 copy-start.2
  6.3 0.0 collective-permute-done.1.mask
  6.3 0.0 collective-permute-done.pair
  6.3 2.3 %right_twin.1 = (bf16[32,32,256]{2,1,0:T(8,128)(2,1)S(1)}, bf16[16,32,256]{2,1,0:T(8,128)(2,1)S(1)}, bf16[16,32,256]{2,1,0:T(8,128)(2,1)S(1)}, bf16[4096,128]{1,0:T(8,128)(2,1)S(1)}, f32[1,32,128]{2,1,0:T(8,128)S(1)}) custom-call(bf16[32,128,128]{2,1,0:T(8,128)(2,1)S(1)} %collective-permute-done.pair, s32[32,128]{1,0:T(8,128)S(1)} %collective-permute-done.1.mask, ...), custom_call_target="tpu_custom_call" | custom-call | tf_op jit(solution)/shard_map/right_twin/pallas_call | solution.py:211
  8.7 0.1 collective-permute-start.3
  8.8 3.5 %collective-permute-start.5 = (bf16[32,32,256]{2,1,0:T(8,128)(2,1)S(1)}, bf16[32,32,256]{2,1,0:T(8,128)(2,1)S(1)}, u32[]{:S(2)}, u32[]{:S(2)}) collective-permute-start(bf16[32,32,256]{2,1,0:T(8,128)(2,1)S(1)} %get-tuple-element.58.rest_2_), channel_id=1, source_target_pairs={{0,4},{1,5},{2,6},{3,7},{4,0},{5,1},{6,2},{7,3},{8,12},{9,13},{10,... | collective-permute-start | bytes 1572872 | tf_op jit(solution)/shard_map/end_right_0/ppermute | solution.py:239
  12.3 1.2 %collective-permute-start.2 = (bf16[16,32,256]{2,1,0:T(8,128)(2,1)S(1)}, bf16[16,32,256]{2,1,0:T(8,128)(2,1)S(1)}, u32[]{:S(2)}, u32[]{:S(2)}) collective-permute-start(bf16[16,32,256]{2,1,0:T(8,128)(2,1)S(1)} %get-tuple-element.57), channel_id=1, source_target_pairs={{0,2},{1,3},{2,0},{3,1},{4,6},{5,7},{6,4},{7,5},{8,10},{9,11},{10,... | collective-permute-start | bytes 786440 | tf_op jit(solution)/shard_map/cross_right_0/ppermute | solution.py:239
  13.6 2.0 %left.1 = (bf16[32,32,256]{2,1,0:T(8,128)(2,1)S(1)}, bf16[16,32,256]{2,1,0:T(8,128)(2,1)S(1)}, bf16[16,32,256]{2,1,0:T(8,128)(2,1)S(1)}) custom-call(bf16[4096,128]{1,0:T(8,128)(2,1)S(1)} %get-tuple-element.45.normed.normed0, bf16[4096,128]{1,0:T(8,128)(2,1)S(1)} %get-tuple-element.51.normed1, f32[1,32,128]{2,1,0:T(8,128)S(1)} %get-tuple-element.52.valid0, ...), custom_call_target="tpu_custom_call" | custom-call | tf_op jit(solution)/shard_map/left/pallas_call | solution.py:211
  15.6 3.5 %collective-permute-done.2.rest_3_ = bf16[16,32,256]{2,1,0:T(8,128)(2,1)S(1)} collective-permute-done((bf16[16,32,256]{2,1,0:T(8,128)(2,1)S(1)}, bf16[16,32,256]{2,1,0:T(8,128)(2,1)S(1)}, u32[]{:S(2)}, u32[]{:S(2)}) %collective-permute-start.2) | collective-permute-done | bytes 262176 | tf_op jit(solution)/shard_map/cross_right_0/ppermute | solution.py:239
  19.0 2.0 %collective-permute-start.9 = (bf16[16,32,256]{2,1,0:T(8,128)(2,1)S(1)}, bf16[16,32,256]{2,1,0:T(8,128)(2,1)S(1)}, u32[]{:S(2)}, u32[]{:S(2)}) collective-permute-start(bf16[16,32,256]{2,1,0:T(8,128)(2,1)S(1)} %collective-permute-done.2.rest_3_), channel_id=1, source_target_pairs={{0,1},{1,0},{2,3},{3,2},{4,8},{5,9},{6,10},{7,11},{8,4},{9,5},{10,... | collective-permute-start | bytes 786440 | tf_op jit(solution)/shard_map/mid_own_10/ppermute | solution.py:239
  21.0 0.6 collective-permute-start.6
  21.7 0.0 collective-permute-done.3.rest_4_
  21.7 1.2 %collective-permute-start.4 = (bf16[16,32,256]{2,1,0:T(8,128)(2,1)S(1)}, bf16[16,32,256]{2,1,0:T(8,128)(2,1)S(1)}, u32[]{:S(2)}, u32[]{:S(2)}) collective-permute-start(bf16[16,32,256]{2,1,0:T(8,128)(2,1)S(1)} %get-tuple-element.59), channel_id=1, source_target_pairs={{0,2},{1,3},{2,0},{3,1},{4,6},{5,7},{6,4},{7,5},{8,10},{9,11},{10,... | collective-permute-start | bytes 786440 | tf_op jit(solution)/shard_map/cross_left_0/ppermute | solution.py:239
  22.9 0.9 %collective-permute-done.5.rest_4_ = bf16[32,32,256]{2,1,0:T(8,128)(2,1)S(1)} collective-permute-done((bf16[32,32,256]{2,1,0:T(8,128)(2,1)S(1)}, bf16[32,32,256]{2,1,0:T(8,128)(2,1)S(1)}, u32[]{:S(2)}, u32[]{:S(2)}) %collective-permute-start.5) | collective-permute-done | bytes 524320 | tf_op jit(solution)/shard_map/end_right_0/ppermute | solution.py:239
  23.8 2.3 %collective-permute-start.10 = (bf16[32,32,256]{2,1,0:T(8,128)(2,1)S(1)}, bf16[32,32,256]{2,1,0:T(8,128)(2,1)S(1)}, u32[]{:S(2)}, u32[]{:S(2)}) collective-permute-start(bf16[32,32,256]{2,1,0:T(8,128)(2,1)S(1)} %collective-permute-done.5.rest_4_), channel_id=1, source_target_pairs={{0,1},{1,0},{2,3},{3,2},{4,8},{5,9},{6,10},{7,11},{8,4},{9,5},{10,... | collective-permute-start | bytes 1572872 | tf_op jit(solution)/shard_map/mid_next_0/ppermute | solution.py:239
  26.2 0.4 collective-permute-start.7
  26.5 0.0 collective-permute-done.9.rest_5_
  26.5 2.9 %collective-permute-done.6.rest_5_ = bf16[16,32,256]{2,1,0:T(8,128)(2,1)S(1)} collective-permute-done((bf16[16,32,256]{2,1,0:T(8,128)(2,1)S(1)}, bf16[16,32,256]{2,1,0:T(8,128)(2,1)S(1)}, u32[]{:S(2)}, u32[]{:S(2)}) %collective-permute-start.6) | collective-permute-done | bytes 262176 | tf_op jit(solution)/shard_map/end_right_10/ppermute | solution.py:239
  29.5 0.0 collective-permute-done.4.rest_1_
  29.5 1.2 %collective-permute-start.12 = (bf16[16,32,256]{2,1,0:T(8,128)(2,1)S(1)}, bf16[16,32,256]{2,1,0:T(8,128)(2,1)S(1)}, u32[]{:S(2)}, u32[]{:S(2)}) collective-permute-start(bf16[16,32,256]{2,1,0:T(8,128)(2,1)S(1)} %get-tuple-element.67), channel_id=1, source_target_pairs={{0,2},{1,3},{2,0},{3,1},{4,6},{5,7},{6,4},{7,5},{8,10},{9,11},{10,... | collective-permute-start | bytes 786440 | tf_op jit(solution)/shard_map/cross_right_1/ppermute | solution.py:239
  30.7 0.9 %gate.1 = f32[32,128,128]{2,1,0:T(8,128)S(1)} custom-call(bf16[4096,128]{1,0:T(8,128)(2,1)S(1)} %get-tuple-element.45.normed.normed0, bf16[128,128]{1,0:T(8,128)(2,1)S(1)} %copy-done.2), custom_call_target="tpu_custom_call" | custom-call | tf_op jit(solution)/shard_map/gate/pallas_call | solution.py:211
  31.6 2.7 %collective-permute-start.11 = (bf16[16,32,256]{2,1,0:T(8,128)(2,1)S(1)}, bf16[16,32,256]{2,1,0:T(8,128)(2,1)S(1)}, u32[]{:S(2)}, u32[]{:S(2)}) collective-permute-start(bf16[16,32,256]{2,1,0:T(8,128)(2,1)S(1)} %collective-permute-done.6.rest_5_), channel_id=1, source_target_pairs={{0,1},{1,0},{2,3},{3,2},{4,8},{5,9},{6,10},{7,11},{8,4},{9,5},{10,... | collective-permute-start | bytes 786440 | tf_op jit(solution)/shard_map/mid_next_10/ppermute | solution.py:239
  34.3 0.0 collective-permute-start.8
  34.3 0.7 collective-permute-done.12.rest_3_
  35.0 3.2 %collective-permute-start.19 = (bf16[16,32,256]{2,1,0:T(8,128)(2,1)S(1)}, bf16[16,32,256]{2,1,0:T(8,128)(2,1)S(1)}, u32[]{:S(2)}, u32[]{:S(2)}) collective-permute-start(bf16[16,32,256]{2,1,0:T(8,128)(2,1)S(1)} %collective-permute-done.12.rest_3_), channel_id=1, source_target_pairs={{0,1},{1,0},{2,3},{3,2},{4,8},{5,9},{6,10},{7,11},{8,4},{9,5},{10,... | collective-permute-start | bytes 786440 | tf_op jit(solution)/shard_map/mid_own_11/ppermute | solution.py:239
  38.2 0.0 collective-permute-done.10.rest_6_
  38.2 1.2 %collective-permute-start.13 = (bf16[16,32,256]{2,1,0:T(8,128)(2,1)S(1)}, bf16[16,32,256]{2,1,0:T(8,128)(2,1)S(1)}, u32[]{:S(2)}, u32[]{:S(2)}) collective-permute-start(bf16[16,32,256]{2,1,0:T(8,128)(2,1)S(1)} %get-tuple-element.68), channel_id=1, source_target_pairs={{0,2},{1,3},{2,0},{3,1},{4,6},{5,7},{6,4},{7,5},{8,10},{9,11},{10,... | collective-permute-start | bytes 786440 | tf_op jit(solution)/shard_map/cross_left_1/ppermute | solution.py:239
  39.4 1.3 %collective-permute-done.7.rest_2_ = bf16[32,32,256]{2,1,0:T(8,128)(2,1)S(1)} collective-permute-done((bf16[32,32,256]{2,1,0:T(8,128)(2,1)S(1)}, bf16[32,32,256]{2,1,0:T(8,128)(2,1)S(1)}, u32[]{:S(2)}, u32[]{:S(2)}) %collective-permute-start.7) | collective-permute-done | bytes 524320 | tf_op jit(solution)/shard_map/end_left_0/ppermute | solution.py:239
  40.7 1.4 %collective-permute-start.18 = (bf16[16,32,256]{2,1,0:T(8,128)(2,1)S(1)}, bf16[16,32,256]{2,1,0:T(8,128)(2,1)S(1)}, u32[]{:S(2)}, u32[]{:S(2)}) collective-permute-start(bf16[16,32,256]{2,1,0:T(8,128)(2,1)S(1)} %collective-permute-done.12.rest_3_), channel_id=1, source_target_pairs={{0,4},{1,5},{2,6},{3,7},{4,0},{5,1},{6,2},{7,3},{8,12},{9,13},{10,... | collective-permute-start | bytes 786440 | tf_op jit(solution)/shard_map/end_right_11/ppermute | solution.py:239
  42.1 4.2 %collective-permute-done.8.rest_3_ = bf16[16,32,256]{2,1,0:T(8,128)(2,1)S(1)} collective-permute-done((bf16[16,32,256]{2,1,0:T(8,128)(2,1)S(1)}, bf16[16,32,256]{2,1,0:T(8,128)(2,1)S(1)}, u32[]{:S(2)}, u32[]{:S(2)}) %collective-permute-start.8) | collective-permute-done | bytes 262176 | tf_op jit(solution)/shard_map/end_left_10/ppermute | solution.py:239
  46.3 0.0 collective-permute-done.13.rest_8_.rest_1_
  46.3 0.5 away.2
  46.8 1.2 %collective-permute-start.14 = (bf16[16,32,256]{2,1,0:T(8,128)(2,1)S(1)}, bf16[16,32,256]{2,1,0:T(8,128)(2,1)S(1)}, u32[]{:S(2)}, u32[]{:S(2)}) collective-permute-start(bf16[16,32,256]{2,1,0:T(8,128)(2,1)S(1)} %get-tuple-element.70), channel_id=1, source_target_pairs={{0,4},{1,5},{2,6},{3,7},{4,0},{5,1},{6,2},{7,3},{8,12},{9,13},{10,... | collective-permute-start | bytes 786440 | tf_op jit(solution)/shard_map/left_11_and_products_back_0/ppermute | solution.py:239
  48.1 0.0 collective-permute-done.19.rest_5_
  48.1 3.9 %collective-permute-done.18.rest_5_ = bf16[16,32,256]{2,1,0:T(8,128)(2,1)S(1)} collective-permute-done((bf16[16,32,256]{2,1,0:T(8,128)(2,1)S(1)}, bf16[16,32,256]{2,1,0:T(8,128)(2,1)S(1)}, u32[]{:S(2)}, u32[]{:S(2)}) %collective-permute-start.18) | collective-permute-done | bytes 262176 | tf_op jit(solution)/shard_map/end_right_11/ppermute | solution.py:239
  51.9 2.3 %collective-permute-start.20 = (bf16[16,32,256]{2,1,0:T(8,128)(2,1)S(1)}, bf16[16,32,256]{2,1,0:T(8,128)(2,1)S(1)}, u32[]{:S(2)}, u32[]{:S(2)}) collective-permute-start(bf16[16,32,256]{2,1,0:T(8,128)(2,1)S(1)} %collective-permute-done.18.rest_5_), channel_id=1, source_target_pairs={{0,1},{1,0},{2,3},{3,2},{4,8},{5,9},{6,10},{7,11},{8,4},{9,5},{10,... | collective-permute-start | bytes 786440 | tf_op jit(solution)/shard_map/mid_next_11/ppermute | solution.py:239
  54.2 0.6 near.2
  54.8 2.7 %collective-permute-done.14.end.rest_3_ = bf16[16,32,256]{2,1,0:T(8,128)(2,1)S(1)} collective-permute-done((bf16[16,32,256]{2,1,0:T(8,128)(2,1)S(1)}, bf16[16,32,256]{2,1,0:T(8,128)(2,1)S(1)}, u32[]{:S(2)}, u32[]{:S(2)}) %collective-permute-start.14) | collective-permute-done | bytes 262176 | tf_op jit(solution)/shard_map/left_11_and_products_back_0/ppermute | solution.py:239
  57.5 0.1 hand_out.2
  57.6 0.5 away.3
  58.2 0.0 copy-start.3
  58.2 0.0 copy-start.6
  58.2 1.2 %collective-permute-start.21 = (bf16[16,32,256]{2,1,0:T(8,128)(2,1)S(1)}, bf16[16,32,256]{2,1,0:T(8,128)(2,1)S(1)}, u32[]{:S(2)}, u32[]{:S(2)}) collective-permute-start(bf16[16,32,256]{2,1,0:T(8,128)(2,1)S(1)} %get-tuple-element.80), channel_id=1, source_target_pairs={{0,4},{1,5},{2,6},{3,7},{4,0},{5,1},{6,2},{7,3},{8,12},{9,13},{10,... | collective-permute-start | bytes 786440 | tf_op jit(solution)/shard_map/products_back_1/ppermute | solution.py:239
  59.4 3.9 %collective-permute-start.15 = (bf16[16,32,128]{2,1,0:T(8,128)(2,1)S(1)}, bf16[16,32,128]{2,1,0:T(8,128)(2,1)S(1)}, u32[]{:S(2)}, u32[]{:S(2)}) collective-permute-start(bf16[16,32,128]{2,1,0:T(8,128)(2,1)S(1)} %get-tuple-element.72), channel_id=1, source_target_pairs={{0,1},{1,0},{2,3},{3,2},{4,5},{5,4},{6,7},{7,6},{8,9},{9,8},{10,11... | collective-permute-start | bytes 393224 | tf_op jit(solution)/shard_map/return_01/ppermute | solution.py:239
  63.3 0.6 near.3
  63.9 1.3 %collective-permute-start.16 = (bf16[16,32,128]{2,1,0:T(8,128)(2,1)S(1)}, bf16[16,32,128]{2,1,0:T(8,128)(2,1)S(1)}, u32[]{:S(2)}, u32[]{:S(2)}) collective-permute-start(bf16[16,32,128]{2,1,0:T(8,128)(2,1)S(1)} %get-tuple-element.73), channel_id=1, source_target_pairs={{0,2},{1,3},{2,0},{3,1},{4,6},{5,7},{6,4},{7,5},{8,10},{9,11},{10,... | collective-permute-start | bytes 393224 | tf_op jit(solution)/shard_map/return_02/ppermute | solution.py:239
  65.2 0.4 collective-permute-start.17
  65.6 0.0 collective-permute-done.21.end
  65.6 0.1 hand_out.3
  65.7 2.1 %collective-permute-start.22 = (bf16[16,32,128]{2,1,0:T(8,128)(2,1)S(1)}, bf16[16,32,128]{2,1,0:T(8,128)(2,1)S(1)}, u32[]{:S(2)}, u32[]{:S(2)}) collective-permute-start(bf16[16,32,128]{2,1,0:T(8,128)(2,1)S(1)} %get-tuple-element.82), channel_id=1, source_target_pairs={{0,1},{1,0},{2,3},{3,2},{4,5},{5,4},{6,7},{7,6},{8,9},{9,8},{10,11... | collective-permute-start | bytes 393224 | tf_op jit(solution)/shard_map/return_11/ppermute | solution.py:239
  67.8 1.3 %collective-permute-start.23 = (bf16[16,32,128]{2,1,0:T(8,128)(2,1)S(1)}, bf16[16,32,128]{2,1,0:T(8,128)(2,1)S(1)}, u32[]{:S(2)}, u32[]{:S(2)}) collective-permute-start(bf16[16,32,128]{2,1,0:T(8,128)(2,1)S(1)} %get-tuple-element.83), channel_id=1, source_target_pairs={{0,2},{1,3},{2,0},{3,1},{4,6},{5,7},{6,4},{7,5},{8,10},{9,11},{10,... | collective-permute-start | bytes 393224 | tf_op jit(solution)/shard_map/return_12/ppermute | solution.py:239
  69.1 0.5 collective-permute-start.24
  69.5 0.0 collective-permute-done.16.rest_2_
  69.5 2.8 %collective-permute-done.17.rest_3_ = bf16[16,32,128]{2,1,0:T(8,128)(2,1)S(1)} collective-permute-done((bf16[16,32,128]{2,1,0:T(8,128)(2,1)S(1)}, bf16[16,32,128]{2,1,0:T(8,128)(2,1)S(1)}, u32[]{:S(2)}, u32[]{:S(2)}) %collective-permute-start.17) | collective-permute-done | bytes 131104 | tf_op jit(solution)/shard_map/return_03/ppermute | solution.py:239
  72.4 2.3 %collective-permute-done.23.rest_6_ = bf16[16,32,128]{2,1,0:T(8,128)(2,1)S(1)} collective-permute-done((bf16[16,32,128]{2,1,0:T(8,128)(2,1)S(1)}, bf16[16,32,128]{2,1,0:T(8,128)(2,1)S(1)}, u32[]{:S(2)}, u32[]{:S(2)}) %collective-permute-start.23) | collective-permute-done | bytes 131104 | tf_op jit(solution)/shard_map/return_12/ppermute | solution.py:239
  74.7 2.9 %collective-permute-done.24.rest_7_ = bf16[16,32,128]{2,1,0:T(8,128)(2,1)S(1)} collective-permute-done((bf16[16,32,128]{2,1,0:T(8,128)(2,1)S(1)}, bf16[16,32,128]{2,1,0:T(8,128)(2,1)S(1)}, u32[]{:S(2)}, u32[]{:S(2)}) %collective-permute-start.24) | collective-permute-done | bytes 131104 | tf_op jit(solution)/shard_map/return_13/ppermute | solution.py:239
  77.6 2.5 %update.1 = bf16[32,128,128]{2,1,0:T(8,128)(2,1)} custom-call(f32[1,128]{1,0:T(1,128)S(1)} %bitcast.3, bf16[128,128]{1,0:T(8,128)(2,1)S(1)} %copy-done.3, f32[32,128,128]{2,1,0:T(8,128)S(1)} %gate.1, bf16[16,32,128]{2,1,0:T(8,128)(2,1)S(1)} %get-tuple-element.71.rest_0_, bf16[16,32,128]{2,1,0:T(8,128)(2,1)S(1)} %collective-permute-done.15.rest_1_, ...), custom_call_target="tpu_custom_call" | custom-call | tf_op jit(solution)/shard_map/update/pallas_call | solution.py:211
  (11 shorter events, 0.0 us)
Async XLA Ops:
  0.0 6.3 %collective-permute-start = (bf16[32,128,128]{2,1,0:T(8,128)(2,1)}, bf16[32,128,128]{2,1,0:T(8,128)(2,1)S(1)}, u32[]{:S(2)}, u32[]{:S(2)}) collective-permute-start(bf16[32,128,128]{2,1,0:T(8,128)(2,1)} %pair.1), channel_id=1, source_target_pairs={{0,1},{1,0},{2,3},{3,2},{4,5},{5,4},{6,7},{7,6},{8,9},{9,8},{10,11... | collective-permute-start | bytes 3145736 | tf_op jit(solution)/shard_map/pair/ppermute | solution.py:239
  0.1 6.3 %collective-permute-start.1 = (s32[32,128]{1,0:T(8,128)}, s32[32,128]{1,0:T(8,128)S(1)}, u32[]{:S(2)}, u32[]{:S(2)}) collective-permute-start(s32[32,128]{1,0:T(8,128)} %mask.1), channel_id=1, source_target_pairs={{0,1},{1,0},{2,3},{3,2},{4,5},{5,4},{6,7},{7,6},{8,9},{9,8},{10,11... | collective-permute-start | bytes 49160 | tf_op jit(solution)/shard_map/mask/ppermute | solution.py:239
  0.5 1.2 %copy-start = (bf16[32,128,128]{2,1,0:T(8,128)(2,1)S(1)}, bf16[32,128,128]{2,1,0:T(8,128)(2,1)}, u32[]{:S(2)}) copy-start(bf16[32,128,128]{2,1,0:T(8,128)(2,1)} %pair.1) | copy-start | bytes 3145732
  1.7 0.9 %copy-start.1 = (bf16[128,512]{1,0:T(8,128)(2,1)S(1)}, bf16[128,512]{1,0:T(8,128)(2,1)}, u32[]{:S(2)}) copy-start(bf16[128,512]{1,0:T(8,128)(2,1)} %weight.3) | copy-start | bytes 393220
  2.6 0.7 copy-start.4
  3.4 0.7 copy-start.5
  6.3 24.4 %copy-start.2 = (bf16[128,128]{1,0:T(8,128)(2,1)S(1)}, bf16[128,128]{1,0:T(8,128)(2,1)}, u32[]{:S(2)}) copy-start(bf16[128,128]{1,0:T(8,128)(2,1)} %weight.4) | copy-start | bytes 98308
  8.7 13.0 %collective-permute-start.3 = (bf16[32,32,256]{2,1,0:T(8,128)(2,1)S(1)}, bf16[32,32,256]{2,1,0:T(8,128)(2,1)S(1)}, u32[]{:S(2)}, u32[]{:S(2)}) collective-permute-start(bf16[32,32,256]{2,1,0:T(8,128)(2,1)S(1)} %get-tuple-element.58.rest_2_), channel_id=1, source_target_pairs={{0,1},{1,0},{2,3},{3,2},{4,8},{5,9},{6,10},{7,11},{8,4},{9,5},{10,... | collective-permute-start | bytes 1572872 | tf_op jit(solution)/shard_map/mid_own_0/ppermute | solution.py:239
  8.8 15.0 %collective-permute-start.5 = (bf16[32,32,256]{2,1,0:T(8,128)(2,1)S(1)}, bf16[32,32,256]{2,1,0:T(8,128)(2,1)S(1)}, u32[]{:S(2)}, u32[]{:S(2)}) collective-permute-start(bf16[32,32,256]{2,1,0:T(8,128)(2,1)S(1)} %get-tuple-element.58.rest_2_), channel_id=1, source_target_pairs={{0,4},{1,5},{2,6},{3,7},{4,0},{5,1},{6,2},{7,3},{8,12},{9,13},{10,... | collective-permute-start | bytes 1572872 | tf_op jit(solution)/shard_map/end_right_0/ppermute | solution.py:239
  12.3 6.7 %collective-permute-start.2 = (bf16[16,32,256]{2,1,0:T(8,128)(2,1)S(1)}, bf16[16,32,256]{2,1,0:T(8,128)(2,1)S(1)}, u32[]{:S(2)}, u32[]{:S(2)}) collective-permute-start(bf16[16,32,256]{2,1,0:T(8,128)(2,1)S(1)} %get-tuple-element.57), channel_id=1, source_target_pairs={{0,2},{1,3},{2,0},{3,1},{4,6},{5,7},{6,4},{7,5},{8,10},{9,11},{10,... | collective-permute-start | bytes 786440 | tf_op jit(solution)/shard_map/cross_right_0/ppermute | solution.py:239
  19.0 7.5 %collective-permute-start.9 = (bf16[16,32,256]{2,1,0:T(8,128)(2,1)S(1)}, bf16[16,32,256]{2,1,0:T(8,128)(2,1)S(1)}, u32[]{:S(2)}, u32[]{:S(2)}) collective-permute-start(bf16[16,32,256]{2,1,0:T(8,128)(2,1)S(1)} %collective-permute-done.2.rest_3_), channel_id=1, source_target_pairs={{0,1},{1,0},{2,3},{3,2},{4,8},{5,9},{6,10},{7,11},{8,4},{9,5},{10,... | collective-permute-start | bytes 786440 | tf_op jit(solution)/shard_map/mid_own_10/ppermute | solution.py:239
  21.0 8.4 %collective-permute-start.6 = (bf16[16,32,256]{2,1,0:T(8,128)(2,1)S(1)}, bf16[16,32,256]{2,1,0:T(8,128)(2,1)S(1)}, u32[]{:S(2)}, u32[]{:S(2)}) collective-permute-start(bf16[16,32,256]{2,1,0:T(8,128)(2,1)S(1)} %collective-permute-done.2.rest_3_), channel_id=1, source_target_pairs={{0,4},{1,5},{2,6},{3,7},{4,0},{5,1},{6,2},{7,3},{8,12},{9,13},{10,... | collective-permute-start | bytes 786440 | tf_op jit(solution)/shard_map/end_right_10/ppermute | solution.py:239
  21.7 7.8 %collective-permute-start.4 = (bf16[16,32,256]{2,1,0:T(8,128)(2,1)S(1)}, bf16[16,32,256]{2,1,0:T(8,128)(2,1)S(1)}, u32[]{:S(2)}, u32[]{:S(2)}) collective-permute-start(bf16[16,32,256]{2,1,0:T(8,128)(2,1)S(1)} %get-tuple-element.59), channel_id=1, source_target_pairs={{0,2},{1,3},{2,0},{3,1},{4,6},{5,7},{6,4},{7,5},{8,10},{9,11},{10,... | collective-permute-start | bytes 786440 | tf_op jit(solution)/shard_map/cross_left_0/ppermute | solution.py:239
  23.8 14.3 %collective-permute-start.10 = (bf16[32,32,256]{2,1,0:T(8,128)(2,1)S(1)}, bf16[32,32,256]{2,1,0:T(8,128)(2,1)S(1)}, u32[]{:S(2)}, u32[]{:S(2)}) collective-permute-start(bf16[32,32,256]{2,1,0:T(8,128)(2,1)S(1)} %collective-permute-done.5.rest_4_), channel_id=1, source_target_pairs={{0,1},{1,0},{2,3},{3,2},{4,8},{5,9},{6,10},{7,11},{8,4},{9,5},{10,... | collective-permute-start | bytes 1572872 | tf_op jit(solution)/shard_map/mid_next_0/ppermute | solution.py:239
  26.2 14.5 %collective-permute-start.7 = (bf16[32,32,256]{2,1,0:T(8,128)(2,1)S(1)}, bf16[32,32,256]{2,1,0:T(8,128)(2,1)S(1)}, u32[]{:S(2)}, u32[]{:S(2)}) collective-permute-start(bf16[32,32,256]{2,1,0:T(8,128)(2,1)S(1)} %get-tuple-element.76.rest_0_), channel_id=1, source_target_pairs={{0,4},{1,5},{2,6},{3,7},{4,0},{5,1},{6,2},{7,3},{8,12},{9,13},{10,... | collective-permute-start | bytes 1572872 | tf_op jit(solution)/shard_map/end_left_0/ppermute | solution.py:239
  29.5 5.5 %collective-permute-start.12 = (bf16[16,32,256]{2,1,0:T(8,128)(2,1)S(1)}, bf16[16,32,256]{2,1,0:T(8,128)(2,1)S(1)}, u32[]{:S(2)}, u32[]{:S(2)}) collective-permute-start(bf16[16,32,256]{2,1,0:T(8,128)(2,1)S(1)} %get-tuple-element.67), channel_id=1, source_target_pairs={{0,2},{1,3},{2,0},{3,1},{4,6},{5,7},{6,4},{7,5},{8,10},{9,11},{10,... | collective-permute-start | bytes 786440 | tf_op jit(solution)/shard_map/cross_right_1/ppermute | solution.py:239
  31.6 10.5 %collective-permute-start.11 = (bf16[16,32,256]{2,1,0:T(8,128)(2,1)S(1)}, bf16[16,32,256]{2,1,0:T(8,128)(2,1)S(1)}, u32[]{:S(2)}, u32[]{:S(2)}) collective-permute-start(bf16[16,32,256]{2,1,0:T(8,128)(2,1)S(1)} %collective-permute-done.6.rest_5_), channel_id=1, source_target_pairs={{0,1},{1,0},{2,3},{3,2},{4,8},{5,9},{6,10},{7,11},{8,4},{9,5},{10,... | collective-permute-start | bytes 786440 | tf_op jit(solution)/shard_map/mid_next_10/ppermute | solution.py:239
  34.3 12.0 %collective-permute-start.8 = (bf16[16,32,256]{2,1,0:T(8,128)(2,1)S(1)}, bf16[16,32,256]{2,1,0:T(8,128)(2,1)S(1)}, u32[]{:S(2)}, u32[]{:S(2)}) collective-permute-start(bf16[16,32,256]{2,1,0:T(8,128)(2,1)S(1)} %collective-permute-done.4.rest_1_), channel_id=1, source_target_pairs={{0,4},{1,5},{2,6},{3,7},{4,0},{5,1},{6,2},{7,3},{8,12},{9,13},{10,... | collective-permute-start | bytes 786440 | tf_op jit(solution)/shard_map/end_left_10/ppermute | solution.py:239
  35.0 13.1 %collective-permute-start.19 = (bf16[16,32,256]{2,1,0:T(8,128)(2,1)S(1)}, bf16[16,32,256]{2,1,0:T(8,128)(2,1)S(1)}, u32[]{:S(2)}, u32[]{:S(2)}) collective-permute-start(bf16[16,32,256]{2,1,0:T(8,128)(2,1)S(1)} %collective-permute-done.12.rest_3_), channel_id=1, source_target_pairs={{0,1},{1,0},{2,3},{3,2},{4,8},{5,9},{6,10},{7,11},{8,4},{9,5},{10,... | collective-permute-start | bytes 786440 | tf_op jit(solution)/shard_map/mid_own_11/ppermute | solution.py:239
  38.2 8.1 %collective-permute-start.13 = (bf16[16,32,256]{2,1,0:T(8,128)(2,1)S(1)}, bf16[16,32,256]{2,1,0:T(8,128)(2,1)S(1)}, u32[]{:S(2)}, u32[]{:S(2)}) collective-permute-start(bf16[16,32,256]{2,1,0:T(8,128)(2,1)S(1)} %get-tuple-element.68), channel_id=1, source_target_pairs={{0,2},{1,3},{2,0},{3,1},{4,6},{5,7},{6,4},{7,5},{8,10},{9,11},{10,... | collective-permute-start | bytes 786440 | tf_op jit(solution)/shard_map/cross_left_1/ppermute | solution.py:239
  40.7 11.2 %collective-permute-start.18 = (bf16[16,32,256]{2,1,0:T(8,128)(2,1)S(1)}, bf16[16,32,256]{2,1,0:T(8,128)(2,1)S(1)}, u32[]{:S(2)}, u32[]{:S(2)}) collective-permute-start(bf16[16,32,256]{2,1,0:T(8,128)(2,1)S(1)} %collective-permute-done.12.rest_3_), channel_id=1, source_target_pairs={{0,4},{1,5},{2,6},{3,7},{4,0},{5,1},{6,2},{7,3},{8,12},{9,13},{10,... | collective-permute-start | bytes 786440 | tf_op jit(solution)/shard_map/end_right_11/ppermute | solution.py:239
  46.8 10.7 %collective-permute-start.14 = (bf16[16,32,256]{2,1,0:T(8,128)(2,1)S(1)}, bf16[16,32,256]{2,1,0:T(8,128)(2,1)S(1)}, u32[]{:S(2)}, u32[]{:S(2)}) collective-permute-start(bf16[16,32,256]{2,1,0:T(8,128)(2,1)S(1)} %get-tuple-element.70), channel_id=1, source_target_pairs={{0,4},{1,5},{2,6},{3,7},{4,0},{5,1},{6,2},{7,3},{8,12},{9,13},{10,... | collective-permute-start | bytes 786440 | tf_op jit(solution)/shard_map/left_11_and_products_back_0/ppermute | solution.py:239
  51.9 5.7 %collective-permute-start.20 = (bf16[16,32,256]{2,1,0:T(8,128)(2,1)S(1)}, bf16[16,32,256]{2,1,0:T(8,128)(2,1)S(1)}, u32[]{:S(2)}, u32[]{:S(2)}) collective-permute-start(bf16[16,32,256]{2,1,0:T(8,128)(2,1)S(1)} %collective-permute-done.18.rest_5_), channel_id=1, source_target_pairs={{0,1},{1,0},{2,3},{3,2},{4,8},{5,9},{6,10},{7,11},{8,4},{9,5},{10,... | collective-permute-start | bytes 786440 | tf_op jit(solution)/shard_map/mid_next_11/ppermute | solution.py:239
  58.2 19.4 %copy-start.3 = (bf16[128,128]{1,0:T(8,128)(2,1)S(1)}, bf16[128,128]{1,0:T(8,128)(2,1)}, u32[]{:S(2)}) copy-start(bf16[128,128]{1,0:T(8,128)(2,1)} %weight.5) | copy-start | bytes 98308
  58.2 19.4 %copy-start.6 = (f32[128]{0:T(128)S(1)}, f32[128]{0:T(128)}, u32[]{:S(2)}) copy-start(f32[128]{0:T(128)} %param.12) | copy-start | bytes 1540
  58.2 7.4 %collective-permute-start.21 = (bf16[16,32,256]{2,1,0:T(8,128)(2,1)S(1)}, bf16[16,32,256]{2,1,0:T(8,128)(2,1)S(1)}, u32[]{:S(2)}, u32[]{:S(2)}) collective-permute-start(bf16[16,32,256]{2,1,0:T(8,128)(2,1)S(1)} %get-tuple-element.80), channel_id=1, source_target_pairs={{0,4},{1,5},{2,6},{3,7},{4,0},{5,1},{6,2},{7,3},{8,12},{9,13},{10,... | collective-permute-start | bytes 786440 | tf_op jit(solution)/shard_map/products_back_1/ppermute | solution.py:239
  59.4 9.7 %collective-permute-start.15 = (bf16[16,32,128]{2,1,0:T(8,128)(2,1)S(1)}, bf16[16,32,128]{2,1,0:T(8,128)(2,1)S(1)}, u32[]{:S(2)}, u32[]{:S(2)}) collective-permute-start(bf16[16,32,128]{2,1,0:T(8,128)(2,1)S(1)} %get-tuple-element.72), channel_id=1, source_target_pairs={{0,1},{1,0},{2,3},{3,2},{4,5},{5,4},{6,7},{7,6},{8,9},{9,8},{10,11... | collective-permute-start | bytes 393224 | tf_op jit(solution)/shard_map/return_01/ppermute | solution.py:239
  63.9 5.7 %collective-permute-start.16 = (bf16[16,32,128]{2,1,0:T(8,128)(2,1)S(1)}, bf16[16,32,128]{2,1,0:T(8,128)(2,1)S(1)}, u32[]{:S(2)}, u32[]{:S(2)}) collective-permute-start(bf16[16,32,128]{2,1,0:T(8,128)(2,1)S(1)} %get-tuple-element.73), channel_id=1, source_target_pairs={{0,2},{1,3},{2,0},{3,1},{4,6},{5,7},{6,4},{7,5},{8,10},{9,11},{10,... | collective-permute-start | bytes 393224 | tf_op jit(solution)/shard_map/return_02/ppermute | solution.py:239
  65.2 7.2 %collective-permute-start.17 = (bf16[16,32,128]{2,1,0:T(8,128)(2,1)S(1)}, bf16[16,32,128]{2,1,0:T(8,128)(2,1)S(1)}, u32[]{:S(2)}, u32[]{:S(2)}) collective-permute-start(bf16[16,32,128]{2,1,0:T(8,128)(2,1)S(1)} %get-tuple-element.74), channel_id=1, source_target_pairs={{0,3},{1,2},{2,1},{3,0},{4,7},{5,6},{6,5},{7,4},{8,11},{9,10},{10,... | collective-permute-start | bytes 393224 | tf_op jit(solution)/shard_map/return_03/ppermute | solution.py:239
  65.7 6.7 %collective-permute-start.22 = (bf16[16,32,128]{2,1,0:T(8,128)(2,1)S(1)}, bf16[16,32,128]{2,1,0:T(8,128)(2,1)S(1)}, u32[]{:S(2)}, u32[]{:S(2)}) collective-permute-start(bf16[16,32,128]{2,1,0:T(8,128)(2,1)S(1)} %get-tuple-element.82), channel_id=1, source_target_pairs={{0,1},{1,0},{2,3},{3,2},{4,5},{5,4},{6,7},{7,6},{8,9},{9,8},{10,11... | collective-permute-start | bytes 393224 | tf_op jit(solution)/shard_map/return_11/ppermute | solution.py:239
  67.8 6.9 %collective-permute-start.23 = (bf16[16,32,128]{2,1,0:T(8,128)(2,1)S(1)}, bf16[16,32,128]{2,1,0:T(8,128)(2,1)S(1)}, u32[]{:S(2)}, u32[]{:S(2)}) collective-permute-start(bf16[16,32,128]{2,1,0:T(8,128)(2,1)S(1)} %get-tuple-element.83), channel_id=1, source_target_pairs={{0,2},{1,3},{2,0},{3,1},{4,6},{5,7},{6,4},{7,5},{8,10},{9,11},{10,... | collective-permute-start | bytes 393224 | tf_op jit(solution)/shard_map/return_12/ppermute | solution.py:239
  69.1 8.5 %collective-permute-start.24 = (bf16[16,32,128]{2,1,0:T(8,128)(2,1)S(1)}, bf16[16,32,128]{2,1,0:T(8,128)(2,1)S(1)}, u32[]{:S(2)}, u32[]{:S(2)}) collective-permute-start(bf16[16,32,128]{2,1,0:T(8,128)(2,1)S(1)} %get-tuple-element.84), channel_id=1, source_target_pairs={{0,3},{1,2},{2,1},{3,0},{4,7},{5,6},{6,5},{7,4},{8,11},{9,10},{10,... | collective-permute-start | bytes 393224 | tf_op jit(solution)/shard_map/return_13/ppermute | solution.py:239

commit v13 on v12

--- a/solution.py
+++ b/solution.py
@@ -25,9 +25,15 @@
 
 
 def normalise(x, gain):
-    mean = jnp.mean(x, axis=-1, keepdims=True)
-    centered = x - mean
-    var = jnp.mean(centered * centered, axis=-1, keepdims=True)
+    width = x.shape[1]
+    ones = jnp.full((width, width), 1.0 / width, BF16)
+    mean = jnp.dot(x, ones, preferred_element_type=F32)
+    centered = x.astype(F32) - mean
+    squares = centered * centered
+    high = squares.astype(BF16)
+    low = (squares - high.astype(F32)).astype(BF16)
+    both = jnp.concatenate([high, low], axis=1)
+    var = jnp.dot(both, jnp.concatenate([ones, ones]), preferred_element_type=F32)
     return (centered * lax.rsqrt(var + 1e-05) * gain).astype(BF16)
 
 
@@ -60,7 +66,7 @@
     @pl.loop(0, rows // GROUP, unroll=UNROLL)
     def _(at):
         first = at * GROUP
-        x = pair[pl.ds(first, GROUP)].astype(F32).reshape(GROUP * toks, -1)
+        x = pair[pl.ds(first, GROUP)].reshape(GROUP * toks, -1)
         normed = normalise(x, gain[...])
         normed_out[pl.ds(first * toks, GROUP * toks), :] = normed
         gated(normed, chosen, valid, first, held)
@@ -258,7 +264,9 @@
         return {1: (0, b, k), planes - 2: (planes - 1, b, k)}.get(p)
 
     gains = in_gain.reshape(1, -1)
-    twin, twin_mask = send(pair, in_plane(1), "pair"), send(pair_mask, in_plane(1), "mask")
+    other = in_plane(1)
+    weight, gains = send(proj_weight, other, "weights"), send(gains, other, "gain")
+    twin_mask, twin = send(pair_mask, other, "mask"), send(after(pair, weight, gains), other, "pair")
 
     def piece(count, height, depth):
         return jax.ShapeDtypeStruct((count, height, depth), BF16)
@@ -274,7 +282,7 @@
         + [rows_all, weights, weights, valid_shape, gains],
         [VMEM] * 4,
         [pltpu.VMEM((4 * hidden, channels), BF16), held],
-    )(pair, pair_mask, gains, proj_weight)
+    )(pair, pair_mask, gains, weight)
     whole = [piece(count, rows, 2 * toks) for count in (part, *counts)]
     *right, normed1, twin_valid = kernel(
         right_twin_kernel,
@@ -360,7 +368,7 @@
     next1.append([mid("next_11", x, next1[0][-1], own1[1], away0) for x in near1[1]])
     swapped = send(swapped, edge, "left_11_and_products_back_0")
     pieces = hand_out(0, close[0], away0, swapped)
-    sides = [(after(left0, pieces[0]), left1[1]), (outer0, swapped)]
+    sides = [(after(left0, pieces[0], close[1]), left1[1]), (outer0, swapped)]
     away1, ends = products(True, first[1], sides, far_planes(1), "away")
     ends = send(ends, edge, "products_back_1")
     pieces += hand_out(1, close[1], away1, ends)

time: 80.6 us -> 83.5 us (1.036)
  Pallas kernels: 12.4 us -> 16 us
  waiting for transfers between devices: 28.1 us -> 30.2 us
  local copies, waits for them, and re-layouts: 3.52 us -> 1.96 us
  starting transfers between devices: 36 us -> 34.8 us
    pallas_call x11, Pallas kernels: 12.4 us -> 16 us  [call(): pl.pallas_call(body, out_shape=out_shape, in_specs=in_specs, out_specs=ou...]
    ppermute x25 -> x27, waiting for transfers between devices: 28.1 us -> 30.2 us  [send(): return lax.ppermute(x, ('row', 'chan'), pairs)]
    unnamed x14 -> x10, local copies, waits for them, and re-layouts: 3.52 us -> 1.96 us
    ppermute x25 -> x27, starting transfers between devices: 36 us -> 34.8 us  [send(): return lax.ppermute(x, ('row', 'chan'), pairs)]
  transfers between devices with their start and end apart: 25 -> 27, of which waited for: 11 -> 12; matrix products, arithmetic and copies ran while one was open for 0% -> 0% of each run, Pallas kernels for 9% -> 11%
where the time goes in v13:
time: 83.5 us; the launch traced here: 83 us
  starting transfers between devices  34.8 us (42%)
  waiting for transfers between devices  30.2 us (36%)
  Pallas kernels  16 us (19%)
  local copies, waits for them, and re-layouts  1.96 us (2%)
    ppermute x27, starting transfers between devices, send(): return lax.ppermute(x, ('row', 'chan'), pairs)  34.8 us
    ppermute x27, waiting for transfers between devices, send(): return lax.ppermute(x, ('row', 'chan'), pairs)  30.2 us
    pallas_call x11, Pallas kernels, call(): pl.pallas_call(body, out_shape=out_shape, in_specs=in_specs, out_specs=ou...  16 us
    unnamed x10, local copies, waits for them, and re-layouts  1.96 us
  transfers between devices with their start and end apart: 27, of which 12 were waited for; matrix products, arithmetic and copies ran while one was open for 0% of the time, Pallas kernels for 11%

profile of v13, /device:TPU:1, one launch (start us, length us, event | category | flops | bytes accessed | tf_op | source)
XLA Modules:
  0.0 83.0 jit_solution(686695867108192523)
XLA Ops:
  0.0 0.1 collective-permute-start.1
  0.1 0.5 collective-permute-start
  0.5 1.0 %collective-permute-done.gain = f32[1,128]{1,0:T(1,128)S(1)} collective-permute-done((f32[1,128]{1,0:T(1,128)}, f32[1,128]{1,0:T(1,128)S(1)}, u32[]{:S(2)}, u32[]{:S(2)}) %collective-permute-start) | collective-permute-done | bytes 544 | tf_op jit(solution)/shard_map/gain/ppermute | solution.py:245
  1.6 0.0 collective-permute-done.1.weight
  1.6 0.2 collective-permute-start.2
  1.8 0.3 collective-permute-start.3
  2.1 1.2 %copy-done = bf16[32,128,128]{2,1,0:T(8,128)(2,1)S(1)} copy-done((bf16[32,128,128]{2,1,0:T(8,128)(2,1)S(1)}, bf16[32,128,128]{2,1,0:T(8,128)(2,1)}, u32[]{:S(2)}) %copy-start) | copy-done | bytes 1048600
  3.3 0.7 copy-done.3
  4.0 4.1 %right_own.1 = (bf16[32,32,128]{2,1,0:T(8,128)(2,1)S(1)}, bf16[16,32,128]{2,1,0:T(8,128)(2,1)S(1)}, bf16[16,32,128]{2,1,0:T(8,128)(2,1)S(1)}, bf16[4096,128]{1,0...) custom-call(bf16[32,128,128]{2,1,0:T(8,128)(2,1)S(1)} %copy-done, ...), custom_call_target="tpu_custom_call" | custom-call | tf_op jit(solution)/shard_map/right_own/pallas_call | solution.py:217
  8.1 0.0 copy-start.1
  8.1 0.0 collective-permute-done.3.mask
  8.1 0.0 collective-permute-done.2.pair
  8.1 4.1 %right_twin.1 = (bf16[32,32,256]{2,1,0:T(8,128)(2,1)S(1)}, bf16[16,32,256]{2,1,0:T(8,128)(2,1)S(1)}, bf16[16,32,256]{2,1,0:T(8,128)(2,1)S(1)}, bf16[4096,128]{1,0:T(8,128)(2,1)S(1)}, f32[1,32,128]{2,1,0:T(8,128)S(1)}) custom-call(bf16[32,128,128]{2,1,0:T(8,128)(2,1)S(1)} %collective-permute-done.2.pair, s32[32,128]{1,0:T(8,128)S(1)} %collective-permute-done.3.mask, ...), custom_call_target="tpu_custom_call" | custom-call | tf_op jit(solution)/shard_map/right_twin/pallas_call | solution.py:217
  12.2 0.3 collective-permute-start.5
  12.5 3.6 %collective-permute-start.7 = (bf16[32,32,256]{2,1,0:T(8,128)(2,1)S(1)}, bf16[32,32,256]{2,1,0:T(8,128)(2,1)S(1)}, u32[]{:S(2)}, u32[]{:S(2)}) collective-permute-start(bf16[32,32,256]{2,1,0:T(8,128)(2,1)S(1)} %get-tuple-element.60.rest_2_), channel_id=1, source_target_pairs={{0,4},{1,5},{2,6},{3,7},{4,0},{5,1},{6,2},{7,3},{8,12},{9,13},{10,... | collective-permute-start | bytes 1572872 | tf_op jit(solution)/shard_map/end_right_0/ppermute | solution.py:245
  16.1 1.2 %collective-permute-start.4 = (bf16[16,32,256]{2,1,0:T(8,128)(2,1)S(1)}, bf16[16,32,256]{2,1,0:T(8,128)(2,1)S(1)}, u32[]{:S(2)}, u32[]{:S(2)}) collective-permute-start(bf16[16,32,256]{2,1,0:T(8,128)(2,1)S(1)} %get-tuple-element.59), channel_id=1, source_target_pairs={{0,2},{1,3},{2,0},{3,1},{4,6},{5,7},{6,4},{7,5},{8,10},{9,11},{10,... | collective-permute-start | bytes 786440 | tf_op jit(solution)/shard_map/cross_right_0/ppermute | solution.py:245
  17.3 2.0 %left.1 = (bf16[32,32,256]{2,1,0:T(8,128)(2,1)S(1)}, bf16[16,32,256]{2,1,0:T(8,128)(2,1)S(1)}, bf16[16,32,256]{2,1,0:T(8,128)(2,1)S(1)}) custom-call(bf16[4096,128]{1,0:T(8,128)(2,1)S(1)} %get-tuple-element.46.normed.normed0, bf16[4096,128]{1,0:T(8,128)(2,1)S(1)} %get-tuple-element.53.normed1, f32[1,32,128]{2,1,0:T(8,128)S(1)} %get-tuple-element.54.valid0, ...), custom_call_target="tpu_custom_call" | custom-call | tf_op jit(solution)/shard_map/left/pallas_call | solution.py:217
  19.3 3.7 %collective-permute-done.4.rest_3_ = bf16[16,32,256]{2,1,0:T(8,128)(2,1)S(1)} collective-permute-done((bf16[16,32,256]{2,1,0:T(8,128)(2,1)S(1)}, bf16[16,32,256]{2,1,0:T(8,128)(2,1)S(1)}, u32[]{:S(2)}, u32[]{:S(2)}) %collective-permute-start.4) | collective-permute-done | bytes 262176 | tf_op jit(solution)/shard_map/cross_right_0/ppermute | solution.py:245
  23.0 1.8 %collective-permute-start.11 = (bf16[16,32,256]{2,1,0:T(8,128)(2,1)S(1)}, bf16[16,32,256]{2,1,0:T(8,128)(2,1)S(1)}, u32[]{:S(2)}, u32[]{:S(2)}) collective-permute-start(bf16[16,32,256]{2,1,0:T(8,128)(2,1)S(1)} %collective-permute-done.4.rest_3_), channel_id=1, source_target_pairs={{0,1},{1,0},{2,3},{3,2},{4,8},{5,9},{6,10},{7,11},{8,4},{9,5},{10,... | collective-permute-start | bytes 786440 | tf_op jit(solution)/shard_map/mid_own_10/ppermute | solution.py:245
  24.8 0.3 collective-permute-start.8
  25.1 1.2 %collective-permute-start.6 = (bf16[16,32,256]{2,1,0:T(8,128)(2,1)S(1)}, bf16[16,32,256]{2,1,0:T(8,128)(2,1)S(1)}, u32[]{:S(2)}, u32[]{:S(2)}) collective-permute-start(bf16[16,32,256]{2,1,0:T(8,128)(2,1)S(1)} %get-tuple-element.61), channel_id=1, source_target_pairs={{0,2},{1,3},{2,0},{3,1},{4,6},{5,7},{6,4},{7,5},{8,10},{9,11},{10,... | collective-permute-start | bytes 786440 | tf_op jit(solution)/shard_map/cross_left_0/ppermute | solution.py:245
  26.3 1.5 %collective-permute-done.7.rest_4_ = bf16[32,32,256]{2,1,0:T(8,128)(2,1)S(1)} collective-permute-done((bf16[32,32,256]{2,1,0:T(8,128)(2,1)S(1)}, bf16[32,32,256]{2,1,0:T(8,128)(2,1)S(1)}, u32[]{:S(2)}, u32[]{:S(2)}) %collective-permute-start.7) | collective-permute-done | bytes 524320 | tf_op jit(solution)/shard_map/end_right_0/ppermute | solution.py:245
  27.8 1.9 %collective-permute-start.12 = (bf16[32,32,256]{2,1,0:T(8,128)(2,1)S(1)}, bf16[32,32,256]{2,1,0:T(8,128)(2,1)S(1)}, u32[]{:S(2)}, u32[]{:S(2)}) collective-permute-start(bf16[32,32,256]{2,1,0:T(8,128)(2,1)S(1)} %collective-permute-done.7.rest_4_), channel_id=1, source_target_pairs={{0,1},{1,0},{2,3},{3,2},{4,8},{5,9},{6,10},{7,11},{8,4},{9,5},{10,... | collective-permute-start | bytes 1572872 | tf_op jit(solution)/shard_map/mid_next_0/ppermute | solution.py:245
  29.7 0.8 %collective-permute-start.9 = (bf16[32,32,256]{2,1,0:T(8,128)(2,1)S(1)}, bf16[32,32,256]{2,1,0:T(8,128)(2,1)S(1)}, u32[]{:S(2)}, u32[]{:S(2)}) collective-permute-start(bf16[32,32,256]{2,1,0:T(8,128)(2,1)S(1)} %get-tuple-element.78.rest_0_), channel_id=1, source_target_pairs={{0,4},{1,5},{2,6},{3,7},{4,0},{5,1},{6,2},{7,3},{8,12},{9,13},{10,... | collective-permute-start | bytes 1572872 | tf_op jit(solution)/shard_map/end_left_0/ppermute | solution.py:245
  30.5 0.0 collective-permute-done.11.rest_5_
  30.5 2.9 %collective-permute-done.8.rest_5_ = bf16[16,32,256]{2,1,0:T(8,128)(2,1)S(1)} collective-permute-done((bf16[16,32,256]{2,1,0:T(8,128)(2,1)S(1)}, bf16[16,32,256]{2,1,0:T(8,128)(2,1)S(1)}, u32[]{:S(2)}, u32[]{:S(2)}) %collective-permute-start.8) | collective-permute-done | bytes 262176 | tf_op jit(solution)/shard_map/end_right_10/ppermute | solution.py:245
  33.4 0.0 collective-permute-done.6.rest_1_
  33.4 1.2 %collective-permute-start.14 = (bf16[16,32,256]{2,1,0:T(8,128)(2,1)S(1)}, bf16[16,32,256]{2,1,0:T(8,128)(2,1)S(1)}, u32[]{:S(2)}, u32[]{:S(2)}) collective-permute-start(bf16[16,32,256]{2,1,0:T(8,128)(2,1)S(1)} %get-tuple-element.69), channel_id=1, source_target_pairs={{0,2},{1,3},{2,0},{3,1},{4,6},{5,7},{6,4},{7,5},{8,10},{9,11},{10,... | collective-permute-start | bytes 786440 | tf_op jit(solution)/shard_map/cross_right_1/ppermute | solution.py:245
  34.7 0.9 %gate.1 = f32[32,128,128]{2,1,0:T(8,128)S(1)} custom-call(bf16[4096,128]{1,0:T(8,128)(2,1)S(1)} %get-tuple-element.46.normed.normed0, bf16[128,128]{1,0:T(8,128)(2,1)S(1)} %copy-done.1), custom_call_target="tpu_custom_call" | custom-call | tf_op jit(solution)/shard_map/gate/pallas_call | solution.py:217
  35.6 2.2 %collective-permute-start.13 = (bf16[16,32,256]{2,1,0:T(8,128)(2,1)S(1)}, bf16[16,32,256]{2,1,0:T(8,128)(2,1)S(1)}, u32[]{:S(2)}, u32[]{:S(2)}) collective-permute-start(bf16[16,32,256]{2,1,0:T(8,128)(2,1)S(1)} %collective-permute-done.8.rest_5_), channel_id=1, source_target_pairs={{0,1},{1,0},{2,3},{3,2},{4,8},{5,9},{6,10},{7,11},{8,4},{9,5},{10,... | collective-permute-start | bytes 786440 | tf_op jit(solution)/shard_map/mid_next_10/ppermute | solution.py:245
  37.8 1.6 %collective-permute-done.14.rest_3_ = bf16[16,32,256]{2,1,0:T(8,128)(2,1)S(1)} collective-permute-done((bf16[16,32,256]{2,1,0:T(8,128)(2,1)S(1)}, bf16[16,32,256]{2,1,0:T(8,128)(2,1)S(1)}, u32[]{:S(2)}, u32[]{:S(2)}) %collective-permute-start.14) | collective-permute-done | bytes 262176 | tf_op jit(solution)/shard_map/cross_right_1/ppermute | solution.py:245
  39.4 2.8 %collective-permute-start.21 = (bf16[16,32,256]{2,1,0:T(8,128)(2,1)S(1)}, bf16[16,32,256]{2,1,0:T(8,128)(2,1)S(1)}, u32[]{:S(2)}, u32[]{:S(2)}) collective-permute-start(bf16[16,32,256]{2,1,0:T(8,128)(2,1)S(1)} %collective-permute-done.14.rest_3_), channel_id=1, source_target_pairs={{0,1},{1,0},{2,3},{3,2},{4,8},{5,9},{6,10},{7,11},{8,4},{9,5},{10,... | collective-permute-start | bytes 786440 | tf_op jit(solution)/shard_map/mid_own_11/ppermute | solution.py:245
  42.2 0.0 collective-permute-done.12.rest_6_
  42.2 1.2 %collective-permute-start.15 = (bf16[16,32,256]{2,1,0:T(8,128)(2,1)S(1)}, bf16[16,32,256]{2,1,0:T(8,128)(2,1)S(1)}, u32[]{:S(2)}, u32[]{:S(2)}) collective-permute-start(bf16[16,32,256]{2,1,0:T(8,128)(2,1)S(1)} %get-tuple-element.70), channel_id=1, source_target_pairs={{0,2},{1,3},{2,0},{3,1},{4,6},{5,7},{6,4},{7,5},{8,10},{9,11},{10,... | collective-permute-start | bytes 786440 | tf_op jit(solution)/shard_map/cross_left_1/ppermute | solution.py:245
  43.4 1.3 %collective-permute-done.9.rest_2_ = bf16[32,32,256]{2,1,0:T(8,128)(2,1)S(1)} collective-permute-done((bf16[32,32,256]{2,1,0:T(8,128)(2,1)S(1)}, bf16[32,32,256]{2,1,0:T(8,128)(2,1)S(1)}, u32[]{:S(2)}, u32[]{:S(2)}) %collective-permute-start.9) | collective-permute-done | bytes 524320 | tf_op jit(solution)/shard_map/end_left_0/ppermute | solution.py:245
  44.7 1.4 %collective-permute-start.20 = (bf16[16,32,256]{2,1,0:T(8,128)(2,1)S(1)}, bf16[16,32,256]{2,1,0:T(8,128)(2,1)S(1)}, u32[]{:S(2)}, u32[]{:S(2)}) collective-permute-start(bf16[16,32,256]{2,1,0:T(8,128)(2,1)S(1)} %collective-permute-done.14.rest_3_), channel_id=1, source_target_pairs={{0,4},{1,5},{2,6},{3,7},{4,0},{5,1},{6,2},{7,3},{8,12},{9,13},{10,... | collective-permute-start | bytes 786440 | tf_op jit(solution)/shard_map/end_right_11/ppermute | solution.py:245
  46.1 4.2 %collective-permute-done.10.rest_3_ = bf16[16,32,256]{2,1,0:T(8,128)(2,1)S(1)} collective-permute-done((bf16[16,32,256]{2,1,0:T(8,128)(2,1)S(1)}, bf16[16,32,256]{2,1,0:T(8,128)(2,1)S(1)}, u32[]{:S(2)}, u32[]{:S(2)}) %collective-permute-start.10) | collective-permute-done | bytes 262176 | tf_op jit(solution)/shard_map/end_left_10/ppermute | solution.py:245
  50.3 0.5 away.2
  50.8 1.2 %collective-permute-start.16 = (bf16[16,32,256]{2,1,0:T(8,128)(2,1)S(1)}, bf16[16,32,256]{2,1,0:T(8,128)(2,1)S(1)}, u32[]{:S(2)}, u32[]{:S(2)}) collective-permute-start(bf16[16,32,256]{2,1,0:T(8,128)(2,1)S(1)} %get-tuple-element.72), channel_id=1, source_target_pairs={{0,4},{1,5},{2,6},{3,7},{4,0},{5,1},{6,2},{7,3},{8,12},{9,13},{10,... | collective-permute-start | bytes 786440 | tf_op jit(solution)/shard_map/left_11_and_products_back_0/ppermute | solution.py:245
  52.0 3.9 %collective-permute-done.20.rest_5_ = bf16[16,32,256]{2,1,0:T(8,128)(2,1)S(1)} collective-permute-done((bf16[16,32,256]{2,1,0:T(8,128)(2,1)S(1)}, bf16[16,32,256]{2,1,0:T(8,128)(2,1)S(1)}, u32[]{:S(2)}, u32[]{:S(2)}) %collective-permute-start.20) | collective-permute-done | bytes 262176 | tf_op jit(solution)/shard_map/end_right_11/ppermute | solution.py:245
  55.9 1.9 %collective-permute-start.22 = (bf16[16,32,256]{2,1,0:T(8,128)(2,1)S(1)}, bf16[16,32,256]{2,1,0:T(8,128)(2,1)S(1)}, u32[]{:S(2)}, u32[]{:S(2)}) collective-permute-start(bf16[16,32,256]{2,1,0:T(8,128)(2,1)S(1)} %collective-permute-done.20.rest_5_), channel_id=1, source_target_pairs={{0,1},{1,0},{2,3},{3,2},{4,8},{5,9},{6,10},{7,11},{8,4},{9,5},{10,... | collective-permute-start | bytes 786440 | tf_op jit(solution)/shard_map/mid_next_11/ppermute | solution.py:245
  57.8 0.6 near.2
  58.3 0.6 near.3
  58.9 2.6 %collective-permute-done.16.end.rest_3_ = bf16[16,32,256]{2,1,0:T(8,128)(2,1)S(1)} collective-permute-done((bf16[16,32,256]{2,1,0:T(8,128)(2,1)S(1)}, bf16[16,32,256]{2,1,0:T(8,128)(2,1)S(1)}, u32[]{:S(2)}, u32[]{:S(2)}) %collective-permute-start.16) | collective-permute-done | bytes 262176 | tf_op jit(solution)/shard_map/left_11_and_products_back_0/ppermute | solution.py:245
  61.5 0.1 hand_out.2
  61.6 0.0 copy-start.2
  61.6 0.0 copy-start.4
  61.6 0.0 collective-permute-done.22.rest_7_
  61.7 0.5 away.3
  62.2 1.2 %collective-permute-start.23 = (bf16[16,32,256]{2,1,0:T(8,128)(2,1)S(1)}, bf16[16,32,256]{2,1,0:T(8,128)(2,1)S(1)}, u32[]{:S(2)}, u32[]{:S(2)}) collective-permute-start(bf16[16,32,256]{2,1,0:T(8,128)(2,1)S(1)} %get-tuple-element.82), channel_id=1, source_target_pairs={{0,4},{1,5},{2,6},{3,7},{4,0},{5,1},{6,2},{7,3},{8,12},{9,13},{10,... | collective-permute-start | bytes 786440 | tf_op jit(solution)/shard_map/products_back_1/ppermute | solution.py:245
  63.4 3.4 %collective-permute-start.17 = (bf16[16,32,128]{2,1,0:T(8,128)(2,1)S(1)}, bf16[16,32,128]{2,1,0:T(8,128)(2,1)S(1)}, u32[]{:S(2)}, u32[]{:S(2)}) collective-permute-start(bf16[16,32,128]{2,1,0:T(8,128)(2,1)S(1)} %get-tuple-element.74), channel_id=1, source_target_pairs={{0,1},{1,0},{2,3},{3,2},{4,5},{5,4},{6,7},{7,6},{8,9},{9,8},{10,11... | collective-permute-start | bytes 393224 | tf_op jit(solution)/shard_map/return_01/ppermute | solution.py:245
  66.8 1.2 %collective-permute-start.18 = (bf16[16,32,128]{2,1,0:T(8,128)(2,1)S(1)}, bf16[16,32,128]{2,1,0:T(8,128)(2,1)S(1)}, u32[]{:S(2)}, u32[]{:S(2)}) collective-permute-start(bf16[16,32,128]{2,1,0:T(8,128)(2,1)S(1)} %get-tuple-element.75), channel_id=1, source_target_pairs={{0,2},{1,3},{2,0},{3,1},{4,6},{5,7},{6,4},{7,5},{8,10},{9,11},{10,... | collective-permute-start | bytes 393224 | tf_op jit(solution)/shard_map/return_02/ppermute | solution.py:245
  68.0 0.4 collective-permute-start.19
  68.4 0.0 collective-permute-done.23.end
  68.4 0.1 hand_out.3
  68.5 2.8 %collective-permute-start.24 = (bf16[16,32,128]{2,1,0:T(8,128)(2,1)S(1)}, bf16[16,32,128]{2,1,0:T(8,128)(2,1)S(1)}, u32[]{:S(2)}, u32[]{:S(2)}) collective-permute-start(bf16[16,32,128]{2,1,0:T(8,128)(2,1)S(1)} %get-tuple-element.84), channel_id=1, source_target_pairs={{0,1},{1,0},{2,3},{3,2},{4,5},{5,4},{6,7},{7,6},{8,9},{9,8},{10,11... | collective-permute-start | bytes 393224 | tf_op jit(solution)/shard_map/return_11/ppermute | solution.py:245
  71.3 1.3 %collective-permute-start.25 = (bf16[16,32,128]{2,1,0:T(8,128)(2,1)S(1)}, bf16[16,32,128]{2,1,0:T(8,128)(2,1)S(1)}, u32[]{:S(2)}, u32[]{:S(2)}) collective-permute-start(bf16[16,32,128]{2,1,0:T(8,128)(2,1)S(1)} %get-tuple-element.85), channel_id=1, source_target_pairs={{0,2},{1,3},{2,0},{3,1},{4,6},{5,7},{6,4},{7,5},{8,10},{9,11},{10,... | collective-permute-start | bytes 393224 | tf_op jit(solution)/shard_map/return_12/ppermute | solution.py:245
  72.6 0.5 collective-permute-start.26
  73.0 0.0 collective-permute-done.18.rest_2_
  73.0 2.2 %collective-permute-done.19.rest_3_ = bf16[16,32,128]{2,1,0:T(8,128)(2,1)S(1)} collective-permute-done((bf16[16,32,128]{2,1,0:T(8,128)(2,1)S(1)}, bf16[16,32,128]{2,1,0:T(8,128)(2,1)S(1)}, u32[]{:S(2)}, u32[]{:S(2)}) %collective-permute-start.19) | collective-permute-done | bytes 131104 | tf_op jit(solution)/shard_map/return_03/ppermute | solution.py:245
  75.2 0.0 collective-permute-done.24.rest_5_
  75.2 2.3 %collective-permute-done.25.rest_6_ = bf16[16,32,128]{2,1,0:T(8,128)(2,1)S(1)} collective-permute-done((bf16[16,32,128]{2,1,0:T(8,128)(2,1)S(1)}, bf16[16,32,128]{2,1,0:T(8,128)(2,1)S(1)}, u32[]{:S(2)}, u32[]{:S(2)}) %collective-permute-start.25) | collective-permute-done | bytes 131104 | tf_op jit(solution)/shard_map/return_12/ppermute | solution.py:245
  77.6 2.9 %collective-permute-done.26.rest_7_ = bf16[16,32,128]{2,1,0:T(8,128)(2,1)S(1)} collective-permute-done((bf16[16,32,128]{2,1,0:T(8,128)(2,1)S(1)}, bf16[16,32,128]{2,1,0:T(8,128)(2,1)S(1)}, u32[]{:S(2)}, u32[]{:S(2)}) %collective-permute-start.26) | collective-permute-done | bytes 131104 | tf_op jit(solution)/shard_map/return_13/ppermute | solution.py:245
  80.5 2.5 %update.1 = bf16[32,128,128]{2,1,0:T(8,128)(2,1)} custom-call(f32[1,128]{1,0:T(1,128)S(1)} %bitcast.2, bf16[128,128]{1,0:T(8,128)(2,1)S(1)} %copy-done.2, f32[32,128,128]{2,1,0:T(8,128)S(1)} %gate.1, bf16[16,32,128]{2,1,0:T(8,128)(2,1)S(1)} %get-tuple-element.73.rest_0_, bf16[16,32,128]{2,1,0:T(8,128)(2,1)S(1)} %collective-permute-done.17.rest_1_, ...), custom_call_target="tpu_custom_call" | custom-call | tf_op jit(solution)/shard_map/update/pallas_call | solution.py:217
  (11 shorter events, 0.0 us)
Async XLA Ops:
  0.0 1.6 %collective-permute-start.1 = (bf16[128,512]{1,0:T(8,128)(2,1)}, bf16[128,512]{1,0:T(8,128)(2,1)S(1)}, u32[]{:S(2)}, u32[]{:S(2)}) collective-permute-start(bf16[128,512]{1,0:T(8,128)(2,1)} %param.10), channel_id=1, source_target_pairs={{0,1},{1,0},{2,3},{3,2},{4,5},{5,4},{6,7},{7,6},{8,9},{9,8},{10,11... | collective-permute-start | bytes 393224 | tf_op jit(solution)/shard_map/weights/ppermute | solution.py:245
  0.1 1.5 %collective-permute-start = (f32[1,128]{1,0:T(1,128)}, f32[1,128]{1,0:T(1,128)S(1)}, u32[]{:S(2)}, u32[]{:S(2)}) collective-permute-start(f32[1,128]{1,0:T(1,128)} %bitcast.3), channel_id=1, source_target_pairs={{0,1},{1,0},{2,3},{3,2},{4,5},{5,4},{6,7},{7,6},{8,9},{9,8},{10,11... | collective-permute-start | bytes 1544 | tf_op jit(solution)/shard_map/gain/ppermute | solution.py:245
  1.6 6.6 %collective-permute-start.2 = (bf16[32,128,128]{2,1,0:T(8,128)(2,1)}, bf16[32,128,128]{2,1,0:T(8,128)(2,1)S(1)}, u32[]{:S(2)}, u32[]{:S(2)}) collective-permute-start(bf16[32,128,128]{2,1,0:T(8,128)(2,1)} %pair.1), channel_id=1, source_target_pairs={{0,1},{1,0},{2,3},{3,2},{4,5},{5,4},{6,7},{7,6},{8,9},{9,8},{10,11... | collective-permute-start | bytes 3145736 | tf_op jit(solution)/shard_map/pair/ppermute | solution.py:245
  1.8 6.3 %collective-permute-start.3 = (s32[32,128]{1,0:T(8,128)}, s32[32,128]{1,0:T(8,128)S(1)}, u32[]{:S(2)}, u32[]{:S(2)}) collective-permute-start(s32[32,128]{1,0:T(8,128)} %mask.1), channel_id=1, source_target_pairs={{0,1},{1,0},{2,3},{3,2},{4,5},{5,4},{6,7},{7,6},{8,9},{9,8},{10,11... | collective-permute-start | bytes 49160 | tf_op jit(solution)/shard_map/mask/ppermute | solution.py:245
  2.1 1.2 %copy-start = (bf16[32,128,128]{2,1,0:T(8,128)(2,1)S(1)}, bf16[32,128,128]{2,1,0:T(8,128)(2,1)}, u32[]{:S(2)}) copy-start(bf16[32,128,128]{2,1,0:T(8,128)(2,1)} %pair.1) | copy-start | bytes 3145732
  3.3 0.7 copy-start.3
  8.1 26.6 %copy-start.1 = (bf16[128,128]{1,0:T(8,128)(2,1)S(1)}, bf16[128,128]{1,0:T(8,128)(2,1)}, u32[]{:S(2)}) copy-start(bf16[128,128]{1,0:T(8,128)(2,1)} %weight.2) | copy-start | bytes 98308
  12.2 12.8 %collective-permute-start.5 = (bf16[32,32,256]{2,1,0:T(8,128)(2,1)S(1)}, bf16[32,32,256]{2,1,0:T(8,128)(2,1)S(1)}, u32[]{:S(2)}, u32[]{:S(2)}) collective-permute-start(bf16[32,32,256]{2,1,0:T(8,128)(2,1)S(1)} %get-tuple-element.60.rest_2_), channel_id=1, source_target_pairs={{0,1},{1,0},{2,3},{3,2},{4,8},{5,9},{6,10},{7,11},{8,4},{9,5},{10,... | collective-permute-start | bytes 1572872 | tf_op jit(solution)/shard_map/mid_own_0/ppermute | solution.py:245
  12.5 15.3 %collective-permute-start.7 = (bf16[32,32,256]{2,1,0:T(8,128)(2,1)S(1)}, bf16[32,32,256]{2,1,0:T(8,128)(2,1)S(1)}, u32[]{:S(2)}, u32[]{:S(2)}) collective-permute-start(bf16[32,32,256]{2,1,0:T(8,128)(2,1)S(1)} %get-tuple-element.60.rest_2_), channel_id=1, source_target_pairs={{0,4},{1,5},{2,6},{3,7},{4,0},{5,1},{6,2},{7,3},{8,12},{9,13},{10,... | collective-permute-start | bytes 1572872 | tf_op jit(solution)/shard_map/end_right_0/ppermute | solution.py:245
  16.1 7.0 %collective-permute-start.4 = (bf16[16,32,256]{2,1,0:T(8,128)(2,1)S(1)}, bf16[16,32,256]{2,1,0:T(8,128)(2,1)S(1)}, u32[]{:S(2)}, u32[]{:S(2)}) collective-permute-start(bf16[16,32,256]{2,1,0:T(8,128)(2,1)S(1)} %get-tuple-element.59), channel_id=1, source_target_pairs={{0,2},{1,3},{2,0},{3,1},{4,6},{5,7},{6,4},{7,5},{8,10},{9,11},{10,... | collective-permute-start | bytes 786440 | tf_op jit(solution)/shard_map/cross_right_0/ppermute | solution.py:245
  23.0 7.5 %collective-permute-start.11 = (bf16[16,32,256]{2,1,0:T(8,128)(2,1)S(1)}, bf16[16,32,256]{2,1,0:T(8,128)(2,1)S(1)}, u32[]{:S(2)}, u32[]{:S(2)}) collective-permute-start(bf16[16,32,256]{2,1,0:T(8,128)(2,1)S(1)} %collective-permute-done.4.rest_3_), channel_id=1, source_target_pairs={{0,1},{1,0},{2,3},{3,2},{4,8},{5,9},{6,10},{7,11},{8,4},{9,5},{10,... | collective-permute-start | bytes 786440 | tf_op jit(solution)/shard_map/mid_own_10/ppermute | solution.py:245
  24.8 8.6 %collective-permute-start.8 = (bf16[16,32,256]{2,1,0:T(8,128)(2,1)S(1)}, bf16[16,32,256]{2,1,0:T(8,128)(2,1)S(1)}, u32[]{:S(2)}, u32[]{:S(2)}) collective-permute-start(bf16[16,32,256]{2,1,0:T(8,128)(2,1)S(1)} %collective-permute-done.4.rest_3_), channel_id=1, source_target_pairs={{0,4},{1,5},{2,6},{3,7},{4,0},{5,1},{6,2},{7,3},{8,12},{9,13},{10,... | collective-permute-start | bytes 786440 | tf_op jit(solution)/shard_map/end_right_10/ppermute | solution.py:245
  25.1 8.4 %collective-permute-start.6 = (bf16[16,32,256]{2,1,0:T(8,128)(2,1)S(1)}, bf16[16,32,256]{2,1,0:T(8,128)(2,1)S(1)}, u32[]{:S(2)}, u32[]{:S(2)}) collective-permute-start(bf16[16,32,256]{2,1,0:T(8,128)(2,1)S(1)} %get-tuple-element.61), channel_id=1, source_target_pairs={{0,2},{1,3},{2,0},{3,1},{4,6},{5,7},{6,4},{7,5},{8,10},{9,11},{10,... | collective-permute-start | bytes 786440 | tf_op jit(solution)/shard_map/cross_left_0/ppermute | solution.py:245
  27.8 14.3 %collective-permute-start.12 = (bf16[32,32,256]{2,1,0:T(8,128)(2,1)S(1)}, bf16[32,32,256]{2,1,0:T(8,128)(2,1)S(1)}, u32[]{:S(2)}, u32[]{:S(2)}) collective-permute-start(bf16[32,32,256]{2,1,0:T(8,128)(2,1)S(1)} %collective-permute-done.7.rest_4_), channel_id=1, source_target_pairs={{0,1},{1,0},{2,3},{3,2},{4,8},{5,9},{6,10},{7,11},{8,4},{9,5},{10,... | collective-permute-start | bytes 1572872 | tf_op jit(solution)/shard_map/mid_next_0/ppermute | solution.py:245
  29.7 15.0 %collective-permute-start.9 = (bf16[32,32,256]{2,1,0:T(8,128)(2,1)S(1)}, bf16[32,32,256]{2,1,0:T(8,128)(2,1)S(1)}, u32[]{:S(2)}, u32[]{:S(2)}) collective-permute-start(bf16[32,32,256]{2,1,0:T(8,128)(2,1)S(1)} %get-tuple-element.78.rest_0_), channel_id=1, source_target_pairs={{0,4},{1,5},{2,6},{3,7},{4,0},{5,1},{6,2},{7,3},{8,12},{9,13},{10,... | collective-permute-start | bytes 1572872 | tf_op jit(solution)/shard_map/end_left_0/ppermute | solution.py:245
  33.4 5.9 %collective-permute-start.14 = (bf16[16,32,256]{2,1,0:T(8,128)(2,1)S(1)}, bf16[16,32,256]{2,1,0:T(8,128)(2,1)S(1)}, u32[]{:S(2)}, u32[]{:S(2)}) collective-permute-start(bf16[16,32,256]{2,1,0:T(8,128)(2,1)S(1)} %get-tuple-element.69), channel_id=1, source_target_pairs={{0,2},{1,3},{2,0},{3,1},{4,6},{5,7},{6,4},{7,5},{8,10},{9,11},{10,... | collective-permute-start | bytes 786440 | tf_op jit(solution)/shard_map/cross_right_1/ppermute | solution.py:245
  35.6 10.5 %collective-permute-start.13 = (bf16[16,32,256]{2,1,0:T(8,128)(2,1)S(1)}, bf16[16,32,256]{2,1,0:T(8,128)(2,1)S(1)}, u32[]{:S(2)}, u32[]{:S(2)}) collective-permute-start(bf16[16,32,256]{2,1,0:T(8,128)(2,1)S(1)} %collective-permute-done.8.rest_5_), channel_id=1, source_target_pairs={{0,1},{1,0},{2,3},{3,2},{4,8},{5,9},{6,10},{7,11},{8,4},{9,5},{10,... | collective-permute-start | bytes 786440 | tf_op jit(solution)/shard_map/mid_next_10/ppermute | solution.py:245
  37.8 12.5 %collective-permute-start.10 = (bf16[16,32,256]{2,1,0:T(8,128)(2,1)S(1)}, bf16[16,32,256]{2,1,0:T(8,128)(2,1)S(1)}, u32[]{:S(2)}, u32[]{:S(2)}) collective-permute-start(bf16[16,32,256]{2,1,0:T(8,128)(2,1)S(1)} %collective-permute-done.6.rest_1_), channel_id=1, source_target_pairs={{0,4},{1,5},{2,6},{3,7},{4,0},{5,1},{6,2},{7,3},{8,12},{9,13},{10,... | collective-permute-start | bytes 786440 | tf_op jit(solution)/shard_map/end_left_10/ppermute | solution.py:245
  39.4 12.7 %collective-permute-start.21 = (bf16[16,32,256]{2,1,0:T(8,128)(2,1)S(1)}, bf16[16,32,256]{2,1,0:T(8,128)(2,1)S(1)}, u32[]{:S(2)}, u32[]{:S(2)}) collective-permute-start(bf16[16,32,256]{2,1,0:T(8,128)(2,1)S(1)} %collective-permute-done.14.rest_3_), channel_id=1, source_target_pairs={{0,1},{1,0},{2,3},{3,2},{4,8},{5,9},{6,10},{7,11},{8,4},{9,5},{10,... | collective-permute-start | bytes 786440 | tf_op jit(solution)/shard_map/mid_own_11/ppermute | solution.py:245
  42.2 8.1 %collective-permute-start.15 = (bf16[16,32,256]{2,1,0:T(8,128)(2,1)S(1)}, bf16[16,32,256]{2,1,0:T(8,128)(2,1)S(1)}, u32[]{:S(2)}, u32[]{:S(2)}) collective-permute-start(bf16[16,32,256]{2,1,0:T(8,128)(2,1)S(1)} %get-tuple-element.70), channel_id=1, source_target_pairs={{0,2},{1,3},{2,0},{3,1},{4,6},{5,7},{6,4},{7,5},{8,10},{9,11},{10,... | collective-permute-start | bytes 786440 | tf_op jit(solution)/shard_map/cross_left_1/ppermute | solution.py:245
  44.7 11.2 %collective-permute-start.20 = (bf16[16,32,256]{2,1,0:T(8,128)(2,1)S(1)}, bf16[16,32,256]{2,1,0:T(8,128)(2,1)S(1)}, u32[]{:S(2)}, u32[]{:S(2)}) collective-permute-start(bf16[16,32,256]{2,1,0:T(8,128)(2,1)S(1)} %collective-permute-done.14.rest_3_), channel_id=1, source_target_pairs={{0,4},{1,5},{2,6},{3,7},{4,0},{5,1},{6,2},{7,3},{8,12},{9,13},{10,... | collective-permute-start | bytes 786440 | tf_op jit(solution)/shard_map/end_right_11/ppermute | solution.py:245
  50.8 10.7 %collective-permute-start.16 = (bf16[16,32,256]{2,1,0:T(8,128)(2,1)S(1)}, bf16[16,32,256]{2,1,0:T(8,128)(2,1)S(1)}, u32[]{:S(2)}, u32[]{:S(2)}) collective-permute-start(bf16[16,32,256]{2,1,0:T(8,128)(2,1)S(1)} %get-tuple-element.72), channel_id=1, source_target_pairs={{0,4},{1,5},{2,6},{3,7},{4,0},{5,1},{6,2},{7,3},{8,12},{9,13},{10,... | collective-permute-start | bytes 786440 | tf_op jit(solution)/shard_map/left_11_and_products_back_0/ppermute | solution.py:245
  55.9 5.7 %collective-permute-start.22 = (bf16[16,32,256]{2,1,0:T(8,128)(2,1)S(1)}, bf16[16,32,256]{2,1,0:T(8,128)(2,1)S(1)}, u32[]{:S(2)}, u32[]{:S(2)}) collective-permute-start(bf16[16,32,256]{2,1,0:T(8,128)(2,1)S(1)} %collective-permute-done.20.rest_5_), channel_id=1, source_target_pairs={{0,1},{1,0},{2,3},{3,2},{4,8},{5,9},{6,10},{7,11},{8,4},{9,5},{10,... | collective-permute-start | bytes 786440 | tf_op jit(solution)/shard_map/mid_next_11/ppermute | solution.py:245
  61.6 18.8 %copy-start.2 = (bf16[128,128]{1,0:T(8,128)(2,1)S(1)}, bf16[128,128]{1,0:T(8,128)(2,1)}, u32[]{:S(2)}) copy-start(bf16[128,128]{1,0:T(8,128)(2,1)} %weight.3) | copy-start | bytes 98308
  61.6 18.8 %copy-start.4 = (f32[128]{0:T(128)S(1)}, f32[128]{0:T(128)}, u32[]{:S(2)}) copy-start(f32[128]{0:T(128)} %param.12) | copy-start | bytes 1540
  62.2 6.2 %collective-permute-start.23 = (bf16[16,32,256]{2,1,0:T(8,128)(2,1)S(1)}, bf16[16,32,256]{2,1,0:T(8,128)(2,1)S(1)}, u32[]{:S(2)}, u32[]{:S(2)}) collective-permute-start(bf16[16,32,256]{2,1,0:T(8,128)(2,1)S(1)} %get-tuple-element.82), channel_id=1, source_target_pairs={{0,4},{1,5},{2,6},{3,7},{4,0},{5,1},{6,2},{7,3},{8,12},{9,13},{10,... | collective-permute-start | bytes 786440 | tf_op jit(solution)/shard_map/products_back_1/ppermute | solution.py:245
  63.4 9.2 %collective-permute-start.17 = (bf16[16,32,128]{2,1,0:T(8,128)(2,1)S(1)}, bf16[16,32,128]{2,1,0:T(8,128)(2,1)S(1)}, u32[]{:S(2)}, u32[]{:S(2)}) collective-permute-start(bf16[16,32,128]{2,1,0:T(8,128)(2,1)S(1)} %get-tuple-element.74), channel_id=1, source_target_pairs={{0,1},{1,0},{2,3},{3,2},{4,5},{5,4},{6,7},{7,6},{8,9},{9,8},{10,11... | collective-permute-start | bytes 393224 | tf_op jit(solution)/shard_map/return_01/ppermute | solution.py:245
  66.8 6.2 %collective-permute-start.18 = (bf16[16,32,128]{2,1,0:T(8,128)(2,1)S(1)}, bf16[16,32,128]{2,1,0:T(8,128)(2,1)S(1)}, u32[]{:S(2)}, u32[]{:S(2)}) collective-permute-start(bf16[16,32,128]{2,1,0:T(8,128)(2,1)S(1)} %get-tuple-element.75), channel_id=1, source_target_pairs={{0,2},{1,3},{2,0},{3,1},{4,6},{5,7},{6,4},{7,5},{8,10},{9,11},{10,... | collective-permute-start | bytes 393224 | tf_op jit(solution)/shard_map/return_02/ppermute | solution.py:245
  68.0 7.2 %collective-permute-start.19 = (bf16[16,32,128]{2,1,0:T(8,128)(2,1)S(1)}, bf16[16,32,128]{2,1,0:T(8,128)(2,1)S(1)}, u32[]{:S(2)}, u32[]{:S(2)}) collective-permute-start(bf16[16,32,128]{2,1,0:T(8,128)(2,1)S(1)} %get-tuple-element.76), channel_id=1, source_target_pairs={{0,3},{1,2},{2,1},{3,0},{4,7},{5,6},{6,5},{7,4},{8,11},{9,10},{10,... | collective-permute-start | bytes 393224 | tf_op jit(solution)/shard_map/return_03/ppermute | solution.py:245
  68.5 6.7 %collective-permute-start.24 = (bf16[16,32,128]{2,1,0:T(8,128)(2,1)S(1)}, bf16[16,32,128]{2,1,0:T(8,128)(2,1)S(1)}, u32[]{:S(2)}, u32[]{:S(2)}) collective-permute-start(bf16[16,32,128]{2,1,0:T(8,128)(2,1)S(1)} %get-tuple-element.84), channel_id=1, source_target_pairs={{0,1},{1,0},{2,3},{3,2},{4,5},{5,4},{6,7},{7,6},{8,9},{9,8},{10,11... | collective-permute-start | bytes 393224 | tf_op jit(solution)/shard_map/return_11/ppermute | solution.py:245
  71.3 6.2 %collective-permute-start.25 = (bf16[16,32,128]{2,1,0:T(8,128)(2,1)S(1)}, bf16[16,32,128]{2,1,0:T(8,128)(2,1)S(1)}, u32[]{:S(2)}, u32[]{:S(2)}) collective-permute-start(bf16[16,32,128]{2,1,0:T(8,128)(2,1)S(1)} %get-tuple-element.85), channel_id=1, source_target_pairs={{0,2},{1,3},{2,0},{3,1},{4,6},{5,7},{6,4},{7,5},{8,10},{9,11},{10,... | collective-permute-start | bytes 393224 | tf_op jit(solution)/shard_map/return_12/ppermute | solution.py:245
  72.6 7.9 %collective-permute-start.26 = (bf16[16,32,128]{2,1,0:T(8,128)(2,1)S(1)}, bf16[16,32,128]{2,1,0:T(8,128)(2,1)S(1)}, u32[]{:S(2)}, u32[]{:S(2)}) collective-permute-start(bf16[16,32,128]{2,1,0:T(8,128)(2,1)S(1)} %get-tuple-element.86), channel_id=1, source_target_pairs={{0,3},{1,2},{2,1},{3,0},{4,7},{5,6},{6,5},{7,4},{8,11},{9,10},{10,... | collective-permute-start | bytes 393224 | tf_op jit(solution)/shard_map/return_13/ppermute | solution.py:245

commit v14 on v12

--- a/solution.py
+++ b/solution.py
@@ -16,7 +16,7 @@
 TN = (((0,), (0,)), ((), ()))
 VMEM = pl.BlockSpec(memory_space=pltpu.VMEM)
 GROUP = 4
-UNROLL = 2
+UNROLL = 4
 
 
 def place():
@@ -189,7 +189,7 @@
                     ]
             base = base + piece.shape[0]
 
-    @pl.loop(0, rows, unroll=8)
+    @pl.loop(0, rows, unroll=16)
     def _(i):
         x = jnp.concatenate(
             [turned[m, pl.ds(i * pitch, hidden), :] for m in range(toks // LANES)], axis=1
@@ -360,7 +360,7 @@
     next1.append([mid("next_11", x, next1[0][-1], own1[1], away0) for x in near1[1]])
     swapped = send(swapped, edge, "left_11_and_products_back_0")
     pieces = hand_out(0, close[0], away0, swapped)
-    sides = [(after(left0, pieces[0]), left1[1]), (outer0, swapped)]
+    sides = [(after(left0, pieces[0], close[1]), left1[1]), (outer0, swapped)]
     away1, ends = products(True, first[1], sides, far_planes(1), "away")
     ends = send(ends, edge, "products_back_1")
     pieces += hand_out(1, close[1], away1, ends)

time: 80.6 us -> 78.8 us (0.978)
  Pallas kernels: 12.4 us -> 10.3 us
    pallas_call x11, Pallas kernels: 12.4 us -> 10.3 us  [call(): pl.pallas_call(body, out_shape=out_shape, in_specs=in_specs, out_specs=ou...]
  transfers between devices with their start and end apart: 25 -> 25, of which waited for: 11 -> 11; matrix products, arithmetic and copies ran while one was open for 0% -> 0% of each run, Pallas kernels for 9% -> 7%
where the time goes in v14:
time: 78.8 us; the launch traced here: 78.4 us
  starting transfers between devices  36.5 us (46%)
  waiting for transfers between devices  27.9 us (35%)
  Pallas kernels  10.3 us (13%)
  local copies, waits for them, and re-layouts  3.52 us (4%)
    ppermute x25, starting transfers between devices, send(): return lax.ppermute(x, ('row', 'chan'), pairs)  36.5 us
    ppermute x25, waiting for transfers between devices, send(): return lax.ppermute(x, ('row', 'chan'), pairs)  27.9 us
    pallas_call x11, Pallas kernels, call(): pl.pallas_call(body, out_shape=out_shape, in_specs=in_specs, out_specs=ou...  10.3 us
    unnamed x14, local copies, waits for them, and re-layouts  3.52 us
  transfers between devices with their start and end apart: 25, of which 11 were waited for; matrix products, arithmetic and copies ran while one was open for 0% of the time, Pallas kernels for 7%

profile of v14, /device:TPU:1, one launch (start us, length us, event | category | flops | bytes accessed | tf_op | source)
XLA Modules:
  0.0 78.4 jit_solution(4665782116780974808)
XLA Ops:
  0.0 0.1 collective-permute-start
  0.1 0.5 collective-permute-start.1
  0.5 1.2 %copy-done = bf16[32,128,128]{2,1,0:T(8,128)(2,1)S(1)} copy-done((bf16[32,128,128]{2,1,0:T(8,128)(2,1)S(1)}, bf16[32,128,128]{2,1,0:T(8,128)(2,1)}, u32[]{:S(2)}) %copy-start) | copy-done | bytes 1048600
  1.7 0.9 %copy-done.1 = bf16[128,512]{1,0:T(8,128)(2,1)S(1)} copy-done((bf16[128,512]{1,0:T(8,128)(2,1)S(1)}, bf16[128,512]{1,0:T(8,128)(2,1)}, u32[]{:S(2)}) %copy-start.1) | copy-done | bytes 131096
  2.6 0.7 copy-done.4
  3.4 0.7 copy-done.5
  4.0 1.9 %right_own.1 = (bf16[32,32,128]{2,1,0:T(8,128)(2,1)S(1)}, bf16[16,32,128]{2,1,0:T(8,128)(2,1)S(1)}, bf16[16,32,128]{2,1,0:T(8,128)(2,1)S(1)}, bf16[4096,128]{1,0...) custom-call(bf16[32,128,128]{2,1,0:T(8,128)(2,1)S(1)} %copy-done, ...), custom_call_target="tpu_custom_call" | custom-call | tf_op jit(solution)/shard_map/right_own/pallas_call | solution.py:211
  5.9 0.0 copy-start.2
  6.0 0.0 collective-permute-done.1.mask
  6.0 0.0 collective-permute-done.pair
  6.0 1.9 %right_twin.1 = (bf16[32,32,256]{2,1,0:T(8,128)(2,1)S(1)}, bf16[16,32,256]{2,1,0:T(8,128)(2,1)S(1)}, bf16[16,32,256]{2,1,0:T(8,128)(2,1)S(1)}, bf16[4096,128]{1,0:T(8,128)(2,1)S(1)}, f32[1,32,128]{2,1,0:T(8,128)S(1)}) custom-call(bf16[32,128,128]{2,1,0:T(8,128)(2,1)S(1)} %collective-permute-done.pair, s32[32,128]{1,0:T(8,128)S(1)} %collective-permute-done.1.mask, ...), custom_call_target="tpu_custom_call" | custom-call | tf_op jit(solution)/shard_map/right_twin/pallas_call | solution.py:211
  7.9 0.1 collective-permute-start.3
  8.0 3.5 %collective-permute-start.5 = (bf16[32,32,256]{2,1,0:T(8,128)(2,1)S(1)}, bf16[32,32,256]{2,1,0:T(8,128)(2,1)S(1)}, u32[]{:S(2)}, u32[]{:S(2)}) collective-permute-start(bf16[32,32,256]{2,1,0:T(8,128)(2,1)S(1)} %get-tuple-element.58.rest_2_), channel_id=1, source_target_pairs={{0,4},{1,5},{2,6},{3,7},{4,0},{5,1},{6,2},{7,3},{8,12},{9,13},{10,... | collective-permute-start | bytes 1572872 | tf_op jit(solution)/shard_map/end_right_0/ppermute | solution.py:239
  11.6 1.2 %collective-permute-start.2 = (bf16[16,32,256]{2,1,0:T(8,128)(2,1)S(1)}, bf16[16,32,256]{2,1,0:T(8,128)(2,1)S(1)}, u32[]{:S(2)}, u32[]{:S(2)}) collective-permute-start(bf16[16,32,256]{2,1,0:T(8,128)(2,1)S(1)} %get-tuple-element.57), channel_id=1, source_target_pairs={{0,2},{1,3},{2,0},{3,1},{4,6},{5,7},{6,4},{7,5},{8,10},{9,11},{10,... | collective-permute-start | bytes 786440 | tf_op jit(solution)/shard_map/cross_right_0/ppermute | solution.py:239
  12.8 1.3 %left.1 = (bf16[32,32,256]{2,1,0:T(8,128)(2,1)S(1)}, bf16[16,32,256]{2,1,0:T(8,128)(2,1)S(1)}, bf16[16,32,256]{2,1,0:T(8,128)(2,1)S(1)}) custom-call(bf16[4096,128]{1,0:T(8,128)(2,1)S(1)} %get-tuple-element.45.normed.normed0, bf16[4096,128]{1,0:T(8,128)(2,1)S(1)} %get-tuple-element.51.normed1, f32[1,32,128]{2,1,0:T(8,128)S(1)} %get-tuple-element.52.valid0, ...), custom_call_target="tpu_custom_call" | custom-call | tf_op jit(solution)/shard_map/left/pallas_call | solution.py:211
  14.2 4.1 %collective-permute-done.2.rest_3_ = bf16[16,32,256]{2,1,0:T(8,128)(2,1)S(1)} collective-permute-done((bf16[16,32,256]{2,1,0:T(8,128)(2,1)S(1)}, bf16[16,32,256]{2,1,0:T(8,128)(2,1)S(1)}, u32[]{:S(2)}, u32[]{:S(2)}) %collective-permute-start.2) | collective-permute-done | bytes 262176 | tf_op jit(solution)/shard_map/cross_right_0/ppermute | solution.py:239
  18.3 2.0 %collective-permute-start.9 = (bf16[16,32,256]{2,1,0:T(8,128)(2,1)S(1)}, bf16[16,32,256]{2,1,0:T(8,128)(2,1)S(1)}, u32[]{:S(2)}, u32[]{:S(2)}) collective-permute-start(bf16[16,32,256]{2,1,0:T(8,128)(2,1)S(1)} %collective-permute-done.2.rest_3_), channel_id=1, source_target_pairs={{0,1},{1,0},{2,3},{3,2},{4,8},{5,9},{6,10},{7,11},{8,4},{9,5},{10,... | collective-permute-start | bytes 786440 | tf_op jit(solution)/shard_map/mid_own_10/ppermute | solution.py:239
  20.3 0.6 collective-permute-start.6
  20.9 0.0 collective-permute-done.3.rest_4_
  20.9 1.2 %collective-permute-start.4 = (bf16[16,32,256]{2,1,0:T(8,128)(2,1)S(1)}, bf16[16,32,256]{2,1,0:T(8,128)(2,1)S(1)}, u32[]{:S(2)}, u32[]{:S(2)}) collective-permute-start(bf16[16,32,256]{2,1,0:T(8,128)(2,1)S(1)} %get-tuple-element.59), channel_id=1, source_target_pairs={{0,2},{1,3},{2,0},{3,1},{4,6},{5,7},{6,4},{7,5},{8,10},{9,11},{10,... | collective-permute-start | bytes 786440 | tf_op jit(solution)/shard_map/cross_left_0/ppermute | solution.py:239
  22.2 0.9 %collective-permute-done.5.rest_4_ = bf16[32,32,256]{2,1,0:T(8,128)(2,1)S(1)} collective-permute-done((bf16[32,32,256]{2,1,0:T(8,128)(2,1)S(1)}, bf16[32,32,256]{2,1,0:T(8,128)(2,1)S(1)}, u32[]{:S(2)}, u32[]{:S(2)}) %collective-permute-start.5) | collective-permute-done | bytes 524320 | tf_op jit(solution)/shard_map/end_right_0/ppermute | solution.py:239
  23.1 2.3 %collective-permute-start.10 = (bf16[32,32,256]{2,1,0:T(8,128)(2,1)S(1)}, bf16[32,32,256]{2,1,0:T(8,128)(2,1)S(1)}, u32[]{:S(2)}, u32[]{:S(2)}) collective-permute-start(bf16[32,32,256]{2,1,0:T(8,128)(2,1)S(1)} %collective-permute-done.5.rest_4_), channel_id=1, source_target_pairs={{0,1},{1,0},{2,3},{3,2},{4,8},{5,9},{6,10},{7,11},{8,4},{9,5},{10,... | collective-permute-start | bytes 1572872 | tf_op jit(solution)/shard_map/mid_next_0/ppermute | solution.py:239
  25.4 0.4 collective-permute-start.7
  25.8 0.0 collective-permute-done.9.rest_5_
  25.8 2.9 %collective-permute-done.6.rest_5_ = bf16[16,32,256]{2,1,0:T(8,128)(2,1)S(1)} collective-permute-done((bf16[16,32,256]{2,1,0:T(8,128)(2,1)S(1)}, bf16[16,32,256]{2,1,0:T(8,128)(2,1)S(1)}, u32[]{:S(2)}, u32[]{:S(2)}) %collective-permute-start.6) | collective-permute-done | bytes 262176 | tf_op jit(solution)/shard_map/end_right_10/ppermute | solution.py:239
  28.7 0.0 collective-permute-done.4.rest_1_
  28.7 1.2 %collective-permute-start.12 = (bf16[16,32,256]{2,1,0:T(8,128)(2,1)S(1)}, bf16[16,32,256]{2,1,0:T(8,128)(2,1)S(1)}, u32[]{:S(2)}, u32[]{:S(2)}) collective-permute-start(bf16[16,32,256]{2,1,0:T(8,128)(2,1)S(1)} %get-tuple-element.67), channel_id=1, source_target_pairs={{0,2},{1,3},{2,0},{3,1},{4,6},{5,7},{6,4},{7,5},{8,10},{9,11},{10,... | collective-permute-start | bytes 786440 | tf_op jit(solution)/shard_map/cross_right_1/ppermute | solution.py:239
  30.0 0.6 gate.1
  30.5 2.7 %collective-permute-start.11 = (bf16[16,32,256]{2,1,0:T(8,128)(2,1)S(1)}, bf16[16,32,256]{2,1,0:T(8,128)(2,1)S(1)}, u32[]{:S(2)}, u32[]{:S(2)}) collective-permute-start(bf16[16,32,256]{2,1,0:T(8,128)(2,1)S(1)} %collective-permute-done.6.rest_5_), channel_id=1, source_target_pairs={{0,1},{1,0},{2,3},{3,2},{4,8},{5,9},{6,10},{7,11},{8,4},{9,5},{10,... | collective-permute-start | bytes 786440 | tf_op jit(solution)/shard_map/mid_next_10/ppermute | solution.py:239
  33.2 0.0 collective-permute-start.8
  33.2 1.0 %collective-permute-done.12.rest_3_ = bf16[16,32,256]{2,1,0:T(8,128)(2,1)S(1)} collective-permute-done((bf16[16,32,256]{2,1,0:T(8,128)(2,1)S(1)}, bf16[16,32,256]{2,1,0:T(8,128)(2,1)S(1)}, u32[]{:S(2)}, u32[]{:S(2)}) %collective-permute-start.12) | collective-permute-done | bytes 262176 | tf_op jit(solution)/shard_map/cross_right_1/ppermute | solution.py:239
  34.2 3.2 %collective-permute-start.19 = (bf16[16,32,256]{2,1,0:T(8,128)(2,1)S(1)}, bf16[16,32,256]{2,1,0:T(8,128)(2,1)S(1)}, u32[]{:S(2)}, u32[]{:S(2)}) collective-permute-start(bf16[16,32,256]{2,1,0:T(8,128)(2,1)S(1)} %collective-permute-done.12.rest_3_), channel_id=1, source_target_pairs={{0,1},{1,0},{2,3},{3,2},{4,8},{5,9},{6,10},{7,11},{8,4},{9,5},{10,... | collective-permute-start | bytes 786440 | tf_op jit(solution)/shard_map/mid_own_11/ppermute | solution.py:239
  37.4 0.0 collective-permute-done.10.rest_6_
  37.4 1.2 %collective-permute-start.13 = (bf16[16,32,256]{2,1,0:T(8,128)(2,1)S(1)}, bf16[16,32,256]{2,1,0:T(8,128)(2,1)S(1)}, u32[]{:S(2)}, u32[]{:S(2)}) collective-permute-start(bf16[16,32,256]{2,1,0:T(8,128)(2,1)S(1)} %get-tuple-element.68), channel_id=1, source_target_pairs={{0,2},{1,3},{2,0},{3,1},{4,6},{5,7},{6,4},{7,5},{8,10},{9,11},{10,... | collective-permute-start | bytes 786440 | tf_op jit(solution)/shard_map/cross_left_1/ppermute | solution.py:239
  38.7 1.3 %collective-permute-done.7.rest_2_ = bf16[32,32,256]{2,1,0:T(8,128)(2,1)S(1)} collective-permute-done((bf16[32,32,256]{2,1,0:T(8,128)(2,1)S(1)}, bf16[32,32,256]{2,1,0:T(8,128)(2,1)S(1)}, u32[]{:S(2)}, u32[]{:S(2)}) %collective-permute-start.7) | collective-permute-done | bytes 524320 | tf_op jit(solution)/shard_map/end_left_0/ppermute | solution.py:239
  39.9 1.4 %collective-permute-start.18 = (bf16[16,32,256]{2,1,0:T(8,128)(2,1)S(1)}, bf16[16,32,256]{2,1,0:T(8,128)(2,1)S(1)}, u32[]{:S(2)}, u32[]{:S(2)}) collective-permute-start(bf16[16,32,256]{2,1,0:T(8,128)(2,1)S(1)} %collective-permute-done.12.rest_3_), channel_id=1, source_target_pairs={{0,4},{1,5},{2,6},{3,7},{4,0},{5,1},{6,2},{7,3},{8,12},{9,13},{10,... | collective-permute-start | bytes 786440 | tf_op jit(solution)/shard_map/end_right_11/ppermute | solution.py:239
  41.4 0.0 collective-permute-done.11.rest_7_
  41.4 4.2 %collective-permute-done.8.rest_3_ = bf16[16,32,256]{2,1,0:T(8,128)(2,1)S(1)} collective-permute-done((bf16[16,32,256]{2,1,0:T(8,128)(2,1)S(1)}, bf16[16,32,256]{2,1,0:T(8,128)(2,1)S(1)}, u32[]{:S(2)}, u32[]{:S(2)}) %collective-permute-start.8) | collective-permute-done | bytes 262176 | tf_op jit(solution)/shard_map/end_left_10/ppermute | solution.py:239
  45.6 0.0 collective-permute-done.13.rest_8_.rest_1_
  45.6 0.5 away.2
  46.1 1.2 %collective-permute-start.14 = (bf16[16,32,256]{2,1,0:T(8,128)(2,1)S(1)}, bf16[16,32,256]{2,1,0:T(8,128)(2,1)S(1)}, u32[]{:S(2)}, u32[]{:S(2)}) collective-permute-start(bf16[16,32,256]{2,1,0:T(8,128)(2,1)S(1)} %get-tuple-element.70), channel_id=1, source_target_pairs={{0,4},{1,5},{2,6},{3,7},{4,0},{5,1},{6,2},{7,3},{8,12},{9,13},{10,... | collective-permute-start | bytes 786440 | tf_op jit(solution)/shard_map/left_11_and_products_back_0/ppermute | solution.py:239
  47.3 0.0 collective-permute-done.19.rest_5_
  47.3 3.9 %collective-permute-done.18.rest_5_ = bf16[16,32,256]{2,1,0:T(8,128)(2,1)S(1)} collective-permute-done((bf16[16,32,256]{2,1,0:T(8,128)(2,1)S(1)}, bf16[16,32,256]{2,1,0:T(8,128)(2,1)S(1)}, u32[]{:S(2)}, u32[]{:S(2)}) %collective-permute-start.18) | collective-permute-done | bytes 262176 | tf_op jit(solution)/shard_map/end_right_11/ppermute | solution.py:239
  51.2 2.3 %collective-permute-start.20 = (bf16[16,32,256]{2,1,0:T(8,128)(2,1)S(1)}, bf16[16,32,256]{2,1,0:T(8,128)(2,1)S(1)}, u32[]{:S(2)}, u32[]{:S(2)}) collective-permute-start(bf16[16,32,256]{2,1,0:T(8,128)(2,1)S(1)} %collective-permute-done.18.rest_5_), channel_id=1, source_target_pairs={{0,1},{1,0},{2,3},{3,2},{4,8},{5,9},{6,10},{7,11},{8,4},{9,5},{10,... | collective-permute-start | bytes 786440 | tf_op jit(solution)/shard_map/mid_next_11/ppermute | solution.py:239
  53.5 0.6 near.2
  54.1 0.6 near.3
  54.6 2.2 %collective-permute-done.14.end.rest_3_ = bf16[16,32,256]{2,1,0:T(8,128)(2,1)S(1)} collective-permute-done((bf16[16,32,256]{2,1,0:T(8,128)(2,1)S(1)}, bf16[16,32,256]{2,1,0:T(8,128)(2,1)S(1)}, u32[]{:S(2)}, u32[]{:S(2)}) %collective-permute-start.14) | collective-permute-done | bytes 262176 | tf_op jit(solution)/shard_map/left_11_and_products_back_0/ppermute | solution.py:239
  56.8 0.1 hand_out.2
  56.9 0.0 copy-start.3
  56.9 0.0 copy-start.6
  56.9 0.0 collective-permute-done.20.rest_7_
  56.9 0.5 away.3
  57.5 1.2 %collective-permute-start.21 = (bf16[16,32,256]{2,1,0:T(8,128)(2,1)S(1)}, bf16[16,32,256]{2,1,0:T(8,128)(2,1)S(1)}, u32[]{:S(2)}, u32[]{:S(2)}) collective-permute-start(bf16[16,32,256]{2,1,0:T(8,128)(2,1)S(1)} %get-tuple-element.80), channel_id=1, source_target_pairs={{0,4},{1,5},{2,6},{3,7},{4,0},{5,1},{6,2},{7,3},{8,12},{9,13},{10,... | collective-permute-start | bytes 786440 | tf_op jit(solution)/shard_map/products_back_1/ppermute | solution.py:239
  58.7 3.9 %collective-permute-start.15 = (bf16[16,32,128]{2,1,0:T(8,128)(2,1)S(1)}, bf16[16,32,128]{2,1,0:T(8,128)(2,1)S(1)}, u32[]{:S(2)}, u32[]{:S(2)}) collective-permute-start(bf16[16,32,128]{2,1,0:T(8,128)(2,1)S(1)} %get-tuple-element.72), channel_id=1, source_target_pairs={{0,1},{1,0},{2,3},{3,2},{4,5},{5,4},{6,7},{7,6},{8,9},{9,8},{10,11... | collective-permute-start | bytes 393224 | tf_op jit(solution)/shard_map/return_01/ppermute | solution.py:239
  62.5 1.2 %collective-permute-start.16 = (bf16[16,32,128]{2,1,0:T(8,128)(2,1)S(1)}, bf16[16,32,128]{2,1,0:T(8,128)(2,1)S(1)}, u32[]{:S(2)}, u32[]{:S(2)}) collective-permute-start(bf16[16,32,128]{2,1,0:T(8,128)(2,1)S(1)} %get-tuple-element.73), channel_id=1, source_target_pairs={{0,2},{1,3},{2,0},{3,1},{4,6},{5,7},{6,4},{7,5},{8,10},{9,11},{10,... | collective-permute-start | bytes 393224 | tf_op jit(solution)/shard_map/return_02/ppermute | solution.py:239
  63.8 0.4 collective-permute-start.17
  64.2 0.1 hand_out.3
  64.3 2.8 %collective-permute-start.22 = (bf16[16,32,128]{2,1,0:T(8,128)(2,1)S(1)}, bf16[16,32,128]{2,1,0:T(8,128)(2,1)S(1)}, u32[]{:S(2)}, u32[]{:S(2)}) collective-permute-start(bf16[16,32,128]{2,1,0:T(8,128)(2,1)S(1)} %get-tuple-element.82), channel_id=1, source_target_pairs={{0,1},{1,0},{2,3},{3,2},{4,5},{5,4},{6,7},{7,6},{8,9},{9,8},{10,11... | collective-permute-start | bytes 393224 | tf_op jit(solution)/shard_map/return_11/ppermute | solution.py:239
  67.0 1.3 %collective-permute-start.23 = (bf16[16,32,128]{2,1,0:T(8,128)(2,1)S(1)}, bf16[16,32,128]{2,1,0:T(8,128)(2,1)S(1)}, u32[]{:S(2)}, u32[]{:S(2)}) collective-permute-start(bf16[16,32,128]{2,1,0:T(8,128)(2,1)S(1)} %get-tuple-element.83), channel_id=1, source_target_pairs={{0,2},{1,3},{2,0},{3,1},{4,6},{5,7},{6,4},{7,5},{8,10},{9,11},{10,... | collective-permute-start | bytes 393224 | tf_op jit(solution)/shard_map/return_12/ppermute | solution.py:239
  68.3 0.5 collective-permute-start.24
  68.8 2.2 %collective-permute-done.17.rest_3_ = bf16[16,32,128]{2,1,0:T(8,128)(2,1)S(1)} collective-permute-done((bf16[16,32,128]{2,1,0:T(8,128)(2,1)S(1)}, bf16[16,32,128]{2,1,0:T(8,128)(2,1)S(1)}, u32[]{:S(2)}, u32[]{:S(2)}) %collective-permute-start.17) | collective-permute-done | bytes 131104 | tf_op jit(solution)/shard_map/return_03/ppermute | solution.py:239
  70.9 2.3 %collective-permute-done.23.rest_6_ = bf16[16,32,128]{2,1,0:T(8,128)(2,1)S(1)} collective-permute-done((bf16[16,32,128]{2,1,0:T(8,128)(2,1)S(1)}, bf16[16,32,128]{2,1,0:T(8,128)(2,1)S(1)}, u32[]{:S(2)}, u32[]{:S(2)}) %collective-permute-start.23) | collective-permute-done | bytes 131104 | tf_op jit(solution)/shard_map/return_12/ppermute | solution.py:239
  73.3 2.9 %collective-permute-done.24.rest_7_ = bf16[16,32,128]{2,1,0:T(8,128)(2,1)S(1)} collective-permute-done((bf16[16,32,128]{2,1,0:T(8,128)(2,1)S(1)}, bf16[16,32,128]{2,1,0:T(8,128)(2,1)S(1)}, u32[]{:S(2)}, u32[]{:S(2)}) %collective-permute-start.24) | collective-permute-done | bytes 131104 | tf_op jit(solution)/shard_map/return_13/ppermute | solution.py:239
  76.2 2.2 %update.1 = bf16[32,128,128]{2,1,0:T(8,128)(2,1)} custom-call(f32[1,128]{1,0:T(1,128)S(1)} %bitcast.3, bf16[128,128]{1,0:T(8,128)(2,1)S(1)} %copy-done.3, f32[32,128,128]{2,1,0:T(8,128)S(1)} %gate.1, bf16[16,32,128]{2,1,0:T(8,128)(2,1)S(1)} %get-tuple-element.71.rest_0_, bf16[16,32,128]{2,1,0:T(8,128)(2,1)S(1)} %collective-permute-done.15.rest_1_, ...), custom_call_target="tpu_custom_call" | custom-call | tf_op jit(solution)/shard_map/update/pallas_call | solution.py:211
  (11 shorter events, 0.0 us)
Async XLA Ops:
  0.0 6.0 %collective-permute-start = (bf16[32,128,128]{2,1,0:T(8,128)(2,1)}, bf16[32,128,128]{2,1,0:T(8,128)(2,1)S(1)}, u32[]{:S(2)}, u32[]{:S(2)}) collective-permute-start(bf16[32,128,128]{2,1,0:T(8,128)(2,1)} %pair.1), channel_id=1, source_target_pairs={{0,1},{1,0},{2,3},{3,2},{4,5},{5,4},{6,7},{7,6},{8,9},{9,8},{10,11... | collective-permute-start | bytes 3145736 | tf_op jit(solution)/shard_map/pair/ppermute | solution.py:239
  0.1 5.9 %collective-permute-start.1 = (s32[32,128]{1,0:T(8,128)}, s32[32,128]{1,0:T(8,128)S(1)}, u32[]{:S(2)}, u32[]{:S(2)}) collective-permute-start(s32[32,128]{1,0:T(8,128)} %mask.1), channel_id=1, source_target_pairs={{0,1},{1,0},{2,3},{3,2},{4,5},{5,4},{6,7},{7,6},{8,9},{9,8},{10,11... | collective-permute-start | bytes 49160 | tf_op jit(solution)/shard_map/mask/ppermute | solution.py:239
  0.5 1.2 %copy-start = (bf16[32,128,128]{2,1,0:T(8,128)(2,1)S(1)}, bf16[32,128,128]{2,1,0:T(8,128)(2,1)}, u32[]{:S(2)}) copy-start(bf16[32,128,128]{2,1,0:T(8,128)(2,1)} %pair.1) | copy-start | bytes 3145732
  1.7 0.9 %copy-start.1 = (bf16[128,512]{1,0:T(8,128)(2,1)S(1)}, bf16[128,512]{1,0:T(8,128)(2,1)}, u32[]{:S(2)}) copy-start(bf16[128,512]{1,0:T(8,128)(2,1)} %weight.3) | copy-start | bytes 393220
  2.6 0.7 copy-start.4
  3.4 0.7 copy-start.5
  5.9 24.0 %copy-start.2 = (bf16[128,128]{1,0:T(8,128)(2,1)S(1)}, bf16[128,128]{1,0:T(8,128)(2,1)}, u32[]{:S(2)}) copy-start(bf16[128,128]{1,0:T(8,128)(2,1)} %weight.4) | copy-start | bytes 98308
  7.9 13.0 %collective-permute-start.3 = (bf16[32,32,256]{2,1,0:T(8,128)(2,1)S(1)}, bf16[32,32,256]{2,1,0:T(8,128)(2,1)S(1)}, u32[]{:S(2)}, u32[]{:S(2)}) collective-permute-start(bf16[32,32,256]{2,1,0:T(8,128)(2,1)S(1)} %get-tuple-element.58.rest_2_), channel_id=1, source_target_pairs={{0,1},{1,0},{2,3},{3,2},{4,8},{5,9},{6,10},{7,11},{8,4},{9,5},{10,... | collective-permute-start | bytes 1572872 | tf_op jit(solution)/shard_map/mid_own_0/ppermute | solution.py:239
  8.0 15.0 %collective-permute-start.5 = (bf16[32,32,256]{2,1,0:T(8,128)(2,1)S(1)}, bf16[32,32,256]{2,1,0:T(8,128)(2,1)S(1)}, u32[]{:S(2)}, u32[]{:S(2)}) collective-permute-start(bf16[32,32,256]{2,1,0:T(8,128)(2,1)S(1)} %get-tuple-element.58.rest_2_), channel_id=1, source_target_pairs={{0,4},{1,5},{2,6},{3,7},{4,0},{5,1},{6,2},{7,3},{8,12},{9,13},{10,... | collective-permute-start | bytes 1572872 | tf_op jit(solution)/shard_map/end_right_0/ppermute | solution.py:239
  11.6 6.7 %collective-permute-start.2 = (bf16[16,32,256]{2,1,0:T(8,128)(2,1)S(1)}, bf16[16,32,256]{2,1,0:T(8,128)(2,1)S(1)}, u32[]{:S(2)}, u32[]{:S(2)}) collective-permute-start(bf16[16,32,256]{2,1,0:T(8,128)(2,1)S(1)} %get-tuple-element.57), channel_id=1, source_target_pairs={{0,2},{1,3},{2,0},{3,1},{4,6},{5,7},{6,4},{7,5},{8,10},{9,11},{10,... | collective-permute-start | bytes 786440 | tf_op jit(solution)/shard_map/cross_right_0/ppermute | solution.py:239
  18.3 7.5 %collective-permute-start.9 = (bf16[16,32,256]{2,1,0:T(8,128)(2,1)S(1)}, bf16[16,32,256]{2,1,0:T(8,128)(2,1)S(1)}, u32[]{:S(2)}, u32[]{:S(2)}) collective-permute-start(bf16[16,32,256]{2,1,0:T(8,128)(2,1)S(1)} %collective-permute-done.2.rest_3_), channel_id=1, source_target_pairs={{0,1},{1,0},{2,3},{3,2},{4,8},{5,9},{6,10},{7,11},{8,4},{9,5},{10,... | collective-permute-start | bytes 786440 | tf_op jit(solution)/shard_map/mid_own_10/ppermute | solution.py:239
  20.3 8.4 %collective-permute-start.6 = (bf16[16,32,256]{2,1,0:T(8,128)(2,1)S(1)}, bf16[16,32,256]{2,1,0:T(8,128)(2,1)S(1)}, u32[]{:S(2)}, u32[]{:S(2)}) collective-permute-start(bf16[16,32,256]{2,1,0:T(8,128)(2,1)S(1)} %collective-permute-done.2.rest_3_), channel_id=1, source_target_pairs={{0,4},{1,5},{2,6},{3,7},{4,0},{5,1},{6,2},{7,3},{8,12},{9,13},{10,... | collective-permute-start | bytes 786440 | tf_op jit(solution)/shard_map/end_right_10/ppermute | solution.py:239
  20.9 7.8 %collective-permute-start.4 = (bf16[16,32,256]{2,1,0:T(8,128)(2,1)S(1)}, bf16[16,32,256]{2,1,0:T(8,128)(2,1)S(1)}, u32[]{:S(2)}, u32[]{:S(2)}) collective-permute-start(bf16[16,32,256]{2,1,0:T(8,128)(2,1)S(1)} %get-tuple-element.59), channel_id=1, source_target_pairs={{0,2},{1,3},{2,0},{3,1},{4,6},{5,7},{6,4},{7,5},{8,10},{9,11},{10,... | collective-permute-start | bytes 786440 | tf_op jit(solution)/shard_map/cross_left_0/ppermute | solution.py:239
  23.1 14.3 %collective-permute-start.10 = (bf16[32,32,256]{2,1,0:T(8,128)(2,1)S(1)}, bf16[32,32,256]{2,1,0:T(8,128)(2,1)S(1)}, u32[]{:S(2)}, u32[]{:S(2)}) collective-permute-start(bf16[32,32,256]{2,1,0:T(8,128)(2,1)S(1)} %collective-permute-done.5.rest_4_), channel_id=1, source_target_pairs={{0,1},{1,0},{2,3},{3,2},{4,8},{5,9},{6,10},{7,11},{8,4},{9,5},{10,... | collective-permute-start | bytes 1572872 | tf_op jit(solution)/shard_map/mid_next_0/ppermute | solution.py:239
  25.4 14.5 %collective-permute-start.7 = (bf16[32,32,256]{2,1,0:T(8,128)(2,1)S(1)}, bf16[32,32,256]{2,1,0:T(8,128)(2,1)S(1)}, u32[]{:S(2)}, u32[]{:S(2)}) collective-permute-start(bf16[32,32,256]{2,1,0:T(8,128)(2,1)S(1)} %get-tuple-element.76.rest_0_), channel_id=1, source_target_pairs={{0,4},{1,5},{2,6},{3,7},{4,0},{5,1},{6,2},{7,3},{8,12},{9,13},{10,... | collective-permute-start | bytes 1572872 | tf_op jit(solution)/shard_map/end_left_0/ppermute | solution.py:239
  28.7 5.5 %collective-permute-start.12 = (bf16[16,32,256]{2,1,0:T(8,128)(2,1)S(1)}, bf16[16,32,256]{2,1,0:T(8,128)(2,1)S(1)}, u32[]{:S(2)}, u32[]{:S(2)}) collective-permute-start(bf16[16,32,256]{2,1,0:T(8,128)(2,1)S(1)} %get-tuple-element.67), channel_id=1, source_target_pairs={{0,2},{1,3},{2,0},{3,1},{4,6},{5,7},{6,4},{7,5},{8,10},{9,11},{10,... | collective-permute-start | bytes 786440 | tf_op jit(solution)/shard_map/cross_right_1/ppermute | solution.py:239
  30.5 10.8 %collective-permute-start.11 = (bf16[16,32,256]{2,1,0:T(8,128)(2,1)S(1)}, bf16[16,32,256]{2,1,0:T(8,128)(2,1)S(1)}, u32[]{:S(2)}, u32[]{:S(2)}) collective-permute-start(bf16[16,32,256]{2,1,0:T(8,128)(2,1)S(1)} %collective-permute-done.6.rest_5_), channel_id=1, source_target_pairs={{0,1},{1,0},{2,3},{3,2},{4,8},{5,9},{6,10},{7,11},{8,4},{9,5},{10,... | collective-permute-start | bytes 786440 | tf_op jit(solution)/shard_map/mid_next_10/ppermute | solution.py:239
  33.2 12.4 %collective-permute-start.8 = (bf16[16,32,256]{2,1,0:T(8,128)(2,1)S(1)}, bf16[16,32,256]{2,1,0:T(8,128)(2,1)S(1)}, u32[]{:S(2)}, u32[]{:S(2)}) collective-permute-start(bf16[16,32,256]{2,1,0:T(8,128)(2,1)S(1)} %collective-permute-done.4.rest_1_), channel_id=1, source_target_pairs={{0,4},{1,5},{2,6},{3,7},{4,0},{5,1},{6,2},{7,3},{8,12},{9,13},{10,... | collective-permute-start | bytes 786440 | tf_op jit(solution)/shard_map/end_left_10/ppermute | solution.py:239
  34.2 13.1 %collective-permute-start.19 = (bf16[16,32,256]{2,1,0:T(8,128)(2,1)S(1)}, bf16[16,32,256]{2,1,0:T(8,128)(2,1)S(1)}, u32[]{:S(2)}, u32[]{:S(2)}) collective-permute-start(bf16[16,32,256]{2,1,0:T(8,128)(2,1)S(1)} %collective-permute-done.12.rest_3_), channel_id=1, source_target_pairs={{0,1},{1,0},{2,3},{3,2},{4,8},{5,9},{6,10},{7,11},{8,4},{9,5},{10,... | collective-permute-start | bytes 786440 | tf_op jit(solution)/shard_map/mid_own_11/ppermute | solution.py:239
  37.4 8.1 %collective-permute-start.13 = (bf16[16,32,256]{2,1,0:T(8,128)(2,1)S(1)}, bf16[16,32,256]{2,1,0:T(8,128)(2,1)S(1)}, u32[]{:S(2)}, u32[]{:S(2)}) collective-permute-start(bf16[16,32,256]{2,1,0:T(8,128)(2,1)S(1)} %get-tuple-element.68), channel_id=1, source_target_pairs={{0,2},{1,3},{2,0},{3,1},{4,6},{5,7},{6,4},{7,5},{8,10},{9,11},{10,... | collective-permute-start | bytes 786440 | tf_op jit(solution)/shard_map/cross_left_1/ppermute | solution.py:239
  39.9 11.2 %collective-permute-start.18 = (bf16[16,32,256]{2,1,0:T(8,128)(2,1)S(1)}, bf16[16,32,256]{2,1,0:T(8,128)(2,1)S(1)}, u32[]{:S(2)}, u32[]{:S(2)}) collective-permute-start(bf16[16,32,256]{2,1,0:T(8,128)(2,1)S(1)} %collective-permute-done.12.rest_3_), channel_id=1, source_target_pairs={{0,4},{1,5},{2,6},{3,7},{4,0},{5,1},{6,2},{7,3},{8,12},{9,13},{10,... | collective-permute-start | bytes 786440 | tf_op jit(solution)/shard_map/end_right_11/ppermute | solution.py:239
  46.1 10.7 %collective-permute-start.14 = (bf16[16,32,256]{2,1,0:T(8,128)(2,1)S(1)}, bf16[16,32,256]{2,1,0:T(8,128)(2,1)S(1)}, u32[]{:S(2)}, u32[]{:S(2)}) collective-permute-start(bf16[16,32,256]{2,1,0:T(8,128)(2,1)S(1)} %get-tuple-element.70), channel_id=1, source_target_pairs={{0,4},{1,5},{2,6},{3,7},{4,0},{5,1},{6,2},{7,3},{8,12},{9,13},{10,... | collective-permute-start | bytes 786440 | tf_op jit(solution)/shard_map/left_11_and_products_back_0/ppermute | solution.py:239
  51.2 5.7 %collective-permute-start.20 = (bf16[16,32,256]{2,1,0:T(8,128)(2,1)S(1)}, bf16[16,32,256]{2,1,0:T(8,128)(2,1)S(1)}, u32[]{:S(2)}, u32[]{:S(2)}) collective-permute-start(bf16[16,32,256]{2,1,0:T(8,128)(2,1)S(1)} %collective-permute-done.18.rest_5_), channel_id=1, source_target_pairs={{0,1},{1,0},{2,3},{3,2},{4,8},{5,9},{6,10},{7,11},{8,4},{9,5},{10,... | collective-permute-start | bytes 786440 | tf_op jit(solution)/shard_map/mid_next_11/ppermute | solution.py:239
  56.9 19.3 %copy-start.3 = (bf16[128,128]{1,0:T(8,128)(2,1)S(1)}, bf16[128,128]{1,0:T(8,128)(2,1)}, u32[]{:S(2)}) copy-start(bf16[128,128]{1,0:T(8,128)(2,1)} %weight.5) | copy-start | bytes 98308
  56.9 19.3 %copy-start.6 = (f32[128]{0:T(128)S(1)}, f32[128]{0:T(128)}, u32[]{:S(2)}) copy-start(f32[128]{0:T(128)} %param.12) | copy-start | bytes 1540
  57.5 6.7 %collective-permute-start.21 = (bf16[16,32,256]{2,1,0:T(8,128)(2,1)S(1)}, bf16[16,32,256]{2,1,0:T(8,128)(2,1)S(1)}, u32[]{:S(2)}, u32[]{:S(2)}) collective-permute-start(bf16[16,32,256]{2,1,0:T(8,128)(2,1)S(1)} %get-tuple-element.80), channel_id=1, source_target_pairs={{0,4},{1,5},{2,6},{3,7},{4,0},{5,1},{6,2},{7,3},{8,12},{9,13},{10,... | collective-permute-start | bytes 786440 | tf_op jit(solution)/shard_map/products_back_1/ppermute | solution.py:239
  58.7 9.6 %collective-permute-start.15 = (bf16[16,32,128]{2,1,0:T(8,128)(2,1)S(1)}, bf16[16,32,128]{2,1,0:T(8,128)(2,1)S(1)}, u32[]{:S(2)}, u32[]{:S(2)}) collective-permute-start(bf16[16,32,128]{2,1,0:T(8,128)(2,1)S(1)} %get-tuple-element.72), channel_id=1, source_target_pairs={{0,1},{1,0},{2,3},{3,2},{4,5},{5,4},{6,7},{7,6},{8,9},{9,8},{10,11... | collective-permute-start | bytes 393224 | tf_op jit(solution)/shard_map/return_01/ppermute | solution.py:239
  62.5 6.2 %collective-permute-start.16 = (bf16[16,32,128]{2,1,0:T(8,128)(2,1)S(1)}, bf16[16,32,128]{2,1,0:T(8,128)(2,1)S(1)}, u32[]{:S(2)}, u32[]{:S(2)}) collective-permute-start(bf16[16,32,128]{2,1,0:T(8,128)(2,1)S(1)} %get-tuple-element.73), channel_id=1, source_target_pairs={{0,2},{1,3},{2,0},{3,1},{4,6},{5,7},{6,4},{7,5},{8,10},{9,11},{10,... | collective-permute-start | bytes 393224 | tf_op jit(solution)/shard_map/return_02/ppermute | solution.py:239
  63.8 7.2 %collective-permute-start.17 = (bf16[16,32,128]{2,1,0:T(8,128)(2,1)S(1)}, bf16[16,32,128]{2,1,0:T(8,128)(2,1)S(1)}, u32[]{:S(2)}, u32[]{:S(2)}) collective-permute-start(bf16[16,32,128]{2,1,0:T(8,128)(2,1)S(1)} %get-tuple-element.74), channel_id=1, source_target_pairs={{0,3},{1,2},{2,1},{3,0},{4,7},{5,6},{6,5},{7,4},{8,11},{9,10},{10,... | collective-permute-start | bytes 393224 | tf_op jit(solution)/shard_map/return_03/ppermute | solution.py:239
  64.3 6.7 %collective-permute-start.22 = (bf16[16,32,128]{2,1,0:T(8,128)(2,1)S(1)}, bf16[16,32,128]{2,1,0:T(8,128)(2,1)S(1)}, u32[]{:S(2)}, u32[]{:S(2)}) collective-permute-start(bf16[16,32,128]{2,1,0:T(8,128)(2,1)S(1)} %get-tuple-element.82), channel_id=1, source_target_pairs={{0,1},{1,0},{2,3},{3,2},{4,5},{5,4},{6,7},{7,6},{8,9},{9,8},{10,11... | collective-permute-start | bytes 393224 | tf_op jit(solution)/shard_map/return_11/ppermute | solution.py:239
  67.0 6.2 %collective-permute-start.23 = (bf16[16,32,128]{2,1,0:T(8,128)(2,1)S(1)}, bf16[16,32,128]{2,1,0:T(8,128)(2,1)S(1)}, u32[]{:S(2)}, u32[]{:S(2)}) collective-permute-start(bf16[16,32,128]{2,1,0:T(8,128)(2,1)S(1)} %get-tuple-element.83), channel_id=1, source_target_pairs={{0,2},{1,3},{2,0},{3,1},{4,6},{5,7},{6,4},{7,5},{8,10},{9,11},{10,... | collective-permute-start | bytes 393224 | tf_op jit(solution)/shard_map/return_12/ppermute | solution.py:239
  68.3 7.9 %collective-permute-start.24 = (bf16[16,32,128]{2,1,0:T(8,128)(2,1)S(1)}, bf16[16,32,128]{2,1,0:T(8,128)(2,1)S(1)}, u32[]{:S(2)}, u32[]{:S(2)}) collective-permute-start(bf16[16,32,128]{2,1,0:T(8,128)(2,1)S(1)} %get-tuple-element.84), channel_id=1, source_target_pairs={{0,3},{1,2},{2,1},{3,0},{4,7},{5,6},{6,5},{7,4},{8,11},{9,10},{10,... | collective-permute-start | bytes 393224 | tf_op jit(solution)/shard_map/return_13/ppermute | solution.py:239

commit v15 on v14

--- a/solution.py
+++ b/solution.py
@@ -16,7 +16,7 @@
 TN = (((0,), (0,)), ((), ()))
 VMEM = pl.BlockSpec(memory_space=pltpu.VMEM)
 GROUP = 4
-UNROLL = 4
+UNROLL = 8
 
 
 def place():
@@ -67,7 +67,7 @@
 
 
 def right_own_kernel(pair, mask, gain, weight, *rest):
-    *outs, normed_out, chosen_right, chosen_left, valid, gain_out, turned, held = rest
+    out, normed_out, first, second, chosen_left, valid, gain_out, turned, held = rest
     gain_out[...] = gain[...]
     hidden = weight.shape[1] // 4
     part = hidden // 4
@@ -75,28 +75,29 @@
     turned[...] = weight[...].T
     valid[0] = mask[...].astype(F32) * 0.5
     for n in range(4):
-        chosen = chosen_left if n < 2 else chosen_right
         half = 0.5 if n % 2 == 0 else 1.0
         for p in range(2):
             start = pl.multiple_of(n * hidden + ((2 * y + core) ^ (2 * p)) * part, part)
-            at = (2 * (n % 2) + p) * part
-            chosen[at : at + part, :] = turned[pl.ds(start, part), :] * half
-    right_rows(pair, valid, gain, chosen_right, normed_out, held)
-    write_pieces(outs, held, 0)
-
-
-def right_twin_kernel(pair, mask, gain, chosen, *rest):
-    count = (len(rest) - 3) // 2
-    before, (*outs, normed_out, valid, held) = rest[:count], rest[count:]
-    for x, out in zip(before, outs):
-        out[:, :, : x.shape[2]] = x[...]
+            columns = turned[pl.ds(start, part), :] * half
+            if n < 2:
+                at = (2 * n + p) * part
+                chosen_left[at : at + part, :] = columns
+            else:
+                chosen = second if p else first
+                chosen[(n - 2) * part : (n - 1) * part, :] = columns
+    right_rows(pair, valid, gain, first, normed_out, held)
+    write_pieces([out], held, 0)
+
+
+def right_twin_kernel(pair, mask, gain, chosen, before, out, normed_out, valid, held):
+    out[:, :, : before.shape[2]] = before[...]
     valid[0] = mask[...].astype(F32) * 0.5
     right_rows(pair, valid, gain, chosen, normed_out, held)
-    write_pieces(outs, held, pair.shape[1])
-
-
-def left_kernel(normed0, normed1, valid0, valid1, chosen, *rest):
-    outs, held = rest[:-1], rest[-1]
+    write_pieces([out], held, pair.shape[1])
+
+
+def rows_kernel(normed0, normed1, valid0, valid1, chosen, *rest):
+    *outs, held = rest
     _, rows, toks = valid0.shape
     for n, (normed, valid) in enumerate(((normed0, valid0), (normed1, valid1))):
 
@@ -189,7 +190,7 @@
                     ]
             base = base + piece.shape[0]
 
-    @pl.loop(0, rows, unroll=16)
+    @pl.loop(0, rows, unroll=32)
     def _(i):
         x = jnp.concatenate(
             [turned[m, pl.ds(i * pitch, hidden), :] for m in range(toks // LANES)], axis=1
@@ -263,27 +264,37 @@
     def piece(count, height, depth):
         return jax.ShapeDtypeStruct((count, height, depth), BF16)
 
-    held = pltpu.VMEM((toks // LANES, 2 * part * (rows + 1), LANES), F32)
+    def columns(count):
+        return pltpu.VMEM((toks // LANES, count * (rows + 1), LANES), F32)
+
     rows_all = jax.ShapeDtypeStruct((rows * toks, channels), BF16)
-    weights = jax.ShapeDtypeStruct((4 * part, channels), BF16)
     valid_shape = jax.ShapeDtypeStruct((1, rows, toks), F32)
-    *mine, normed0, chosen_right, chosen_left, valid, gains = kernel(
+    weights = [jax.ShapeDtypeStruct((n * part, channels), BF16) for n in (2, 2, 4)]
+    before, normed0, first, second, chosen_left, valid, gains = kernel(
         right_own_kernel,
         "right_own",
-        [piece(count, rows, toks) for count in (part, *counts)]
-        + [rows_all, weights, weights, valid_shape, gains],
+        [piece(part, rows, toks), rows_all, *weights, valid_shape, gains],
         [VMEM] * 4,
-        [pltpu.VMEM((4 * hidden, channels), BF16), held],
+        [pltpu.VMEM((4 * hidden, channels), BF16), columns(part)],
     )(pair, pair_mask, gains, proj_weight)
-    whole = [piece(count, rows, 2 * toks) for count in (part, *counts)]
-    *right, normed1, twin_valid = kernel(
+    right0, normed1, twin_valid = kernel(
         right_twin_kernel,
         "right_twin",
-        whole + [rows_all, valid_shape],
-        [VMEM] * (4 + len(mine)),
-        [held],
-    )(twin, twin_mask, gains, chosen_right, *mine)
-    right0, right1 = right[0], list(right[1:])
+        [piece(part, rows, 2 * toks), rows_all, valid_shape],
+        [VMEM] * 5,
+        [columns(part)],
+    )(twin, twin_mask, gains, first, before)
+
+    def operand(chosen, shares, name):
+        return kernel(
+            rows_kernel,
+            name,
+            [piece(count, rows, 2 * toks) for count in shares],
+            [VMEM] * 5,
+            [columns(sum(shares))],
+        )(normed0, normed1, valid, twin_valid, chosen)
+
+    right1 = list(operand(second, counts, "right_neighbour"))
 
     def mid(name, x, *earlier):
         return send(after(x, *earlier), mirrored, f"mid_{name}")
@@ -301,10 +312,7 @@
     own0 = mid("own_0", right0)
     crossed = cross("right_0", right1[0])
     near0 = end_right("0", right0)
-    left = kernel(left_kernel, "left", whole, [VMEM] * 5, [held])(
-        normed0, normed1, valid, twin_valid, chosen_left
-    )
-    left0, left1 = left[0], list(left[1:])
+    left0, *left1 = operand(chosen_left, (part, *counts), "left")
     gate = kernel(
         gate_kernel, "gate", jax.ShapeDtypeStruct((rows, toks, channels), F32), [VMEM] * 2
     )(normed0, gate_weight)

time: 78.8 us -> 77.7 us (0.986)
  starting transfers between devices: 36.5 us -> 34.4 us
  waiting for transfers between devices: 27.9 us -> 29.5 us
    ppermute x25, starting transfers between devices: 36.5 us -> 34.4 us  [send(): return lax.ppermute(x, ('row', 'chan'), pairs)]
    ppermute x25, waiting for transfers between devices: 27.9 us -> 29.5 us  [send(): return lax.ppermute(x, ('row', 'chan'), pairs)]
    pallas_call x11 -> x12, Pallas kernels: 10.3 us -> 9.75 us  [call(): pl.pallas_call(body, out_shape=out_shape, in_specs=in_specs, out_specs=ou...]
  transfers between devices with their start and end apart: 25 -> 25, of which waited for: 11 -> 10; matrix products, arithmetic and copies ran while one was open for 0% -> 0% of each run, Pallas kernels for 7% -> 7%
where the time goes in v15:
time: 77.7 us; the launch traced here: 77.3 us
  starting transfers between devices  34.4 us (44%)
  waiting for transfers between devices  29.5 us (38%)
  Pallas kernels  9.75 us (13%)
  local copies, waits for them, and re-layouts  3.52 us (5%)
    ppermute x25, starting transfers between devices, send(): return lax.ppermute(x, ('row', 'chan'), pairs)  34.4 us
    ppermute x25, waiting for transfers between devices, send(): return lax.ppermute(x, ('row', 'chan'), pairs)  29.5 us
    pallas_call x12, Pallas kernels, call(): pl.pallas_call(body, out_shape=out_shape, in_specs=in_specs, out_specs=ou...  9.75 us
    unnamed x14, local copies, waits for them, and re-layouts  3.52 us
  transfers between devices with their start and end apart: 25, of which 10 were waited for; matrix products, arithmetic and copies ran while one was open for 0% of the time, Pallas kernels for 7%

profile of v15, /device:TPU:1, one launch (start us, length us, event | category | flops | bytes accessed | tf_op | source)
XLA Modules:
  0.0 77.3 jit_solution(11692824964464546251)
XLA Ops:
  0.0 0.1 collective-permute-start
  0.1 0.5 collective-permute-start.1
  0.5 1.2 %copy-done = bf16[32,128,128]{2,1,0:T(8,128)(2,1)S(1)} copy-done((bf16[32,128,128]{2,1,0:T(8,128)(2,1)S(1)}, bf16[32,128,128]{2,1,0:T(8,128)(2,1)}, u32[]{:S(2)}) %copy-start) | copy-done | bytes 1048600
  1.7 0.9 %copy-done.1 = bf16[128,512]{1,0:T(8,128)(2,1)S(1)} copy-done((bf16[128,512]{1,0:T(8,128)(2,1)S(1)}, bf16[128,512]{1,0:T(8,128)(2,1)}, u32[]{:S(2)}) %copy-start.1) | copy-done | bytes 131096
  2.6 0.7 copy-done.4
  3.4 0.7 copy-done.5
  4.0 1.5 %right_own.1 = (bf16[32,32,128]{2,1,0:T(8,128)(2,1)S(1)}, bf16[4096,128]{1,0:T(8,128)(2,1)S(1)}, bf16[64,128]{1,0:T(8,128)(2,1)S(1)}, bf16[64,128]{1,0:T(8,128)(...) custom-call(bf16[32,128,128]{2,1,0:T(8,128)(2,1)S(1)} %copy-done, ...), custom_call_target="tpu_custom_call" | custom-call | tf_op jit(solution)/shard_map/right_own/pallas_call | solution.py:212
  5.5 0.0 collective-permute-done.1.mask
  5.5 0.0 collective-permute-done.pair
  5.5 1.6 %right_twin.1 = (bf16[32,32,256]{2,1,0:T(8,128)(2,1)S(1)}, bf16[4096,128]{1,0:T(8,128)(2,1)S(1)}, f32[1,32,128]{2,1,0:T(8,128)S(1)}) custom-call(bf16[32,128,128]{2,1,0:T(8,128)(2,1)S(1)} %collective-permute-done.pair, s32[32,128]{1,0:T(8,128)S(1)} %collective-permute-done.1.mask, f32[1,128]{1,0:T(1,128)S(1)} %get-tuple-element.45.gain, ...), custom_call_target="tpu_custom_call" | custom-call | tf_op jit(solution)/shard_map/right_twin/pallas_call | solution.py:212
  7.1 0.1 collective-permute-start.3
  7.3 3.5 %collective-permute-start.5 = (bf16[32,32,256]{2,1,0:T(8,128)(2,1)S(1)}, bf16[32,32,256]{2,1,0:T(8,128)(2,1)S(1)}, u32[]{:S(2)}, u32[]{:S(2)}) collective-permute-start(bf16[32,32,256]{2,1,0:T(8,128)(2,1)S(1)} %get-tuple-element.56.rest_2_), channel_id=1, source_target_pairs={{0,4},{1,5},{2,6},{3,7},{4,0},{5,1},{6,2},{7,3},{8,12},{9,13},{10,... | collective-permute-start | bytes 1572872 | tf_op jit(solution)/shard_map/end_right_0/ppermute | solution.py:240
  10.8 0.9 %right_neighbour.1 = (bf16[16,32,256]{2,1,0:T(8,128)(2,1)S(1)}, bf16[16,32,256]{2,1,0:T(8,128)(2,1)S(1)}) custom-call(bf16[4096,128]{1,0:T(8,128)(2,1)S(1)} %get-tuple-element.44.normed.normed0, bf16[4096,128]{1,0:T(8,128)(2,1)S(1)} %get-tuple-element.48.normed1, f32[1,32,128]{2,1,0:T(8,128)S(1)} %get-tuple-element.49.valid0, ...), custom_call_target="tpu_custom_call" | custom-call | tf_op jit(solution)/shard_map/right_neighbour/pallas_call | solution.py:212
  11.7 1.3 %collective-permute-start.2 = (bf16[16,32,256]{2,1,0:T(8,128)(2,1)S(1)}, bf16[16,32,256]{2,1,0:T(8,128)(2,1)S(1)}, u32[]{:S(2)}, u32[]{:S(2)}) collective-permute-start(bf16[16,32,256]{2,1,0:T(8,128)(2,1)S(1)} %get-tuple-element.55), channel_id=1, source_target_pairs={{0,2},{1,3},{2,0},{3,1},{4,6},{5,7},{6,4},{7,5},{8,10},{9,11},{10,... | collective-permute-start | bytes 786440 | tf_op jit(solution)/shard_map/cross_right_0/ppermute | solution.py:240
  13.0 0.9 %left.1 = (bf16[32,32,256]{2,1,0:T(8,128)(2,1)S(1)}, bf16[16,32,256]{2,1,0:T(8,128)(2,1)S(1)}, bf16[16,32,256]{2,1,0:T(8,128)(2,1)S(1)}) custom-call(bf16[4096,128]{1,0:T(8,128)(2,1)S(1)} %get-tuple-element.44.normed.normed0, bf16[4096,128]{1,0:T(8,128)(2,1)S(1)} %get-tuple-element.48.normed1, f32[1,32,128]{2,1,0:T(8,128)S(1)} %get-tuple-element.49.valid0, ...), custom_call_target="tpu_custom_call" | custom-call | tf_op jit(solution)/shard_map/left/pallas_call | solution.py:212
  13.9 4.6 %collective-permute-done.2.rest_3_ = bf16[16,32,256]{2,1,0:T(8,128)(2,1)S(1)} collective-permute-done((bf16[16,32,256]{2,1,0:T(8,128)(2,1)S(1)}, bf16[16,32,256]{2,1,0:T(8,128)(2,1)S(1)}, u32[]{:S(2)}, u32[]{:S(2)}) %collective-permute-start.2) | collective-permute-done | bytes 262176 | tf_op jit(solution)/shard_map/cross_right_0/ppermute | solution.py:240
  18.5 2.0 %collective-permute-start.9 = (bf16[16,32,256]{2,1,0:T(8,128)(2,1)S(1)}, bf16[16,32,256]{2,1,0:T(8,128)(2,1)S(1)}, u32[]{:S(2)}, u32[]{:S(2)}) collective-permute-start(bf16[16,32,256]{2,1,0:T(8,128)(2,1)S(1)} %collective-permute-done.2.rest_3_), channel_id=1, source_target_pairs={{0,1},{1,0},{2,3},{3,2},{4,8},{5,9},{6,10},{7,11},{8,4},{9,5},{10,... | collective-permute-start | bytes 786440 | tf_op jit(solution)/shard_map/mid_own_10/ppermute | solution.py:240
  20.5 0.6 collective-permute-start.6
  21.1 0.0 collective-permute-done.3.rest_4_
  21.1 1.2 %collective-permute-start.4 = (bf16[16,32,256]{2,1,0:T(8,128)(2,1)S(1)}, bf16[16,32,256]{2,1,0:T(8,128)(2,1)S(1)}, u32[]{:S(2)}, u32[]{:S(2)}) collective-permute-start(bf16[16,32,256]{2,1,0:T(8,128)(2,1)S(1)} %get-tuple-element.57), channel_id=1, source_target_pairs={{0,2},{1,3},{2,0},{3,1},{4,6},{5,7},{6,4},{7,5},{8,10},{9,11},{10,... | collective-permute-start | bytes 786440 | tf_op jit(solution)/shard_map/cross_left_0/ppermute | solution.py:240
  22.4 0.0 collective-permute-done.5.rest_4_
  22.4 2.0 %collective-permute-start.10 = (bf16[32,32,256]{2,1,0:T(8,128)(2,1)S(1)}, bf16[32,32,256]{2,1,0:T(8,128)(2,1)S(1)}, u32[]{:S(2)}, u32[]{:S(2)}) collective-permute-start(bf16[32,32,256]{2,1,0:T(8,128)(2,1)S(1)} %collective-permute-done.5.rest_4_), channel_id=1, source_target_pairs={{0,1},{1,0},{2,3},{3,2},{4,8},{5,9},{6,10},{7,11},{8,4},{9,5},{10,... | collective-permute-start | bytes 1572872 | tf_op jit(solution)/shard_map/mid_next_0/ppermute | solution.py:240
  24.4 0.6 collective-permute-start.7
  25.0 3.1 %collective-permute-done.6.rest_5_ = bf16[16,32,256]{2,1,0:T(8,128)(2,1)S(1)} collective-permute-done((bf16[16,32,256]{2,1,0:T(8,128)(2,1)S(1)}, bf16[16,32,256]{2,1,0:T(8,128)(2,1)S(1)}, u32[]{:S(2)}, u32[]{:S(2)}) %collective-permute-start.6) | collective-permute-done | bytes 262176 | tf_op jit(solution)/shard_map/end_right_10/ppermute | solution.py:240
  28.1 1.2 %collective-permute-start.12 = (bf16[16,32,256]{2,1,0:T(8,128)(2,1)S(1)}, bf16[16,32,256]{2,1,0:T(8,128)(2,1)S(1)}, u32[]{:S(2)}, u32[]{:S(2)}) collective-permute-start(bf16[16,32,256]{2,1,0:T(8,128)(2,1)S(1)} %get-tuple-element.65), channel_id=1, source_target_pairs={{0,2},{1,3},{2,0},{3,1},{4,6},{5,7},{6,4},{7,5},{8,10},{9,11},{10,... | collective-permute-start | bytes 786440 | tf_op jit(solution)/shard_map/cross_right_1/ppermute | solution.py:240
  29.4 0.4 gate.1
  29.8 2.2 %collective-permute-start.11 = (bf16[16,32,256]{2,1,0:T(8,128)(2,1)S(1)}, bf16[16,32,256]{2,1,0:T(8,128)(2,1)S(1)}, u32[]{:S(2)}, u32[]{:S(2)}) collective-permute-start(bf16[16,32,256]{2,1,0:T(8,128)(2,1)S(1)} %collective-permute-done.6.rest_5_), channel_id=1, source_target_pairs={{0,1},{1,0},{2,3},{3,2},{4,8},{5,9},{6,10},{7,11},{8,4},{9,5},{10,... | collective-permute-start | bytes 786440 | tf_op jit(solution)/shard_map/mid_next_10/ppermute | solution.py:240
  32.0 2.1 %collective-permute-done.12.rest_3_ = bf16[16,32,256]{2,1,0:T(8,128)(2,1)S(1)} collective-permute-done((bf16[16,32,256]{2,1,0:T(8,128)(2,1)S(1)}, bf16[16,32,256]{2,1,0:T(8,128)(2,1)S(1)}, u32[]{:S(2)}, u32[]{:S(2)}) %collective-permute-start.12) | collective-permute-done | bytes 262176 | tf_op jit(solution)/shard_map/cross_right_1/ppermute | solution.py:240
  34.1 2.8 %collective-permute-start.19 = (bf16[16,32,256]{2,1,0:T(8,128)(2,1)S(1)}, bf16[16,32,256]{2,1,0:T(8,128)(2,1)S(1)}, u32[]{:S(2)}, u32[]{:S(2)}) collective-permute-start(bf16[16,32,256]{2,1,0:T(8,128)(2,1)S(1)} %collective-permute-done.12.rest_3_), channel_id=1, source_target_pairs={{0,1},{1,0},{2,3},{3,2},{4,8},{5,9},{6,10},{7,11},{8,4},{9,5},{10,... | collective-permute-start | bytes 786440 | tf_op jit(solution)/shard_map/mid_own_11/ppermute | solution.py:240
  36.9 0.0 collective-permute-done.10.rest_6_
  36.9 1.2 %collective-permute-start.13 = (bf16[16,32,256]{2,1,0:T(8,128)(2,1)S(1)}, bf16[16,32,256]{2,1,0:T(8,128)(2,1)S(1)}, u32[]{:S(2)}, u32[]{:S(2)}) collective-permute-start(bf16[16,32,256]{2,1,0:T(8,128)(2,1)S(1)} %get-tuple-element.66), channel_id=1, source_target_pairs={{0,2},{1,3},{2,0},{3,1},{4,6},{5,7},{6,4},{7,5},{8,10},{9,11},{10,... | collective-permute-start | bytes 786440 | tf_op jit(solution)/shard_map/cross_left_1/ppermute | solution.py:240
  38.1 1.3 %collective-permute-done.7.rest_2_ = bf16[32,32,256]{2,1,0:T(8,128)(2,1)S(1)} collective-permute-done((bf16[32,32,256]{2,1,0:T(8,128)(2,1)S(1)}, bf16[32,32,256]{2,1,0:T(8,128)(2,1)S(1)}, u32[]{:S(2)}, u32[]{:S(2)}) %collective-permute-start.7) | collective-permute-done | bytes 524320 | tf_op jit(solution)/shard_map/end_left_0/ppermute | solution.py:240
  39.4 1.2 %collective-permute-start.18 = (bf16[16,32,256]{2,1,0:T(8,128)(2,1)S(1)}, bf16[16,32,256]{2,1,0:T(8,128)(2,1)S(1)}, u32[]{:S(2)}, u32[]{:S(2)}) collective-permute-start(bf16[16,32,256]{2,1,0:T(8,128)(2,1)S(1)} %collective-permute-done.12.rest_3_), channel_id=1, source_target_pairs={{0,4},{1,5},{2,6},{3,7},{4,0},{5,1},{6,2},{7,3},{8,12},{9,13},{10,... | collective-permute-start | bytes 786440 | tf_op jit(solution)/shard_map/end_right_11/ppermute | solution.py:240
  40.6 0.0 collective-permute-done.11.rest_7_
  40.6 4.4 %collective-permute-done.8.rest_3_ = bf16[16,32,256]{2,1,0:T(8,128)(2,1)S(1)} collective-permute-done((bf16[16,32,256]{2,1,0:T(8,128)(2,1)S(1)}, bf16[16,32,256]{2,1,0:T(8,128)(2,1)S(1)}, u32[]{:S(2)}, u32[]{:S(2)}) %collective-permute-start.8) | collective-permute-done | bytes 262176 | tf_op jit(solution)/shard_map/end_left_10/ppermute | solution.py:240
  45.0 0.0 collective-permute-done.13.rest_8_.rest_1_
  45.0 0.5 away.2
  45.5 1.1 %collective-permute-start.14 = (bf16[16,32,256]{2,1,0:T(8,128)(2,1)S(1)}, bf16[16,32,256]{2,1,0:T(8,128)(2,1)S(1)}, u32[]{:S(2)}, u32[]{:S(2)}) collective-permute-start(bf16[16,32,256]{2,1,0:T(8,128)(2,1)S(1)} %get-tuple-element.68), channel_id=1, source_target_pairs={{0,4},{1,5},{2,6},{3,7},{4,0},{5,1},{6,2},{7,3},{8,12},{9,13},{10,... | collective-permute-start | bytes 786440 | tf_op jit(solution)/shard_map/left_11_and_products_back_0/ppermute | solution.py:240
  46.7 0.0 collective-permute-done.19.rest_5_
  46.7 3.9 %collective-permute-done.18.rest_5_ = bf16[16,32,256]{2,1,0:T(8,128)(2,1)S(1)} collective-permute-done((bf16[16,32,256]{2,1,0:T(8,128)(2,1)S(1)}, bf16[16,32,256]{2,1,0:T(8,128)(2,1)S(1)}, u32[]{:S(2)}, u32[]{:S(2)}) %collective-permute-start.18) | collective-permute-done | bytes 262176 | tf_op jit(solution)/shard_map/end_right_11/ppermute | solution.py:240
  50.6 1.9 %collective-permute-start.20 = (bf16[16,32,256]{2,1,0:T(8,128)(2,1)S(1)}, bf16[16,32,256]{2,1,0:T(8,128)(2,1)S(1)}, u32[]{:S(2)}, u32[]{:S(2)}) collective-permute-start(bf16[16,32,256]{2,1,0:T(8,128)(2,1)S(1)} %collective-permute-done.18.rest_5_), channel_id=1, source_target_pairs={{0,1},{1,0},{2,3},{3,2},{4,8},{5,9},{6,10},{7,11},{8,4},{9,5},{10,... | collective-permute-start | bytes 786440 | tf_op jit(solution)/shard_map/mid_next_11/ppermute | solution.py:240
  52.5 0.6 near.2
  53.1 0.6 near.3
  53.6 2.6 %collective-permute-done.14.end.rest_3_ = bf16[16,32,256]{2,1,0:T(8,128)(2,1)S(1)} collective-permute-done((bf16[16,32,256]{2,1,0:T(8,128)(2,1)S(1)}, bf16[16,32,256]{2,1,0:T(8,128)(2,1)S(1)}, u32[]{:S(2)}, u32[]{:S(2)}) %collective-permute-start.14) | collective-permute-done | bytes 262176 | tf_op jit(solution)/shard_map/left_11_and_products_back_0/ppermute | solution.py:240
  56.2 0.1 hand_out.2
  56.3 0.0 copy-start.3
  56.3 0.0 copy-start.6
  56.4 0.0 collective-permute-done.20.rest_7_
  56.4 0.5 away.3
  56.9 1.1 %collective-permute-start.21 = (bf16[16,32,256]{2,1,0:T(8,128)(2,1)S(1)}, bf16[16,32,256]{2,1,0:T(8,128)(2,1)S(1)}, u32[]{:S(2)}, u32[]{:S(2)}) collective-permute-start(bf16[16,32,256]{2,1,0:T(8,128)(2,1)S(1)} %get-tuple-element.78), channel_id=1, source_target_pairs={{0,4},{1,5},{2,6},{3,7},{4,0},{5,1},{6,2},{7,3},{8,12},{9,13},{10,... | collective-permute-start | bytes 786440 | tf_op jit(solution)/shard_map/products_back_1/ppermute | solution.py:240
  58.0 3.5 %collective-permute-start.15 = (bf16[16,32,128]{2,1,0:T(8,128)(2,1)S(1)}, bf16[16,32,128]{2,1,0:T(8,128)(2,1)S(1)}, u32[]{:S(2)}, u32[]{:S(2)}) collective-permute-start(bf16[16,32,128]{2,1,0:T(8,128)(2,1)S(1)} %get-tuple-element.70), channel_id=1, source_target_pairs={{0,1},{1,0},{2,3},{3,2},{4,5},{5,4},{6,7},{7,6},{8,9},{9,8},{10,11... | collective-permute-start | bytes 393224 | tf_op jit(solution)/shard_map/return_01/ppermute | solution.py:240
  61.6 1.2 %collective-permute-start.16 = (bf16[16,32,128]{2,1,0:T(8,128)(2,1)S(1)}, bf16[16,32,128]{2,1,0:T(8,128)(2,1)S(1)}, u32[]{:S(2)}, u32[]{:S(2)}) collective-permute-start(bf16[16,32,128]{2,1,0:T(8,128)(2,1)S(1)} %get-tuple-element.71), channel_id=1, source_target_pairs={{0,2},{1,3},{2,0},{3,1},{4,6},{5,7},{6,4},{7,5},{8,10},{9,11},{10,... | collective-permute-start | bytes 393224 | tf_op jit(solution)/shard_map/return_02/ppermute | solution.py:240
  62.8 0.4 collective-permute-start.17
  63.2 0.0 collective-permute-done.21.end
  63.2 0.1 hand_out.3
  63.3 2.8 %collective-permute-start.22 = (bf16[16,32,128]{2,1,0:T(8,128)(2,1)S(1)}, bf16[16,32,128]{2,1,0:T(8,128)(2,1)S(1)}, u32[]{:S(2)}, u32[]{:S(2)}) collective-permute-start(bf16[16,32,128]{2,1,0:T(8,128)(2,1)S(1)} %get-tuple-element.80), channel_id=1, source_target_pairs={{0,1},{1,0},{2,3},{3,2},{4,5},{5,4},{6,7},{7,6},{8,9},{9,8},{10,11... | collective-permute-start | bytes 393224 | tf_op jit(solution)/shard_map/return_11/ppermute | solution.py:240
  66.1 1.3 %collective-permute-start.23 = (bf16[16,32,128]{2,1,0:T(8,128)(2,1)S(1)}, bf16[16,32,128]{2,1,0:T(8,128)(2,1)S(1)}, u32[]{:S(2)}, u32[]{:S(2)}) collective-permute-start(bf16[16,32,128]{2,1,0:T(8,128)(2,1)S(1)} %get-tuple-element.81), channel_id=1, source_target_pairs={{0,2},{1,3},{2,0},{3,1},{4,6},{5,7},{6,4},{7,5},{8,10},{9,11},{10,... | collective-permute-start | bytes 393224 | tf_op jit(solution)/shard_map/return_12/ppermute | solution.py:240
  67.3 0.5 collective-permute-start.24
  67.8 0.0 collective-permute-done.16.rest_2_
  67.8 2.2 %collective-permute-done.17.rest_3_ = bf16[16,32,128]{2,1,0:T(8,128)(2,1)S(1)} collective-permute-done((bf16[16,32,128]{2,1,0:T(8,128)(2,1)S(1)}, bf16[16,32,128]{2,1,0:T(8,128)(2,1)S(1)}, u32[]{:S(2)}, u32[]{:S(2)}) %collective-permute-start.17) | collective-permute-done | bytes 131104 | tf_op jit(solution)/shard_map/return_03/ppermute | solution.py:240
  70.0 0.0 collective-permute-done.22.rest_5_
  70.0 2.3 %collective-permute-done.23.rest_6_ = bf16[16,32,128]{2,1,0:T(8,128)(2,1)S(1)} collective-permute-done((bf16[16,32,128]{2,1,0:T(8,128)(2,1)S(1)}, bf16[16,32,128]{2,1,0:T(8,128)(2,1)S(1)}, u32[]{:S(2)}, u32[]{:S(2)}) %collective-permute-start.23) | collective-permute-done | bytes 131104 | tf_op jit(solution)/shard_map/return_12/ppermute | solution.py:240
  72.3 2.9 %collective-permute-done.24.rest_7_ = bf16[16,32,128]{2,1,0:T(8,128)(2,1)S(1)} collective-permute-done((bf16[16,32,128]{2,1,0:T(8,128)(2,1)S(1)}, bf16[16,32,128]{2,1,0:T(8,128)(2,1)S(1)}, u32[]{:S(2)}, u32[]{:S(2)}) %collective-permute-start.24) | collective-permute-done | bytes 131104 | tf_op jit(solution)/shard_map/return_13/ppermute | solution.py:240
  75.2 2.0 %update.1 = bf16[32,128,128]{2,1,0:T(8,128)(2,1)} custom-call(f32[1,128]{1,0:T(1,128)S(1)} %bitcast.3, bf16[128,128]{1,0:T(8,128)(2,1)S(1)} %copy-done.3, f32[32,128,128]{2,1,0:T(8,128)S(1)} %gate.1, bf16[16,32,128]{2,1,0:T(8,128)(2,1)S(1)} %get-tuple-element.69.rest_0_, bf16[16,32,128]{2,1,0:T(8,128)(2,1)S(1)} %collective-permute-done.15.rest_1_, ...), custom_call_target="tpu_custom_call" | custom-call | tf_op jit(solution)/shard_map/update/pallas_call | solution.py:212
  (12 shorter events, 0.0 us)
Async XLA Ops:
  0.0 5.5 %collective-permute-start = (bf16[32,128,128]{2,1,0:T(8,128)(2,1)}, bf16[32,128,128]{2,1,0:T(8,128)(2,1)S(1)}, u32[]{:S(2)}, u32[]{:S(2)}) collective-permute-start(bf16[32,128,128]{2,1,0:T(8,128)(2,1)} %pair.1), channel_id=1, source_target_pairs={{0,1},{1,0},{2,3},{3,2},{4,5},{5,4},{6,7},{7,6},{8,9},{9,8},{10,11... | collective-permute-start | bytes 3145736 | tf_op jit(solution)/shard_map/pair/ppermute | solution.py:240
  0.1 5.5 %collective-permute-start.1 = (s32[32,128]{1,0:T(8,128)}, s32[32,128]{1,0:T(8,128)S(1)}, u32[]{:S(2)}, u32[]{:S(2)}) collective-permute-start(s32[32,128]{1,0:T(8,128)} %mask.1), channel_id=1, source_target_pairs={{0,1},{1,0},{2,3},{3,2},{4,5},{5,4},{6,7},{7,6},{8,9},{9,8},{10,11... | collective-permute-start | bytes 49160 | tf_op jit(solution)/shard_map/mask/ppermute | solution.py:240
  0.5 1.2 %copy-start = (bf16[32,128,128]{2,1,0:T(8,128)(2,1)S(1)}, bf16[32,128,128]{2,1,0:T(8,128)(2,1)}, u32[]{:S(2)}) copy-start(bf16[32,128,128]{2,1,0:T(8,128)(2,1)} %pair.1) | copy-start | bytes 3145732
  1.7 0.9 %copy-start.1 = (bf16[128,512]{1,0:T(8,128)(2,1)S(1)}, bf16[128,512]{1,0:T(8,128)(2,1)}, u32[]{:S(2)}) copy-start(bf16[128,512]{1,0:T(8,128)(2,1)} %weight.3) | copy-start | bytes 393220
  2.6 0.7 copy-start.4
  3.4 0.7 copy-start.5
  7.1 14.0 %collective-permute-start.3 = (bf16[32,32,256]{2,1,0:T(8,128)(2,1)S(1)}, bf16[32,32,256]{2,1,0:T(8,128)(2,1)S(1)}, u32[]{:S(2)}, u32[]{:S(2)}) collective-permute-start(bf16[32,32,256]{2,1,0:T(8,128)(2,1)S(1)} %get-tuple-element.56.rest_2_), channel_id=1, source_target_pairs={{0,1},{1,0},{2,3},{3,2},{4,8},{5,9},{6,10},{7,11},{8,4},{9,5},{10,... | collective-permute-start | bytes 1572872 | tf_op jit(solution)/shard_map/mid_own_0/ppermute | solution.py:240
  7.3 15.1 %collective-permute-start.5 = (bf16[32,32,256]{2,1,0:T(8,128)(2,1)S(1)}, bf16[32,32,256]{2,1,0:T(8,128)(2,1)S(1)}, u32[]{:S(2)}, u32[]{:S(2)}) collective-permute-start(bf16[32,32,256]{2,1,0:T(8,128)(2,1)S(1)} %get-tuple-element.56.rest_2_), channel_id=1, source_target_pairs={{0,4},{1,5},{2,6},{3,7},{4,0},{5,1},{6,2},{7,3},{8,12},{9,13},{10,... | collective-permute-start | bytes 1572872 | tf_op jit(solution)/shard_map/end_right_0/ppermute | solution.py:240
  10.8 18.6 %copy-start.2 = (bf16[128,128]{1,0:T(8,128)(2,1)S(1)}, bf16[128,128]{1,0:T(8,128)(2,1)}, u32[]{:S(2)}) copy-start(bf16[128,128]{1,0:T(8,128)(2,1)} %weight.4) | copy-start | bytes 98308
  11.7 6.8 %collective-permute-start.2 = (bf16[16,32,256]{2,1,0:T(8,128)(2,1)S(1)}, bf16[16,32,256]{2,1,0:T(8,128)(2,1)S(1)}, u32[]{:S(2)}, u32[]{:S(2)}) collective-permute-start(bf16[16,32,256]{2,1,0:T(8,128)(2,1)S(1)} %get-tuple-element.55), channel_id=1, source_target_pairs={{0,2},{1,3},{2,0},{3,1},{4,6},{5,7},{6,4},{7,5},{8,10},{9,11},{10,... | collective-permute-start | bytes 786440 | tf_op jit(solution)/shard_map/cross_right_0/ppermute | solution.py:240
  18.5 6.5 %collective-permute-start.9 = (bf16[16,32,256]{2,1,0:T(8,128)(2,1)S(1)}, bf16[16,32,256]{2,1,0:T(8,128)(2,1)S(1)}, u32[]{:S(2)}, u32[]{:S(2)}) collective-permute-start(bf16[16,32,256]{2,1,0:T(8,128)(2,1)S(1)} %collective-permute-done.2.rest_3_), channel_id=1, source_target_pairs={{0,1},{1,0},{2,3},{3,2},{4,8},{5,9},{6,10},{7,11},{8,4},{9,5},{10,... | collective-permute-start | bytes 786440 | tf_op jit(solution)/shard_map/mid_own_10/ppermute | solution.py:240
  20.5 7.6 %collective-permute-start.6 = (bf16[16,32,256]{2,1,0:T(8,128)(2,1)S(1)}, bf16[16,32,256]{2,1,0:T(8,128)(2,1)S(1)}, u32[]{:S(2)}, u32[]{:S(2)}) collective-permute-start(bf16[16,32,256]{2,1,0:T(8,128)(2,1)S(1)} %collective-permute-done.2.rest_3_), channel_id=1, source_target_pairs={{0,4},{1,5},{2,6},{3,7},{4,0},{5,1},{6,2},{7,3},{8,12},{9,13},{10,... | collective-permute-start | bytes 786440 | tf_op jit(solution)/shard_map/end_right_10/ppermute | solution.py:240
  21.1 7.0 %collective-permute-start.4 = (bf16[16,32,256]{2,1,0:T(8,128)(2,1)S(1)}, bf16[16,32,256]{2,1,0:T(8,128)(2,1)S(1)}, u32[]{:S(2)}, u32[]{:S(2)}) collective-permute-start(bf16[16,32,256]{2,1,0:T(8,128)(2,1)S(1)} %get-tuple-element.57), channel_id=1, source_target_pairs={{0,2},{1,3},{2,0},{3,1},{4,6},{5,7},{6,4},{7,5},{8,10},{9,11},{10,... | collective-permute-start | bytes 786440 | tf_op jit(solution)/shard_map/cross_left_0/ppermute | solution.py:240
  22.4 14.5 %collective-permute-start.10 = (bf16[32,32,256]{2,1,0:T(8,128)(2,1)S(1)}, bf16[32,32,256]{2,1,0:T(8,128)(2,1)S(1)}, u32[]{:S(2)}, u32[]{:S(2)}) collective-permute-start(bf16[32,32,256]{2,1,0:T(8,128)(2,1)S(1)} %collective-permute-done.5.rest_4_), channel_id=1, source_target_pairs={{0,1},{1,0},{2,3},{3,2},{4,8},{5,9},{6,10},{7,11},{8,4},{9,5},{10,... | collective-permute-start | bytes 1572872 | tf_op jit(solution)/shard_map/mid_next_0/ppermute | solution.py:240
  24.4 15.0 %collective-permute-start.7 = (bf16[32,32,256]{2,1,0:T(8,128)(2,1)S(1)}, bf16[32,32,256]{2,1,0:T(8,128)(2,1)S(1)}, u32[]{:S(2)}, u32[]{:S(2)}) collective-permute-start(bf16[32,32,256]{2,1,0:T(8,128)(2,1)S(1)} %get-tuple-element.74.rest_0_), channel_id=1, source_target_pairs={{0,4},{1,5},{2,6},{3,7},{4,0},{5,1},{6,2},{7,3},{8,12},{9,13},{10,... | collective-permute-start | bytes 1572872 | tf_op jit(solution)/shard_map/end_left_0/ppermute | solution.py:240
  28.1 5.9 %collective-permute-start.12 = (bf16[16,32,256]{2,1,0:T(8,128)(2,1)S(1)}, bf16[16,32,256]{2,1,0:T(8,128)(2,1)S(1)}, u32[]{:S(2)}, u32[]{:S(2)}) collective-permute-start(bf16[16,32,256]{2,1,0:T(8,128)(2,1)S(1)} %get-tuple-element.65), channel_id=1, source_target_pairs={{0,2},{1,3},{2,0},{3,1},{4,6},{5,7},{6,4},{7,5},{8,10},{9,11},{10,... | collective-permute-start | bytes 786440 | tf_op jit(solution)/shard_map/cross_right_1/ppermute | solution.py:240
  29.8 10.7 %collective-permute-start.11 = (bf16[16,32,256]{2,1,0:T(8,128)(2,1)S(1)}, bf16[16,32,256]{2,1,0:T(8,128)(2,1)S(1)}, u32[]{:S(2)}, u32[]{:S(2)}) collective-permute-start(bf16[16,32,256]{2,1,0:T(8,128)(2,1)S(1)} %collective-permute-done.6.rest_5_), channel_id=1, source_target_pairs={{0,1},{1,0},{2,3},{3,2},{4,8},{5,9},{6,10},{7,11},{8,4},{9,5},{10,... | collective-permute-start | bytes 786440 | tf_op jit(solution)/shard_map/mid_next_10/ppermute | solution.py:240
  32.0 13.0 %collective-permute-start.8 = (bf16[16,32,256]{2,1,0:T(8,128)(2,1)S(1)}, bf16[16,32,256]{2,1,0:T(8,128)(2,1)S(1)}, u32[]{:S(2)}, u32[]{:S(2)}) collective-permute-start(bf16[16,32,256]{2,1,0:T(8,128)(2,1)S(1)} %collective-permute-done.4.rest_1_), channel_id=1, source_target_pairs={{0,4},{1,5},{2,6},{3,7},{4,0},{5,1},{6,2},{7,3},{8,12},{9,13},{10,... | collective-permute-start | bytes 786440 | tf_op jit(solution)/shard_map/end_left_10/ppermute | solution.py:240
  34.1 12.6 %collective-permute-start.19 = (bf16[16,32,256]{2,1,0:T(8,128)(2,1)S(1)}, bf16[16,32,256]{2,1,0:T(8,128)(2,1)S(1)}, u32[]{:S(2)}, u32[]{:S(2)}) collective-permute-start(bf16[16,32,256]{2,1,0:T(8,128)(2,1)S(1)} %collective-permute-done.12.rest_3_), channel_id=1, source_target_pairs={{0,1},{1,0},{2,3},{3,2},{4,8},{5,9},{6,10},{7,11},{8,4},{9,5},{10,... | collective-permute-start | bytes 786440 | tf_op jit(solution)/shard_map/mid_own_11/ppermute | solution.py:240
  36.9 8.1 %collective-permute-start.13 = (bf16[16,32,256]{2,1,0:T(8,128)(2,1)S(1)}, bf16[16,32,256]{2,1,0:T(8,128)(2,1)S(1)}, u32[]{:S(2)}, u32[]{:S(2)}) collective-permute-start(bf16[16,32,256]{2,1,0:T(8,128)(2,1)S(1)} %get-tuple-element.66), channel_id=1, source_target_pairs={{0,2},{1,3},{2,0},{3,1},{4,6},{5,7},{6,4},{7,5},{8,10},{9,11},{10,... | collective-permute-start | bytes 786440 | tf_op jit(solution)/shard_map/cross_left_1/ppermute | solution.py:240
  39.4 11.2 %collective-permute-start.18 = (bf16[16,32,256]{2,1,0:T(8,128)(2,1)S(1)}, bf16[16,32,256]{2,1,0:T(8,128)(2,1)S(1)}, u32[]{:S(2)}, u32[]{:S(2)}) collective-permute-start(bf16[16,32,256]{2,1,0:T(8,128)(2,1)S(1)} %collective-permute-done.12.rest_3_), channel_id=1, source_target_pairs={{0,4},{1,5},{2,6},{3,7},{4,0},{5,1},{6,2},{7,3},{8,12},{9,13},{10,... | collective-permute-start | bytes 786440 | tf_op jit(solution)/shard_map/end_right_11/ppermute | solution.py:240
  45.5 10.7 %collective-permute-start.14 = (bf16[16,32,256]{2,1,0:T(8,128)(2,1)S(1)}, bf16[16,32,256]{2,1,0:T(8,128)(2,1)S(1)}, u32[]{:S(2)}, u32[]{:S(2)}) collective-permute-start(bf16[16,32,256]{2,1,0:T(8,128)(2,1)S(1)} %get-tuple-element.68), channel_id=1, source_target_pairs={{0,4},{1,5},{2,6},{3,7},{4,0},{5,1},{6,2},{7,3},{8,12},{9,13},{10,... | collective-permute-start | bytes 786440 | tf_op jit(solution)/shard_map/left_11_and_products_back_0/ppermute | solution.py:240
  50.6 5.7 %collective-permute-start.20 = (bf16[16,32,256]{2,1,0:T(8,128)(2,1)S(1)}, bf16[16,32,256]{2,1,0:T(8,128)(2,1)S(1)}, u32[]{:S(2)}, u32[]{:S(2)}) collective-permute-start(bf16[16,32,256]{2,1,0:T(8,128)(2,1)S(1)} %collective-permute-done.18.rest_5_), channel_id=1, source_target_pairs={{0,1},{1,0},{2,3},{3,2},{4,8},{5,9},{6,10},{7,11},{8,4},{9,5},{10,... | collective-permute-start | bytes 786440 | tf_op jit(solution)/shard_map/mid_next_11/ppermute | solution.py:240
  56.3 18.9 %copy-start.3 = (bf16[128,128]{1,0:T(8,128)(2,1)S(1)}, bf16[128,128]{1,0:T(8,128)(2,1)}, u32[]{:S(2)}) copy-start(bf16[128,128]{1,0:T(8,128)(2,1)} %weight.5) | copy-start | bytes 98308
  56.3 18.9 %copy-start.6 = (f32[128]{0:T(128)S(1)}, f32[128]{0:T(128)}, u32[]{:S(2)}) copy-start(f32[128]{0:T(128)} %param.12) | copy-start | bytes 1540
  56.9 6.3 %collective-permute-start.21 = (bf16[16,32,256]{2,1,0:T(8,128)(2,1)S(1)}, bf16[16,32,256]{2,1,0:T(8,128)(2,1)S(1)}, u32[]{:S(2)}, u32[]{:S(2)}) collective-permute-start(bf16[16,32,256]{2,1,0:T(8,128)(2,1)S(1)} %get-tuple-element.78), channel_id=1, source_target_pairs={{0,4},{1,5},{2,6},{3,7},{4,0},{5,1},{6,2},{7,3},{8,12},{9,13},{10,... | collective-permute-start | bytes 786440 | tf_op jit(solution)/shard_map/products_back_1/ppermute | solution.py:240
  58.0 9.3 %collective-permute-start.15 = (bf16[16,32,128]{2,1,0:T(8,128)(2,1)S(1)}, bf16[16,32,128]{2,1,0:T(8,128)(2,1)S(1)}, u32[]{:S(2)}, u32[]{:S(2)}) collective-permute-start(bf16[16,32,128]{2,1,0:T(8,128)(2,1)S(1)} %get-tuple-element.70), channel_id=1, source_target_pairs={{0,1},{1,0},{2,3},{3,2},{4,5},{5,4},{6,7},{7,6},{8,9},{9,8},{10,11... | collective-permute-start | bytes 393224 | tf_op jit(solution)/shard_map/return_01/ppermute | solution.py:240
  61.6 6.2 %collective-permute-start.16 = (bf16[16,32,128]{2,1,0:T(8,128)(2,1)S(1)}, bf16[16,32,128]{2,1,0:T(8,128)(2,1)S(1)}, u32[]{:S(2)}, u32[]{:S(2)}) collective-permute-start(bf16[16,32,128]{2,1,0:T(8,128)(2,1)S(1)} %get-tuple-element.71), channel_id=1, source_target_pairs={{0,2},{1,3},{2,0},{3,1},{4,6},{5,7},{6,4},{7,5},{8,10},{9,11},{10,... | collective-permute-start | bytes 393224 | tf_op jit(solution)/shard_map/return_02/ppermute | solution.py:240
  62.8 7.2 %collective-permute-start.17 = (bf16[16,32,128]{2,1,0:T(8,128)(2,1)S(1)}, bf16[16,32,128]{2,1,0:T(8,128)(2,1)S(1)}, u32[]{:S(2)}, u32[]{:S(2)}) collective-permute-start(bf16[16,32,128]{2,1,0:T(8,128)(2,1)S(1)} %get-tuple-element.72), channel_id=1, source_target_pairs={{0,3},{1,2},{2,1},{3,0},{4,7},{5,6},{6,5},{7,4},{8,11},{9,10},{10,... | collective-permute-start | bytes 393224 | tf_op jit(solution)/shard_map/return_03/ppermute | solution.py:240
  63.3 6.7 %collective-permute-start.22 = (bf16[16,32,128]{2,1,0:T(8,128)(2,1)S(1)}, bf16[16,32,128]{2,1,0:T(8,128)(2,1)S(1)}, u32[]{:S(2)}, u32[]{:S(2)}) collective-permute-start(bf16[16,32,128]{2,1,0:T(8,128)(2,1)S(1)} %get-tuple-element.80), channel_id=1, source_target_pairs={{0,1},{1,0},{2,3},{3,2},{4,5},{5,4},{6,7},{7,6},{8,9},{9,8},{10,11... | collective-permute-start | bytes 393224 | tf_op jit(solution)/shard_map/return_11/ppermute | solution.py:240
  66.1 6.2 %collective-permute-start.23 = (bf16[16,32,128]{2,1,0:T(8,128)(2,1)S(1)}, bf16[16,32,128]{2,1,0:T(8,128)(2,1)S(1)}, u32[]{:S(2)}, u32[]{:S(2)}) collective-permute-start(bf16[16,32,128]{2,1,0:T(8,128)(2,1)S(1)} %get-tuple-element.81), channel_id=1, source_target_pairs={{0,2},{1,3},{2,0},{3,1},{4,6},{5,7},{6,4},{7,5},{8,10},{9,11},{10,... | collective-permute-start | bytes 393224 | tf_op jit(solution)/shard_map/return_12/ppermute | solution.py:240
  67.3 7.9 %collective-permute-start.24 = (bf16[16,32,128]{2,1,0:T(8,128)(2,1)S(1)}, bf16[16,32,128]{2,1,0:T(8,128)(2,1)S(1)}, u32[]{:S(2)}, u32[]{:S(2)}) collective-permute-start(bf16[16,32,128]{2,1,0:T(8,128)(2,1)S(1)} %get-tuple-element.82), channel_id=1, source_target_pairs={{0,3},{1,2},{2,1},{3,0},{4,7},{5,6},{6,5},{7,4},{8,11},{9,10},{10,... | collective-permute-start | bytes 393224 | tf_op jit(solution)/shard_map/return_13/ppermute | solution.py:240

commit v16 on v15

--- a/solution.py
+++ b/solution.py
@@ -215,7 +215,9 @@
             in_specs=in_specs,
             out_specs=outs,
             scratch_shapes=list(scratch),
-            compiler_params=pltpu.CompilerParams(vmem_limit_bytes=size + SPARE),
+            compiler_params=pltpu.CompilerParams(
+                vmem_limit_bytes=size + SPARE, fuse_transposed_lhs_in_matmul=True
+            ),
             name=name,
         )(*args)
 
@@ -319,7 +321,7 @@
     right1[0] = after(crossed, left0)
     own1 = [mid("own_10", right1[0])]
     near1 = [end_right("10", right1[0])]
-    left1[0] = cross("left_0", left1[0], crossed, own0)
+    left1[0] = cross("left_0", left1[0], crossed, near0[-1])
     next0 = [mid("next_0", x, own0) for x in near0]
     outer0 = end_left("0", left0, own0)
     right1[1] = cross("right_1", right1[1], left1[0], own1[0], near1[0][-1])

time: 77.7 us -> 77.5 us (level)
  waiting for transfers between devices: 29.5 us -> 27.9 us
  starting transfers between devices: 34.4 us -> 35.7 us
    ppermute x25, waiting for transfers between devices: 29.5 us -> 27.9 us  [send(): return lax.ppermute(x, ('row', 'chan'), pairs)]
    ppermute x25, starting transfers between devices: 34.4 us -> 35.7 us  [send(): return lax.ppermute(x, ('row', 'chan'), pairs)]
  transfers between devices with their start and end apart: 25 -> 25, of which waited for: 10 -> 13; matrix products, arithmetic and copies ran while one was open for 0% -> 0% of each run, Pallas kernels for 7% -> 7%
where the time goes in v16:
time: 77.5 us; the launch traced here: 77 us
  starting transfers between devices  35.7 us (46%)
  waiting for transfers between devices  27.9 us (36%)
  Pallas kernels  9.72 us (13%)
  local copies, waits for them, and re-layouts  3.52 us (5%)
    ppermute x25, starting transfers between devices, send(): return lax.ppermute(x, ('row', 'chan'), pairs)  35.7 us
    ppermute x25, waiting for transfers between devices, send(): return lax.ppermute(x, ('row', 'chan'), pairs)  27.9 us
    pallas_call x12, Pallas kernels, call(): pl.pallas_call(body, out_shape=out_shape, in_specs=in_specs, out_specs=ou...  9.72 us
    unnamed x14, local copies, waits for them, and re-layouts  3.52 us
  transfers between devices with their start and end apart: 25, of which 13 were waited for; matrix products, arithmetic and copies ran while one was open for 0% of the time, Pallas kernels for 7%

profile of v16, /device:TPU:1, one launch (start us, length us, event | category | flops | bytes accessed | tf_op | source)
XLA Modules:
  0.0 77.0 jit_solution(39653235005291371)
XLA Ops:
  0.0 0.1 collective-permute-start
  0.1 0.5 collective-permute-start.1
  0.5 1.2 %copy-done = bf16[32,128,128]{2,1,0:T(8,128)(2,1)S(1)} copy-done((bf16[32,128,128]{2,1,0:T(8,128)(2,1)S(1)}, bf16[32,128,128]{2,1,0:T(8,128)(2,1)}, u32[]{:S(2)}) %copy-start) | copy-done | bytes 1048600
  1.7 0.9 %copy-done.1 = bf16[128,512]{1,0:T(8,128)(2,1)S(1)} copy-done((bf16[128,512]{1,0:T(8,128)(2,1)S(1)}, bf16[128,512]{1,0:T(8,128)(2,1)}, u32[]{:S(2)}) %copy-start.1) | copy-done | bytes 131096
  2.6 0.7 copy-done.4
  3.4 0.7 copy-done.5
  4.0 1.5 %right_own.1 = (bf16[32,32,128]{2,1,0:T(8,128)(2,1)S(1)}, bf16[4096,128]{1,0:T(8,128)(2,1)S(1)}, bf16[64,128]{1,0:T(8,128)(2,1)S(1)}, bf16[64,128]{1,0:T(8,128)(...) custom-call(bf16[32,128,128]{2,1,0:T(8,128)(2,1)S(1)} %copy-done, ...), custom_call_target="tpu_custom_call" | custom-call | tf_op jit(solution)/shard_map/right_own/pallas_call | solution.py:212
  5.5 0.0 collective-permute-done.1.mask
  5.5 0.0 collective-permute-done.pair
  5.5 1.6 %right_twin.1 = (bf16[32,32,256]{2,1,0:T(8,128)(2,1)S(1)}, bf16[4096,128]{1,0:T(8,128)(2,1)S(1)}, f32[1,32,128]{2,1,0:T(8,128)S(1)}) custom-call(bf16[32,128,128]{2,1,0:T(8,128)(2,1)S(1)} %collective-permute-done.pair, s32[32,128]{1,0:T(8,128)S(1)} %collective-permute-done.1.mask, f32[1,128]{1,0:T(1,128)S(1)} %get-tuple-element.45.gain, ...), custom_call_target="tpu_custom_call" | custom-call | tf_op jit(solution)/shard_map/right_twin/pallas_call | solution.py:212
  7.1 2.4 %collective-permute-start.3 = (bf16[32,32,256]{2,1,0:T(8,128)(2,1)S(1)}, bf16[32,32,256]{2,1,0:T(8,128)(2,1)S(1)}, u32[]{:S(2)}, u32[]{:S(2)}) collective-permute-start(bf16[32,32,256]{2,1,0:T(8,128)(2,1)S(1)} %get-tuple-element.56.rest_2_), channel_id=1, source_target_pairs={{0,4},{1,5},{2,6},{3,7},{4,0},{5,1},{6,2},{7,3},{8,12},{9,13},{10,... | collective-permute-start | bytes 1572872 | tf_op jit(solution)/shard_map/end_right_0/ppermute | solution.py:242
  9.5 0.8 %collective-permute-start.6 = (bf16[32,32,256]{2,1,0:T(8,128)(2,1)S(1)}, bf16[32,32,256]{2,1,0:T(8,128)(2,1)S(1)}, u32[]{:S(2)}, u32[]{:S(2)}) collective-permute-start(bf16[32,32,256]{2,1,0:T(8,128)(2,1)S(1)} %get-tuple-element.56.rest_2_), channel_id=1, source_target_pairs={{0,1},{1,0},{2,3},{3,2},{4,8},{5,9},{6,10},{7,11},{8,4},{9,5},{10,... | collective-permute-start | bytes 1572872 | tf_op jit(solution)/shard_map/mid_own_0/ppermute | solution.py:242
  10.3 0.9 %right_neighbour.1 = (bf16[16,32,256]{2,1,0:T(8,128)(2,1)S(1)}, bf16[16,32,256]{2,1,0:T(8,128)(2,1)S(1)}) custom-call(bf16[4096,128]{1,0:T(8,128)(2,1)S(1)} %get-tuple-element.44.normed.normed0, bf16[4096,128]{1,0:T(8,128)(2,1)S(1)} %get-tuple-element.48.normed1, f32[1,32,128]{2,1,0:T(8,128)S(1)} %get-tuple-element.49.valid0, ...), custom_call_target="tpu_custom_call" | custom-call | tf_op jit(solution)/shard_map/right_neighbour/pallas_call | solution.py:212
  11.2 1.3 %collective-permute-start.2 = (bf16[16,32,256]{2,1,0:T(8,128)(2,1)S(1)}, bf16[16,32,256]{2,1,0:T(8,128)(2,1)S(1)}, u32[]{:S(2)}, u32[]{:S(2)}) collective-permute-start(bf16[16,32,256]{2,1,0:T(8,128)(2,1)S(1)} %get-tuple-element.55), channel_id=1, source_target_pairs={{0,2},{1,3},{2,0},{3,1},{4,6},{5,7},{6,4},{7,5},{8,10},{9,11},{10,... | collective-permute-start | bytes 786440 | tf_op jit(solution)/shard_map/cross_right_0/ppermute | solution.py:242
  12.5 0.9 %left.1 = (bf16[32,32,256]{2,1,0:T(8,128)(2,1)S(1)}, bf16[16,32,256]{2,1,0:T(8,128)(2,1)S(1)}, bf16[16,32,256]{2,1,0:T(8,128)(2,1)S(1)}) custom-call(bf16[4096,128]{1,0:T(8,128)(2,1)S(1)} %get-tuple-element.44.normed.normed0, bf16[4096,128]{1,0:T(8,128)(2,1)S(1)} %get-tuple-element.48.normed1, f32[1,32,128]{2,1,0:T(8,128)S(1)} %get-tuple-element.49.valid0, ...), custom_call_target="tpu_custom_call" | custom-call | tf_op jit(solution)/shard_map/left/pallas_call | solution.py:212
  13.4 5.8 %collective-permute-done.2.rest_3_ = bf16[16,32,256]{2,1,0:T(8,128)(2,1)S(1)} collective-permute-done((bf16[16,32,256]{2,1,0:T(8,128)(2,1)S(1)}, bf16[16,32,256]{2,1,0:T(8,128)(2,1)S(1)}, u32[]{:S(2)}, u32[]{:S(2)}) %collective-permute-start.2) | collective-permute-done | bytes 262176 | tf_op jit(solution)/shard_map/cross_right_0/ppermute | solution.py:242
  19.2 0.8 %collective-permute-start.9 = (bf16[16,32,256]{2,1,0:T(8,128)(2,1)S(1)}, bf16[16,32,256]{2,1,0:T(8,128)(2,1)S(1)}, u32[]{:S(2)}, u32[]{:S(2)}) collective-permute-start(bf16[16,32,256]{2,1,0:T(8,128)(2,1)S(1)} %collective-permute-done.2.rest_3_), channel_id=1, source_target_pairs={{0,1},{1,0},{2,3},{3,2},{4,8},{5,9},{6,10},{7,11},{8,4},{9,5},{10,... | collective-permute-start | bytes 786440 | tf_op jit(solution)/shard_map/mid_own_10/ppermute | solution.py:242
  20.0 0.1 collective-permute-start.5
  20.1 1.2 %collective-permute-done.3.rest_4_ = bf16[32,32,256]{2,1,0:T(8,128)(2,1)S(1)} collective-permute-done((bf16[32,32,256]{2,1,0:T(8,128)(2,1)S(1)}, bf16[32,32,256]{2,1,0:T(8,128)(2,1)S(1)}, u32[]{:S(2)}, u32[]{:S(2)}) %collective-permute-start.3) | collective-permute-done | bytes 524320 | tf_op jit(solution)/shard_map/end_right_0/ppermute | solution.py:242
  21.3 1.1 %collective-permute-start.4 = (bf16[16,32,256]{2,1,0:T(8,128)(2,1)S(1)}, bf16[16,32,256]{2,1,0:T(8,128)(2,1)S(1)}, u32[]{:S(2)}, u32[]{:S(2)}) collective-permute-start(bf16[16,32,256]{2,1,0:T(8,128)(2,1)S(1)} %get-tuple-element.57), channel_id=1, source_target_pairs={{0,2},{1,3},{2,0},{3,1},{4,6},{5,7},{6,4},{7,5},{8,10},{9,11},{10,... | collective-permute-start | bytes 786440 | tf_op jit(solution)/shard_map/cross_left_0/ppermute | solution.py:242
  22.4 0.0 collective-permute-done.6.rest_4_
  22.4 1.6 %collective-permute-start.10 = (bf16[32,32,256]{2,1,0:T(8,128)(2,1)S(1)}, bf16[32,32,256]{2,1,0:T(8,128)(2,1)S(1)}, u32[]{:S(2)}, u32[]{:S(2)}) collective-permute-start(bf16[32,32,256]{2,1,0:T(8,128)(2,1)S(1)} %collective-permute-done.3.rest_4_), channel_id=1, source_target_pairs={{0,1},{1,0},{2,3},{3,2},{4,8},{5,9},{6,10},{7,11},{8,4},{9,5},{10,... | collective-permute-start | bytes 1572872 | tf_op jit(solution)/shard_map/mid_next_0/ppermute | solution.py:242
  24.1 1.0 %collective-permute-start.7 = (bf16[32,32,256]{2,1,0:T(8,128)(2,1)S(1)}, bf16[32,32,256]{2,1,0:T(8,128)(2,1)S(1)}, u32[]{:S(2)}, u32[]{:S(2)}) collective-permute-start(bf16[32,32,256]{2,1,0:T(8,128)(2,1)S(1)} %get-tuple-element.74.rest_0_), channel_id=1, source_target_pairs={{0,4},{1,5},{2,6},{3,7},{4,0},{5,1},{6,2},{7,3},{8,12},{9,13},{10,... | collective-permute-start | bytes 1572872 | tf_op jit(solution)/shard_map/end_left_0/ppermute | solution.py:242
  25.0 0.0 collective-permute-done.9.rest_5_
  25.0 2.5 %collective-permute-done.5.rest_5_ = bf16[16,32,256]{2,1,0:T(8,128)(2,1)S(1)} collective-permute-done((bf16[16,32,256]{2,1,0:T(8,128)(2,1)S(1)}, bf16[16,32,256]{2,1,0:T(8,128)(2,1)S(1)}, u32[]{:S(2)}, u32[]{:S(2)}) %collective-permute-start.5) | collective-permute-done | bytes 262176 | tf_op jit(solution)/shard_map/end_right_10/ppermute | solution.py:242
  27.5 0.6 collective-permute-done.4.rest_1_
  28.1 0.7 collective-permute-start.12
  28.8 0.4 gate.1
  29.3 2.6 %collective-permute-start.11 = (bf16[16,32,256]{2,1,0:T(8,128)(2,1)S(1)}, bf16[16,32,256]{2,1,0:T(8,128)(2,1)S(1)}, u32[]{:S(2)}, u32[]{:S(2)}) collective-permute-start(bf16[16,32,256]{2,1,0:T(8,128)(2,1)S(1)} %collective-permute-done.5.rest_5_), channel_id=1, source_target_pairs={{0,1},{1,0},{2,3},{3,2},{4,8},{5,9},{6,10},{7,11},{8,4},{9,5},{10,... | collective-permute-start | bytes 786440 | tf_op jit(solution)/shard_map/mid_next_10/ppermute | solution.py:242
  31.9 0.2 collective-permute-start.8
  32.1 1.8 %collective-permute-done.12.rest_3_ = bf16[16,32,256]{2,1,0:T(8,128)(2,1)S(1)} collective-permute-done((bf16[16,32,256]{2,1,0:T(8,128)(2,1)S(1)}, bf16[16,32,256]{2,1,0:T(8,128)(2,1)S(1)}, u32[]{:S(2)}, u32[]{:S(2)}) %collective-permute-start.12) | collective-permute-done | bytes 262176 | tf_op jit(solution)/shard_map/cross_right_1/ppermute | solution.py:242
  33.9 2.9 %collective-permute-start.19 = (bf16[16,32,256]{2,1,0:T(8,128)(2,1)S(1)}, bf16[16,32,256]{2,1,0:T(8,128)(2,1)S(1)}, u32[]{:S(2)}, u32[]{:S(2)}) collective-permute-start(bf16[16,32,256]{2,1,0:T(8,128)(2,1)S(1)} %collective-permute-done.12.rest_3_), channel_id=1, source_target_pairs={{0,1},{1,0},{2,3},{3,2},{4,8},{5,9},{6,10},{7,11},{8,4},{9,5},{10,... | collective-permute-start | bytes 786440 | tf_op jit(solution)/shard_map/mid_own_11/ppermute | solution.py:242
  36.8 0.0 collective-permute-done.10.rest_6_
  36.8 0.7 collective-permute-start.13
  37.6 0.8 %collective-permute-done.7.rest_2_ = bf16[32,32,256]{2,1,0:T(8,128)(2,1)S(1)} collective-permute-done((bf16[32,32,256]{2,1,0:T(8,128)(2,1)S(1)}, bf16[32,32,256]{2,1,0:T(8,128)(2,1)S(1)}, u32[]{:S(2)}, u32[]{:S(2)}) %collective-permute-start.7) | collective-permute-done | bytes 524320 | tf_op jit(solution)/shard_map/end_left_0/ppermute | solution.py:242
  38.4 3.3 %collective-permute-start.18 = (bf16[16,32,256]{2,1,0:T(8,128)(2,1)S(1)}, bf16[16,32,256]{2,1,0:T(8,128)(2,1)S(1)}, u32[]{:S(2)}, u32[]{:S(2)}) collective-permute-start(bf16[16,32,256]{2,1,0:T(8,128)(2,1)S(1)} %collective-permute-done.12.rest_3_), channel_id=1, source_target_pairs={{0,4},{1,5},{2,6},{3,7},{4,0},{5,1},{6,2},{7,3},{8,12},{9,13},{10,... | collective-permute-start | bytes 786440 | tf_op jit(solution)/shard_map/end_right_11/ppermute | solution.py:242
  41.7 0.0 collective-permute-done.11.rest_7_
  41.7 2.3 %collective-permute-done.8.rest_3_ = bf16[16,32,256]{2,1,0:T(8,128)(2,1)S(1)} collective-permute-done((bf16[16,32,256]{2,1,0:T(8,128)(2,1)S(1)}, bf16[16,32,256]{2,1,0:T(8,128)(2,1)S(1)}, u32[]{:S(2)}, u32[]{:S(2)}) %collective-permute-start.8) | collective-permute-done | bytes 262176 | tf_op jit(solution)/shard_map/end_left_10/ppermute | solution.py:242
  44.0 0.7 collective-permute-done.13.rest_8_.rest_1_
  44.7 0.5 away.2
  45.3 1.4 %collective-permute-start.14 = (bf16[16,32,256]{2,1,0:T(8,128)(2,1)S(1)}, bf16[16,32,256]{2,1,0:T(8,128)(2,1)S(1)}, u32[]{:S(2)}, u32[]{:S(2)}) collective-permute-start(bf16[16,32,256]{2,1,0:T(8,128)(2,1)S(1)} %get-tuple-element.68), channel_id=1, source_target_pairs={{0,4},{1,5},{2,6},{3,7},{4,0},{5,1},{6,2},{7,3},{8,12},{9,13},{10,... | collective-permute-start | bytes 786440 | tf_op jit(solution)/shard_map/left_11_and_products_back_0/ppermute | solution.py:242
  46.7 0.0 collective-permute-done.19.rest_5_
  46.7 3.0 %collective-permute-done.18.rest_5_ = bf16[16,32,256]{2,1,0:T(8,128)(2,1)S(1)} collective-permute-done((bf16[16,32,256]{2,1,0:T(8,128)(2,1)S(1)}, bf16[16,32,256]{2,1,0:T(8,128)(2,1)S(1)}, u32[]{:S(2)}, u32[]{:S(2)}) %collective-permute-start.18) | collective-permute-done | bytes 262176 | tf_op jit(solution)/shard_map/end_right_11/ppermute | solution.py:242
  49.6 2.7 %collective-permute-start.20 = (bf16[16,32,256]{2,1,0:T(8,128)(2,1)S(1)}, bf16[16,32,256]{2,1,0:T(8,128)(2,1)S(1)}, u32[]{:S(2)}, u32[]{:S(2)}) collective-permute-start(bf16[16,32,256]{2,1,0:T(8,128)(2,1)S(1)} %collective-permute-done.18.rest_5_), channel_id=1, source_target_pairs={{0,1},{1,0},{2,3},{3,2},{4,8},{5,9},{6,10},{7,11},{8,4},{9,5},{10,... | collective-permute-start | bytes 786440 | tf_op jit(solution)/shard_map/mid_next_11/ppermute | solution.py:242
  52.3 0.6 near.2
  52.9 0.6 near.3
  53.5 1.8 %collective-permute-done.14.end.rest_3_ = bf16[16,32,256]{2,1,0:T(8,128)(2,1)S(1)} collective-permute-done((bf16[16,32,256]{2,1,0:T(8,128)(2,1)S(1)}, bf16[16,32,256]{2,1,0:T(8,128)(2,1)S(1)}, u32[]{:S(2)}, u32[]{:S(2)}) %collective-permute-start.14) | collective-permute-done | bytes 262176 | tf_op jit(solution)/shard_map/left_11_and_products_back_0/ppermute | solution.py:242
  55.3 0.1 hand_out.2
  55.4 0.0 copy-start.3
  55.4 0.0 copy-start.6
  55.4 0.5 away.3
  55.9 2.3 %collective-permute-start.21 = (bf16[16,32,256]{2,1,0:T(8,128)(2,1)S(1)}, bf16[16,32,256]{2,1,0:T(8,128)(2,1)S(1)}, u32[]{:S(2)}, u32[]{:S(2)}) collective-permute-start(bf16[16,32,256]{2,1,0:T(8,128)(2,1)S(1)} %get-tuple-element.78), channel_id=1, source_target_pairs={{0,4},{1,5},{2,6},{3,7},{4,0},{5,1},{6,2},{7,3},{8,12},{9,13},{10,... | collective-permute-start | bytes 786440 | tf_op jit(solution)/shard_map/products_back_1/ppermute | solution.py:242
  58.2 3.1 %collective-permute-start.15 = (bf16[16,32,128]{2,1,0:T(8,128)(2,1)S(1)}, bf16[16,32,128]{2,1,0:T(8,128)(2,1)S(1)}, u32[]{:S(2)}, u32[]{:S(2)}) collective-permute-start(bf16[16,32,128]{2,1,0:T(8,128)(2,1)S(1)} %get-tuple-element.70), channel_id=1, source_target_pairs={{0,1},{1,0},{2,3},{3,2},{4,5},{5,4},{6,7},{7,6},{8,9},{9,8},{10,11... | collective-permute-start | bytes 393224 | tf_op jit(solution)/shard_map/return_01/ppermute | solution.py:242
  61.3 1.2 %collective-permute-start.16 = (bf16[16,32,128]{2,1,0:T(8,128)(2,1)S(1)}, bf16[16,32,128]{2,1,0:T(8,128)(2,1)S(1)}, u32[]{:S(2)}, u32[]{:S(2)}) collective-permute-start(bf16[16,32,128]{2,1,0:T(8,128)(2,1)S(1)} %get-tuple-element.71), channel_id=1, source_target_pairs={{0,2},{1,3},{2,0},{3,1},{4,6},{5,7},{6,4},{7,5},{8,10},{9,11},{10,... | collective-permute-start | bytes 393224 | tf_op jit(solution)/shard_map/return_02/ppermute | solution.py:242
  62.5 0.4 collective-permute-start.17
  62.9 0.1 hand_out.3
  63.0 2.8 %collective-permute-start.22 = (bf16[16,32,128]{2,1,0:T(8,128)(2,1)S(1)}, bf16[16,32,128]{2,1,0:T(8,128)(2,1)S(1)}, u32[]{:S(2)}, u32[]{:S(2)}) collective-permute-start(bf16[16,32,128]{2,1,0:T(8,128)(2,1)S(1)} %get-tuple-element.80), channel_id=1, source_target_pairs={{0,1},{1,0},{2,3},{3,2},{4,5},{5,4},{6,7},{7,6},{8,9},{9,8},{10,11... | collective-permute-start | bytes 393224 | tf_op jit(solution)/shard_map/return_11/ppermute | solution.py:242
  65.8 1.3 %collective-permute-start.23 = (bf16[16,32,128]{2,1,0:T(8,128)(2,1)S(1)}, bf16[16,32,128]{2,1,0:T(8,128)(2,1)S(1)}, u32[]{:S(2)}, u32[]{:S(2)}) collective-permute-start(bf16[16,32,128]{2,1,0:T(8,128)(2,1)S(1)} %get-tuple-element.81), channel_id=1, source_target_pairs={{0,2},{1,3},{2,0},{3,1},{4,6},{5,7},{6,4},{7,5},{8,10},{9,11},{10,... | collective-permute-start | bytes 393224 | tf_op jit(solution)/shard_map/return_12/ppermute | solution.py:242
  67.1 0.5 collective-permute-start.24
  67.5 2.2 %collective-permute-done.17.rest_3_ = bf16[16,32,128]{2,1,0:T(8,128)(2,1)S(1)} collective-permute-done((bf16[16,32,128]{2,1,0:T(8,128)(2,1)S(1)}, bf16[16,32,128]{2,1,0:T(8,128)(2,1)S(1)}, u32[]{:S(2)}, u32[]{:S(2)}) %collective-permute-start.17) | collective-permute-done | bytes 131104 | tf_op jit(solution)/shard_map/return_03/ppermute | solution.py:242
  69.7 0.0 collective-permute-done.22.rest_5_
  69.7 2.3 %collective-permute-done.23.rest_6_ = bf16[16,32,128]{2,1,0:T(8,128)(2,1)S(1)} collective-permute-done((bf16[16,32,128]{2,1,0:T(8,128)(2,1)S(1)}, bf16[16,32,128]{2,1,0:T(8,128)(2,1)S(1)}, u32[]{:S(2)}, u32[]{:S(2)}) %collective-permute-start.23) | collective-permute-done | bytes 131104 | tf_op jit(solution)/shard_map/return_12/ppermute | solution.py:242
  72.0 2.9 %collective-permute-done.24.rest_7_ = bf16[16,32,128]{2,1,0:T(8,128)(2,1)S(1)} collective-permute-done((bf16[16,32,128]{2,1,0:T(8,128)(2,1)S(1)}, bf16[16,32,128]{2,1,0:T(8,128)(2,1)S(1)}, u32[]{:S(2)}, u32[]{:S(2)}) %collective-permute-start.24) | collective-permute-done | bytes 131104 | tf_op jit(solution)/shard_map/return_13/ppermute | solution.py:242
  75.0 2.0 %update.1 = bf16[32,128,128]{2,1,0:T(8,128)(2,1)} custom-call(f32[1,128]{1,0:T(1,128)S(1)} %bitcast.3, bf16[128,128]{1,0:T(8,128)(2,1)S(1)} %copy-done.3, f32[32,128,128]{2,1,0:T(8,128)S(1)} %gate.1, bf16[16,32,128]{2,1,0:T(8,128)(2,1)S(1)} %get-tuple-element.69.rest_0_, bf16[16,32,128]{2,1,0:T(8,128)(2,1)S(1)} %collective-permute-done.15.rest_1_, ...), custom_call_target="tpu_custom_call" | custom-call | tf_op jit(solution)/shard_map/update/pallas_call | solution.py:212
  (12 shorter events, 0.0 us)
Async XLA Ops:
  0.0 5.5 %collective-permute-start = (bf16[32,128,128]{2,1,0:T(8,128)(2,1)}, bf16[32,128,128]{2,1,0:T(8,128)(2,1)S(1)}, u32[]{:S(2)}, u32[]{:S(2)}) collective-permute-start(bf16[32,128,128]{2,1,0:T(8,128)(2,1)} %pair.1), channel_id=1, source_target_pairs={{0,1},{1,0},{2,3},{3,2},{4,5},{5,4},{6,7},{7,6},{8,9},{9,8},{10,11... | collective-permute-start | bytes 3145736 | tf_op jit(solution)/shard_map/pair/ppermute | solution.py:242
  0.1 5.5 %collective-permute-start.1 = (s32[32,128]{1,0:T(8,128)}, s32[32,128]{1,0:T(8,128)S(1)}, u32[]{:S(2)}, u32[]{:S(2)}) collective-permute-start(s32[32,128]{1,0:T(8,128)} %mask.1), channel_id=1, source_target_pairs={{0,1},{1,0},{2,3},{3,2},{4,5},{5,4},{6,7},{7,6},{8,9},{9,8},{10,11... | collective-permute-start | bytes 49160 | tf_op jit(solution)/shard_map/mask/ppermute | solution.py:242
  0.5 1.2 %copy-start = (bf16[32,128,128]{2,1,0:T(8,128)(2,1)S(1)}, bf16[32,128,128]{2,1,0:T(8,128)(2,1)}, u32[]{:S(2)}) copy-start(bf16[32,128,128]{2,1,0:T(8,128)(2,1)} %pair.1) | copy-start | bytes 3145732
  1.7 0.9 %copy-start.1 = (bf16[128,512]{1,0:T(8,128)(2,1)S(1)}, bf16[128,512]{1,0:T(8,128)(2,1)}, u32[]{:S(2)}) copy-start(bf16[128,512]{1,0:T(8,128)(2,1)} %weight.3) | copy-start | bytes 393220
  2.6 0.7 copy-start.4
  3.4 0.7 copy-start.5
  7.1 14.2 %collective-permute-start.3 = (bf16[32,32,256]{2,1,0:T(8,128)(2,1)S(1)}, bf16[32,32,256]{2,1,0:T(8,128)(2,1)S(1)}, u32[]{:S(2)}, u32[]{:S(2)}) collective-permute-start(bf16[32,32,256]{2,1,0:T(8,128)(2,1)S(1)} %get-tuple-element.56.rest_2_), channel_id=1, source_target_pairs={{0,4},{1,5},{2,6},{3,7},{4,0},{5,1},{6,2},{7,3},{8,12},{9,13},{10,... | collective-permute-start | bytes 1572872 | tf_op jit(solution)/shard_map/end_right_0/ppermute | solution.py:242
  9.5 12.9 %collective-permute-start.6 = (bf16[32,32,256]{2,1,0:T(8,128)(2,1)S(1)}, bf16[32,32,256]{2,1,0:T(8,128)(2,1)S(1)}, u32[]{:S(2)}, u32[]{:S(2)}) collective-permute-start(bf16[32,32,256]{2,1,0:T(8,128)(2,1)S(1)} %get-tuple-element.56.rest_2_), channel_id=1, source_target_pairs={{0,1},{1,0},{2,3},{3,2},{4,8},{5,9},{6,10},{7,11},{8,4},{9,5},{10,... | collective-permute-start | bytes 1572872 | tf_op jit(solution)/shard_map/mid_own_0/ppermute | solution.py:242
  10.3 18.6 %copy-start.2 = (bf16[128,128]{1,0:T(8,128)(2,1)S(1)}, bf16[128,128]{1,0:T(8,128)(2,1)}, u32[]{:S(2)}) copy-start(bf16[128,128]{1,0:T(8,128)(2,1)} %weight.4) | copy-start | bytes 98308
  11.2 8.0 %collective-permute-start.2 = (bf16[16,32,256]{2,1,0:T(8,128)(2,1)S(1)}, bf16[16,32,256]{2,1,0:T(8,128)(2,1)S(1)}, u32[]{:S(2)}, u32[]{:S(2)}) collective-permute-start(bf16[16,32,256]{2,1,0:T(8,128)(2,1)S(1)} %get-tuple-element.55), channel_id=1, source_target_pairs={{0,2},{1,3},{2,0},{3,1},{4,6},{5,7},{6,4},{7,5},{8,10},{9,11},{10,... | collective-permute-start | bytes 786440 | tf_op jit(solution)/shard_map/cross_right_0/ppermute | solution.py:242
  19.2 5.8 %collective-permute-start.9 = (bf16[16,32,256]{2,1,0:T(8,128)(2,1)S(1)}, bf16[16,32,256]{2,1,0:T(8,128)(2,1)S(1)}, u32[]{:S(2)}, u32[]{:S(2)}) collective-permute-start(bf16[16,32,256]{2,1,0:T(8,128)(2,1)S(1)} %collective-permute-done.2.rest_3_), channel_id=1, source_target_pairs={{0,1},{1,0},{2,3},{3,2},{4,8},{5,9},{6,10},{7,11},{8,4},{9,5},{10,... | collective-permute-start | bytes 786440 | tf_op jit(solution)/shard_map/mid_own_10/ppermute | solution.py:242
  20.0 7.5 %collective-permute-start.5 = (bf16[16,32,256]{2,1,0:T(8,128)(2,1)S(1)}, bf16[16,32,256]{2,1,0:T(8,128)(2,1)S(1)}, u32[]{:S(2)}, u32[]{:S(2)}) collective-permute-start(bf16[16,32,256]{2,1,0:T(8,128)(2,1)S(1)} %collective-permute-done.2.rest_3_), channel_id=1, source_target_pairs={{0,4},{1,5},{2,6},{3,7},{4,0},{5,1},{6,2},{7,3},{8,12},{9,13},{10,... | collective-permute-start | bytes 786440 | tf_op jit(solution)/shard_map/end_right_10/ppermute | solution.py:242
  21.3 6.8 %collective-permute-start.4 = (bf16[16,32,256]{2,1,0:T(8,128)(2,1)S(1)}, bf16[16,32,256]{2,1,0:T(8,128)(2,1)S(1)}, u32[]{:S(2)}, u32[]{:S(2)}) collective-permute-start(bf16[16,32,256]{2,1,0:T(8,128)(2,1)S(1)} %get-tuple-element.57), channel_id=1, source_target_pairs={{0,2},{1,3},{2,0},{3,1},{4,6},{5,7},{6,4},{7,5},{8,10},{9,11},{10,... | collective-permute-start | bytes 786440 | tf_op jit(solution)/shard_map/cross_left_0/ppermute | solution.py:242
  22.4 14.4 %collective-permute-start.10 = (bf16[32,32,256]{2,1,0:T(8,128)(2,1)S(1)}, bf16[32,32,256]{2,1,0:T(8,128)(2,1)S(1)}, u32[]{:S(2)}, u32[]{:S(2)}) collective-permute-start(bf16[32,32,256]{2,1,0:T(8,128)(2,1)S(1)} %collective-permute-done.3.rest_4_), channel_id=1, source_target_pairs={{0,1},{1,0},{2,3},{3,2},{4,8},{5,9},{6,10},{7,11},{8,4},{9,5},{10,... | collective-permute-start | bytes 1572872 | tf_op jit(solution)/shard_map/mid_next_0/ppermute | solution.py:242
  24.1 14.4 %collective-permute-start.7 = (bf16[32,32,256]{2,1,0:T(8,128)(2,1)S(1)}, bf16[32,32,256]{2,1,0:T(8,128)(2,1)S(1)}, u32[]{:S(2)}, u32[]{:S(2)}) collective-permute-start(bf16[32,32,256]{2,1,0:T(8,128)(2,1)S(1)} %get-tuple-element.74.rest_0_), channel_id=1, source_target_pairs={{0,4},{1,5},{2,6},{3,7},{4,0},{5,1},{6,2},{7,3},{8,12},{9,13},{10,... | collective-permute-start | bytes 1572872 | tf_op jit(solution)/shard_map/end_left_0/ppermute | solution.py:242
  28.1 5.8 %collective-permute-start.12 = (bf16[16,32,256]{2,1,0:T(8,128)(2,1)S(1)}, bf16[16,32,256]{2,1,0:T(8,128)(2,1)S(1)}, u32[]{:S(2)}, u32[]{:S(2)}) collective-permute-start(bf16[16,32,256]{2,1,0:T(8,128)(2,1)S(1)} %get-tuple-element.65), channel_id=1, source_target_pairs={{0,2},{1,3},{2,0},{3,1},{4,6},{5,7},{6,4},{7,5},{8,10},{9,11},{10,... | collective-permute-start | bytes 786440 | tf_op jit(solution)/shard_map/cross_right_1/ppermute | solution.py:242
  29.3 12.4 %collective-permute-start.11 = (bf16[16,32,256]{2,1,0:T(8,128)(2,1)S(1)}, bf16[16,32,256]{2,1,0:T(8,128)(2,1)S(1)}, u32[]{:S(2)}, u32[]{:S(2)}) collective-permute-start(bf16[16,32,256]{2,1,0:T(8,128)(2,1)S(1)} %collective-permute-done.5.rest_5_), channel_id=1, source_target_pairs={{0,1},{1,0},{2,3},{3,2},{4,8},{5,9},{6,10},{7,11},{8,4},{9,5},{10,... | collective-permute-start | bytes 786440 | tf_op jit(solution)/shard_map/mid_next_10/ppermute | solution.py:242
  31.9 12.1 %collective-permute-start.8 = (bf16[16,32,256]{2,1,0:T(8,128)(2,1)S(1)}, bf16[16,32,256]{2,1,0:T(8,128)(2,1)S(1)}, u32[]{:S(2)}, u32[]{:S(2)}) collective-permute-start(bf16[16,32,256]{2,1,0:T(8,128)(2,1)S(1)} %collective-permute-done.4.rest_1_), channel_id=1, source_target_pairs={{0,4},{1,5},{2,6},{3,7},{4,0},{5,1},{6,2},{7,3},{8,12},{9,13},{10,... | collective-permute-start | bytes 786440 | tf_op jit(solution)/shard_map/end_left_10/ppermute | solution.py:242
  33.9 12.8 %collective-permute-start.19 = (bf16[16,32,256]{2,1,0:T(8,128)(2,1)S(1)}, bf16[16,32,256]{2,1,0:T(8,128)(2,1)S(1)}, u32[]{:S(2)}, u32[]{:S(2)}) collective-permute-start(bf16[16,32,256]{2,1,0:T(8,128)(2,1)S(1)} %collective-permute-done.12.rest_3_), channel_id=1, source_target_pairs={{0,1},{1,0},{2,3},{3,2},{4,8},{5,9},{6,10},{7,11},{8,4},{9,5},{10,... | collective-permute-start | bytes 786440 | tf_op jit(solution)/shard_map/mid_own_11/ppermute | solution.py:242
  36.8 7.9 %collective-permute-start.13 = (bf16[16,32,256]{2,1,0:T(8,128)(2,1)S(1)}, bf16[16,32,256]{2,1,0:T(8,128)(2,1)S(1)}, u32[]{:S(2)}, u32[]{:S(2)}) collective-permute-start(bf16[16,32,256]{2,1,0:T(8,128)(2,1)S(1)} %get-tuple-element.66), channel_id=1, source_target_pairs={{0,2},{1,3},{2,0},{3,1},{4,6},{5,7},{6,4},{7,5},{8,10},{9,11},{10,... | collective-permute-start | bytes 786440 | tf_op jit(solution)/shard_map/cross_left_1/ppermute | solution.py:242
  38.4 11.2 %collective-permute-start.18 = (bf16[16,32,256]{2,1,0:T(8,128)(2,1)S(1)}, bf16[16,32,256]{2,1,0:T(8,128)(2,1)S(1)}, u32[]{:S(2)}, u32[]{:S(2)}) collective-permute-start(bf16[16,32,256]{2,1,0:T(8,128)(2,1)S(1)} %collective-permute-done.12.rest_3_), channel_id=1, source_target_pairs={{0,4},{1,5},{2,6},{3,7},{4,0},{5,1},{6,2},{7,3},{8,12},{9,13},{10,... | collective-permute-start | bytes 786440 | tf_op jit(solution)/shard_map/end_right_11/ppermute | solution.py:242
  45.3 10.0 %collective-permute-start.14 = (bf16[16,32,256]{2,1,0:T(8,128)(2,1)S(1)}, bf16[16,32,256]{2,1,0:T(8,128)(2,1)S(1)}, u32[]{:S(2)}, u32[]{:S(2)}) collective-permute-start(bf16[16,32,256]{2,1,0:T(8,128)(2,1)S(1)} %get-tuple-element.68), channel_id=1, source_target_pairs={{0,4},{1,5},{2,6},{3,7},{4,0},{5,1},{6,2},{7,3},{8,12},{9,13},{10,... | collective-permute-start | bytes 786440 | tf_op jit(solution)/shard_map/left_11_and_products_back_0/ppermute | solution.py:242
  49.6 5.7 %collective-permute-start.20 = (bf16[16,32,256]{2,1,0:T(8,128)(2,1)S(1)}, bf16[16,32,256]{2,1,0:T(8,128)(2,1)S(1)}, u32[]{:S(2)}, u32[]{:S(2)}) collective-permute-start(bf16[16,32,256]{2,1,0:T(8,128)(2,1)S(1)} %collective-permute-done.18.rest_5_), channel_id=1, source_target_pairs={{0,1},{1,0},{2,3},{3,2},{4,8},{5,9},{6,10},{7,11},{8,4},{9,5},{10,... | collective-permute-start | bytes 786440 | tf_op jit(solution)/shard_map/mid_next_11/ppermute | solution.py:242
  55.4 19.6 %copy-start.3 = (bf16[128,128]{1,0:T(8,128)(2,1)S(1)}, bf16[128,128]{1,0:T(8,128)(2,1)}, u32[]{:S(2)}) copy-start(bf16[128,128]{1,0:T(8,128)(2,1)} %weight.5) | copy-start | bytes 98308
  55.4 19.6 %copy-start.6 = (f32[128]{0:T(128)S(1)}, f32[128]{0:T(128)}, u32[]{:S(2)}) copy-start(f32[128]{0:T(128)} %param.12) | copy-start | bytes 1540
  55.9 7.0 %collective-permute-start.21 = (bf16[16,32,256]{2,1,0:T(8,128)(2,1)S(1)}, bf16[16,32,256]{2,1,0:T(8,128)(2,1)S(1)}, u32[]{:S(2)}, u32[]{:S(2)}) collective-permute-start(bf16[16,32,256]{2,1,0:T(8,128)(2,1)S(1)} %get-tuple-element.78), channel_id=1, source_target_pairs={{0,4},{1,5},{2,6},{3,7},{4,0},{5,1},{6,2},{7,3},{8,12},{9,13},{10,... | collective-permute-start | bytes 786440 | tf_op jit(solution)/shard_map/products_back_1/ppermute | solution.py:242
  58.2 8.9 %collective-permute-start.15 = (bf16[16,32,128]{2,1,0:T(8,128)(2,1)S(1)}, bf16[16,32,128]{2,1,0:T(8,128)(2,1)S(1)}, u32[]{:S(2)}, u32[]{:S(2)}) collective-permute-start(bf16[16,32,128]{2,1,0:T(8,128)(2,1)S(1)} %get-tuple-element.70), channel_id=1, source_target_pairs={{0,1},{1,0},{2,3},{3,2},{4,5},{5,4},{6,7},{7,6},{8,9},{9,8},{10,11... | collective-permute-start | bytes 393224 | tf_op jit(solution)/shard_map/return_01/ppermute | solution.py:242
  61.3 6.2 %collective-permute-start.16 = (bf16[16,32,128]{2,1,0:T(8,128)(2,1)S(1)}, bf16[16,32,128]{2,1,0:T(8,128)(2,1)S(1)}, u32[]{:S(2)}, u32[]{:S(2)}) collective-permute-start(bf16[16,32,128]{2,1,0:T(8,128)(2,1)S(1)} %get-tuple-element.71), channel_id=1, source_target_pairs={{0,2},{1,3},{2,0},{3,1},{4,6},{5,7},{6,4},{7,5},{8,10},{9,11},{10,... | collective-permute-start | bytes 393224 | tf_op jit(solution)/shard_map/return_02/ppermute | solution.py:242
  62.5 7.2 %collective-permute-start.17 = (bf16[16,32,128]{2,1,0:T(8,128)(2,1)S(1)}, bf16[16,32,128]{2,1,0:T(8,128)(2,1)S(1)}, u32[]{:S(2)}, u32[]{:S(2)}) collective-permute-start(bf16[16,32,128]{2,1,0:T(8,128)(2,1)S(1)} %get-tuple-element.72), channel_id=1, source_target_pairs={{0,3},{1,2},{2,1},{3,0},{4,7},{5,6},{6,5},{7,4},{8,11},{9,10},{10,... | collective-permute-start | bytes 393224 | tf_op jit(solution)/shard_map/return_03/ppermute | solution.py:242
  63.0 6.7 %collective-permute-start.22 = (bf16[16,32,128]{2,1,0:T(8,128)(2,1)S(1)}, bf16[16,32,128]{2,1,0:T(8,128)(2,1)S(1)}, u32[]{:S(2)}, u32[]{:S(2)}) collective-permute-start(bf16[16,32,128]{2,1,0:T(8,128)(2,1)S(1)} %get-tuple-element.80), channel_id=1, source_target_pairs={{0,1},{1,0},{2,3},{3,2},{4,5},{5,4},{6,7},{7,6},{8,9},{9,8},{10,11... | collective-permute-start | bytes 393224 | tf_op jit(solution)/shard_map/return_11/ppermute | solution.py:242
  65.8 6.2 %collective-permute-start.23 = (bf16[16,32,128]{2,1,0:T(8,128)(2,1)S(1)}, bf16[16,32,128]{2,1,0:T(8,128)(2,1)S(1)}, u32[]{:S(2)}, u32[]{:S(2)}) collective-permute-start(bf16[16,32,128]{2,1,0:T(8,128)(2,1)S(1)} %get-tuple-element.81), channel_id=1, source_target_pairs={{0,2},{1,3},{2,0},{3,1},{4,6},{5,7},{6,4},{7,5},{8,10},{9,11},{10,... | collective-permute-start | bytes 393224 | tf_op jit(solution)/shard_map/return_12/ppermute | solution.py:242
  67.1 7.9 %collective-permute-start.24 = (bf16[16,32,128]{2,1,0:T(8,128)(2,1)S(1)}, bf16[16,32,128]{2,1,0:T(8,128)(2,1)S(1)}, u32[]{:S(2)}, u32[]{:S(2)}) collective-permute-start(bf16[16,32,128]{2,1,0:T(8,128)(2,1)S(1)} %get-tuple-element.82), channel_id=1, source_target_pairs={{0,3},{1,2},{2,1},{3,0},{4,7},{5,6},{6,5},{7,4},{8,11},{9,10},{10,... | collective-permute-start | bytes 393224 | tf_op jit(solution)/shard_map/return_13/ppermute | solution.py:242

commit v17 on v16

--- a/solution.py
+++ b/solution.py
@@ -11,7 +11,7 @@
 F32, BF16 = jnp.float32, jnp.bfloat16
 LANES = 128
 SPARE = 6 * 1024 * 1024
-SHARES = (4, 4)
+SHARES = (9, 7)
 NT = (((1,), (1,)), ((), ()))
 TN = (((0,), (0,)), ((), ()))
 VMEM = pl.BlockSpec(memory_space=pltpu.VMEM)
@@ -146,7 +146,7 @@
 
         @pl.when(at_end)
         def _():
-            outs[1][...] = other[...]
+            outs[1][: other.shape[0]] = other[...]
 
 
 def hand_out_kernel(planes, near, far, end, *outs):

time: 77.5 us -> 77.4 us (level)
  starting transfers between devices: 35.7 us -> 30.9 us
  waiting for transfers between devices: 27.9 us -> 32.6 us
    ppermute x25, starting transfers between devices: 35.7 us -> 30.9 us  [send(): return lax.ppermute(x, ('row', 'chan'), pairs)]
    ppermute x25, waiting for transfers between devices: 27.9 us -> 32.6 us  [send(): return lax.ppermute(x, ('row', 'chan'), pairs)]
  transfers between devices with their start and end apart: 25 -> 25, of which waited for: 13 -> 12; matrix products, arithmetic and copies ran while one was open for 0% -> 0% of each run, Pallas kernels for 7% -> 7%
where the time goes in v17:
time: 77.4 us; the launch traced here: 76.9 us
  waiting for transfers between devices  32.6 us (42%)
  starting transfers between devices  30.9 us (40%)
  Pallas kernels  9.74 us (13%)
  local copies, waits for them, and re-layouts  3.52 us (5%)
    ppermute x25, waiting for transfers between devices, send(): return lax.ppermute(x, ('row', 'chan'), pairs)  32.6 us
    ppermute x25, starting transfers between devices, send(): return lax.ppermute(x, ('row', 'chan'), pairs)  30.9 us
    pallas_call x12, Pallas kernels, call(): pl.pallas_call(body, out_shape=out_shape, in_specs=in_specs, out_specs=ou...  9.74 us
    unnamed x14, local copies, waits for them, and re-layouts  3.52 us
  transfers between devices with their start and end apart: 25, of which 12 were waited for; matrix products, arithmetic and copies ran while one was open for 0% of the time, Pallas kernels for 7%

profile of v17, /device:TPU:1, one launch (start us, length us, event | category | flops | bytes accessed | tf_op | source)
XLA Modules:
  0.0 76.9 jit_solution(8616159144109170282)
XLA Ops:
  0.0 0.1 collective-permute-start
  0.1 0.5 collective-permute-start.1
  0.5 1.2 %copy-done = bf16[32,128,128]{2,1,0:T(8,128)(2,1)S(1)} copy-done((bf16[32,128,128]{2,1,0:T(8,128)(2,1)S(1)}, bf16[32,128,128]{2,1,0:T(8,128)(2,1)}, u32[]{:S(2)}) %copy-start) | copy-done | bytes 1048600
  1.7 0.9 %copy-done.1 = bf16[128,512]{1,0:T(8,128)(2,1)S(1)} copy-done((bf16[128,512]{1,0:T(8,128)(2,1)S(1)}, bf16[128,512]{1,0:T(8,128)(2,1)}, u32[]{:S(2)}) %copy-start.1) | copy-done | bytes 131096
  2.6 0.7 copy-done.4
  3.4 0.7 copy-done.5
  4.0 1.5 %right_own.1 = (bf16[32,32,128]{2,1,0:T(8,128)(2,1)S(1)}, bf16[4096,128]{1,0:T(8,128)(2,1)S(1)}, bf16[64,128]{1,0:T(8,128)(2,1)S(1)}, bf16[64,128]{1,0:T(8,128)(...) custom-call(bf16[32,128,128]{2,1,0:T(8,128)(2,1)S(1)} %copy-done, ...), custom_call_target="tpu_custom_call" | custom-call | tf_op jit(solution)/shard_map/right_own/pallas_call | solution.py:212
  5.5 0.0 collective-permute-done.1.mask
  5.5 0.0 collective-permute-done.pair
  5.5 1.6 %right_twin.1 = (bf16[32,32,256]{2,1,0:T(8,128)(2,1)S(1)}, bf16[4096,128]{1,0:T(8,128)(2,1)S(1)}, f32[1,32,128]{2,1,0:T(8,128)S(1)}) custom-call(bf16[32,128,128]{2,1,0:T(8,128)(2,1)S(1)} %collective-permute-done.pair, s32[32,128]{1,0:T(8,128)S(1)} %collective-permute-done.1.mask, f32[1,128]{1,0:T(1,128)S(1)} %get-tuple-element.45.gain, ...), custom_call_target="tpu_custom_call" | custom-call | tf_op jit(solution)/shard_map/right_twin/pallas_call | solution.py:212
  7.1 2.4 %collective-permute-start.3 = (bf16[32,32,256]{2,1,0:T(8,128)(2,1)S(1)}, bf16[32,32,256]{2,1,0:T(8,128)(2,1)S(1)}, u32[]{:S(2)}, u32[]{:S(2)}) collective-permute-start(bf16[32,32,256]{2,1,0:T(8,128)(2,1)S(1)} %get-tuple-element.56.rest_2_), channel_id=1, source_target_pairs={{0,4},{1,5},{2,6},{3,7},{4,0},{5,1},{6,2},{7,3},{8,12},{9,13},{10,... | collective-permute-start | bytes 1572872 | tf_op jit(solution)/shard_map/end_right_0/ppermute | solution.py:242
  9.5 0.8 %collective-permute-start.6 = (bf16[32,32,256]{2,1,0:T(8,128)(2,1)S(1)}, bf16[32,32,256]{2,1,0:T(8,128)(2,1)S(1)}, u32[]{:S(2)}, u32[]{:S(2)}) collective-permute-start(bf16[32,32,256]{2,1,0:T(8,128)(2,1)S(1)} %get-tuple-element.56.rest_2_), channel_id=1, source_target_pairs={{0,1},{1,0},{2,3},{3,2},{4,8},{5,9},{6,10},{7,11},{8,4},{9,5},{10,... | collective-permute-start | bytes 1572872 | tf_op jit(solution)/shard_map/mid_own_0/ppermute | solution.py:242
  10.3 0.9 %right_neighbour.1 = (bf16[18,32,256]{2,1,0:T(8,128)(2,1)S(1)}, bf16[14,32,256]{2,1,0:T(8,128)(2,1)S(1)}) custom-call(bf16[4096,128]{1,0:T(8,128)(2,1)S(1)} %get-tuple-element.44.normed.normed0, bf16[4096,128]{1,0:T(8,128)(2,1)S(1)} %get-tuple-element.48.normed1, f32[1,32,128]{2,1,0:T(8,128)S(1)} %get-tuple-element.49.valid0, ...), custom_call_target="tpu_custom_call" | custom-call | tf_op jit(solution)/shard_map/right_neighbour/pallas_call | solution.py:212
  11.2 1.3 %collective-permute-start.2 = (bf16[18,32,256]{2,1,0:T(8,128)(2,1)S(1)}, bf16[18,32,256]{2,1,0:T(8,128)(2,1)S(1)}, u32[]{:S(2)}, u32[]{:S(2)}) collective-permute-start(bf16[18,32,256]{2,1,0:T(8,128)(2,1)S(1)} %get-tuple-element.55), channel_id=1, source_target_pairs={{0,2},{1,3},{2,0},{3,1},{4,6},{5,7},{6,4},{7,5},{8,10},{9,11},{10,... | collective-permute-start | bytes 884744 | tf_op jit(solution)/shard_map/cross_right_0/ppermute | solution.py:242
  12.5 0.9 %left.1 = (bf16[32,32,256]{2,1,0:T(8,128)(2,1)S(1)}, bf16[18,32,256]{2,1,0:T(8,128)(2,1)S(1)}, bf16[14,32,256]{2,1,0:T(8,128)(2,1)S(1)}) custom-call(bf16[4096,128]{1,0:T(8,128)(2,1)S(1)} %get-tuple-element.44.normed.normed0, bf16[4096,128]{1,0:T(8,128)(2,1)S(1)} %get-tuple-element.48.normed1, f32[1,32,128]{2,1,0:T(8,128)S(1)} %get-tuple-element.49.valid0, ...), custom_call_target="tpu_custom_call" | custom-call | tf_op jit(solution)/shard_map/left/pallas_call | solution.py:212
  13.4 6.5 %collective-permute-done.2.rest_3_ = bf16[18,32,256]{2,1,0:T(8,128)(2,1)S(1)} collective-permute-done((bf16[18,32,256]{2,1,0:T(8,128)(2,1)S(1)}, bf16[18,32,256]{2,1,0:T(8,128)(2,1)S(1)}, u32[]{:S(2)}, u32[]{:S(2)}) %collective-permute-start.2) | collective-permute-done | bytes 294944 | tf_op jit(solution)/shard_map/cross_right_0/ppermute | solution.py:242
  19.9 0.8 %collective-permute-start.9 = (bf16[18,32,256]{2,1,0:T(8,128)(2,1)S(1)}, bf16[18,32,256]{2,1,0:T(8,128)(2,1)S(1)}, u32[]{:S(2)}, u32[]{:S(2)}) collective-permute-start(bf16[18,32,256]{2,1,0:T(8,128)(2,1)S(1)} %collective-permute-done.2.rest_3_), channel_id=1, source_target_pairs={{0,1},{1,0},{2,3},{3,2},{4,8},{5,9},{6,10},{7,11},{8,4},{9,5},{10,... | collective-permute-start | bytes 884744 | tf_op jit(solution)/shard_map/mid_own_10/ppermute | solution.py:242
  20.7 0.1 collective-permute-start.5
  20.8 0.5 collective-permute-done.3.rest_4_
  21.3 1.1 %collective-permute-start.4 = (bf16[18,32,256]{2,1,0:T(8,128)(2,1)S(1)}, bf16[18,32,256]{2,1,0:T(8,128)(2,1)S(1)}, u32[]{:S(2)}, u32[]{:S(2)}) collective-permute-start(bf16[18,32,256]{2,1,0:T(8,128)(2,1)S(1)} %get-tuple-element.57), channel_id=1, source_target_pairs={{0,2},{1,3},{2,0},{3,1},{4,6},{5,7},{6,4},{7,5},{8,10},{9,11},{10,... | collective-permute-start | bytes 884744 | tf_op jit(solution)/shard_map/cross_left_0/ppermute | solution.py:242
  22.4 0.0 collective-permute-done.6.rest_4_
  22.4 2.2 %collective-permute-start.10 = (bf16[32,32,256]{2,1,0:T(8,128)(2,1)S(1)}, bf16[32,32,256]{2,1,0:T(8,128)(2,1)S(1)}, u32[]{:S(2)}, u32[]{:S(2)}) collective-permute-start(bf16[32,32,256]{2,1,0:T(8,128)(2,1)S(1)} %collective-permute-done.3.rest_4_), channel_id=1, source_target_pairs={{0,1},{1,0},{2,3},{3,2},{4,8},{5,9},{6,10},{7,11},{8,4},{9,5},{10,... | collective-permute-start | bytes 1572872 | tf_op jit(solution)/shard_map/mid_next_0/ppermute | solution.py:242
  24.6 0.4 collective-permute-start.7
  25.0 3.9 %collective-permute-done.5.rest_5_ = bf16[18,32,256]{2,1,0:T(8,128)(2,1)S(1)} collective-permute-done((bf16[18,32,256]{2,1,0:T(8,128)(2,1)S(1)}, bf16[18,32,256]{2,1,0:T(8,128)(2,1)S(1)}, u32[]{:S(2)}, u32[]{:S(2)}) %collective-permute-start.5) | collective-permute-done | bytes 294944 | tf_op jit(solution)/shard_map/end_right_10/ppermute | solution.py:242
  28.9 0.0 collective-permute-done.4.rest_1_
  28.9 1.3 %collective-permute-start.12 = (bf16[14,32,256]{2,1,0:T(8,128)(2,1)S(1)}, bf16[14,32,256]{2,1,0:T(8,128)(2,1)S(1)}, u32[]{:S(2)}, u32[]{:S(2)}) collective-permute-start(bf16[14,32,256]{2,1,0:T(8,128)(2,1)S(1)} %get-tuple-element.65), channel_id=1, source_target_pairs={{0,2},{1,3},{2,0},{3,1},{4,6},{5,7},{6,4},{7,5},{8,10},{9,11},{10,... | collective-permute-start | bytes 688136 | tf_op jit(solution)/shard_map/cross_right_1/ppermute | solution.py:242
  30.2 0.4 gate.1
  30.6 2.3 %collective-permute-start.11 = (bf16[18,32,256]{2,1,0:T(8,128)(2,1)S(1)}, bf16[18,32,256]{2,1,0:T(8,128)(2,1)S(1)}, u32[]{:S(2)}, u32[]{:S(2)}) collective-permute-start(bf16[18,32,256]{2,1,0:T(8,128)(2,1)S(1)} %collective-permute-done.5.rest_5_), channel_id=1, source_target_pairs={{0,1},{1,0},{2,3},{3,2},{4,8},{5,9},{6,10},{7,11},{8,4},{9,5},{10,... | collective-permute-start | bytes 884744 | tf_op jit(solution)/shard_map/mid_next_10/ppermute | solution.py:242
  32.9 0.0 collective-permute-start.8
  32.9 1.2 %collective-permute-done.12.rest_3_ = bf16[14,32,256]{2,1,0:T(8,128)(2,1)S(1)} collective-permute-done((bf16[14,32,256]{2,1,0:T(8,128)(2,1)S(1)}, bf16[14,32,256]{2,1,0:T(8,128)(2,1)S(1)}, u32[]{:S(2)}, u32[]{:S(2)}) %collective-permute-start.12) | collective-permute-done | bytes 229408 | tf_op jit(solution)/shard_map/cross_right_1/ppermute | solution.py:242
  34.1 1.3 %collective-permute-start.13 = (bf16[14,32,256]{2,1,0:T(8,128)(2,1)S(1)}, bf16[14,32,256]{2,1,0:T(8,128)(2,1)S(1)}, u32[]{:S(2)}, u32[]{:S(2)}) collective-permute-start(bf16[14,32,256]{2,1,0:T(8,128)(2,1)S(1)} %get-tuple-element.66), channel_id=1, source_target_pairs={{0,2},{1,3},{2,0},{3,1},{4,6},{5,7},{6,4},{7,5},{8,10},{9,11},{10,... | collective-permute-start | bytes 688136 | tf_op jit(solution)/shard_map/cross_left_1/ppermute | solution.py:242
  35.4 4.8 %collective-permute-done.7.rest_2_ = bf16[32,32,256]{2,1,0:T(8,128)(2,1)S(1)} collective-permute-done((bf16[32,32,256]{2,1,0:T(8,128)(2,1)S(1)}, bf16[32,32,256]{2,1,0:T(8,128)(2,1)S(1)}, u32[]{:S(2)}, u32[]{:S(2)}) %collective-permute-start.7) | collective-permute-done | bytes 524320 | tf_op jit(solution)/shard_map/end_left_0/ppermute | solution.py:242
  40.2 2.0 %collective-permute-start.18 = (bf16[14,32,256]{2,1,0:T(8,128)(2,1)S(1)}, bf16[14,32,256]{2,1,0:T(8,128)(2,1)S(1)}, u32[]{:S(2)}, u32[]{:S(2)}) collective-permute-start(bf16[14,32,256]{2,1,0:T(8,128)(2,1)S(1)} %collective-permute-done.12.rest_3_), channel_id=1, source_target_pairs={{0,4},{1,5},{2,6},{3,7},{4,0},{5,1},{6,2},{7,3},{8,12},{9,13},{10,... | collective-permute-start | bytes 688136 | tf_op jit(solution)/shard_map/end_right_11/ppermute | solution.py:242
  42.2 3.3 %collective-permute-start.19 = (bf16[14,32,256]{2,1,0:T(8,128)(2,1)S(1)}, bf16[14,32,256]{2,1,0:T(8,128)(2,1)S(1)}, u32[]{:S(2)}, u32[]{:S(2)}) collective-permute-start(bf16[14,32,256]{2,1,0:T(8,128)(2,1)S(1)} %collective-permute-done.12.rest_3_), channel_id=1, source_target_pairs={{0,1},{1,0},{2,3},{3,2},{4,8},{5,9},{6,10},{7,11},{8,4},{9,5},{10,... | collective-permute-start | bytes 688136 | tf_op jit(solution)/shard_map/mid_own_11/ppermute | solution.py:242
  45.5 1.0 %collective-permute-done.8.rest_3_ = bf16[18,32,256]{2,1,0:T(8,128)(2,1)S(1)} collective-permute-done((bf16[18,32,256]{2,1,0:T(8,128)(2,1)S(1)}, bf16[18,32,256]{2,1,0:T(8,128)(2,1)S(1)}, u32[]{:S(2)}, u32[]{:S(2)}) %collective-permute-start.8) | collective-permute-done | bytes 294944 | tf_op jit(solution)/shard_map/end_left_10/ppermute | solution.py:242
  46.5 0.0 collective-permute-done.13.rest_8_.rest_1_
  46.5 0.6 away.2
  47.1 0.9 %collective-permute-start.14 = (bf16[18,32,256]{2,1,0:T(8,128)(2,1)S(1)}, bf16[18,32,256]{2,1,0:T(8,128)(2,1)S(1)}, u32[]{:S(2)}, u32[]{:S(2)}) collective-permute-start(bf16[18,32,256]{2,1,0:T(8,128)(2,1)S(1)} %get-tuple-element.68), channel_id=1, source_target_pairs={{0,4},{1,5},{2,6},{3,7},{4,0},{5,1},{6,2},{7,3},{8,12},{9,13},{10,... | collective-permute-start | bytes 884744 | tf_op jit(solution)/shard_map/left_11_and_products_back_0/ppermute | solution.py:242
  47.9 3.5 %collective-permute-done.18.rest_5_ = bf16[14,32,256]{2,1,0:T(8,128)(2,1)S(1)} collective-permute-done((bf16[14,32,256]{2,1,0:T(8,128)(2,1)S(1)}, bf16[14,32,256]{2,1,0:T(8,128)(2,1)S(1)}, u32[]{:S(2)}, u32[]{:S(2)}) %collective-permute-start.18) | collective-permute-done | bytes 229408 | tf_op jit(solution)/shard_map/end_right_11/ppermute | solution.py:242
  51.4 0.0 collective-permute-done.19.rest_5_
  51.4 2.0 %collective-permute-start.20 = (bf16[14,32,256]{2,1,0:T(8,128)(2,1)S(1)}, bf16[14,32,256]{2,1,0:T(8,128)(2,1)S(1)}, u32[]{:S(2)}, u32[]{:S(2)}) collective-permute-start(bf16[14,32,256]{2,1,0:T(8,128)(2,1)S(1)} %collective-permute-done.18.rest_5_), channel_id=1, source_target_pairs={{0,1},{1,0},{2,3},{3,2},{4,8},{5,9},{6,10},{7,11},{8,4},{9,5},{10,... | collective-permute-start | bytes 688136 | tf_op jit(solution)/shard_map/mid_next_11/ppermute | solution.py:242
  53.4 0.6 near.2
  54.0 0.5 near.3
  54.5 3.2 %collective-permute-done.14.end.rest_3_ = bf16[18,32,256]{2,1,0:T(8,128)(2,1)S(1)} collective-permute-done((bf16[18,32,256]{2,1,0:T(8,128)(2,1)S(1)}, bf16[18,32,256]{2,1,0:T(8,128)(2,1)S(1)}, u32[]{:S(2)}, u32[]{:S(2)}) %collective-permute-start.14) | collective-permute-done | bytes 294944 | tf_op jit(solution)/shard_map/left_11_and_products_back_0/ppermute | solution.py:242
  57.7 0.1 hand_out.2
  57.8 0.0 copy-start.3
  57.8 0.0 copy-start.6
  57.8 0.0 collective-permute-done.20.rest_7_
  57.9 0.5 away.3
  58.3 0.1 collective-permute-start.21
  58.4 2.8 %collective-permute-start.15 = (bf16[18,32,128]{2,1,0:T(8,128)(2,1)S(1)}, bf16[18,32,128]{2,1,0:T(8,128)(2,1)S(1)}, u32[]{:S(2)}, u32[]{:S(2)}) collective-permute-start(bf16[18,32,128]{2,1,0:T(8,128)(2,1)S(1)} %get-tuple-element.70), channel_id=1, source_target_pairs={{0,1},{1,0},{2,3},{3,2},{4,5},{5,4},{6,7},{7,6},{8,9},{9,8},{10,11... | collective-permute-start | bytes 442376 | tf_op jit(solution)/shard_map/return_01/ppermute | solution.py:242
  61.2 1.2 %collective-permute-start.16 = (bf16[18,32,128]{2,1,0:T(8,128)(2,1)S(1)}, bf16[18,32,128]{2,1,0:T(8,128)(2,1)S(1)}, u32[]{:S(2)}, u32[]{:S(2)}) collective-permute-start(bf16[18,32,128]{2,1,0:T(8,128)(2,1)S(1)} %get-tuple-element.71), channel_id=1, source_target_pairs={{0,2},{1,3},{2,0},{3,1},{4,6},{5,7},{6,4},{7,5},{8,10},{9,11},{10,... | collective-permute-start | bytes 442376 | tf_op jit(solution)/shard_map/return_02/ppermute | solution.py:242
  62.4 0.4 collective-permute-start.17
  62.8 1.5 %collective-permute-done.21.end = bf16[14,32,256]{2,1,0:T(8,128)(2,1)S(1)} collective-permute-done((bf16[14,32,256]{2,1,0:T(8,128)(2,1)S(1)}, bf16[14,32,256]{2,1,0:T(8,128)(2,1)S(1)}, u32[]{:S(2)}, u32[]{:S(2)}) %collective-permute-start.21) | collective-permute-done | bytes 229408 | tf_op jit(solution)/shard_map/products_back_1/ppermute | solution.py:242
  64.3 0.1 hand_out.3
  64.4 2.2 %collective-permute-start.22 = (bf16[14,32,128]{2,1,0:T(8,128)(2,1)S(1)}, bf16[14,32,128]{2,1,0:T(8,128)(2,1)S(1)}, u32[]{:S(2)}, u32[]{:S(2)}) collective-permute-start(bf16[14,32,128]{2,1,0:T(8,128)(2,1)S(1)} %get-tuple-element.80), channel_id=1, source_target_pairs={{0,1},{1,0},{2,3},{3,2},{4,5},{5,4},{6,7},{7,6},{8,9},{9,8},{10,11... | collective-permute-start | bytes 344072 | tf_op jit(solution)/shard_map/return_11/ppermute | solution.py:242
  66.6 1.3 %collective-permute-start.23 = (bf16[14,32,128]{2,1,0:T(8,128)(2,1)S(1)}, bf16[14,32,128]{2,1,0:T(8,128)(2,1)S(1)}, u32[]{:S(2)}, u32[]{:S(2)}) collective-permute-start(bf16[14,32,128]{2,1,0:T(8,128)(2,1)S(1)} %get-tuple-element.81), channel_id=1, source_target_pairs={{0,2},{1,3},{2,0},{3,1},{4,6},{5,7},{6,4},{7,5},{8,10},{9,11},{10,... | collective-permute-start | bytes 344072 | tf_op jit(solution)/shard_map/return_12/ppermute | solution.py:242
  67.9 0.4 collective-permute-start.24
  68.3 0.0 collective-permute-done.16.rest_2_
  68.3 2.0 %collective-permute-done.17.rest_3_ = bf16[18,32,128]{2,1,0:T(8,128)(2,1)S(1)} collective-permute-done((bf16[18,32,128]{2,1,0:T(8,128)(2,1)S(1)}, bf16[18,32,128]{2,1,0:T(8,128)(2,1)S(1)}, u32[]{:S(2)}, u32[]{:S(2)}) %collective-permute-start.17) | collective-permute-done | bytes 147488 | tf_op jit(solution)/shard_map/return_03/ppermute | solution.py:242
  70.3 0.0 collective-permute-done.22.rest_5_
  70.3 2.0 %collective-permute-done.23.rest_6_ = bf16[14,32,128]{2,1,0:T(8,128)(2,1)S(1)} collective-permute-done((bf16[14,32,128]{2,1,0:T(8,128)(2,1)S(1)}, bf16[14,32,128]{2,1,0:T(8,128)(2,1)S(1)}, u32[]{:S(2)}, u32[]{:S(2)}) %collective-permute-start.23) | collective-permute-done | bytes 114720 | tf_op jit(solution)/shard_map/return_12/ppermute | solution.py:242
  72.3 2.6 %collective-permute-done.24.rest_7_ = bf16[14,32,128]{2,1,0:T(8,128)(2,1)S(1)} collective-permute-done((bf16[14,32,128]{2,1,0:T(8,128)(2,1)S(1)}, bf16[14,32,128]{2,1,0:T(8,128)(2,1)S(1)}, u32[]{:S(2)}, u32[]{:S(2)}) %collective-permute-start.24) | collective-permute-done | bytes 114720 | tf_op jit(solution)/shard_map/return_13/ppermute | solution.py:242
  74.9 2.0 %update.1 = bf16[32,128,128]{2,1,0:T(8,128)(2,1)} custom-call(f32[1,128]{1,0:T(1,128)S(1)} %bitcast.3, bf16[128,128]{1,0:T(8,128)(2,1)S(1)} %copy-done.3, f32[32,128,128]{2,1,0:T(8,128)S(1)} %gate.1, bf16[18,32,128]{2,1,0:T(8,128)(2,1)S(1)} %get-tuple-element.69.rest_0_, bf16[18,32,128]{2,1,0:T(8,128)(2,1)S(1)} %collective-permute-done.15.rest_1_, ...), custom_call_target="tpu_custom_call" | custom-call | tf_op jit(solution)/shard_map/update/pallas_call | solution.py:212
  (12 shorter events, 0.0 us)
Async XLA Ops:
  0.0 5.5 %collective-permute-start = (bf16[32,128,128]{2,1,0:T(8,128)(2,1)}, bf16[32,128,128]{2,1,0:T(8,128)(2,1)S(1)}, u32[]{:S(2)}, u32[]{:S(2)}) collective-permute-start(bf16[32,128,128]{2,1,0:T(8,128)(2,1)} %pair.1), channel_id=1, source_target_pairs={{0,1},{1,0},{2,3},{3,2},{4,5},{5,4},{6,7},{7,6},{8,9},{9,8},{10,11... | collective-permute-start | bytes 3145736 | tf_op jit(solution)/shard_map/pair/ppermute | solution.py:242
  0.1 5.5 %collective-permute-start.1 = (s32[32,128]{1,0:T(8,128)}, s32[32,128]{1,0:T(8,128)S(1)}, u32[]{:S(2)}, u32[]{:S(2)}) collective-permute-start(s32[32,128]{1,0:T(8,128)} %mask.1), channel_id=1, source_target_pairs={{0,1},{1,0},{2,3},{3,2},{4,5},{5,4},{6,7},{7,6},{8,9},{9,8},{10,11... | collective-permute-start | bytes 49160 | tf_op jit(solution)/shard_map/mask/ppermute | solution.py:242
  0.5 1.2 %copy-start = (bf16[32,128,128]{2,1,0:T(8,128)(2,1)S(1)}, bf16[32,128,128]{2,1,0:T(8,128)(2,1)}, u32[]{:S(2)}) copy-start(bf16[32,128,128]{2,1,0:T(8,128)(2,1)} %pair.1) | copy-start | bytes 3145732
  1.7 0.9 %copy-start.1 = (bf16[128,512]{1,0:T(8,128)(2,1)S(1)}, bf16[128,512]{1,0:T(8,128)(2,1)}, u32[]{:S(2)}) copy-start(bf16[128,512]{1,0:T(8,128)(2,1)} %weight.3) | copy-start | bytes 393220
  2.6 0.7 copy-start.4
  3.4 0.7 copy-start.5
  7.1 14.2 %collective-permute-start.3 = (bf16[32,32,256]{2,1,0:T(8,128)(2,1)S(1)}, bf16[32,32,256]{2,1,0:T(8,128)(2,1)S(1)}, u32[]{:S(2)}, u32[]{:S(2)}) collective-permute-start(bf16[32,32,256]{2,1,0:T(8,128)(2,1)S(1)} %get-tuple-element.56.rest_2_), channel_id=1, source_target_pairs={{0,4},{1,5},{2,6},{3,7},{4,0},{5,1},{6,2},{7,3},{8,12},{9,13},{10,... | collective-permute-start | bytes 1572872 | tf_op jit(solution)/shard_map/end_right_0/ppermute | solution.py:242
  9.5 12.9 %collective-permute-start.6 = (bf16[32,32,256]{2,1,0:T(8,128)(2,1)S(1)}, bf16[32,32,256]{2,1,0:T(8,128)(2,1)S(1)}, u32[]{:S(2)}, u32[]{:S(2)}) collective-permute-start(bf16[32,32,256]{2,1,0:T(8,128)(2,1)S(1)} %get-tuple-element.56.rest_2_), channel_id=1, source_target_pairs={{0,1},{1,0},{2,3},{3,2},{4,8},{5,9},{6,10},{7,11},{8,4},{9,5},{10,... | collective-permute-start | bytes 1572872 | tf_op jit(solution)/shard_map/mid_own_0/ppermute | solution.py:242
  10.3 19.9 %copy-start.2 = (bf16[128,128]{1,0:T(8,128)(2,1)S(1)}, bf16[128,128]{1,0:T(8,128)(2,1)}, u32[]{:S(2)}) copy-start(bf16[128,128]{1,0:T(8,128)(2,1)} %weight.4) | copy-start | bytes 98308
  11.2 8.7 %collective-permute-start.2 = (bf16[18,32,256]{2,1,0:T(8,128)(2,1)S(1)}, bf16[18,32,256]{2,1,0:T(8,128)(2,1)S(1)}, u32[]{:S(2)}, u32[]{:S(2)}) collective-permute-start(bf16[18,32,256]{2,1,0:T(8,128)(2,1)S(1)} %get-tuple-element.55), channel_id=1, source_target_pairs={{0,2},{1,3},{2,0},{3,1},{4,6},{5,7},{6,4},{7,5},{8,10},{9,11},{10,... | collective-permute-start | bytes 884744 | tf_op jit(solution)/shard_map/cross_right_0/ppermute | solution.py:242
  19.9 5.1 %collective-permute-start.9 = (bf16[18,32,256]{2,1,0:T(8,128)(2,1)S(1)}, bf16[18,32,256]{2,1,0:T(8,128)(2,1)S(1)}, u32[]{:S(2)}, u32[]{:S(2)}) collective-permute-start(bf16[18,32,256]{2,1,0:T(8,128)(2,1)S(1)} %collective-permute-done.2.rest_3_), channel_id=1, source_target_pairs={{0,1},{1,0},{2,3},{3,2},{4,8},{5,9},{6,10},{7,11},{8,4},{9,5},{10,... | collective-permute-start | bytes 884744 | tf_op jit(solution)/shard_map/mid_own_10/ppermute | solution.py:242
  20.7 8.2 %collective-permute-start.5 = (bf16[18,32,256]{2,1,0:T(8,128)(2,1)S(1)}, bf16[18,32,256]{2,1,0:T(8,128)(2,1)S(1)}, u32[]{:S(2)}, u32[]{:S(2)}) collective-permute-start(bf16[18,32,256]{2,1,0:T(8,128)(2,1)S(1)} %collective-permute-done.2.rest_3_), channel_id=1, source_target_pairs={{0,4},{1,5},{2,6},{3,7},{4,0},{5,1},{6,2},{7,3},{8,12},{9,13},{10,... | collective-permute-start | bytes 884744 | tf_op jit(solution)/shard_map/end_right_10/ppermute | solution.py:242
  21.3 7.6 %collective-permute-start.4 = (bf16[18,32,256]{2,1,0:T(8,128)(2,1)S(1)}, bf16[18,32,256]{2,1,0:T(8,128)(2,1)S(1)}, u32[]{:S(2)}, u32[]{:S(2)}) collective-permute-start(bf16[18,32,256]{2,1,0:T(8,128)(2,1)S(1)} %get-tuple-element.57), channel_id=1, source_target_pairs={{0,2},{1,3},{2,0},{3,1},{4,6},{5,7},{6,4},{7,5},{8,10},{9,11},{10,... | collective-permute-start | bytes 884744 | tf_op jit(solution)/shard_map/cross_left_0/ppermute | solution.py:242
  22.4 11.7 %collective-permute-start.10 = (bf16[32,32,256]{2,1,0:T(8,128)(2,1)S(1)}, bf16[32,32,256]{2,1,0:T(8,128)(2,1)S(1)}, u32[]{:S(2)}, u32[]{:S(2)}) collective-permute-start(bf16[32,32,256]{2,1,0:T(8,128)(2,1)S(1)} %collective-permute-done.3.rest_4_), channel_id=1, source_target_pairs={{0,1},{1,0},{2,3},{3,2},{4,8},{5,9},{6,10},{7,11},{8,4},{9,5},{10,... | collective-permute-start | bytes 1572872 | tf_op jit(solution)/shard_map/mid_next_0/ppermute | solution.py:242
  24.6 15.6 %collective-permute-start.7 = (bf16[32,32,256]{2,1,0:T(8,128)(2,1)S(1)}, bf16[32,32,256]{2,1,0:T(8,128)(2,1)S(1)}, u32[]{:S(2)}, u32[]{:S(2)}) collective-permute-start(bf16[32,32,256]{2,1,0:T(8,128)(2,1)S(1)} %get-tuple-element.74.rest_0_), channel_id=1, source_target_pairs={{0,4},{1,5},{2,6},{3,7},{4,0},{5,1},{6,2},{7,3},{8,12},{9,13},{10,... | collective-permute-start | bytes 1572872 | tf_op jit(solution)/shard_map/end_left_0/ppermute | solution.py:242
  28.9 5.2 %collective-permute-start.12 = (bf16[14,32,256]{2,1,0:T(8,128)(2,1)S(1)}, bf16[14,32,256]{2,1,0:T(8,128)(2,1)S(1)}, u32[]{:S(2)}, u32[]{:S(2)}) collective-permute-start(bf16[14,32,256]{2,1,0:T(8,128)(2,1)S(1)} %get-tuple-element.65), channel_id=1, source_target_pairs={{0,2},{1,3},{2,0},{3,1},{4,6},{5,7},{6,4},{7,5},{8,10},{9,11},{10,... | collective-permute-start | bytes 688136 | tf_op jit(solution)/shard_map/cross_right_1/ppermute | solution.py:242
  30.6 14.9 %collective-permute-start.11 = (bf16[18,32,256]{2,1,0:T(8,128)(2,1)S(1)}, bf16[18,32,256]{2,1,0:T(8,128)(2,1)S(1)}, u32[]{:S(2)}, u32[]{:S(2)}) collective-permute-start(bf16[18,32,256]{2,1,0:T(8,128)(2,1)S(1)} %collective-permute-done.5.rest_5_), channel_id=1, source_target_pairs={{0,1},{1,0},{2,3},{3,2},{4,8},{5,9},{6,10},{7,11},{8,4},{9,5},{10,... | collective-permute-start | bytes 884744 | tf_op jit(solution)/shard_map/mid_next_10/ppermute | solution.py:242
  32.9 13.6 %collective-permute-start.8 = (bf16[18,32,256]{2,1,0:T(8,128)(2,1)S(1)}, bf16[18,32,256]{2,1,0:T(8,128)(2,1)S(1)}, u32[]{:S(2)}, u32[]{:S(2)}) collective-permute-start(bf16[18,32,256]{2,1,0:T(8,128)(2,1)S(1)} %collective-permute-done.4.rest_1_), channel_id=1, source_target_pairs={{0,4},{1,5},{2,6},{3,7},{4,0},{5,1},{6,2},{7,3},{8,12},{9,13},{10,... | collective-permute-start | bytes 884744 | tf_op jit(solution)/shard_map/end_left_10/ppermute | solution.py:242
  34.1 12.4 %collective-permute-start.13 = (bf16[14,32,256]{2,1,0:T(8,128)(2,1)S(1)}, bf16[14,32,256]{2,1,0:T(8,128)(2,1)S(1)}, u32[]{:S(2)}, u32[]{:S(2)}) collective-permute-start(bf16[14,32,256]{2,1,0:T(8,128)(2,1)S(1)} %get-tuple-element.66), channel_id=1, source_target_pairs={{0,2},{1,3},{2,0},{3,1},{4,6},{5,7},{6,4},{7,5},{8,10},{9,11},{10,... | collective-permute-start | bytes 688136 | tf_op jit(solution)/shard_map/cross_left_1/ppermute | solution.py:242
  40.2 11.2 %collective-permute-start.18 = (bf16[14,32,256]{2,1,0:T(8,128)(2,1)S(1)}, bf16[14,32,256]{2,1,0:T(8,128)(2,1)S(1)}, u32[]{:S(2)}, u32[]{:S(2)}) collective-permute-start(bf16[14,32,256]{2,1,0:T(8,128)(2,1)S(1)} %collective-permute-done.12.rest_3_), channel_id=1, source_target_pairs={{0,4},{1,5},{2,6},{3,7},{4,0},{5,1},{6,2},{7,3},{8,12},{9,13},{10,... | collective-permute-start | bytes 688136 | tf_op jit(solution)/shard_map/end_right_11/ppermute | solution.py:242
  42.2 9.2 %collective-permute-start.19 = (bf16[14,32,256]{2,1,0:T(8,128)(2,1)S(1)}, bf16[14,32,256]{2,1,0:T(8,128)(2,1)S(1)}, u32[]{:S(2)}, u32[]{:S(2)}) collective-permute-start(bf16[14,32,256]{2,1,0:T(8,128)(2,1)S(1)} %collective-permute-done.12.rest_3_), channel_id=1, source_target_pairs={{0,1},{1,0},{2,3},{3,2},{4,8},{5,9},{6,10},{7,11},{8,4},{9,5},{10,... | collective-permute-start | bytes 688136 | tf_op jit(solution)/shard_map/mid_own_11/ppermute | solution.py:242
  47.1 10.6 %collective-permute-start.14 = (bf16[18,32,256]{2,1,0:T(8,128)(2,1)S(1)}, bf16[18,32,256]{2,1,0:T(8,128)(2,1)S(1)}, u32[]{:S(2)}, u32[]{:S(2)}) collective-permute-start(bf16[18,32,256]{2,1,0:T(8,128)(2,1)S(1)} %get-tuple-element.68), channel_id=1, source_target_pairs={{0,4},{1,5},{2,6},{3,7},{4,0},{5,1},{6,2},{7,3},{8,12},{9,13},{10,... | collective-permute-start | bytes 884744 | tf_op jit(solution)/shard_map/left_11_and_products_back_0/ppermute | solution.py:242
  51.4 6.4 %collective-permute-start.20 = (bf16[14,32,256]{2,1,0:T(8,128)(2,1)S(1)}, bf16[14,32,256]{2,1,0:T(8,128)(2,1)S(1)}, u32[]{:S(2)}, u32[]{:S(2)}) collective-permute-start(bf16[14,32,256]{2,1,0:T(8,128)(2,1)S(1)} %collective-permute-done.18.rest_5_), channel_id=1, source_target_pairs={{0,1},{1,0},{2,3},{3,2},{4,8},{5,9},{6,10},{7,11},{8,4},{9,5},{10,... | collective-permute-start | bytes 688136 | tf_op jit(solution)/shard_map/mid_next_11/ppermute | solution.py:242
  57.8 17.0 %copy-start.3 = (bf16[128,128]{1,0:T(8,128)(2,1)S(1)}, bf16[128,128]{1,0:T(8,128)(2,1)}, u32[]{:S(2)}) copy-start(bf16[128,128]{1,0:T(8,128)(2,1)} %weight.5) | copy-start | bytes 98308
  57.8 17.0 %copy-start.6 = (f32[128]{0:T(128)S(1)}, f32[128]{0:T(128)}, u32[]{:S(2)}) copy-start(f32[128]{0:T(128)} %param.12) | copy-start | bytes 1540
  58.3 6.0 %collective-permute-start.21 = (bf16[14,32,256]{2,1,0:T(8,128)(2,1)S(1)}, bf16[14,32,256]{2,1,0:T(8,128)(2,1)S(1)}, u32[]{:S(2)}, u32[]{:S(2)}) collective-permute-start(bf16[14,32,256]{2,1,0:T(8,128)(2,1)S(1)} %get-tuple-element.78), channel_id=1, source_target_pairs={{0,4},{1,5},{2,6},{3,7},{4,0},{5,1},{6,2},{7,3},{8,12},{9,13},{10,... | collective-permute-start | bytes 688136 | tf_op jit(solution)/shard_map/products_back_1/ppermute | solution.py:242
  58.4 9.4 %collective-permute-start.15 = (bf16[18,32,128]{2,1,0:T(8,128)(2,1)S(1)}, bf16[18,32,128]{2,1,0:T(8,128)(2,1)S(1)}, u32[]{:S(2)}, u32[]{:S(2)}) collective-permute-start(bf16[18,32,128]{2,1,0:T(8,128)(2,1)S(1)} %get-tuple-element.70), channel_id=1, source_target_pairs={{0,1},{1,0},{2,3},{3,2},{4,5},{5,4},{6,7},{7,6},{8,9},{9,8},{10,11... | collective-permute-start | bytes 442376 | tf_op jit(solution)/shard_map/return_01/ppermute | solution.py:242
  61.2 7.1 %collective-permute-start.16 = (bf16[18,32,128]{2,1,0:T(8,128)(2,1)S(1)}, bf16[18,32,128]{2,1,0:T(8,128)(2,1)S(1)}, u32[]{:S(2)}, u32[]{:S(2)}) collective-permute-start(bf16[18,32,128]{2,1,0:T(8,128)(2,1)S(1)} %get-tuple-element.71), channel_id=1, source_target_pairs={{0,2},{1,3},{2,0},{3,1},{4,6},{5,7},{6,4},{7,5},{8,10},{9,11},{10,... | collective-permute-start | bytes 442376 | tf_op jit(solution)/shard_map/return_02/ppermute | solution.py:242
  62.4 7.9 %collective-permute-start.17 = (bf16[18,32,128]{2,1,0:T(8,128)(2,1)S(1)}, bf16[18,32,128]{2,1,0:T(8,128)(2,1)S(1)}, u32[]{:S(2)}, u32[]{:S(2)}) collective-permute-start(bf16[18,32,128]{2,1,0:T(8,128)(2,1)S(1)} %get-tuple-element.72), channel_id=1, source_target_pairs={{0,3},{1,2},{2,1},{3,0},{4,7},{5,6},{6,5},{7,4},{8,11},{9,10},{10,... | collective-permute-start | bytes 442376 | tf_op jit(solution)/shard_map/return_03/ppermute | solution.py:242
  64.4 5.9 %collective-permute-start.22 = (bf16[14,32,128]{2,1,0:T(8,128)(2,1)S(1)}, bf16[14,32,128]{2,1,0:T(8,128)(2,1)S(1)}, u32[]{:S(2)}, u32[]{:S(2)}) collective-permute-start(bf16[14,32,128]{2,1,0:T(8,128)(2,1)S(1)} %get-tuple-element.80), channel_id=1, source_target_pairs={{0,1},{1,0},{2,3},{3,2},{4,5},{5,4},{6,7},{7,6},{8,9},{9,8},{10,11... | collective-permute-start | bytes 344072 | tf_op jit(solution)/shard_map/return_11/ppermute | solution.py:242
  66.6 5.7 %collective-permute-start.23 = (bf16[14,32,128]{2,1,0:T(8,128)(2,1)S(1)}, bf16[14,32,128]{2,1,0:T(8,128)(2,1)S(1)}, u32[]{:S(2)}, u32[]{:S(2)}) collective-permute-start(bf16[14,32,128]{2,1,0:T(8,128)(2,1)S(1)} %get-tuple-element.81), channel_id=1, source_target_pairs={{0,2},{1,3},{2,0},{3,1},{4,6},{5,7},{6,4},{7,5},{8,10},{9,11},{10,... | collective-permute-start | bytes 344072 | tf_op jit(solution)/shard_map/return_12/ppermute | solution.py:242
  67.9 7.0 %collective-permute-start.24 = (bf16[14,32,128]{2,1,0:T(8,128)(2,1)S(1)}, bf16[14,32,128]{2,1,0:T(8,128)(2,1)S(1)}, u32[]{:S(2)}, u32[]{:S(2)}) collective-permute-start(bf16[14,32,128]{2,1,0:T(8,128)(2,1)S(1)} %get-tuple-element.82), channel_id=1, source_target_pairs={{0,3},{1,2},{2,1},{3,0},{4,7},{5,6},{6,5},{7,4},{8,11},{9,10},{10,... | collective-permute-start | bytes 344072 | tf_op jit(solution)/shard_map/return_13/ppermute | solution.py:242

commit v18 on v17

--- a/solution.py
+++ b/solution.py
@@ -171,6 +171,85 @@
             outs[r][...] = end[:, :, lanes]
 
 
+def choose_kernel(planes, at_ends, elsewhere, out):
+    z, _, _ = place()
+    is_end = (z == 0) | (z == planes - 1)
+
+    @pl.when(is_end)
+    def _():
+        out[: at_ends.shape[0]] = at_ends[...]
+
+    @pl.when(jnp.logical_not(is_end))
+    def _():
+        out[: elsewhere.shape[0]] = elsewhere[...]
+
+
+def last_far_kernel(first, *refs):
+    left, outer, next_mid, next_end, last = (refs[2 * n : 2 * n + 2] for n in range(5))
+    away, ends, held, padded = refs[10:]
+    count, span, _ = away.shape
+    rows = span // 2
+    z, y, _ = place()
+    at_end = (z == 0) | (z == 3)
+    at = z // 2 * span
+    for p in range(2):
+        start = pl.multiple_of(at + (y ^ p) * rows, rows)
+        own = slice(first, first + count) if p == 0 else slice(0, count)
+
+        @pl.when(at_end)
+        def _():
+            held[:, pl.ds(start, rows), :] = next_end[p][own]
+
+        @pl.when(jnp.logical_not(at_end))
+        def _():
+            held[:, pl.ds(start, rows), :] = next_mid[p][own]
+
+        start = pl.multiple_of(span - at + (y ^ p) * rows, rows)
+        held[:, pl.ds(start, rows), :] = last[p][own]
+        start = pl.multiple_of(span + (y ^ p) * rows, rows)
+        padded[:, pl.ds(start, rows), :] = last[p][own]
+    padded[:, :span, :] = jnp.zeros((count, span, padded.shape[2]), BF16)
+    padded[:, 2 * span :, :] = jnp.zeros((count, span, padded.shape[2]), BF16)
+    for c in range(count):
+        mine = jnp.concatenate([left[0][first + c], left[1][c]], axis=0)
+        away[c] = lax.dot_general(mine, held[c], NT, preferred_element_type=F32).astype(BF16)
+        one = lax.dot_general(
+            outer[0][first + c], padded[c, span:, :], NT, preferred_element_type=F32
+        )
+        two = lax.dot_general(
+            outer[1][c], padded[c, : 2 * span, :], NT, preferred_element_type=F32
+        )
+        ends[c] = (one + two).astype(BF16)
+
+
+def last_hand_out_kernel(near, far, end, *outs):
+    _, rows, toks = outs[0].shape
+    z, _, core = place()
+    for r in range(4):
+        p = r // 2
+        is_near = (core ^ (r % 2)) == z // 2
+        span = slice(p * rows, (p + 1) * rows)
+
+        @pl.when(is_near)
+        def _():
+            outs[r][...] = near[:, span, :]
+
+        @pl.when(jnp.logical_not(is_near) & ((z == 1) | (z == 2)))
+        def _():
+            outs[r][...] = far[:, span, :]
+
+        for plane, upper in ((0, 1), (3, 0)):
+
+            @pl.when(jnp.logical_not(is_near) & (z == plane))
+            def _():
+                last = end[...].astype(F32)
+                if p != upper:
+                    last = pltpu.roll(last, toks // 2, 2)
+                lane = lax.broadcasted_iota(jnp.int32, last.shape, 2)
+                mixed = jnp.where(lane // (toks // 2) == upper, last, far[:, span, :].astype(F32))
+                outs[r][...] = mixed.astype(BF16)
+
+
 def update_kernel(gain, weight, gate, *rest):
     pieces, out, turned = rest[:-2], rest[-2], rest[-1]
     part = sum(x.shape[0] for x in pieces[::4])
@@ -318,18 +397,32 @@
     gate = kernel(
         gate_kernel, "gate", jax.ShapeDtypeStruct((rows, toks, channels), F32), [VMEM] * 2
     )(normed0, gate_weight)
+    split = planes == 4
+
+    def chosen(at_ends, elsewhere):
+        if not split:
+            return at_ends
+        longer = max(at_ends.shape[0], elsewhere.shape[0])
+        return kernel(
+            functools.partial(choose_kernel, planes),
+            "choose",
+            piece(longer, rows, 2 * toks),
+            [VMEM] * 2,
+        )(at_ends, elsewhere)
+
     right1[0] = after(crossed, left0)
     own1 = [mid("own_10", right1[0])]
     near1 = [end_right("10", right1[0])]
-    left1[0] = cross("left_0", left1[0], crossed, near0[-1])
+    right1[1] = cross("right_1", right1[1], crossed)
+    own1.append(mid("own_11", right1[1]))
+    left1[0] = cross("left_0", left1[0], right1[1], near0[-1], near1[0][-1], own1[0])
     next0 = [mid("next_0", x, own0) for x in near0]
-    outer0 = end_left("0", left0, own0)
-    right1[1] = cross("right_1", right1[1], left1[0], own1[0], near1[0][-1])
+    outer0 = end_left("0", chosen(left0, own0), near0[-1])
     next1 = [[mid("next_10", x, own1[0], gate) for x in near1[0]]]
-    outer1 = [end_left("10", left1[0], near1[0][-1])]
-    left1[1] = cross("left_1", left1[1], right1[1], next0[-1])
-    own1.append(mid("own_11", right1[1], own1[0]))
+    outer1 = [end_left("10", chosen(left1[0], own1[1]), near1[0][-1])]
+    left1[1] = cross("left_1", left1[1], left1[0], own1[1])
     near1.append(end_right("11", right1[1], outer0))
+
     def products(mirror, first, lefts, rights, name, instead=()):
         span = 2 * rows * len(rights)
         count = lefts[0][1].shape[0]
@@ -351,9 +444,9 @@
     def far_planes(g):
         return list(zip([own0, *next0], [own1[g], *next1[g]]))
 
-    def hand_out(g, close, away, ends):
+    def hand_out(g, body, close, away, ends):
         handed = kernel(
-            functools.partial(hand_out_kernel, planes),
+            body,
             "hand_out",
             [piece(counts[g], rows, toks)] * 4,
             [VMEM] * 3,
@@ -369,11 +462,23 @@
     away0, swapped = products(True, first[0], sides, far_planes(0), "away", [left1[1]])
     next1.append([mid("next_11", x, next1[0][-1], own1[1], away0) for x in near1[1]])
     swapped = send(swapped, edge, "left_11_and_products_back_0")
-    pieces = hand_out(0, close[0], away0, swapped)
+    body = functools.partial(hand_out_kernel, planes)
+    pieces = hand_out(0, body, close[0], away0, swapped)
     sides = [(after(left0, pieces[0], close[1]), left1[1]), (outer0, swapped)]
-    away1, ends = products(True, first[1], sides, far_planes(1), "away")
+    if split:
+        args = [*sides[0], *sides[1], own0, own1[1], outer0, outer1[0], next0[-1], next1[1][-1]]
+        away1, ends = kernel(
+            functools.partial(last_far_kernel, first[1]),
+            "away_last",
+            [piece(counts[1], 2 * rows, toks), piece(counts[1], rows, toks)],
+            [VMEM] * len(args),
+            [pltpu.VMEM((counts[1], n * rows, 2 * toks), BF16) for n in (4, 6)],
+        )(*args)
+    else:
+        away1, ends = products(True, first[1], sides, far_planes(1), "away")
     ends = send(ends, edge, "products_back_1")
-    pieces += hand_out(1, close[1], away1, ends)
+    body = last_hand_out_kernel if split else functools.partial(hand_out_kernel, planes)
+    pieces += hand_out(1, body, close[1], away1, ends)
 
     return kernel(
         update_kernel,

time: 77.4 us -> 81.7 us (1.056)
  starting transfers between devices: 30.9 us -> 38.4 us
  waiting for transfers between devices: 32.6 us -> 28.8 us
    ppermute x25, starting transfers between devices: 30.9 us -> 38.4 us  [send(): return lax.ppermute(x, ('row', 'chan'), pairs)]
    ppermute x25, waiting for transfers between devices: 32.6 us -> 28.8 us  [send(): return lax.ppermute(x, ('row', 'chan'), pairs)]
    pallas_call x12 -> x14, Pallas kernels: 9.74 us -> 10.5 us  [call(): pl.pallas_call(body, out_shape=out_shape, in_specs=in_specs, out_specs=ou...]
  transfers between devices with their start and end apart: 25 -> 25, of which waited for: 12 -> 12; matrix products, arithmetic and copies ran while one was open for 0% -> 0% of each run, Pallas kernels for 7% -> 9%
where the time goes in v18:
time: 81.7 us; the launch traced here: 81.4 us
  starting transfers between devices  38.4 us (47%)
  waiting for transfers between devices  28.8 us (35%)
  Pallas kernels  10.5 us (13%)
  local copies, waits for them, and re-layouts  3.52 us (4%)
    ppermute x25, starting transfers between devices, send(): return lax.ppermute(x, ('row', 'chan'), pairs)  38.4 us
    ppermute x25, waiting for transfers between devices, send(): return lax.ppermute(x, ('row', 'chan'), pairs)  28.8 us
    pallas_call x14, Pallas kernels, call(): pl.pallas_call(body, out_shape=out_shape, in_specs=in_specs, out_specs=ou...  10.5 us
    unnamed x14, local copies, waits for them, and re-layouts  3.52 us
  transfers between devices with their start and end apart: 25, of which 12 were waited for; matrix products, arithmetic and copies ran while one was open for 0% of the time, Pallas kernels for 9%

profile of v18, /device:TPU:1, one launch (start us, length us, event | category | flops | bytes accessed | tf_op | source)
XLA Modules:
  0.0 81.4 jit_solution(14609841128207746830)
XLA Ops:
  0.0 0.1 collective-permute-start
  0.1 0.5 collective-permute-start.1
  0.5 1.2 %copy-done = bf16[32,128,128]{2,1,0:T(8,128)(2,1)S(1)} copy-done((bf16[32,128,128]{2,1,0:T(8,128)(2,1)S(1)}, bf16[32,128,128]{2,1,0:T(8,128)(2,1)}, u32[]{:S(2)}) %copy-start) | copy-done | bytes 1048600
  1.7 0.9 %copy-done.1 = bf16[128,512]{1,0:T(8,128)(2,1)S(1)} copy-done((bf16[128,512]{1,0:T(8,128)(2,1)S(1)}, bf16[128,512]{1,0:T(8,128)(2,1)}, u32[]{:S(2)}) %copy-start.1) | copy-done | bytes 131096
  2.6 0.7 copy-done.4
  3.4 0.7 copy-done.5
  4.0 1.5 %right_own.1 = (bf16[32,32,128]{2,1,0:T(8,128)(2,1)S(1)}, bf16[4096,128]{1,0:T(8,128)(2,1)S(1)}, bf16[64,128]{1,0:T(8,128)(2,1)S(1)}, bf16[64,128]{1,0:T(8,128)(...) custom-call(bf16[32,128,128]{2,1,0:T(8,128)(2,1)S(1)} %copy-done, ...), custom_call_target="tpu_custom_call" | custom-call | tf_op jit(solution)/shard_map/right_own/pallas_call | solution.py:291
  5.5 0.0 collective-permute-done.1.mask
  5.5 0.0 collective-permute-done.pair
  5.5 1.6 %right_twin.1 = (bf16[32,32,256]{2,1,0:T(8,128)(2,1)S(1)}, bf16[4096,128]{1,0:T(8,128)(2,1)S(1)}, f32[1,32,128]{2,1,0:T(8,128)S(1)}) custom-call(bf16[32,128,128]{2,1,0:T(8,128)(2,1)S(1)} %collective-permute-done.pair, s32[32,128]{1,0:T(8,128)S(1)} %collective-permute-done.1.mask, f32[1,128]{1,0:T(1,128)S(1)} %get-tuple-element.44.gain, ...), custom_call_target="tpu_custom_call" | custom-call | tf_op jit(solution)/shard_map/right_twin/pallas_call | solution.py:291
  7.1 0.1 collective-permute-start.8
  7.3 3.5 %collective-permute-start.4 = (bf16[32,32,256]{2,1,0:T(8,128)(2,1)S(1)}, bf16[32,32,256]{2,1,0:T(8,128)(2,1)S(1)}, u32[]{:S(2)}, u32[]{:S(2)}) collective-permute-start(bf16[32,32,256]{2,1,0:T(8,128)(2,1)S(1)} %get-tuple-element.57.rest_2_), channel_id=1, source_target_pairs={{0,4},{1,5},{2,6},{3,7},{4,0},{5,1},{6,2},{7,3},{8,12},{9,13},{10,... | collective-permute-start | bytes 1572872 | tf_op jit(solution)/shard_map/end_right_0/ppermute | solution.py:321
  10.8 0.9 %right_neighbour.1 = (bf16[18,32,256]{2,1,0:T(8,128)(2,1)S(1)}, bf16[14,32,256]{2,1,0:T(8,128)(2,1)S(1)}) custom-call(bf16[4096,128]{1,0:T(8,128)(2,1)S(1)} %get-tuple-element.43.normed.normed0, bf16[4096,128]{1,0:T(8,128)(2,1)S(1)} %get-tuple-element.47.normed1, f32[1,32,128]{2,1,0:T(8,128)S(1)} %get-tuple-element.48.valid0, ...), custom_call_target="tpu_custom_call" | custom-call | tf_op jit(solution)/shard_map/right_neighbour/pallas_call | solution.py:291
  11.7 0.0 copy-start.2
  11.7 1.3 %collective-permute-start.2 = (bf16[18,32,256]{2,1,0:T(8,128)(2,1)S(1)}, bf16[18,32,256]{2,1,0:T(8,128)(2,1)S(1)}, u32[]{:S(2)}, u32[]{:S(2)}) collective-permute-start(bf16[18,32,256]{2,1,0:T(8,128)(2,1)S(1)} %get-tuple-element.55), channel_id=1, source_target_pairs={{0,2},{1,3},{2,0},{3,1},{4,6},{5,7},{6,4},{7,5},{8,10},{9,11},{10,... | collective-permute-start | bytes 884744 | tf_op jit(solution)/shard_map/cross_right_0/ppermute | solution.py:321
  13.0 0.9 %left.1 = (bf16[32,32,256]{2,1,0:T(8,128)(2,1)S(1)}, bf16[18,32,256]{2,1,0:T(8,128)(2,1)S(1)}, bf16[14,32,256]{2,1,0:T(8,128)(2,1)S(1)}) custom-call(bf16[4096,128]{1,0:T(8,128)(2,1)S(1)} %get-tuple-element.43.normed.normed0, bf16[4096,128]{1,0:T(8,128)(2,1)S(1)} %get-tuple-element.47.normed1, f32[1,32,128]{2,1,0:T(8,128)S(1)} %get-tuple-element.48.valid0, ...), custom_call_target="tpu_custom_call" | custom-call | tf_op jit(solution)/shard_map/left/pallas_call | solution.py:291
  13.9 5.3 %collective-permute-done.2.rest_3_ = bf16[18,32,256]{2,1,0:T(8,128)(2,1)S(1)} collective-permute-done((bf16[18,32,256]{2,1,0:T(8,128)(2,1)S(1)}, bf16[18,32,256]{2,1,0:T(8,128)(2,1)S(1)}, u32[]{:S(2)}, u32[]{:S(2)}) %collective-permute-start.2) | collective-permute-done | bytes 294944 | tf_op jit(solution)/shard_map/cross_right_0/ppermute | solution.py:321
  19.2 2.0 %collective-permute-start.6 = (bf16[18,32,256]{2,1,0:T(8,128)(2,1)S(1)}, bf16[18,32,256]{2,1,0:T(8,128)(2,1)S(1)}, u32[]{:S(2)}, u32[]{:S(2)}) collective-permute-start(bf16[18,32,256]{2,1,0:T(8,128)(2,1)S(1)} %collective-permute-done.2.rest_3_), channel_id=1, source_target_pairs={{0,1},{1,0},{2,3},{3,2},{4,8},{5,9},{6,10},{7,11},{8,4},{9,5},{10,... | collective-permute-start | bytes 884744 | tf_op jit(solution)/shard_map/mid_own_10/ppermute | solution.py:321
  21.2 0.6 collective-permute-start.5
  21.9 1.2 %collective-permute-start.3 = (bf16[14,32,256]{2,1,0:T(8,128)(2,1)S(1)}, bf16[14,32,256]{2,1,0:T(8,128)(2,1)S(1)}, u32[]{:S(2)}, u32[]{:S(2)}) collective-permute-start(bf16[14,32,256]{2,1,0:T(8,128)(2,1)S(1)} %get-tuple-element.56), channel_id=1, source_target_pairs={{0,2},{1,3},{2,0},{3,1},{4,6},{5,7},{6,4},{7,5},{8,10},{9,11},{10,... | collective-permute-start | bytes 688136 | tf_op jit(solution)/shard_map/cross_right_1/ppermute | solution.py:321
  23.1 0.0 collective-permute-done.8.elsewhere.rest_4_.refs_4_
  23.1 0.0 collective-permute-done.4.rest_4_
  23.2 0.9 %collective-permute-start.9 = (bf16[32,32,256]{2,1,0:T(8,128)(2,1)S(1)}, bf16[32,32,256]{2,1,0:T(8,128)(2,1)S(1)}, u32[]{:S(2)}, u32[]{:S(2)}) collective-permute-start(bf16[32,32,256]{2,1,0:T(8,128)(2,1)S(1)} %choose.2), channel_id=1, source_target_pairs={{0,4},{1,5},{2,6},{3,7},{4,0},{5,1},{6,2},{7,3},{8,12},{9,13},{10,... | collective-permute-start | bytes 1572872 | tf_op jit(solution)/shard_map/end_left_0/ppermute | solution.py:321
  24.0 3.2 %collective-permute-done.3.rest_3_ = bf16[14,32,256]{2,1,0:T(8,128)(2,1)S(1)} collective-permute-done((bf16[14,32,256]{2,1,0:T(8,128)(2,1)S(1)}, bf16[14,32,256]{2,1,0:T(8,128)(2,1)S(1)}, u32[]{:S(2)}, u32[]{:S(2)}) %collective-permute-start.3) | collective-permute-done | bytes 229408 | tf_op jit(solution)/shard_map/cross_right_1/ppermute | solution.py:321
  27.2 0.0 collective-permute-done.6.rest_5_
  27.2 2.2 %collective-permute-done.5.rest_5_ = bf16[18,32,256]{2,1,0:T(8,128)(2,1)S(1)} collective-permute-done((bf16[18,32,256]{2,1,0:T(8,128)(2,1)S(1)}, bf16[18,32,256]{2,1,0:T(8,128)(2,1)S(1)}, u32[]{:S(2)}, u32[]{:S(2)}) %collective-permute-start.5) | collective-permute-done | bytes 294944 | tf_op jit(solution)/shard_map/end_right_10/ppermute | solution.py:321
  29.4 1.2 %collective-permute-start.7 = (bf16[18,32,256]{2,1,0:T(8,128)(2,1)S(1)}, bf16[18,32,256]{2,1,0:T(8,128)(2,1)S(1)}, u32[]{:S(2)}, u32[]{:S(2)}) collective-permute-start(bf16[18,32,256]{2,1,0:T(8,128)(2,1)S(1)} %get-tuple-element.59), channel_id=1, source_target_pairs={{0,2},{1,3},{2,0},{3,1},{4,6},{5,7},{6,4},{7,5},{8,10},{9,11},{10,... | collective-permute-start | bytes 884744 | tf_op jit(solution)/shard_map/cross_left_0/ppermute | solution.py:321
  30.7 2.2 %collective-permute-start.10 = (bf16[14,32,256]{2,1,0:T(8,128)(2,1)S(1)}, bf16[14,32,256]{2,1,0:T(8,128)(2,1)S(1)}, u32[]{:S(2)}, u32[]{:S(2)}) collective-permute-start(bf16[14,32,256]{2,1,0:T(8,128)(2,1)S(1)} %collective-permute-done.3.rest_3_), channel_id=1, source_target_pairs={{0,1},{1,0},{2,3},{3,2},{4,8},{5,9},{6,10},{7,11},{8,4},{9,5},{10,... | collective-permute-start | bytes 688136 | tf_op jit(solution)/shard_map/mid_own_11/ppermute | solution.py:321
  32.9 0.0 collective-permute-start.12
  32.9 0.4 gate.1
  33.4 0.6 collective-permute-start.13
  33.9 0.1 collective-permute-done.10.elsewhere.refs_5_
  34.1 1.9 %collective-permute-done.7.rest_1_.at_ends = bf16[18,32,256]{2,1,0:T(8,128)(2,1)S(1)} collective-permute-done((bf16[18,32,256]{2,1,0:T(8,128)(2,1)S(1)}, bf16[18,32,256]{2,1,0:T(8,128)(2,1)S(1)}, u32[]{:S(2)}, u32[]{:S(2)}) %collective-permute-start.7) | collective-permute-done | bytes 294944 | tf_op jit(solution)/shard_map/cross_left_0/ppermute | solution.py:321
  36.0 0.1 collective-permute-start.11
  36.1 1.3 %collective-permute-start.14 = (bf16[14,32,256]{2,1,0:T(8,128)(2,1)S(1)}, bf16[14,32,256]{2,1,0:T(8,128)(2,1)S(1)}, u32[]{:S(2)}, u32[]{:S(2)}) collective-permute-start(bf16[14,32,256]{2,1,0:T(8,128)(2,1)S(1)} %get-tuple-element.65), channel_id=1, source_target_pairs={{0,2},{1,3},{2,0},{3,1},{4,6},{5,7},{6,4},{7,5},{8,10},{9,11},{10,... | collective-permute-start | bytes 688136 | tf_op jit(solution)/shard_map/cross_left_1/ppermute | solution.py:321
  37.4 3.3 %collective-permute-done.9.rest_2_.refs_2_.refs_6_ = bf16[32,32,256]{2,1,0:T(8,128)(2,1)S(1)} collective-permute-done((bf16[32,32,256]{2,1,0:T(8,128)(2,1)S(1)}, bf16[32,32,256]{2,1,0:T(8,128)(2,1)S(1)}, u32[]{:S(2)}, u32[]{:S(2)}) %collective-permute-start.9) | collective-permute-done | bytes 524320 | tf_op jit(solution)/shard_map/end_left_0/ppermute | solution.py:321
  40.7 0.0 collective-permute-start.19
  40.7 0.6 collective-permute-done.14.rest_8_.rest_1_.refs_1_
  41.3 3.0 %collective-permute-done.11.rest_3_.refs_7_ = bf16[18,32,256]{2,1,0:T(8,128)(2,1)S(1)} collective-permute-done((bf16[18,32,256]{2,1,0:T(8,128)(2,1)S(1)}, bf16[18,32,256]{2,1,0:T(8,128)(2,1)S(1)}, u32[]{:S(2)}, u32[]{:S(2)}) %collective-permute-start.11) | collective-permute-done | bytes 294944 | tf_op jit(solution)/shard_map/end_left_10/ppermute | solution.py:321
  44.3 0.6 away.1
  44.9 6.6 %collective-permute-start.15 = (bf16[18,32,256]{2,1,0:T(8,128)(2,1)S(1)}, bf16[18,32,256]{2,1,0:T(8,128)(2,1)S(1)}, u32[]{:S(2)}, u32[]{:S(2)}) collective-permute-start(bf16[18,32,256]{2,1,0:T(8,128)(2,1)S(1)} %get-tuple-element.67), channel_id=1, source_target_pairs={{0,4},{1,5},{2,6},{3,7},{4,0},{5,1},{6,2},{7,3},{8,12},{9,13},{10,... | collective-permute-start | bytes 884744 | tf_op jit(solution)/shard_map/left_11_and_products_back_0/ppermute | solution.py:321
  51.5 6.0 %collective-permute-start.20 = (bf16[14,32,256]{2,1,0:T(8,128)(2,1)S(1)}, bf16[14,32,256]{2,1,0:T(8,128)(2,1)S(1)}, u32[]{:S(2)}, u32[]{:S(2)}) collective-permute-start(bf16[14,32,256]{2,1,0:T(8,128)(2,1)S(1)} %collective-permute-done.19.rest_5_), channel_id=1, source_target_pairs={{0,1},{1,0},{2,3},{3,2},{4,8},{5,9},{6,10},{7,11},{8,4},{9,5},{10,... | collective-permute-start | bytes 688136 | tf_op jit(solution)/shard_map/mid_next_11/ppermute | solution.py:321
  57.5 0.6 near.2
  58.1 0.0 collective-permute-done.15.end.refs_3_
  58.2 0.1 hand_out.2
  58.3 4.1 %collective-permute-start.16 = (bf16[18,32,128]{2,1,0:T(8,128)(2,1)S(1)}, bf16[18,32,128]{2,1,0:T(8,128)(2,1)S(1)}, u32[]{:S(2)}, u32[]{:S(2)}) collective-permute-start(bf16[18,32,128]{2,1,0:T(8,128)(2,1)S(1)} %get-tuple-element.69), channel_id=1, source_target_pairs={{0,1},{1,0},{2,3},{3,2},{4,5},{5,4},{6,7},{7,6},{8,9},{9,8},{10,11... | collective-permute-start | bytes 442376 | tf_op jit(solution)/shard_map/return_01/ppermute | solution.py:321
  62.4 0.5 near.3
  62.9 0.0 copy-start.6
  62.9 0.0 collective-permute-done.20.refs_9_
  62.9 1.1 %away_last.1 = (bf16[14,64,128]{2,1,0:T(8,128)(2,1)S(1)}, bf16[14,32,128]{2,1,0:T(8,128)(2,1)S(1)}) custom-call(bf16[32,32,256]{2,1,0:T(8,128)(2,1)S(1)} %get-tuple-element.73.rest_0_.at_ends.refs_0_, bf16[14,32,256]{2,1,0:T(8,128)(2,1)S(1)} %collective-permute-done.14.rest_8_.rest_1_.refs_1_, ...), custom_call_target="tpu_custom_call" | custom-call | tf_op jit(solution)/shard_map/away_last/pallas_call | solution.py:291
  64.1 1.7 %collective-permute-start.21 = (bf16[14,32,128]{2,1,0:T(8,128)(2,1)S(1)}, bf16[14,32,128]{2,1,0:T(8,128)(2,1)S(1)}, u32[]{:S(2)}, u32[]{:S(2)}) collective-permute-start(bf16[14,32,128]{2,1,0:T(8,128)(2,1)S(1)} %get-tuple-element.76), channel_id=1, source_target_pairs={{0,4},{1,5},{2,6},{3,7},{4,0},{5,1},{6,2},{7,3},{8,12},{9,13},{10,... | collective-permute-start | bytes 344072 | tf_op jit(solution)/shard_map/products_back_1/ppermute | solution.py:321
  65.8 0.2 collective-permute-start.17
  66.0 1.7 %collective-permute-start.18 = (bf16[18,32,128]{2,1,0:T(8,128)(2,1)S(1)}, bf16[18,32,128]{2,1,0:T(8,128)(2,1)S(1)}, u32[]{:S(2)}, u32[]{:S(2)}) collective-permute-start(bf16[18,32,128]{2,1,0:T(8,128)(2,1)S(1)} %get-tuple-element.71), channel_id=1, source_target_pairs={{0,3},{1,2},{2,1},{3,0},{4,7},{5,6},{6,5},{7,4},{8,11},{9,10},{10,... | collective-permute-start | bytes 442376 | tf_op jit(solution)/shard_map/return_03/ppermute | solution.py:321
  67.7 1.5 %collective-permute-done.21.end = bf16[14,32,128]{2,1,0:T(8,128)(2,1)S(1)} collective-permute-done((bf16[14,32,128]{2,1,0:T(8,128)(2,1)S(1)}, bf16[14,32,128]{2,1,0:T(8,128)(2,1)S(1)}, u32[]{:S(2)}, u32[]{:S(2)}) %collective-permute-start.21) | collective-permute-done | bytes 114720 | tf_op jit(solution)/shard_map/products_back_1/ppermute | solution.py:321
  69.3 0.2 hand_out.3
  69.4 0.7 collective-permute-start.22
  70.2 0.2 collective-permute-start.23
  70.4 0.0 collective-permute-done.16.rest_1_
  70.4 1.5 %collective-permute-start.24 = (bf16[14,32,128]{2,1,0:T(8,128)(2,1)S(1)}, bf16[14,32,128]{2,1,0:T(8,128)(2,1)S(1)}, u32[]{:S(2)}, u32[]{:S(2)}) collective-permute-start(bf16[14,32,128]{2,1,0:T(8,128)(2,1)S(1)} %get-tuple-element.80), channel_id=1, source_target_pairs={{0,3},{1,2},{2,1},{3,0},{4,7},{5,6},{6,5},{7,4},{8,11},{9,10},{10,... | collective-permute-start | bytes 344072 | tf_op jit(solution)/shard_map/return_13/ppermute | solution.py:321
  71.9 3.4 %collective-permute-done.18.rest_3_ = bf16[18,32,128]{2,1,0:T(8,128)(2,1)S(1)} collective-permute-done((bf16[18,32,128]{2,1,0:T(8,128)(2,1)S(1)}, bf16[18,32,128]{2,1,0:T(8,128)(2,1)S(1)}, u32[]{:S(2)}, u32[]{:S(2)}) %collective-permute-start.18) | collective-permute-done | bytes 147488 | tf_op jit(solution)/shard_map/return_03/ppermute | solution.py:321
  75.2 0.0 collective-permute-done.22.rest_5_
  75.2 1.3 %collective-permute-done.23.rest_6_ = bf16[14,32,128]{2,1,0:T(8,128)(2,1)S(1)} collective-permute-done((bf16[14,32,128]{2,1,0:T(8,128)(2,1)S(1)}, bf16[14,32,128]{2,1,0:T(8,128)(2,1)S(1)}, u32[]{:S(2)}, u32[]{:S(2)}) %collective-permute-start.23) | collective-permute-done | bytes 114720 | tf_op jit(solution)/shard_map/return_12/ppermute | solution.py:321
  76.6 2.9 %collective-permute-done.24.rest_7_ = bf16[14,32,128]{2,1,0:T(8,128)(2,1)S(1)} collective-permute-done((bf16[14,32,128]{2,1,0:T(8,128)(2,1)S(1)}, bf16[14,32,128]{2,1,0:T(8,128)(2,1)S(1)}, u32[]{:S(2)}, u32[]{:S(2)}) %collective-permute-start.24) | collective-permute-done | bytes 114720 | tf_op jit(solution)/shard_map/return_13/ppermute | solution.py:321
  79.4 2.0 %update.1 = bf16[32,128,128]{2,1,0:T(8,128)(2,1)} custom-call(f32[1,128]{1,0:T(1,128)S(1)} %bitcast.3, bf16[128,128]{1,0:T(8,128)(2,1)S(1)} %copy-done.3, f32[32,128,128]{2,1,0:T(8,128)S(1)} %gate.1, bf16[18,32,128]{2,1,0:T(8,128)(2,1)S(1)} %get-tuple-element.68.rest_0_, bf16[18,32,128]{2,1,0:T(8,128)(2,1)S(1)} %collective-permute-done.16.rest_1_, ...), custom_call_target="tpu_custom_call" | custom-call | tf_op jit(solution)/shard_map/update/pallas_call | solution.py:291
  (14 shorter events, 0.1 us)
Async XLA Ops:
  0.0 5.5 %collective-permute-start = (bf16[32,128,128]{2,1,0:T(8,128)(2,1)}, bf16[32,128,128]{2,1,0:T(8,128)(2,1)S(1)}, u32[]{:S(2)}, u32[]{:S(2)}) collective-permute-start(bf16[32,128,128]{2,1,0:T(8,128)(2,1)} %pair.1), channel_id=1, source_target_pairs={{0,1},{1,0},{2,3},{3,2},{4,5},{5,4},{6,7},{7,6},{8,9},{9,8},{10,11... | collective-permute-start | bytes 3145736 | tf_op jit(solution)/shard_map/pair/ppermute | solution.py:321
  0.1 5.5 %collective-permute-start.1 = (s32[32,128]{1,0:T(8,128)}, s32[32,128]{1,0:T(8,128)S(1)}, u32[]{:S(2)}, u32[]{:S(2)}) collective-permute-start(s32[32,128]{1,0:T(8,128)} %mask.1), channel_id=1, source_target_pairs={{0,1},{1,0},{2,3},{3,2},{4,5},{5,4},{6,7},{7,6},{8,9},{9,8},{10,11... | collective-permute-start | bytes 49160 | tf_op jit(solution)/shard_map/mask/ppermute | solution.py:321
  0.5 1.2 %copy-start = (bf16[32,128,128]{2,1,0:T(8,128)(2,1)S(1)}, bf16[32,128,128]{2,1,0:T(8,128)(2,1)}, u32[]{:S(2)}) copy-start(bf16[32,128,128]{2,1,0:T(8,128)(2,1)} %pair.1) | copy-start | bytes 3145732
  1.7 0.9 %copy-start.1 = (bf16[128,512]{1,0:T(8,128)(2,1)S(1)}, bf16[128,512]{1,0:T(8,128)(2,1)}, u32[]{:S(2)}) copy-start(bf16[128,512]{1,0:T(8,128)(2,1)} %weight.3) | copy-start | bytes 393220
  2.6 0.7 copy-start.4
  3.4 0.7 copy-start.5
  7.1 16.0 %collective-permute-start.8 = (bf16[32,32,256]{2,1,0:T(8,128)(2,1)S(1)}, bf16[32,32,256]{2,1,0:T(8,128)(2,1)S(1)}, u32[]{:S(2)}, u32[]{:S(2)}) collective-permute-start(bf16[32,32,256]{2,1,0:T(8,128)(2,1)S(1)} %get-tuple-element.57.rest_2_), channel_id=1, source_target_pairs={{0,1},{1,0},{2,3},{3,2},{4,8},{5,9},{6,10},{7,11},{8,4},{9,5},{10,... | collective-permute-start | bytes 1572872 | tf_op jit(solution)/shard_map/mid_own_0/ppermute | solution.py:321
  7.3 15.9 %collective-permute-start.4 = (bf16[32,32,256]{2,1,0:T(8,128)(2,1)S(1)}, bf16[32,32,256]{2,1,0:T(8,128)(2,1)S(1)}, u32[]{:S(2)}, u32[]{:S(2)}) collective-permute-start(bf16[32,32,256]{2,1,0:T(8,128)(2,1)S(1)} %get-tuple-element.57.rest_2_), channel_id=1, source_target_pairs={{0,4},{1,5},{2,6},{3,7},{4,0},{5,1},{6,2},{7,3},{8,12},{9,13},{10,... | collective-permute-start | bytes 1572872 | tf_op jit(solution)/shard_map/end_right_0/ppermute | solution.py:321
  11.7 21.2 %copy-start.2 = (bf16[128,128]{1,0:T(8,128)(2,1)S(1)}, bf16[128,128]{1,0:T(8,128)(2,1)}, u32[]{:S(2)}) copy-start(bf16[128,128]{1,0:T(8,128)(2,1)} %weight.4) | copy-start | bytes 98308
  11.7 7.5 %collective-permute-start.2 = (bf16[18,32,256]{2,1,0:T(8,128)(2,1)S(1)}, bf16[18,32,256]{2,1,0:T(8,128)(2,1)S(1)}, u32[]{:S(2)}, u32[]{:S(2)}) collective-permute-start(bf16[18,32,256]{2,1,0:T(8,128)(2,1)S(1)} %get-tuple-element.55), channel_id=1, source_target_pairs={{0,2},{1,3},{2,0},{3,1},{4,6},{5,7},{6,4},{7,5},{8,10},{9,11},{10,... | collective-permute-start | bytes 884744 | tf_op jit(solution)/shard_map/cross_right_0/ppermute | solution.py:321
  19.2 8.0 %collective-permute-start.6 = (bf16[18,32,256]{2,1,0:T(8,128)(2,1)S(1)}, bf16[18,32,256]{2,1,0:T(8,128)(2,1)S(1)}, u32[]{:S(2)}, u32[]{:S(2)}) collective-permute-start(bf16[18,32,256]{2,1,0:T(8,128)(2,1)S(1)} %collective-permute-done.2.rest_3_), channel_id=1, source_target_pairs={{0,1},{1,0},{2,3},{3,2},{4,8},{5,9},{6,10},{7,11},{8,4},{9,5},{10,... | collective-permute-start | bytes 884744 | tf_op jit(solution)/shard_map/mid_own_10/ppermute | solution.py:321
  21.2 8.2 %collective-permute-start.5 = (bf16[18,32,256]{2,1,0:T(8,128)(2,1)S(1)}, bf16[18,32,256]{2,1,0:T(8,128)(2,1)S(1)}, u32[]{:S(2)}, u32[]{:S(2)}) collective-permute-start(bf16[18,32,256]{2,1,0:T(8,128)(2,1)S(1)} %collective-permute-done.2.rest_3_), channel_id=1, source_target_pairs={{0,4},{1,5},{2,6},{3,7},{4,0},{5,1},{6,2},{7,3},{8,12},{9,13},{10,... | collective-permute-start | bytes 884744 | tf_op jit(solution)/shard_map/end_right_10/ppermute | solution.py:321
  21.9 5.4 %collective-permute-start.3 = (bf16[14,32,256]{2,1,0:T(8,128)(2,1)S(1)}, bf16[14,32,256]{2,1,0:T(8,128)(2,1)S(1)}, u32[]{:S(2)}, u32[]{:S(2)}) collective-permute-start(bf16[14,32,256]{2,1,0:T(8,128)(2,1)S(1)} %get-tuple-element.56), channel_id=1, source_target_pairs={{0,2},{1,3},{2,0},{3,1},{4,6},{5,7},{6,4},{7,5},{8,10},{9,11},{10,... | collective-permute-start | bytes 688136 | tf_op jit(solution)/shard_map/cross_right_1/ppermute | solution.py:321
  23.2 17.5 %collective-permute-start.9 = (bf16[32,32,256]{2,1,0:T(8,128)(2,1)S(1)}, bf16[32,32,256]{2,1,0:T(8,128)(2,1)S(1)}, u32[]{:S(2)}, u32[]{:S(2)}) collective-permute-start(bf16[32,32,256]{2,1,0:T(8,128)(2,1)S(1)} %choose.2), channel_id=1, source_target_pairs={{0,4},{1,5},{2,6},{3,7},{4,0},{5,1},{6,2},{7,3},{8,12},{9,13},{10,... | collective-permute-start | bytes 1572872 | tf_op jit(solution)/shard_map/end_left_0/ppermute | solution.py:321
  29.4 6.5 %collective-permute-start.7 = (bf16[18,32,256]{2,1,0:T(8,128)(2,1)S(1)}, bf16[18,32,256]{2,1,0:T(8,128)(2,1)S(1)}, u32[]{:S(2)}, u32[]{:S(2)}) collective-permute-start(bf16[18,32,256]{2,1,0:T(8,128)(2,1)S(1)} %get-tuple-element.59), channel_id=1, source_target_pairs={{0,2},{1,3},{2,0},{3,1},{4,6},{5,7},{6,4},{7,5},{8,10},{9,11},{10,... | collective-permute-start | bytes 884744 | tf_op jit(solution)/shard_map/cross_left_0/ppermute | solution.py:321
  30.7 3.4 %collective-permute-start.10 = (bf16[14,32,256]{2,1,0:T(8,128)(2,1)S(1)}, bf16[14,32,256]{2,1,0:T(8,128)(2,1)S(1)}, u32[]{:S(2)}, u32[]{:S(2)}) collective-permute-start(bf16[14,32,256]{2,1,0:T(8,128)(2,1)S(1)} %collective-permute-done.3.rest_3_), channel_id=1, source_target_pairs={{0,1},{1,0},{2,3},{3,2},{4,8},{5,9},{6,10},{7,11},{8,4},{9,5},{10,... | collective-permute-start | bytes 688136 | tf_op jit(solution)/shard_map/mid_own_11/ppermute | solution.py:321
  32.9 7.8 %collective-permute-start.12 = (bf16[32,32,256]{2,1,0:T(8,128)(2,1)S(1)}, bf16[32,32,256]{2,1,0:T(8,128)(2,1)S(1)}, u32[]{:S(2)}, u32[]{:S(2)}) collective-permute-start(bf16[32,32,256]{2,1,0:T(8,128)(2,1)S(1)} %collective-permute-done.4.rest_4_), channel_id=1, source_target_pairs={{0,1},{1,0},{2,3},{3,2},{4,8},{5,9},{6,10},{7,11},{8,4},{9,5},{10,... | collective-permute-start | bytes 1572872 | tf_op jit(solution)/shard_map/mid_next_0/ppermute | solution.py:321
  33.4 7.3 %collective-permute-start.13 = (bf16[18,32,256]{2,1,0:T(8,128)(2,1)S(1)}, bf16[18,32,256]{2,1,0:T(8,128)(2,1)S(1)}, u32[]{:S(2)}, u32[]{:S(2)}) collective-permute-start(bf16[18,32,256]{2,1,0:T(8,128)(2,1)S(1)} %collective-permute-done.5.rest_5_), channel_id=1, source_target_pairs={{0,1},{1,0},{2,3},{3,2},{4,8},{5,9},{6,10},{7,11},{8,4},{9,5},{10,... | collective-permute-start | bytes 884744 | tf_op jit(solution)/shard_map/mid_next_10/ppermute | solution.py:321
  36.0 8.3 %collective-permute-start.11 = (bf16[18,32,256]{2,1,0:T(8,128)(2,1)S(1)}, bf16[18,32,256]{2,1,0:T(8,128)(2,1)S(1)}, u32[]{:S(2)}, u32[]{:S(2)}) collective-permute-start(bf16[18,32,256]{2,1,0:T(8,128)(2,1)S(1)} %choose.3), channel_id=1, source_target_pairs={{0,4},{1,5},{2,6},{3,7},{4,0},{5,1},{6,2},{7,3},{8,12},{9,13},{10,... | collective-permute-start | bytes 884744 | tf_op jit(solution)/shard_map/end_left_10/ppermute | solution.py:321
  36.1 5.2 %collective-permute-start.14 = (bf16[14,32,256]{2,1,0:T(8,128)(2,1)S(1)}, bf16[14,32,256]{2,1,0:T(8,128)(2,1)S(1)}, u32[]{:S(2)}, u32[]{:S(2)}) collective-permute-start(bf16[14,32,256]{2,1,0:T(8,128)(2,1)S(1)} %get-tuple-element.65), channel_id=1, source_target_pairs={{0,2},{1,3},{2,0},{3,1},{4,6},{5,7},{6,4},{7,5},{8,10},{9,11},{10,... | collective-permute-start | bytes 688136 | tf_op jit(solution)/shard_map/cross_left_1/ppermute | solution.py:321
  40.7 10.8 %collective-permute-start.19 = (bf16[14,32,256]{2,1,0:T(8,128)(2,1)S(1)}, bf16[14,32,256]{2,1,0:T(8,128)(2,1)S(1)}, u32[]{:S(2)}, u32[]{:S(2)}) collective-permute-start(bf16[14,32,256]{2,1,0:T(8,128)(2,1)S(1)} %collective-permute-done.3.rest_3_), channel_id=1, source_target_pairs={{0,4},{1,5},{2,6},{3,7},{4,0},{5,1},{6,2},{7,3},{8,12},{9,13},{10,... | collective-permute-start | bytes 688136 | tf_op jit(solution)/shard_map/end_right_11/ppermute | solution.py:321
  44.9 13.2 %collective-permute-start.15 = (bf16[18,32,256]{2,1,0:T(8,128)(2,1)S(1)}, bf16[18,32,256]{2,1,0:T(8,128)(2,1)S(1)}, u32[]{:S(2)}, u32[]{:S(2)}) collective-permute-start(bf16[18,32,256]{2,1,0:T(8,128)(2,1)S(1)} %get-tuple-element.67), channel_id=1, source_target_pairs={{0,4},{1,5},{2,6},{3,7},{4,0},{5,1},{6,2},{7,3},{8,12},{9,13},{10,... | collective-permute-start | bytes 884744 | tf_op jit(solution)/shard_map/left_11_and_products_back_0/ppermute | solution.py:321
  51.5 11.4 %collective-permute-start.20 = (bf16[14,32,256]{2,1,0:T(8,128)(2,1)S(1)}, bf16[14,32,256]{2,1,0:T(8,128)(2,1)S(1)}, u32[]{:S(2)}, u32[]{:S(2)}) collective-permute-start(bf16[14,32,256]{2,1,0:T(8,128)(2,1)S(1)} %collective-permute-done.19.rest_5_), channel_id=1, source_target_pairs={{0,1},{1,0},{2,3},{3,2},{4,8},{5,9},{6,10},{7,11},{8,4},{9,5},{10,... | collective-permute-start | bytes 688136 | tf_op jit(solution)/shard_map/mid_next_11/ppermute | solution.py:321
  58.3 12.1 %collective-permute-start.16 = (bf16[18,32,128]{2,1,0:T(8,128)(2,1)S(1)}, bf16[18,32,128]{2,1,0:T(8,128)(2,1)S(1)}, u32[]{:S(2)}, u32[]{:S(2)}) collective-permute-start(bf16[18,32,128]{2,1,0:T(8,128)(2,1)S(1)} %get-tuple-element.69), channel_id=1, source_target_pairs={{0,1},{1,0},{2,3},{3,2},{4,5},{5,4},{6,7},{7,6},{8,9},{9,8},{10,11... | collective-permute-start | bytes 442376 | tf_op jit(solution)/shard_map/return_01/ppermute | solution.py:321
  62.9 16.5 %copy-start.3 = (bf16[128,128]{1,0:T(8,128)(2,1)S(1)}, bf16[128,128]{1,0:T(8,128)(2,1)}, u32[]{:S(2)}) copy-start(bf16[128,128]{1,0:T(8,128)(2,1)} %weight.5) | copy-start | bytes 98308
  62.9 16.5 %copy-start.6 = (f32[128]{0:T(128)S(1)}, f32[128]{0:T(128)}, u32[]{:S(2)}) copy-start(f32[128]{0:T(128)} %param.12) | copy-start | bytes 1540
  64.1 5.2 %collective-permute-start.21 = (bf16[14,32,128]{2,1,0:T(8,128)(2,1)S(1)}, bf16[14,32,128]{2,1,0:T(8,128)(2,1)S(1)}, u32[]{:S(2)}, u32[]{:S(2)}) collective-permute-start(bf16[14,32,128]{2,1,0:T(8,128)(2,1)S(1)} %get-tuple-element.76), channel_id=1, source_target_pairs={{0,4},{1,5},{2,6},{3,7},{4,0},{5,1},{6,2},{7,3},{8,12},{9,13},{10,... | collective-permute-start | bytes 344072 | tf_op jit(solution)/shard_map/products_back_1/ppermute | solution.py:321
  65.8 6.1 %collective-permute-start.17 = (bf16[18,32,128]{2,1,0:T(8,128)(2,1)S(1)}, bf16[18,32,128]{2,1,0:T(8,128)(2,1)S(1)}, u32[]{:S(2)}, u32[]{:S(2)}) collective-permute-start(bf16[18,32,128]{2,1,0:T(8,128)(2,1)S(1)} %get-tuple-element.70), channel_id=1, source_target_pairs={{0,2},{1,3},{2,0},{3,1},{4,6},{5,7},{6,4},{7,5},{8,10},{9,11},{10,... | collective-permute-start | bytes 442376 | tf_op jit(solution)/shard_map/return_02/ppermute | solution.py:321
  66.0 9.2 %collective-permute-start.18 = (bf16[18,32,128]{2,1,0:T(8,128)(2,1)S(1)}, bf16[18,32,128]{2,1,0:T(8,128)(2,1)S(1)}, u32[]{:S(2)}, u32[]{:S(2)}) collective-permute-start(bf16[18,32,128]{2,1,0:T(8,128)(2,1)S(1)} %get-tuple-element.71), channel_id=1, source_target_pairs={{0,3},{1,2},{2,1},{3,0},{4,7},{5,6},{6,5},{7,4},{8,11},{9,10},{10,... | collective-permute-start | bytes 442376 | tf_op jit(solution)/shard_map/return_03/ppermute | solution.py:321
  69.4 5.8 %collective-permute-start.22 = (bf16[14,32,128]{2,1,0:T(8,128)(2,1)S(1)}, bf16[14,32,128]{2,1,0:T(8,128)(2,1)S(1)}, u32[]{:S(2)}, u32[]{:S(2)}) collective-permute-start(bf16[14,32,128]{2,1,0:T(8,128)(2,1)S(1)} %get-tuple-element.78), channel_id=1, source_target_pairs={{0,1},{1,0},{2,3},{3,2},{4,5},{5,4},{6,7},{7,6},{8,9},{9,8},{10,11... | collective-permute-start | bytes 344072 | tf_op jit(solution)/shard_map/return_11/ppermute | solution.py:321
  70.2 6.4 %collective-permute-start.23 = (bf16[14,32,128]{2,1,0:T(8,128)(2,1)S(1)}, bf16[14,32,128]{2,1,0:T(8,128)(2,1)S(1)}, u32[]{:S(2)}, u32[]{:S(2)}) collective-permute-start(bf16[14,32,128]{2,1,0:T(8,128)(2,1)S(1)} %get-tuple-element.79), channel_id=1, source_target_pairs={{0,2},{1,3},{2,0},{3,1},{4,6},{5,7},{6,4},{7,5},{8,10},{9,11},{10,... | collective-permute-start | bytes 344072 | tf_op jit(solution)/shard_map/return_12/ppermute | solution.py:321
  70.4 9.0 %collective-permute-start.24 = (bf16[14,32,128]{2,1,0:T(8,128)(2,1)S(1)}, bf16[14,32,128]{2,1,0:T(8,128)(2,1)S(1)}, u32[]{:S(2)}, u32[]{:S(2)}) collective-permute-start(bf16[14,32,128]{2,1,0:T(8,128)(2,1)S(1)} %get-tuple-element.80), channel_id=1, source_target_pairs={{0,3},{1,2},{2,1},{3,0},{4,7},{5,6},{6,5},{7,4},{8,11},{9,10},{10,... | collective-permute-start | bytes 344072 | tf_op jit(solution)/shard_map/return_13/ppermute | solution.py:321

commit v19 on v17

--- a/solution.py
+++ b/solution.py
@@ -257,8 +257,8 @@
         swap = {0: 1, 1: 0, planes - 1: planes - 2, planes - 2: planes - 1}
         return (swap[p], b, k) if p in swap else (p, b, 1 - k)
 
-    def outward(p, b, k):
-        return {1: (0, b, k), planes - 2: (planes - 1, b, k)}.get(p)
+    def inward(p, b, k):
+        return {0: (1, b, k), planes - 1: (planes - 2, b, k)}.get(p)
 
     gains = in_gain.reshape(1, -1)
     twin, twin_mask = send(pair, in_plane(1), "pair"), send(pair_mask, in_plane(1), "mask")
@@ -306,7 +306,7 @@
         return [send(x, shifted(s), f"end_right_{name}") for s in range(1, half)]
 
     def end_left(name, x, *earlier):
-        return send(after(x, *earlier), edge, f"end_left_{name}")
+        return send(after(x, *earlier), inward, f"end_left_{name}")
 
     def cross(name, x, *earlier):
         return send(after(x, *earlier), in_plane(2), f"cross_{name}")

time: 77.4 us -> 77.4 us (level)
  waiting for transfers between devices: 32.6 us -> 18.1 us
  starting transfers between devices: 30.9 us -> 45.3 us
    ppermute x25, waiting for transfers between devices: 32.6 us -> 18.1 us  [send(): return lax.ppermute(x, ('row', 'chan'), pairs)]
    ppermute x25, starting transfers between devices: 30.9 us -> 45.3 us  [send(): return lax.ppermute(x, ('row', 'chan'), pairs)]
  transfers between devices with their start and end apart: 25 -> 25, of which waited for: 12 -> 7; matrix products, arithmetic and copies ran while one was open for 0% -> 0% of each run, Pallas kernels for 7% -> 7%
where the time goes in v19:
time: 77.4 us; the launch traced here: 76.9 us
  starting transfers between devices  45.3 us (59%)
  waiting for transfers between devices  18.1 us (23%)
  Pallas kernels  9.74 us (13%)
  local copies, waits for them, and re-layouts  3.52 us (5%)
    ppermute x25, starting transfers between devices, send(): return lax.ppermute(x, ('row', 'chan'), pairs)  45.3 us
    ppermute x25, waiting for transfers between devices, send(): return lax.ppermute(x, ('row', 'chan'), pairs)  18.1 us
    pallas_call x12, Pallas kernels, call(): pl.pallas_call(body, out_shape=out_shape, in_specs=in_specs, out_specs=ou...  9.74 us
    unnamed x14, local copies, waits for them, and re-layouts  3.52 us
  transfers between devices with their start and end apart: 25, of which 7 were waited for; matrix products, arithmetic and copies ran while one was open for 0% of the time, Pallas kernels for 7%

profile of v19, /device:TPU:1, one launch (start us, length us, event | category | flops | bytes accessed | tf_op | source)
XLA Modules:
  0.0 76.9 jit_solution(17340523985113526884)
XLA Ops:
  0.0 0.1 collective-permute-start
  0.1 0.5 collective-permute-start.1
  0.5 1.2 %copy-done = bf16[32,128,128]{2,1,0:T(8,128)(2,1)S(1)} copy-done((bf16[32,128,128]{2,1,0:T(8,128)(2,1)S(1)}, bf16[32,128,128]{2,1,0:T(8,128)(2,1)}, u32[]{:S(2)}) %copy-start) | copy-done | bytes 1048600
  1.7 0.9 %copy-done.1 = bf16[128,512]{1,0:T(8,128)(2,1)S(1)} copy-done((bf16[128,512]{1,0:T(8,128)(2,1)S(1)}, bf16[128,512]{1,0:T(8,128)(2,1)}, u32[]{:S(2)}) %copy-start.1) | copy-done | bytes 131096
  2.6 0.7 copy-done.4
  3.4 0.7 copy-done.5
  4.0 1.5 %right_own.1 = (bf16[32,32,128]{2,1,0:T(8,128)(2,1)S(1)}, bf16[4096,128]{1,0:T(8,128)(2,1)S(1)}, bf16[64,128]{1,0:T(8,128)(2,1)S(1)}, bf16[64,128]{1,0:T(8,128)(...) custom-call(bf16[32,128,128]{2,1,0:T(8,128)(2,1)S(1)} %copy-done, ...), custom_call_target="tpu_custom_call" | custom-call | tf_op jit(solution)/shard_map/right_own/pallas_call | solution.py:212
  5.5 0.0 collective-permute-done.1.mask
  5.5 0.0 collective-permute-done.pair
  5.5 1.6 %right_twin.1 = (bf16[32,32,256]{2,1,0:T(8,128)(2,1)S(1)}, bf16[4096,128]{1,0:T(8,128)(2,1)S(1)}, f32[1,32,128]{2,1,0:T(8,128)S(1)}) custom-call(bf16[32,128,128]{2,1,0:T(8,128)(2,1)S(1)} %collective-permute-done.pair, s32[32,128]{1,0:T(8,128)S(1)} %collective-permute-done.1.mask, f32[1,128]{1,0:T(1,128)S(1)} %get-tuple-element.45.gain, ...), custom_call_target="tpu_custom_call" | custom-call | tf_op jit(solution)/shard_map/right_twin/pallas_call | solution.py:212
  7.1 2.4 %collective-permute-start.3 = (bf16[32,32,256]{2,1,0:T(8,128)(2,1)S(1)}, bf16[32,32,256]{2,1,0:T(8,128)(2,1)S(1)}, u32[]{:S(2)}, u32[]{:S(2)}) collective-permute-start(bf16[32,32,256]{2,1,0:T(8,128)(2,1)S(1)} %get-tuple-element.56.rest_2_), channel_id=1, source_target_pairs={{0,4},{1,5},{2,6},{3,7},{4,0},{5,1},{6,2},{7,3},{8,12},{9,13},{10,... | collective-permute-start | bytes 1572872 | tf_op jit(solution)/shard_map/end_right_0/ppermute | solution.py:242
  9.5 0.8 %collective-permute-start.6 = (bf16[32,32,256]{2,1,0:T(8,128)(2,1)S(1)}, bf16[32,32,256]{2,1,0:T(8,128)(2,1)S(1)}, u32[]{:S(2)}, u32[]{:S(2)}) collective-permute-start(bf16[32,32,256]{2,1,0:T(8,128)(2,1)S(1)} %get-tuple-element.56.rest_2_), channel_id=1, source_target_pairs={{0,1},{1,0},{2,3},{3,2},{4,8},{5,9},{6,10},{7,11},{8,4},{9,5},{10,... | collective-permute-start | bytes 1572872 | tf_op jit(solution)/shard_map/mid_own_0/ppermute | solution.py:242
  10.3 0.9 %right_neighbour.1 = (bf16[18,32,256]{2,1,0:T(8,128)(2,1)S(1)}, bf16[14,32,256]{2,1,0:T(8,128)(2,1)S(1)}) custom-call(bf16[4096,128]{1,0:T(8,128)(2,1)S(1)} %get-tuple-element.44.normed.normed0, bf16[4096,128]{1,0:T(8,128)(2,1)S(1)} %get-tuple-element.48.normed1, f32[1,32,128]{2,1,0:T(8,128)S(1)} %get-tuple-element.49.valid0, ...), custom_call_target="tpu_custom_call" | custom-call | tf_op jit(solution)/shard_map/right_neighbour/pallas_call | solution.py:212
  11.2 1.3 %collective-permute-start.2 = (bf16[18,32,256]{2,1,0:T(8,128)(2,1)S(1)}, bf16[18,32,256]{2,1,0:T(8,128)(2,1)S(1)}, u32[]{:S(2)}, u32[]{:S(2)}) collective-permute-start(bf16[18,32,256]{2,1,0:T(8,128)(2,1)S(1)} %get-tuple-element.55), channel_id=1, source_target_pairs={{0,2},{1,3},{2,0},{3,1},{4,6},{5,7},{6,4},{7,5},{8,10},{9,11},{10,... | collective-permute-start | bytes 884744 | tf_op jit(solution)/shard_map/cross_right_0/ppermute | solution.py:242
  12.5 0.9 %left.1 = (bf16[32,32,256]{2,1,0:T(8,128)(2,1)S(1)}, bf16[18,32,256]{2,1,0:T(8,128)(2,1)S(1)}, bf16[14,32,256]{2,1,0:T(8,128)(2,1)S(1)}) custom-call(bf16[4096,128]{1,0:T(8,128)(2,1)S(1)} %get-tuple-element.44.normed.normed0, bf16[4096,128]{1,0:T(8,128)(2,1)S(1)} %get-tuple-element.48.normed1, f32[1,32,128]{2,1,0:T(8,128)S(1)} %get-tuple-element.49.valid0, ...), custom_call_target="tpu_custom_call" | custom-call | tf_op jit(solution)/shard_map/left/pallas_call | solution.py:212
  13.4 6.5 %collective-permute-done.2.rest_3_ = bf16[18,32,256]{2,1,0:T(8,128)(2,1)S(1)} collective-permute-done((bf16[18,32,256]{2,1,0:T(8,128)(2,1)S(1)}, bf16[18,32,256]{2,1,0:T(8,128)(2,1)S(1)}, u32[]{:S(2)}, u32[]{:S(2)}) %collective-permute-start.2) | collective-permute-done | bytes 294944 | tf_op jit(solution)/shard_map/cross_right_0/ppermute | solution.py:242
  19.9 0.8 %collective-permute-start.9 = (bf16[18,32,256]{2,1,0:T(8,128)(2,1)S(1)}, bf16[18,32,256]{2,1,0:T(8,128)(2,1)S(1)}, u32[]{:S(2)}, u32[]{:S(2)}) collective-permute-start(bf16[18,32,256]{2,1,0:T(8,128)(2,1)S(1)} %collective-permute-done.2.rest_3_), channel_id=1, source_target_pairs={{0,1},{1,0},{2,3},{3,2},{4,8},{5,9},{6,10},{7,11},{8,4},{9,5},{10,... | collective-permute-start | bytes 884744 | tf_op jit(solution)/shard_map/mid_own_10/ppermute | solution.py:242
  20.7 0.1 collective-permute-start.5
  20.8 0.5 collective-permute-done.3.rest_4_
  21.3 1.1 %collective-permute-start.4 = (bf16[18,32,256]{2,1,0:T(8,128)(2,1)S(1)}, bf16[18,32,256]{2,1,0:T(8,128)(2,1)S(1)}, u32[]{:S(2)}, u32[]{:S(2)}) collective-permute-start(bf16[18,32,256]{2,1,0:T(8,128)(2,1)S(1)} %get-tuple-element.57), channel_id=1, source_target_pairs={{0,2},{1,3},{2,0},{3,1},{4,6},{5,7},{6,4},{7,5},{8,10},{9,11},{10,... | collective-permute-start | bytes 884744 | tf_op jit(solution)/shard_map/cross_left_0/ppermute | solution.py:242
  22.4 0.0 collective-permute-done.6.rest_4_
  22.4 2.2 %collective-permute-start.10 = (bf16[32,32,256]{2,1,0:T(8,128)(2,1)S(1)}, bf16[32,32,256]{2,1,0:T(8,128)(2,1)S(1)}, u32[]{:S(2)}, u32[]{:S(2)}) collective-permute-start(bf16[32,32,256]{2,1,0:T(8,128)(2,1)S(1)} %collective-permute-done.3.rest_4_), channel_id=1, source_target_pairs={{0,1},{1,0},{2,3},{3,2},{4,8},{5,9},{6,10},{7,11},{8,4},{9,5},{10,... | collective-permute-start | bytes 1572872 | tf_op jit(solution)/shard_map/mid_next_0/ppermute | solution.py:242
  24.6 2.4 %collective-permute-start.7 = (bf16[32,32,256]{2,1,0:T(8,128)(2,1)S(1)}, bf16[32,32,256]{2,1,0:T(8,128)(2,1)S(1)}, u32[]{:S(2)}, u32[]{:S(2)}) collective-permute-start(bf16[32,32,256]{2,1,0:T(8,128)(2,1)S(1)} %get-tuple-element.74.rest_0_), channel_id=1, source_target_pairs={{0,4},{1,5},{2,6},{3,7},{12,8},{13,9},{14,10},{15,11},{16,20},{17,... | collective-permute-start | bytes 1572872 | tf_op jit(solution)/shard_map/end_left_0/ppermute | solution.py:242
  26.9 0.0 collective-permute-done.9.rest_5_
  27.0 2.0 %collective-permute-done.5.rest_5_ = bf16[18,32,256]{2,1,0:T(8,128)(2,1)S(1)} collective-permute-done((bf16[18,32,256]{2,1,0:T(8,128)(2,1)S(1)}, bf16[18,32,256]{2,1,0:T(8,128)(2,1)S(1)}, u32[]{:S(2)}, u32[]{:S(2)}) %collective-permute-start.5) | collective-permute-done | bytes 294944 | tf_op jit(solution)/shard_map/end_right_10/ppermute | solution.py:242
  28.9 0.0 collective-permute-done.4.rest_1_
  28.9 1.3 %collective-permute-start.12 = (bf16[14,32,256]{2,1,0:T(8,128)(2,1)S(1)}, bf16[14,32,256]{2,1,0:T(8,128)(2,1)S(1)}, u32[]{:S(2)}, u32[]{:S(2)}) collective-permute-start(bf16[14,32,256]{2,1,0:T(8,128)(2,1)S(1)} %get-tuple-element.65), channel_id=1, source_target_pairs={{0,2},{1,3},{2,0},{3,1},{4,6},{5,7},{6,4},{7,5},{8,10},{9,11},{10,... | collective-permute-start | bytes 688136 | tf_op jit(solution)/shard_map/cross_right_1/ppermute | solution.py:242
  30.2 0.4 gate.1
  30.6 2.0 %collective-permute-start.11 = (bf16[18,32,256]{2,1,0:T(8,128)(2,1)S(1)}, bf16[18,32,256]{2,1,0:T(8,128)(2,1)S(1)}, u32[]{:S(2)}, u32[]{:S(2)}) collective-permute-start(bf16[18,32,256]{2,1,0:T(8,128)(2,1)S(1)} %collective-permute-done.5.rest_5_), channel_id=1, source_target_pairs={{0,1},{1,0},{2,3},{3,2},{4,8},{5,9},{6,10},{7,11},{8,4},{9,5},{10,... | collective-permute-start | bytes 884744 | tf_op jit(solution)/shard_map/mid_next_10/ppermute | solution.py:242
  32.6 2.1 %collective-permute-start.8 = (bf16[18,32,256]{2,1,0:T(8,128)(2,1)S(1)}, bf16[18,32,256]{2,1,0:T(8,128)(2,1)S(1)}, u32[]{:S(2)}, u32[]{:S(2)}) collective-permute-start(bf16[18,32,256]{2,1,0:T(8,128)(2,1)S(1)} %collective-permute-done.4.rest_1_), channel_id=1, source_target_pairs={{0,4},{1,5},{2,6},{3,7},{12,8},{13,9},{14,10},{15,11},{16,20},{17,... | collective-permute-start | bytes 884744 | tf_op jit(solution)/shard_map/end_left_10/ppermute | solution.py:242
  34.7 0.0 collective-permute-done.12.rest_3_
  34.7 0.0 collective-permute-done.10.rest_6_
  34.7 0.9 %collective-permute-start.13 = (bf16[14,32,256]{2,1,0:T(8,128)(2,1)S(1)}, bf16[14,32,256]{2,1,0:T(8,128)(2,1)S(1)}, u32[]{:S(2)}, u32[]{:S(2)}) collective-permute-start(bf16[14,32,256]{2,1,0:T(8,128)(2,1)S(1)} %get-tuple-element.66), channel_id=1, source_target_pairs={{0,2},{1,3},{2,0},{3,1},{4,6},{5,7},{6,4},{7,5},{8,10},{9,11},{10,... | collective-permute-start | bytes 688136 | tf_op jit(solution)/shard_map/cross_left_1/ppermute | solution.py:242
  35.6 0.0 collective-permute-done.7.rest_2_
  35.6 6.6 %collective-permute-start.18 = (bf16[14,32,256]{2,1,0:T(8,128)(2,1)S(1)}, bf16[14,32,256]{2,1,0:T(8,128)(2,1)S(1)}, u32[]{:S(2)}, u32[]{:S(2)}) collective-permute-start(bf16[14,32,256]{2,1,0:T(8,128)(2,1)S(1)} %collective-permute-done.12.rest_3_), channel_id=1, source_target_pairs={{0,4},{1,5},{2,6},{3,7},{4,0},{5,1},{6,2},{7,3},{8,12},{9,13},{10,... | collective-permute-start | bytes 688136 | tf_op jit(solution)/shard_map/end_right_11/ppermute | solution.py:242
  42.2 3.3 %collective-permute-start.19 = (bf16[14,32,256]{2,1,0:T(8,128)(2,1)S(1)}, bf16[14,32,256]{2,1,0:T(8,128)(2,1)S(1)}, u32[]{:S(2)}, u32[]{:S(2)}) collective-permute-start(bf16[14,32,256]{2,1,0:T(8,128)(2,1)S(1)} %collective-permute-done.12.rest_3_), channel_id=1, source_target_pairs={{0,1},{1,0},{2,3},{3,2},{4,8},{5,9},{6,10},{7,11},{8,4},{9,5},{10,... | collective-permute-start | bytes 688136 | tf_op jit(solution)/shard_map/mid_own_11/ppermute | solution.py:242
  45.5 0.0 collective-permute-done.11.rest_7_
  45.5 0.0 collective-permute-done.8.rest_3_
  45.5 0.6 away.2
  46.1 1.9 %collective-permute-start.14 = (bf16[18,32,256]{2,1,0:T(8,128)(2,1)S(1)}, bf16[18,32,256]{2,1,0:T(8,128)(2,1)S(1)}, u32[]{:S(2)}, u32[]{:S(2)}) collective-permute-start(bf16[18,32,256]{2,1,0:T(8,128)(2,1)S(1)} %get-tuple-element.68), channel_id=1, source_target_pairs={{0,4},{1,5},{2,6},{3,7},{4,0},{5,1},{6,2},{7,3},{8,12},{9,13},{10,... | collective-permute-start | bytes 884744 | tf_op jit(solution)/shard_map/left_11_and_products_back_0/ppermute | solution.py:242
  47.9 4.2 %collective-permute-start.20 = (bf16[14,32,256]{2,1,0:T(8,128)(2,1)S(1)}, bf16[14,32,256]{2,1,0:T(8,128)(2,1)S(1)}, u32[]{:S(2)}, u32[]{:S(2)}) collective-permute-start(bf16[14,32,256]{2,1,0:T(8,128)(2,1)S(1)} %collective-permute-done.18.rest_5_), channel_id=1, source_target_pairs={{0,1},{1,0},{2,3},{3,2},{4,8},{5,9},{6,10},{7,11},{8,4},{9,5},{10,... | collective-permute-start | bytes 688136 | tf_op jit(solution)/shard_map/mid_next_11/ppermute | solution.py:242
  52.1 0.6 near.2
  52.8 0.5 near.3
  53.3 1.3 %collective-permute-done.14.end.rest_3_ = bf16[18,32,256]{2,1,0:T(8,128)(2,1)S(1)} collective-permute-done((bf16[18,32,256]{2,1,0:T(8,128)(2,1)S(1)}, bf16[18,32,256]{2,1,0:T(8,128)(2,1)S(1)}, u32[]{:S(2)}, u32[]{:S(2)}) %collective-permute-start.14) | collective-permute-done | bytes 294944 | tf_op jit(solution)/shard_map/left_11_and_products_back_0/ppermute | solution.py:242
  54.6 0.1 hand_out.2
  54.7 0.0 copy-start.3
  54.8 0.0 copy-start.6
  54.8 0.0 collective-permute-done.20.rest_7_
  54.8 0.5 away.3
  55.3 2.6 %collective-permute-start.21 = (bf16[14,32,256]{2,1,0:T(8,128)(2,1)S(1)}, bf16[14,32,256]{2,1,0:T(8,128)(2,1)S(1)}, u32[]{:S(2)}, u32[]{:S(2)}) collective-permute-start(bf16[14,32,256]{2,1,0:T(8,128)(2,1)S(1)} %get-tuple-element.78), channel_id=1, source_target_pairs={{0,4},{1,5},{2,6},{3,7},{4,0},{5,1},{6,2},{7,3},{8,12},{9,13},{10,... | collective-permute-start | bytes 688136 | tf_op jit(solution)/shard_map/products_back_1/ppermute | solution.py:242
  57.9 3.3 %collective-permute-start.15 = (bf16[18,32,128]{2,1,0:T(8,128)(2,1)S(1)}, bf16[18,32,128]{2,1,0:T(8,128)(2,1)S(1)}, u32[]{:S(2)}, u32[]{:S(2)}) collective-permute-start(bf16[18,32,128]{2,1,0:T(8,128)(2,1)S(1)} %get-tuple-element.70), channel_id=1, source_target_pairs={{0,1},{1,0},{2,3},{3,2},{4,5},{5,4},{6,7},{7,6},{8,9},{9,8},{10,11... | collective-permute-start | bytes 442376 | tf_op jit(solution)/shard_map/return_01/ppermute | solution.py:242
  61.2 1.2 %collective-permute-start.16 = (bf16[18,32,128]{2,1,0:T(8,128)(2,1)S(1)}, bf16[18,32,128]{2,1,0:T(8,128)(2,1)S(1)}, u32[]{:S(2)}, u32[]{:S(2)}) collective-permute-start(bf16[18,32,128]{2,1,0:T(8,128)(2,1)S(1)} %get-tuple-element.71), channel_id=1, source_target_pairs={{0,2},{1,3},{2,0},{3,1},{4,6},{5,7},{6,4},{7,5},{8,10},{9,11},{10,... | collective-permute-start | bytes 442376 | tf_op jit(solution)/shard_map/return_02/ppermute | solution.py:242
  62.4 0.4 collective-permute-start.17
  62.8 0.0 collective-permute-done.21.end
  62.8 0.1 hand_out.3
  62.9 2.4 %collective-permute-start.22 = (bf16[14,32,128]{2,1,0:T(8,128)(2,1)S(1)}, bf16[14,32,128]{2,1,0:T(8,128)(2,1)S(1)}, u32[]{:S(2)}, u32[]{:S(2)}) collective-permute-start(bf16[14,32,128]{2,1,0:T(8,128)(2,1)S(1)} %get-tuple-element.80), channel_id=1, source_target_pairs={{0,1},{1,0},{2,3},{3,2},{4,5},{5,4},{6,7},{7,6},{8,9},{9,8},{10,11... | collective-permute-start | bytes 344072 | tf_op jit(solution)/shard_map/return_11/ppermute | solution.py:242
  65.4 1.3 %collective-permute-start.23 = (bf16[14,32,128]{2,1,0:T(8,128)(2,1)S(1)}, bf16[14,32,128]{2,1,0:T(8,128)(2,1)S(1)}, u32[]{:S(2)}, u32[]{:S(2)}) collective-permute-start(bf16[14,32,128]{2,1,0:T(8,128)(2,1)S(1)} %get-tuple-element.81), channel_id=1, source_target_pairs={{0,2},{1,3},{2,0},{3,1},{4,6},{5,7},{6,4},{7,5},{8,10},{9,11},{10,... | collective-permute-start | bytes 344072 | tf_op jit(solution)/shard_map/return_12/ppermute | solution.py:242
  66.6 0.0 collective-permute-done.15.rest_1_
  66.6 0.5 collective-permute-start.24
  67.1 3.2 %collective-permute-done.17.rest_3_ = bf16[18,32,128]{2,1,0:T(8,128)(2,1)S(1)} collective-permute-done((bf16[18,32,128]{2,1,0:T(8,128)(2,1)S(1)}, bf16[18,32,128]{2,1,0:T(8,128)(2,1)S(1)}, u32[]{:S(2)}, u32[]{:S(2)}) %collective-permute-start.17) | collective-permute-done | bytes 147488 | tf_op jit(solution)/shard_map/return_03/ppermute | solution.py:242
  70.3 0.0 collective-permute-done.22.rest_5_
  70.3 2.0 %collective-permute-done.23.rest_6_ = bf16[14,32,128]{2,1,0:T(8,128)(2,1)S(1)} collective-permute-done((bf16[14,32,128]{2,1,0:T(8,128)(2,1)S(1)}, bf16[14,32,128]{2,1,0:T(8,128)(2,1)S(1)}, u32[]{:S(2)}, u32[]{:S(2)}) %collective-permute-start.23) | collective-permute-done | bytes 114720 | tf_op jit(solution)/shard_map/return_12/ppermute | solution.py:242
  72.3 2.6 %collective-permute-done.24.rest_7_ = bf16[14,32,128]{2,1,0:T(8,128)(2,1)S(1)} collective-permute-done((bf16[14,32,128]{2,1,0:T(8,128)(2,1)S(1)}, bf16[14,32,128]{2,1,0:T(8,128)(2,1)S(1)}, u32[]{:S(2)}, u32[]{:S(2)}) %collective-permute-start.24) | collective-permute-done | bytes 114720 | tf_op jit(solution)/shard_map/return_13/ppermute | solution.py:242
  74.9 2.0 %update.1 = bf16[32,128,128]{2,1,0:T(8,128)(2,1)} custom-call(f32[1,128]{1,0:T(1,128)S(1)} %bitcast.3, bf16[128,128]{1,0:T(8,128)(2,1)S(1)} %copy-done.3, f32[32,128,128]{2,1,0:T(8,128)S(1)} %gate.1, bf16[18,32,128]{2,1,0:T(8,128)(2,1)S(1)} %get-tuple-element.69.rest_0_, bf16[18,32,128]{2,1,0:T(8,128)(2,1)S(1)} %collective-permute-done.15.rest_1_, ...), custom_call_target="tpu_custom_call" | custom-call | tf_op jit(solution)/shard_map/update/pallas_call | solution.py:212
  (12 shorter events, 0.0 us)
Async XLA Ops:
  0.0 5.5 %collective-permute-start = (bf16[32,128,128]{2,1,0:T(8,128)(2,1)}, bf16[32,128,128]{2,1,0:T(8,128)(2,1)S(1)}, u32[]{:S(2)}, u32[]{:S(2)}) collective-permute-start(bf16[32,128,128]{2,1,0:T(8,128)(2,1)} %pair.1), channel_id=1, source_target_pairs={{0,1},{1,0},{2,3},{3,2},{4,5},{5,4},{6,7},{7,6},{8,9},{9,8},{10,11... | collective-permute-start | bytes 3145736 | tf_op jit(solution)/shard_map/pair/ppermute | solution.py:242
  0.1 5.5 %collective-permute-start.1 = (s32[32,128]{1,0:T(8,128)}, s32[32,128]{1,0:T(8,128)S(1)}, u32[]{:S(2)}, u32[]{:S(2)}) collective-permute-start(s32[32,128]{1,0:T(8,128)} %mask.1), channel_id=1, source_target_pairs={{0,1},{1,0},{2,3},{3,2},{4,5},{5,4},{6,7},{7,6},{8,9},{9,8},{10,11... | collective-permute-start | bytes 49160 | tf_op jit(solution)/shard_map/mask/ppermute | solution.py:242
  0.5 1.2 %copy-start = (bf16[32,128,128]{2,1,0:T(8,128)(2,1)S(1)}, bf16[32,128,128]{2,1,0:T(8,128)(2,1)}, u32[]{:S(2)}) copy-start(bf16[32,128,128]{2,1,0:T(8,128)(2,1)} %pair.1) | copy-start | bytes 3145732
  1.7 0.9 %copy-start.1 = (bf16[128,512]{1,0:T(8,128)(2,1)S(1)}, bf16[128,512]{1,0:T(8,128)(2,1)}, u32[]{:S(2)}) copy-start(bf16[128,512]{1,0:T(8,128)(2,1)} %weight.3) | copy-start | bytes 393220
  2.6 0.7 copy-start.4
  3.4 0.7 copy-start.5
  7.1 14.2 %collective-permute-start.3 = (bf16[32,32,256]{2,1,0:T(8,128)(2,1)S(1)}, bf16[32,32,256]{2,1,0:T(8,128)(2,1)S(1)}, u32[]{:S(2)}, u32[]{:S(2)}) collective-permute-start(bf16[32,32,256]{2,1,0:T(8,128)(2,1)S(1)} %get-tuple-element.56.rest_2_), channel_id=1, source_target_pairs={{0,4},{1,5},{2,6},{3,7},{4,0},{5,1},{6,2},{7,3},{8,12},{9,13},{10,... | collective-permute-start | bytes 1572872 | tf_op jit(solution)/shard_map/end_right_0/ppermute | solution.py:242
  9.5 12.9 %collective-permute-start.6 = (bf16[32,32,256]{2,1,0:T(8,128)(2,1)S(1)}, bf16[32,32,256]{2,1,0:T(8,128)(2,1)S(1)}, u32[]{:S(2)}, u32[]{:S(2)}) collective-permute-start(bf16[32,32,256]{2,1,0:T(8,128)(2,1)S(1)} %get-tuple-element.56.rest_2_), channel_id=1, source_target_pairs={{0,1},{1,0},{2,3},{3,2},{4,8},{5,9},{6,10},{7,11},{8,4},{9,5},{10,... | collective-permute-start | bytes 1572872 | tf_op jit(solution)/shard_map/mid_own_0/ppermute | solution.py:242
  10.3 19.9 %copy-start.2 = (bf16[128,128]{1,0:T(8,128)(2,1)S(1)}, bf16[128,128]{1,0:T(8,128)(2,1)}, u32[]{:S(2)}) copy-start(bf16[128,128]{1,0:T(8,128)(2,1)} %weight.4) | copy-start | bytes 98308
  11.2 8.7 %collective-permute-start.2 = (bf16[18,32,256]{2,1,0:T(8,128)(2,1)S(1)}, bf16[18,32,256]{2,1,0:T(8,128)(2,1)S(1)}, u32[]{:S(2)}, u32[]{:S(2)}) collective-permute-start(bf16[18,32,256]{2,1,0:T(8,128)(2,1)S(1)} %get-tuple-element.55), channel_id=1, source_target_pairs={{0,2},{1,3},{2,0},{3,1},{4,6},{5,7},{6,4},{7,5},{8,10},{9,11},{10,... | collective-permute-start | bytes 884744 | tf_op jit(solution)/shard_map/cross_right_0/ppermute | solution.py:242
  19.9 7.0 %collective-permute-start.9 = (bf16[18,32,256]{2,1,0:T(8,128)(2,1)S(1)}, bf16[18,32,256]{2,1,0:T(8,128)(2,1)S(1)}, u32[]{:S(2)}, u32[]{:S(2)}) collective-permute-start(bf16[18,32,256]{2,1,0:T(8,128)(2,1)S(1)} %collective-permute-done.2.rest_3_), channel_id=1, source_target_pairs={{0,1},{1,0},{2,3},{3,2},{4,8},{5,9},{6,10},{7,11},{8,4},{9,5},{10,... | collective-permute-start | bytes 884744 | tf_op jit(solution)/shard_map/mid_own_10/ppermute | solution.py:242
  20.7 8.2 %collective-permute-start.5 = (bf16[18,32,256]{2,1,0:T(8,128)(2,1)S(1)}, bf16[18,32,256]{2,1,0:T(8,128)(2,1)S(1)}, u32[]{:S(2)}, u32[]{:S(2)}) collective-permute-start(bf16[18,32,256]{2,1,0:T(8,128)(2,1)S(1)} %collective-permute-done.2.rest_3_), channel_id=1, source_target_pairs={{0,4},{1,5},{2,6},{3,7},{4,0},{5,1},{6,2},{7,3},{8,12},{9,13},{10,... | collective-permute-start | bytes 884744 | tf_op jit(solution)/shard_map/end_right_10/ppermute | solution.py:242
  21.3 7.6 %collective-permute-start.4 = (bf16[18,32,256]{2,1,0:T(8,128)(2,1)S(1)}, bf16[18,32,256]{2,1,0:T(8,128)(2,1)S(1)}, u32[]{:S(2)}, u32[]{:S(2)}) collective-permute-start(bf16[18,32,256]{2,1,0:T(8,128)(2,1)S(1)} %get-tuple-element.57), channel_id=1, source_target_pairs={{0,2},{1,3},{2,0},{3,1},{4,6},{5,7},{6,4},{7,5},{8,10},{9,11},{10,... | collective-permute-start | bytes 884744 | tf_op jit(solution)/shard_map/cross_left_0/ppermute | solution.py:242
  22.4 12.3 %collective-permute-start.10 = (bf16[32,32,256]{2,1,0:T(8,128)(2,1)S(1)}, bf16[32,32,256]{2,1,0:T(8,128)(2,1)S(1)}, u32[]{:S(2)}, u32[]{:S(2)}) collective-permute-start(bf16[32,32,256]{2,1,0:T(8,128)(2,1)S(1)} %collective-permute-done.3.rest_4_), channel_id=1, source_target_pairs={{0,1},{1,0},{2,3},{3,2},{4,8},{5,9},{6,10},{7,11},{8,4},{9,5},{10,... | collective-permute-start | bytes 1572872 | tf_op jit(solution)/shard_map/mid_next_0/ppermute | solution.py:242
  24.6 11.1 %collective-permute-start.7 = (bf16[32,32,256]{2,1,0:T(8,128)(2,1)S(1)}, bf16[32,32,256]{2,1,0:T(8,128)(2,1)S(1)}, u32[]{:S(2)}, u32[]{:S(2)}) collective-permute-start(bf16[32,32,256]{2,1,0:T(8,128)(2,1)S(1)} %get-tuple-element.74.rest_0_), channel_id=1, source_target_pairs={{0,4},{1,5},{2,6},{3,7},{12,8},{13,9},{14,10},{15,11},{16,20},{17,... | collective-permute-start | bytes 1572872 | tf_op jit(solution)/shard_map/end_left_0/ppermute | solution.py:242
  28.9 5.8 %collective-permute-start.12 = (bf16[14,32,256]{2,1,0:T(8,128)(2,1)S(1)}, bf16[14,32,256]{2,1,0:T(8,128)(2,1)S(1)}, u32[]{:S(2)}, u32[]{:S(2)}) collective-permute-start(bf16[14,32,256]{2,1,0:T(8,128)(2,1)S(1)} %get-tuple-element.65), channel_id=1, source_target_pairs={{0,2},{1,3},{2,0},{3,1},{4,6},{5,7},{6,4},{7,5},{8,10},{9,11},{10,... | collective-permute-start | bytes 688136 | tf_op jit(solution)/shard_map/cross_right_1/ppermute | solution.py:242
  30.6 14.9 %collective-permute-start.11 = (bf16[18,32,256]{2,1,0:T(8,128)(2,1)S(1)}, bf16[18,32,256]{2,1,0:T(8,128)(2,1)S(1)}, u32[]{:S(2)}, u32[]{:S(2)}) collective-permute-start(bf16[18,32,256]{2,1,0:T(8,128)(2,1)S(1)} %collective-permute-done.5.rest_5_), channel_id=1, source_target_pairs={{0,1},{1,0},{2,3},{3,2},{4,8},{5,9},{6,10},{7,11},{8,4},{9,5},{10,... | collective-permute-start | bytes 884744 | tf_op jit(solution)/shard_map/mid_next_10/ppermute | solution.py:242
  32.6 12.9 %collective-permute-start.8 = (bf16[18,32,256]{2,1,0:T(8,128)(2,1)S(1)}, bf16[18,32,256]{2,1,0:T(8,128)(2,1)S(1)}, u32[]{:S(2)}, u32[]{:S(2)}) collective-permute-start(bf16[18,32,256]{2,1,0:T(8,128)(2,1)S(1)} %collective-permute-done.4.rest_1_), channel_id=1, source_target_pairs={{0,4},{1,5},{2,6},{3,7},{12,8},{13,9},{14,10},{15,11},{16,20},{17,... | collective-permute-start | bytes 884744 | tf_op jit(solution)/shard_map/end_left_10/ppermute | solution.py:242
  34.7 10.7 %collective-permute-start.13 = (bf16[14,32,256]{2,1,0:T(8,128)(2,1)S(1)}, bf16[14,32,256]{2,1,0:T(8,128)(2,1)S(1)}, u32[]{:S(2)}, u32[]{:S(2)}) collective-permute-start(bf16[14,32,256]{2,1,0:T(8,128)(2,1)S(1)} %get-tuple-element.66), channel_id=1, source_target_pairs={{0,2},{1,3},{2,0},{3,1},{4,6},{5,7},{6,4},{7,5},{8,10},{9,11},{10,... | collective-permute-start | bytes 688136 | tf_op jit(solution)/shard_map/cross_left_1/ppermute | solution.py:242
  35.6 12.3 %collective-permute-start.18 = (bf16[14,32,256]{2,1,0:T(8,128)(2,1)S(1)}, bf16[14,32,256]{2,1,0:T(8,128)(2,1)S(1)}, u32[]{:S(2)}, u32[]{:S(2)}) collective-permute-start(bf16[14,32,256]{2,1,0:T(8,128)(2,1)S(1)} %collective-permute-done.12.rest_3_), channel_id=1, source_target_pairs={{0,4},{1,5},{2,6},{3,7},{4,0},{5,1},{6,2},{7,3},{8,12},{9,13},{10,... | collective-permute-start | bytes 688136 | tf_op jit(solution)/shard_map/end_right_11/ppermute | solution.py:242
  42.2 5.7 %collective-permute-start.19 = (bf16[14,32,256]{2,1,0:T(8,128)(2,1)S(1)}, bf16[14,32,256]{2,1,0:T(8,128)(2,1)S(1)}, u32[]{:S(2)}, u32[]{:S(2)}) collective-permute-start(bf16[14,32,256]{2,1,0:T(8,128)(2,1)S(1)} %collective-permute-done.12.rest_3_), channel_id=1, source_target_pairs={{0,1},{1,0},{2,3},{3,2},{4,8},{5,9},{6,10},{7,11},{8,4},{9,5},{10,... | collective-permute-start | bytes 688136 | tf_op jit(solution)/shard_map/mid_own_11/ppermute | solution.py:242
  46.1 8.6 %collective-permute-start.14 = (bf16[18,32,256]{2,1,0:T(8,128)(2,1)S(1)}, bf16[18,32,256]{2,1,0:T(8,128)(2,1)S(1)}, u32[]{:S(2)}, u32[]{:S(2)}) collective-permute-start(bf16[18,32,256]{2,1,0:T(8,128)(2,1)S(1)} %get-tuple-element.68), channel_id=1, source_target_pairs={{0,4},{1,5},{2,6},{3,7},{4,0},{5,1},{6,2},{7,3},{8,12},{9,13},{10,... | collective-permute-start | bytes 884744 | tf_op jit(solution)/shard_map/left_11_and_products_back_0/ppermute | solution.py:242
  47.9 6.8 %collective-permute-start.20 = (bf16[14,32,256]{2,1,0:T(8,128)(2,1)S(1)}, bf16[14,32,256]{2,1,0:T(8,128)(2,1)S(1)}, u32[]{:S(2)}, u32[]{:S(2)}) collective-permute-start(bf16[14,32,256]{2,1,0:T(8,128)(2,1)S(1)} %collective-permute-done.18.rest_5_), channel_id=1, source_target_pairs={{0,1},{1,0},{2,3},{3,2},{4,8},{5,9},{6,10},{7,11},{8,4},{9,5},{10,... | collective-permute-start | bytes 688136 | tf_op jit(solution)/shard_map/mid_next_11/ppermute | solution.py:242
  54.7 20.1 %copy-start.3 = (bf16[128,128]{1,0:T(8,128)(2,1)S(1)}, bf16[128,128]{1,0:T(8,128)(2,1)}, u32[]{:S(2)}) copy-start(bf16[128,128]{1,0:T(8,128)(2,1)} %weight.5) | copy-start | bytes 98308
  54.8 20.1 %copy-start.6 = (f32[128]{0:T(128)S(1)}, f32[128]{0:T(128)}, u32[]{:S(2)}) copy-start(f32[128]{0:T(128)} %param.12) | copy-start | bytes 1540
  55.3 7.6 %collective-permute-start.21 = (bf16[14,32,256]{2,1,0:T(8,128)(2,1)S(1)}, bf16[14,32,256]{2,1,0:T(8,128)(2,1)S(1)}, u32[]{:S(2)}, u32[]{:S(2)}) collective-permute-start(bf16[14,32,256]{2,1,0:T(8,128)(2,1)S(1)} %get-tuple-element.78), channel_id=1, source_target_pairs={{0,4},{1,5},{2,6},{3,7},{4,0},{5,1},{6,2},{7,3},{8,12},{9,13},{10,... | collective-permute-start | bytes 688136 | tf_op jit(solution)/shard_map/products_back_1/ppermute | solution.py:242
  57.9 8.7 %collective-permute-start.15 = (bf16[18,32,128]{2,1,0:T(8,128)(2,1)S(1)}, bf16[18,32,128]{2,1,0:T(8,128)(2,1)S(1)}, u32[]{:S(2)}, u32[]{:S(2)}) collective-permute-start(bf16[18,32,128]{2,1,0:T(8,128)(2,1)S(1)} %get-tuple-element.70), channel_id=1, source_target_pairs={{0,1},{1,0},{2,3},{3,2},{4,5},{5,4},{6,7},{7,6},{8,9},{9,8},{10,11... | collective-permute-start | bytes 442376 | tf_op jit(solution)/shard_map/return_01/ppermute | solution.py:242
  61.2 5.9 %collective-permute-start.16 = (bf16[18,32,128]{2,1,0:T(8,128)(2,1)S(1)}, bf16[18,32,128]{2,1,0:T(8,128)(2,1)S(1)}, u32[]{:S(2)}, u32[]{:S(2)}) collective-permute-start(bf16[18,32,128]{2,1,0:T(8,128)(2,1)S(1)} %get-tuple-element.71), channel_id=1, source_target_pairs={{0,2},{1,3},{2,0},{3,1},{4,6},{5,7},{6,4},{7,5},{8,10},{9,11},{10,... | collective-permute-start | bytes 442376 | tf_op jit(solution)/shard_map/return_02/ppermute | solution.py:242
  62.4 7.9 %collective-permute-start.17 = (bf16[18,32,128]{2,1,0:T(8,128)(2,1)S(1)}, bf16[18,32,128]{2,1,0:T(8,128)(2,1)S(1)}, u32[]{:S(2)}, u32[]{:S(2)}) collective-permute-start(bf16[18,32,128]{2,1,0:T(8,128)(2,1)S(1)} %get-tuple-element.72), channel_id=1, source_target_pairs={{0,3},{1,2},{2,1},{3,0},{4,7},{5,6},{6,5},{7,4},{8,11},{9,10},{10,... | collective-permute-start | bytes 442376 | tf_op jit(solution)/shard_map/return_03/ppermute | solution.py:242
  62.9 7.4 %collective-permute-start.22 = (bf16[14,32,128]{2,1,0:T(8,128)(2,1)S(1)}, bf16[14,32,128]{2,1,0:T(8,128)(2,1)S(1)}, u32[]{:S(2)}, u32[]{:S(2)}) collective-permute-start(bf16[14,32,128]{2,1,0:T(8,128)(2,1)S(1)} %get-tuple-element.80), channel_id=1, source_target_pairs={{0,1},{1,0},{2,3},{3,2},{4,5},{5,4},{6,7},{7,6},{8,9},{9,8},{10,11... | collective-permute-start | bytes 344072 | tf_op jit(solution)/shard_map/return_11/ppermute | solution.py:242
  65.4 6.9 %collective-permute-start.23 = (bf16[14,32,128]{2,1,0:T(8,128)(2,1)S(1)}, bf16[14,32,128]{2,1,0:T(8,128)(2,1)S(1)}, u32[]{:S(2)}, u32[]{:S(2)}) collective-permute-start(bf16[14,32,128]{2,1,0:T(8,128)(2,1)S(1)} %get-tuple-element.81), channel_id=1, source_target_pairs={{0,2},{1,3},{2,0},{3,1},{4,6},{5,7},{6,4},{7,5},{8,10},{9,11},{10,... | collective-permute-start | bytes 344072 | tf_op jit(solution)/shard_map/return_12/ppermute | solution.py:242
  66.6 8.2 %collective-permute-start.24 = (bf16[14,32,128]{2,1,0:T(8,128)(2,1)S(1)}, bf16[14,32,128]{2,1,0:T(8,128)(2,1)S(1)}, u32[]{:S(2)}, u32[]{:S(2)}) collective-permute-start(bf16[14,32,128]{2,1,0:T(8,128)(2,1)S(1)} %get-tuple-element.82), channel_id=1, source_target_pairs={{0,3},{1,2},{2,1},{3,0},{4,7},{5,6},{6,5},{7,4},{8,11},{9,10},{10,... | collective-permute-start | bytes 344072 | tf_op jit(solution)/shard_map/return_13/ppermute | solution.py:242

commit v20 on v17

--- a/solution.py
+++ b/solution.py
@@ -11,7 +11,7 @@
 F32, BF16 = jnp.float32, jnp.bfloat16
 LANES = 128
 SPARE = 6 * 1024 * 1024
-SHARES = (9, 7)
+SHARES = (10, 6)
 NT = (((1,), (1,)), ((), ()))
 TN = (((0,), (0,)), ((), ()))
 VMEM = pl.BlockSpec(memory_space=pltpu.VMEM)

time: 77.4 us -> 78.4 us (1.013)
  waiting for transfers between devices: 32.6 us -> 35.1 us
  starting transfers between devices: 30.9 us -> 29.5 us
    ppermute x25, waiting for transfers between devices: 32.6 us -> 35.1 us  [send(): return lax.ppermute(x, ('row', 'chan'), pairs)]
    ppermute x25, starting transfers between devices: 30.9 us -> 29.5 us  [send(): return lax.ppermute(x, ('row', 'chan'), pairs)]
  transfers between devices with their start and end apart: 25 -> 25, of which waited for: 12 -> 11; matrix products, arithmetic and copies ran while one was open for 0% -> 0% of each run, Pallas kernels for 7% -> 7%
where the time goes in v20:
time: 78.4 us; the launch traced here: 77.9 us
  waiting for transfers between devices  35.1 us (45%)
  starting transfers between devices  29.5 us (38%)
  Pallas kernels  9.7 us (12%)
  local copies, waits for them, and re-layouts  3.52 us (4%)
    ppermute x25, waiting for transfers between devices, send(): return lax.ppermute(x, ('row', 'chan'), pairs)  35.1 us
    ppermute x25, starting transfers between devices, send(): return lax.ppermute(x, ('row', 'chan'), pairs)  29.5 us
    pallas_call x12, Pallas kernels, call(): pl.pallas_call(body, out_shape=out_shape, in_specs=in_specs, out_specs=ou...  9.7 us
    unnamed x14, local copies, waits for them, and re-layouts  3.52 us
  transfers between devices with their start and end apart: 25, of which 11 were waited for; matrix products, arithmetic and copies ran while one was open for 0% of the time, Pallas kernels for 7%

profile of v20, /device:TPU:1, one launch (start us, length us, event | category | flops | bytes accessed | tf_op | source)
XLA Modules:
  0.0 77.9 jit_solution(13711173625317208807)
XLA Ops:
  0.0 0.1 collective-permute-start
  0.1 0.5 collective-permute-start.1
  0.5 1.2 %copy-done = bf16[32,128,128]{2,1,0:T(8,128)(2,1)S(1)} copy-done((bf16[32,128,128]{2,1,0:T(8,128)(2,1)S(1)}, bf16[32,128,128]{2,1,0:T(8,128)(2,1)}, u32[]{:S(2)}) %copy-start) | copy-done | bytes 1048600
  1.7 0.9 %copy-done.1 = bf16[128,512]{1,0:T(8,128)(2,1)S(1)} copy-done((bf16[128,512]{1,0:T(8,128)(2,1)S(1)}, bf16[128,512]{1,0:T(8,128)(2,1)}, u32[]{:S(2)}) %copy-start.1) | copy-done | bytes 131096
  2.6 0.7 copy-done.4
  3.4 0.7 copy-done.5
  4.0 1.5 %right_own.1 = (bf16[32,32,128]{2,1,0:T(8,128)(2,1)S(1)}, bf16[4096,128]{1,0:T(8,128)(2,1)S(1)}, bf16[64,128]{1,0:T(8,128)(2,1)S(1)}, bf16[64,128]{1,0:T(8,128)(...) custom-call(bf16[32,128,128]{2,1,0:T(8,128)(2,1)S(1)} %copy-done, ...), custom_call_target="tpu_custom_call" | custom-call | tf_op jit(solution)/shard_map/right_own/pallas_call | solution.py:212
  5.5 0.0 collective-permute-done.1.mask
  5.5 0.0 collective-permute-done.pair
  5.5 1.6 %right_twin.1 = (bf16[32,32,256]{2,1,0:T(8,128)(2,1)S(1)}, bf16[4096,128]{1,0:T(8,128)(2,1)S(1)}, f32[1,32,128]{2,1,0:T(8,128)S(1)}) custom-call(bf16[32,128,128]{2,1,0:T(8,128)(2,1)S(1)} %collective-permute-done.pair, s32[32,128]{1,0:T(8,128)S(1)} %collective-permute-done.1.mask, f32[1,128]{1,0:T(1,128)S(1)} %get-tuple-element.45.gain, ...), custom_call_target="tpu_custom_call" | custom-call | tf_op jit(solution)/shard_map/right_twin/pallas_call | solution.py:212
  7.1 2.4 %collective-permute-start.3 = (bf16[32,32,256]{2,1,0:T(8,128)(2,1)S(1)}, bf16[32,32,256]{2,1,0:T(8,128)(2,1)S(1)}, u32[]{:S(2)}, u32[]{:S(2)}) collective-permute-start(bf16[32,32,256]{2,1,0:T(8,128)(2,1)S(1)} %get-tuple-element.56.rest_2_), channel_id=1, source_target_pairs={{0,4},{1,5},{2,6},{3,7},{4,0},{5,1},{6,2},{7,3},{8,12},{9,13},{10,... | collective-permute-start | bytes 1572872 | tf_op jit(solution)/shard_map/end_right_0/ppermute | solution.py:242
  9.5 0.8 %collective-permute-start.6 = (bf16[32,32,256]{2,1,0:T(8,128)(2,1)S(1)}, bf16[32,32,256]{2,1,0:T(8,128)(2,1)S(1)}, u32[]{:S(2)}, u32[]{:S(2)}) collective-permute-start(bf16[32,32,256]{2,1,0:T(8,128)(2,1)S(1)} %get-tuple-element.56.rest_2_), channel_id=1, source_target_pairs={{0,1},{1,0},{2,3},{3,2},{4,8},{5,9},{6,10},{7,11},{8,4},{9,5},{10,... | collective-permute-start | bytes 1572872 | tf_op jit(solution)/shard_map/mid_own_0/ppermute | solution.py:242
  10.3 0.9 %right_neighbour.1 = (bf16[20,32,256]{2,1,0:T(8,128)(2,1)S(1)}, bf16[12,32,256]{2,1,0:T(8,128)(2,1)S(1)}) custom-call(bf16[4096,128]{1,0:T(8,128)(2,1)S(1)} %get-tuple-element.44.normed.normed0, bf16[4096,128]{1,0:T(8,128)(2,1)S(1)} %get-tuple-element.48.normed1, f32[1,32,128]{2,1,0:T(8,128)S(1)} %get-tuple-element.49.valid0, ...), custom_call_target="tpu_custom_call" | custom-call | tf_op jit(solution)/shard_map/right_neighbour/pallas_call | solution.py:212
  11.2 1.3 %collective-permute-start.2 = (bf16[20,32,256]{2,1,0:T(8,128)(2,1)S(1)}, bf16[20,32,256]{2,1,0:T(8,128)(2,1)S(1)}, u32[]{:S(2)}, u32[]{:S(2)}) collective-permute-start(bf16[20,32,256]{2,1,0:T(8,128)(2,1)S(1)} %get-tuple-element.55), channel_id=1, source_target_pairs={{0,2},{1,3},{2,0},{3,1},{4,6},{5,7},{6,4},{7,5},{8,10},{9,11},{10,... | collective-permute-start | bytes 983048 | tf_op jit(solution)/shard_map/cross_right_0/ppermute | solution.py:242
  12.5 0.9 %left.1 = (bf16[32,32,256]{2,1,0:T(8,128)(2,1)S(1)}, bf16[20,32,256]{2,1,0:T(8,128)(2,1)S(1)}, bf16[12,32,256]{2,1,0:T(8,128)(2,1)S(1)}) custom-call(bf16[4096,128]{1,0:T(8,128)(2,1)S(1)} %get-tuple-element.44.normed.normed0, bf16[4096,128]{1,0:T(8,128)(2,1)S(1)} %get-tuple-element.48.normed1, f32[1,32,128]{2,1,0:T(8,128)S(1)} %get-tuple-element.49.valid0, ...), custom_call_target="tpu_custom_call" | custom-call | tf_op jit(solution)/shard_map/left/pallas_call | solution.py:212
  13.4 7.2 %collective-permute-done.2.rest_3_ = bf16[20,32,256]{2,1,0:T(8,128)(2,1)S(1)} collective-permute-done((bf16[20,32,256]{2,1,0:T(8,128)(2,1)S(1)}, bf16[20,32,256]{2,1,0:T(8,128)(2,1)S(1)}, u32[]{:S(2)}, u32[]{:S(2)}) %collective-permute-start.2) | collective-permute-done | bytes 327712 | tf_op jit(solution)/shard_map/cross_right_0/ppermute | solution.py:242
  20.6 0.8 %collective-permute-start.9 = (bf16[20,32,256]{2,1,0:T(8,128)(2,1)S(1)}, bf16[20,32,256]{2,1,0:T(8,128)(2,1)S(1)}, u32[]{:S(2)}, u32[]{:S(2)}) collective-permute-start(bf16[20,32,256]{2,1,0:T(8,128)(2,1)S(1)} %collective-permute-done.2.rest_3_), channel_id=1, source_target_pairs={{0,1},{1,0},{2,3},{3,2},{4,8},{5,9},{6,10},{7,11},{8,4},{9,5},{10,... | collective-permute-start | bytes 983048 | tf_op jit(solution)/shard_map/mid_own_10/ppermute | solution.py:242
  21.4 0.1 collective-permute-start.5
  21.5 1.2 %collective-permute-start.4 = (bf16[20,32,256]{2,1,0:T(8,128)(2,1)S(1)}, bf16[20,32,256]{2,1,0:T(8,128)(2,1)S(1)}, u32[]{:S(2)}, u32[]{:S(2)}) collective-permute-start(bf16[20,32,256]{2,1,0:T(8,128)(2,1)S(1)} %get-tuple-element.57), channel_id=1, source_target_pairs={{0,2},{1,3},{2,0},{3,1},{4,6},{5,7},{6,4},{7,5},{8,10},{9,11},{10,... | collective-permute-start | bytes 983048 | tf_op jit(solution)/shard_map/cross_left_0/ppermute | solution.py:242
  22.8 0.0 collective-permute-done.6.rest_4_
  22.8 2.5 %collective-permute-start.10 = (bf16[32,32,256]{2,1,0:T(8,128)(2,1)S(1)}, bf16[32,32,256]{2,1,0:T(8,128)(2,1)S(1)}, u32[]{:S(2)}, u32[]{:S(2)}) collective-permute-start(bf16[32,32,256]{2,1,0:T(8,128)(2,1)S(1)} %collective-permute-done.3.rest_4_), channel_id=1, source_target_pairs={{0,1},{1,0},{2,3},{3,2},{4,8},{5,9},{6,10},{7,11},{8,4},{9,5},{10,... | collective-permute-start | bytes 1572872 | tf_op jit(solution)/shard_map/mid_next_0/ppermute | solution.py:242
  25.3 0.1 collective-permute-start.7
  25.4 0.0 collective-permute-done.9.rest_5_
  25.4 4.9 %collective-permute-done.5.rest_5_ = bf16[20,32,256]{2,1,0:T(8,128)(2,1)S(1)} collective-permute-done((bf16[20,32,256]{2,1,0:T(8,128)(2,1)S(1)}, bf16[20,32,256]{2,1,0:T(8,128)(2,1)S(1)}, u32[]{:S(2)}, u32[]{:S(2)}) %collective-permute-start.5) | collective-permute-done | bytes 327712 | tf_op jit(solution)/shard_map/end_right_10/ppermute | solution.py:242
  30.3 0.0 collective-permute-done.4.rest_1_
  30.3 1.3 %collective-permute-start.12 = (bf16[12,32,256]{2,1,0:T(8,128)(2,1)S(1)}, bf16[12,32,256]{2,1,0:T(8,128)(2,1)S(1)}, u32[]{:S(2)}, u32[]{:S(2)}) collective-permute-start(bf16[12,32,256]{2,1,0:T(8,128)(2,1)S(1)} %get-tuple-element.65), channel_id=1, source_target_pairs={{0,2},{1,3},{2,0},{3,1},{4,6},{5,7},{6,4},{7,5},{8,10},{9,11},{10,... | collective-permute-start | bytes 589832 | tf_op jit(solution)/shard_map/cross_right_1/ppermute | solution.py:242
  31.6 0.4 gate.1
  32.0 2.3 %collective-permute-start.11 = (bf16[20,32,256]{2,1,0:T(8,128)(2,1)S(1)}, bf16[20,32,256]{2,1,0:T(8,128)(2,1)S(1)}, u32[]{:S(2)}, u32[]{:S(2)}) collective-permute-start(bf16[20,32,256]{2,1,0:T(8,128)(2,1)S(1)} %collective-permute-done.5.rest_5_), channel_id=1, source_target_pairs={{0,1},{1,0},{2,3},{3,2},{4,8},{5,9},{6,10},{7,11},{8,4},{9,5},{10,... | collective-permute-start | bytes 983048 | tf_op jit(solution)/shard_map/mid_next_10/ppermute | solution.py:242
  34.3 0.0 collective-permute-start.8
  34.3 0.8 %collective-permute-done.12.rest_3_ = bf16[12,32,256]{2,1,0:T(8,128)(2,1)S(1)} collective-permute-done((bf16[12,32,256]{2,1,0:T(8,128)(2,1)S(1)}, bf16[12,32,256]{2,1,0:T(8,128)(2,1)S(1)}, u32[]{:S(2)}, u32[]{:S(2)}) %collective-permute-start.12) | collective-permute-done | bytes 196640 | tf_op jit(solution)/shard_map/cross_right_1/ppermute | solution.py:242
  35.2 0.0 collective-permute-done.10.rest_6_
  35.2 1.3 %collective-permute-start.13 = (bf16[12,32,256]{2,1,0:T(8,128)(2,1)S(1)}, bf16[12,32,256]{2,1,0:T(8,128)(2,1)S(1)}, u32[]{:S(2)}, u32[]{:S(2)}) collective-permute-start(bf16[12,32,256]{2,1,0:T(8,128)(2,1)S(1)} %get-tuple-element.66), channel_id=1, source_target_pairs={{0,2},{1,3},{2,0},{3,1},{4,6},{5,7},{6,4},{7,5},{8,10},{9,11},{10,... | collective-permute-start | bytes 589832 | tf_op jit(solution)/shard_map/cross_left_1/ppermute | solution.py:242
  36.4 5.2 %collective-permute-done.7.rest_2_ = bf16[32,32,256]{2,1,0:T(8,128)(2,1)S(1)} collective-permute-done((bf16[32,32,256]{2,1,0:T(8,128)(2,1)S(1)}, bf16[32,32,256]{2,1,0:T(8,128)(2,1)S(1)}, u32[]{:S(2)}, u32[]{:S(2)}) %collective-permute-start.7) | collective-permute-done | bytes 524320 | tf_op jit(solution)/shard_map/end_left_0/ppermute | solution.py:242
  41.6 0.6 collective-permute-start.18
  42.2 4.7 %collective-permute-start.19 = (bf16[12,32,256]{2,1,0:T(8,128)(2,1)S(1)}, bf16[12,32,256]{2,1,0:T(8,128)(2,1)S(1)}, u32[]{:S(2)}, u32[]{:S(2)}) collective-permute-start(bf16[12,32,256]{2,1,0:T(8,128)(2,1)S(1)} %collective-permute-done.12.rest_3_), channel_id=1, source_target_pairs={{0,1},{1,0},{2,3},{3,2},{4,8},{5,9},{6,10},{7,11},{8,4},{9,5},{10,... | collective-permute-start | bytes 589832 | tf_op jit(solution)/shard_map/mid_own_11/ppermute | solution.py:242
  46.9 0.0 collective-permute-done.11.rest_7_
  46.9 1.7 %collective-permute-done.8.rest_3_ = bf16[20,32,256]{2,1,0:T(8,128)(2,1)S(1)} collective-permute-done((bf16[20,32,256]{2,1,0:T(8,128)(2,1)S(1)}, bf16[20,32,256]{2,1,0:T(8,128)(2,1)S(1)}, u32[]{:S(2)}, u32[]{:S(2)}) %collective-permute-start.8) | collective-permute-done | bytes 327712 | tf_op jit(solution)/shard_map/end_left_10/ppermute | solution.py:242
  48.6 0.6 away.2
  49.2 0.1 collective-permute-start.14
  49.3 3.5 %collective-permute-done.18.rest_5_ = bf16[12,32,256]{2,1,0:T(8,128)(2,1)S(1)} collective-permute-done((bf16[12,32,256]{2,1,0:T(8,128)(2,1)S(1)}, bf16[12,32,256]{2,1,0:T(8,128)(2,1)S(1)}, u32[]{:S(2)}, u32[]{:S(2)}) %collective-permute-start.18) | collective-permute-done | bytes 196640 | tf_op jit(solution)/shard_map/end_right_11/ppermute | solution.py:242
  52.8 2.0 %collective-permute-start.20 = (bf16[12,32,256]{2,1,0:T(8,128)(2,1)S(1)}, bf16[12,32,256]{2,1,0:T(8,128)(2,1)S(1)}, u32[]{:S(2)}, u32[]{:S(2)}) collective-permute-start(bf16[12,32,256]{2,1,0:T(8,128)(2,1)S(1)} %collective-permute-done.18.rest_5_), channel_id=1, source_target_pairs={{0,1},{1,0},{2,3},{3,2},{4,8},{5,9},{6,10},{7,11},{8,4},{9,5},{10,... | collective-permute-start | bytes 589832 | tf_op jit(solution)/shard_map/mid_next_11/ppermute | solution.py:242
  54.8 0.7 near.2
  55.5 0.5 near.3
  55.9 0.0 copy-start.3
  55.9 0.0 copy-start.6
  56.0 3.8 %collective-permute-done.14.end.rest_3_ = bf16[20,32,256]{2,1,0:T(8,128)(2,1)S(1)} collective-permute-done((bf16[20,32,256]{2,1,0:T(8,128)(2,1)S(1)}, bf16[20,32,256]{2,1,0:T(8,128)(2,1)S(1)}, u32[]{:S(2)}, u32[]{:S(2)}) %collective-permute-start.14) | collective-permute-done | bytes 327712 | tf_op jit(solution)/shard_map/left_11_and_products_back_0/ppermute | solution.py:242
  59.7 0.1 hand_out.2
  59.8 0.0 collective-permute-done.20.rest_7_
  59.8 0.4 away.3
  60.3 0.1 collective-permute-start.21
  60.4 1.9 %collective-permute-start.15 = (bf16[20,32,128]{2,1,0:T(8,128)(2,1)S(1)}, bf16[20,32,128]{2,1,0:T(8,128)(2,1)S(1)}, u32[]{:S(2)}, u32[]{:S(2)}) collective-permute-start(bf16[20,32,128]{2,1,0:T(8,128)(2,1)S(1)} %get-tuple-element.70), channel_id=1, source_target_pairs={{0,1},{1,0},{2,3},{3,2},{4,5},{5,4},{6,7},{7,6},{8,9},{9,8},{10,11... | collective-permute-start | bytes 491528 | tf_op jit(solution)/shard_map/return_01/ppermute | solution.py:242
  62.3 1.2 %collective-permute-start.16 = (bf16[20,32,128]{2,1,0:T(8,128)(2,1)S(1)}, bf16[20,32,128]{2,1,0:T(8,128)(2,1)S(1)}, u32[]{:S(2)}, u32[]{:S(2)}) collective-permute-start(bf16[20,32,128]{2,1,0:T(8,128)(2,1)S(1)} %get-tuple-element.71), channel_id=1, source_target_pairs={{0,2},{1,3},{2,0},{3,1},{4,6},{5,7},{6,4},{7,5},{8,10},{9,11},{10,... | collective-permute-start | bytes 491528 | tf_op jit(solution)/shard_map/return_02/ppermute | solution.py:242
  63.5 0.4 collective-permute-start.17
  63.9 1.6 %collective-permute-done.21.end = bf16[12,32,256]{2,1,0:T(8,128)(2,1)S(1)} collective-permute-done((bf16[12,32,256]{2,1,0:T(8,128)(2,1)S(1)}, bf16[12,32,256]{2,1,0:T(8,128)(2,1)S(1)}, u32[]{:S(2)}, u32[]{:S(2)}) %collective-permute-start.21) | collective-permute-done | bytes 196640 | tf_op jit(solution)/shard_map/products_back_1/ppermute | solution.py:242
  65.4 0.1 hand_out.3
  65.5 2.3 %collective-permute-start.22 = (bf16[12,32,128]{2,1,0:T(8,128)(2,1)S(1)}, bf16[12,32,128]{2,1,0:T(8,128)(2,1)S(1)}, u32[]{:S(2)}, u32[]{:S(2)}) collective-permute-start(bf16[12,32,128]{2,1,0:T(8,128)(2,1)S(1)} %get-tuple-element.80), channel_id=1, source_target_pairs={{0,1},{1,0},{2,3},{3,2},{4,5},{5,4},{6,7},{7,6},{8,9},{9,8},{10,11... | collective-permute-start | bytes 294920 | tf_op jit(solution)/shard_map/return_11/ppermute | solution.py:242
  67.8 1.3 %collective-permute-start.23 = (bf16[12,32,128]{2,1,0:T(8,128)(2,1)S(1)}, bf16[12,32,128]{2,1,0:T(8,128)(2,1)S(1)}, u32[]{:S(2)}, u32[]{:S(2)}) collective-permute-start(bf16[12,32,128]{2,1,0:T(8,128)(2,1)S(1)} %get-tuple-element.81), channel_id=1, source_target_pairs={{0,2},{1,3},{2,0},{3,1},{4,6},{5,7},{6,4},{7,5},{8,10},{9,11},{10,... | collective-permute-start | bytes 294920 | tf_op jit(solution)/shard_map/return_12/ppermute | solution.py:242
  69.1 0.4 collective-permute-start.24
  69.5 0.0 collective-permute-done.16.rest_2_
  69.5 2.6 %collective-permute-done.17.rest_3_ = bf16[20,32,128]{2,1,0:T(8,128)(2,1)S(1)} collective-permute-done((bf16[20,32,128]{2,1,0:T(8,128)(2,1)S(1)}, bf16[20,32,128]{2,1,0:T(8,128)(2,1)S(1)}, u32[]{:S(2)}, u32[]{:S(2)}) %collective-permute-start.17) | collective-permute-done | bytes 163872 | tf_op jit(solution)/shard_map/return_03/ppermute | solution.py:242
  72.1 0.0 collective-permute-done.22.rest_5_
  72.1 1.6 %collective-permute-done.23.rest_6_ = bf16[12,32,128]{2,1,0:T(8,128)(2,1)S(1)} collective-permute-done((bf16[12,32,128]{2,1,0:T(8,128)(2,1)S(1)}, bf16[12,32,128]{2,1,0:T(8,128)(2,1)S(1)}, u32[]{:S(2)}, u32[]{:S(2)}) %collective-permute-start.23) | collective-permute-done | bytes 98336 | tf_op jit(solution)/shard_map/return_12/ppermute | solution.py:242
  73.7 2.2 %collective-permute-done.24.rest_7_ = bf16[12,32,128]{2,1,0:T(8,128)(2,1)S(1)} collective-permute-done((bf16[12,32,128]{2,1,0:T(8,128)(2,1)S(1)}, bf16[12,32,128]{2,1,0:T(8,128)(2,1)S(1)}, u32[]{:S(2)}, u32[]{:S(2)}) %collective-permute-start.24) | collective-permute-done | bytes 98336 | tf_op jit(solution)/shard_map/return_13/ppermute | solution.py:242
  75.9 2.0 %update.1 = bf16[32,128,128]{2,1,0:T(8,128)(2,1)} custom-call(f32[1,128]{1,0:T(1,128)S(1)} %bitcast.3, bf16[128,128]{1,0:T(8,128)(2,1)S(1)} %copy-done.3, f32[32,128,128]{2,1,0:T(8,128)S(1)} %gate.1, bf16[20,32,128]{2,1,0:T(8,128)(2,1)S(1)} %get-tuple-element.69.rest_0_, bf16[20,32,128]{2,1,0:T(8,128)(2,1)S(1)} %collective-permute-done.15.rest_1_, ...), custom_call_target="tpu_custom_call" | custom-call | tf_op jit(solution)/shard_map/update/pallas_call | solution.py:212
  (12 shorter events, 0.0 us)
Async XLA Ops:
  0.0 5.5 %collective-permute-start = (bf16[32,128,128]{2,1,0:T(8,128)(2,1)}, bf16[32,128,128]{2,1,0:T(8,128)(2,1)S(1)}, u32[]{:S(2)}, u32[]{:S(2)}) collective-permute-start(bf16[32,128,128]{2,1,0:T(8,128)(2,1)} %pair.1), channel_id=1, source_target_pairs={{0,1},{1,0},{2,3},{3,2},{4,5},{5,4},{6,7},{7,6},{8,9},{9,8},{10,11... | collective-permute-start | bytes 3145736 | tf_op jit(solution)/shard_map/pair/ppermute | solution.py:242
  0.1 5.5 %collective-permute-start.1 = (s32[32,128]{1,0:T(8,128)}, s32[32,128]{1,0:T(8,128)S(1)}, u32[]{:S(2)}, u32[]{:S(2)}) collective-permute-start(s32[32,128]{1,0:T(8,128)} %mask.1), channel_id=1, source_target_pairs={{0,1},{1,0},{2,3},{3,2},{4,5},{5,4},{6,7},{7,6},{8,9},{9,8},{10,11... | collective-permute-start | bytes 49160 | tf_op jit(solution)/shard_map/mask/ppermute | solution.py:242
  0.5 1.2 %copy-start = (bf16[32,128,128]{2,1,0:T(8,128)(2,1)S(1)}, bf16[32,128,128]{2,1,0:T(8,128)(2,1)}, u32[]{:S(2)}) copy-start(bf16[32,128,128]{2,1,0:T(8,128)(2,1)} %pair.1) | copy-start | bytes 3145732
  1.7 0.9 %copy-start.1 = (bf16[128,512]{1,0:T(8,128)(2,1)S(1)}, bf16[128,512]{1,0:T(8,128)(2,1)}, u32[]{:S(2)}) copy-start(bf16[128,512]{1,0:T(8,128)(2,1)} %weight.3) | copy-start | bytes 393220
  2.6 0.7 copy-start.4
  3.4 0.7 copy-start.5
  7.1 14.4 %collective-permute-start.3 = (bf16[32,32,256]{2,1,0:T(8,128)(2,1)S(1)}, bf16[32,32,256]{2,1,0:T(8,128)(2,1)S(1)}, u32[]{:S(2)}, u32[]{:S(2)}) collective-permute-start(bf16[32,32,256]{2,1,0:T(8,128)(2,1)S(1)} %get-tuple-element.56.rest_2_), channel_id=1, source_target_pairs={{0,4},{1,5},{2,6},{3,7},{4,0},{5,1},{6,2},{7,3},{8,12},{9,13},{10,... | collective-permute-start | bytes 1572872 | tf_op jit(solution)/shard_map/end_right_0/ppermute | solution.py:242
  9.5 13.3 %collective-permute-start.6 = (bf16[32,32,256]{2,1,0:T(8,128)(2,1)S(1)}, bf16[32,32,256]{2,1,0:T(8,128)(2,1)S(1)}, u32[]{:S(2)}, u32[]{:S(2)}) collective-permute-start(bf16[32,32,256]{2,1,0:T(8,128)(2,1)S(1)} %get-tuple-element.56.rest_2_), channel_id=1, source_target_pairs={{0,1},{1,0},{2,3},{3,2},{4,8},{5,9},{6,10},{7,11},{8,4},{9,5},{10,... | collective-permute-start | bytes 1572872 | tf_op jit(solution)/shard_map/mid_own_0/ppermute | solution.py:242
  10.3 21.3 %copy-start.2 = (bf16[128,128]{1,0:T(8,128)(2,1)S(1)}, bf16[128,128]{1,0:T(8,128)(2,1)}, u32[]{:S(2)}) copy-start(bf16[128,128]{1,0:T(8,128)(2,1)} %weight.4) | copy-start | bytes 98308
  11.2 9.4 %collective-permute-start.2 = (bf16[20,32,256]{2,1,0:T(8,128)(2,1)S(1)}, bf16[20,32,256]{2,1,0:T(8,128)(2,1)S(1)}, u32[]{:S(2)}, u32[]{:S(2)}) collective-permute-start(bf16[20,32,256]{2,1,0:T(8,128)(2,1)S(1)} %get-tuple-element.55), channel_id=1, source_target_pairs={{0,2},{1,3},{2,0},{3,1},{4,6},{5,7},{6,4},{7,5},{8,10},{9,11},{10,... | collective-permute-start | bytes 983048 | tf_op jit(solution)/shard_map/cross_right_0/ppermute | solution.py:242
  20.6 4.8 %collective-permute-start.9 = (bf16[20,32,256]{2,1,0:T(8,128)(2,1)S(1)}, bf16[20,32,256]{2,1,0:T(8,128)(2,1)S(1)}, u32[]{:S(2)}, u32[]{:S(2)}) collective-permute-start(bf16[20,32,256]{2,1,0:T(8,128)(2,1)S(1)} %collective-permute-done.2.rest_3_), channel_id=1, source_target_pairs={{0,1},{1,0},{2,3},{3,2},{4,8},{5,9},{6,10},{7,11},{8,4},{9,5},{10,... | collective-permute-start | bytes 983048 | tf_op jit(solution)/shard_map/mid_own_10/ppermute | solution.py:242
  21.4 8.9 %collective-permute-start.5 = (bf16[20,32,256]{2,1,0:T(8,128)(2,1)S(1)}, bf16[20,32,256]{2,1,0:T(8,128)(2,1)S(1)}, u32[]{:S(2)}, u32[]{:S(2)}) collective-permute-start(bf16[20,32,256]{2,1,0:T(8,128)(2,1)S(1)} %collective-permute-done.2.rest_3_), channel_id=1, source_target_pairs={{0,4},{1,5},{2,6},{3,7},{4,0},{5,1},{6,2},{7,3},{8,12},{9,13},{10,... | collective-permute-start | bytes 983048 | tf_op jit(solution)/shard_map/end_right_10/ppermute | solution.py:242
  21.5 8.8 %collective-permute-start.4 = (bf16[20,32,256]{2,1,0:T(8,128)(2,1)S(1)}, bf16[20,32,256]{2,1,0:T(8,128)(2,1)S(1)}, u32[]{:S(2)}, u32[]{:S(2)}) collective-permute-start(bf16[20,32,256]{2,1,0:T(8,128)(2,1)S(1)} %get-tuple-element.57), channel_id=1, source_target_pairs={{0,2},{1,3},{2,0},{3,1},{4,6},{5,7},{6,4},{7,5},{8,10},{9,11},{10,... | collective-permute-start | bytes 983048 | tf_op jit(solution)/shard_map/cross_left_0/ppermute | solution.py:242
  22.8 12.4 %collective-permute-start.10 = (bf16[32,32,256]{2,1,0:T(8,128)(2,1)S(1)}, bf16[32,32,256]{2,1,0:T(8,128)(2,1)S(1)}, u32[]{:S(2)}, u32[]{:S(2)}) collective-permute-start(bf16[32,32,256]{2,1,0:T(8,128)(2,1)S(1)} %collective-permute-done.3.rest_4_), channel_id=1, source_target_pairs={{0,1},{1,0},{2,3},{3,2},{4,8},{5,9},{6,10},{7,11},{8,4},{9,5},{10,... | collective-permute-start | bytes 1572872 | tf_op jit(solution)/shard_map/mid_next_0/ppermute | solution.py:242
  25.3 16.3 %collective-permute-start.7 = (bf16[32,32,256]{2,1,0:T(8,128)(2,1)S(1)}, bf16[32,32,256]{2,1,0:T(8,128)(2,1)S(1)}, u32[]{:S(2)}, u32[]{:S(2)}) collective-permute-start(bf16[32,32,256]{2,1,0:T(8,128)(2,1)S(1)} %get-tuple-element.74.rest_0_), channel_id=1, source_target_pairs={{0,4},{1,5},{2,6},{3,7},{4,0},{5,1},{6,2},{7,3},{8,12},{9,13},{10,... | collective-permute-start | bytes 1572872 | tf_op jit(solution)/shard_map/end_left_0/ppermute | solution.py:242
  30.3 4.8 %collective-permute-start.12 = (bf16[12,32,256]{2,1,0:T(8,128)(2,1)S(1)}, bf16[12,32,256]{2,1,0:T(8,128)(2,1)S(1)}, u32[]{:S(2)}, u32[]{:S(2)}) collective-permute-start(bf16[12,32,256]{2,1,0:T(8,128)(2,1)S(1)} %get-tuple-element.65), channel_id=1, source_target_pairs={{0,2},{1,3},{2,0},{3,1},{4,6},{5,7},{6,4},{7,5},{8,10},{9,11},{10,... | collective-permute-start | bytes 589832 | tf_op jit(solution)/shard_map/cross_right_1/ppermute | solution.py:242
  32.0 14.9 %collective-permute-start.11 = (bf16[20,32,256]{2,1,0:T(8,128)(2,1)S(1)}, bf16[20,32,256]{2,1,0:T(8,128)(2,1)S(1)}, u32[]{:S(2)}, u32[]{:S(2)}) collective-permute-start(bf16[20,32,256]{2,1,0:T(8,128)(2,1)S(1)} %collective-permute-done.5.rest_5_), channel_id=1, source_target_pairs={{0,1},{1,0},{2,3},{3,2},{4,8},{5,9},{6,10},{7,11},{8,4},{9,5},{10,... | collective-permute-start | bytes 983048 | tf_op jit(solution)/shard_map/mid_next_10/ppermute | solution.py:242
  34.3 14.3 %collective-permute-start.8 = (bf16[20,32,256]{2,1,0:T(8,128)(2,1)S(1)}, bf16[20,32,256]{2,1,0:T(8,128)(2,1)S(1)}, u32[]{:S(2)}, u32[]{:S(2)}) collective-permute-start(bf16[20,32,256]{2,1,0:T(8,128)(2,1)S(1)} %collective-permute-done.4.rest_1_), channel_id=1, source_target_pairs={{0,4},{1,5},{2,6},{3,7},{4,0},{5,1},{6,2},{7,3},{8,12},{9,13},{10,... | collective-permute-start | bytes 983048 | tf_op jit(solution)/shard_map/end_left_10/ppermute | solution.py:242
  35.2 13.4 %collective-permute-start.13 = (bf16[12,32,256]{2,1,0:T(8,128)(2,1)S(1)}, bf16[12,32,256]{2,1,0:T(8,128)(2,1)S(1)}, u32[]{:S(2)}, u32[]{:S(2)}) collective-permute-start(bf16[12,32,256]{2,1,0:T(8,128)(2,1)S(1)} %get-tuple-element.66), channel_id=1, source_target_pairs={{0,2},{1,3},{2,0},{3,1},{4,6},{5,7},{6,4},{7,5},{8,10},{9,11},{10,... | collective-permute-start | bytes 589832 | tf_op jit(solution)/shard_map/cross_left_1/ppermute | solution.py:242
  41.6 11.2 %collective-permute-start.18 = (bf16[12,32,256]{2,1,0:T(8,128)(2,1)S(1)}, bf16[12,32,256]{2,1,0:T(8,128)(2,1)S(1)}, u32[]{:S(2)}, u32[]{:S(2)}) collective-permute-start(bf16[12,32,256]{2,1,0:T(8,128)(2,1)S(1)} %collective-permute-done.12.rest_3_), channel_id=1, source_target_pairs={{0,4},{1,5},{2,6},{3,7},{4,0},{5,1},{6,2},{7,3},{8,12},{9,13},{10,... | collective-permute-start | bytes 589832 | tf_op jit(solution)/shard_map/end_right_11/ppermute | solution.py:242
  42.2 10.6 %collective-permute-start.19 = (bf16[12,32,256]{2,1,0:T(8,128)(2,1)S(1)}, bf16[12,32,256]{2,1,0:T(8,128)(2,1)S(1)}, u32[]{:S(2)}, u32[]{:S(2)}) collective-permute-start(bf16[12,32,256]{2,1,0:T(8,128)(2,1)S(1)} %collective-permute-done.12.rest_3_), channel_id=1, source_target_pairs={{0,1},{1,0},{2,3},{3,2},{4,8},{5,9},{6,10},{7,11},{8,4},{9,5},{10,... | collective-permute-start | bytes 589832 | tf_op jit(solution)/shard_map/mid_own_11/ppermute | solution.py:242
  49.2 10.5 %collective-permute-start.14 = (bf16[20,32,256]{2,1,0:T(8,128)(2,1)S(1)}, bf16[20,32,256]{2,1,0:T(8,128)(2,1)S(1)}, u32[]{:S(2)}, u32[]{:S(2)}) collective-permute-start(bf16[20,32,256]{2,1,0:T(8,128)(2,1)S(1)} %get-tuple-element.68), channel_id=1, source_target_pairs={{0,4},{1,5},{2,6},{3,7},{4,0},{5,1},{6,2},{7,3},{8,12},{9,13},{10,... | collective-permute-start | bytes 983048 | tf_op jit(solution)/shard_map/left_11_and_products_back_0/ppermute | solution.py:242
  52.8 7.0 %collective-permute-start.20 = (bf16[12,32,256]{2,1,0:T(8,128)(2,1)S(1)}, bf16[12,32,256]{2,1,0:T(8,128)(2,1)S(1)}, u32[]{:S(2)}, u32[]{:S(2)}) collective-permute-start(bf16[12,32,256]{2,1,0:T(8,128)(2,1)S(1)} %collective-permute-done.18.rest_5_), channel_id=1, source_target_pairs={{0,1},{1,0},{2,3},{3,2},{4,8},{5,9},{6,10},{7,11},{8,4},{9,5},{10,... | collective-permute-start | bytes 589832 | tf_op jit(solution)/shard_map/mid_next_11/ppermute | solution.py:242
  55.9 20.0 %copy-start.3 = (bf16[128,128]{1,0:T(8,128)(2,1)S(1)}, bf16[128,128]{1,0:T(8,128)(2,1)}, u32[]{:S(2)}) copy-start(bf16[128,128]{1,0:T(8,128)(2,1)} %weight.5) | copy-start | bytes 98308
  55.9 20.0 %copy-start.6 = (f32[128]{0:T(128)S(1)}, f32[128]{0:T(128)}, u32[]{:S(2)}) copy-start(f32[128]{0:T(128)} %param.12) | copy-start | bytes 1540
  60.3 5.2 %collective-permute-start.21 = (bf16[12,32,256]{2,1,0:T(8,128)(2,1)S(1)}, bf16[12,32,256]{2,1,0:T(8,128)(2,1)S(1)}, u32[]{:S(2)}, u32[]{:S(2)}) collective-permute-start(bf16[12,32,256]{2,1,0:T(8,128)(2,1)S(1)} %get-tuple-element.78), channel_id=1, source_target_pairs={{0,4},{1,5},{2,6},{3,7},{4,0},{5,1},{6,2},{7,3},{8,12},{9,13},{10,... | collective-permute-start | bytes 589832 | tf_op jit(solution)/shard_map/products_back_1/ppermute | solution.py:242
  60.4 8.7 %collective-permute-start.15 = (bf16[20,32,128]{2,1,0:T(8,128)(2,1)S(1)}, bf16[20,32,128]{2,1,0:T(8,128)(2,1)S(1)}, u32[]{:S(2)}, u32[]{:S(2)}) collective-permute-start(bf16[20,32,128]{2,1,0:T(8,128)(2,1)S(1)} %get-tuple-element.70), channel_id=1, source_target_pairs={{0,1},{1,0},{2,3},{3,2},{4,5},{5,4},{6,7},{7,6},{8,9},{9,8},{10,11... | collective-permute-start | bytes 491528 | tf_op jit(solution)/shard_map/return_01/ppermute | solution.py:242
  62.3 7.3 %collective-permute-start.16 = (bf16[20,32,128]{2,1,0:T(8,128)(2,1)S(1)}, bf16[20,32,128]{2,1,0:T(8,128)(2,1)S(1)}, u32[]{:S(2)}, u32[]{:S(2)}) collective-permute-start(bf16[20,32,128]{2,1,0:T(8,128)(2,1)S(1)} %get-tuple-element.71), channel_id=1, source_target_pairs={{0,2},{1,3},{2,0},{3,1},{4,6},{5,7},{6,4},{7,5},{8,10},{9,11},{10,... | collective-permute-start | bytes 491528 | tf_op jit(solution)/shard_map/return_02/ppermute | solution.py:242
  63.5 8.6 %collective-permute-start.17 = (bf16[20,32,128]{2,1,0:T(8,128)(2,1)S(1)}, bf16[20,32,128]{2,1,0:T(8,128)(2,1)S(1)}, u32[]{:S(2)}, u32[]{:S(2)}) collective-permute-start(bf16[20,32,128]{2,1,0:T(8,128)(2,1)S(1)} %get-tuple-element.72), channel_id=1, source_target_pairs={{0,3},{1,2},{2,1},{3,0},{4,7},{5,6},{6,5},{7,4},{8,11},{9,10},{10,... | collective-permute-start | bytes 491528 | tf_op jit(solution)/shard_map/return_03/ppermute | solution.py:242
  65.5 6.6 %collective-permute-start.22 = (bf16[12,32,128]{2,1,0:T(8,128)(2,1)S(1)}, bf16[12,32,128]{2,1,0:T(8,128)(2,1)S(1)}, u32[]{:S(2)}, u32[]{:S(2)}) collective-permute-start(bf16[12,32,128]{2,1,0:T(8,128)(2,1)S(1)} %get-tuple-element.80), channel_id=1, source_target_pairs={{0,1},{1,0},{2,3},{3,2},{4,5},{5,4},{6,7},{7,6},{8,9},{9,8},{10,11... | collective-permute-start | bytes 294920 | tf_op jit(solution)/shard_map/return_11/ppermute | solution.py:242
  67.8 5.9 %collective-permute-start.23 = (bf16[12,32,128]{2,1,0:T(8,128)(2,1)S(1)}, bf16[12,32,128]{2,1,0:T(8,128)(2,1)S(1)}, u32[]{:S(2)}, u32[]{:S(2)}) collective-permute-start(bf16[12,32,128]{2,1,0:T(8,128)(2,1)S(1)} %get-tuple-element.81), channel_id=1, source_target_pairs={{0,2},{1,3},{2,0},{3,1},{4,6},{5,7},{6,4},{7,5},{8,10},{9,11},{10,... | collective-permute-start | bytes 294920 | tf_op jit(solution)/shard_map/return_12/ppermute | solution.py:242
  69.1 6.8 %collective-permute-start.24 = (bf16[12,32,128]{2,1,0:T(8,128)(2,1)S(1)}, bf16[12,32,128]{2,1,0:T(8,128)(2,1)S(1)}, u32[]{:S(2)}, u32[]{:S(2)}) collective-permute-start(bf16[12,32,128]{2,1,0:T(8,128)(2,1)S(1)} %get-tuple-element.82), channel_id=1, source_target_pairs={{0,3},{1,2},{2,1},{3,0},{4,7},{5,6},{6,5},{7,4},{8,11},{9,10},{10,... | collective-permute-start | bytes 294920 | tf_op jit(solution)/shard_map/return_13/ppermute | solution.py:242

commit v21 on v17

--- a/solution.py
+++ b/solution.py
@@ -11,12 +11,14 @@
 F32, BF16 = jnp.float32, jnp.bfloat16
 LANES = 128
 SPARE = 6 * 1024 * 1024
+GRANT = 52 * 1024 * 1024
 SHARES = (9, 7)
 NT = (((1,), (1,)), ((), ()))
 TN = (((0,), (0,)), ((), ()))
 VMEM = pl.BlockSpec(memory_space=pltpu.VMEM)
 GROUP = 4
 UNROLL = 8
+PARTS = 4
 
 
 def place():
@@ -54,12 +56,13 @@
             row += rows + 1
 
 
-def right_rows(pair, valid, gain, chosen, normed_out, held):
-    rows, toks, _ = pair.shape
+def right_rows(pair, valid, gain, chosen, normed_out, held, start=0, rows=None):
+    toks = pair.shape[1]
+    rows = rows or pair.shape[0]
 
     @pl.loop(0, rows // GROUP, unroll=UNROLL)
     def _(at):
-        first = at * GROUP
+        first = start + at * GROUP
         x = pair[pl.ds(first, GROUP)].astype(F32).reshape(GROUP * toks, -1)
         normed = normalise(x, gain[...])
         normed_out[pl.ds(first * toks, GROUP * toks), :] = normed
@@ -67,7 +70,13 @@
 
 
 def right_own_kernel(pair, mask, gain, weight, *rest):
-    out, normed_out, first, second, chosen_left, valid, gain_out, turned, held = rest
+    out, normed_out, first, second, chosen_left, valid, gain_out, turned, held, arrived, sems = rest
+    step = arrived.shape[0] // PARTS
+    copies = []
+    for n in range(PARTS):
+        span = pl.ds(n * step, step)
+        copies.append(pltpu.make_async_copy(pair.at[span], arrived.at[span], sems.at[n]))
+        copies[n].start()
     gain_out[...] = gain[...]
     hidden = weight.shape[1] // 4
     part = hidden // 4
@@ -85,7 +94,9 @@
             else:
                 chosen = second if p else first
                 chosen[(n - 2) * part : (n - 1) * part, :] = columns
-    right_rows(pair, valid, gain, first, normed_out, held)
+    for n in range(PARTS):
+        copies[n].wait()
+        right_rows(arrived, valid, gain, first, normed_out, held, n * step, step)
     write_pieces([out], held, 0)
 
 
@@ -203,11 +214,12 @@
         out[i] = (gate[i] * mapped).astype(BF16)
 
 
-def kernel(body, name, out_shape, in_specs, scratch=()):
+def kernel(body, name, out_shape, in_specs, scratch=(), limit=None):
     outs = jax.tree.map(lambda _: VMEM, out_shape)
 
     def call(*args):
         arrays = [*args, *jax.tree.leaves(out_shape), *scratch]
+        arrays = [x for x in arrays if hasattr(x.dtype, "itemsize")]
         size = sum(x.dtype.itemsize * math.prod(x.shape) for x in arrays)
         return pl.pallas_call(
             body,
@@ -216,7 +228,7 @@
             out_specs=outs,
             scratch_shapes=list(scratch),
             compiler_params=pltpu.CompilerParams(
-                vmem_limit_bytes=size + SPARE, fuse_transposed_lhs_in_matmul=True
+                vmem_limit_bytes=limit or size + SPARE, fuse_transposed_lhs_in_matmul=True
             ),
             name=name,
         )(*args)
@@ -276,8 +288,14 @@
         right_own_kernel,
         "right_own",
         [piece(part, rows, toks), rows_all, *weights, valid_shape, gains],
-        [VMEM] * 4,
-        [pltpu.VMEM((4 * hidden, channels), BF16), columns(part)],
+        [pl.BlockSpec(memory_space=pl.ANY)] + [VMEM] * 3,
+        [
+            pltpu.VMEM((4 * hidden, channels), BF16),
+            columns(part),
+            pltpu.VMEM(pair.shape, BF16),
+            pltpu.SemaphoreType.DMA((PARTS,)),
+        ],
+        GRANT,
     )(pair, pair_mask, gains, proj_weight)
     right0, normed1, twin_valid = kernel(
         right_twin_kernel,

time: 77.4 us -> 78.6 us (1.016)
  Pallas kernels: 9.74 us -> 12.2 us
  local copies, waits for them, and re-layouts: 3.52 us -> 2.29 us
    pallas_call x12, Pallas kernels: 9.74 us -> 12.2 us  [call(): pl.pallas_call(body, out_shape=out_shape, in_specs=in_specs, out_specs=ou...]
    unnamed x14 -> x12, local copies, waits for them, and re-layouts: 3.52 us -> 2.29 us
  transfers between devices with their start and end apart: 25 -> 25, of which waited for: 12 -> 12; matrix products, arithmetic and copies ran while one was open for 0% -> 0% of each run, Pallas kernels for 7% -> 10%
where the time goes in v21:
time: 78.6 us; the launch traced here: 78.1 us
  waiting for transfers between devices  32.6 us (41%)
  starting transfers between devices  30.8 us (39%)
  Pallas kernels  12.2 us (16%)
  local copies, waits for them, and re-layouts  2.29 us (3%)
    ppermute x25, waiting for transfers between devices, send(): return lax.ppermute(x, ('row', 'chan'), pairs)  32.6 us
    ppermute x25, starting transfers between devices, send(): return lax.ppermute(x, ('row', 'chan'), pairs)  30.8 us
    pallas_call x12, Pallas kernels, call(): pl.pallas_call(body, out_shape=out_shape, in_specs=in_specs, out_specs=ou...  12.2 us
    unnamed x12, local copies, waits for them, and re-layouts  2.29 us
  transfers between devices with their start and end apart: 25, of which 12 were waited for; matrix products, arithmetic and copies ran while one was open for 0% of the time, Pallas kernels for 10%

profile of v21, /device:TPU:1, one launch (start us, length us, event | category | flops | bytes accessed | tf_op | source)
XLA Modules:
  0.0 78.1 jit_solution(4452887273372026000)
XLA Ops:
  0.0 0.1 collective-permute-start
  0.1 0.5 collective-permute-start.1
  0.5 0.9 %copy-done = bf16[128,512]{1,0:T(8,128)(2,1)S(1)} copy-done((bf16[128,512]{1,0:T(8,128)(2,1)S(1)}, bf16[128,512]{1,0:T(8,128)(2,1)}, u32[]{:S(2)}) %copy-start) | copy-done | bytes 131096
  1.4 0.7 copy-done.3
  2.1 0.7 copy-done.4
  2.8 4.0 %right_own.1 = (bf16[32,32,128]{2,1,0:T(8,128)(2,1)S(1)}, bf16[4096,128]{1,0:T(8,128)(2,1)S(1)}, bf16[64,128]{1,0:T(8,128)(2,1)S(1)}, bf16[64,128]{1,0:T(8,128)(...) custom-call(bf16[32,128,128]{2,1,0:T(8,128)(2,1)} %pair.1, ...), custom_call_target="tpu_custom_call" | custom-call | tf_op jit(solution)/shard_map/right_own/pallas_call | solution.py:224
  6.8 0.0 collective-permute-done.1.mask
  6.8 0.0 collective-permute-done.pair
  6.8 1.6 %right_twin.1 = (bf16[32,32,256]{2,1,0:T(8,128)(2,1)S(1)}, bf16[4096,128]{1,0:T(8,128)(2,1)S(1)}, f32[1,32,128]{2,1,0:T(8,128)S(1)}) custom-call(bf16[32,128,128]{2,1,0:T(8,128)(2,1)S(1)} %collective-permute-done.pair, s32[32,128]{1,0:T(8,128)S(1)} %collective-permute-done.1.mask, f32[1,128]{1,0:T(1,128)S(1)} %get-tuple-element.45.gain, ...), custom_call_target="tpu_custom_call" | custom-call | tf_op jit(solution)/shard_map/right_twin/pallas_call | solution.py:224
  8.4 2.4 %collective-permute-start.3 = (bf16[32,32,256]{2,1,0:T(8,128)(2,1)S(1)}, bf16[32,32,256]{2,1,0:T(8,128)(2,1)S(1)}, u32[]{:S(2)}, u32[]{:S(2)}) collective-permute-start(bf16[32,32,256]{2,1,0:T(8,128)(2,1)S(1)} %get-tuple-element.56.rest_2_), channel_id=1, source_target_pairs={{0,4},{1,5},{2,6},{3,7},{4,0},{5,1},{6,2},{7,3},{8,12},{9,13},{10,... | collective-permute-start | bytes 1572872 | tf_op jit(solution)/shard_map/end_right_0/ppermute | solution.py:254
  10.7 0.8 %collective-permute-start.6 = (bf16[32,32,256]{2,1,0:T(8,128)(2,1)S(1)}, bf16[32,32,256]{2,1,0:T(8,128)(2,1)S(1)}, u32[]{:S(2)}, u32[]{:S(2)}) collective-permute-start(bf16[32,32,256]{2,1,0:T(8,128)(2,1)S(1)} %get-tuple-element.56.rest_2_), channel_id=1, source_target_pairs={{0,1},{1,0},{2,3},{3,2},{4,8},{5,9},{6,10},{7,11},{8,4},{9,5},{10,... | collective-permute-start | bytes 1572872 | tf_op jit(solution)/shard_map/mid_own_0/ppermute | solution.py:254
  11.5 0.9 %right_neighbour.1 = (bf16[18,32,256]{2,1,0:T(8,128)(2,1)S(1)}, bf16[14,32,256]{2,1,0:T(8,128)(2,1)S(1)}) custom-call(bf16[4096,128]{1,0:T(8,128)(2,1)S(1)} %get-tuple-element.44.normed.normed0, bf16[4096,128]{1,0:T(8,128)(2,1)S(1)} %get-tuple-element.48.normed1, f32[1,32,128]{2,1,0:T(8,128)S(1)} %get-tuple-element.49.valid0, ...), custom_call_target="tpu_custom_call" | custom-call | tf_op jit(solution)/shard_map/right_neighbour/pallas_call | solution.py:224
  12.4 1.3 %collective-permute-start.2 = (bf16[18,32,256]{2,1,0:T(8,128)(2,1)S(1)}, bf16[18,32,256]{2,1,0:T(8,128)(2,1)S(1)}, u32[]{:S(2)}, u32[]{:S(2)}) collective-permute-start(bf16[18,32,256]{2,1,0:T(8,128)(2,1)S(1)} %get-tuple-element.55), channel_id=1, source_target_pairs={{0,2},{1,3},{2,0},{3,1},{4,6},{5,7},{6,4},{7,5},{8,10},{9,11},{10,... | collective-permute-start | bytes 884744 | tf_op jit(solution)/shard_map/cross_right_0/ppermute | solution.py:254
  13.8 0.9 %left.1 = (bf16[32,32,256]{2,1,0:T(8,128)(2,1)S(1)}, bf16[18,32,256]{2,1,0:T(8,128)(2,1)S(1)}, bf16[14,32,256]{2,1,0:T(8,128)(2,1)S(1)}) custom-call(bf16[4096,128]{1,0:T(8,128)(2,1)S(1)} %get-tuple-element.44.normed.normed0, bf16[4096,128]{1,0:T(8,128)(2,1)S(1)} %get-tuple-element.48.normed1, f32[1,32,128]{2,1,0:T(8,128)S(1)} %get-tuple-element.49.valid0, ...), custom_call_target="tpu_custom_call" | custom-call | tf_op jit(solution)/shard_map/left/pallas_call | solution.py:224
  14.7 6.5 %collective-permute-done.2.rest_3_ = bf16[18,32,256]{2,1,0:T(8,128)(2,1)S(1)} collective-permute-done((bf16[18,32,256]{2,1,0:T(8,128)(2,1)S(1)}, bf16[18,32,256]{2,1,0:T(8,128)(2,1)S(1)}, u32[]{:S(2)}, u32[]{:S(2)}) %collective-permute-start.2) | collective-permute-done | bytes 294944 | tf_op jit(solution)/shard_map/cross_right_0/ppermute | solution.py:254
  21.2 0.8 %collective-permute-start.9 = (bf16[18,32,256]{2,1,0:T(8,128)(2,1)S(1)}, bf16[18,32,256]{2,1,0:T(8,128)(2,1)S(1)}, u32[]{:S(2)}, u32[]{:S(2)}) collective-permute-start(bf16[18,32,256]{2,1,0:T(8,128)(2,1)S(1)} %collective-permute-done.2.rest_3_), channel_id=1, source_target_pairs={{0,1},{1,0},{2,3},{3,2},{4,8},{5,9},{6,10},{7,11},{8,4},{9,5},{10,... | collective-permute-start | bytes 884744 | tf_op jit(solution)/shard_map/mid_own_10/ppermute | solution.py:254
  21.9 0.1 collective-permute-start.5
  22.1 0.5 collective-permute-done.3.rest_4_
  22.6 1.1 %collective-permute-start.4 = (bf16[18,32,256]{2,1,0:T(8,128)(2,1)S(1)}, bf16[18,32,256]{2,1,0:T(8,128)(2,1)S(1)}, u32[]{:S(2)}, u32[]{:S(2)}) collective-permute-start(bf16[18,32,256]{2,1,0:T(8,128)(2,1)S(1)} %get-tuple-element.57), channel_id=1, source_target_pairs={{0,2},{1,3},{2,0},{3,1},{4,6},{5,7},{6,4},{7,5},{8,10},{9,11},{10,... | collective-permute-start | bytes 884744 | tf_op jit(solution)/shard_map/cross_left_0/ppermute | solution.py:254
  23.7 0.0 collective-permute-done.6.rest_4_
  23.7 2.2 %collective-permute-start.10 = (bf16[32,32,256]{2,1,0:T(8,128)(2,1)S(1)}, bf16[32,32,256]{2,1,0:T(8,128)(2,1)S(1)}, u32[]{:S(2)}, u32[]{:S(2)}) collective-permute-start(bf16[32,32,256]{2,1,0:T(8,128)(2,1)S(1)} %collective-permute-done.3.rest_4_), channel_id=1, source_target_pairs={{0,1},{1,0},{2,3},{3,2},{4,8},{5,9},{6,10},{7,11},{8,4},{9,5},{10,... | collective-permute-start | bytes 1572872 | tf_op jit(solution)/shard_map/mid_next_0/ppermute | solution.py:254
  25.8 0.4 collective-permute-start.7
  26.3 0.0 collective-permute-done.9.rest_5_
  26.3 3.9 %collective-permute-done.5.rest_5_ = bf16[18,32,256]{2,1,0:T(8,128)(2,1)S(1)} collective-permute-done((bf16[18,32,256]{2,1,0:T(8,128)(2,1)S(1)}, bf16[18,32,256]{2,1,0:T(8,128)(2,1)S(1)}, u32[]{:S(2)}, u32[]{:S(2)}) %collective-permute-start.5) | collective-permute-done | bytes 294944 | tf_op jit(solution)/shard_map/end_right_10/ppermute | solution.py:254
  30.2 0.0 collective-permute-done.4.rest_1_
  30.2 1.2 %collective-permute-start.12 = (bf16[14,32,256]{2,1,0:T(8,128)(2,1)S(1)}, bf16[14,32,256]{2,1,0:T(8,128)(2,1)S(1)}, u32[]{:S(2)}, u32[]{:S(2)}) collective-permute-start(bf16[14,32,256]{2,1,0:T(8,128)(2,1)S(1)} %get-tuple-element.65), channel_id=1, source_target_pairs={{0,2},{1,3},{2,0},{3,1},{4,6},{5,7},{6,4},{7,5},{8,10},{9,11},{10,... | collective-permute-start | bytes 688136 | tf_op jit(solution)/shard_map/cross_right_1/ppermute | solution.py:254
  31.4 0.4 gate.1
  31.9 2.3 %collective-permute-start.11 = (bf16[18,32,256]{2,1,0:T(8,128)(2,1)S(1)}, bf16[18,32,256]{2,1,0:T(8,128)(2,1)S(1)}, u32[]{:S(2)}, u32[]{:S(2)}) collective-permute-start(bf16[18,32,256]{2,1,0:T(8,128)(2,1)S(1)} %collective-permute-done.5.rest_5_), channel_id=1, source_target_pairs={{0,1},{1,0},{2,3},{3,2},{4,8},{5,9},{6,10},{7,11},{8,4},{9,5},{10,... | collective-permute-start | bytes 884744 | tf_op jit(solution)/shard_map/mid_next_10/ppermute | solution.py:254
  34.2 0.0 collective-permute-start.8
  34.2 1.2 %collective-permute-done.12.rest_3_ = bf16[14,32,256]{2,1,0:T(8,128)(2,1)S(1)} collective-permute-done((bf16[14,32,256]{2,1,0:T(8,128)(2,1)S(1)}, bf16[14,32,256]{2,1,0:T(8,128)(2,1)S(1)}, u32[]{:S(2)}, u32[]{:S(2)}) %collective-permute-start.12) | collective-permute-done | bytes 229408 | tf_op jit(solution)/shard_map/cross_right_1/ppermute | solution.py:254
  35.4 0.0 collective-permute-done.10.rest_6_
  35.4 1.2 %collective-permute-start.13 = (bf16[14,32,256]{2,1,0:T(8,128)(2,1)S(1)}, bf16[14,32,256]{2,1,0:T(8,128)(2,1)S(1)}, u32[]{:S(2)}, u32[]{:S(2)}) collective-permute-start(bf16[14,32,256]{2,1,0:T(8,128)(2,1)S(1)} %get-tuple-element.66), channel_id=1, source_target_pairs={{0,2},{1,3},{2,0},{3,1},{4,6},{5,7},{6,4},{7,5},{8,10},{9,11},{10,... | collective-permute-start | bytes 688136 | tf_op jit(solution)/shard_map/cross_left_1/ppermute | solution.py:254
  36.6 4.8 %collective-permute-done.7.rest_2_ = bf16[32,32,256]{2,1,0:T(8,128)(2,1)S(1)} collective-permute-done((bf16[32,32,256]{2,1,0:T(8,128)(2,1)S(1)}, bf16[32,32,256]{2,1,0:T(8,128)(2,1)S(1)}, u32[]{:S(2)}, u32[]{:S(2)}) %collective-permute-start.7) | collective-permute-done | bytes 524320 | tf_op jit(solution)/shard_map/end_left_0/ppermute | solution.py:254
  41.4 2.0 %collective-permute-start.18 = (bf16[14,32,256]{2,1,0:T(8,128)(2,1)S(1)}, bf16[14,32,256]{2,1,0:T(8,128)(2,1)S(1)}, u32[]{:S(2)}, u32[]{:S(2)}) collective-permute-start(bf16[14,32,256]{2,1,0:T(8,128)(2,1)S(1)} %collective-permute-done.12.rest_3_), channel_id=1, source_target_pairs={{0,4},{1,5},{2,6},{3,7},{4,0},{5,1},{6,2},{7,3},{8,12},{9,13},{10,... | collective-permute-start | bytes 688136 | tf_op jit(solution)/shard_map/end_right_11/ppermute | solution.py:254
  43.5 3.3 %collective-permute-start.19 = (bf16[14,32,256]{2,1,0:T(8,128)(2,1)S(1)}, bf16[14,32,256]{2,1,0:T(8,128)(2,1)S(1)}, u32[]{:S(2)}, u32[]{:S(2)}) collective-permute-start(bf16[14,32,256]{2,1,0:T(8,128)(2,1)S(1)} %collective-permute-done.12.rest_3_), channel_id=1, source_target_pairs={{0,1},{1,0},{2,3},{3,2},{4,8},{5,9},{6,10},{7,11},{8,4},{9,5},{10,... | collective-permute-start | bytes 688136 | tf_op jit(solution)/shard_map/mid_own_11/ppermute | solution.py:254
  46.7 0.0 collective-permute-done.11.rest_7_
  46.7 1.0 %collective-permute-done.8.rest_3_ = bf16[18,32,256]{2,1,0:T(8,128)(2,1)S(1)} collective-permute-done((bf16[18,32,256]{2,1,0:T(8,128)(2,1)S(1)}, bf16[18,32,256]{2,1,0:T(8,128)(2,1)S(1)}, u32[]{:S(2)}, u32[]{:S(2)}) %collective-permute-start.8) | collective-permute-done | bytes 294944 | tf_op jit(solution)/shard_map/end_left_10/ppermute | solution.py:254
  47.7 0.0 collective-permute-done.13.rest_8_.rest_1_
  47.7 0.6 away.2
  48.3 0.9 %collective-permute-start.14 = (bf16[18,32,256]{2,1,0:T(8,128)(2,1)S(1)}, bf16[18,32,256]{2,1,0:T(8,128)(2,1)S(1)}, u32[]{:S(2)}, u32[]{:S(2)}) collective-permute-start(bf16[18,32,256]{2,1,0:T(8,128)(2,1)S(1)} %get-tuple-element.68), channel_id=1, source_target_pairs={{0,4},{1,5},{2,6},{3,7},{4,0},{5,1},{6,2},{7,3},{8,12},{9,13},{10,... | collective-permute-start | bytes 884744 | tf_op jit(solution)/shard_map/left_11_and_products_back_0/ppermute | solution.py:254
  49.2 3.4 %collective-permute-done.18.rest_5_ = bf16[14,32,256]{2,1,0:T(8,128)(2,1)S(1)} collective-permute-done((bf16[14,32,256]{2,1,0:T(8,128)(2,1)S(1)}, bf16[14,32,256]{2,1,0:T(8,128)(2,1)S(1)}, u32[]{:S(2)}, u32[]{:S(2)}) %collective-permute-start.18) | collective-permute-done | bytes 229408 | tf_op jit(solution)/shard_map/end_right_11/ppermute | solution.py:254
  52.7 0.0 collective-permute-done.19.rest_5_
  52.7 2.0 %collective-permute-start.20 = (bf16[14,32,256]{2,1,0:T(8,128)(2,1)S(1)}, bf16[14,32,256]{2,1,0:T(8,128)(2,1)S(1)}, u32[]{:S(2)}, u32[]{:S(2)}) collective-permute-start(bf16[14,32,256]{2,1,0:T(8,128)(2,1)S(1)} %collective-permute-done.18.rest_5_), channel_id=1, source_target_pairs={{0,1},{1,0},{2,3},{3,2},{4,8},{5,9},{6,10},{7,11},{8,4},{9,5},{10,... | collective-permute-start | bytes 688136 | tf_op jit(solution)/shard_map/mid_next_11/ppermute | solution.py:254
  54.6 0.6 near.2
  55.3 0.5 near.3
  55.8 3.2 %collective-permute-done.14.end.rest_3_ = bf16[18,32,256]{2,1,0:T(8,128)(2,1)S(1)} collective-permute-done((bf16[18,32,256]{2,1,0:T(8,128)(2,1)S(1)}, bf16[18,32,256]{2,1,0:T(8,128)(2,1)S(1)}, u32[]{:S(2)}, u32[]{:S(2)}) %collective-permute-start.14) | collective-permute-done | bytes 294944 | tf_op jit(solution)/shard_map/left_11_and_products_back_0/ppermute | solution.py:254
  59.0 0.1 hand_out.2
  59.1 0.0 copy-start.2
  59.1 0.0 copy-start.5
  59.1 0.5 away.3
  59.6 0.1 collective-permute-start.21
  59.7 2.7 %collective-permute-start.15 = (bf16[18,32,128]{2,1,0:T(8,128)(2,1)S(1)}, bf16[18,32,128]{2,1,0:T(8,128)(2,1)S(1)}, u32[]{:S(2)}, u32[]{:S(2)}) collective-permute-start(bf16[18,32,128]{2,1,0:T(8,128)(2,1)S(1)} %get-tuple-element.70), channel_id=1, source_target_pairs={{0,1},{1,0},{2,3},{3,2},{4,5},{5,4},{6,7},{7,6},{8,9},{9,8},{10,11... | collective-permute-start | bytes 442376 | tf_op jit(solution)/shard_map/return_01/ppermute | solution.py:254
  62.4 1.2 %collective-permute-start.16 = (bf16[18,32,128]{2,1,0:T(8,128)(2,1)S(1)}, bf16[18,32,128]{2,1,0:T(8,128)(2,1)S(1)}, u32[]{:S(2)}, u32[]{:S(2)}) collective-permute-start(bf16[18,32,128]{2,1,0:T(8,128)(2,1)S(1)} %get-tuple-element.71), channel_id=1, source_target_pairs={{0,2},{1,3},{2,0},{3,1},{4,6},{5,7},{6,4},{7,5},{8,10},{9,11},{10,... | collective-permute-start | bytes 442376 | tf_op jit(solution)/shard_map/return_02/ppermute | solution.py:254
  63.7 0.4 collective-permute-start.17
  64.1 1.5 %collective-permute-done.21.end = bf16[14,32,256]{2,1,0:T(8,128)(2,1)S(1)} collective-permute-done((bf16[14,32,256]{2,1,0:T(8,128)(2,1)S(1)}, bf16[14,32,256]{2,1,0:T(8,128)(2,1)S(1)}, u32[]{:S(2)}, u32[]{:S(2)}) %collective-permute-start.21) | collective-permute-done | bytes 229408 | tf_op jit(solution)/shard_map/products_back_1/ppermute | solution.py:254
  65.6 0.1 hand_out.3
  65.7 2.2 %collective-permute-start.22 = (bf16[14,32,128]{2,1,0:T(8,128)(2,1)S(1)}, bf16[14,32,128]{2,1,0:T(8,128)(2,1)S(1)}, u32[]{:S(2)}, u32[]{:S(2)}) collective-permute-start(bf16[14,32,128]{2,1,0:T(8,128)(2,1)S(1)} %get-tuple-element.80), channel_id=1, source_target_pairs={{0,1},{1,0},{2,3},{3,2},{4,5},{5,4},{6,7},{7,6},{8,9},{9,8},{10,11... | collective-permute-start | bytes 344072 | tf_op jit(solution)/shard_map/return_11/ppermute | solution.py:254
  67.8 1.3 %collective-permute-start.23 = (bf16[14,32,128]{2,1,0:T(8,128)(2,1)S(1)}, bf16[14,32,128]{2,1,0:T(8,128)(2,1)S(1)}, u32[]{:S(2)}, u32[]{:S(2)}) collective-permute-start(bf16[14,32,128]{2,1,0:T(8,128)(2,1)S(1)} %get-tuple-element.81), channel_id=1, source_target_pairs={{0,2},{1,3},{2,0},{3,1},{4,6},{5,7},{6,4},{7,5},{8,10},{9,11},{10,... | collective-permute-start | bytes 344072 | tf_op jit(solution)/shard_map/return_12/ppermute | solution.py:254
  69.1 0.0 collective-permute-done.15.rest_1_
  69.1 0.5 collective-permute-start.24
  69.6 2.0 %collective-permute-done.17.rest_3_ = bf16[18,32,128]{2,1,0:T(8,128)(2,1)S(1)} collective-permute-done((bf16[18,32,128]{2,1,0:T(8,128)(2,1)S(1)}, bf16[18,32,128]{2,1,0:T(8,128)(2,1)S(1)}, u32[]{:S(2)}, u32[]{:S(2)}) %collective-permute-start.17) | collective-permute-done | bytes 147488 | tf_op jit(solution)/shard_map/return_03/ppermute | solution.py:254
  71.5 2.0 %collective-permute-done.23.rest_6_ = bf16[14,32,128]{2,1,0:T(8,128)(2,1)S(1)} collective-permute-done((bf16[14,32,128]{2,1,0:T(8,128)(2,1)S(1)}, bf16[14,32,128]{2,1,0:T(8,128)(2,1)S(1)}, u32[]{:S(2)}, u32[]{:S(2)}) %collective-permute-start.23) | collective-permute-done | bytes 114720 | tf_op jit(solution)/shard_map/return_12/ppermute | solution.py:254
  73.5 2.6 %collective-permute-done.24.rest_7_ = bf16[14,32,128]{2,1,0:T(8,128)(2,1)S(1)} collective-permute-done((bf16[14,32,128]{2,1,0:T(8,128)(2,1)S(1)}, bf16[14,32,128]{2,1,0:T(8,128)(2,1)S(1)}, u32[]{:S(2)}, u32[]{:S(2)}) %collective-permute-start.24) | collective-permute-done | bytes 114720 | tf_op jit(solution)/shard_map/return_13/ppermute | solution.py:254
  76.1 2.0 %update.1 = bf16[32,128,128]{2,1,0:T(8,128)(2,1)} custom-call(f32[1,128]{1,0:T(1,128)S(1)} %bitcast.3, bf16[128,128]{1,0:T(8,128)(2,1)S(1)} %copy-done.2, f32[32,128,128]{2,1,0:T(8,128)S(1)} %gate.1, bf16[18,32,128]{2,1,0:T(8,128)(2,1)S(1)} %get-tuple-element.69.rest_0_, bf16[18,32,128]{2,1,0:T(8,128)(2,1)S(1)} %collective-permute-done.15.rest_1_, ...), custom_call_target="tpu_custom_call" | custom-call | tf_op jit(solution)/shard_map/update/pallas_call | solution.py:224
  (10 shorter events, 0.0 us)
Async XLA Ops:
  0.0 6.8 %collective-permute-start = (bf16[32,128,128]{2,1,0:T(8,128)(2,1)}, bf16[32,128,128]{2,1,0:T(8,128)(2,1)S(1)}, u32[]{:S(2)}, u32[]{:S(2)}) collective-permute-start(bf16[32,128,128]{2,1,0:T(8,128)(2,1)} %pair.1), channel_id=1, source_target_pairs={{0,1},{1,0},{2,3},{3,2},{4,5},{5,4},{6,7},{7,6},{8,9},{9,8},{10,11... | collective-permute-start | bytes 3145736 | tf_op jit(solution)/shard_map/pair/ppermute | solution.py:254
  0.1 6.7 %collective-permute-start.1 = (s32[32,128]{1,0:T(8,128)}, s32[32,128]{1,0:T(8,128)S(1)}, u32[]{:S(2)}, u32[]{:S(2)}) collective-permute-start(s32[32,128]{1,0:T(8,128)} %mask.1), channel_id=1, source_target_pairs={{0,1},{1,0},{2,3},{3,2},{4,5},{5,4},{6,7},{7,6},{8,9},{9,8},{10,11... | collective-permute-start | bytes 49160 | tf_op jit(solution)/shard_map/mask/ppermute | solution.py:254
  0.5 0.9 %copy-start = (bf16[128,512]{1,0:T(8,128)(2,1)S(1)}, bf16[128,512]{1,0:T(8,128)(2,1)}, u32[]{:S(2)}) copy-start(bf16[128,512]{1,0:T(8,128)(2,1)} %weight.3) | copy-start | bytes 393220
  1.4 0.7 copy-start.3
  2.1 0.7 copy-start.4
  8.4 14.2 %collective-permute-start.3 = (bf16[32,32,256]{2,1,0:T(8,128)(2,1)S(1)}, bf16[32,32,256]{2,1,0:T(8,128)(2,1)S(1)}, u32[]{:S(2)}, u32[]{:S(2)}) collective-permute-start(bf16[32,32,256]{2,1,0:T(8,128)(2,1)S(1)} %get-tuple-element.56.rest_2_), channel_id=1, source_target_pairs={{0,4},{1,5},{2,6},{3,7},{4,0},{5,1},{6,2},{7,3},{8,12},{9,13},{10,... | collective-permute-start | bytes 1572872 | tf_op jit(solution)/shard_map/end_right_0/ppermute | solution.py:254
  10.7 12.9 %collective-permute-start.6 = (bf16[32,32,256]{2,1,0:T(8,128)(2,1)S(1)}, bf16[32,32,256]{2,1,0:T(8,128)(2,1)S(1)}, u32[]{:S(2)}, u32[]{:S(2)}) collective-permute-start(bf16[32,32,256]{2,1,0:T(8,128)(2,1)S(1)} %get-tuple-element.56.rest_2_), channel_id=1, source_target_pairs={{0,1},{1,0},{2,3},{3,2},{4,8},{5,9},{6,10},{7,11},{8,4},{9,5},{10,... | collective-permute-start | bytes 1572872 | tf_op jit(solution)/shard_map/mid_own_0/ppermute | solution.py:254
  11.5 19.9 %copy-start.1 = (bf16[128,128]{1,0:T(8,128)(2,1)S(1)}, bf16[128,128]{1,0:T(8,128)(2,1)}, u32[]{:S(2)}) copy-start(bf16[128,128]{1,0:T(8,128)(2,1)} %weight.4) | copy-start | bytes 98308
  12.4 8.7 %collective-permute-start.2 = (bf16[18,32,256]{2,1,0:T(8,128)(2,1)S(1)}, bf16[18,32,256]{2,1,0:T(8,128)(2,1)S(1)}, u32[]{:S(2)}, u32[]{:S(2)}) collective-permute-start(bf16[18,32,256]{2,1,0:T(8,128)(2,1)S(1)} %get-tuple-element.55), channel_id=1, source_target_pairs={{0,2},{1,3},{2,0},{3,1},{4,6},{5,7},{6,4},{7,5},{8,10},{9,11},{10,... | collective-permute-start | bytes 884744 | tf_op jit(solution)/shard_map/cross_right_0/ppermute | solution.py:254
  21.2 5.1 %collective-permute-start.9 = (bf16[18,32,256]{2,1,0:T(8,128)(2,1)S(1)}, bf16[18,32,256]{2,1,0:T(8,128)(2,1)S(1)}, u32[]{:S(2)}, u32[]{:S(2)}) collective-permute-start(bf16[18,32,256]{2,1,0:T(8,128)(2,1)S(1)} %collective-permute-done.2.rest_3_), channel_id=1, source_target_pairs={{0,1},{1,0},{2,3},{3,2},{4,8},{5,9},{6,10},{7,11},{8,4},{9,5},{10,... | collective-permute-start | bytes 884744 | tf_op jit(solution)/shard_map/mid_own_10/ppermute | solution.py:254
  21.9 8.2 %collective-permute-start.5 = (bf16[18,32,256]{2,1,0:T(8,128)(2,1)S(1)}, bf16[18,32,256]{2,1,0:T(8,128)(2,1)S(1)}, u32[]{:S(2)}, u32[]{:S(2)}) collective-permute-start(bf16[18,32,256]{2,1,0:T(8,128)(2,1)S(1)} %collective-permute-done.2.rest_3_), channel_id=1, source_target_pairs={{0,4},{1,5},{2,6},{3,7},{4,0},{5,1},{6,2},{7,3},{8,12},{9,13},{10,... | collective-permute-start | bytes 884744 | tf_op jit(solution)/shard_map/end_right_10/ppermute | solution.py:254
  22.6 7.6 %collective-permute-start.4 = (bf16[18,32,256]{2,1,0:T(8,128)(2,1)S(1)}, bf16[18,32,256]{2,1,0:T(8,128)(2,1)S(1)}, u32[]{:S(2)}, u32[]{:S(2)}) collective-permute-start(bf16[18,32,256]{2,1,0:T(8,128)(2,1)S(1)} %get-tuple-element.57), channel_id=1, source_target_pairs={{0,2},{1,3},{2,0},{3,1},{4,6},{5,7},{6,4},{7,5},{8,10},{9,11},{10,... | collective-permute-start | bytes 884744 | tf_op jit(solution)/shard_map/cross_left_0/ppermute | solution.py:254
  23.7 11.7 %collective-permute-start.10 = (bf16[32,32,256]{2,1,0:T(8,128)(2,1)S(1)}, bf16[32,32,256]{2,1,0:T(8,128)(2,1)S(1)}, u32[]{:S(2)}, u32[]{:S(2)}) collective-permute-start(bf16[32,32,256]{2,1,0:T(8,128)(2,1)S(1)} %collective-permute-done.3.rest_4_), channel_id=1, source_target_pairs={{0,1},{1,0},{2,3},{3,2},{4,8},{5,9},{6,10},{7,11},{8,4},{9,5},{10,... | collective-permute-start | bytes 1572872 | tf_op jit(solution)/shard_map/mid_next_0/ppermute | solution.py:254
  25.8 15.6 %collective-permute-start.7 = (bf16[32,32,256]{2,1,0:T(8,128)(2,1)S(1)}, bf16[32,32,256]{2,1,0:T(8,128)(2,1)S(1)}, u32[]{:S(2)}, u32[]{:S(2)}) collective-permute-start(bf16[32,32,256]{2,1,0:T(8,128)(2,1)S(1)} %get-tuple-element.74.rest_0_), channel_id=1, source_target_pairs={{0,4},{1,5},{2,6},{3,7},{4,0},{5,1},{6,2},{7,3},{8,12},{9,13},{10,... | collective-permute-start | bytes 1572872 | tf_op jit(solution)/shard_map/end_left_0/ppermute | solution.py:254
  30.2 5.2 %collective-permute-start.12 = (bf16[14,32,256]{2,1,0:T(8,128)(2,1)S(1)}, bf16[14,32,256]{2,1,0:T(8,128)(2,1)S(1)}, u32[]{:S(2)}, u32[]{:S(2)}) collective-permute-start(bf16[14,32,256]{2,1,0:T(8,128)(2,1)S(1)} %get-tuple-element.65), channel_id=1, source_target_pairs={{0,2},{1,3},{2,0},{3,1},{4,6},{5,7},{6,4},{7,5},{8,10},{9,11},{10,... | collective-permute-start | bytes 688136 | tf_op jit(solution)/shard_map/cross_right_1/ppermute | solution.py:254
  31.9 14.9 %collective-permute-start.11 = (bf16[18,32,256]{2,1,0:T(8,128)(2,1)S(1)}, bf16[18,32,256]{2,1,0:T(8,128)(2,1)S(1)}, u32[]{:S(2)}, u32[]{:S(2)}) collective-permute-start(bf16[18,32,256]{2,1,0:T(8,128)(2,1)S(1)} %collective-permute-done.5.rest_5_), channel_id=1, source_target_pairs={{0,1},{1,0},{2,3},{3,2},{4,8},{5,9},{6,10},{7,11},{8,4},{9,5},{10,... | collective-permute-start | bytes 884744 | tf_op jit(solution)/shard_map/mid_next_10/ppermute | solution.py:254
  34.2 13.6 %collective-permute-start.8 = (bf16[18,32,256]{2,1,0:T(8,128)(2,1)S(1)}, bf16[18,32,256]{2,1,0:T(8,128)(2,1)S(1)}, u32[]{:S(2)}, u32[]{:S(2)}) collective-permute-start(bf16[18,32,256]{2,1,0:T(8,128)(2,1)S(1)} %collective-permute-done.4.rest_1_), channel_id=1, source_target_pairs={{0,4},{1,5},{2,6},{3,7},{4,0},{5,1},{6,2},{7,3},{8,12},{9,13},{10,... | collective-permute-start | bytes 884744 | tf_op jit(solution)/shard_map/end_left_10/ppermute | solution.py:254
  35.4 12.4 %collective-permute-start.13 = (bf16[14,32,256]{2,1,0:T(8,128)(2,1)S(1)}, bf16[14,32,256]{2,1,0:T(8,128)(2,1)S(1)}, u32[]{:S(2)}, u32[]{:S(2)}) collective-permute-start(bf16[14,32,256]{2,1,0:T(8,128)(2,1)S(1)} %get-tuple-element.66), channel_id=1, source_target_pairs={{0,2},{1,3},{2,0},{3,1},{4,6},{5,7},{6,4},{7,5},{8,10},{9,11},{10,... | collective-permute-start | bytes 688136 | tf_op jit(solution)/shard_map/cross_left_1/ppermute | solution.py:254
  41.4 11.2 %collective-permute-start.18 = (bf16[14,32,256]{2,1,0:T(8,128)(2,1)S(1)}, bf16[14,32,256]{2,1,0:T(8,128)(2,1)S(1)}, u32[]{:S(2)}, u32[]{:S(2)}) collective-permute-start(bf16[14,32,256]{2,1,0:T(8,128)(2,1)S(1)} %collective-permute-done.12.rest_3_), channel_id=1, source_target_pairs={{0,4},{1,5},{2,6},{3,7},{4,0},{5,1},{6,2},{7,3},{8,12},{9,13},{10,... | collective-permute-start | bytes 688136 | tf_op jit(solution)/shard_map/end_right_11/ppermute | solution.py:254
  43.5 9.2 %collective-permute-start.19 = (bf16[14,32,256]{2,1,0:T(8,128)(2,1)S(1)}, bf16[14,32,256]{2,1,0:T(8,128)(2,1)S(1)}, u32[]{:S(2)}, u32[]{:S(2)}) collective-permute-start(bf16[14,32,256]{2,1,0:T(8,128)(2,1)S(1)} %collective-permute-done.12.rest_3_), channel_id=1, source_target_pairs={{0,1},{1,0},{2,3},{3,2},{4,8},{5,9},{6,10},{7,11},{8,4},{9,5},{10,... | collective-permute-start | bytes 688136 | tf_op jit(solution)/shard_map/mid_own_11/ppermute | solution.py:254
  48.3 10.6 %collective-permute-start.14 = (bf16[18,32,256]{2,1,0:T(8,128)(2,1)S(1)}, bf16[18,32,256]{2,1,0:T(8,128)(2,1)S(1)}, u32[]{:S(2)}, u32[]{:S(2)}) collective-permute-start(bf16[18,32,256]{2,1,0:T(8,128)(2,1)S(1)} %get-tuple-element.68), channel_id=1, source_target_pairs={{0,4},{1,5},{2,6},{3,7},{4,0},{5,1},{6,2},{7,3},{8,12},{9,13},{10,... | collective-permute-start | bytes 884744 | tf_op jit(solution)/shard_map/left_11_and_products_back_0/ppermute | solution.py:254
  52.7 6.4 %collective-permute-start.20 = (bf16[14,32,256]{2,1,0:T(8,128)(2,1)S(1)}, bf16[14,32,256]{2,1,0:T(8,128)(2,1)S(1)}, u32[]{:S(2)}, u32[]{:S(2)}) collective-permute-start(bf16[14,32,256]{2,1,0:T(8,128)(2,1)S(1)} %collective-permute-done.18.rest_5_), channel_id=1, source_target_pairs={{0,1},{1,0},{2,3},{3,2},{4,8},{5,9},{6,10},{7,11},{8,4},{9,5},{10,... | collective-permute-start | bytes 688136 | tf_op jit(solution)/shard_map/mid_next_11/ppermute | solution.py:254
  59.1 17.0 %copy-start.2 = (bf16[128,128]{1,0:T(8,128)(2,1)S(1)}, bf16[128,128]{1,0:T(8,128)(2,1)}, u32[]{:S(2)}) copy-start(bf16[128,128]{1,0:T(8,128)(2,1)} %weight.5) | copy-start | bytes 98308
  59.1 17.0 %copy-start.5 = (f32[128]{0:T(128)S(1)}, f32[128]{0:T(128)}, u32[]{:S(2)}) copy-start(f32[128]{0:T(128)} %param.12) | copy-start | bytes 1540
  59.6 6.0 %collective-permute-start.21 = (bf16[14,32,256]{2,1,0:T(8,128)(2,1)S(1)}, bf16[14,32,256]{2,1,0:T(8,128)(2,1)S(1)}, u32[]{:S(2)}, u32[]{:S(2)}) collective-permute-start(bf16[14,32,256]{2,1,0:T(8,128)(2,1)S(1)} %get-tuple-element.78), channel_id=1, source_target_pairs={{0,4},{1,5},{2,6},{3,7},{4,0},{5,1},{6,2},{7,3},{8,12},{9,13},{10,... | collective-permute-start | bytes 688136 | tf_op jit(solution)/shard_map/products_back_1/ppermute | solution.py:254
  59.7 9.4 %collective-permute-start.15 = (bf16[18,32,128]{2,1,0:T(8,128)(2,1)S(1)}, bf16[18,32,128]{2,1,0:T(8,128)(2,1)S(1)}, u32[]{:S(2)}, u32[]{:S(2)}) collective-permute-start(bf16[18,32,128]{2,1,0:T(8,128)(2,1)S(1)} %get-tuple-element.70), channel_id=1, source_target_pairs={{0,1},{1,0},{2,3},{3,2},{4,5},{5,4},{6,7},{7,6},{8,9},{9,8},{10,11... | collective-permute-start | bytes 442376 | tf_op jit(solution)/shard_map/return_01/ppermute | solution.py:254
  62.4 7.1 %collective-permute-start.16 = (bf16[18,32,128]{2,1,0:T(8,128)(2,1)S(1)}, bf16[18,32,128]{2,1,0:T(8,128)(2,1)S(1)}, u32[]{:S(2)}, u32[]{:S(2)}) collective-permute-start(bf16[18,32,128]{2,1,0:T(8,128)(2,1)S(1)} %get-tuple-element.71), channel_id=1, source_target_pairs={{0,2},{1,3},{2,0},{3,1},{4,6},{5,7},{6,4},{7,5},{8,10},{9,11},{10,... | collective-permute-start | bytes 442376 | tf_op jit(solution)/shard_map/return_02/ppermute | solution.py:254
  63.7 7.9 %collective-permute-start.17 = (bf16[18,32,128]{2,1,0:T(8,128)(2,1)S(1)}, bf16[18,32,128]{2,1,0:T(8,128)(2,1)S(1)}, u32[]{:S(2)}, u32[]{:S(2)}) collective-permute-start(bf16[18,32,128]{2,1,0:T(8,128)(2,1)S(1)} %get-tuple-element.72), channel_id=1, source_target_pairs={{0,3},{1,2},{2,1},{3,0},{4,7},{5,6},{6,5},{7,4},{8,11},{9,10},{10,... | collective-permute-start | bytes 442376 | tf_op jit(solution)/shard_map/return_03/ppermute | solution.py:254
  65.7 5.9 %collective-permute-start.22 = (bf16[14,32,128]{2,1,0:T(8,128)(2,1)S(1)}, bf16[14,32,128]{2,1,0:T(8,128)(2,1)S(1)}, u32[]{:S(2)}, u32[]{:S(2)}) collective-permute-start(bf16[14,32,128]{2,1,0:T(8,128)(2,1)S(1)} %get-tuple-element.80), channel_id=1, source_target_pairs={{0,1},{1,0},{2,3},{3,2},{4,5},{5,4},{6,7},{7,6},{8,9},{9,8},{10,11... | collective-permute-start | bytes 344072 | tf_op jit(solution)/shard_map/return_11/ppermute | solution.py:254
  67.8 5.7 %collective-permute-start.23 = (bf16[14,32,128]{2,1,0:T(8,128)(2,1)S(1)}, bf16[14,32,128]{2,1,0:T(8,128)(2,1)S(1)}, u32[]{:S(2)}, u32[]{:S(2)}) collective-permute-start(bf16[14,32,128]{2,1,0:T(8,128)(2,1)S(1)} %get-tuple-element.81), channel_id=1, source_target_pairs={{0,2},{1,3},{2,0},{3,1},{4,6},{5,7},{6,4},{7,5},{8,10},{9,11},{10,... | collective-permute-start | bytes 344072 | tf_op jit(solution)/shard_map/return_12/ppermute | solution.py:254
  69.1 7.0 %collective-permute-start.24 = (bf16[14,32,128]{2,1,0:T(8,128)(2,1)S(1)}, bf16[14,32,128]{2,1,0:T(8,128)(2,1)S(1)}, u32[]{:S(2)}, u32[]{:S(2)}) collective-permute-start(bf16[14,32,128]{2,1,0:T(8,128)(2,1)S(1)} %get-tuple-element.82), channel_id=1, source_target_pairs={{0,3},{1,2},{2,1},{3,0},{4,7},{5,6},{6,5},{7,4},{8,11},{9,10},{10,... | collective-permute-start | bytes 344072 | tf_op jit(solution)/shard_map/return_13/ppermute | solution.py:254

commit v22 on v17

--- a/solution.py
+++ b/solution.py
@@ -215,9 +215,7 @@
             in_specs=in_specs,
             out_specs=outs,
             scratch_shapes=list(scratch),
-            compiler_params=pltpu.CompilerParams(
-                vmem_limit_bytes=size + SPARE, fuse_transposed_lhs_in_matmul=True
-            ),
+            compiler_params=pltpu.CompilerParams(vmem_limit_bytes=size + SPARE),
             name=name,
         )(*args)
 

time: 77.4 us -> 77.4 us (level)
  no operation moved by 1% of the time
where the time goes in v22:
time: 77.4 us; the launch traced here: 76.9 us
  waiting for transfers between devices  32.6 us (42%)
  starting transfers between devices  30.9 us (40%)
  Pallas kernels  9.76 us (13%)
  local copies, waits for them, and re-layouts  3.52 us (5%)
    ppermute x25, waiting for transfers between devices, send(): return lax.ppermute(x, ('row', 'chan'), pairs)  32.6 us
    ppermute x25, starting transfers between devices, send(): return lax.ppermute(x, ('row', 'chan'), pairs)  30.9 us
    pallas_call x12, Pallas kernels, call(): pl.pallas_call(body, out_shape=out_shape, in_specs=in_specs, out_specs=ou...  9.76 us
    unnamed x14, local copies, waits for them, and re-layouts  3.52 us
  transfers between devices with their start and end apart: 25, of which 12 were waited for; matrix products, arithmetic and copies ran while one was open for 0% of the time, Pallas kernels for 7%

profile of v22, /device:TPU:1, one launch (start us, length us, event | category | flops | bytes accessed | tf_op | source)
XLA Modules:
  0.0 76.9 jit_solution(13336519281993357930)
XLA Ops:
  0.0 0.1 collective-permute-start
  0.1 0.5 collective-permute-start.1
  0.5 1.2 %copy-done = bf16[32,128,128]{2,1,0:T(8,128)(2,1)S(1)} copy-done((bf16[32,128,128]{2,1,0:T(8,128)(2,1)S(1)}, bf16[32,128,128]{2,1,0:T(8,128)(2,1)}, u32[]{:S(2)}) %copy-start) | copy-done | bytes 1048600
  1.7 0.9 %copy-done.1 = bf16[128,512]{1,0:T(8,128)(2,1)S(1)} copy-done((bf16[128,512]{1,0:T(8,128)(2,1)S(1)}, bf16[128,512]{1,0:T(8,128)(2,1)}, u32[]{:S(2)}) %copy-start.1) | copy-done | bytes 131096
  2.6 0.7 copy-done.4
  3.4 0.7 copy-done.5
  4.0 1.5 %right_own.1 = (bf16[32,32,128]{2,1,0:T(8,128)(2,1)S(1)}, bf16[4096,128]{1,0:T(8,128)(2,1)S(1)}, bf16[64,128]{1,0:T(8,128)(2,1)S(1)}, bf16[64,128]{1,0:T(8,128)(...) custom-call(bf16[32,128,128]{2,1,0:T(8,128)(2,1)S(1)} %copy-done, ...), custom_call_target="tpu_custom_call" | custom-call | tf_op jit(solution)/shard_map/right_own/pallas_call | solution.py:212
  5.5 0.0 collective-permute-done.1.mask
  5.5 0.0 collective-permute-done.pair
  5.5 1.6 %right_twin.1 = (bf16[32,32,256]{2,1,0:T(8,128)(2,1)S(1)}, bf16[4096,128]{1,0:T(8,128)(2,1)S(1)}, f32[1,32,128]{2,1,0:T(8,128)S(1)}) custom-call(bf16[32,128,128]{2,1,0:T(8,128)(2,1)S(1)} %collective-permute-done.pair, s32[32,128]{1,0:T(8,128)S(1)} %collective-permute-done.1.mask, f32[1,128]{1,0:T(1,128)S(1)} %get-tuple-element.45.gain, ...), custom_call_target="tpu_custom_call" | custom-call | tf_op jit(solution)/shard_map/right_twin/pallas_call | solution.py:212
  7.1 2.4 %collective-permute-start.3 = (bf16[32,32,256]{2,1,0:T(8,128)(2,1)S(1)}, bf16[32,32,256]{2,1,0:T(8,128)(2,1)S(1)}, u32[]{:S(2)}, u32[]{:S(2)}) collective-permute-start(bf16[32,32,256]{2,1,0:T(8,128)(2,1)S(1)} %get-tuple-element.56.rest_2_), channel_id=1, source_target_pairs={{0,4},{1,5},{2,6},{3,7},{4,0},{5,1},{6,2},{7,3},{8,12},{9,13},{10,... | collective-permute-start | bytes 1572872 | tf_op jit(solution)/shard_map/end_right_0/ppermute | solution.py:240
  9.5 0.8 %collective-permute-start.6 = (bf16[32,32,256]{2,1,0:T(8,128)(2,1)S(1)}, bf16[32,32,256]{2,1,0:T(8,128)(2,1)S(1)}, u32[]{:S(2)}, u32[]{:S(2)}) collective-permute-start(bf16[32,32,256]{2,1,0:T(8,128)(2,1)S(1)} %get-tuple-element.56.rest_2_), channel_id=1, source_target_pairs={{0,1},{1,0},{2,3},{3,2},{4,8},{5,9},{6,10},{7,11},{8,4},{9,5},{10,... | collective-permute-start | bytes 1572872 | tf_op jit(solution)/shard_map/mid_own_0/ppermute | solution.py:240
  10.3 0.9 %right_neighbour.1 = (bf16[18,32,256]{2,1,0:T(8,128)(2,1)S(1)}, bf16[14,32,256]{2,1,0:T(8,128)(2,1)S(1)}) custom-call(bf16[4096,128]{1,0:T(8,128)(2,1)S(1)} %get-tuple-element.44.normed.normed0, bf16[4096,128]{1,0:T(8,128)(2,1)S(1)} %get-tuple-element.48.normed1, f32[1,32,128]{2,1,0:T(8,128)S(1)} %get-tuple-element.49.valid0, ...), custom_call_target="tpu_custom_call" | custom-call | tf_op jit(solution)/shard_map/right_neighbour/pallas_call | solution.py:212
  11.2 1.3 %collective-permute-start.2 = (bf16[18,32,256]{2,1,0:T(8,128)(2,1)S(1)}, bf16[18,32,256]{2,1,0:T(8,128)(2,1)S(1)}, u32[]{:S(2)}, u32[]{:S(2)}) collective-permute-start(bf16[18,32,256]{2,1,0:T(8,128)(2,1)S(1)} %get-tuple-element.55), channel_id=1, source_target_pairs={{0,2},{1,3},{2,0},{3,1},{4,6},{5,7},{6,4},{7,5},{8,10},{9,11},{10,... | collective-permute-start | bytes 884744 | tf_op jit(solution)/shard_map/cross_right_0/ppermute | solution.py:240
  12.5 0.9 %left.1 = (bf16[32,32,256]{2,1,0:T(8,128)(2,1)S(1)}, bf16[18,32,256]{2,1,0:T(8,128)(2,1)S(1)}, bf16[14,32,256]{2,1,0:T(8,128)(2,1)S(1)}) custom-call(bf16[4096,128]{1,0:T(8,128)(2,1)S(1)} %get-tuple-element.44.normed.normed0, bf16[4096,128]{1,0:T(8,128)(2,1)S(1)} %get-tuple-element.48.normed1, f32[1,32,128]{2,1,0:T(8,128)S(1)} %get-tuple-element.49.valid0, ...), custom_call_target="tpu_custom_call" | custom-call | tf_op jit(solution)/shard_map/left/pallas_call | solution.py:212
  13.4 6.5 %collective-permute-done.2.rest_3_ = bf16[18,32,256]{2,1,0:T(8,128)(2,1)S(1)} collective-permute-done((bf16[18,32,256]{2,1,0:T(8,128)(2,1)S(1)}, bf16[18,32,256]{2,1,0:T(8,128)(2,1)S(1)}, u32[]{:S(2)}, u32[]{:S(2)}) %collective-permute-start.2) | collective-permute-done | bytes 294944 | tf_op jit(solution)/shard_map/cross_right_0/ppermute | solution.py:240
  19.9 0.8 %collective-permute-start.9 = (bf16[18,32,256]{2,1,0:T(8,128)(2,1)S(1)}, bf16[18,32,256]{2,1,0:T(8,128)(2,1)S(1)}, u32[]{:S(2)}, u32[]{:S(2)}) collective-permute-start(bf16[18,32,256]{2,1,0:T(8,128)(2,1)S(1)} %collective-permute-done.2.rest_3_), channel_id=1, source_target_pairs={{0,1},{1,0},{2,3},{3,2},{4,8},{5,9},{6,10},{7,11},{8,4},{9,5},{10,... | collective-permute-start | bytes 884744 | tf_op jit(solution)/shard_map/mid_own_10/ppermute | solution.py:240
  20.7 0.1 collective-permute-start.5
  20.8 0.5 collective-permute-done.3.rest_4_
  21.3 1.1 %collective-permute-start.4 = (bf16[18,32,256]{2,1,0:T(8,128)(2,1)S(1)}, bf16[18,32,256]{2,1,0:T(8,128)(2,1)S(1)}, u32[]{:S(2)}, u32[]{:S(2)}) collective-permute-start(bf16[18,32,256]{2,1,0:T(8,128)(2,1)S(1)} %get-tuple-element.57), channel_id=1, source_target_pairs={{0,2},{1,3},{2,0},{3,1},{4,6},{5,7},{6,4},{7,5},{8,10},{9,11},{10,... | collective-permute-start | bytes 884744 | tf_op jit(solution)/shard_map/cross_left_0/ppermute | solution.py:240
  22.4 0.0 collective-permute-done.6.rest_4_
  22.4 2.2 %collective-permute-start.10 = (bf16[32,32,256]{2,1,0:T(8,128)(2,1)S(1)}, bf16[32,32,256]{2,1,0:T(8,128)(2,1)S(1)}, u32[]{:S(2)}, u32[]{:S(2)}) collective-permute-start(bf16[32,32,256]{2,1,0:T(8,128)(2,1)S(1)} %collective-permute-done.3.rest_4_), channel_id=1, source_target_pairs={{0,1},{1,0},{2,3},{3,2},{4,8},{5,9},{6,10},{7,11},{8,4},{9,5},{10,... | collective-permute-start | bytes 1572872 | tf_op jit(solution)/shard_map/mid_next_0/ppermute | solution.py:240
  24.6 0.4 collective-permute-start.7
  25.0 0.0 collective-permute-done.9.rest_5_
  25.0 3.9 %collective-permute-done.5.rest_5_ = bf16[18,32,256]{2,1,0:T(8,128)(2,1)S(1)} collective-permute-done((bf16[18,32,256]{2,1,0:T(8,128)(2,1)S(1)}, bf16[18,32,256]{2,1,0:T(8,128)(2,1)S(1)}, u32[]{:S(2)}, u32[]{:S(2)}) %collective-permute-start.5) | collective-permute-done | bytes 294944 | tf_op jit(solution)/shard_map/end_right_10/ppermute | solution.py:240
  28.9 0.0 collective-permute-done.4.rest_1_
  28.9 1.3 %collective-permute-start.12 = (bf16[14,32,256]{2,1,0:T(8,128)(2,1)S(1)}, bf16[14,32,256]{2,1,0:T(8,128)(2,1)S(1)}, u32[]{:S(2)}, u32[]{:S(2)}) collective-permute-start(bf16[14,32,256]{2,1,0:T(8,128)(2,1)S(1)} %get-tuple-element.65), channel_id=1, source_target_pairs={{0,2},{1,3},{2,0},{3,1},{4,6},{5,7},{6,4},{7,5},{8,10},{9,11},{10,... | collective-permute-start | bytes 688136 | tf_op jit(solution)/shard_map/cross_right_1/ppermute | solution.py:240
  30.2 0.4 gate.1
  30.6 2.3 %collective-permute-start.11 = (bf16[18,32,256]{2,1,0:T(8,128)(2,1)S(1)}, bf16[18,32,256]{2,1,0:T(8,128)(2,1)S(1)}, u32[]{:S(2)}, u32[]{:S(2)}) collective-permute-start(bf16[18,32,256]{2,1,0:T(8,128)(2,1)S(1)} %collective-permute-done.5.rest_5_), channel_id=1, source_target_pairs={{0,1},{1,0},{2,3},{3,2},{4,8},{5,9},{6,10},{7,11},{8,4},{9,5},{10,... | collective-permute-start | bytes 884744 | tf_op jit(solution)/shard_map/mid_next_10/ppermute | solution.py:240
  32.9 1.2 %collective-permute-done.12.rest_3_ = bf16[14,32,256]{2,1,0:T(8,128)(2,1)S(1)} collective-permute-done((bf16[14,32,256]{2,1,0:T(8,128)(2,1)S(1)}, bf16[14,32,256]{2,1,0:T(8,128)(2,1)S(1)}, u32[]{:S(2)}, u32[]{:S(2)}) %collective-permute-start.12) | collective-permute-done | bytes 229408 | tf_op jit(solution)/shard_map/cross_right_1/ppermute | solution.py:240
  34.1 0.0 collective-permute-done.10.rest_6_
  34.1 1.3 %collective-permute-start.13 = (bf16[14,32,256]{2,1,0:T(8,128)(2,1)S(1)}, bf16[14,32,256]{2,1,0:T(8,128)(2,1)S(1)}, u32[]{:S(2)}, u32[]{:S(2)}) collective-permute-start(bf16[14,32,256]{2,1,0:T(8,128)(2,1)S(1)} %get-tuple-element.66), channel_id=1, source_target_pairs={{0,2},{1,3},{2,0},{3,1},{4,6},{5,7},{6,4},{7,5},{8,10},{9,11},{10,... | collective-permute-start | bytes 688136 | tf_op jit(solution)/shard_map/cross_left_1/ppermute | solution.py:240
  35.4 4.8 %collective-permute-done.7.rest_2_ = bf16[32,32,256]{2,1,0:T(8,128)(2,1)S(1)} collective-permute-done((bf16[32,32,256]{2,1,0:T(8,128)(2,1)S(1)}, bf16[32,32,256]{2,1,0:T(8,128)(2,1)S(1)}, u32[]{:S(2)}, u32[]{:S(2)}) %collective-permute-start.7) | collective-permute-done | bytes 524320 | tf_op jit(solution)/shard_map/end_left_0/ppermute | solution.py:240
  40.2 2.0 %collective-permute-start.18 = (bf16[14,32,256]{2,1,0:T(8,128)(2,1)S(1)}, bf16[14,32,256]{2,1,0:T(8,128)(2,1)S(1)}, u32[]{:S(2)}, u32[]{:S(2)}) collective-permute-start(bf16[14,32,256]{2,1,0:T(8,128)(2,1)S(1)} %collective-permute-done.12.rest_3_), channel_id=1, source_target_pairs={{0,4},{1,5},{2,6},{3,7},{4,0},{5,1},{6,2},{7,3},{8,12},{9,13},{10,... | collective-permute-start | bytes 688136 | tf_op jit(solution)/shard_map/end_right_11/ppermute | solution.py:240
  42.2 3.3 %collective-permute-start.19 = (bf16[14,32,256]{2,1,0:T(8,128)(2,1)S(1)}, bf16[14,32,256]{2,1,0:T(8,128)(2,1)S(1)}, u32[]{:S(2)}, u32[]{:S(2)}) collective-permute-start(bf16[14,32,256]{2,1,0:T(8,128)(2,1)S(1)} %collective-permute-done.12.rest_3_), channel_id=1, source_target_pairs={{0,1},{1,0},{2,3},{3,2},{4,8},{5,9},{6,10},{7,11},{8,4},{9,5},{10,... | collective-permute-start | bytes 688136 | tf_op jit(solution)/shard_map/mid_own_11/ppermute | solution.py:240
  45.5 1.0 %collective-permute-done.8.rest_3_ = bf16[18,32,256]{2,1,0:T(8,128)(2,1)S(1)} collective-permute-done((bf16[18,32,256]{2,1,0:T(8,128)(2,1)S(1)}, bf16[18,32,256]{2,1,0:T(8,128)(2,1)S(1)}, u32[]{:S(2)}, u32[]{:S(2)}) %collective-permute-start.8) | collective-permute-done | bytes 294944 | tf_op jit(solution)/shard_map/end_left_10/ppermute | solution.py:240
  46.5 0.0 collective-permute-done.13.rest_8_.rest_1_
  46.5 0.6 away.2
  47.1 0.9 %collective-permute-start.14 = (bf16[18,32,256]{2,1,0:T(8,128)(2,1)S(1)}, bf16[18,32,256]{2,1,0:T(8,128)(2,1)S(1)}, u32[]{:S(2)}, u32[]{:S(2)}) collective-permute-start(bf16[18,32,256]{2,1,0:T(8,128)(2,1)S(1)} %get-tuple-element.68), channel_id=1, source_target_pairs={{0,4},{1,5},{2,6},{3,7},{4,0},{5,1},{6,2},{7,3},{8,12},{9,13},{10,... | collective-permute-start | bytes 884744 | tf_op jit(solution)/shard_map/left_11_and_products_back_0/ppermute | solution.py:240
  47.9 3.5 %collective-permute-done.18.rest_5_ = bf16[14,32,256]{2,1,0:T(8,128)(2,1)S(1)} collective-permute-done((bf16[14,32,256]{2,1,0:T(8,128)(2,1)S(1)}, bf16[14,32,256]{2,1,0:T(8,128)(2,1)S(1)}, u32[]{:S(2)}, u32[]{:S(2)}) %collective-permute-start.18) | collective-permute-done | bytes 229408 | tf_op jit(solution)/shard_map/end_right_11/ppermute | solution.py:240
  51.4 0.0 collective-permute-done.19.rest_5_
  51.4 2.0 %collective-permute-start.20 = (bf16[14,32,256]{2,1,0:T(8,128)(2,1)S(1)}, bf16[14,32,256]{2,1,0:T(8,128)(2,1)S(1)}, u32[]{:S(2)}, u32[]{:S(2)}) collective-permute-start(bf16[14,32,256]{2,1,0:T(8,128)(2,1)S(1)} %collective-permute-done.18.rest_5_), channel_id=1, source_target_pairs={{0,1},{1,0},{2,3},{3,2},{4,8},{5,9},{6,10},{7,11},{8,4},{9,5},{10,... | collective-permute-start | bytes 688136 | tf_op jit(solution)/shard_map/mid_next_11/ppermute | solution.py:240
  53.4 0.6 near.2
  54.0 0.5 near.3
  54.5 3.2 %collective-permute-done.14.end.rest_3_ = bf16[18,32,256]{2,1,0:T(8,128)(2,1)S(1)} collective-permute-done((bf16[18,32,256]{2,1,0:T(8,128)(2,1)S(1)}, bf16[18,32,256]{2,1,0:T(8,128)(2,1)S(1)}, u32[]{:S(2)}, u32[]{:S(2)}) %collective-permute-start.14) | collective-permute-done | bytes 294944 | tf_op jit(solution)/shard_map/left_11_and_products_back_0/ppermute | solution.py:240
  57.7 0.1 hand_out.2
  57.8 0.0 copy-start.3
  57.8 0.0 copy-start.6
  57.9 0.5 away.3
  58.3 0.1 collective-permute-start.21
  58.4 2.8 %collective-permute-start.15 = (bf16[18,32,128]{2,1,0:T(8,128)(2,1)S(1)}, bf16[18,32,128]{2,1,0:T(8,128)(2,1)S(1)}, u32[]{:S(2)}, u32[]{:S(2)}) collective-permute-start(bf16[18,32,128]{2,1,0:T(8,128)(2,1)S(1)} %get-tuple-element.70), channel_id=1, source_target_pairs={{0,1},{1,0},{2,3},{3,2},{4,5},{5,4},{6,7},{7,6},{8,9},{9,8},{10,11... | collective-permute-start | bytes 442376 | tf_op jit(solution)/shard_map/return_01/ppermute | solution.py:240
  61.2 1.2 %collective-permute-start.16 = (bf16[18,32,128]{2,1,0:T(8,128)(2,1)S(1)}, bf16[18,32,128]{2,1,0:T(8,128)(2,1)S(1)}, u32[]{:S(2)}, u32[]{:S(2)}) collective-permute-start(bf16[18,32,128]{2,1,0:T(8,128)(2,1)S(1)} %get-tuple-element.71), channel_id=1, source_target_pairs={{0,2},{1,3},{2,0},{3,1},{4,6},{5,7},{6,4},{7,5},{8,10},{9,11},{10,... | collective-permute-start | bytes 442376 | tf_op jit(solution)/shard_map/return_02/ppermute | solution.py:240
  62.4 0.4 collective-permute-start.17
  62.8 1.5 %collective-permute-done.21.end = bf16[14,32,256]{2,1,0:T(8,128)(2,1)S(1)} collective-permute-done((bf16[14,32,256]{2,1,0:T(8,128)(2,1)S(1)}, bf16[14,32,256]{2,1,0:T(8,128)(2,1)S(1)}, u32[]{:S(2)}, u32[]{:S(2)}) %collective-permute-start.21) | collective-permute-done | bytes 229408 | tf_op jit(solution)/shard_map/products_back_1/ppermute | solution.py:240
  64.3 0.1 hand_out.3
  64.4 2.2 %collective-permute-start.22 = (bf16[14,32,128]{2,1,0:T(8,128)(2,1)S(1)}, bf16[14,32,128]{2,1,0:T(8,128)(2,1)S(1)}, u32[]{:S(2)}, u32[]{:S(2)}) collective-permute-start(bf16[14,32,128]{2,1,0:T(8,128)(2,1)S(1)} %get-tuple-element.80), channel_id=1, source_target_pairs={{0,1},{1,0},{2,3},{3,2},{4,5},{5,4},{6,7},{7,6},{8,9},{9,8},{10,11... | collective-permute-start | bytes 344072 | tf_op jit(solution)/shard_map/return_11/ppermute | solution.py:240
  66.6 1.3 %collective-permute-start.23 = (bf16[14,32,128]{2,1,0:T(8,128)(2,1)S(1)}, bf16[14,32,128]{2,1,0:T(8,128)(2,1)S(1)}, u32[]{:S(2)}, u32[]{:S(2)}) collective-permute-start(bf16[14,32,128]{2,1,0:T(8,128)(2,1)S(1)} %get-tuple-element.81), channel_id=1, source_target_pairs={{0,2},{1,3},{2,0},{3,1},{4,6},{5,7},{6,4},{7,5},{8,10},{9,11},{10,... | collective-permute-start | bytes 344072 | tf_op jit(solution)/shard_map/return_12/ppermute | solution.py:240
  67.9 0.0 collective-permute-done.15.rest_1_
  67.9 0.4 collective-permute-start.24
  68.3 2.0 %collective-permute-done.17.rest_3_ = bf16[18,32,128]{2,1,0:T(8,128)(2,1)S(1)} collective-permute-done((bf16[18,32,128]{2,1,0:T(8,128)(2,1)S(1)}, bf16[18,32,128]{2,1,0:T(8,128)(2,1)S(1)}, u32[]{:S(2)}, u32[]{:S(2)}) %collective-permute-start.17) | collective-permute-done | bytes 147488 | tf_op jit(solution)/shard_map/return_03/ppermute | solution.py:240
  70.3 0.0 collective-permute-done.22.rest_5_
  70.3 2.0 %collective-permute-done.23.rest_6_ = bf16[14,32,128]{2,1,0:T(8,128)(2,1)S(1)} collective-permute-done((bf16[14,32,128]{2,1,0:T(8,128)(2,1)S(1)}, bf16[14,32,128]{2,1,0:T(8,128)(2,1)S(1)}, u32[]{:S(2)}, u32[]{:S(2)}) %collective-permute-start.23) | collective-permute-done | bytes 114720 | tf_op jit(solution)/shard_map/return_12/ppermute | solution.py:240
  72.3 2.6 %collective-permute-done.24.rest_7_ = bf16[14,32,128]{2,1,0:T(8,128)(2,1)S(1)} collective-permute-done((bf16[14,32,128]{2,1,0:T(8,128)(2,1)S(1)}, bf16[14,32,128]{2,1,0:T(8,128)(2,1)S(1)}, u32[]{:S(2)}, u32[]{:S(2)}) %collective-permute-start.24) | collective-permute-done | bytes 114720 | tf_op jit(solution)/shard_map/return_13/ppermute | solution.py:240
  74.9 2.0 %update.1 = bf16[32,128,128]{2,1,0:T(8,128)(2,1)} custom-call(f32[1,128]{1,0:T(1,128)S(1)} %bitcast.3, bf16[128,128]{1,0:T(8,128)(2,1)S(1)} %copy-done.3, f32[32,128,128]{2,1,0:T(8,128)S(1)} %gate.1, bf16[18,32,128]{2,1,0:T(8,128)(2,1)S(1)} %get-tuple-element.69.rest_0_, bf16[18,32,128]{2,1,0:T(8,128)(2,1)S(1)} %collective-permute-done.15.rest_1_, ...), custom_call_target="tpu_custom_call" | custom-call | tf_op jit(solution)/shard_map/update/pallas_call | solution.py:212
  (12 shorter events, 0.0 us)
Async XLA Ops:
  0.0 5.5 %collective-permute-start = (bf16[32,128,128]{2,1,0:T(8,128)(2,1)}, bf16[32,128,128]{2,1,0:T(8,128)(2,1)S(1)}, u32[]{:S(2)}, u32[]{:S(2)}) collective-permute-start(bf16[32,128,128]{2,1,0:T(8,128)(2,1)} %pair.1), channel_id=1, source_target_pairs={{0,1},{1,0},{2,3},{3,2},{4,5},{5,4},{6,7},{7,6},{8,9},{9,8},{10,11... | collective-permute-start | bytes 3145736 | tf_op jit(solution)/shard_map/pair/ppermute | solution.py:240
  0.1 5.5 %collective-permute-start.1 = (s32[32,128]{1,0:T(8,128)}, s32[32,128]{1,0:T(8,128)S(1)}, u32[]{:S(2)}, u32[]{:S(2)}) collective-permute-start(s32[32,128]{1,0:T(8,128)} %mask.1), channel_id=1, source_target_pairs={{0,1},{1,0},{2,3},{3,2},{4,5},{5,4},{6,7},{7,6},{8,9},{9,8},{10,11... | collective-permute-start | bytes 49160 | tf_op jit(solution)/shard_map/mask/ppermute | solution.py:240
  0.5 1.2 %copy-start = (bf16[32,128,128]{2,1,0:T(8,128)(2,1)S(1)}, bf16[32,128,128]{2,1,0:T(8,128)(2,1)}, u32[]{:S(2)}) copy-start(bf16[32,128,128]{2,1,0:T(8,128)(2,1)} %pair.1) | copy-start | bytes 3145732
  1.7 0.9 %copy-start.1 = (bf16[128,512]{1,0:T(8,128)(2,1)S(1)}, bf16[128,512]{1,0:T(8,128)(2,1)}, u32[]{:S(2)}) copy-start(bf16[128,512]{1,0:T(8,128)(2,1)} %weight.3) | copy-start | bytes 393220
  2.6 0.7 copy-start.4
  3.4 0.7 copy-start.5
  7.1 14.2 %collective-permute-start.3 = (bf16[32,32,256]{2,1,0:T(8,128)(2,1)S(1)}, bf16[32,32,256]{2,1,0:T(8,128)(2,1)S(1)}, u32[]{:S(2)}, u32[]{:S(2)}) collective-permute-start(bf16[32,32,256]{2,1,0:T(8,128)(2,1)S(1)} %get-tuple-element.56.rest_2_), channel_id=1, source_target_pairs={{0,4},{1,5},{2,6},{3,7},{4,0},{5,1},{6,2},{7,3},{8,12},{9,13},{10,... | collective-permute-start | bytes 1572872 | tf_op jit(solution)/shard_map/end_right_0/ppermute | solution.py:240
  9.5 12.9 %collective-permute-start.6 = (bf16[32,32,256]{2,1,0:T(8,128)(2,1)S(1)}, bf16[32,32,256]{2,1,0:T(8,128)(2,1)S(1)}, u32[]{:S(2)}, u32[]{:S(2)}) collective-permute-start(bf16[32,32,256]{2,1,0:T(8,128)(2,1)S(1)} %get-tuple-element.56.rest_2_), channel_id=1, source_target_pairs={{0,1},{1,0},{2,3},{3,2},{4,8},{5,9},{6,10},{7,11},{8,4},{9,5},{10,... | collective-permute-start | bytes 1572872 | tf_op jit(solution)/shard_map/mid_own_0/ppermute | solution.py:240
  10.3 19.9 %copy-start.2 = (bf16[128,128]{1,0:T(8,128)(2,1)S(1)}, bf16[128,128]{1,0:T(8,128)(2,1)}, u32[]{:S(2)}) copy-start(bf16[128,128]{1,0:T(8,128)(2,1)} %weight.4) | copy-start | bytes 98308
  11.2 8.7 %collective-permute-start.2 = (bf16[18,32,256]{2,1,0:T(8,128)(2,1)S(1)}, bf16[18,32,256]{2,1,0:T(8,128)(2,1)S(1)}, u32[]{:S(2)}, u32[]{:S(2)}) collective-permute-start(bf16[18,32,256]{2,1,0:T(8,128)(2,1)S(1)} %get-tuple-element.55), channel_id=1, source_target_pairs={{0,2},{1,3},{2,0},{3,1},{4,6},{5,7},{6,4},{7,5},{8,10},{9,11},{10,... | collective-permute-start | bytes 884744 | tf_op jit(solution)/shard_map/cross_right_0/ppermute | solution.py:240
  19.9 5.1 %collective-permute-start.9 = (bf16[18,32,256]{2,1,0:T(8,128)(2,1)S(1)}, bf16[18,32,256]{2,1,0:T(8,128)(2,1)S(1)}, u32[]{:S(2)}, u32[]{:S(2)}) collective-permute-start(bf16[18,32,256]{2,1,0:T(8,128)(2,1)S(1)} %collective-permute-done.2.rest_3_), channel_id=1, source_target_pairs={{0,1},{1,0},{2,3},{3,2},{4,8},{5,9},{6,10},{7,11},{8,4},{9,5},{10,... | collective-permute-start | bytes 884744 | tf_op jit(solution)/shard_map/mid_own_10/ppermute | solution.py:240
  20.7 8.2 %collective-permute-start.5 = (bf16[18,32,256]{2,1,0:T(8,128)(2,1)S(1)}, bf16[18,32,256]{2,1,0:T(8,128)(2,1)S(1)}, u32[]{:S(2)}, u32[]{:S(2)}) collective-permute-start(bf16[18,32,256]{2,1,0:T(8,128)(2,1)S(1)} %collective-permute-done.2.rest_3_), channel_id=1, source_target_pairs={{0,4},{1,5},{2,6},{3,7},{4,0},{5,1},{6,2},{7,3},{8,12},{9,13},{10,... | collective-permute-start | bytes 884744 | tf_op jit(solution)/shard_map/end_right_10/ppermute | solution.py:240
  21.3 7.6 %collective-permute-start.4 = (bf16[18,32,256]{2,1,0:T(8,128)(2,1)S(1)}, bf16[18,32,256]{2,1,0:T(8,128)(2,1)S(1)}, u32[]{:S(2)}, u32[]{:S(2)}) collective-permute-start(bf16[18,32,256]{2,1,0:T(8,128)(2,1)S(1)} %get-tuple-element.57), channel_id=1, source_target_pairs={{0,2},{1,3},{2,0},{3,1},{4,6},{5,7},{6,4},{7,5},{8,10},{9,11},{10,... | collective-permute-start | bytes 884744 | tf_op jit(solution)/shard_map/cross_left_0/ppermute | solution.py:240
  22.4 11.7 %collective-permute-start.10 = (bf16[32,32,256]{2,1,0:T(8,128)(2,1)S(1)}, bf16[32,32,256]{2,1,0:T(8,128)(2,1)S(1)}, u32[]{:S(2)}, u32[]{:S(2)}) collective-permute-start(bf16[32,32,256]{2,1,0:T(8,128)(2,1)S(1)} %collective-permute-done.3.rest_4_), channel_id=1, source_target_pairs={{0,1},{1,0},{2,3},{3,2},{4,8},{5,9},{6,10},{7,11},{8,4},{9,5},{10,... | collective-permute-start | bytes 1572872 | tf_op jit(solution)/shard_map/mid_next_0/ppermute | solution.py:240
  24.6 15.6 %collective-permute-start.7 = (bf16[32,32,256]{2,1,0:T(8,128)(2,1)S(1)}, bf16[32,32,256]{2,1,0:T(8,128)(2,1)S(1)}, u32[]{:S(2)}, u32[]{:S(2)}) collective-permute-start(bf16[32,32,256]{2,1,0:T(8,128)(2,1)S(1)} %get-tuple-element.74.rest_0_), channel_id=1, source_target_pairs={{0,4},{1,5},{2,6},{3,7},{4,0},{5,1},{6,2},{7,3},{8,12},{9,13},{10,... | collective-permute-start | bytes 1572872 | tf_op jit(solution)/shard_map/end_left_0/ppermute | solution.py:240
  28.9 5.2 %collective-permute-start.12 = (bf16[14,32,256]{2,1,0:T(8,128)(2,1)S(1)}, bf16[14,32,256]{2,1,0:T(8,128)(2,1)S(1)}, u32[]{:S(2)}, u32[]{:S(2)}) collective-permute-start(bf16[14,32,256]{2,1,0:T(8,128)(2,1)S(1)} %get-tuple-element.65), channel_id=1, source_target_pairs={{0,2},{1,3},{2,0},{3,1},{4,6},{5,7},{6,4},{7,5},{8,10},{9,11},{10,... | collective-permute-start | bytes 688136 | tf_op jit(solution)/shard_map/cross_right_1/ppermute | solution.py:240
  30.6 14.9 %collective-permute-start.11 = (bf16[18,32,256]{2,1,0:T(8,128)(2,1)S(1)}, bf16[18,32,256]{2,1,0:T(8,128)(2,1)S(1)}, u32[]{:S(2)}, u32[]{:S(2)}) collective-permute-start(bf16[18,32,256]{2,1,0:T(8,128)(2,1)S(1)} %collective-permute-done.5.rest_5_), channel_id=1, source_target_pairs={{0,1},{1,0},{2,3},{3,2},{4,8},{5,9},{6,10},{7,11},{8,4},{9,5},{10,... | collective-permute-start | bytes 884744 | tf_op jit(solution)/shard_map/mid_next_10/ppermute | solution.py:240
  32.9 13.6 %collective-permute-start.8 = (bf16[18,32,256]{2,1,0:T(8,128)(2,1)S(1)}, bf16[18,32,256]{2,1,0:T(8,128)(2,1)S(1)}, u32[]{:S(2)}, u32[]{:S(2)}) collective-permute-start(bf16[18,32,256]{2,1,0:T(8,128)(2,1)S(1)} %collective-permute-done.4.rest_1_), channel_id=1, source_target_pairs={{0,4},{1,5},{2,6},{3,7},{4,0},{5,1},{6,2},{7,3},{8,12},{9,13},{10,... | collective-permute-start | bytes 884744 | tf_op jit(solution)/shard_map/end_left_10/ppermute | solution.py:240
  34.1 12.4 %collective-permute-start.13 = (bf16[14,32,256]{2,1,0:T(8,128)(2,1)S(1)}, bf16[14,32,256]{2,1,0:T(8,128)(2,1)S(1)}, u32[]{:S(2)}, u32[]{:S(2)}) collective-permute-start(bf16[14,32,256]{2,1,0:T(8,128)(2,1)S(1)} %get-tuple-element.66), channel_id=1, source_target_pairs={{0,2},{1,3},{2,0},{3,1},{4,6},{5,7},{6,4},{7,5},{8,10},{9,11},{10,... | collective-permute-start | bytes 688136 | tf_op jit(solution)/shard_map/cross_left_1/ppermute | solution.py:240
  40.2 11.2 %collective-permute-start.18 = (bf16[14,32,256]{2,1,0:T(8,128)(2,1)S(1)}, bf16[14,32,256]{2,1,0:T(8,128)(2,1)S(1)}, u32[]{:S(2)}, u32[]{:S(2)}) collective-permute-start(bf16[14,32,256]{2,1,0:T(8,128)(2,1)S(1)} %collective-permute-done.12.rest_3_), channel_id=1, source_target_pairs={{0,4},{1,5},{2,6},{3,7},{4,0},{5,1},{6,2},{7,3},{8,12},{9,13},{10,... | collective-permute-start | bytes 688136 | tf_op jit(solution)/shard_map/end_right_11/ppermute | solution.py:240
  42.2 9.2 %collective-permute-start.19 = (bf16[14,32,256]{2,1,0:T(8,128)(2,1)S(1)}, bf16[14,32,256]{2,1,0:T(8,128)(2,1)S(1)}, u32[]{:S(2)}, u32[]{:S(2)}) collective-permute-start(bf16[14,32,256]{2,1,0:T(8,128)(2,1)S(1)} %collective-permute-done.12.rest_3_), channel_id=1, source_target_pairs={{0,1},{1,0},{2,3},{3,2},{4,8},{5,9},{6,10},{7,11},{8,4},{9,5},{10,... | collective-permute-start | bytes 688136 | tf_op jit(solution)/shard_map/mid_own_11/ppermute | solution.py:240
  47.1 10.6 %collective-permute-start.14 = (bf16[18,32,256]{2,1,0:T(8,128)(2,1)S(1)}, bf16[18,32,256]{2,1,0:T(8,128)(2,1)S(1)}, u32[]{:S(2)}, u32[]{:S(2)}) collective-permute-start(bf16[18,32,256]{2,1,0:T(8,128)(2,1)S(1)} %get-tuple-element.68), channel_id=1, source_target_pairs={{0,4},{1,5},{2,6},{3,7},{4,0},{5,1},{6,2},{7,3},{8,12},{9,13},{10,... | collective-permute-start | bytes 884744 | tf_op jit(solution)/shard_map/left_11_and_products_back_0/ppermute | solution.py:240
  51.4 6.4 %collective-permute-start.20 = (bf16[14,32,256]{2,1,0:T(8,128)(2,1)S(1)}, bf16[14,32,256]{2,1,0:T(8,128)(2,1)S(1)}, u32[]{:S(2)}, u32[]{:S(2)}) collective-permute-start(bf16[14,32,256]{2,1,0:T(8,128)(2,1)S(1)} %collective-permute-done.18.rest_5_), channel_id=1, source_target_pairs={{0,1},{1,0},{2,3},{3,2},{4,8},{5,9},{6,10},{7,11},{8,4},{9,5},{10,... | collective-permute-start | bytes 688136 | tf_op jit(solution)/shard_map/mid_next_11/ppermute | solution.py:240
  57.8 17.0 %copy-start.3 = (bf16[128,128]{1,0:T(8,128)(2,1)S(1)}, bf16[128,128]{1,0:T(8,128)(2,1)}, u32[]{:S(2)}) copy-start(bf16[128,128]{1,0:T(8,128)(2,1)} %weight.5) | copy-start | bytes 98308
  57.8 17.0 %copy-start.6 = (f32[128]{0:T(128)S(1)}, f32[128]{0:T(128)}, u32[]{:S(2)}) copy-start(f32[128]{0:T(128)} %param.12) | copy-start | bytes 1540
  58.3 6.0 %collective-permute-start.21 = (bf16[14,32,256]{2,1,0:T(8,128)(2,1)S(1)}, bf16[14,32,256]{2,1,0:T(8,128)(2,1)S(1)}, u32[]{:S(2)}, u32[]{:S(2)}) collective-permute-start(bf16[14,32,256]{2,1,0:T(8,128)(2,1)S(1)} %get-tuple-element.78), channel_id=1, source_target_pairs={{0,4},{1,5},{2,6},{3,7},{4,0},{5,1},{6,2},{7,3},{8,12},{9,13},{10,... | collective-permute-start | bytes 688136 | tf_op jit(solution)/shard_map/products_back_1/ppermute | solution.py:240
  58.4 9.4 %collective-permute-start.15 = (bf16[18,32,128]{2,1,0:T(8,128)(2,1)S(1)}, bf16[18,32,128]{2,1,0:T(8,128)(2,1)S(1)}, u32[]{:S(2)}, u32[]{:S(2)}) collective-permute-start(bf16[18,32,128]{2,1,0:T(8,128)(2,1)S(1)} %get-tuple-element.70), channel_id=1, source_target_pairs={{0,1},{1,0},{2,3},{3,2},{4,5},{5,4},{6,7},{7,6},{8,9},{9,8},{10,11... | collective-permute-start | bytes 442376 | tf_op jit(solution)/shard_map/return_01/ppermute | solution.py:240
  61.2 7.1 %collective-permute-start.16 = (bf16[18,32,128]{2,1,0:T(8,128)(2,1)S(1)}, bf16[18,32,128]{2,1,0:T(8,128)(2,1)S(1)}, u32[]{:S(2)}, u32[]{:S(2)}) collective-permute-start(bf16[18,32,128]{2,1,0:T(8,128)(2,1)S(1)} %get-tuple-element.71), channel_id=1, source_target_pairs={{0,2},{1,3},{2,0},{3,1},{4,6},{5,7},{6,4},{7,5},{8,10},{9,11},{10,... | collective-permute-start | bytes 442376 | tf_op jit(solution)/shard_map/return_02/ppermute | solution.py:240
  62.4 7.9 %collective-permute-start.17 = (bf16[18,32,128]{2,1,0:T(8,128)(2,1)S(1)}, bf16[18,32,128]{2,1,0:T(8,128)(2,1)S(1)}, u32[]{:S(2)}, u32[]{:S(2)}) collective-permute-start(bf16[18,32,128]{2,1,0:T(8,128)(2,1)S(1)} %get-tuple-element.72), channel_id=1, source_target_pairs={{0,3},{1,2},{2,1},{3,0},{4,7},{5,6},{6,5},{7,4},{8,11},{9,10},{10,... | collective-permute-start | bytes 442376 | tf_op jit(solution)/shard_map/return_03/ppermute | solution.py:240
  64.4 5.9 %collective-permute-start.22 = (bf16[14,32,128]{2,1,0:T(8,128)(2,1)S(1)}, bf16[14,32,128]{2,1,0:T(8,128)(2,1)S(1)}, u32[]{:S(2)}, u32[]{:S(2)}) collective-permute-start(bf16[14,32,128]{2,1,0:T(8,128)(2,1)S(1)} %get-tuple-element.80), channel_id=1, source_target_pairs={{0,1},{1,0},{2,3},{3,2},{4,5},{5,4},{6,7},{7,6},{8,9},{9,8},{10,11... | collective-permute-start | bytes 344072 | tf_op jit(solution)/shard_map/return_11/ppermute | solution.py:240
  66.6 5.7 %collective-permute-start.23 = (bf16[14,32,128]{2,1,0:T(8,128)(2,1)S(1)}, bf16[14,32,128]{2,1,0:T(8,128)(2,1)S(1)}, u32[]{:S(2)}, u32[]{:S(2)}) collective-permute-start(bf16[14,32,128]{2,1,0:T(8,128)(2,1)S(1)} %get-tuple-element.81), channel_id=1, source_target_pairs={{0,2},{1,3},{2,0},{3,1},{4,6},{5,7},{6,4},{7,5},{8,10},{9,11},{10,... | collective-permute-start | bytes 344072 | tf_op jit(solution)/shard_map/return_12/ppermute | solution.py:240
  67.9 7.0 %collective-permute-start.24 = (bf16[14,32,128]{2,1,0:T(8,128)(2,1)S(1)}, bf16[14,32,128]{2,1,0:T(8,128)(2,1)S(1)}, u32[]{:S(2)}, u32[]{:S(2)}) collective-permute-start(bf16[14,32,128]{2,1,0:T(8,128)(2,1)S(1)} %get-tuple-element.82), channel_id=1, source_target_pairs={{0,3},{1,2},{2,1},{3,0},{4,7},{5,6},{6,5},{7,4},{8,11},{9,10},{10,... | collective-permute-start | bytes 344072 | tf_op jit(solution)/shard_map/return_13/ppermute | solution.py:240

commit v23 on v22

--- a/solution.py
+++ b/solution.py
@@ -15,8 +15,8 @@
 NT = (((1,), (1,)), ((), ()))
 TN = (((0,), (0,)), ((), ()))
 VMEM = pl.BlockSpec(memory_space=pltpu.VMEM)
-GROUP = 4
-UNROLL = 8
+GROUP = 16
+UNROLL = 2
 
 
 def place():

time: 77.4 us -> 77.3 us (level)
  no operation moved by 1% of the time
where the time goes in v23:
time: 77.3 us; the launch traced here: 76.8 us
  waiting for transfers between devices  32.6 us (42%)
  starting transfers between devices  30.9 us (40%)
  Pallas kernels  9.68 us (13%)
  local copies, waits for them, and re-layouts  3.52 us (5%)
    ppermute x25, waiting for transfers between devices, send(): return lax.ppermute(x, ('row', 'chan'), pairs)  32.6 us
    ppermute x25, starting transfers between devices, send(): return lax.ppermute(x, ('row', 'chan'), pairs)  30.9 us
    pallas_call x12, Pallas kernels, call(): pl.pallas_call(body, out_shape=out_shape, in_specs=in_specs, out_specs=ou...  9.68 us
    unnamed x14, local copies, waits for them, and re-layouts  3.52 us
  transfers between devices with their start and end apart: 25, of which 12 were waited for; matrix products, arithmetic and copies ran while one was open for 0% of the time, Pallas kernels for 7%

profile of v23, /device:TPU:1, one launch (start us, length us, event | category | flops | bytes accessed | tf_op | source)
XLA Modules:
  0.0 76.8 jit_solution(5726819429244257884)
XLA Ops:
  0.0 0.1 collective-permute-start
  0.1 0.5 collective-permute-start.1
  0.5 1.2 %copy-done = bf16[32,128,128]{2,1,0:T(8,128)(2,1)S(1)} copy-done((bf16[32,128,128]{2,1,0:T(8,128)(2,1)S(1)}, bf16[32,128,128]{2,1,0:T(8,128)(2,1)}, u32[]{:S(2)}) %copy-start) | copy-done | bytes 1048600
  1.7 0.9 %copy-done.1 = bf16[128,512]{1,0:T(8,128)(2,1)S(1)} copy-done((bf16[128,512]{1,0:T(8,128)(2,1)S(1)}, bf16[128,512]{1,0:T(8,128)(2,1)}, u32[]{:S(2)}) %copy-start.1) | copy-done | bytes 131096
  2.6 0.7 copy-done.4
  3.4 0.7 copy-done.5
  4.0 1.5 %right_own.1 = (bf16[32,32,128]{2,1,0:T(8,128)(2,1)S(1)}, bf16[4096,128]{1,0:T(8,128)(2,1)S(1)}, bf16[64,128]{1,0:T(8,128)(2,1)S(1)}, bf16[64,128]{1,0:T(8,128)(...) custom-call(bf16[32,128,128]{2,1,0:T(8,128)(2,1)S(1)} %copy-done, ...), custom_call_target="tpu_custom_call" | custom-call | tf_op jit(solution)/shard_map/right_own/pallas_call | solution.py:212
  5.5 0.0 collective-permute-done.1.mask
  5.5 0.0 collective-permute-done.pair
  5.5 1.5 %right_twin.1 = (bf16[32,32,256]{2,1,0:T(8,128)(2,1)S(1)}, bf16[4096,128]{1,0:T(8,128)(2,1)S(1)}, f32[1,32,128]{2,1,0:T(8,128)S(1)}) custom-call(bf16[32,128,128]{2,1,0:T(8,128)(2,1)S(1)} %collective-permute-done.pair, s32[32,128]{1,0:T(8,128)S(1)} %collective-permute-done.1.mask, f32[1,128]{1,0:T(1,128)S(1)} %get-tuple-element.45.gain, ...), custom_call_target="tpu_custom_call" | custom-call | tf_op jit(solution)/shard_map/right_twin/pallas_call | solution.py:212
  7.1 2.4 %collective-permute-start.3 = (bf16[32,32,256]{2,1,0:T(8,128)(2,1)S(1)}, bf16[32,32,256]{2,1,0:T(8,128)(2,1)S(1)}, u32[]{:S(2)}, u32[]{:S(2)}) collective-permute-start(bf16[32,32,256]{2,1,0:T(8,128)(2,1)S(1)} %get-tuple-element.56.rest_2_), channel_id=1, source_target_pairs={{0,4},{1,5},{2,6},{3,7},{4,0},{5,1},{6,2},{7,3},{8,12},{9,13},{10,... | collective-permute-start | bytes 1572872 | tf_op jit(solution)/shard_map/end_right_0/ppermute | solution.py:240
  9.4 0.8 %collective-permute-start.6 = (bf16[32,32,256]{2,1,0:T(8,128)(2,1)S(1)}, bf16[32,32,256]{2,1,0:T(8,128)(2,1)S(1)}, u32[]{:S(2)}, u32[]{:S(2)}) collective-permute-start(bf16[32,32,256]{2,1,0:T(8,128)(2,1)S(1)} %get-tuple-element.56.rest_2_), channel_id=1, source_target_pairs={{0,1},{1,0},{2,3},{3,2},{4,8},{5,9},{6,10},{7,11},{8,4},{9,5},{10,... | collective-permute-start | bytes 1572872 | tf_op jit(solution)/shard_map/mid_own_0/ppermute | solution.py:240
  10.2 0.9 %right_neighbour.1 = (bf16[18,32,256]{2,1,0:T(8,128)(2,1)S(1)}, bf16[14,32,256]{2,1,0:T(8,128)(2,1)S(1)}) custom-call(bf16[4096,128]{1,0:T(8,128)(2,1)S(1)} %get-tuple-element.44.normed.normed0, bf16[4096,128]{1,0:T(8,128)(2,1)S(1)} %get-tuple-element.48.normed1, f32[1,32,128]{2,1,0:T(8,128)S(1)} %get-tuple-element.49.valid0, ...), custom_call_target="tpu_custom_call" | custom-call | tf_op jit(solution)/shard_map/right_neighbour/pallas_call | solution.py:212
  11.1 1.3 %collective-permute-start.2 = (bf16[18,32,256]{2,1,0:T(8,128)(2,1)S(1)}, bf16[18,32,256]{2,1,0:T(8,128)(2,1)S(1)}, u32[]{:S(2)}, u32[]{:S(2)}) collective-permute-start(bf16[18,32,256]{2,1,0:T(8,128)(2,1)S(1)} %get-tuple-element.55), channel_id=1, source_target_pairs={{0,2},{1,3},{2,0},{3,1},{4,6},{5,7},{6,4},{7,5},{8,10},{9,11},{10,... | collective-permute-start | bytes 884744 | tf_op jit(solution)/shard_map/cross_right_0/ppermute | solution.py:240
  12.4 0.9 %left.1 = (bf16[32,32,256]{2,1,0:T(8,128)(2,1)S(1)}, bf16[18,32,256]{2,1,0:T(8,128)(2,1)S(1)}, bf16[14,32,256]{2,1,0:T(8,128)(2,1)S(1)}) custom-call(bf16[4096,128]{1,0:T(8,128)(2,1)S(1)} %get-tuple-element.44.normed.normed0, bf16[4096,128]{1,0:T(8,128)(2,1)S(1)} %get-tuple-element.48.normed1, f32[1,32,128]{2,1,0:T(8,128)S(1)} %get-tuple-element.49.valid0, ...), custom_call_target="tpu_custom_call" | custom-call | tf_op jit(solution)/shard_map/left/pallas_call | solution.py:212
  13.4 6.5 %collective-permute-done.2.rest_3_ = bf16[18,32,256]{2,1,0:T(8,128)(2,1)S(1)} collective-permute-done((bf16[18,32,256]{2,1,0:T(8,128)(2,1)S(1)}, bf16[18,32,256]{2,1,0:T(8,128)(2,1)S(1)}, u32[]{:S(2)}, u32[]{:S(2)}) %collective-permute-start.2) | collective-permute-done | bytes 294944 | tf_op jit(solution)/shard_map/cross_right_0/ppermute | solution.py:240
  19.8 0.8 %collective-permute-start.9 = (bf16[18,32,256]{2,1,0:T(8,128)(2,1)S(1)}, bf16[18,32,256]{2,1,0:T(8,128)(2,1)S(1)}, u32[]{:S(2)}, u32[]{:S(2)}) collective-permute-start(bf16[18,32,256]{2,1,0:T(8,128)(2,1)S(1)} %collective-permute-done.2.rest_3_), channel_id=1, source_target_pairs={{0,1},{1,0},{2,3},{3,2},{4,8},{5,9},{6,10},{7,11},{8,4},{9,5},{10,... | collective-permute-start | bytes 884744 | tf_op jit(solution)/shard_map/mid_own_10/ppermute | solution.py:240
  20.6 0.1 collective-permute-start.5
  20.8 0.5 collective-permute-done.3.rest_4_
  21.3 1.1 %collective-permute-start.4 = (bf16[18,32,256]{2,1,0:T(8,128)(2,1)S(1)}, bf16[18,32,256]{2,1,0:T(8,128)(2,1)S(1)}, u32[]{:S(2)}, u32[]{:S(2)}) collective-permute-start(bf16[18,32,256]{2,1,0:T(8,128)(2,1)S(1)} %get-tuple-element.57), channel_id=1, source_target_pairs={{0,2},{1,3},{2,0},{3,1},{4,6},{5,7},{6,4},{7,5},{8,10},{9,11},{10,... | collective-permute-start | bytes 884744 | tf_op jit(solution)/shard_map/cross_left_0/ppermute | solution.py:240
  22.3 0.0 collective-permute-done.6.rest_4_
  22.3 2.2 %collective-permute-start.10 = (bf16[32,32,256]{2,1,0:T(8,128)(2,1)S(1)}, bf16[32,32,256]{2,1,0:T(8,128)(2,1)S(1)}, u32[]{:S(2)}, u32[]{:S(2)}) collective-permute-start(bf16[32,32,256]{2,1,0:T(8,128)(2,1)S(1)} %collective-permute-done.3.rest_4_), channel_id=1, source_target_pairs={{0,1},{1,0},{2,3},{3,2},{4,8},{5,9},{6,10},{7,11},{8,4},{9,5},{10,... | collective-permute-start | bytes 1572872 | tf_op jit(solution)/shard_map/mid_next_0/ppermute | solution.py:240
  24.5 0.4 collective-permute-start.7
  24.9 0.0 collective-permute-done.9.rest_5_
  24.9 3.9 %collective-permute-done.5.rest_5_ = bf16[18,32,256]{2,1,0:T(8,128)(2,1)S(1)} collective-permute-done((bf16[18,32,256]{2,1,0:T(8,128)(2,1)S(1)}, bf16[18,32,256]{2,1,0:T(8,128)(2,1)S(1)}, u32[]{:S(2)}, u32[]{:S(2)}) %collective-permute-start.5) | collective-permute-done | bytes 294944 | tf_op jit(solution)/shard_map/end_right_10/ppermute | solution.py:240
  28.9 0.0 collective-permute-done.4.rest_1_
  28.9 1.2 %collective-permute-start.12 = (bf16[14,32,256]{2,1,0:T(8,128)(2,1)S(1)}, bf16[14,32,256]{2,1,0:T(8,128)(2,1)S(1)}, u32[]{:S(2)}, u32[]{:S(2)}) collective-permute-start(bf16[14,32,256]{2,1,0:T(8,128)(2,1)S(1)} %get-tuple-element.65), channel_id=1, source_target_pairs={{0,2},{1,3},{2,0},{3,1},{4,6},{5,7},{6,4},{7,5},{8,10},{9,11},{10,... | collective-permute-start | bytes 688136 | tf_op jit(solution)/shard_map/cross_right_1/ppermute | solution.py:240
  30.1 0.4 gate.1
  30.5 2.3 %collective-permute-start.11 = (bf16[18,32,256]{2,1,0:T(8,128)(2,1)S(1)}, bf16[18,32,256]{2,1,0:T(8,128)(2,1)S(1)}, u32[]{:S(2)}, u32[]{:S(2)}) collective-permute-start(bf16[18,32,256]{2,1,0:T(8,128)(2,1)S(1)} %collective-permute-done.5.rest_5_), channel_id=1, source_target_pairs={{0,1},{1,0},{2,3},{3,2},{4,8},{5,9},{6,10},{7,11},{8,4},{9,5},{10,... | collective-permute-start | bytes 884744 | tf_op jit(solution)/shard_map/mid_next_10/ppermute | solution.py:240
  32.8 0.0 collective-permute-start.8
  32.8 1.2 %collective-permute-done.12.rest_3_ = bf16[14,32,256]{2,1,0:T(8,128)(2,1)S(1)} collective-permute-done((bf16[14,32,256]{2,1,0:T(8,128)(2,1)S(1)}, bf16[14,32,256]{2,1,0:T(8,128)(2,1)S(1)}, u32[]{:S(2)}, u32[]{:S(2)}) %collective-permute-start.12) | collective-permute-done | bytes 229408 | tf_op jit(solution)/shard_map/cross_right_1/ppermute | solution.py:240
  34.0 0.0 collective-permute-done.10.rest_6_
  34.0 1.2 %collective-permute-start.13 = (bf16[14,32,256]{2,1,0:T(8,128)(2,1)S(1)}, bf16[14,32,256]{2,1,0:T(8,128)(2,1)S(1)}, u32[]{:S(2)}, u32[]{:S(2)}) collective-permute-start(bf16[14,32,256]{2,1,0:T(8,128)(2,1)S(1)} %get-tuple-element.66), channel_id=1, source_target_pairs={{0,2},{1,3},{2,0},{3,1},{4,6},{5,7},{6,4},{7,5},{8,10},{9,11},{10,... | collective-permute-start | bytes 688136 | tf_op jit(solution)/shard_map/cross_left_1/ppermute | solution.py:240
  35.3 4.8 %collective-permute-done.7.rest_2_ = bf16[32,32,256]{2,1,0:T(8,128)(2,1)S(1)} collective-permute-done((bf16[32,32,256]{2,1,0:T(8,128)(2,1)S(1)}, bf16[32,32,256]{2,1,0:T(8,128)(2,1)S(1)}, u32[]{:S(2)}, u32[]{:S(2)}) %collective-permute-start.7) | collective-permute-done | bytes 524320 | tf_op jit(solution)/shard_map/end_left_0/ppermute | solution.py:240
  40.1 2.0 %collective-permute-start.18 = (bf16[14,32,256]{2,1,0:T(8,128)(2,1)S(1)}, bf16[14,32,256]{2,1,0:T(8,128)(2,1)S(1)}, u32[]{:S(2)}, u32[]{:S(2)}) collective-permute-start(bf16[14,32,256]{2,1,0:T(8,128)(2,1)S(1)} %collective-permute-done.12.rest_3_), channel_id=1, source_target_pairs={{0,4},{1,5},{2,6},{3,7},{4,0},{5,1},{6,2},{7,3},{8,12},{9,13},{10,... | collective-permute-start | bytes 688136 | tf_op jit(solution)/shard_map/end_right_11/ppermute | solution.py:240
  42.1 3.3 %collective-permute-start.19 = (bf16[14,32,256]{2,1,0:T(8,128)(2,1)S(1)}, bf16[14,32,256]{2,1,0:T(8,128)(2,1)S(1)}, u32[]{:S(2)}, u32[]{:S(2)}) collective-permute-start(bf16[14,32,256]{2,1,0:T(8,128)(2,1)S(1)} %collective-permute-done.12.rest_3_), channel_id=1, source_target_pairs={{0,1},{1,0},{2,3},{3,2},{4,8},{5,9},{6,10},{7,11},{8,4},{9,5},{10,... | collective-permute-start | bytes 688136 | tf_op jit(solution)/shard_map/mid_own_11/ppermute | solution.py:240
  45.4 0.0 collective-permute-done.11.rest_7_
  45.4 1.0 %collective-permute-done.8.rest_3_ = bf16[18,32,256]{2,1,0:T(8,128)(2,1)S(1)} collective-permute-done((bf16[18,32,256]{2,1,0:T(8,128)(2,1)S(1)}, bf16[18,32,256]{2,1,0:T(8,128)(2,1)S(1)}, u32[]{:S(2)}, u32[]{:S(2)}) %collective-permute-start.8) | collective-permute-done | bytes 294944 | tf_op jit(solution)/shard_map/end_left_10/ppermute | solution.py:240
  46.4 0.6 away.2
  47.0 0.9 %collective-permute-start.14 = (bf16[18,32,256]{2,1,0:T(8,128)(2,1)S(1)}, bf16[18,32,256]{2,1,0:T(8,128)(2,1)S(1)}, u32[]{:S(2)}, u32[]{:S(2)}) collective-permute-start(bf16[18,32,256]{2,1,0:T(8,128)(2,1)S(1)} %get-tuple-element.68), channel_id=1, source_target_pairs={{0,4},{1,5},{2,6},{3,7},{4,0},{5,1},{6,2},{7,3},{8,12},{9,13},{10,... | collective-permute-start | bytes 884744 | tf_op jit(solution)/shard_map/left_11_and_products_back_0/ppermute | solution.py:240
  47.9 3.5 %collective-permute-done.18.rest_5_ = bf16[14,32,256]{2,1,0:T(8,128)(2,1)S(1)} collective-permute-done((bf16[14,32,256]{2,1,0:T(8,128)(2,1)S(1)}, bf16[14,32,256]{2,1,0:T(8,128)(2,1)S(1)}, u32[]{:S(2)}, u32[]{:S(2)}) %collective-permute-start.18) | collective-permute-done | bytes 229408 | tf_op jit(solution)/shard_map/end_right_11/ppermute | solution.py:240
  51.3 2.0 %collective-permute-start.20 = (bf16[14,32,256]{2,1,0:T(8,128)(2,1)S(1)}, bf16[14,32,256]{2,1,0:T(8,128)(2,1)S(1)}, u32[]{:S(2)}, u32[]{:S(2)}) collective-permute-start(bf16[14,32,256]{2,1,0:T(8,128)(2,1)S(1)} %collective-permute-done.18.rest_5_), channel_id=1, source_target_pairs={{0,1},{1,0},{2,3},{3,2},{4,8},{5,9},{6,10},{7,11},{8,4},{9,5},{10,... | collective-permute-start | bytes 688136 | tf_op jit(solution)/shard_map/mid_next_11/ppermute | solution.py:240
  53.3 0.6 near.2
  53.9 0.5 near.3
  54.4 3.2 %collective-permute-done.14.end.rest_3_ = bf16[18,32,256]{2,1,0:T(8,128)(2,1)S(1)} collective-permute-done((bf16[18,32,256]{2,1,0:T(8,128)(2,1)S(1)}, bf16[18,32,256]{2,1,0:T(8,128)(2,1)S(1)}, u32[]{:S(2)}, u32[]{:S(2)}) %collective-permute-start.14) | collective-permute-done | bytes 294944 | tf_op jit(solution)/shard_map/left_11_and_products_back_0/ppermute | solution.py:240
  57.6 0.1 hand_out.2
  57.7 0.0 copy-start.3
  57.8 0.0 copy-start.6
  57.8 0.0 collective-permute-done.20.rest_7_
  57.8 0.5 away.3
  58.3 0.1 collective-permute-start.21
  58.4 2.8 %collective-permute-start.15 = (bf16[18,32,128]{2,1,0:T(8,128)(2,1)S(1)}, bf16[18,32,128]{2,1,0:T(8,128)(2,1)S(1)}, u32[]{:S(2)}, u32[]{:S(2)}) collective-permute-start(bf16[18,32,128]{2,1,0:T(8,128)(2,1)S(1)} %get-tuple-element.70), channel_id=1, source_target_pairs={{0,1},{1,0},{2,3},{3,2},{4,5},{5,4},{6,7},{7,6},{8,9},{9,8},{10,11... | collective-permute-start | bytes 442376 | tf_op jit(solution)/shard_map/return_01/ppermute | solution.py:240
  61.1 1.2 %collective-permute-start.16 = (bf16[18,32,128]{2,1,0:T(8,128)(2,1)S(1)}, bf16[18,32,128]{2,1,0:T(8,128)(2,1)S(1)}, u32[]{:S(2)}, u32[]{:S(2)}) collective-permute-start(bf16[18,32,128]{2,1,0:T(8,128)(2,1)S(1)} %get-tuple-element.71), channel_id=1, source_target_pairs={{0,2},{1,3},{2,0},{3,1},{4,6},{5,7},{6,4},{7,5},{8,10},{9,11},{10,... | collective-permute-start | bytes 442376 | tf_op jit(solution)/shard_map/return_02/ppermute | solution.py:240
  62.4 0.4 collective-permute-start.17
  62.8 1.5 %collective-permute-done.21.end = bf16[14,32,256]{2,1,0:T(8,128)(2,1)S(1)} collective-permute-done((bf16[14,32,256]{2,1,0:T(8,128)(2,1)S(1)}, bf16[14,32,256]{2,1,0:T(8,128)(2,1)S(1)}, u32[]{:S(2)}, u32[]{:S(2)}) %collective-permute-start.21) | collective-permute-done | bytes 229408 | tf_op jit(solution)/shard_map/products_back_1/ppermute | solution.py:240
  64.3 0.1 hand_out.3
  64.3 2.2 %collective-permute-start.22 = (bf16[14,32,128]{2,1,0:T(8,128)(2,1)S(1)}, bf16[14,32,128]{2,1,0:T(8,128)(2,1)S(1)}, u32[]{:S(2)}, u32[]{:S(2)}) collective-permute-start(bf16[14,32,128]{2,1,0:T(8,128)(2,1)S(1)} %get-tuple-element.80), channel_id=1, source_target_pairs={{0,1},{1,0},{2,3},{3,2},{4,5},{5,4},{6,7},{7,6},{8,9},{9,8},{10,11... | collective-permute-start | bytes 344072 | tf_op jit(solution)/shard_map/return_11/ppermute | solution.py:240
  66.5 1.3 %collective-permute-start.23 = (bf16[14,32,128]{2,1,0:T(8,128)(2,1)S(1)}, bf16[14,32,128]{2,1,0:T(8,128)(2,1)S(1)}, u32[]{:S(2)}, u32[]{:S(2)}) collective-permute-start(bf16[14,32,128]{2,1,0:T(8,128)(2,1)S(1)} %get-tuple-element.81), channel_id=1, source_target_pairs={{0,2},{1,3},{2,0},{3,1},{4,6},{5,7},{6,4},{7,5},{8,10},{9,11},{10,... | collective-permute-start | bytes 344072 | tf_op jit(solution)/shard_map/return_12/ppermute | solution.py:240
  67.8 0.0 collective-permute-done.15.rest_1_
  67.8 0.5 collective-permute-start.24
  68.2 2.0 %collective-permute-done.17.rest_3_ = bf16[18,32,128]{2,1,0:T(8,128)(2,1)S(1)} collective-permute-done((bf16[18,32,128]{2,1,0:T(8,128)(2,1)S(1)}, bf16[18,32,128]{2,1,0:T(8,128)(2,1)S(1)}, u32[]{:S(2)}, u32[]{:S(2)}) %collective-permute-start.17) | collective-permute-done | bytes 147488 | tf_op jit(solution)/shard_map/return_03/ppermute | solution.py:240
  70.3 2.0 %collective-permute-done.23.rest_6_ = bf16[14,32,128]{2,1,0:T(8,128)(2,1)S(1)} collective-permute-done((bf16[14,32,128]{2,1,0:T(8,128)(2,1)S(1)}, bf16[14,32,128]{2,1,0:T(8,128)(2,1)S(1)}, u32[]{:S(2)}, u32[]{:S(2)}) %collective-permute-start.23) | collective-permute-done | bytes 114720 | tf_op jit(solution)/shard_map/return_12/ppermute | solution.py:240
  72.2 2.6 %collective-permute-done.24.rest_7_ = bf16[14,32,128]{2,1,0:T(8,128)(2,1)S(1)} collective-permute-done((bf16[14,32,128]{2,1,0:T(8,128)(2,1)S(1)}, bf16[14,32,128]{2,1,0:T(8,128)(2,1)S(1)}, u32[]{:S(2)}, u32[]{:S(2)}) %collective-permute-start.24) | collective-permute-done | bytes 114720 | tf_op jit(solution)/shard_map/return_13/ppermute | solution.py:240
  74.8 2.0 %update.1 = bf16[32,128,128]{2,1,0:T(8,128)(2,1)} custom-call(f32[1,128]{1,0:T(1,128)S(1)} %bitcast.3, bf16[128,128]{1,0:T(8,128)(2,1)S(1)} %copy-done.3, f32[32,128,128]{2,1,0:T(8,128)S(1)} %gate.1, bf16[18,32,128]{2,1,0:T(8,128)(2,1)S(1)} %get-tuple-element.69.rest_0_, bf16[18,32,128]{2,1,0:T(8,128)(2,1)S(1)} %collective-permute-done.15.rest_1_, ...), custom_call_target="tpu_custom_call" | custom-call | tf_op jit(solution)/shard_map/update/pallas_call | solution.py:212
  (12 shorter events, 0.0 us)
Async XLA Ops:
  0.0 5.5 %collective-permute-start = (bf16[32,128,128]{2,1,0:T(8,128)(2,1)}, bf16[32,128,128]{2,1,0:T(8,128)(2,1)S(1)}, u32[]{:S(2)}, u32[]{:S(2)}) collective-permute-start(bf16[32,128,128]{2,1,0:T(8,128)(2,1)} %pair.1), channel_id=1, source_target_pairs={{0,1},{1,0},{2,3},{3,2},{4,5},{5,4},{6,7},{7,6},{8,9},{9,8},{10,11... | collective-permute-start | bytes 3145736 | tf_op jit(solution)/shard_map/pair/ppermute | solution.py:240
  0.1 5.4 %collective-permute-start.1 = (s32[32,128]{1,0:T(8,128)}, s32[32,128]{1,0:T(8,128)S(1)}, u32[]{:S(2)}, u32[]{:S(2)}) collective-permute-start(s32[32,128]{1,0:T(8,128)} %mask.1), channel_id=1, source_target_pairs={{0,1},{1,0},{2,3},{3,2},{4,5},{5,4},{6,7},{7,6},{8,9},{9,8},{10,11... | collective-permute-start | bytes 49160 | tf_op jit(solution)/shard_map/mask/ppermute | solution.py:240
  0.5 1.2 %copy-start = (bf16[32,128,128]{2,1,0:T(8,128)(2,1)S(1)}, bf16[32,128,128]{2,1,0:T(8,128)(2,1)}, u32[]{:S(2)}) copy-start(bf16[32,128,128]{2,1,0:T(8,128)(2,1)} %pair.1) | copy-start | bytes 3145732
  1.7 0.9 %copy-start.1 = (bf16[128,512]{1,0:T(8,128)(2,1)S(1)}, bf16[128,512]{1,0:T(8,128)(2,1)}, u32[]{:S(2)}) copy-start(bf16[128,512]{1,0:T(8,128)(2,1)} %weight.3) | copy-start | bytes 393220
  2.6 0.7 copy-start.4
  3.4 0.7 copy-start.5
  7.1 14.2 %collective-permute-start.3 = (bf16[32,32,256]{2,1,0:T(8,128)(2,1)S(1)}, bf16[32,32,256]{2,1,0:T(8,128)(2,1)S(1)}, u32[]{:S(2)}, u32[]{:S(2)}) collective-permute-start(bf16[32,32,256]{2,1,0:T(8,128)(2,1)S(1)} %get-tuple-element.56.rest_2_), channel_id=1, source_target_pairs={{0,4},{1,5},{2,6},{3,7},{4,0},{5,1},{6,2},{7,3},{8,12},{9,13},{10,... | collective-permute-start | bytes 1572872 | tf_op jit(solution)/shard_map/end_right_0/ppermute | solution.py:240
  9.4 12.9 %collective-permute-start.6 = (bf16[32,32,256]{2,1,0:T(8,128)(2,1)S(1)}, bf16[32,32,256]{2,1,0:T(8,128)(2,1)S(1)}, u32[]{:S(2)}, u32[]{:S(2)}) collective-permute-start(bf16[32,32,256]{2,1,0:T(8,128)(2,1)S(1)} %get-tuple-element.56.rest_2_), channel_id=1, source_target_pairs={{0,1},{1,0},{2,3},{3,2},{4,8},{5,9},{6,10},{7,11},{8,4},{9,5},{10,... | collective-permute-start | bytes 1572872 | tf_op jit(solution)/shard_map/mid_own_0/ppermute | solution.py:240
  10.2 19.9 %copy-start.2 = (bf16[128,128]{1,0:T(8,128)(2,1)S(1)}, bf16[128,128]{1,0:T(8,128)(2,1)}, u32[]{:S(2)}) copy-start(bf16[128,128]{1,0:T(8,128)(2,1)} %weight.4) | copy-start | bytes 98308
  11.1 8.7 %collective-permute-start.2 = (bf16[18,32,256]{2,1,0:T(8,128)(2,1)S(1)}, bf16[18,32,256]{2,1,0:T(8,128)(2,1)S(1)}, u32[]{:S(2)}, u32[]{:S(2)}) collective-permute-start(bf16[18,32,256]{2,1,0:T(8,128)(2,1)S(1)} %get-tuple-element.55), channel_id=1, source_target_pairs={{0,2},{1,3},{2,0},{3,1},{4,6},{5,7},{6,4},{7,5},{8,10},{9,11},{10,... | collective-permute-start | bytes 884744 | tf_op jit(solution)/shard_map/cross_right_0/ppermute | solution.py:240
  19.8 5.1 %collective-permute-start.9 = (bf16[18,32,256]{2,1,0:T(8,128)(2,1)S(1)}, bf16[18,32,256]{2,1,0:T(8,128)(2,1)S(1)}, u32[]{:S(2)}, u32[]{:S(2)}) collective-permute-start(bf16[18,32,256]{2,1,0:T(8,128)(2,1)S(1)} %collective-permute-done.2.rest_3_), channel_id=1, source_target_pairs={{0,1},{1,0},{2,3},{3,2},{4,8},{5,9},{6,10},{7,11},{8,4},{9,5},{10,... | collective-permute-start | bytes 884744 | tf_op jit(solution)/shard_map/mid_own_10/ppermute | solution.py:240
  20.6 8.2 %collective-permute-start.5 = (bf16[18,32,256]{2,1,0:T(8,128)(2,1)S(1)}, bf16[18,32,256]{2,1,0:T(8,128)(2,1)S(1)}, u32[]{:S(2)}, u32[]{:S(2)}) collective-permute-start(bf16[18,32,256]{2,1,0:T(8,128)(2,1)S(1)} %collective-permute-done.2.rest_3_), channel_id=1, source_target_pairs={{0,4},{1,5},{2,6},{3,7},{4,0},{5,1},{6,2},{7,3},{8,12},{9,13},{10,... | collective-permute-start | bytes 884744 | tf_op jit(solution)/shard_map/end_right_10/ppermute | solution.py:240
  21.3 7.6 %collective-permute-start.4 = (bf16[18,32,256]{2,1,0:T(8,128)(2,1)S(1)}, bf16[18,32,256]{2,1,0:T(8,128)(2,1)S(1)}, u32[]{:S(2)}, u32[]{:S(2)}) collective-permute-start(bf16[18,32,256]{2,1,0:T(8,128)(2,1)S(1)} %get-tuple-element.57), channel_id=1, source_target_pairs={{0,2},{1,3},{2,0},{3,1},{4,6},{5,7},{6,4},{7,5},{8,10},{9,11},{10,... | collective-permute-start | bytes 884744 | tf_op jit(solution)/shard_map/cross_left_0/ppermute | solution.py:240
  22.3 11.7 %collective-permute-start.10 = (bf16[32,32,256]{2,1,0:T(8,128)(2,1)S(1)}, bf16[32,32,256]{2,1,0:T(8,128)(2,1)S(1)}, u32[]{:S(2)}, u32[]{:S(2)}) collective-permute-start(bf16[32,32,256]{2,1,0:T(8,128)(2,1)S(1)} %collective-permute-done.3.rest_4_), channel_id=1, source_target_pairs={{0,1},{1,0},{2,3},{3,2},{4,8},{5,9},{6,10},{7,11},{8,4},{9,5},{10,... | collective-permute-start | bytes 1572872 | tf_op jit(solution)/shard_map/mid_next_0/ppermute | solution.py:240
  24.5 15.6 %collective-permute-start.7 = (bf16[32,32,256]{2,1,0:T(8,128)(2,1)S(1)}, bf16[32,32,256]{2,1,0:T(8,128)(2,1)S(1)}, u32[]{:S(2)}, u32[]{:S(2)}) collective-permute-start(bf16[32,32,256]{2,1,0:T(8,128)(2,1)S(1)} %get-tuple-element.74.rest_0_), channel_id=1, source_target_pairs={{0,4},{1,5},{2,6},{3,7},{4,0},{5,1},{6,2},{7,3},{8,12},{9,13},{10,... | collective-permute-start | bytes 1572872 | tf_op jit(solution)/shard_map/end_left_0/ppermute | solution.py:240
  28.9 5.2 %collective-permute-start.12 = (bf16[14,32,256]{2,1,0:T(8,128)(2,1)S(1)}, bf16[14,32,256]{2,1,0:T(8,128)(2,1)S(1)}, u32[]{:S(2)}, u32[]{:S(2)}) collective-permute-start(bf16[14,32,256]{2,1,0:T(8,128)(2,1)S(1)} %get-tuple-element.65), channel_id=1, source_target_pairs={{0,2},{1,3},{2,0},{3,1},{4,6},{5,7},{6,4},{7,5},{8,10},{9,11},{10,... | collective-permute-start | bytes 688136 | tf_op jit(solution)/shard_map/cross_right_1/ppermute | solution.py:240
  30.5 14.9 %collective-permute-start.11 = (bf16[18,32,256]{2,1,0:T(8,128)(2,1)S(1)}, bf16[18,32,256]{2,1,0:T(8,128)(2,1)S(1)}, u32[]{:S(2)}, u32[]{:S(2)}) collective-permute-start(bf16[18,32,256]{2,1,0:T(8,128)(2,1)S(1)} %collective-permute-done.5.rest_5_), channel_id=1, source_target_pairs={{0,1},{1,0},{2,3},{3,2},{4,8},{5,9},{6,10},{7,11},{8,4},{9,5},{10,... | collective-permute-start | bytes 884744 | tf_op jit(solution)/shard_map/mid_next_10/ppermute | solution.py:240
  32.8 13.6 %collective-permute-start.8 = (bf16[18,32,256]{2,1,0:T(8,128)(2,1)S(1)}, bf16[18,32,256]{2,1,0:T(8,128)(2,1)S(1)}, u32[]{:S(2)}, u32[]{:S(2)}) collective-permute-start(bf16[18,32,256]{2,1,0:T(8,128)(2,1)S(1)} %collective-permute-done.4.rest_1_), channel_id=1, source_target_pairs={{0,4},{1,5},{2,6},{3,7},{4,0},{5,1},{6,2},{7,3},{8,12},{9,13},{10,... | collective-permute-start | bytes 884744 | tf_op jit(solution)/shard_map/end_left_10/ppermute | solution.py:240
  34.0 12.4 %collective-permute-start.13 = (bf16[14,32,256]{2,1,0:T(8,128)(2,1)S(1)}, bf16[14,32,256]{2,1,0:T(8,128)(2,1)S(1)}, u32[]{:S(2)}, u32[]{:S(2)}) collective-permute-start(bf16[14,32,256]{2,1,0:T(8,128)(2,1)S(1)} %get-tuple-element.66), channel_id=1, source_target_pairs={{0,2},{1,3},{2,0},{3,1},{4,6},{5,7},{6,4},{7,5},{8,10},{9,11},{10,... | collective-permute-start | bytes 688136 | tf_op jit(solution)/shard_map/cross_left_1/ppermute | solution.py:240
  40.1 11.2 %collective-permute-start.18 = (bf16[14,32,256]{2,1,0:T(8,128)(2,1)S(1)}, bf16[14,32,256]{2,1,0:T(8,128)(2,1)S(1)}, u32[]{:S(2)}, u32[]{:S(2)}) collective-permute-start(bf16[14,32,256]{2,1,0:T(8,128)(2,1)S(1)} %collective-permute-done.12.rest_3_), channel_id=1, source_target_pairs={{0,4},{1,5},{2,6},{3,7},{4,0},{5,1},{6,2},{7,3},{8,12},{9,13},{10,... | collective-permute-start | bytes 688136 | tf_op jit(solution)/shard_map/end_right_11/ppermute | solution.py:240
  42.1 9.2 %collective-permute-start.19 = (bf16[14,32,256]{2,1,0:T(8,128)(2,1)S(1)}, bf16[14,32,256]{2,1,0:T(8,128)(2,1)S(1)}, u32[]{:S(2)}, u32[]{:S(2)}) collective-permute-start(bf16[14,32,256]{2,1,0:T(8,128)(2,1)S(1)} %collective-permute-done.12.rest_3_), channel_id=1, source_target_pairs={{0,1},{1,0},{2,3},{3,2},{4,8},{5,9},{6,10},{7,11},{8,4},{9,5},{10,... | collective-permute-start | bytes 688136 | tf_op jit(solution)/shard_map/mid_own_11/ppermute | solution.py:240
  47.0 10.6 %collective-permute-start.14 = (bf16[18,32,256]{2,1,0:T(8,128)(2,1)S(1)}, bf16[18,32,256]{2,1,0:T(8,128)(2,1)S(1)}, u32[]{:S(2)}, u32[]{:S(2)}) collective-permute-start(bf16[18,32,256]{2,1,0:T(8,128)(2,1)S(1)} %get-tuple-element.68), channel_id=1, source_target_pairs={{0,4},{1,5},{2,6},{3,7},{4,0},{5,1},{6,2},{7,3},{8,12},{9,13},{10,... | collective-permute-start | bytes 884744 | tf_op jit(solution)/shard_map/left_11_and_products_back_0/ppermute | solution.py:240
  51.3 6.4 %collective-permute-start.20 = (bf16[14,32,256]{2,1,0:T(8,128)(2,1)S(1)}, bf16[14,32,256]{2,1,0:T(8,128)(2,1)S(1)}, u32[]{:S(2)}, u32[]{:S(2)}) collective-permute-start(bf16[14,32,256]{2,1,0:T(8,128)(2,1)S(1)} %collective-permute-done.18.rest_5_), channel_id=1, source_target_pairs={{0,1},{1,0},{2,3},{3,2},{4,8},{5,9},{6,10},{7,11},{8,4},{9,5},{10,... | collective-permute-start | bytes 688136 | tf_op jit(solution)/shard_map/mid_next_11/ppermute | solution.py:240
  57.7 17.0 %copy-start.3 = (bf16[128,128]{1,0:T(8,128)(2,1)S(1)}, bf16[128,128]{1,0:T(8,128)(2,1)}, u32[]{:S(2)}) copy-start(bf16[128,128]{1,0:T(8,128)(2,1)} %weight.5) | copy-start | bytes 98308
  57.8 17.0 %copy-start.6 = (f32[128]{0:T(128)S(1)}, f32[128]{0:T(128)}, u32[]{:S(2)}) copy-start(f32[128]{0:T(128)} %param.12) | copy-start | bytes 1540
  58.3 6.0 %collective-permute-start.21 = (bf16[14,32,256]{2,1,0:T(8,128)(2,1)S(1)}, bf16[14,32,256]{2,1,0:T(8,128)(2,1)S(1)}, u32[]{:S(2)}, u32[]{:S(2)}) collective-permute-start(bf16[14,32,256]{2,1,0:T(8,128)(2,1)S(1)} %get-tuple-element.78), channel_id=1, source_target_pairs={{0,4},{1,5},{2,6},{3,7},{4,0},{5,1},{6,2},{7,3},{8,12},{9,13},{10,... | collective-permute-start | bytes 688136 | tf_op jit(solution)/shard_map/products_back_1/ppermute | solution.py:240
  58.4 9.4 %collective-permute-start.15 = (bf16[18,32,128]{2,1,0:T(8,128)(2,1)S(1)}, bf16[18,32,128]{2,1,0:T(8,128)(2,1)S(1)}, u32[]{:S(2)}, u32[]{:S(2)}) collective-permute-start(bf16[18,32,128]{2,1,0:T(8,128)(2,1)S(1)} %get-tuple-element.70), channel_id=1, source_target_pairs={{0,1},{1,0},{2,3},{3,2},{4,5},{5,4},{6,7},{7,6},{8,9},{9,8},{10,11... | collective-permute-start | bytes 442376 | tf_op jit(solution)/shard_map/return_01/ppermute | solution.py:240
  61.1 7.1 %collective-permute-start.16 = (bf16[18,32,128]{2,1,0:T(8,128)(2,1)S(1)}, bf16[18,32,128]{2,1,0:T(8,128)(2,1)S(1)}, u32[]{:S(2)}, u32[]{:S(2)}) collective-permute-start(bf16[18,32,128]{2,1,0:T(8,128)(2,1)S(1)} %get-tuple-element.71), channel_id=1, source_target_pairs={{0,2},{1,3},{2,0},{3,1},{4,6},{5,7},{6,4},{7,5},{8,10},{9,11},{10,... | collective-permute-start | bytes 442376 | tf_op jit(solution)/shard_map/return_02/ppermute | solution.py:240
  62.4 7.9 %collective-permute-start.17 = (bf16[18,32,128]{2,1,0:T(8,128)(2,1)S(1)}, bf16[18,32,128]{2,1,0:T(8,128)(2,1)S(1)}, u32[]{:S(2)}, u32[]{:S(2)}) collective-permute-start(bf16[18,32,128]{2,1,0:T(8,128)(2,1)S(1)} %get-tuple-element.72), channel_id=1, source_target_pairs={{0,3},{1,2},{2,1},{3,0},{4,7},{5,6},{6,5},{7,4},{8,11},{9,10},{10,... | collective-permute-start | bytes 442376 | tf_op jit(solution)/shard_map/return_03/ppermute | solution.py:240
  64.3 5.9 %collective-permute-start.22 = (bf16[14,32,128]{2,1,0:T(8,128)(2,1)S(1)}, bf16[14,32,128]{2,1,0:T(8,128)(2,1)S(1)}, u32[]{:S(2)}, u32[]{:S(2)}) collective-permute-start(bf16[14,32,128]{2,1,0:T(8,128)(2,1)S(1)} %get-tuple-element.80), channel_id=1, source_target_pairs={{0,1},{1,0},{2,3},{3,2},{4,5},{5,4},{6,7},{7,6},{8,9},{9,8},{10,11... | collective-permute-start | bytes 344072 | tf_op jit(solution)/shard_map/return_11/ppermute | solution.py:240
  66.5 5.7 %collective-permute-start.23 = (bf16[14,32,128]{2,1,0:T(8,128)(2,1)S(1)}, bf16[14,32,128]{2,1,0:T(8,128)(2,1)S(1)}, u32[]{:S(2)}, u32[]{:S(2)}) collective-permute-start(bf16[14,32,128]{2,1,0:T(8,128)(2,1)S(1)} %get-tuple-element.81), channel_id=1, source_target_pairs={{0,2},{1,3},{2,0},{3,1},{4,6},{5,7},{6,4},{7,5},{8,10},{9,11},{10,... | collective-permute-start | bytes 344072 | tf_op jit(solution)/shard_map/return_12/ppermute | solution.py:240
  67.8 7.0 %collective-permute-start.24 = (bf16[14,32,128]{2,1,0:T(8,128)(2,1)S(1)}, bf16[14,32,128]{2,1,0:T(8,128)(2,1)S(1)}, u32[]{:S(2)}, u32[]{:S(2)}) collective-permute-start(bf16[14,32,128]{2,1,0:T(8,128)(2,1)S(1)} %get-tuple-element.82), channel_id=1, source_target_pairs={{0,3},{1,2},{2,1},{3,0},{4,7},{5,6},{6,5},{7,4},{8,11},{9,10},{10,... | collective-permute-start | bytes 344072 | tf_op jit(solution)/shard_map/return_13/ppermute | solution.py:240

commit v24 on v22

--- a/solution.py
+++ b/solution.py
@@ -265,7 +265,7 @@
         return jax.ShapeDtypeStruct((count, height, depth), BF16)
 
     def columns(count):
-        return pltpu.VMEM((toks // LANES, count * (rows + 1), LANES), F32)
+        return pltpu.VMEM((toks // LANES, (count + 1) * (rows + 1), LANES), F32)
 
     rows_all = jax.ShapeDtypeStruct((rows * toks, channels), BF16)
     valid_shape = jax.ShapeDtypeStruct((1, rows, toks), F32)
@@ -378,7 +378,7 @@
         "update",
         jax.ShapeDtypeStruct((rows, toks, channels), BF16),
         [VMEM] * (3 + len(pieces)),
-        [pltpu.VMEM((toks // LANES, rows * (hidden + 1), LANES), F32)],
+        [pltpu.VMEM((toks // LANES, (rows + 1) * (hidden + 1), LANES), F32)],
     )(out_gain.reshape(1, -1), out_weight, gate, *pieces)
 
 

time: 77.4 us -> 77.3 us (level)
  no operation moved by 1% of the time
where the time goes in v24:
time: 77.3 us; the launch traced here: 76.9 us
  waiting for transfers between devices  32.7 us (42%)
  starting transfers between devices  30.7 us (40%)
  Pallas kernels  9.72 us (13%)
  local copies, waits for them, and re-layouts  3.52 us (5%)
    ppermute x25, waiting for transfers between devices, send(): return lax.ppermute(x, ('row', 'chan'), pairs)  32.7 us
    ppermute x25, starting transfers between devices, send(): return lax.ppermute(x, ('row', 'chan'), pairs)  30.7 us
    pallas_call x12, Pallas kernels, call(): pl.pallas_call(body, out_shape=out_shape, in_specs=in_specs, out_specs=ou...  9.72 us
    unnamed x14, local copies, waits for them, and re-layouts  3.52 us
  transfers between devices with their start and end apart: 25, of which 12 were waited for; matrix products, arithmetic and copies ran while one was open for 0% of the time, Pallas kernels for 7%

profile of v24, /device:TPU:1, one launch (start us, length us, event | category | flops | bytes accessed | tf_op | source)
XLA Modules:
  0.0 76.9 jit_solution(11465829352306707361)
XLA Ops:
  0.0 0.1 collective-permute-start
  0.1 0.5 collective-permute-start.1
  0.5 1.2 %copy-done = bf16[32,128,128]{2,1,0:T(8,128)(2,1)S(1)} copy-done((bf16[32,128,128]{2,1,0:T(8,128)(2,1)S(1)}, bf16[32,128,128]{2,1,0:T(8,128)(2,1)}, u32[]{:S(2)}) %copy-start) | copy-done | bytes 1048600
  1.7 0.9 %copy-done.1 = bf16[128,512]{1,0:T(8,128)(2,1)S(1)} copy-done((bf16[128,512]{1,0:T(8,128)(2,1)S(1)}, bf16[128,512]{1,0:T(8,128)(2,1)}, u32[]{:S(2)}) %copy-start.1) | copy-done | bytes 131096
  2.6 0.7 copy-done.4
  3.4 0.7 copy-done.5
  4.0 1.5 %right_own.1 = (bf16[32,32,128]{2,1,0:T(8,128)(2,1)S(1)}, bf16[4096,128]{1,0:T(8,128)(2,1)S(1)}, bf16[64,128]{1,0:T(8,128)(2,1)S(1)}, bf16[64,128]{1,0:T(8,128)(...) custom-call(bf16[32,128,128]{2,1,0:T(8,128)(2,1)S(1)} %copy-done, ...), custom_call_target="tpu_custom_call" | custom-call | tf_op jit(solution)/shard_map/right_own/pallas_call | solution.py:212
  5.5 0.0 collective-permute-done.1.mask
  5.5 0.0 collective-permute-done.pair
  5.5 1.6 %right_twin.1 = (bf16[32,32,256]{2,1,0:T(8,128)(2,1)S(1)}, bf16[4096,128]{1,0:T(8,128)(2,1)S(1)}, f32[1,32,128]{2,1,0:T(8,128)S(1)}) custom-call(bf16[32,128,128]{2,1,0:T(8,128)(2,1)S(1)} %collective-permute-done.pair, s32[32,128]{1,0:T(8,128)S(1)} %collective-permute-done.1.mask, f32[1,128]{1,0:T(1,128)S(1)} %get-tuple-element.45.gain, ...), custom_call_target="tpu_custom_call" | custom-call | tf_op jit(solution)/shard_map/right_twin/pallas_call | solution.py:212
  7.1 2.4 %collective-permute-start.3 = (bf16[32,32,256]{2,1,0:T(8,128)(2,1)S(1)}, bf16[32,32,256]{2,1,0:T(8,128)(2,1)S(1)}, u32[]{:S(2)}, u32[]{:S(2)}) collective-permute-start(bf16[32,32,256]{2,1,0:T(8,128)(2,1)S(1)} %get-tuple-element.56.rest_2_), channel_id=1, source_target_pairs={{0,4},{1,5},{2,6},{3,7},{4,0},{5,1},{6,2},{7,3},{8,12},{9,13},{10,... | collective-permute-start | bytes 1572872 | tf_op jit(solution)/shard_map/end_right_0/ppermute | solution.py:240
  9.5 0.8 %collective-permute-start.6 = (bf16[32,32,256]{2,1,0:T(8,128)(2,1)S(1)}, bf16[32,32,256]{2,1,0:T(8,128)(2,1)S(1)}, u32[]{:S(2)}, u32[]{:S(2)}) collective-permute-start(bf16[32,32,256]{2,1,0:T(8,128)(2,1)S(1)} %get-tuple-element.56.rest_2_), channel_id=1, source_target_pairs={{0,1},{1,0},{2,3},{3,2},{4,8},{5,9},{6,10},{7,11},{8,4},{9,5},{10,... | collective-permute-start | bytes 1572872 | tf_op jit(solution)/shard_map/mid_own_0/ppermute | solution.py:240
  10.3 0.9 %right_neighbour.1 = (bf16[18,32,256]{2,1,0:T(8,128)(2,1)S(1)}, bf16[14,32,256]{2,1,0:T(8,128)(2,1)S(1)}) custom-call(bf16[4096,128]{1,0:T(8,128)(2,1)S(1)} %get-tuple-element.44.normed.normed0, bf16[4096,128]{1,0:T(8,128)(2,1)S(1)} %get-tuple-element.48.normed1, f32[1,32,128]{2,1,0:T(8,128)S(1)} %get-tuple-element.49.valid0, ...), custom_call_target="tpu_custom_call" | custom-call | tf_op jit(solution)/shard_map/right_neighbour/pallas_call | solution.py:212
  11.2 1.3 %collective-permute-start.2 = (bf16[18,32,256]{2,1,0:T(8,128)(2,1)S(1)}, bf16[18,32,256]{2,1,0:T(8,128)(2,1)S(1)}, u32[]{:S(2)}, u32[]{:S(2)}) collective-permute-start(bf16[18,32,256]{2,1,0:T(8,128)(2,1)S(1)} %get-tuple-element.55), channel_id=1, source_target_pairs={{0,2},{1,3},{2,0},{3,1},{4,6},{5,7},{6,4},{7,5},{8,10},{9,11},{10,... | collective-permute-start | bytes 884744 | tf_op jit(solution)/shard_map/cross_right_0/ppermute | solution.py:240
  12.5 0.9 %left.1 = (bf16[32,32,256]{2,1,0:T(8,128)(2,1)S(1)}, bf16[18,32,256]{2,1,0:T(8,128)(2,1)S(1)}, bf16[14,32,256]{2,1,0:T(8,128)(2,1)S(1)}) custom-call(bf16[4096,128]{1,0:T(8,128)(2,1)S(1)} %get-tuple-element.44.normed.normed0, bf16[4096,128]{1,0:T(8,128)(2,1)S(1)} %get-tuple-element.48.normed1, f32[1,32,128]{2,1,0:T(8,128)S(1)} %get-tuple-element.49.valid0, ...), custom_call_target="tpu_custom_call" | custom-call | tf_op jit(solution)/shard_map/left/pallas_call | solution.py:212
  13.4 6.5 %collective-permute-done.2.rest_3_ = bf16[18,32,256]{2,1,0:T(8,128)(2,1)S(1)} collective-permute-done((bf16[18,32,256]{2,1,0:T(8,128)(2,1)S(1)}, bf16[18,32,256]{2,1,0:T(8,128)(2,1)S(1)}, u32[]{:S(2)}, u32[]{:S(2)}) %collective-permute-start.2) | collective-permute-done | bytes 294944 | tf_op jit(solution)/shard_map/cross_right_0/ppermute | solution.py:240
  19.9 0.8 %collective-permute-start.9 = (bf16[18,32,256]{2,1,0:T(8,128)(2,1)S(1)}, bf16[18,32,256]{2,1,0:T(8,128)(2,1)S(1)}, u32[]{:S(2)}, u32[]{:S(2)}) collective-permute-start(bf16[18,32,256]{2,1,0:T(8,128)(2,1)S(1)} %collective-permute-done.2.rest_3_), channel_id=1, source_target_pairs={{0,1},{1,0},{2,3},{3,2},{4,8},{5,9},{6,10},{7,11},{8,4},{9,5},{10,... | collective-permute-start | bytes 884744 | tf_op jit(solution)/shard_map/mid_own_10/ppermute | solution.py:240
  20.7 0.1 collective-permute-start.5
  20.8 0.5 collective-permute-done.3.rest_4_
  21.3 1.1 %collective-permute-start.4 = (bf16[18,32,256]{2,1,0:T(8,128)(2,1)S(1)}, bf16[18,32,256]{2,1,0:T(8,128)(2,1)S(1)}, u32[]{:S(2)}, u32[]{:S(2)}) collective-permute-start(bf16[18,32,256]{2,1,0:T(8,128)(2,1)S(1)} %get-tuple-element.57), channel_id=1, source_target_pairs={{0,2},{1,3},{2,0},{3,1},{4,6},{5,7},{6,4},{7,5},{8,10},{9,11},{10,... | collective-permute-start | bytes 884744 | tf_op jit(solution)/shard_map/cross_left_0/ppermute | solution.py:240
  22.4 0.0 collective-permute-done.6.rest_4_
  22.4 2.2 %collective-permute-start.10 = (bf16[32,32,256]{2,1,0:T(8,128)(2,1)S(1)}, bf16[32,32,256]{2,1,0:T(8,128)(2,1)S(1)}, u32[]{:S(2)}, u32[]{:S(2)}) collective-permute-start(bf16[32,32,256]{2,1,0:T(8,128)(2,1)S(1)} %collective-permute-done.3.rest_4_), channel_id=1, source_target_pairs={{0,1},{1,0},{2,3},{3,2},{4,8},{5,9},{6,10},{7,11},{8,4},{9,5},{10,... | collective-permute-start | bytes 1572872 | tf_op jit(solution)/shard_map/mid_next_0/ppermute | solution.py:240
  24.6 0.4 collective-permute-start.7
  25.0 0.0 collective-permute-done.9.rest_5_
  25.0 3.9 %collective-permute-done.5.rest_5_ = bf16[18,32,256]{2,1,0:T(8,128)(2,1)S(1)} collective-permute-done((bf16[18,32,256]{2,1,0:T(8,128)(2,1)S(1)}, bf16[18,32,256]{2,1,0:T(8,128)(2,1)S(1)}, u32[]{:S(2)}, u32[]{:S(2)}) %collective-permute-start.5) | collective-permute-done | bytes 294944 | tf_op jit(solution)/shard_map/end_right_10/ppermute | solution.py:240
  28.9 0.0 collective-permute-done.4.rest_1_
  28.9 1.2 %collective-permute-start.12 = (bf16[14,32,256]{2,1,0:T(8,128)(2,1)S(1)}, bf16[14,32,256]{2,1,0:T(8,128)(2,1)S(1)}, u32[]{:S(2)}, u32[]{:S(2)}) collective-permute-start(bf16[14,32,256]{2,1,0:T(8,128)(2,1)S(1)} %get-tuple-element.65), channel_id=1, source_target_pairs={{0,2},{1,3},{2,0},{3,1},{4,6},{5,7},{6,4},{7,5},{8,10},{9,11},{10,... | collective-permute-start | bytes 688136 | tf_op jit(solution)/shard_map/cross_right_1/ppermute | solution.py:240
  30.2 0.4 gate.1
  30.6 2.3 %collective-permute-start.11 = (bf16[18,32,256]{2,1,0:T(8,128)(2,1)S(1)}, bf16[18,32,256]{2,1,0:T(8,128)(2,1)S(1)}, u32[]{:S(2)}, u32[]{:S(2)}) collective-permute-start(bf16[18,32,256]{2,1,0:T(8,128)(2,1)S(1)} %collective-permute-done.5.rest_5_), channel_id=1, source_target_pairs={{0,1},{1,0},{2,3},{3,2},{4,8},{5,9},{6,10},{7,11},{8,4},{9,5},{10,... | collective-permute-start | bytes 884744 | tf_op jit(solution)/shard_map/mid_next_10/ppermute | solution.py:240
  32.9 0.0 collective-permute-start.8
  32.9 1.2 %collective-permute-done.12.rest_3_ = bf16[14,32,256]{2,1,0:T(8,128)(2,1)S(1)} collective-permute-done((bf16[14,32,256]{2,1,0:T(8,128)(2,1)S(1)}, bf16[14,32,256]{2,1,0:T(8,128)(2,1)S(1)}, u32[]{:S(2)}, u32[]{:S(2)}) %collective-permute-start.12) | collective-permute-done | bytes 229408 | tf_op jit(solution)/shard_map/cross_right_1/ppermute | solution.py:240
  34.1 1.2 %collective-permute-start.13 = (bf16[14,32,256]{2,1,0:T(8,128)(2,1)S(1)}, bf16[14,32,256]{2,1,0:T(8,128)(2,1)S(1)}, u32[]{:S(2)}, u32[]{:S(2)}) collective-permute-start(bf16[14,32,256]{2,1,0:T(8,128)(2,1)S(1)} %get-tuple-element.66), channel_id=1, source_target_pairs={{0,2},{1,3},{2,0},{3,1},{4,6},{5,7},{6,4},{7,5},{8,10},{9,11},{10,... | collective-permute-start | bytes 688136 | tf_op jit(solution)/shard_map/cross_left_1/ppermute | solution.py:240
  35.4 4.8 %collective-permute-done.7.rest_2_ = bf16[32,32,256]{2,1,0:T(8,128)(2,1)S(1)} collective-permute-done((bf16[32,32,256]{2,1,0:T(8,128)(2,1)S(1)}, bf16[32,32,256]{2,1,0:T(8,128)(2,1)S(1)}, u32[]{:S(2)}, u32[]{:S(2)}) %collective-permute-start.7) | collective-permute-done | bytes 524320 | tf_op jit(solution)/shard_map/end_left_0/ppermute | solution.py:240
  40.2 2.0 %collective-permute-start.18 = (bf16[14,32,256]{2,1,0:T(8,128)(2,1)S(1)}, bf16[14,32,256]{2,1,0:T(8,128)(2,1)S(1)}, u32[]{:S(2)}, u32[]{:S(2)}) collective-permute-start(bf16[14,32,256]{2,1,0:T(8,128)(2,1)S(1)} %collective-permute-done.12.rest_3_), channel_id=1, source_target_pairs={{0,4},{1,5},{2,6},{3,7},{4,0},{5,1},{6,2},{7,3},{8,12},{9,13},{10,... | collective-permute-start | bytes 688136 | tf_op jit(solution)/shard_map/end_right_11/ppermute | solution.py:240
  42.2 3.3 %collective-permute-start.19 = (bf16[14,32,256]{2,1,0:T(8,128)(2,1)S(1)}, bf16[14,32,256]{2,1,0:T(8,128)(2,1)S(1)}, u32[]{:S(2)}, u32[]{:S(2)}) collective-permute-start(bf16[14,32,256]{2,1,0:T(8,128)(2,1)S(1)} %collective-permute-done.12.rest_3_), channel_id=1, source_target_pairs={{0,1},{1,0},{2,3},{3,2},{4,8},{5,9},{6,10},{7,11},{8,4},{9,5},{10,... | collective-permute-start | bytes 688136 | tf_op jit(solution)/shard_map/mid_own_11/ppermute | solution.py:240
  45.5 0.0 collective-permute-done.11.rest_7_
  45.5 1.0 %collective-permute-done.8.rest_3_ = bf16[18,32,256]{2,1,0:T(8,128)(2,1)S(1)} collective-permute-done((bf16[18,32,256]{2,1,0:T(8,128)(2,1)S(1)}, bf16[18,32,256]{2,1,0:T(8,128)(2,1)S(1)}, u32[]{:S(2)}, u32[]{:S(2)}) %collective-permute-start.8) | collective-permute-done | bytes 294944 | tf_op jit(solution)/shard_map/end_left_10/ppermute | solution.py:240
  46.5 0.0 collective-permute-done.13.rest_8_.rest_1_
  46.5 0.6 away.2
  47.1 0.9 %collective-permute-start.14 = (bf16[18,32,256]{2,1,0:T(8,128)(2,1)S(1)}, bf16[18,32,256]{2,1,0:T(8,128)(2,1)S(1)}, u32[]{:S(2)}, u32[]{:S(2)}) collective-permute-start(bf16[18,32,256]{2,1,0:T(8,128)(2,1)S(1)} %get-tuple-element.68), channel_id=1, source_target_pairs={{0,4},{1,5},{2,6},{3,7},{4,0},{5,1},{6,2},{7,3},{8,12},{9,13},{10,... | collective-permute-start | bytes 884744 | tf_op jit(solution)/shard_map/left_11_and_products_back_0/ppermute | solution.py:240
  47.9 3.5 %collective-permute-done.18.rest_5_ = bf16[14,32,256]{2,1,0:T(8,128)(2,1)S(1)} collective-permute-done((bf16[14,32,256]{2,1,0:T(8,128)(2,1)S(1)}, bf16[14,32,256]{2,1,0:T(8,128)(2,1)S(1)}, u32[]{:S(2)}, u32[]{:S(2)}) %collective-permute-start.18) | collective-permute-done | bytes 229408 | tf_op jit(solution)/shard_map/end_right_11/ppermute | solution.py:240
  51.4 1.9 %collective-permute-start.20 = (bf16[14,32,256]{2,1,0:T(8,128)(2,1)S(1)}, bf16[14,32,256]{2,1,0:T(8,128)(2,1)S(1)}, u32[]{:S(2)}, u32[]{:S(2)}) collective-permute-start(bf16[14,32,256]{2,1,0:T(8,128)(2,1)S(1)} %collective-permute-done.18.rest_5_), channel_id=1, source_target_pairs={{0,1},{1,0},{2,3},{3,2},{4,8},{5,9},{6,10},{7,11},{8,4},{9,5},{10,... | collective-permute-start | bytes 688136 | tf_op jit(solution)/shard_map/mid_next_11/ppermute | solution.py:240
  53.4 0.6 near.2
  54.0 0.5 near.3
  54.5 3.2 %collective-permute-done.14.end.rest_3_ = bf16[18,32,256]{2,1,0:T(8,128)(2,1)S(1)} collective-permute-done((bf16[18,32,256]{2,1,0:T(8,128)(2,1)S(1)}, bf16[18,32,256]{2,1,0:T(8,128)(2,1)S(1)}, u32[]{:S(2)}, u32[]{:S(2)}) %collective-permute-start.14) | collective-permute-done | bytes 294944 | tf_op jit(solution)/shard_map/left_11_and_products_back_0/ppermute | solution.py:240
  57.7 0.1 hand_out.2
  57.8 0.0 copy-start.3
  57.8 0.0 copy-start.6
  57.9 0.5 away.3
  58.4 0.1 collective-permute-start.21
  58.4 2.7 %collective-permute-start.15 = (bf16[18,32,128]{2,1,0:T(8,128)(2,1)S(1)}, bf16[18,32,128]{2,1,0:T(8,128)(2,1)S(1)}, u32[]{:S(2)}, u32[]{:S(2)}) collective-permute-start(bf16[18,32,128]{2,1,0:T(8,128)(2,1)S(1)} %get-tuple-element.70), channel_id=1, source_target_pairs={{0,1},{1,0},{2,3},{3,2},{4,5},{5,4},{6,7},{7,6},{8,9},{9,8},{10,11... | collective-permute-start | bytes 442376 | tf_op jit(solution)/shard_map/return_01/ppermute | solution.py:240
  61.2 1.2 %collective-permute-start.16 = (bf16[18,32,128]{2,1,0:T(8,128)(2,1)S(1)}, bf16[18,32,128]{2,1,0:T(8,128)(2,1)S(1)}, u32[]{:S(2)}, u32[]{:S(2)}) collective-permute-start(bf16[18,32,128]{2,1,0:T(8,128)(2,1)S(1)} %get-tuple-element.71), channel_id=1, source_target_pairs={{0,2},{1,3},{2,0},{3,1},{4,6},{5,7},{6,4},{7,5},{8,10},{9,11},{10,... | collective-permute-start | bytes 442376 | tf_op jit(solution)/shard_map/return_02/ppermute | solution.py:240
  62.4 0.4 collective-permute-start.17
  62.8 1.5 %collective-permute-done.21.end = bf16[14,32,256]{2,1,0:T(8,128)(2,1)S(1)} collective-permute-done((bf16[14,32,256]{2,1,0:T(8,128)(2,1)S(1)}, bf16[14,32,256]{2,1,0:T(8,128)(2,1)S(1)}, u32[]{:S(2)}, u32[]{:S(2)}) %collective-permute-start.21) | collective-permute-done | bytes 229408 | tf_op jit(solution)/shard_map/products_back_1/ppermute | solution.py:240
  64.3 0.1 hand_out.3
  64.4 2.2 %collective-permute-start.22 = (bf16[14,32,128]{2,1,0:T(8,128)(2,1)S(1)}, bf16[14,32,128]{2,1,0:T(8,128)(2,1)S(1)}, u32[]{:S(2)}, u32[]{:S(2)}) collective-permute-start(bf16[14,32,128]{2,1,0:T(8,128)(2,1)S(1)} %get-tuple-element.80), channel_id=1, source_target_pairs={{0,1},{1,0},{2,3},{3,2},{4,5},{5,4},{6,7},{7,6},{8,9},{9,8},{10,11... | collective-permute-start | bytes 344072 | tf_op jit(solution)/shard_map/return_11/ppermute | solution.py:240
  66.6 1.3 %collective-permute-start.23 = (bf16[14,32,128]{2,1,0:T(8,128)(2,1)S(1)}, bf16[14,32,128]{2,1,0:T(8,128)(2,1)S(1)}, u32[]{:S(2)}, u32[]{:S(2)}) collective-permute-start(bf16[14,32,128]{2,1,0:T(8,128)(2,1)S(1)} %get-tuple-element.81), channel_id=1, source_target_pairs={{0,2},{1,3},{2,0},{3,1},{4,6},{5,7},{6,4},{7,5},{8,10},{9,11},{10,... | collective-permute-start | bytes 344072 | tf_op jit(solution)/shard_map/return_12/ppermute | solution.py:240
  67.9 0.5 collective-permute-start.24
  68.3 0.0 collective-permute-done.16.rest_2_
  68.3 2.0 %collective-permute-done.17.rest_3_ = bf16[18,32,128]{2,1,0:T(8,128)(2,1)S(1)} collective-permute-done((bf16[18,32,128]{2,1,0:T(8,128)(2,1)S(1)}, bf16[18,32,128]{2,1,0:T(8,128)(2,1)S(1)}, u32[]{:S(2)}, u32[]{:S(2)}) %collective-permute-start.17) | collective-permute-done | bytes 147488 | tf_op jit(solution)/shard_map/return_03/ppermute | solution.py:240
  70.3 0.0 collective-permute-done.22.rest_5_
  70.3 2.0 %collective-permute-done.23.rest_6_ = bf16[14,32,128]{2,1,0:T(8,128)(2,1)S(1)} collective-permute-done((bf16[14,32,128]{2,1,0:T(8,128)(2,1)S(1)}, bf16[14,32,128]{2,1,0:T(8,128)(2,1)S(1)}, u32[]{:S(2)}, u32[]{:S(2)}) %collective-permute-start.23) | collective-permute-done | bytes 114720 | tf_op jit(solution)/shard_map/return_12/ppermute | solution.py:240
  72.3 2.6 %collective-permute-done.24.rest_7_ = bf16[14,32,128]{2,1,0:T(8,128)(2,1)S(1)} collective-permute-done((bf16[14,32,128]{2,1,0:T(8,128)(2,1)S(1)}, bf16[14,32,128]{2,1,0:T(8,128)(2,1)S(1)}, u32[]{:S(2)}, u32[]{:S(2)}) %collective-permute-start.24) | collective-permute-done | bytes 114720 | tf_op jit(solution)/shard_map/return_13/ppermute | solution.py:240
  74.8 2.0 %update.1 = bf16[32,128,128]{2,1,0:T(8,128)(2,1)} custom-call(f32[1,128]{1,0:T(1,128)S(1)} %bitcast.3, bf16[128,128]{1,0:T(8,128)(2,1)S(1)} %copy-done.3, f32[32,128,128]{2,1,0:T(8,128)S(1)} %gate.1, bf16[18,32,128]{2,1,0:T(8,128)(2,1)S(1)} %get-tuple-element.69.rest_0_, bf16[18,32,128]{2,1,0:T(8,128)(2,1)S(1)} %collective-permute-done.15.rest_1_, ...), custom_call_target="tpu_custom_call" | custom-call | tf_op jit(solution)/shard_map/update/pallas_call | solution.py:212
  (12 shorter events, 0.0 us)
Async XLA Ops:
  0.0 5.5 %collective-permute-start = (bf16[32,128,128]{2,1,0:T(8,128)(2,1)}, bf16[32,128,128]{2,1,0:T(8,128)(2,1)S(1)}, u32[]{:S(2)}, u32[]{:S(2)}) collective-permute-start(bf16[32,128,128]{2,1,0:T(8,128)(2,1)} %pair.1), channel_id=1, source_target_pairs={{0,1},{1,0},{2,3},{3,2},{4,5},{5,4},{6,7},{7,6},{8,9},{9,8},{10,11... | collective-permute-start | bytes 3145736 | tf_op jit(solution)/shard_map/pair/ppermute | solution.py:240
  0.1 5.5 %collective-permute-start.1 = (s32[32,128]{1,0:T(8,128)}, s32[32,128]{1,0:T(8,128)S(1)}, u32[]{:S(2)}, u32[]{:S(2)}) collective-permute-start(s32[32,128]{1,0:T(8,128)} %mask.1), channel_id=1, source_target_pairs={{0,1},{1,0},{2,3},{3,2},{4,5},{5,4},{6,7},{7,6},{8,9},{9,8},{10,11... | collective-permute-start | bytes 49160 | tf_op jit(solution)/shard_map/mask/ppermute | solution.py:240
  0.5 1.2 %copy-start = (bf16[32,128,128]{2,1,0:T(8,128)(2,1)S(1)}, bf16[32,128,128]{2,1,0:T(8,128)(2,1)}, u32[]{:S(2)}) copy-start(bf16[32,128,128]{2,1,0:T(8,128)(2,1)} %pair.1) | copy-start | bytes 3145732
  1.7 0.9 %copy-start.1 = (bf16[128,512]{1,0:T(8,128)(2,1)S(1)}, bf16[128,512]{1,0:T(8,128)(2,1)}, u32[]{:S(2)}) copy-start(bf16[128,512]{1,0:T(8,128)(2,1)} %weight.3) | copy-start | bytes 393220
  2.6 0.7 copy-start.4
  3.4 0.7 copy-start.5
  7.1 14.2 %collective-permute-start.3 = (bf16[32,32,256]{2,1,0:T(8,128)(2,1)S(1)}, bf16[32,32,256]{2,1,0:T(8,128)(2,1)S(1)}, u32[]{:S(2)}, u32[]{:S(2)}) collective-permute-start(bf16[32,32,256]{2,1,0:T(8,128)(2,1)S(1)} %get-tuple-element.56.rest_2_), channel_id=1, source_target_pairs={{0,4},{1,5},{2,6},{3,7},{4,0},{5,1},{6,2},{7,3},{8,12},{9,13},{10,... | collective-permute-start | bytes 1572872 | tf_op jit(solution)/shard_map/end_right_0/ppermute | solution.py:240
  9.5 12.9 %collective-permute-start.6 = (bf16[32,32,256]{2,1,0:T(8,128)(2,1)S(1)}, bf16[32,32,256]{2,1,0:T(8,128)(2,1)S(1)}, u32[]{:S(2)}, u32[]{:S(2)}) collective-permute-start(bf16[32,32,256]{2,1,0:T(8,128)(2,1)S(1)} %get-tuple-element.56.rest_2_), channel_id=1, source_target_pairs={{0,1},{1,0},{2,3},{3,2},{4,8},{5,9},{6,10},{7,11},{8,4},{9,5},{10,... | collective-permute-start | bytes 1572872 | tf_op jit(solution)/shard_map/mid_own_0/ppermute | solution.py:240
  10.3 19.9 %copy-start.2 = (bf16[128,128]{1,0:T(8,128)(2,1)S(1)}, bf16[128,128]{1,0:T(8,128)(2,1)}, u32[]{:S(2)}) copy-start(bf16[128,128]{1,0:T(8,128)(2,1)} %weight.4) | copy-start | bytes 98308
  11.2 8.7 %collective-permute-start.2 = (bf16[18,32,256]{2,1,0:T(8,128)(2,1)S(1)}, bf16[18,32,256]{2,1,0:T(8,128)(2,1)S(1)}, u32[]{:S(2)}, u32[]{:S(2)}) collective-permute-start(bf16[18,32,256]{2,1,0:T(8,128)(2,1)S(1)} %get-tuple-element.55), channel_id=1, source_target_pairs={{0,2},{1,3},{2,0},{3,1},{4,6},{5,7},{6,4},{7,5},{8,10},{9,11},{10,... | collective-permute-start | bytes 884744 | tf_op jit(solution)/shard_map/cross_right_0/ppermute | solution.py:240
  19.9 5.1 %collective-permute-start.9 = (bf16[18,32,256]{2,1,0:T(8,128)(2,1)S(1)}, bf16[18,32,256]{2,1,0:T(8,128)(2,1)S(1)}, u32[]{:S(2)}, u32[]{:S(2)}) collective-permute-start(bf16[18,32,256]{2,1,0:T(8,128)(2,1)S(1)} %collective-permute-done.2.rest_3_), channel_id=1, source_target_pairs={{0,1},{1,0},{2,3},{3,2},{4,8},{5,9},{6,10},{7,11},{8,4},{9,5},{10,... | collective-permute-start | bytes 884744 | tf_op jit(solution)/shard_map/mid_own_10/ppermute | solution.py:240
  20.7 8.2 %collective-permute-start.5 = (bf16[18,32,256]{2,1,0:T(8,128)(2,1)S(1)}, bf16[18,32,256]{2,1,0:T(8,128)(2,1)S(1)}, u32[]{:S(2)}, u32[]{:S(2)}) collective-permute-start(bf16[18,32,256]{2,1,0:T(8,128)(2,1)S(1)} %collective-permute-done.2.rest_3_), channel_id=1, source_target_pairs={{0,4},{1,5},{2,6},{3,7},{4,0},{5,1},{6,2},{7,3},{8,12},{9,13},{10,... | collective-permute-start | bytes 884744 | tf_op jit(solution)/shard_map/end_right_10/ppermute | solution.py:240
  21.3 7.6 %collective-permute-start.4 = (bf16[18,32,256]{2,1,0:T(8,128)(2,1)S(1)}, bf16[18,32,256]{2,1,0:T(8,128)(2,1)S(1)}, u32[]{:S(2)}, u32[]{:S(2)}) collective-permute-start(bf16[18,32,256]{2,1,0:T(8,128)(2,1)S(1)} %get-tuple-element.57), channel_id=1, source_target_pairs={{0,2},{1,3},{2,0},{3,1},{4,6},{5,7},{6,4},{7,5},{8,10},{9,11},{10,... | collective-permute-start | bytes 884744 | tf_op jit(solution)/shard_map/cross_left_0/ppermute | solution.py:240
  22.4 11.7 %collective-permute-start.10 = (bf16[32,32,256]{2,1,0:T(8,128)(2,1)S(1)}, bf16[32,32,256]{2,1,0:T(8,128)(2,1)S(1)}, u32[]{:S(2)}, u32[]{:S(2)}) collective-permute-start(bf16[32,32,256]{2,1,0:T(8,128)(2,1)S(1)} %collective-permute-done.3.rest_4_), channel_id=1, source_target_pairs={{0,1},{1,0},{2,3},{3,2},{4,8},{5,9},{6,10},{7,11},{8,4},{9,5},{10,... | collective-permute-start | bytes 1572872 | tf_op jit(solution)/shard_map/mid_next_0/ppermute | solution.py:240
  24.6 15.6 %collective-permute-start.7 = (bf16[32,32,256]{2,1,0:T(8,128)(2,1)S(1)}, bf16[32,32,256]{2,1,0:T(8,128)(2,1)S(1)}, u32[]{:S(2)}, u32[]{:S(2)}) collective-permute-start(bf16[32,32,256]{2,1,0:T(8,128)(2,1)S(1)} %get-tuple-element.74.rest_0_), channel_id=1, source_target_pairs={{0,4},{1,5},{2,6},{3,7},{4,0},{5,1},{6,2},{7,3},{8,12},{9,13},{10,... | collective-permute-start | bytes 1572872 | tf_op jit(solution)/shard_map/end_left_0/ppermute | solution.py:240
  28.9 5.2 %collective-permute-start.12 = (bf16[14,32,256]{2,1,0:T(8,128)(2,1)S(1)}, bf16[14,32,256]{2,1,0:T(8,128)(2,1)S(1)}, u32[]{:S(2)}, u32[]{:S(2)}) collective-permute-start(bf16[14,32,256]{2,1,0:T(8,128)(2,1)S(1)} %get-tuple-element.65), channel_id=1, source_target_pairs={{0,2},{1,3},{2,0},{3,1},{4,6},{5,7},{6,4},{7,5},{8,10},{9,11},{10,... | collective-permute-start | bytes 688136 | tf_op jit(solution)/shard_map/cross_right_1/ppermute | solution.py:240
  30.6 14.9 %collective-permute-start.11 = (bf16[18,32,256]{2,1,0:T(8,128)(2,1)S(1)}, bf16[18,32,256]{2,1,0:T(8,128)(2,1)S(1)}, u32[]{:S(2)}, u32[]{:S(2)}) collective-permute-start(bf16[18,32,256]{2,1,0:T(8,128)(2,1)S(1)} %collective-permute-done.5.rest_5_), channel_id=1, source_target_pairs={{0,1},{1,0},{2,3},{3,2},{4,8},{5,9},{6,10},{7,11},{8,4},{9,5},{10,... | collective-permute-start | bytes 884744 | tf_op jit(solution)/shard_map/mid_next_10/ppermute | solution.py:240
  32.9 13.6 %collective-permute-start.8 = (bf16[18,32,256]{2,1,0:T(8,128)(2,1)S(1)}, bf16[18,32,256]{2,1,0:T(8,128)(2,1)S(1)}, u32[]{:S(2)}, u32[]{:S(2)}) collective-permute-start(bf16[18,32,256]{2,1,0:T(8,128)(2,1)S(1)} %collective-permute-done.4.rest_1_), channel_id=1, source_target_pairs={{0,4},{1,5},{2,6},{3,7},{4,0},{5,1},{6,2},{7,3},{8,12},{9,13},{10,... | collective-permute-start | bytes 884744 | tf_op jit(solution)/shard_map/end_left_10/ppermute | solution.py:240
  34.1 12.4 %collective-permute-start.13 = (bf16[14,32,256]{2,1,0:T(8,128)(2,1)S(1)}, bf16[14,32,256]{2,1,0:T(8,128)(2,1)S(1)}, u32[]{:S(2)}, u32[]{:S(2)}) collective-permute-start(bf16[14,32,256]{2,1,0:T(8,128)(2,1)S(1)} %get-tuple-element.66), channel_id=1, source_target_pairs={{0,2},{1,3},{2,0},{3,1},{4,6},{5,7},{6,4},{7,5},{8,10},{9,11},{10,... | collective-permute-start | bytes 688136 | tf_op jit(solution)/shard_map/cross_left_1/ppermute | solution.py:240
  40.2 11.2 %collective-permute-start.18 = (bf16[14,32,256]{2,1,0:T(8,128)(2,1)S(1)}, bf16[14,32,256]{2,1,0:T(8,128)(2,1)S(1)}, u32[]{:S(2)}, u32[]{:S(2)}) collective-permute-start(bf16[14,32,256]{2,1,0:T(8,128)(2,1)S(1)} %collective-permute-done.12.rest_3_), channel_id=1, source_target_pairs={{0,4},{1,5},{2,6},{3,7},{4,0},{5,1},{6,2},{7,3},{8,12},{9,13},{10,... | collective-permute-start | bytes 688136 | tf_op jit(solution)/shard_map/end_right_11/ppermute | solution.py:240
  42.2 9.2 %collective-permute-start.19 = (bf16[14,32,256]{2,1,0:T(8,128)(2,1)S(1)}, bf16[14,32,256]{2,1,0:T(8,128)(2,1)S(1)}, u32[]{:S(2)}, u32[]{:S(2)}) collective-permute-start(bf16[14,32,256]{2,1,0:T(8,128)(2,1)S(1)} %collective-permute-done.12.rest_3_), channel_id=1, source_target_pairs={{0,1},{1,0},{2,3},{3,2},{4,8},{5,9},{6,10},{7,11},{8,4},{9,5},{10,... | collective-permute-start | bytes 688136 | tf_op jit(solution)/shard_map/mid_own_11/ppermute | solution.py:240
  47.1 10.6 %collective-permute-start.14 = (bf16[18,32,256]{2,1,0:T(8,128)(2,1)S(1)}, bf16[18,32,256]{2,1,0:T(8,128)(2,1)S(1)}, u32[]{:S(2)}, u32[]{:S(2)}) collective-permute-start(bf16[18,32,256]{2,1,0:T(8,128)(2,1)S(1)} %get-tuple-element.68), channel_id=1, source_target_pairs={{0,4},{1,5},{2,6},{3,7},{4,0},{5,1},{6,2},{7,3},{8,12},{9,13},{10,... | collective-permute-start | bytes 884744 | tf_op jit(solution)/shard_map/left_11_and_products_back_0/ppermute | solution.py:240
  51.4 6.4 %collective-permute-start.20 = (bf16[14,32,256]{2,1,0:T(8,128)(2,1)S(1)}, bf16[14,32,256]{2,1,0:T(8,128)(2,1)S(1)}, u32[]{:S(2)}, u32[]{:S(2)}) collective-permute-start(bf16[14,32,256]{2,1,0:T(8,128)(2,1)S(1)} %collective-permute-done.18.rest_5_), channel_id=1, source_target_pairs={{0,1},{1,0},{2,3},{3,2},{4,8},{5,9},{6,10},{7,11},{8,4},{9,5},{10,... | collective-permute-start | bytes 688136 | tf_op jit(solution)/shard_map/mid_next_11/ppermute | solution.py:240
  57.8 17.0 %copy-start.3 = (bf16[128,128]{1,0:T(8,128)(2,1)S(1)}, bf16[128,128]{1,0:T(8,128)(2,1)}, u32[]{:S(2)}) copy-start(bf16[128,128]{1,0:T(8,128)(2,1)} %weight.5) | copy-start | bytes 98308
  57.8 17.0 %copy-start.6 = (f32[128]{0:T(128)S(1)}, f32[128]{0:T(128)}, u32[]{:S(2)}) copy-start(f32[128]{0:T(128)} %param.12) | copy-start | bytes 1540
  58.4 6.0 %collective-permute-start.21 = (bf16[14,32,256]{2,1,0:T(8,128)(2,1)S(1)}, bf16[14,32,256]{2,1,0:T(8,128)(2,1)S(1)}, u32[]{:S(2)}, u32[]{:S(2)}) collective-permute-start(bf16[14,32,256]{2,1,0:T(8,128)(2,1)S(1)} %get-tuple-element.78), channel_id=1, source_target_pairs={{0,4},{1,5},{2,6},{3,7},{4,0},{5,1},{6,2},{7,3},{8,12},{9,13},{10,... | collective-permute-start | bytes 688136 | tf_op jit(solution)/shard_map/products_back_1/ppermute | solution.py:240
  58.4 9.4 %collective-permute-start.15 = (bf16[18,32,128]{2,1,0:T(8,128)(2,1)S(1)}, bf16[18,32,128]{2,1,0:T(8,128)(2,1)S(1)}, u32[]{:S(2)}, u32[]{:S(2)}) collective-permute-start(bf16[18,32,128]{2,1,0:T(8,128)(2,1)S(1)} %get-tuple-element.70), channel_id=1, source_target_pairs={{0,1},{1,0},{2,3},{3,2},{4,5},{5,4},{6,7},{7,6},{8,9},{9,8},{10,11... | collective-permute-start | bytes 442376 | tf_op jit(solution)/shard_map/return_01/ppermute | solution.py:240
  61.2 7.2 %collective-permute-start.16 = (bf16[18,32,128]{2,1,0:T(8,128)(2,1)S(1)}, bf16[18,32,128]{2,1,0:T(8,128)(2,1)S(1)}, u32[]{:S(2)}, u32[]{:S(2)}) collective-permute-start(bf16[18,32,128]{2,1,0:T(8,128)(2,1)S(1)} %get-tuple-element.71), channel_id=1, source_target_pairs={{0,2},{1,3},{2,0},{3,1},{4,6},{5,7},{6,4},{7,5},{8,10},{9,11},{10,... | collective-permute-start | bytes 442376 | tf_op jit(solution)/shard_map/return_02/ppermute | solution.py:240
  62.4 7.9 %collective-permute-start.17 = (bf16[18,32,128]{2,1,0:T(8,128)(2,1)S(1)}, bf16[18,32,128]{2,1,0:T(8,128)(2,1)S(1)}, u32[]{:S(2)}, u32[]{:S(2)}) collective-permute-start(bf16[18,32,128]{2,1,0:T(8,128)(2,1)S(1)} %get-tuple-element.72), channel_id=1, source_target_pairs={{0,3},{1,2},{2,1},{3,0},{4,7},{5,6},{6,5},{7,4},{8,11},{9,10},{10,... | collective-permute-start | bytes 442376 | tf_op jit(solution)/shard_map/return_03/ppermute | solution.py:240
  64.4 5.9 %collective-permute-start.22 = (bf16[14,32,128]{2,1,0:T(8,128)(2,1)S(1)}, bf16[14,32,128]{2,1,0:T(8,128)(2,1)S(1)}, u32[]{:S(2)}, u32[]{:S(2)}) collective-permute-start(bf16[14,32,128]{2,1,0:T(8,128)(2,1)S(1)} %get-tuple-element.80), channel_id=1, source_target_pairs={{0,1},{1,0},{2,3},{3,2},{4,5},{5,4},{6,7},{7,6},{8,9},{9,8},{10,11... | collective-permute-start | bytes 344072 | tf_op jit(solution)/shard_map/return_11/ppermute | solution.py:240
  66.6 5.7 %collective-permute-start.23 = (bf16[14,32,128]{2,1,0:T(8,128)(2,1)S(1)}, bf16[14,32,128]{2,1,0:T(8,128)(2,1)S(1)}, u32[]{:S(2)}, u32[]{:S(2)}) collective-permute-start(bf16[14,32,128]{2,1,0:T(8,128)(2,1)S(1)} %get-tuple-element.81), channel_id=1, source_target_pairs={{0,2},{1,3},{2,0},{3,1},{4,6},{5,7},{6,4},{7,5},{8,10},{9,11},{10,... | collective-permute-start | bytes 344072 | tf_op jit(solution)/shard_map/return_12/ppermute | solution.py:240
  67.9 7.0 %collective-permute-start.24 = (bf16[14,32,128]{2,1,0:T(8,128)(2,1)S(1)}, bf16[14,32,128]{2,1,0:T(8,128)(2,1)S(1)}, u32[]{:S(2)}, u32[]{:S(2)}) collective-permute-start(bf16[14,32,128]{2,1,0:T(8,128)(2,1)S(1)} %get-tuple-element.82), channel_id=1, source_target_pairs={{0,3},{1,2},{2,1},{3,0},{4,7},{5,6},{6,5},{7,4},{8,11},{9,10},{10,... | collective-permute-start | bytes 344072 | tf_op jit(solution)/shard_map/return_13/ppermute | solution.py:240

commit v25 on v24

--- a/solution.py
+++ b/solution.py
@@ -319,7 +319,7 @@
     right1[0] = after(crossed, left0)
     own1 = [mid("own_10", right1[0])]
     near1 = [end_right("10", right1[0])]
-    left1[0] = cross("left_0", left1[0], crossed, near0[-1])
+    left1[0] = cross("left_0", left1[0], crossed, own0)
     next0 = [mid("next_0", x, own0) for x in near0]
     outer0 = end_left("0", left0, own0)
     right1[1] = cross("right_1", right1[1], left1[0], own1[0], near1[0][-1])

time: 77.3 us -> 78.8 us (1.019)
  starting transfers between devices: 30.7 us -> 32.5 us
    ppermute x25, starting transfers between devices: 30.7 us -> 32.5 us  [send(): return lax.ppermute(x, ('row', 'chan'), pairs)]
  transfers between devices with their start and end apart: 25 -> 25, of which waited for: 12 -> 11; matrix products, arithmetic and copies ran while one was open for 0% -> 0% of each run, Pallas kernels for 7% -> 7%
where the time goes in v25:
time: 78.8 us; the launch traced here: 78.3 us
  starting transfers between devices  32.5 us (41%)
  waiting for transfers between devices  32.4 us (41%)
  Pallas kernels  9.74 us (12%)
  local copies, waits for them, and re-layouts  3.52 us (4%)
    ppermute x25, starting transfers between devices, send(): return lax.ppermute(x, ('row', 'chan'), pairs)  32.5 us
    ppermute x25, waiting for transfers between devices, send(): return lax.ppermute(x, ('row', 'chan'), pairs)  32.4 us
    pallas_call x12, Pallas kernels, call(): pl.pallas_call(body, out_shape=out_shape, in_specs=in_specs, out_specs=ou...  9.74 us
    unnamed x14, local copies, waits for them, and re-layouts  3.52 us
  transfers between devices with their start and end apart: 25, of which 11 were waited for; matrix products, arithmetic and copies ran while one was open for 0% of the time, Pallas kernels for 7%

profile of v25, /device:TPU:1, one launch (start us, length us, event | category | flops | bytes accessed | tf_op | source)
XLA Modules:
  0.0 78.3 jit_solution(14464725031107729456)
XLA Ops:
  0.0 0.1 collective-permute-start
  0.1 0.5 collective-permute-start.1
  0.5 1.2 %copy-done = bf16[32,128,128]{2,1,0:T(8,128)(2,1)S(1)} copy-done((bf16[32,128,128]{2,1,0:T(8,128)(2,1)S(1)}, bf16[32,128,128]{2,1,0:T(8,128)(2,1)}, u32[]{:S(2)}) %copy-start) | copy-done | bytes 1048600
  1.7 0.9 %copy-done.1 = bf16[128,512]{1,0:T(8,128)(2,1)S(1)} copy-done((bf16[128,512]{1,0:T(8,128)(2,1)S(1)}, bf16[128,512]{1,0:T(8,128)(2,1)}, u32[]{:S(2)}) %copy-start.1) | copy-done | bytes 131096
  2.6 0.7 copy-done.4
  3.4 0.7 copy-done.5
  4.0 1.5 %right_own.1 = (bf16[32,32,128]{2,1,0:T(8,128)(2,1)S(1)}, bf16[4096,128]{1,0:T(8,128)(2,1)S(1)}, bf16[64,128]{1,0:T(8,128)(2,1)S(1)}, bf16[64,128]{1,0:T(8,128)(...) custom-call(bf16[32,128,128]{2,1,0:T(8,128)(2,1)S(1)} %copy-done, ...), custom_call_target="tpu_custom_call" | custom-call | tf_op jit(solution)/shard_map/right_own/pallas_call | solution.py:212
  5.5 0.0 collective-permute-done.1.mask
  5.5 0.0 collective-permute-done.pair
  5.5 1.6 %right_twin.1 = (bf16[32,32,256]{2,1,0:T(8,128)(2,1)S(1)}, bf16[4096,128]{1,0:T(8,128)(2,1)S(1)}, f32[1,32,128]{2,1,0:T(8,128)S(1)}) custom-call(bf16[32,128,128]{2,1,0:T(8,128)(2,1)S(1)} %collective-permute-done.pair, s32[32,128]{1,0:T(8,128)S(1)} %collective-permute-done.1.mask, f32[1,128]{1,0:T(1,128)S(1)} %get-tuple-element.45.gain, ...), custom_call_target="tpu_custom_call" | custom-call | tf_op jit(solution)/shard_map/right_twin/pallas_call | solution.py:212
  7.1 0.1 collective-permute-start.3
  7.3 3.5 %collective-permute-start.5 = (bf16[32,32,256]{2,1,0:T(8,128)(2,1)S(1)}, bf16[32,32,256]{2,1,0:T(8,128)(2,1)S(1)}, u32[]{:S(2)}, u32[]{:S(2)}) collective-permute-start(bf16[32,32,256]{2,1,0:T(8,128)(2,1)S(1)} %get-tuple-element.56.rest_2_), channel_id=1, source_target_pairs={{0,4},{1,5},{2,6},{3,7},{4,0},{5,1},{6,2},{7,3},{8,12},{9,13},{10,... | collective-permute-start | bytes 1572872 | tf_op jit(solution)/shard_map/end_right_0/ppermute | solution.py:240
  10.8 0.9 %right_neighbour.1 = (bf16[18,32,256]{2,1,0:T(8,128)(2,1)S(1)}, bf16[14,32,256]{2,1,0:T(8,128)(2,1)S(1)}) custom-call(bf16[4096,128]{1,0:T(8,128)(2,1)S(1)} %get-tuple-element.44.normed.normed0, bf16[4096,128]{1,0:T(8,128)(2,1)S(1)} %get-tuple-element.48.normed1, f32[1,32,128]{2,1,0:T(8,128)S(1)} %get-tuple-element.49.valid0, ...), custom_call_target="tpu_custom_call" | custom-call | tf_op jit(solution)/shard_map/right_neighbour/pallas_call | solution.py:212
  11.7 1.3 %collective-permute-start.2 = (bf16[18,32,256]{2,1,0:T(8,128)(2,1)S(1)}, bf16[18,32,256]{2,1,0:T(8,128)(2,1)S(1)}, u32[]{:S(2)}, u32[]{:S(2)}) collective-permute-start(bf16[18,32,256]{2,1,0:T(8,128)(2,1)S(1)} %get-tuple-element.55), channel_id=1, source_target_pairs={{0,2},{1,3},{2,0},{3,1},{4,6},{5,7},{6,4},{7,5},{8,10},{9,11},{10,... | collective-permute-start | bytes 884744 | tf_op jit(solution)/shard_map/cross_right_0/ppermute | solution.py:240
  13.0 0.9 %left.1 = (bf16[32,32,256]{2,1,0:T(8,128)(2,1)S(1)}, bf16[18,32,256]{2,1,0:T(8,128)(2,1)S(1)}, bf16[14,32,256]{2,1,0:T(8,128)(2,1)S(1)}) custom-call(bf16[4096,128]{1,0:T(8,128)(2,1)S(1)} %get-tuple-element.44.normed.normed0, bf16[4096,128]{1,0:T(8,128)(2,1)S(1)} %get-tuple-element.48.normed1, f32[1,32,128]{2,1,0:T(8,128)S(1)} %get-tuple-element.49.valid0, ...), custom_call_target="tpu_custom_call" | custom-call | tf_op jit(solution)/shard_map/left/pallas_call | solution.py:212
  13.9 5.3 %collective-permute-done.2.rest_3_ = bf16[18,32,256]{2,1,0:T(8,128)(2,1)S(1)} collective-permute-done((bf16[18,32,256]{2,1,0:T(8,128)(2,1)S(1)}, bf16[18,32,256]{2,1,0:T(8,128)(2,1)S(1)}, u32[]{:S(2)}, u32[]{:S(2)}) %collective-permute-start.2) | collective-permute-done | bytes 294944 | tf_op jit(solution)/shard_map/cross_right_0/ppermute | solution.py:240
  19.2 2.0 %collective-permute-start.9 = (bf16[18,32,256]{2,1,0:T(8,128)(2,1)S(1)}, bf16[18,32,256]{2,1,0:T(8,128)(2,1)S(1)}, u32[]{:S(2)}, u32[]{:S(2)}) collective-permute-start(bf16[18,32,256]{2,1,0:T(8,128)(2,1)S(1)} %collective-permute-done.2.rest_3_), channel_id=1, source_target_pairs={{0,1},{1,0},{2,3},{3,2},{4,8},{5,9},{6,10},{7,11},{8,4},{9,5},{10,... | collective-permute-start | bytes 884744 | tf_op jit(solution)/shard_map/mid_own_10/ppermute | solution.py:240
  21.2 0.7 collective-permute-start.6
  21.8 0.0 collective-permute-done.3.rest_4_
  21.9 1.2 %collective-permute-start.4 = (bf16[18,32,256]{2,1,0:T(8,128)(2,1)S(1)}, bf16[18,32,256]{2,1,0:T(8,128)(2,1)S(1)}, u32[]{:S(2)}, u32[]{:S(2)}) collective-permute-start(bf16[18,32,256]{2,1,0:T(8,128)(2,1)S(1)} %get-tuple-element.57), channel_id=1, source_target_pairs={{0,2},{1,3},{2,0},{3,1},{4,6},{5,7},{6,4},{7,5},{8,10},{9,11},{10,... | collective-permute-start | bytes 884744 | tf_op jit(solution)/shard_map/cross_left_0/ppermute | solution.py:240
  23.1 0.0 collective-permute-done.5.rest_4_
  23.1 2.0 %collective-permute-start.10 = (bf16[32,32,256]{2,1,0:T(8,128)(2,1)S(1)}, bf16[32,32,256]{2,1,0:T(8,128)(2,1)S(1)}, u32[]{:S(2)}, u32[]{:S(2)}) collective-permute-start(bf16[32,32,256]{2,1,0:T(8,128)(2,1)S(1)} %collective-permute-done.5.rest_4_), channel_id=1, source_target_pairs={{0,1},{1,0},{2,3},{3,2},{4,8},{5,9},{6,10},{7,11},{8,4},{9,5},{10,... | collective-permute-start | bytes 1572872 | tf_op jit(solution)/shard_map/mid_next_0/ppermute | solution.py:240
  25.1 0.0 collective-permute-start.7
  25.1 0.0 collective-permute-done.9.rest_5_
  25.1 4.3 %collective-permute-done.6.rest_5_ = bf16[18,32,256]{2,1,0:T(8,128)(2,1)S(1)} collective-permute-done((bf16[18,32,256]{2,1,0:T(8,128)(2,1)S(1)}, bf16[18,32,256]{2,1,0:T(8,128)(2,1)S(1)}, u32[]{:S(2)}, u32[]{:S(2)}) %collective-permute-start.6) | collective-permute-done | bytes 294944 | tf_op jit(solution)/shard_map/end_right_10/ppermute | solution.py:240
  29.4 0.0 collective-permute-done.4.rest_1_
  29.4 1.3 %collective-permute-start.12 = (bf16[14,32,256]{2,1,0:T(8,128)(2,1)S(1)}, bf16[14,32,256]{2,1,0:T(8,128)(2,1)S(1)}, u32[]{:S(2)}, u32[]{:S(2)}) collective-permute-start(bf16[14,32,256]{2,1,0:T(8,128)(2,1)S(1)} %get-tuple-element.65), channel_id=1, source_target_pairs={{0,2},{1,3},{2,0},{3,1},{4,6},{5,7},{6,4},{7,5},{8,10},{9,11},{10,... | collective-permute-start | bytes 688136 | tf_op jit(solution)/shard_map/cross_right_1/ppermute | solution.py:240
  30.7 0.4 gate.1
  31.1 2.3 %collective-permute-start.11 = (bf16[18,32,256]{2,1,0:T(8,128)(2,1)S(1)}, bf16[18,32,256]{2,1,0:T(8,128)(2,1)S(1)}, u32[]{:S(2)}, u32[]{:S(2)}) collective-permute-start(bf16[18,32,256]{2,1,0:T(8,128)(2,1)S(1)} %collective-permute-done.6.rest_5_), channel_id=1, source_target_pairs={{0,1},{1,0},{2,3},{3,2},{4,8},{5,9},{6,10},{7,11},{8,4},{9,5},{10,... | collective-permute-start | bytes 884744 | tf_op jit(solution)/shard_map/mid_next_10/ppermute | solution.py:240
  33.4 0.0 collective-permute-start.8
  33.4 1.2 %collective-permute-done.12.rest_3_ = bf16[14,32,256]{2,1,0:T(8,128)(2,1)S(1)} collective-permute-done((bf16[14,32,256]{2,1,0:T(8,128)(2,1)S(1)}, bf16[14,32,256]{2,1,0:T(8,128)(2,1)S(1)}, u32[]{:S(2)}, u32[]{:S(2)}) %collective-permute-start.12) | collective-permute-done | bytes 229408 | tf_op jit(solution)/shard_map/cross_right_1/ppermute | solution.py:240
  34.6 0.0 collective-permute-done.10.rest_6_
  34.6 1.3 %collective-permute-start.13 = (bf16[14,32,256]{2,1,0:T(8,128)(2,1)S(1)}, bf16[14,32,256]{2,1,0:T(8,128)(2,1)S(1)}, u32[]{:S(2)}, u32[]{:S(2)}) collective-permute-start(bf16[14,32,256]{2,1,0:T(8,128)(2,1)S(1)} %get-tuple-element.66), channel_id=1, source_target_pairs={{0,2},{1,3},{2,0},{3,1},{4,6},{5,7},{6,4},{7,5},{8,10},{9,11},{10,... | collective-permute-start | bytes 688136 | tf_op jit(solution)/shard_map/cross_left_1/ppermute | solution.py:240
  35.9 3.1 %collective-permute-start.19 = (bf16[14,32,256]{2,1,0:T(8,128)(2,1)S(1)}, bf16[14,32,256]{2,1,0:T(8,128)(2,1)S(1)}, u32[]{:S(2)}, u32[]{:S(2)}) collective-permute-start(bf16[14,32,256]{2,1,0:T(8,128)(2,1)S(1)} %collective-permute-done.12.rest_3_), channel_id=1, source_target_pairs={{0,1},{1,0},{2,3},{3,2},{4,8},{5,9},{6,10},{7,11},{8,4},{9,5},{10,... | collective-permute-start | bytes 688136 | tf_op jit(solution)/shard_map/mid_own_11/ppermute | solution.py:240
  39.0 1.7 %collective-permute-done.7.rest_2_ = bf16[32,32,256]{2,1,0:T(8,128)(2,1)S(1)} collective-permute-done((bf16[32,32,256]{2,1,0:T(8,128)(2,1)S(1)}, bf16[32,32,256]{2,1,0:T(8,128)(2,1)S(1)}, u32[]{:S(2)}, u32[]{:S(2)}) %collective-permute-start.7) | collective-permute-done | bytes 524320 | tf_op jit(solution)/shard_map/end_left_0/ppermute | solution.py:240
  40.7 1.4 %collective-permute-start.18 = (bf16[14,32,256]{2,1,0:T(8,128)(2,1)S(1)}, bf16[14,32,256]{2,1,0:T(8,128)(2,1)S(1)}, u32[]{:S(2)}, u32[]{:S(2)}) collective-permute-start(bf16[14,32,256]{2,1,0:T(8,128)(2,1)S(1)} %collective-permute-done.12.rest_3_), channel_id=1, source_target_pairs={{0,4},{1,5},{2,6},{3,7},{4,0},{5,1},{6,2},{7,3},{8,12},{9,13},{10,... | collective-permute-start | bytes 688136 | tf_op jit(solution)/shard_map/end_right_11/ppermute | solution.py:240
  42.0 5.0 %collective-permute-done.8.rest_3_ = bf16[18,32,256]{2,1,0:T(8,128)(2,1)S(1)} collective-permute-done((bf16[18,32,256]{2,1,0:T(8,128)(2,1)S(1)}, bf16[18,32,256]{2,1,0:T(8,128)(2,1)S(1)}, u32[]{:S(2)}, u32[]{:S(2)}) %collective-permute-start.8) | collective-permute-done | bytes 294944 | tf_op jit(solution)/shard_map/end_left_10/ppermute | solution.py:240
  47.0 0.0 collective-permute-done.13.rest_8_.rest_1_
  47.0 0.6 away.2
  47.6 0.1 collective-permute-start.14
  47.7 4.2 %collective-permute-done.18.rest_5_ = bf16[14,32,256]{2,1,0:T(8,128)(2,1)S(1)} collective-permute-done((bf16[14,32,256]{2,1,0:T(8,128)(2,1)S(1)}, bf16[14,32,256]{2,1,0:T(8,128)(2,1)S(1)}, u32[]{:S(2)}, u32[]{:S(2)}) %collective-permute-start.18) | collective-permute-done | bytes 229408 | tf_op jit(solution)/shard_map/end_right_11/ppermute | solution.py:240
  51.9 2.0 %collective-permute-start.20 = (bf16[14,32,256]{2,1,0:T(8,128)(2,1)S(1)}, bf16[14,32,256]{2,1,0:T(8,128)(2,1)S(1)}, u32[]{:S(2)}, u32[]{:S(2)}) collective-permute-start(bf16[14,32,256]{2,1,0:T(8,128)(2,1)S(1)} %collective-permute-done.18.rest_5_), channel_id=1, source_target_pairs={{0,1},{1,0},{2,3},{3,2},{4,8},{5,9},{6,10},{7,11},{8,4},{9,5},{10,... | collective-permute-start | bytes 688136 | tf_op jit(solution)/shard_map/mid_next_11/ppermute | solution.py:240
  53.9 0.6 near.2
  54.5 0.5 near.3
  55.0 3.2 %collective-permute-done.14.end.rest_3_ = bf16[18,32,256]{2,1,0:T(8,128)(2,1)S(1)} collective-permute-done((bf16[18,32,256]{2,1,0:T(8,128)(2,1)S(1)}, bf16[18,32,256]{2,1,0:T(8,128)(2,1)S(1)}, u32[]{:S(2)}, u32[]{:S(2)}) %collective-permute-start.14) | collective-permute-done | bytes 294944 | tf_op jit(solution)/shard_map/left_11_and_products_back_0/ppermute | solution.py:240
  58.2 0.1 hand_out.2
  58.3 0.0 copy-start.3
  58.3 0.0 copy-start.6
  58.4 0.5 away.3
  58.9 0.1 collective-permute-start.21
  58.9 3.6 %collective-permute-start.15 = (bf16[18,32,128]{2,1,0:T(8,128)(2,1)S(1)}, bf16[18,32,128]{2,1,0:T(8,128)(2,1)S(1)}, u32[]{:S(2)}, u32[]{:S(2)}) collective-permute-start(bf16[18,32,128]{2,1,0:T(8,128)(2,1)S(1)} %get-tuple-element.70), channel_id=1, source_target_pairs={{0,1},{1,0},{2,3},{3,2},{4,5},{5,4},{6,7},{7,6},{8,9},{9,8},{10,11... | collective-permute-start | bytes 442376 | tf_op jit(solution)/shard_map/return_01/ppermute | solution.py:240
  62.6 1.2 %collective-permute-start.16 = (bf16[18,32,128]{2,1,0:T(8,128)(2,1)S(1)}, bf16[18,32,128]{2,1,0:T(8,128)(2,1)S(1)}, u32[]{:S(2)}, u32[]{:S(2)}) collective-permute-start(bf16[18,32,128]{2,1,0:T(8,128)(2,1)S(1)} %get-tuple-element.71), channel_id=1, source_target_pairs={{0,2},{1,3},{2,0},{3,1},{4,6},{5,7},{6,4},{7,5},{8,10},{9,11},{10,... | collective-permute-start | bytes 442376 | tf_op jit(solution)/shard_map/return_02/ppermute | solution.py:240
  63.8 0.4 collective-permute-start.17
  64.2 0.2 collective-permute-done.21.end
  64.4 0.1 hand_out.3
  64.5 2.6 %collective-permute-start.22 = (bf16[14,32,128]{2,1,0:T(8,128)(2,1)S(1)}, bf16[14,32,128]{2,1,0:T(8,128)(2,1)S(1)}, u32[]{:S(2)}, u32[]{:S(2)}) collective-permute-start(bf16[14,32,128]{2,1,0:T(8,128)(2,1)S(1)} %get-tuple-element.80), channel_id=1, source_target_pairs={{0,1},{1,0},{2,3},{3,2},{4,5},{5,4},{6,7},{7,6},{8,9},{9,8},{10,11... | collective-permute-start | bytes 344072 | tf_op jit(solution)/shard_map/return_11/ppermute | solution.py:240
  67.1 1.3 %collective-permute-start.23 = (bf16[14,32,128]{2,1,0:T(8,128)(2,1)S(1)}, bf16[14,32,128]{2,1,0:T(8,128)(2,1)S(1)}, u32[]{:S(2)}, u32[]{:S(2)}) collective-permute-start(bf16[14,32,128]{2,1,0:T(8,128)(2,1)S(1)} %get-tuple-element.81), channel_id=1, source_target_pairs={{0,2},{1,3},{2,0},{3,1},{4,6},{5,7},{6,4},{7,5},{8,10},{9,11},{10,... | collective-permute-start | bytes 344072 | tf_op jit(solution)/shard_map/return_12/ppermute | solution.py:240
  68.4 0.0 collective-permute-done.15.rest_1_
  68.4 0.4 collective-permute-start.24
  68.8 0.0 collective-permute-done.16.rest_2_
  68.8 2.9 %collective-permute-done.17.rest_3_ = bf16[18,32,128]{2,1,0:T(8,128)(2,1)S(1)} collective-permute-done((bf16[18,32,128]{2,1,0:T(8,128)(2,1)S(1)}, bf16[18,32,128]{2,1,0:T(8,128)(2,1)S(1)}, u32[]{:S(2)}, u32[]{:S(2)}) %collective-permute-start.17) | collective-permute-done | bytes 147488 | tf_op jit(solution)/shard_map/return_03/ppermute | solution.py:240
  71.7 2.0 %collective-permute-done.23.rest_6_ = bf16[14,32,128]{2,1,0:T(8,128)(2,1)S(1)} collective-permute-done((bf16[14,32,128]{2,1,0:T(8,128)(2,1)S(1)}, bf16[14,32,128]{2,1,0:T(8,128)(2,1)S(1)}, u32[]{:S(2)}, u32[]{:S(2)}) %collective-permute-start.23) | collective-permute-done | bytes 114720 | tf_op jit(solution)/shard_map/return_12/ppermute | solution.py:240
  73.7 2.6 %collective-permute-done.24.rest_7_ = bf16[14,32,128]{2,1,0:T(8,128)(2,1)S(1)} collective-permute-done((bf16[14,32,128]{2,1,0:T(8,128)(2,1)S(1)}, bf16[14,32,128]{2,1,0:T(8,128)(2,1)S(1)}, u32[]{:S(2)}, u32[]{:S(2)}) %collective-permute-start.24) | collective-permute-done | bytes 114720 | tf_op jit(solution)/shard_map/return_13/ppermute | solution.py:240
  76.2 2.0 %update.1 = bf16[32,128,128]{2,1,0:T(8,128)(2,1)} custom-call(f32[1,128]{1,0:T(1,128)S(1)} %bitcast.3, bf16[128,128]{1,0:T(8,128)(2,1)S(1)} %copy-done.3, f32[32,128,128]{2,1,0:T(8,128)S(1)} %gate.1, bf16[18,32,128]{2,1,0:T(8,128)(2,1)S(1)} %get-tuple-element.69.rest_0_, bf16[18,32,128]{2,1,0:T(8,128)(2,1)S(1)} %collective-permute-done.15.rest_1_, ...), custom_call_target="tpu_custom_call" | custom-call | tf_op jit(solution)/shard_map/update/pallas_call | solution.py:212
  (12 shorter events, 0.0 us)
Async XLA Ops:
  0.0 5.5 %collective-permute-start = (bf16[32,128,128]{2,1,0:T(8,128)(2,1)}, bf16[32,128,128]{2,1,0:T(8,128)(2,1)S(1)}, u32[]{:S(2)}, u32[]{:S(2)}) collective-permute-start(bf16[32,128,128]{2,1,0:T(8,128)(2,1)} %pair.1), channel_id=1, source_target_pairs={{0,1},{1,0},{2,3},{3,2},{4,5},{5,4},{6,7},{7,6},{8,9},{9,8},{10,11... | collective-permute-start | bytes 3145736 | tf_op jit(solution)/shard_map/pair/ppermute | solution.py:240
  0.1 5.5 %collective-permute-start.1 = (s32[32,128]{1,0:T(8,128)}, s32[32,128]{1,0:T(8,128)S(1)}, u32[]{:S(2)}, u32[]{:S(2)}) collective-permute-start(s32[32,128]{1,0:T(8,128)} %mask.1), channel_id=1, source_target_pairs={{0,1},{1,0},{2,3},{3,2},{4,5},{5,4},{6,7},{7,6},{8,9},{9,8},{10,11... | collective-permute-start | bytes 49160 | tf_op jit(solution)/shard_map/mask/ppermute | solution.py:240
  0.5 1.2 %copy-start = (bf16[32,128,128]{2,1,0:T(8,128)(2,1)S(1)}, bf16[32,128,128]{2,1,0:T(8,128)(2,1)}, u32[]{:S(2)}) copy-start(bf16[32,128,128]{2,1,0:T(8,128)(2,1)} %pair.1) | copy-start | bytes 3145732
  1.7 0.9 %copy-start.1 = (bf16[128,512]{1,0:T(8,128)(2,1)S(1)}, bf16[128,512]{1,0:T(8,128)(2,1)}, u32[]{:S(2)}) copy-start(bf16[128,512]{1,0:T(8,128)(2,1)} %weight.3) | copy-start | bytes 393220
  2.6 0.7 copy-start.4
  3.4 0.7 copy-start.5
  7.1 14.7 %collective-permute-start.3 = (bf16[32,32,256]{2,1,0:T(8,128)(2,1)S(1)}, bf16[32,32,256]{2,1,0:T(8,128)(2,1)S(1)}, u32[]{:S(2)}, u32[]{:S(2)}) collective-permute-start(bf16[32,32,256]{2,1,0:T(8,128)(2,1)S(1)} %get-tuple-element.56.rest_2_), channel_id=1, source_target_pairs={{0,1},{1,0},{2,3},{3,2},{4,8},{5,9},{6,10},{7,11},{8,4},{9,5},{10,... | collective-permute-start | bytes 1572872 | tf_op jit(solution)/shard_map/mid_own_0/ppermute | solution.py:240
  7.3 15.8 %collective-permute-start.5 = (bf16[32,32,256]{2,1,0:T(8,128)(2,1)S(1)}, bf16[32,32,256]{2,1,0:T(8,128)(2,1)S(1)}, u32[]{:S(2)}, u32[]{:S(2)}) collective-permute-start(bf16[32,32,256]{2,1,0:T(8,128)(2,1)S(1)} %get-tuple-element.56.rest_2_), channel_id=1, source_target_pairs={{0,4},{1,5},{2,6},{3,7},{4,0},{5,1},{6,2},{7,3},{8,12},{9,13},{10,... | collective-permute-start | bytes 1572872 | tf_op jit(solution)/shard_map/end_right_0/ppermute | solution.py:240
  10.8 19.9 %copy-start.2 = (bf16[128,128]{1,0:T(8,128)(2,1)S(1)}, bf16[128,128]{1,0:T(8,128)(2,1)}, u32[]{:S(2)}) copy-start(bf16[128,128]{1,0:T(8,128)(2,1)} %weight.4) | copy-start | bytes 98308
  11.7 7.5 %collective-permute-start.2 = (bf16[18,32,256]{2,1,0:T(8,128)(2,1)S(1)}, bf16[18,32,256]{2,1,0:T(8,128)(2,1)S(1)}, u32[]{:S(2)}, u32[]{:S(2)}) collective-permute-start(bf16[18,32,256]{2,1,0:T(8,128)(2,1)S(1)} %get-tuple-element.55), channel_id=1, source_target_pairs={{0,2},{1,3},{2,0},{3,1},{4,6},{5,7},{6,4},{7,5},{8,10},{9,11},{10,... | collective-permute-start | bytes 884744 | tf_op jit(solution)/shard_map/cross_right_0/ppermute | solution.py:240
  19.2 5.9 %collective-permute-start.9 = (bf16[18,32,256]{2,1,0:T(8,128)(2,1)S(1)}, bf16[18,32,256]{2,1,0:T(8,128)(2,1)S(1)}, u32[]{:S(2)}, u32[]{:S(2)}) collective-permute-start(bf16[18,32,256]{2,1,0:T(8,128)(2,1)S(1)} %collective-permute-done.2.rest_3_), channel_id=1, source_target_pairs={{0,1},{1,0},{2,3},{3,2},{4,8},{5,9},{6,10},{7,11},{8,4},{9,5},{10,... | collective-permute-start | bytes 884744 | tf_op jit(solution)/shard_map/mid_own_10/ppermute | solution.py:240
  21.2 8.2 %collective-permute-start.6 = (bf16[18,32,256]{2,1,0:T(8,128)(2,1)S(1)}, bf16[18,32,256]{2,1,0:T(8,128)(2,1)S(1)}, u32[]{:S(2)}, u32[]{:S(2)}) collective-permute-start(bf16[18,32,256]{2,1,0:T(8,128)(2,1)S(1)} %collective-permute-done.2.rest_3_), channel_id=1, source_target_pairs={{0,4},{1,5},{2,6},{3,7},{4,0},{5,1},{6,2},{7,3},{8,12},{9,13},{10,... | collective-permute-start | bytes 884744 | tf_op jit(solution)/shard_map/end_right_10/ppermute | solution.py:240
  21.9 7.6 %collective-permute-start.4 = (bf16[18,32,256]{2,1,0:T(8,128)(2,1)S(1)}, bf16[18,32,256]{2,1,0:T(8,128)(2,1)S(1)}, u32[]{:S(2)}, u32[]{:S(2)}) collective-permute-start(bf16[18,32,256]{2,1,0:T(8,128)(2,1)S(1)} %get-tuple-element.57), channel_id=1, source_target_pairs={{0,2},{1,3},{2,0},{3,1},{4,6},{5,7},{6,4},{7,5},{8,10},{9,11},{10,... | collective-permute-start | bytes 884744 | tf_op jit(solution)/shard_map/cross_left_0/ppermute | solution.py:240
  23.1 11.5 %collective-permute-start.10 = (bf16[32,32,256]{2,1,0:T(8,128)(2,1)S(1)}, bf16[32,32,256]{2,1,0:T(8,128)(2,1)S(1)}, u32[]{:S(2)}, u32[]{:S(2)}) collective-permute-start(bf16[32,32,256]{2,1,0:T(8,128)(2,1)S(1)} %collective-permute-done.5.rest_4_), channel_id=1, source_target_pairs={{0,1},{1,0},{2,3},{3,2},{4,8},{5,9},{6,10},{7,11},{8,4},{9,5},{10,... | collective-permute-start | bytes 1572872 | tf_op jit(solution)/shard_map/mid_next_0/ppermute | solution.py:240
  25.1 15.6 %collective-permute-start.7 = (bf16[32,32,256]{2,1,0:T(8,128)(2,1)S(1)}, bf16[32,32,256]{2,1,0:T(8,128)(2,1)S(1)}, u32[]{:S(2)}, u32[]{:S(2)}) collective-permute-start(bf16[32,32,256]{2,1,0:T(8,128)(2,1)S(1)} %get-tuple-element.74.rest_0_), channel_id=1, source_target_pairs={{0,4},{1,5},{2,6},{3,7},{4,0},{5,1},{6,2},{7,3},{8,12},{9,13},{10,... | collective-permute-start | bytes 1572872 | tf_op jit(solution)/shard_map/end_left_0/ppermute | solution.py:240
  29.4 5.2 %collective-permute-start.12 = (bf16[14,32,256]{2,1,0:T(8,128)(2,1)S(1)}, bf16[14,32,256]{2,1,0:T(8,128)(2,1)S(1)}, u32[]{:S(2)}, u32[]{:S(2)}) collective-permute-start(bf16[14,32,256]{2,1,0:T(8,128)(2,1)S(1)} %get-tuple-element.65), channel_id=1, source_target_pairs={{0,2},{1,3},{2,0},{3,1},{4,6},{5,7},{6,4},{7,5},{8,10},{9,11},{10,... | collective-permute-start | bytes 688136 | tf_op jit(solution)/shard_map/cross_right_1/ppermute | solution.py:240
  31.1 10.9 %collective-permute-start.11 = (bf16[18,32,256]{2,1,0:T(8,128)(2,1)S(1)}, bf16[18,32,256]{2,1,0:T(8,128)(2,1)S(1)}, u32[]{:S(2)}, u32[]{:S(2)}) collective-permute-start(bf16[18,32,256]{2,1,0:T(8,128)(2,1)S(1)} %collective-permute-done.6.rest_5_), channel_id=1, source_target_pairs={{0,1},{1,0},{2,3},{3,2},{4,8},{5,9},{6,10},{7,11},{8,4},{9,5},{10,... | collective-permute-start | bytes 884744 | tf_op jit(solution)/shard_map/mid_next_10/ppermute | solution.py:240
  33.4 13.6 %collective-permute-start.8 = (bf16[18,32,256]{2,1,0:T(8,128)(2,1)S(1)}, bf16[18,32,256]{2,1,0:T(8,128)(2,1)S(1)}, u32[]{:S(2)}, u32[]{:S(2)}) collective-permute-start(bf16[18,32,256]{2,1,0:T(8,128)(2,1)S(1)} %collective-permute-done.4.rest_1_), channel_id=1, source_target_pairs={{0,4},{1,5},{2,6},{3,7},{4,0},{5,1},{6,2},{7,3},{8,12},{9,13},{10,... | collective-permute-start | bytes 884744 | tf_op jit(solution)/shard_map/end_left_10/ppermute | solution.py:240
  34.6 12.4 %collective-permute-start.13 = (bf16[14,32,256]{2,1,0:T(8,128)(2,1)S(1)}, bf16[14,32,256]{2,1,0:T(8,128)(2,1)S(1)}, u32[]{:S(2)}, u32[]{:S(2)}) collective-permute-start(bf16[14,32,256]{2,1,0:T(8,128)(2,1)S(1)} %get-tuple-element.66), channel_id=1, source_target_pairs={{0,2},{1,3},{2,0},{3,1},{4,6},{5,7},{6,4},{7,5},{8,10},{9,11},{10,... | collective-permute-start | bytes 688136 | tf_op jit(solution)/shard_map/cross_left_1/ppermute | solution.py:240
  35.9 11.8 %collective-permute-start.19 = (bf16[14,32,256]{2,1,0:T(8,128)(2,1)S(1)}, bf16[14,32,256]{2,1,0:T(8,128)(2,1)S(1)}, u32[]{:S(2)}, u32[]{:S(2)}) collective-permute-start(bf16[14,32,256]{2,1,0:T(8,128)(2,1)S(1)} %collective-permute-done.12.rest_3_), channel_id=1, source_target_pairs={{0,1},{1,0},{2,3},{3,2},{4,8},{5,9},{6,10},{7,11},{8,4},{9,5},{10,... | collective-permute-start | bytes 688136 | tf_op jit(solution)/shard_map/mid_own_11/ppermute | solution.py:240
  40.7 11.2 %collective-permute-start.18 = (bf16[14,32,256]{2,1,0:T(8,128)(2,1)S(1)}, bf16[14,32,256]{2,1,0:T(8,128)(2,1)S(1)}, u32[]{:S(2)}, u32[]{:S(2)}) collective-permute-start(bf16[14,32,256]{2,1,0:T(8,128)(2,1)S(1)} %collective-permute-done.12.rest_3_), channel_id=1, source_target_pairs={{0,4},{1,5},{2,6},{3,7},{4,0},{5,1},{6,2},{7,3},{8,12},{9,13},{10,... | collective-permute-start | bytes 688136 | tf_op jit(solution)/shard_map/end_right_11/ppermute | solution.py:240
  47.6 10.6 %collective-permute-start.14 = (bf16[18,32,256]{2,1,0:T(8,128)(2,1)S(1)}, bf16[18,32,256]{2,1,0:T(8,128)(2,1)S(1)}, u32[]{:S(2)}, u32[]{:S(2)}) collective-permute-start(bf16[18,32,256]{2,1,0:T(8,128)(2,1)S(1)} %get-tuple-element.68), channel_id=1, source_target_pairs={{0,4},{1,5},{2,6},{3,7},{4,0},{5,1},{6,2},{7,3},{8,12},{9,13},{10,... | collective-permute-start | bytes 884744 | tf_op jit(solution)/shard_map/left_11_and_products_back_0/ppermute | solution.py:240
  51.9 6.4 %collective-permute-start.20 = (bf16[14,32,256]{2,1,0:T(8,128)(2,1)S(1)}, bf16[14,32,256]{2,1,0:T(8,128)(2,1)S(1)}, u32[]{:S(2)}, u32[]{:S(2)}) collective-permute-start(bf16[14,32,256]{2,1,0:T(8,128)(2,1)S(1)} %collective-permute-done.18.rest_5_), channel_id=1, source_target_pairs={{0,1},{1,0},{2,3},{3,2},{4,8},{5,9},{6,10},{7,11},{8,4},{9,5},{10,... | collective-permute-start | bytes 688136 | tf_op jit(solution)/shard_map/mid_next_11/ppermute | solution.py:240
  58.3 17.9 %copy-start.3 = (bf16[128,128]{1,0:T(8,128)(2,1)S(1)}, bf16[128,128]{1,0:T(8,128)(2,1)}, u32[]{:S(2)}) copy-start(bf16[128,128]{1,0:T(8,128)(2,1)} %weight.5) | copy-start | bytes 98308
  58.3 17.9 %copy-start.6 = (f32[128]{0:T(128)S(1)}, f32[128]{0:T(128)}, u32[]{:S(2)}) copy-start(f32[128]{0:T(128)} %param.12) | copy-start | bytes 1540
  58.9 5.5 %collective-permute-start.21 = (bf16[14,32,256]{2,1,0:T(8,128)(2,1)S(1)}, bf16[14,32,256]{2,1,0:T(8,128)(2,1)S(1)}, u32[]{:S(2)}, u32[]{:S(2)}) collective-permute-start(bf16[14,32,256]{2,1,0:T(8,128)(2,1)S(1)} %get-tuple-element.78), channel_id=1, source_target_pairs={{0,4},{1,5},{2,6},{3,7},{4,0},{5,1},{6,2},{7,3},{8,12},{9,13},{10,... | collective-permute-start | bytes 688136 | tf_op jit(solution)/shard_map/products_back_1/ppermute | solution.py:240
  58.9 9.4 %collective-permute-start.15 = (bf16[18,32,128]{2,1,0:T(8,128)(2,1)S(1)}, bf16[18,32,128]{2,1,0:T(8,128)(2,1)S(1)}, u32[]{:S(2)}, u32[]{:S(2)}) collective-permute-start(bf16[18,32,128]{2,1,0:T(8,128)(2,1)S(1)} %get-tuple-element.70), channel_id=1, source_target_pairs={{0,1},{1,0},{2,3},{3,2},{4,5},{5,4},{6,7},{7,6},{8,9},{9,8},{10,11... | collective-permute-start | bytes 442376 | tf_op jit(solution)/shard_map/return_01/ppermute | solution.py:240
  62.6 6.2 %collective-permute-start.16 = (bf16[18,32,128]{2,1,0:T(8,128)(2,1)S(1)}, bf16[18,32,128]{2,1,0:T(8,128)(2,1)S(1)}, u32[]{:S(2)}, u32[]{:S(2)}) collective-permute-start(bf16[18,32,128]{2,1,0:T(8,128)(2,1)S(1)} %get-tuple-element.71), channel_id=1, source_target_pairs={{0,2},{1,3},{2,0},{3,1},{4,6},{5,7},{6,4},{7,5},{8,10},{9,11},{10,... | collective-permute-start | bytes 442376 | tf_op jit(solution)/shard_map/return_02/ppermute | solution.py:240
  63.8 7.9 %collective-permute-start.17 = (bf16[18,32,128]{2,1,0:T(8,128)(2,1)S(1)}, bf16[18,32,128]{2,1,0:T(8,128)(2,1)S(1)}, u32[]{:S(2)}, u32[]{:S(2)}) collective-permute-start(bf16[18,32,128]{2,1,0:T(8,128)(2,1)S(1)} %get-tuple-element.72), channel_id=1, source_target_pairs={{0,3},{1,2},{2,1},{3,0},{4,7},{5,6},{6,5},{7,4},{8,11},{9,10},{10,... | collective-permute-start | bytes 442376 | tf_op jit(solution)/shard_map/return_03/ppermute | solution.py:240
  64.5 7.2 %collective-permute-start.22 = (bf16[14,32,128]{2,1,0:T(8,128)(2,1)S(1)}, bf16[14,32,128]{2,1,0:T(8,128)(2,1)S(1)}, u32[]{:S(2)}, u32[]{:S(2)}) collective-permute-start(bf16[14,32,128]{2,1,0:T(8,128)(2,1)S(1)} %get-tuple-element.80), channel_id=1, source_target_pairs={{0,1},{1,0},{2,3},{3,2},{4,5},{5,4},{6,7},{7,6},{8,9},{9,8},{10,11... | collective-permute-start | bytes 344072 | tf_op jit(solution)/shard_map/return_11/ppermute | solution.py:240
  67.1 6.6 %collective-permute-start.23 = (bf16[14,32,128]{2,1,0:T(8,128)(2,1)S(1)}, bf16[14,32,128]{2,1,0:T(8,128)(2,1)S(1)}, u32[]{:S(2)}, u32[]{:S(2)}) collective-permute-start(bf16[14,32,128]{2,1,0:T(8,128)(2,1)S(1)} %get-tuple-element.81), channel_id=1, source_target_pairs={{0,2},{1,3},{2,0},{3,1},{4,6},{5,7},{6,4},{7,5},{8,10},{9,11},{10,... | collective-permute-start | bytes 344072 | tf_op jit(solution)/shard_map/return_12/ppermute | solution.py:240
  68.4 7.9 %collective-permute-start.24 = (bf16[14,32,128]{2,1,0:T(8,128)(2,1)S(1)}, bf16[14,32,128]{2,1,0:T(8,128)(2,1)S(1)}, u32[]{:S(2)}, u32[]{:S(2)}) collective-permute-start(bf16[14,32,128]{2,1,0:T(8,128)(2,1)S(1)} %get-tuple-element.82), channel_id=1, source_target_pairs={{0,3},{1,2},{2,1},{3,0},{4,7},{5,6},{6,5},{7,4},{8,11},{9,10},{10,... | collective-permute-start | bytes 344072 | tf_op jit(solution)/shard_map/return_13/ppermute | solution.py:240

commit v26 on v24

--- a/solution.py
+++ b/solution.py
@@ -149,7 +149,7 @@
             outs[1][: other.shape[0]] = other[...]
 
 
-def hand_out_kernel(planes, near, far, end, *outs):
+def hand_out_kernel(planes, beside, near, far, end, *outs):
     _, rows, toks = outs[0].shape
     z, _, core = place()
     at_end = (z == 0) | (z == planes - 1)
@@ -168,7 +168,7 @@
 
         @pl.when(jnp.logical_not(is_near) & at_end)
         def _():
-            outs[r][...] = end[:, :, lanes]
+            outs[r][...] = end[:, :, lanes] if beside else end[:, span, :]
 
 
 def update_kernel(gain, weight, gate, *rest):
@@ -330,7 +330,7 @@
     near1.append(end_right("11", right1[1], outer0))
     def products(mirror, first, lefts, rights, name, instead=()):
         span = 2 * rows * len(rights)
-        count = lefts[0][1].shape[0]
+        count = rights[0][1].shape[0]
         args = [x for arrays in (*lefts, *rights) for x in arrays] + [*instead]
         shapes = [piece(count, 2 * rows, span), piece(count, rows, 2 * span)]
         return kernel(
@@ -351,7 +351,7 @@
 
     def hand_out(g, close, away, ends):
         handed = kernel(
-            functools.partial(hand_out_kernel, planes),
+            functools.partial(hand_out_kernel, planes, g == 0),
             "hand_out",
             [piece(counts[g], rows, toks)] * 4,
             [VMEM] * 3,
@@ -368,8 +368,9 @@
     next1.append([mid("next_11", x, next1[0][-1], own1[1], away0) for x in near1[1]])
     swapped = send(swapped, edge, "left_11_and_products_back_0")
     pieces = hand_out(0, close[0], away0, swapped)
-    sides = [(after(left0, pieces[0], close[1]), left1[1]), (outer0, swapped)]
-    away1, ends = products(True, first[1], sides, far_planes(1), "away")
+    side = (after(outer0, pieces[0], close[1]), swapped)
+    (ends,) = products(True, first[1], [side], far_planes(1), "away_for_ends")
+    (away1,) = products(True, first[1], [(after(left0, ends), left1[1])], far_planes(1), "away")
     ends = send(ends, edge, "products_back_1")
     pieces += hand_out(1, close[1], away1, ends)
 

time: 77.3 us -> 77.4 us (level)
    pallas_call x12 -> x13, Pallas kernels: 9.72 us -> 10.2 us  [call(): pl.pallas_call(body, out_shape=out_shape, in_specs=in_specs, out_specs=ou...]
  transfers between devices with their start and end apart: 25 -> 25, of which waited for: 12 -> 12; matrix products, arithmetic and copies ran while one was open for 0% -> 0% of each run, Pallas kernels for 7% -> 8%
where the time goes in v26:
time: 77.4 us; the launch traced here: 76.9 us
  waiting for transfers between devices  32.2 us (42%)
  starting transfers between devices  30.8 us (40%)
  Pallas kernels  10.2 us (13%)
  local copies, waits for them, and re-layouts  3.51 us (5%)
    ppermute x25, waiting for transfers between devices, send(): return lax.ppermute(x, ('row', 'chan'), pairs)  32.2 us
    ppermute x25, starting transfers between devices, send(): return lax.ppermute(x, ('row', 'chan'), pairs)  30.8 us
    pallas_call x13, Pallas kernels, call(): pl.pallas_call(body, out_shape=out_shape, in_specs=in_specs, out_specs=ou...  10.2 us
    unnamed x14, local copies, waits for them, and re-layouts  3.51 us
  transfers between devices with their start and end apart: 25, of which 12 were waited for; matrix products, arithmetic and copies ran while one was open for 0% of the time, Pallas kernels for 8%

profile of v26, /device:TPU:1, one launch (start us, length us, event | category | flops | bytes accessed | tf_op | source)
XLA Modules:
  0.0 76.9 jit_solution(15192703298361340618)
XLA Ops:
  0.0 0.1 collective-permute-start
  0.1 0.5 collective-permute-start.1
  0.5 1.2 %copy-done = bf16[32,128,128]{2,1,0:T(8,128)(2,1)S(1)} copy-done((bf16[32,128,128]{2,1,0:T(8,128)(2,1)S(1)}, bf16[32,128,128]{2,1,0:T(8,128)(2,1)}, u32[]{:S(2)}) %copy-start) | copy-done | bytes 1048600
  1.7 0.9 %copy-done.1 = bf16[128,512]{1,0:T(8,128)(2,1)S(1)} copy-done((bf16[128,512]{1,0:T(8,128)(2,1)S(1)}, bf16[128,512]{1,0:T(8,128)(2,1)}, u32[]{:S(2)}) %copy-start.1) | copy-done | bytes 131096
  2.6 0.7 copy-done.4
  3.4 0.7 copy-done.5
  4.0 1.5 %right_own.1 = (bf16[32,32,128]{2,1,0:T(8,128)(2,1)S(1)}, bf16[4096,128]{1,0:T(8,128)(2,1)S(1)}, bf16[64,128]{1,0:T(8,128)(2,1)S(1)}, bf16[64,128]{1,0:T(8,128)(...) custom-call(bf16[32,128,128]{2,1,0:T(8,128)(2,1)S(1)} %copy-done, ...), custom_call_target="tpu_custom_call" | custom-call | tf_op jit(solution)/shard_map/right_own/pallas_call | solution.py:212
  5.5 0.0 collective-permute-done.1.mask
  5.5 0.0 collective-permute-done.pair
  5.5 1.6 %right_twin.1 = (bf16[32,32,256]{2,1,0:T(8,128)(2,1)S(1)}, bf16[4096,128]{1,0:T(8,128)(2,1)S(1)}, f32[1,32,128]{2,1,0:T(8,128)S(1)}) custom-call(bf16[32,128,128]{2,1,0:T(8,128)(2,1)S(1)} %collective-permute-done.pair, s32[32,128]{1,0:T(8,128)S(1)} %collective-permute-done.1.mask, f32[1,128]{1,0:T(1,128)S(1)} %get-tuple-element.44.gain, ...), custom_call_target="tpu_custom_call" | custom-call | tf_op jit(solution)/shard_map/right_twin/pallas_call | solution.py:212
  7.1 2.4 %collective-permute-start.3 = (bf16[32,32,256]{2,1,0:T(8,128)(2,1)S(1)}, bf16[32,32,256]{2,1,0:T(8,128)(2,1)S(1)}, u32[]{:S(2)}, u32[]{:S(2)}) collective-permute-start(bf16[32,32,256]{2,1,0:T(8,128)(2,1)S(1)} %get-tuple-element.55.rest_2_), channel_id=1, source_target_pairs={{0,4},{1,5},{2,6},{3,7},{4,0},{5,1},{6,2},{7,3},{8,12},{9,13},{10,... | collective-permute-start | bytes 1572872 | tf_op jit(solution)/shard_map/end_right_0/ppermute | solution.py:240
  9.5 0.8 %collective-permute-start.6 = (bf16[32,32,256]{2,1,0:T(8,128)(2,1)S(1)}, bf16[32,32,256]{2,1,0:T(8,128)(2,1)S(1)}, u32[]{:S(2)}, u32[]{:S(2)}) collective-permute-start(bf16[32,32,256]{2,1,0:T(8,128)(2,1)S(1)} %get-tuple-element.55.rest_2_), channel_id=1, source_target_pairs={{0,1},{1,0},{2,3},{3,2},{4,8},{5,9},{6,10},{7,11},{8,4},{9,5},{10,... | collective-permute-start | bytes 1572872 | tf_op jit(solution)/shard_map/mid_own_0/ppermute | solution.py:240
  10.3 0.9 %right_neighbour.1 = (bf16[18,32,256]{2,1,0:T(8,128)(2,1)S(1)}, bf16[14,32,256]{2,1,0:T(8,128)(2,1)S(1)}) custom-call(bf16[4096,128]{1,0:T(8,128)(2,1)S(1)} %get-tuple-element.43.normed.normed0, bf16[4096,128]{1,0:T(8,128)(2,1)S(1)} %get-tuple-element.47.normed1, f32[1,32,128]{2,1,0:T(8,128)S(1)} %get-tuple-element.48.valid0, ...), custom_call_target="tpu_custom_call" | custom-call | tf_op jit(solution)/shard_map/right_neighbour/pallas_call | solution.py:212
  11.2 1.3 %collective-permute-start.2 = (bf16[18,32,256]{2,1,0:T(8,128)(2,1)S(1)}, bf16[18,32,256]{2,1,0:T(8,128)(2,1)S(1)}, u32[]{:S(2)}, u32[]{:S(2)}) collective-permute-start(bf16[18,32,256]{2,1,0:T(8,128)(2,1)S(1)} %get-tuple-element.54), channel_id=1, source_target_pairs={{0,2},{1,3},{2,0},{3,1},{4,6},{5,7},{6,4},{7,5},{8,10},{9,11},{10,... | collective-permute-start | bytes 884744 | tf_op jit(solution)/shard_map/cross_right_0/ppermute | solution.py:240
  12.5 0.9 %left.1 = (bf16[32,32,256]{2,1,0:T(8,128)(2,1)S(1)}, bf16[18,32,256]{2,1,0:T(8,128)(2,1)S(1)}, bf16[14,32,256]{2,1,0:T(8,128)(2,1)S(1)}) custom-call(bf16[4096,128]{1,0:T(8,128)(2,1)S(1)} %get-tuple-element.43.normed.normed0, bf16[4096,128]{1,0:T(8,128)(2,1)S(1)} %get-tuple-element.47.normed1, f32[1,32,128]{2,1,0:T(8,128)S(1)} %get-tuple-element.48.valid0, ...), custom_call_target="tpu_custom_call" | custom-call | tf_op jit(solution)/shard_map/left/pallas_call | solution.py:212
  13.4 6.5 %collective-permute-done.2.rest_3_ = bf16[18,32,256]{2,1,0:T(8,128)(2,1)S(1)} collective-permute-done((bf16[18,32,256]{2,1,0:T(8,128)(2,1)S(1)}, bf16[18,32,256]{2,1,0:T(8,128)(2,1)S(1)}, u32[]{:S(2)}, u32[]{:S(2)}) %collective-permute-start.2) | collective-permute-done | bytes 294944 | tf_op jit(solution)/shard_map/cross_right_0/ppermute | solution.py:240
  19.9 0.8 %collective-permute-start.9 = (bf16[18,32,256]{2,1,0:T(8,128)(2,1)S(1)}, bf16[18,32,256]{2,1,0:T(8,128)(2,1)S(1)}, u32[]{:S(2)}, u32[]{:S(2)}) collective-permute-start(bf16[18,32,256]{2,1,0:T(8,128)(2,1)S(1)} %collective-permute-done.2.rest_3_), channel_id=1, source_target_pairs={{0,1},{1,0},{2,3},{3,2},{4,8},{5,9},{6,10},{7,11},{8,4},{9,5},{10,... | collective-permute-start | bytes 884744 | tf_op jit(solution)/shard_map/mid_own_10/ppermute | solution.py:240
  20.7 0.1 collective-permute-start.5
  20.8 0.5 collective-permute-done.3.rest_4_
  21.3 1.1 %collective-permute-start.4 = (bf16[18,32,256]{2,1,0:T(8,128)(2,1)S(1)}, bf16[18,32,256]{2,1,0:T(8,128)(2,1)S(1)}, u32[]{:S(2)}, u32[]{:S(2)}) collective-permute-start(bf16[18,32,256]{2,1,0:T(8,128)(2,1)S(1)} %get-tuple-element.56), channel_id=1, source_target_pairs={{0,2},{1,3},{2,0},{3,1},{4,6},{5,7},{6,4},{7,5},{8,10},{9,11},{10,... | collective-permute-start | bytes 884744 | tf_op jit(solution)/shard_map/cross_left_0/ppermute | solution.py:240
  22.4 0.0 collective-permute-done.6.rest_4_.rest_2_
  22.4 2.2 %collective-permute-start.10 = (bf16[32,32,256]{2,1,0:T(8,128)(2,1)S(1)}, bf16[32,32,256]{2,1,0:T(8,128)(2,1)S(1)}, u32[]{:S(2)}, u32[]{:S(2)}) collective-permute-start(bf16[32,32,256]{2,1,0:T(8,128)(2,1)S(1)} %collective-permute-done.3.rest_4_), channel_id=1, source_target_pairs={{0,1},{1,0},{2,3},{3,2},{4,8},{5,9},{6,10},{7,11},{8,4},{9,5},{10,... | collective-permute-start | bytes 1572872 | tf_op jit(solution)/shard_map/mid_next_0/ppermute | solution.py:240
  24.6 0.4 collective-permute-start.7
  25.0 0.0 collective-permute-done.9.rest_5_
  25.0 3.9 %collective-permute-done.5.rest_5_ = bf16[18,32,256]{2,1,0:T(8,128)(2,1)S(1)} collective-permute-done((bf16[18,32,256]{2,1,0:T(8,128)(2,1)S(1)}, bf16[18,32,256]{2,1,0:T(8,128)(2,1)S(1)}, u32[]{:S(2)}, u32[]{:S(2)}) %collective-permute-start.5) | collective-permute-done | bytes 294944 | tf_op jit(solution)/shard_map/end_right_10/ppermute | solution.py:240
  28.9 0.0 collective-permute-done.4.rest_1_
  28.9 1.2 %collective-permute-start.12 = (bf16[14,32,256]{2,1,0:T(8,128)(2,1)S(1)}, bf16[14,32,256]{2,1,0:T(8,128)(2,1)S(1)}, u32[]{:S(2)}, u32[]{:S(2)}) collective-permute-start(bf16[14,32,256]{2,1,0:T(8,128)(2,1)S(1)} %get-tuple-element.64), channel_id=1, source_target_pairs={{0,2},{1,3},{2,0},{3,1},{4,6},{5,7},{6,4},{7,5},{8,10},{9,11},{10,... | collective-permute-start | bytes 688136 | tf_op jit(solution)/shard_map/cross_right_1/ppermute | solution.py:240
  30.2 0.4 gate.1
  30.6 2.3 %collective-permute-start.11 = (bf16[18,32,256]{2,1,0:T(8,128)(2,1)S(1)}, bf16[18,32,256]{2,1,0:T(8,128)(2,1)S(1)}, u32[]{:S(2)}, u32[]{:S(2)}) collective-permute-start(bf16[18,32,256]{2,1,0:T(8,128)(2,1)S(1)} %collective-permute-done.5.rest_5_), channel_id=1, source_target_pairs={{0,1},{1,0},{2,3},{3,2},{4,8},{5,9},{6,10},{7,11},{8,4},{9,5},{10,... | collective-permute-start | bytes 884744 | tf_op jit(solution)/shard_map/mid_next_10/ppermute | solution.py:240
  32.9 1.2 %collective-permute-done.12.rest_3_ = bf16[14,32,256]{2,1,0:T(8,128)(2,1)S(1)} collective-permute-done((bf16[14,32,256]{2,1,0:T(8,128)(2,1)S(1)}, bf16[14,32,256]{2,1,0:T(8,128)(2,1)S(1)}, u32[]{:S(2)}, u32[]{:S(2)}) %collective-permute-start.12) | collective-permute-done | bytes 229408 | tf_op jit(solution)/shard_map/cross_right_1/ppermute | solution.py:240
  34.1 0.0 collective-permute-done.10.rest_6_.rest_4_
  34.1 1.2 %collective-permute-start.13 = (bf16[14,32,256]{2,1,0:T(8,128)(2,1)S(1)}, bf16[14,32,256]{2,1,0:T(8,128)(2,1)S(1)}, u32[]{:S(2)}, u32[]{:S(2)}) collective-permute-start(bf16[14,32,256]{2,1,0:T(8,128)(2,1)S(1)} %get-tuple-element.65), channel_id=1, source_target_pairs={{0,2},{1,3},{2,0},{3,1},{4,6},{5,7},{6,4},{7,5},{8,10},{9,11},{10,... | collective-permute-start | bytes 688136 | tf_op jit(solution)/shard_map/cross_left_1/ppermute | solution.py:240
  35.4 4.8 %collective-permute-done.7.rest_2_.rest_0_ = bf16[32,32,256]{2,1,0:T(8,128)(2,1)S(1)} collective-permute-done((bf16[32,32,256]{2,1,0:T(8,128)(2,1)S(1)}, bf16[32,32,256]{2,1,0:T(8,128)(2,1)S(1)}, u32[]{:S(2)}, u32[]{:S(2)}) %collective-permute-start.7) | collective-permute-done | bytes 524320 | tf_op jit(solution)/shard_map/end_left_0/ppermute | solution.py:240
  40.2 2.0 %collective-permute-start.18 = (bf16[14,32,256]{2,1,0:T(8,128)(2,1)S(1)}, bf16[14,32,256]{2,1,0:T(8,128)(2,1)S(1)}, u32[]{:S(2)}, u32[]{:S(2)}) collective-permute-start(bf16[14,32,256]{2,1,0:T(8,128)(2,1)S(1)} %collective-permute-done.12.rest_3_), channel_id=1, source_target_pairs={{0,4},{1,5},{2,6},{3,7},{4,0},{5,1},{6,2},{7,3},{8,12},{9,13},{10,... | collective-permute-start | bytes 688136 | tf_op jit(solution)/shard_map/end_right_11/ppermute | solution.py:240
  42.2 3.3 %collective-permute-start.19 = (bf16[14,32,256]{2,1,0:T(8,128)(2,1)S(1)}, bf16[14,32,256]{2,1,0:T(8,128)(2,1)S(1)}, u32[]{:S(2)}, u32[]{:S(2)}) collective-permute-start(bf16[14,32,256]{2,1,0:T(8,128)(2,1)S(1)} %collective-permute-done.12.rest_3_), channel_id=1, source_target_pairs={{0,1},{1,0},{2,3},{3,2},{4,8},{5,9},{6,10},{7,11},{8,4},{9,5},{10,... | collective-permute-start | bytes 688136 | tf_op jit(solution)/shard_map/mid_own_11/ppermute | solution.py:240
  45.5 1.0 %collective-permute-done.8.rest_3_ = bf16[18,32,256]{2,1,0:T(8,128)(2,1)S(1)} collective-permute-done((bf16[18,32,256]{2,1,0:T(8,128)(2,1)S(1)}, bf16[18,32,256]{2,1,0:T(8,128)(2,1)S(1)}, u32[]{:S(2)}, u32[]{:S(2)}) %collective-permute-start.8) | collective-permute-done | bytes 294944 | tf_op jit(solution)/shard_map/end_left_10/ppermute | solution.py:240
  46.5 0.6 away.2
  47.1 0.8 %collective-permute-start.14 = (bf16[18,32,256]{2,1,0:T(8,128)(2,1)S(1)}, bf16[18,32,256]{2,1,0:T(8,128)(2,1)S(1)}, u32[]{:S(2)}, u32[]{:S(2)}) collective-permute-start(bf16[18,32,256]{2,1,0:T(8,128)(2,1)S(1)} %get-tuple-element.67), channel_id=1, source_target_pairs={{0,4},{1,5},{2,6},{3,7},{4,0},{5,1},{6,2},{7,3},{8,12},{9,13},{10,... | collective-permute-start | bytes 884744 | tf_op jit(solution)/shard_map/left_11_and_products_back_0/ppermute | solution.py:240
  47.9 3.5 %collective-permute-done.18.rest_5_ = bf16[14,32,256]{2,1,0:T(8,128)(2,1)S(1)} collective-permute-done((bf16[14,32,256]{2,1,0:T(8,128)(2,1)S(1)}, bf16[14,32,256]{2,1,0:T(8,128)(2,1)S(1)}, u32[]{:S(2)}, u32[]{:S(2)}) %collective-permute-start.18) | collective-permute-done | bytes 229408 | tf_op jit(solution)/shard_map/end_right_11/ppermute | solution.py:240
  51.4 0.0 collective-permute-done.19.rest_3_
  51.4 1.9 %collective-permute-start.20 = (bf16[14,32,256]{2,1,0:T(8,128)(2,1)S(1)}, bf16[14,32,256]{2,1,0:T(8,128)(2,1)S(1)}, u32[]{:S(2)}, u32[]{:S(2)}) collective-permute-start(bf16[14,32,256]{2,1,0:T(8,128)(2,1)S(1)} %collective-permute-done.18.rest_5_), channel_id=1, source_target_pairs={{0,1},{1,0},{2,3},{3,2},{4,8},{5,9},{6,10},{7,11},{8,4},{9,5},{10,... | collective-permute-start | bytes 688136 | tf_op jit(solution)/shard_map/mid_next_11/ppermute | solution.py:240
  53.4 0.6 near.2
  54.0 0.5 near.3
  54.5 3.2 %collective-permute-done.14.end.rest_1_ = bf16[18,32,256]{2,1,0:T(8,128)(2,1)S(1)} collective-permute-done((bf16[18,32,256]{2,1,0:T(8,128)(2,1)S(1)}, bf16[18,32,256]{2,1,0:T(8,128)(2,1)S(1)}, u32[]{:S(2)}, u32[]{:S(2)}) %collective-permute-start.14) | collective-permute-done | bytes 294944 | tf_op jit(solution)/shard_map/left_11_and_products_back_0/ppermute | solution.py:240
  57.7 0.1 hand_out.2
  57.8 0.0 collective-permute-done.20.rest_5_
  57.8 0.5 away_for_ends.1
  58.4 0.0 copy-start.6
  58.4 0.1 collective-permute-start.21
  58.5 2.7 %collective-permute-start.15 = (bf16[18,32,128]{2,1,0:T(8,128)(2,1)S(1)}, bf16[18,32,128]{2,1,0:T(8,128)(2,1)S(1)}, u32[]{:S(2)}, u32[]{:S(2)}) collective-permute-start(bf16[18,32,128]{2,1,0:T(8,128)(2,1)S(1)} %get-tuple-element.69), channel_id=1, source_target_pairs={{0,1},{1,0},{2,3},{3,2},{4,5},{5,4},{6,7},{7,6},{8,9},{9,8},{10,11... | collective-permute-start | bytes 442376 | tf_op jit(solution)/shard_map/return_01/ppermute | solution.py:240
  61.2 1.2 %collective-permute-start.16 = (bf16[18,32,128]{2,1,0:T(8,128)(2,1)S(1)}, bf16[18,32,128]{2,1,0:T(8,128)(2,1)S(1)}, u32[]{:S(2)}, u32[]{:S(2)}) collective-permute-start(bf16[18,32,128]{2,1,0:T(8,128)(2,1)S(1)} %get-tuple-element.70), channel_id=1, source_target_pairs={{0,2},{1,3},{2,0},{3,1},{4,6},{5,7},{6,4},{7,5},{8,10},{9,11},{10,... | collective-permute-start | bytes 442376 | tf_op jit(solution)/shard_map/return_02/ppermute | solution.py:240
  62.5 0.4 collective-permute-start.17
  62.9 0.5 away.3.far
  63.4 1.0 %collective-permute-done.21.end = bf16[14,64,128]{2,1,0:T(8,128)(2,1)S(1)} collective-permute-done((bf16[14,64,128]{2,1,0:T(8,128)(2,1)S(1)}, bf16[14,64,128]{2,1,0:T(8,128)(2,1)S(1)}, u32[]{:S(2)}, u32[]{:S(2)}) %collective-permute-start.21) | collective-permute-done | bytes 229408 | tf_op jit(solution)/shard_map/products_back_1/ppermute | solution.py:240
  64.4 0.1 hand_out.3
  64.4 2.2 %collective-permute-start.22 = (bf16[14,32,128]{2,1,0:T(8,128)(2,1)S(1)}, bf16[14,32,128]{2,1,0:T(8,128)(2,1)S(1)}, u32[]{:S(2)}, u32[]{:S(2)}) collective-permute-start(bf16[14,32,128]{2,1,0:T(8,128)(2,1)S(1)} %get-tuple-element.78), channel_id=1, source_target_pairs={{0,1},{1,0},{2,3},{3,2},{4,5},{5,4},{6,7},{7,6},{8,9},{9,8},{10,11... | collective-permute-start | bytes 344072 | tf_op jit(solution)/shard_map/return_11/ppermute | solution.py:240
  66.6 1.3 %collective-permute-start.23 = (bf16[14,32,128]{2,1,0:T(8,128)(2,1)S(1)}, bf16[14,32,128]{2,1,0:T(8,128)(2,1)S(1)}, u32[]{:S(2)}, u32[]{:S(2)}) collective-permute-start(bf16[14,32,128]{2,1,0:T(8,128)(2,1)S(1)} %get-tuple-element.79), channel_id=1, source_target_pairs={{0,2},{1,3},{2,0},{3,1},{4,6},{5,7},{6,4},{7,5},{8,10},{9,11},{10,... | collective-permute-start | bytes 344072 | tf_op jit(solution)/shard_map/return_12/ppermute | solution.py:240
  67.9 0.5 collective-permute-start.24
  68.3 0.0 collective-permute-done.16.rest_2_
  68.3 2.0 %collective-permute-done.17.rest_3_ = bf16[18,32,128]{2,1,0:T(8,128)(2,1)S(1)} collective-permute-done((bf16[18,32,128]{2,1,0:T(8,128)(2,1)S(1)}, bf16[18,32,128]{2,1,0:T(8,128)(2,1)S(1)}, u32[]{:S(2)}, u32[]{:S(2)}) %collective-permute-start.17) | collective-permute-done | bytes 147488 | tf_op jit(solution)/shard_map/return_03/ppermute | solution.py:240
  70.3 0.0 collective-permute-done.22.rest_5_
  70.3 2.0 %collective-permute-done.23.rest_6_ = bf16[14,32,128]{2,1,0:T(8,128)(2,1)S(1)} collective-permute-done((bf16[14,32,128]{2,1,0:T(8,128)(2,1)S(1)}, bf16[14,32,128]{2,1,0:T(8,128)(2,1)S(1)}, u32[]{:S(2)}, u32[]{:S(2)}) %collective-permute-start.23) | collective-permute-done | bytes 114720 | tf_op jit(solution)/shard_map/return_12/ppermute | solution.py:240
  72.3 2.6 %collective-permute-done.24.rest_7_ = bf16[14,32,128]{2,1,0:T(8,128)(2,1)S(1)} collective-permute-done((bf16[14,32,128]{2,1,0:T(8,128)(2,1)S(1)}, bf16[14,32,128]{2,1,0:T(8,128)(2,1)S(1)}, u32[]{:S(2)}, u32[]{:S(2)}) %collective-permute-start.24) | collective-permute-done | bytes 114720 | tf_op jit(solution)/shard_map/return_13/ppermute | solution.py:240
  74.9 2.0 %update.1 = bf16[32,128,128]{2,1,0:T(8,128)(2,1)} custom-call(f32[1,128]{1,0:T(1,128)S(1)} %bitcast.3, bf16[128,128]{1,0:T(8,128)(2,1)S(1)} %copy-done.3, f32[32,128,128]{2,1,0:T(8,128)S(1)} %gate.1, bf16[18,32,128]{2,1,0:T(8,128)(2,1)S(1)} %get-tuple-element.68.rest_0_, bf16[18,32,128]{2,1,0:T(8,128)(2,1)S(1)} %collective-permute-done.15.rest_1_, ...), custom_call_target="tpu_custom_call" | custom-call | tf_op jit(solution)/shard_map/update/pallas_call | solution.py:212
  (13 shorter events, 0.0 us)
Async XLA Ops:
  0.0 5.5 %collective-permute-start = (bf16[32,128,128]{2,1,0:T(8,128)(2,1)}, bf16[32,128,128]{2,1,0:T(8,128)(2,1)S(1)}, u32[]{:S(2)}, u32[]{:S(2)}) collective-permute-start(bf16[32,128,128]{2,1,0:T(8,128)(2,1)} %pair.1), channel_id=1, source_target_pairs={{0,1},{1,0},{2,3},{3,2},{4,5},{5,4},{6,7},{7,6},{8,9},{9,8},{10,11... | collective-permute-start | bytes 3145736 | tf_op jit(solution)/shard_map/pair/ppermute | solution.py:240
  0.1 5.5 %collective-permute-start.1 = (s32[32,128]{1,0:T(8,128)}, s32[32,128]{1,0:T(8,128)S(1)}, u32[]{:S(2)}, u32[]{:S(2)}) collective-permute-start(s32[32,128]{1,0:T(8,128)} %mask.1), channel_id=1, source_target_pairs={{0,1},{1,0},{2,3},{3,2},{4,5},{5,4},{6,7},{7,6},{8,9},{9,8},{10,11... | collective-permute-start | bytes 49160 | tf_op jit(solution)/shard_map/mask/ppermute | solution.py:240
  0.5 1.2 %copy-start = (bf16[32,128,128]{2,1,0:T(8,128)(2,1)S(1)}, bf16[32,128,128]{2,1,0:T(8,128)(2,1)}, u32[]{:S(2)}) copy-start(bf16[32,128,128]{2,1,0:T(8,128)(2,1)} %pair.1) | copy-start | bytes 3145732
  1.7 0.9 %copy-start.1 = (bf16[128,512]{1,0:T(8,128)(2,1)S(1)}, bf16[128,512]{1,0:T(8,128)(2,1)}, u32[]{:S(2)}) copy-start(bf16[128,512]{1,0:T(8,128)(2,1)} %weight.3) | copy-start | bytes 393220
  2.6 0.7 copy-start.4
  3.4 0.7 copy-start.5
  7.1 14.2 %collective-permute-start.3 = (bf16[32,32,256]{2,1,0:T(8,128)(2,1)S(1)}, bf16[32,32,256]{2,1,0:T(8,128)(2,1)S(1)}, u32[]{:S(2)}, u32[]{:S(2)}) collective-permute-start(bf16[32,32,256]{2,1,0:T(8,128)(2,1)S(1)} %get-tuple-element.55.rest_2_), channel_id=1, source_target_pairs={{0,4},{1,5},{2,6},{3,7},{4,0},{5,1},{6,2},{7,3},{8,12},{9,13},{10,... | collective-permute-start | bytes 1572872 | tf_op jit(solution)/shard_map/end_right_0/ppermute | solution.py:240
  9.5 12.9 %collective-permute-start.6 = (bf16[32,32,256]{2,1,0:T(8,128)(2,1)S(1)}, bf16[32,32,256]{2,1,0:T(8,128)(2,1)S(1)}, u32[]{:S(2)}, u32[]{:S(2)}) collective-permute-start(bf16[32,32,256]{2,1,0:T(8,128)(2,1)S(1)} %get-tuple-element.55.rest_2_), channel_id=1, source_target_pairs={{0,1},{1,0},{2,3},{3,2},{4,8},{5,9},{6,10},{7,11},{8,4},{9,5},{10,... | collective-permute-start | bytes 1572872 | tf_op jit(solution)/shard_map/mid_own_0/ppermute | solution.py:240
  10.3 19.9 %copy-start.2 = (bf16[128,128]{1,0:T(8,128)(2,1)S(1)}, bf16[128,128]{1,0:T(8,128)(2,1)}, u32[]{:S(2)}) copy-start(bf16[128,128]{1,0:T(8,128)(2,1)} %weight.4) | copy-start | bytes 98308
  11.2 8.7 %collective-permute-start.2 = (bf16[18,32,256]{2,1,0:T(8,128)(2,1)S(1)}, bf16[18,32,256]{2,1,0:T(8,128)(2,1)S(1)}, u32[]{:S(2)}, u32[]{:S(2)}) collective-permute-start(bf16[18,32,256]{2,1,0:T(8,128)(2,1)S(1)} %get-tuple-element.54), channel_id=1, source_target_pairs={{0,2},{1,3},{2,0},{3,1},{4,6},{5,7},{6,4},{7,5},{8,10},{9,11},{10,... | collective-permute-start | bytes 884744 | tf_op jit(solution)/shard_map/cross_right_0/ppermute | solution.py:240
  19.9 5.1 %collective-permute-start.9 = (bf16[18,32,256]{2,1,0:T(8,128)(2,1)S(1)}, bf16[18,32,256]{2,1,0:T(8,128)(2,1)S(1)}, u32[]{:S(2)}, u32[]{:S(2)}) collective-permute-start(bf16[18,32,256]{2,1,0:T(8,128)(2,1)S(1)} %collective-permute-done.2.rest_3_), channel_id=1, source_target_pairs={{0,1},{1,0},{2,3},{3,2},{4,8},{5,9},{6,10},{7,11},{8,4},{9,5},{10,... | collective-permute-start | bytes 884744 | tf_op jit(solution)/shard_map/mid_own_10/ppermute | solution.py:240
  20.7 8.2 %collective-permute-start.5 = (bf16[18,32,256]{2,1,0:T(8,128)(2,1)S(1)}, bf16[18,32,256]{2,1,0:T(8,128)(2,1)S(1)}, u32[]{:S(2)}, u32[]{:S(2)}) collective-permute-start(bf16[18,32,256]{2,1,0:T(8,128)(2,1)S(1)} %collective-permute-done.2.rest_3_), channel_id=1, source_target_pairs={{0,4},{1,5},{2,6},{3,7},{4,0},{5,1},{6,2},{7,3},{8,12},{9,13},{10,... | collective-permute-start | bytes 884744 | tf_op jit(solution)/shard_map/end_right_10/ppermute | solution.py:240
  21.3 7.6 %collective-permute-start.4 = (bf16[18,32,256]{2,1,0:T(8,128)(2,1)S(1)}, bf16[18,32,256]{2,1,0:T(8,128)(2,1)S(1)}, u32[]{:S(2)}, u32[]{:S(2)}) collective-permute-start(bf16[18,32,256]{2,1,0:T(8,128)(2,1)S(1)} %get-tuple-element.56), channel_id=1, source_target_pairs={{0,2},{1,3},{2,0},{3,1},{4,6},{5,7},{6,4},{7,5},{8,10},{9,11},{10,... | collective-permute-start | bytes 884744 | tf_op jit(solution)/shard_map/cross_left_0/ppermute | solution.py:240
  22.4 11.7 %collective-permute-start.10 = (bf16[32,32,256]{2,1,0:T(8,128)(2,1)S(1)}, bf16[32,32,256]{2,1,0:T(8,128)(2,1)S(1)}, u32[]{:S(2)}, u32[]{:S(2)}) collective-permute-start(bf16[32,32,256]{2,1,0:T(8,128)(2,1)S(1)} %collective-permute-done.3.rest_4_), channel_id=1, source_target_pairs={{0,1},{1,0},{2,3},{3,2},{4,8},{5,9},{6,10},{7,11},{8,4},{9,5},{10,... | collective-permute-start | bytes 1572872 | tf_op jit(solution)/shard_map/mid_next_0/ppermute | solution.py:240
  24.6 15.6 %collective-permute-start.7 = (bf16[32,32,256]{2,1,0:T(8,128)(2,1)S(1)}, bf16[32,32,256]{2,1,0:T(8,128)(2,1)S(1)}, u32[]{:S(2)}, u32[]{:S(2)}) collective-permute-start(bf16[32,32,256]{2,1,0:T(8,128)(2,1)S(1)} %get-tuple-element.76.rest_0_), channel_id=1, source_target_pairs={{0,4},{1,5},{2,6},{3,7},{4,0},{5,1},{6,2},{7,3},{8,12},{9,13},{10,... | collective-permute-start | bytes 1572872 | tf_op jit(solution)/shard_map/end_left_0/ppermute | solution.py:240
  28.9 5.2 %collective-permute-start.12 = (bf16[14,32,256]{2,1,0:T(8,128)(2,1)S(1)}, bf16[14,32,256]{2,1,0:T(8,128)(2,1)S(1)}, u32[]{:S(2)}, u32[]{:S(2)}) collective-permute-start(bf16[14,32,256]{2,1,0:T(8,128)(2,1)S(1)} %get-tuple-element.64), channel_id=1, source_target_pairs={{0,2},{1,3},{2,0},{3,1},{4,6},{5,7},{6,4},{7,5},{8,10},{9,11},{10,... | collective-permute-start | bytes 688136 | tf_op jit(solution)/shard_map/cross_right_1/ppermute | solution.py:240
  30.6 14.9 %collective-permute-start.11 = (bf16[18,32,256]{2,1,0:T(8,128)(2,1)S(1)}, bf16[18,32,256]{2,1,0:T(8,128)(2,1)S(1)}, u32[]{:S(2)}, u32[]{:S(2)}) collective-permute-start(bf16[18,32,256]{2,1,0:T(8,128)(2,1)S(1)} %collective-permute-done.5.rest_5_), channel_id=1, source_target_pairs={{0,1},{1,0},{2,3},{3,2},{4,8},{5,9},{6,10},{7,11},{8,4},{9,5},{10,... | collective-permute-start | bytes 884744 | tf_op jit(solution)/shard_map/mid_next_10/ppermute | solution.py:240
  32.9 13.6 %collective-permute-start.8 = (bf16[18,32,256]{2,1,0:T(8,128)(2,1)S(1)}, bf16[18,32,256]{2,1,0:T(8,128)(2,1)S(1)}, u32[]{:S(2)}, u32[]{:S(2)}) collective-permute-start(bf16[18,32,256]{2,1,0:T(8,128)(2,1)S(1)} %collective-permute-done.4.rest_1_), channel_id=1, source_target_pairs={{0,4},{1,5},{2,6},{3,7},{4,0},{5,1},{6,2},{7,3},{8,12},{9,13},{10,... | collective-permute-start | bytes 884744 | tf_op jit(solution)/shard_map/end_left_10/ppermute | solution.py:240
  34.1 12.4 %collective-permute-start.13 = (bf16[14,32,256]{2,1,0:T(8,128)(2,1)S(1)}, bf16[14,32,256]{2,1,0:T(8,128)(2,1)S(1)}, u32[]{:S(2)}, u32[]{:S(2)}) collective-permute-start(bf16[14,32,256]{2,1,0:T(8,128)(2,1)S(1)} %get-tuple-element.65), channel_id=1, source_target_pairs={{0,2},{1,3},{2,0},{3,1},{4,6},{5,7},{6,4},{7,5},{8,10},{9,11},{10,... | collective-permute-start | bytes 688136 | tf_op jit(solution)/shard_map/cross_left_1/ppermute | solution.py:240
  40.2 11.2 %collective-permute-start.18 = (bf16[14,32,256]{2,1,0:T(8,128)(2,1)S(1)}, bf16[14,32,256]{2,1,0:T(8,128)(2,1)S(1)}, u32[]{:S(2)}, u32[]{:S(2)}) collective-permute-start(bf16[14,32,256]{2,1,0:T(8,128)(2,1)S(1)} %collective-permute-done.12.rest_3_), channel_id=1, source_target_pairs={{0,4},{1,5},{2,6},{3,7},{4,0},{5,1},{6,2},{7,3},{8,12},{9,13},{10,... | collective-permute-start | bytes 688136 | tf_op jit(solution)/shard_map/end_right_11/ppermute | solution.py:240
  42.2 9.2 %collective-permute-start.19 = (bf16[14,32,256]{2,1,0:T(8,128)(2,1)S(1)}, bf16[14,32,256]{2,1,0:T(8,128)(2,1)S(1)}, u32[]{:S(2)}, u32[]{:S(2)}) collective-permute-start(bf16[14,32,256]{2,1,0:T(8,128)(2,1)S(1)} %collective-permute-done.12.rest_3_), channel_id=1, source_target_pairs={{0,1},{1,0},{2,3},{3,2},{4,8},{5,9},{6,10},{7,11},{8,4},{9,5},{10,... | collective-permute-start | bytes 688136 | tf_op jit(solution)/shard_map/mid_own_11/ppermute | solution.py:240
  47.1 10.6 %collective-permute-start.14 = (bf16[18,32,256]{2,1,0:T(8,128)(2,1)S(1)}, bf16[18,32,256]{2,1,0:T(8,128)(2,1)S(1)}, u32[]{:S(2)}, u32[]{:S(2)}) collective-permute-start(bf16[18,32,256]{2,1,0:T(8,128)(2,1)S(1)} %get-tuple-element.67), channel_id=1, source_target_pairs={{0,4},{1,5},{2,6},{3,7},{4,0},{5,1},{6,2},{7,3},{8,12},{9,13},{10,... | collective-permute-start | bytes 884744 | tf_op jit(solution)/shard_map/left_11_and_products_back_0/ppermute | solution.py:240
  51.4 6.4 %collective-permute-start.20 = (bf16[14,32,256]{2,1,0:T(8,128)(2,1)S(1)}, bf16[14,32,256]{2,1,0:T(8,128)(2,1)S(1)}, u32[]{:S(2)}, u32[]{:S(2)}) collective-permute-start(bf16[14,32,256]{2,1,0:T(8,128)(2,1)S(1)} %collective-permute-done.18.rest_5_), channel_id=1, source_target_pairs={{0,1},{1,0},{2,3},{3,2},{4,8},{5,9},{6,10},{7,11},{8,4},{9,5},{10,... | collective-permute-start | bytes 688136 | tf_op jit(solution)/shard_map/mid_next_11/ppermute | solution.py:240
  58.4 16.5 %copy-start.3 = (bf16[128,128]{1,0:T(8,128)(2,1)S(1)}, bf16[128,128]{1,0:T(8,128)(2,1)}, u32[]{:S(2)}) copy-start(bf16[128,128]{1,0:T(8,128)(2,1)} %weight.5) | copy-start | bytes 98308
  58.4 16.5 %copy-start.6 = (f32[128]{0:T(128)S(1)}, f32[128]{0:T(128)}, u32[]{:S(2)}) copy-start(f32[128]{0:T(128)} %param.12) | copy-start | bytes 1540
  58.4 6.0 %collective-permute-start.21 = (bf16[14,64,128]{2,1,0:T(8,128)(2,1)S(1)}, bf16[14,64,128]{2,1,0:T(8,128)(2,1)S(1)}, u32[]{:S(2)}, u32[]{:S(2)}) collective-permute-start(bf16[14,64,128]{2,1,0:T(8,128)(2,1)S(1)} %away_for_ends.1), channel_id=1, source_target_pairs={{0,4},{1,5},{2,6},{3,7},{4,0},{5,1},{6,2},{7,3},{8,12},{9,13},{10,... | collective-permute-start | bytes 688136 | tf_op jit(solution)/shard_map/products_back_1/ppermute | solution.py:240
  58.5 9.4 %collective-permute-start.15 = (bf16[18,32,128]{2,1,0:T(8,128)(2,1)S(1)}, bf16[18,32,128]{2,1,0:T(8,128)(2,1)S(1)}, u32[]{:S(2)}, u32[]{:S(2)}) collective-permute-start(bf16[18,32,128]{2,1,0:T(8,128)(2,1)S(1)} %get-tuple-element.69), channel_id=1, source_target_pairs={{0,1},{1,0},{2,3},{3,2},{4,5},{5,4},{6,7},{7,6},{8,9},{9,8},{10,11... | collective-permute-start | bytes 442376 | tf_op jit(solution)/shard_map/return_01/ppermute | solution.py:240
  61.2 7.1 %collective-permute-start.16 = (bf16[18,32,128]{2,1,0:T(8,128)(2,1)S(1)}, bf16[18,32,128]{2,1,0:T(8,128)(2,1)S(1)}, u32[]{:S(2)}, u32[]{:S(2)}) collective-permute-start(bf16[18,32,128]{2,1,0:T(8,128)(2,1)S(1)} %get-tuple-element.70), channel_id=1, source_target_pairs={{0,2},{1,3},{2,0},{3,1},{4,6},{5,7},{6,4},{7,5},{8,10},{9,11},{10,... | collective-permute-start | bytes 442376 | tf_op jit(solution)/shard_map/return_02/ppermute | solution.py:240
  62.5 7.9 %collective-permute-start.17 = (bf16[18,32,128]{2,1,0:T(8,128)(2,1)S(1)}, bf16[18,32,128]{2,1,0:T(8,128)(2,1)S(1)}, u32[]{:S(2)}, u32[]{:S(2)}) collective-permute-start(bf16[18,32,128]{2,1,0:T(8,128)(2,1)S(1)} %get-tuple-element.71), channel_id=1, source_target_pairs={{0,3},{1,2},{2,1},{3,0},{4,7},{5,6},{6,5},{7,4},{8,11},{9,10},{10,... | collective-permute-start | bytes 442376 | tf_op jit(solution)/shard_map/return_03/ppermute | solution.py:240
  64.4 5.9 %collective-permute-start.22 = (bf16[14,32,128]{2,1,0:T(8,128)(2,1)S(1)}, bf16[14,32,128]{2,1,0:T(8,128)(2,1)S(1)}, u32[]{:S(2)}, u32[]{:S(2)}) collective-permute-start(bf16[14,32,128]{2,1,0:T(8,128)(2,1)S(1)} %get-tuple-element.78), channel_id=1, source_target_pairs={{0,1},{1,0},{2,3},{3,2},{4,5},{5,4},{6,7},{7,6},{8,9},{9,8},{10,11... | collective-permute-start | bytes 344072 | tf_op jit(solution)/shard_map/return_11/ppermute | solution.py:240
  66.6 5.7 %collective-permute-start.23 = (bf16[14,32,128]{2,1,0:T(8,128)(2,1)S(1)}, bf16[14,32,128]{2,1,0:T(8,128)(2,1)S(1)}, u32[]{:S(2)}, u32[]{:S(2)}) collective-permute-start(bf16[14,32,128]{2,1,0:T(8,128)(2,1)S(1)} %get-tuple-element.79), channel_id=1, source_target_pairs={{0,2},{1,3},{2,0},{3,1},{4,6},{5,7},{6,4},{7,5},{8,10},{9,11},{10,... | collective-permute-start | bytes 344072 | tf_op jit(solution)/shard_map/return_12/ppermute | solution.py:240
  67.9 7.0 %collective-permute-start.24 = (bf16[14,32,128]{2,1,0:T(8,128)(2,1)S(1)}, bf16[14,32,128]{2,1,0:T(8,128)(2,1)S(1)}, u32[]{:S(2)}, u32[]{:S(2)}) collective-permute-start(bf16[14,32,128]{2,1,0:T(8,128)(2,1)S(1)} %get-tuple-element.80), channel_id=1, source_target_pairs={{0,3},{1,2},{2,1},{3,0},{4,7},{5,6},{6,5},{7,4},{8,11},{9,10},{10,... | collective-permute-start | bytes 344072 | tf_op jit(solution)/shard_map/return_13/ppermute | solution.py:240

commit v27 on v26

--- a/solution.py
+++ b/solution.py
@@ -11,7 +11,7 @@
 F32, BF16 = jnp.float32, jnp.bfloat16
 LANES = 128
 SPARE = 6 * 1024 * 1024
-SHARES = (9, 7)
+SHARES = (17, 15)
 NT = (((1,), (1,)), ((), ()))
 TN = (((0,), (0,)), ((), ()))
 VMEM = pl.BlockSpec(memory_space=pltpu.VMEM)

time: 77.4 us -> 78.6 us (1.016)
  starting transfers between devices: 30.8 us -> 39 us
  waiting for transfers between devices: 32.2 us -> 25.1 us
    ppermute x25, starting transfers between devices: 30.8 us -> 39 us  [send(): return lax.ppermute(x, ('row', 'chan'), pairs)]
    ppermute x25, waiting for transfers between devices: 32.2 us -> 25.1 us  [send(): return lax.ppermute(x, ('row', 'chan'), pairs)]
  transfers between devices with their start and end apart: 25 -> 25, of which waited for: 12 -> 11; matrix products, arithmetic and copies ran while one was open for 0% -> 0% of each run, Pallas kernels for 8% -> 8%
where the time goes in v27:
time: 78.6 us; the launch traced here: 78.1 us
  starting transfers between devices  39 us (50%)
  waiting for transfers between devices  25.1 us (32%)
  Pallas kernels  10.3 us (13%)
  local copies, waits for them, and re-layouts  3.51 us (4%)
    ppermute x25, starting transfers between devices, send(): return lax.ppermute(x, ('row', 'chan'), pairs)  39 us
    ppermute x25, waiting for transfers between devices, send(): return lax.ppermute(x, ('row', 'chan'), pairs)  25.1 us
    pallas_call x13, Pallas kernels, call(): pl.pallas_call(body, out_shape=out_shape, in_specs=in_specs, out_specs=ou...  10.3 us
    unnamed x14, local copies, waits for them, and re-layouts  3.51 us
  transfers between devices with their start and end apart: 25, of which 11 were waited for; matrix products, arithmetic and copies ran while one was open for 0% of the time, Pallas kernels for 8%

profile of v27, /device:TPU:1, one launch (start us, length us, event | category | flops | bytes accessed | tf_op | source)
XLA Modules:
  0.0 78.1 jit_solution(3922017029156064486)
XLA Ops:
  0.0 0.1 collective-permute-start
  0.1 0.5 collective-permute-start.1
  0.5 1.2 %copy-done = bf16[32,128,128]{2,1,0:T(8,128)(2,1)S(1)} copy-done((bf16[32,128,128]{2,1,0:T(8,128)(2,1)S(1)}, bf16[32,128,128]{2,1,0:T(8,128)(2,1)}, u32[]{:S(2)}) %copy-start) | copy-done | bytes 1048600
  1.7 0.9 %copy-done.1 = bf16[128,512]{1,0:T(8,128)(2,1)S(1)} copy-done((bf16[128,512]{1,0:T(8,128)(2,1)S(1)}, bf16[128,512]{1,0:T(8,128)(2,1)}, u32[]{:S(2)}) %copy-start.1) | copy-done | bytes 131096
  2.6 0.7 copy-done.4
  3.4 0.7 copy-done.5
  4.0 1.5 %right_own.1 = (bf16[32,32,128]{2,1,0:T(8,128)(2,1)S(1)}, bf16[4096,128]{1,0:T(8,128)(2,1)S(1)}, bf16[64,128]{1,0:T(8,128)(2,1)S(1)}, bf16[64,128]{1,0:T(8,128)(...) custom-call(bf16[32,128,128]{2,1,0:T(8,128)(2,1)S(1)} %copy-done, ...), custom_call_target="tpu_custom_call" | custom-call | tf_op jit(solution)/shard_map/right_own/pallas_call | solution.py:212
  5.5 0.0 collective-permute-done.1.mask
  5.5 0.0 collective-permute-done.pair
  5.5 1.6 %right_twin.1 = (bf16[32,32,256]{2,1,0:T(8,128)(2,1)S(1)}, bf16[4096,128]{1,0:T(8,128)(2,1)S(1)}, f32[1,32,128]{2,1,0:T(8,128)S(1)}) custom-call(bf16[32,128,128]{2,1,0:T(8,128)(2,1)S(1)} %collective-permute-done.pair, s32[32,128]{1,0:T(8,128)S(1)} %collective-permute-done.1.mask, f32[1,128]{1,0:T(1,128)S(1)} %get-tuple-element.44.gain, ...), custom_call_target="tpu_custom_call" | custom-call | tf_op jit(solution)/shard_map/right_twin/pallas_call | solution.py:212
  7.1 2.4 %collective-permute-start.3 = (bf16[32,32,256]{2,1,0:T(8,128)(2,1)S(1)}, bf16[32,32,256]{2,1,0:T(8,128)(2,1)S(1)}, u32[]{:S(2)}, u32[]{:S(2)}) collective-permute-start(bf16[32,32,256]{2,1,0:T(8,128)(2,1)S(1)} %get-tuple-element.55.rest_2_), channel_id=1, source_target_pairs={{0,4},{1,5},{2,6},{3,7},{4,0},{5,1},{6,2},{7,3},{8,12},{9,13},{10,... | collective-permute-start | bytes 1572872 | tf_op jit(solution)/shard_map/end_right_0/ppermute | solution.py:240
  9.5 0.8 %collective-permute-start.6 = (bf16[32,32,256]{2,1,0:T(8,128)(2,1)S(1)}, bf16[32,32,256]{2,1,0:T(8,128)(2,1)S(1)}, u32[]{:S(2)}, u32[]{:S(2)}) collective-permute-start(bf16[32,32,256]{2,1,0:T(8,128)(2,1)S(1)} %get-tuple-element.55.rest_2_), channel_id=1, source_target_pairs={{0,1},{1,0},{2,3},{3,2},{4,8},{5,9},{6,10},{7,11},{8,4},{9,5},{10,... | collective-permute-start | bytes 1572872 | tf_op jit(solution)/shard_map/mid_own_0/ppermute | solution.py:240
  10.3 0.9 %right_neighbour.1 = (bf16[17,32,256]{2,1,0:T(8,128)(2,1)S(1)}, bf16[15,32,256]{2,1,0:T(8,128)(2,1)S(1)}) custom-call(bf16[4096,128]{1,0:T(8,128)(2,1)S(1)} %get-tuple-element.43.normed.normed0, bf16[4096,128]{1,0:T(8,128)(2,1)S(1)} %get-tuple-element.47.normed1, f32[1,32,128]{2,1,0:T(8,128)S(1)} %get-tuple-element.48.valid0, ...), custom_call_target="tpu_custom_call" | custom-call | tf_op jit(solution)/shard_map/right_neighbour/pallas_call | solution.py:212
  11.2 1.3 %collective-permute-start.2 = (bf16[17,32,256]{2,1,0:T(8,128)(2,1)S(1)}, bf16[17,32,256]{2,1,0:T(8,128)(2,1)S(1)}, u32[]{:S(2)}, u32[]{:S(2)}) collective-permute-start(bf16[17,32,256]{2,1,0:T(8,128)(2,1)S(1)} %get-tuple-element.54), channel_id=1, source_target_pairs={{0,2},{1,3},{2,0},{3,1},{4,6},{5,7},{6,4},{7,5},{8,10},{9,11},{10,... | collective-permute-start | bytes 835592 | tf_op jit(solution)/shard_map/cross_right_0/ppermute | solution.py:240
  12.5 0.9 %left.1 = (bf16[32,32,256]{2,1,0:T(8,128)(2,1)S(1)}, bf16[17,32,256]{2,1,0:T(8,128)(2,1)S(1)}, bf16[15,32,256]{2,1,0:T(8,128)(2,1)S(1)}) custom-call(bf16[4096,128]{1,0:T(8,128)(2,1)S(1)} %get-tuple-element.43.normed.normed0, bf16[4096,128]{1,0:T(8,128)(2,1)S(1)} %get-tuple-element.47.normed1, f32[1,32,128]{2,1,0:T(8,128)S(1)} %get-tuple-element.48.valid0, ...), custom_call_target="tpu_custom_call" | custom-call | tf_op jit(solution)/shard_map/left/pallas_call | solution.py:212
  13.4 6.2 %collective-permute-done.2.rest_3_ = bf16[17,32,256]{2,1,0:T(8,128)(2,1)S(1)} collective-permute-done((bf16[17,32,256]{2,1,0:T(8,128)(2,1)S(1)}, bf16[17,32,256]{2,1,0:T(8,128)(2,1)S(1)}, u32[]{:S(2)}, u32[]{:S(2)}) %collective-permute-start.2) | collective-permute-done | bytes 278560 | tf_op jit(solution)/shard_map/cross_right_0/ppermute | solution.py:240
  19.6 0.8 %collective-permute-start.9 = (bf16[17,32,256]{2,1,0:T(8,128)(2,1)S(1)}, bf16[17,32,256]{2,1,0:T(8,128)(2,1)S(1)}, u32[]{:S(2)}, u32[]{:S(2)}) collective-permute-start(bf16[17,32,256]{2,1,0:T(8,128)(2,1)S(1)} %collective-permute-done.2.rest_3_), channel_id=1, source_target_pairs={{0,1},{1,0},{2,3},{3,2},{4,8},{5,9},{6,10},{7,11},{8,4},{9,5},{10,... | collective-permute-start | bytes 835592 | tf_op jit(solution)/shard_map/mid_own_10/ppermute | solution.py:240
  20.3 0.1 collective-permute-start.5
  20.5 0.9 %collective-permute-done.3.rest_4_ = bf16[32,32,256]{2,1,0:T(8,128)(2,1)S(1)} collective-permute-done((bf16[32,32,256]{2,1,0:T(8,128)(2,1)S(1)}, bf16[32,32,256]{2,1,0:T(8,128)(2,1)S(1)}, u32[]{:S(2)}, u32[]{:S(2)}) %collective-permute-start.3) | collective-permute-done | bytes 524320 | tf_op jit(solution)/shard_map/end_right_0/ppermute | solution.py:240
  21.3 1.1 %collective-permute-start.4 = (bf16[17,32,256]{2,1,0:T(8,128)(2,1)S(1)}, bf16[17,32,256]{2,1,0:T(8,128)(2,1)S(1)}, u32[]{:S(2)}, u32[]{:S(2)}) collective-permute-start(bf16[17,32,256]{2,1,0:T(8,128)(2,1)S(1)} %get-tuple-element.56), channel_id=1, source_target_pairs={{0,2},{1,3},{2,0},{3,1},{4,6},{5,7},{6,4},{7,5},{8,10},{9,11},{10,... | collective-permute-start | bytes 835592 | tf_op jit(solution)/shard_map/cross_left_0/ppermute | solution.py:240
  22.4 0.0 collective-permute-done.6.rest_4_.rest_2_
  22.4 1.8 %collective-permute-start.10 = (bf16[32,32,256]{2,1,0:T(8,128)(2,1)S(1)}, bf16[32,32,256]{2,1,0:T(8,128)(2,1)S(1)}, u32[]{:S(2)}, u32[]{:S(2)}) collective-permute-start(bf16[32,32,256]{2,1,0:T(8,128)(2,1)S(1)} %collective-permute-done.3.rest_4_), channel_id=1, source_target_pairs={{0,1},{1,0},{2,3},{3,2},{4,8},{5,9},{6,10},{7,11},{8,4},{9,5},{10,... | collective-permute-start | bytes 1572872 | tf_op jit(solution)/shard_map/mid_next_0/ppermute | solution.py:240
  24.2 0.8 %collective-permute-start.7 = (bf16[32,32,256]{2,1,0:T(8,128)(2,1)S(1)}, bf16[32,32,256]{2,1,0:T(8,128)(2,1)S(1)}, u32[]{:S(2)}, u32[]{:S(2)}) collective-permute-start(bf16[32,32,256]{2,1,0:T(8,128)(2,1)S(1)} %get-tuple-element.76.rest_0_), channel_id=1, source_target_pairs={{0,4},{1,5},{2,6},{3,7},{4,0},{5,1},{6,2},{7,3},{8,12},{9,13},{10,... | collective-permute-start | bytes 1572872 | tf_op jit(solution)/shard_map/end_left_0/ppermute | solution.py:240
  25.0 0.0 collective-permute-done.9.rest_5_
  25.0 3.2 %collective-permute-done.5.rest_5_ = bf16[17,32,256]{2,1,0:T(8,128)(2,1)S(1)} collective-permute-done((bf16[17,32,256]{2,1,0:T(8,128)(2,1)S(1)}, bf16[17,32,256]{2,1,0:T(8,128)(2,1)S(1)}, u32[]{:S(2)}, u32[]{:S(2)}) %collective-permute-start.5) | collective-permute-done | bytes 278560 | tf_op jit(solution)/shard_map/end_right_10/ppermute | solution.py:240
  28.2 1.2 %collective-permute-start.12 = (bf16[15,32,256]{2,1,0:T(8,128)(2,1)S(1)}, bf16[15,32,256]{2,1,0:T(8,128)(2,1)S(1)}, u32[]{:S(2)}, u32[]{:S(2)}) collective-permute-start(bf16[15,32,256]{2,1,0:T(8,128)(2,1)S(1)} %get-tuple-element.64), channel_id=1, source_target_pairs={{0,2},{1,3},{2,0},{3,1},{4,6},{5,7},{6,4},{7,5},{8,10},{9,11},{10,... | collective-permute-start | bytes 737288 | tf_op jit(solution)/shard_map/cross_right_1/ppermute | solution.py:240
  29.5 0.4 gate.1
  29.9 2.4 %collective-permute-start.11 = (bf16[17,32,256]{2,1,0:T(8,128)(2,1)S(1)}, bf16[17,32,256]{2,1,0:T(8,128)(2,1)S(1)}, u32[]{:S(2)}, u32[]{:S(2)}) collective-permute-start(bf16[17,32,256]{2,1,0:T(8,128)(2,1)S(1)} %collective-permute-done.5.rest_5_), channel_id=1, source_target_pairs={{0,1},{1,0},{2,3},{3,2},{4,8},{5,9},{6,10},{7,11},{8,4},{9,5},{10,... | collective-permute-start | bytes 835592 | tf_op jit(solution)/shard_map/mid_next_10/ppermute | solution.py:240
  32.3 0.2 collective-permute-start.8
  32.5 1.1 %collective-permute-done.12.rest_3_ = bf16[15,32,256]{2,1,0:T(8,128)(2,1)S(1)} collective-permute-done((bf16[15,32,256]{2,1,0:T(8,128)(2,1)S(1)}, bf16[15,32,256]{2,1,0:T(8,128)(2,1)S(1)}, u32[]{:S(2)}, u32[]{:S(2)}) %collective-permute-start.12) | collective-permute-done | bytes 245792 | tf_op jit(solution)/shard_map/cross_right_1/ppermute | solution.py:240
  33.6 1.3 %collective-permute-start.13 = (bf16[15,32,256]{2,1,0:T(8,128)(2,1)S(1)}, bf16[15,32,256]{2,1,0:T(8,128)(2,1)S(1)}, u32[]{:S(2)}, u32[]{:S(2)}) collective-permute-start(bf16[15,32,256]{2,1,0:T(8,128)(2,1)S(1)} %get-tuple-element.65), channel_id=1, source_target_pairs={{0,2},{1,3},{2,0},{3,1},{4,6},{5,7},{6,4},{7,5},{8,10},{9,11},{10,... | collective-permute-start | bytes 737288 | tf_op jit(solution)/shard_map/cross_left_1/ppermute | solution.py:240
  34.9 3.2 %collective-permute-start.19 = (bf16[15,32,256]{2,1,0:T(8,128)(2,1)S(1)}, bf16[15,32,256]{2,1,0:T(8,128)(2,1)S(1)}, u32[]{:S(2)}, u32[]{:S(2)}) collective-permute-start(bf16[15,32,256]{2,1,0:T(8,128)(2,1)S(1)} %collective-permute-done.12.rest_3_), channel_id=1, source_target_pairs={{0,1},{1,0},{2,3},{3,2},{4,8},{5,9},{6,10},{7,11},{8,4},{9,5},{10,... | collective-permute-start | bytes 737288 | tf_op jit(solution)/shard_map/mid_own_11/ppermute | solution.py:240
  38.1 1.3 %collective-permute-done.7.rest_2_.rest_0_ = bf16[32,32,256]{2,1,0:T(8,128)(2,1)S(1)} collective-permute-done((bf16[32,32,256]{2,1,0:T(8,128)(2,1)S(1)}, bf16[32,32,256]{2,1,0:T(8,128)(2,1)S(1)}, u32[]{:S(2)}, u32[]{:S(2)}) %collective-permute-start.7) | collective-permute-done | bytes 524320 | tf_op jit(solution)/shard_map/end_left_0/ppermute | solution.py:240
  39.5 3.7 %collective-permute-start.18 = (bf16[15,32,256]{2,1,0:T(8,128)(2,1)S(1)}, bf16[15,32,256]{2,1,0:T(8,128)(2,1)S(1)}, u32[]{:S(2)}, u32[]{:S(2)}) collective-permute-start(bf16[15,32,256]{2,1,0:T(8,128)(2,1)S(1)} %collective-permute-done.12.rest_3_), channel_id=1, source_target_pairs={{0,4},{1,5},{2,6},{3,7},{4,0},{5,1},{6,2},{7,3},{8,12},{9,13},{10,... | collective-permute-start | bytes 737288 | tf_op jit(solution)/shard_map/end_right_11/ppermute | solution.py:240
  43.2 2.2 %collective-permute-done.8.rest_3_ = bf16[17,32,256]{2,1,0:T(8,128)(2,1)S(1)} collective-permute-done((bf16[17,32,256]{2,1,0:T(8,128)(2,1)S(1)}, bf16[17,32,256]{2,1,0:T(8,128)(2,1)S(1)}, u32[]{:S(2)}, u32[]{:S(2)}) %collective-permute-start.8) | collective-permute-done | bytes 278560 | tf_op jit(solution)/shard_map/end_left_10/ppermute | solution.py:240
  45.4 0.0 collective-permute-done.13.rest_8_.rest_1_
  45.4 0.6 away.2
  46.0 1.4 %collective-permute-start.14 = (bf16[17,32,256]{2,1,0:T(8,128)(2,1)S(1)}, bf16[17,32,256]{2,1,0:T(8,128)(2,1)S(1)}, u32[]{:S(2)}, u32[]{:S(2)}) collective-permute-start(bf16[17,32,256]{2,1,0:T(8,128)(2,1)S(1)} %get-tuple-element.67), channel_id=1, source_target_pairs={{0,4},{1,5},{2,6},{3,7},{4,0},{5,1},{6,2},{7,3},{8,12},{9,13},{10,... | collective-permute-start | bytes 835592 | tf_op jit(solution)/shard_map/left_11_and_products_back_0/ppermute | solution.py:240
  47.4 0.0 collective-permute-done.19.rest_3_
  47.4 2.1 %collective-permute-done.18.rest_5_ = bf16[15,32,256]{2,1,0:T(8,128)(2,1)S(1)} collective-permute-done((bf16[15,32,256]{2,1,0:T(8,128)(2,1)S(1)}, bf16[15,32,256]{2,1,0:T(8,128)(2,1)S(1)}, u32[]{:S(2)}, u32[]{:S(2)}) %collective-permute-start.18) | collective-permute-done | bytes 245792 | tf_op jit(solution)/shard_map/end_right_11/ppermute | solution.py:240
  49.5 4.4 %collective-permute-start.20 = (bf16[15,32,256]{2,1,0:T(8,128)(2,1)S(1)}, bf16[15,32,256]{2,1,0:T(8,128)(2,1)S(1)}, u32[]{:S(2)}, u32[]{:S(2)}) collective-permute-start(bf16[15,32,256]{2,1,0:T(8,128)(2,1)S(1)} %collective-permute-done.18.rest_5_), channel_id=1, source_target_pairs={{0,1},{1,0},{2,3},{3,2},{4,8},{5,9},{6,10},{7,11},{8,4},{9,5},{10,... | collective-permute-start | bytes 737288 | tf_op jit(solution)/shard_map/mid_next_11/ppermute | solution.py:240
  53.9 0.6 near.2
  54.5 0.6 near.3
  55.0 0.4 collective-permute-done.14.end.rest_1_
  55.5 0.1 hand_out.2
  55.6 0.0 collective-permute-done.20.rest_5_
  55.6 0.6 away_for_ends.1
  56.1 0.0 copy-start.6
  56.1 1.9 %collective-permute-start.21 = (bf16[15,64,128]{2,1,0:T(8,128)(2,1)S(1)}, bf16[15,64,128]{2,1,0:T(8,128)(2,1)S(1)}, u32[]{:S(2)}, u32[]{:S(2)}) collective-permute-start(bf16[15,64,128]{2,1,0:T(8,128)(2,1)S(1)} %away_for_ends.1), channel_id=1, source_target_pairs={{0,4},{1,5},{2,6},{3,7},{4,0},{5,1},{6,2},{7,3},{8,12},{9,13},{10,... | collective-permute-start | bytes 737288 | tf_op jit(solution)/shard_map/products_back_1/ppermute | solution.py:240
  58.0 4.4 %collective-permute-start.15 = (bf16[17,32,128]{2,1,0:T(8,128)(2,1)S(1)}, bf16[17,32,128]{2,1,0:T(8,128)(2,1)S(1)}, u32[]{:S(2)}, u32[]{:S(2)}) collective-permute-start(bf16[17,32,128]{2,1,0:T(8,128)(2,1)S(1)} %get-tuple-element.69), channel_id=1, source_target_pairs={{0,1},{1,0},{2,3},{3,2},{4,5},{5,4},{6,7},{7,6},{8,9},{9,8},{10,11... | collective-permute-start | bytes 417800 | tf_op jit(solution)/shard_map/return_01/ppermute | solution.py:240
  62.4 0.1 collective-permute-start.16
  62.6 1.5 %collective-permute-start.17 = (bf16[17,32,128]{2,1,0:T(8,128)(2,1)S(1)}, bf16[17,32,128]{2,1,0:T(8,128)(2,1)S(1)}, u32[]{:S(2)}, u32[]{:S(2)}) collective-permute-start(bf16[17,32,128]{2,1,0:T(8,128)(2,1)S(1)} %get-tuple-element.71), channel_id=1, source_target_pairs={{0,3},{1,2},{2,1},{3,0},{4,7},{5,6},{6,5},{7,4},{8,11},{9,10},{10,... | collective-permute-start | bytes 417800 | tf_op jit(solution)/shard_map/return_03/ppermute | solution.py:240
  64.1 0.6 away.3.far
  64.6 0.0 collective-permute-done.21.end
  64.6 0.1 hand_out.3
  64.7 2.0 %collective-permute-start.22 = (bf16[15,32,128]{2,1,0:T(8,128)(2,1)S(1)}, bf16[15,32,128]{2,1,0:T(8,128)(2,1)S(1)}, u32[]{:S(2)}, u32[]{:S(2)}) collective-permute-start(bf16[15,32,128]{2,1,0:T(8,128)(2,1)S(1)} %get-tuple-element.78), channel_id=1, source_target_pairs={{0,1},{1,0},{2,3},{3,2},{4,5},{5,4},{6,7},{7,6},{8,9},{9,8},{10,11... | collective-permute-start | bytes 368648 | tf_op jit(solution)/shard_map/return_11/ppermute | solution.py:240
  66.7 0.2 collective-permute-start.23
  67.0 0.0 collective-permute-done.15.rest_1_
  67.0 1.5 %collective-permute-start.24 = (bf16[15,32,128]{2,1,0:T(8,128)(2,1)S(1)}, bf16[15,32,128]{2,1,0:T(8,128)(2,1)S(1)}, u32[]{:S(2)}, u32[]{:S(2)}) collective-permute-start(bf16[15,32,128]{2,1,0:T(8,128)(2,1)S(1)} %get-tuple-element.80), channel_id=1, source_target_pairs={{0,3},{1,2},{2,1},{3,0},{4,7},{5,6},{6,5},{7,4},{8,11},{9,10},{10,... | collective-permute-start | bytes 368648 | tf_op jit(solution)/shard_map/return_13/ppermute | solution.py:240
  68.5 2.7 %collective-permute-done.17.rest_3_ = bf16[17,32,128]{2,1,0:T(8,128)(2,1)S(1)} collective-permute-done((bf16[17,32,128]{2,1,0:T(8,128)(2,1)S(1)}, bf16[17,32,128]{2,1,0:T(8,128)(2,1)S(1)}, u32[]{:S(2)}, u32[]{:S(2)}) %collective-permute-start.17) | collective-permute-done | bytes 139296 | tf_op jit(solution)/shard_map/return_03/ppermute | solution.py:240
  71.2 0.0 collective-permute-done.22.rest_5_
  71.2 2.2 %collective-permute-done.23.rest_6_ = bf16[15,32,128]{2,1,0:T(8,128)(2,1)S(1)} collective-permute-done((bf16[15,32,128]{2,1,0:T(8,128)(2,1)S(1)}, bf16[15,32,128]{2,1,0:T(8,128)(2,1)S(1)}, u32[]{:S(2)}, u32[]{:S(2)}) %collective-permute-start.23) | collective-permute-done | bytes 122912 | tf_op jit(solution)/shard_map/return_12/ppermute | solution.py:240
  73.4 2.7 %collective-permute-done.24.rest_7_ = bf16[15,32,128]{2,1,0:T(8,128)(2,1)S(1)} collective-permute-done((bf16[15,32,128]{2,1,0:T(8,128)(2,1)S(1)}, bf16[15,32,128]{2,1,0:T(8,128)(2,1)S(1)}, u32[]{:S(2)}, u32[]{:S(2)}) %collective-permute-start.24) | collective-permute-done | bytes 122912 | tf_op jit(solution)/shard_map/return_13/ppermute | solution.py:240
  76.1 2.0 %update.1 = bf16[32,128,128]{2,1,0:T(8,128)(2,1)} custom-call(f32[1,128]{1,0:T(1,128)S(1)} %bitcast.3, bf16[128,128]{1,0:T(8,128)(2,1)S(1)} %copy-done.3, f32[32,128,128]{2,1,0:T(8,128)S(1)} %gate.1, bf16[17,32,128]{2,1,0:T(8,128)(2,1)S(1)} %get-tuple-element.68.rest_0_, bf16[17,32,128]{2,1,0:T(8,128)(2,1)S(1)} %collective-permute-done.15.rest_1_, ...), custom_call_target="tpu_custom_call" | custom-call | tf_op jit(solution)/shard_map/update/pallas_call | solution.py:212
  (13 shorter events, 0.0 us)
Async XLA Ops:
  0.0 5.5 %collective-permute-start = (bf16[32,128,128]{2,1,0:T(8,128)(2,1)}, bf16[32,128,128]{2,1,0:T(8,128)(2,1)S(1)}, u32[]{:S(2)}, u32[]{:S(2)}) collective-permute-start(bf16[32,128,128]{2,1,0:T(8,128)(2,1)} %pair.1), channel_id=1, source_target_pairs={{0,1},{1,0},{2,3},{3,2},{4,5},{5,4},{6,7},{7,6},{8,9},{9,8},{10,11... | collective-permute-start | bytes 3145736 | tf_op jit(solution)/shard_map/pair/ppermute | solution.py:240
  0.1 5.5 %collective-permute-start.1 = (s32[32,128]{1,0:T(8,128)}, s32[32,128]{1,0:T(8,128)S(1)}, u32[]{:S(2)}, u32[]{:S(2)}) collective-permute-start(s32[32,128]{1,0:T(8,128)} %mask.1), channel_id=1, source_target_pairs={{0,1},{1,0},{2,3},{3,2},{4,5},{5,4},{6,7},{7,6},{8,9},{9,8},{10,11... | collective-permute-start | bytes 49160 | tf_op jit(solution)/shard_map/mask/ppermute | solution.py:240
  0.5 1.2 %copy-start = (bf16[32,128,128]{2,1,0:T(8,128)(2,1)S(1)}, bf16[32,128,128]{2,1,0:T(8,128)(2,1)}, u32[]{:S(2)}) copy-start(bf16[32,128,128]{2,1,0:T(8,128)(2,1)} %pair.1) | copy-start | bytes 3145732
  1.7 0.9 %copy-start.1 = (bf16[128,512]{1,0:T(8,128)(2,1)S(1)}, bf16[128,512]{1,0:T(8,128)(2,1)}, u32[]{:S(2)}) copy-start(bf16[128,512]{1,0:T(8,128)(2,1)} %weight.3) | copy-start | bytes 393220
  2.6 0.7 copy-start.4
  3.4 0.7 copy-start.5
  7.1 14.2 %collective-permute-start.3 = (bf16[32,32,256]{2,1,0:T(8,128)(2,1)S(1)}, bf16[32,32,256]{2,1,0:T(8,128)(2,1)S(1)}, u32[]{:S(2)}, u32[]{:S(2)}) collective-permute-start(bf16[32,32,256]{2,1,0:T(8,128)(2,1)S(1)} %get-tuple-element.55.rest_2_), channel_id=1, source_target_pairs={{0,4},{1,5},{2,6},{3,7},{4,0},{5,1},{6,2},{7,3},{8,12},{9,13},{10,... | collective-permute-start | bytes 1572872 | tf_op jit(solution)/shard_map/end_right_0/ppermute | solution.py:240
  9.5 12.9 %collective-permute-start.6 = (bf16[32,32,256]{2,1,0:T(8,128)(2,1)S(1)}, bf16[32,32,256]{2,1,0:T(8,128)(2,1)S(1)}, u32[]{:S(2)}, u32[]{:S(2)}) collective-permute-start(bf16[32,32,256]{2,1,0:T(8,128)(2,1)S(1)} %get-tuple-element.55.rest_2_), channel_id=1, source_target_pairs={{0,1},{1,0},{2,3},{3,2},{4,8},{5,9},{6,10},{7,11},{8,4},{9,5},{10,... | collective-permute-start | bytes 1572872 | tf_op jit(solution)/shard_map/mid_own_0/ppermute | solution.py:240
  10.3 19.2 %copy-start.2 = (bf16[128,128]{1,0:T(8,128)(2,1)S(1)}, bf16[128,128]{1,0:T(8,128)(2,1)}, u32[]{:S(2)}) copy-start(bf16[128,128]{1,0:T(8,128)(2,1)} %weight.4) | copy-start | bytes 98308
  11.2 8.4 %collective-permute-start.2 = (bf16[17,32,256]{2,1,0:T(8,128)(2,1)S(1)}, bf16[17,32,256]{2,1,0:T(8,128)(2,1)S(1)}, u32[]{:S(2)}, u32[]{:S(2)}) collective-permute-start(bf16[17,32,256]{2,1,0:T(8,128)(2,1)S(1)} %get-tuple-element.54), channel_id=1, source_target_pairs={{0,2},{1,3},{2,0},{3,1},{4,6},{5,7},{6,4},{7,5},{8,10},{9,11},{10,... | collective-permute-start | bytes 835592 | tf_op jit(solution)/shard_map/cross_right_0/ppermute | solution.py:240
  19.6 5.5 %collective-permute-start.9 = (bf16[17,32,256]{2,1,0:T(8,128)(2,1)S(1)}, bf16[17,32,256]{2,1,0:T(8,128)(2,1)S(1)}, u32[]{:S(2)}, u32[]{:S(2)}) collective-permute-start(bf16[17,32,256]{2,1,0:T(8,128)(2,1)S(1)} %collective-permute-done.2.rest_3_), channel_id=1, source_target_pairs={{0,1},{1,0},{2,3},{3,2},{4,8},{5,9},{6,10},{7,11},{8,4},{9,5},{10,... | collective-permute-start | bytes 835592 | tf_op jit(solution)/shard_map/mid_own_10/ppermute | solution.py:240
  20.3 7.9 %collective-permute-start.5 = (bf16[17,32,256]{2,1,0:T(8,128)(2,1)S(1)}, bf16[17,32,256]{2,1,0:T(8,128)(2,1)S(1)}, u32[]{:S(2)}, u32[]{:S(2)}) collective-permute-start(bf16[17,32,256]{2,1,0:T(8,128)(2,1)S(1)} %collective-permute-done.2.rest_3_), channel_id=1, source_target_pairs={{0,4},{1,5},{2,6},{3,7},{4,0},{5,1},{6,2},{7,3},{8,12},{9,13},{10,... | collective-permute-start | bytes 835592 | tf_op jit(solution)/shard_map/end_right_10/ppermute | solution.py:240
  21.3 6.9 %collective-permute-start.4 = (bf16[17,32,256]{2,1,0:T(8,128)(2,1)S(1)}, bf16[17,32,256]{2,1,0:T(8,128)(2,1)S(1)}, u32[]{:S(2)}, u32[]{:S(2)}) collective-permute-start(bf16[17,32,256]{2,1,0:T(8,128)(2,1)S(1)} %get-tuple-element.56), channel_id=1, source_target_pairs={{0,2},{1,3},{2,0},{3,1},{4,6},{5,7},{6,4},{7,5},{8,10},{9,11},{10,... | collective-permute-start | bytes 835592 | tf_op jit(solution)/shard_map/cross_left_0/ppermute | solution.py:240
  22.4 11.2 %collective-permute-start.10 = (bf16[32,32,256]{2,1,0:T(8,128)(2,1)S(1)}, bf16[32,32,256]{2,1,0:T(8,128)(2,1)S(1)}, u32[]{:S(2)}, u32[]{:S(2)}) collective-permute-start(bf16[32,32,256]{2,1,0:T(8,128)(2,1)S(1)} %collective-permute-done.3.rest_4_), channel_id=1, source_target_pairs={{0,1},{1,0},{2,3},{3,2},{4,8},{5,9},{6,10},{7,11},{8,4},{9,5},{10,... | collective-permute-start | bytes 1572872 | tf_op jit(solution)/shard_map/mid_next_0/ppermute | solution.py:240
  24.2 15.2 %collective-permute-start.7 = (bf16[32,32,256]{2,1,0:T(8,128)(2,1)S(1)}, bf16[32,32,256]{2,1,0:T(8,128)(2,1)S(1)}, u32[]{:S(2)}, u32[]{:S(2)}) collective-permute-start(bf16[32,32,256]{2,1,0:T(8,128)(2,1)S(1)} %get-tuple-element.76.rest_0_), channel_id=1, source_target_pairs={{0,4},{1,5},{2,6},{3,7},{4,0},{5,1},{6,2},{7,3},{8,12},{9,13},{10,... | collective-permute-start | bytes 1572872 | tf_op jit(solution)/shard_map/end_left_0/ppermute | solution.py:240
  28.2 5.3 %collective-permute-start.12 = (bf16[15,32,256]{2,1,0:T(8,128)(2,1)S(1)}, bf16[15,32,256]{2,1,0:T(8,128)(2,1)S(1)}, u32[]{:S(2)}, u32[]{:S(2)}) collective-permute-start(bf16[15,32,256]{2,1,0:T(8,128)(2,1)S(1)} %get-tuple-element.64), channel_id=1, source_target_pairs={{0,2},{1,3},{2,0},{3,1},{4,6},{5,7},{6,4},{7,5},{8,10},{9,11},{10,... | collective-permute-start | bytes 737288 | tf_op jit(solution)/shard_map/cross_right_1/ppermute | solution.py:240
  29.9 13.3 %collective-permute-start.11 = (bf16[17,32,256]{2,1,0:T(8,128)(2,1)S(1)}, bf16[17,32,256]{2,1,0:T(8,128)(2,1)S(1)}, u32[]{:S(2)}, u32[]{:S(2)}) collective-permute-start(bf16[17,32,256]{2,1,0:T(8,128)(2,1)S(1)} %collective-permute-done.5.rest_5_), channel_id=1, source_target_pairs={{0,1},{1,0},{2,3},{3,2},{4,8},{5,9},{6,10},{7,11},{8,4},{9,5},{10,... | collective-permute-start | bytes 835592 | tf_op jit(solution)/shard_map/mid_next_10/ppermute | solution.py:240
  32.3 13.2 %collective-permute-start.8 = (bf16[17,32,256]{2,1,0:T(8,128)(2,1)S(1)}, bf16[17,32,256]{2,1,0:T(8,128)(2,1)S(1)}, u32[]{:S(2)}, u32[]{:S(2)}) collective-permute-start(bf16[17,32,256]{2,1,0:T(8,128)(2,1)S(1)} %collective-permute-done.4.rest_1_), channel_id=1, source_target_pairs={{0,4},{1,5},{2,6},{3,7},{4,0},{5,1},{6,2},{7,3},{8,12},{9,13},{10,... | collective-permute-start | bytes 835592 | tf_op jit(solution)/shard_map/end_left_10/ppermute | solution.py:240
  33.6 11.9 %collective-permute-start.13 = (bf16[15,32,256]{2,1,0:T(8,128)(2,1)S(1)}, bf16[15,32,256]{2,1,0:T(8,128)(2,1)S(1)}, u32[]{:S(2)}, u32[]{:S(2)}) collective-permute-start(bf16[15,32,256]{2,1,0:T(8,128)(2,1)S(1)} %get-tuple-element.65), channel_id=1, source_target_pairs={{0,2},{1,3},{2,0},{3,1},{4,6},{5,7},{6,4},{7,5},{8,10},{9,11},{10,... | collective-permute-start | bytes 737288 | tf_op jit(solution)/shard_map/cross_left_1/ppermute | solution.py:240
  34.9 12.5 %collective-permute-start.19 = (bf16[15,32,256]{2,1,0:T(8,128)(2,1)S(1)}, bf16[15,32,256]{2,1,0:T(8,128)(2,1)S(1)}, u32[]{:S(2)}, u32[]{:S(2)}) collective-permute-start(bf16[15,32,256]{2,1,0:T(8,128)(2,1)S(1)} %collective-permute-done.12.rest_3_), channel_id=1, source_target_pairs={{0,1},{1,0},{2,3},{3,2},{4,8},{5,9},{6,10},{7,11},{8,4},{9,5},{10,... | collective-permute-start | bytes 737288 | tf_op jit(solution)/shard_map/mid_own_11/ppermute | solution.py:240
  39.5 10.0 %collective-permute-start.18 = (bf16[15,32,256]{2,1,0:T(8,128)(2,1)S(1)}, bf16[15,32,256]{2,1,0:T(8,128)(2,1)S(1)}, u32[]{:S(2)}, u32[]{:S(2)}) collective-permute-start(bf16[15,32,256]{2,1,0:T(8,128)(2,1)S(1)} %collective-permute-done.12.rest_3_), channel_id=1, source_target_pairs={{0,4},{1,5},{2,6},{3,7},{4,0},{5,1},{6,2},{7,3},{8,12},{9,13},{10,... | collective-permute-start | bytes 737288 | tf_op jit(solution)/shard_map/end_right_11/ppermute | solution.py:240
  46.0 9.5 %collective-permute-start.14 = (bf16[17,32,256]{2,1,0:T(8,128)(2,1)S(1)}, bf16[17,32,256]{2,1,0:T(8,128)(2,1)S(1)}, u32[]{:S(2)}, u32[]{:S(2)}) collective-permute-start(bf16[17,32,256]{2,1,0:T(8,128)(2,1)S(1)} %get-tuple-element.67), channel_id=1, source_target_pairs={{0,4},{1,5},{2,6},{3,7},{4,0},{5,1},{6,2},{7,3},{8,12},{9,13},{10,... | collective-permute-start | bytes 835592 | tf_op jit(solution)/shard_map/left_11_and_products_back_0/ppermute | solution.py:240
  49.5 6.1 %collective-permute-start.20 = (bf16[15,32,256]{2,1,0:T(8,128)(2,1)S(1)}, bf16[15,32,256]{2,1,0:T(8,128)(2,1)S(1)}, u32[]{:S(2)}, u32[]{:S(2)}) collective-permute-start(bf16[15,32,256]{2,1,0:T(8,128)(2,1)S(1)} %collective-permute-done.18.rest_5_), channel_id=1, source_target_pairs={{0,1},{1,0},{2,3},{3,2},{4,8},{5,9},{6,10},{7,11},{8,4},{9,5},{10,... | collective-permute-start | bytes 737288 | tf_op jit(solution)/shard_map/mid_next_11/ppermute | solution.py:240
  56.1 20.0 %copy-start.3 = (bf16[128,128]{1,0:T(8,128)(2,1)S(1)}, bf16[128,128]{1,0:T(8,128)(2,1)}, u32[]{:S(2)}) copy-start(bf16[128,128]{1,0:T(8,128)(2,1)} %weight.5) | copy-start | bytes 98308
  56.1 20.0 %copy-start.6 = (f32[128]{0:T(128)S(1)}, f32[128]{0:T(128)}, u32[]{:S(2)}) copy-start(f32[128]{0:T(128)} %param.12) | copy-start | bytes 1540
  56.1 8.5 %collective-permute-start.21 = (bf16[15,64,128]{2,1,0:T(8,128)(2,1)S(1)}, bf16[15,64,128]{2,1,0:T(8,128)(2,1)S(1)}, u32[]{:S(2)}, u32[]{:S(2)}) collective-permute-start(bf16[15,64,128]{2,1,0:T(8,128)(2,1)S(1)} %away_for_ends.1), channel_id=1, source_target_pairs={{0,4},{1,5},{2,6},{3,7},{4,0},{5,1},{6,2},{7,3},{8,12},{9,13},{10,... | collective-permute-start | bytes 737288 | tf_op jit(solution)/shard_map/products_back_1/ppermute | solution.py:240
  58.0 9.0 %collective-permute-start.15 = (bf16[17,32,128]{2,1,0:T(8,128)(2,1)S(1)}, bf16[17,32,128]{2,1,0:T(8,128)(2,1)S(1)}, u32[]{:S(2)}, u32[]{:S(2)}) collective-permute-start(bf16[17,32,128]{2,1,0:T(8,128)(2,1)S(1)} %get-tuple-element.69), channel_id=1, source_target_pairs={{0,1},{1,0},{2,3},{3,2},{4,5},{5,4},{6,7},{7,6},{8,9},{9,8},{10,11... | collective-permute-start | bytes 417800 | tf_op jit(solution)/shard_map/return_01/ppermute | solution.py:240
  62.4 6.0 %collective-permute-start.16 = (bf16[17,32,128]{2,1,0:T(8,128)(2,1)S(1)}, bf16[17,32,128]{2,1,0:T(8,128)(2,1)S(1)}, u32[]{:S(2)}, u32[]{:S(2)}) collective-permute-start(bf16[17,32,128]{2,1,0:T(8,128)(2,1)S(1)} %get-tuple-element.70), channel_id=1, source_target_pairs={{0,2},{1,3},{2,0},{3,1},{4,6},{5,7},{6,4},{7,5},{8,10},{9,11},{10,... | collective-permute-start | bytes 417800 | tf_op jit(solution)/shard_map/return_02/ppermute | solution.py:240
  62.6 8.6 %collective-permute-start.17 = (bf16[17,32,128]{2,1,0:T(8,128)(2,1)S(1)}, bf16[17,32,128]{2,1,0:T(8,128)(2,1)S(1)}, u32[]{:S(2)}, u32[]{:S(2)}) collective-permute-start(bf16[17,32,128]{2,1,0:T(8,128)(2,1)S(1)} %get-tuple-element.71), channel_id=1, source_target_pairs={{0,3},{1,2},{2,1},{3,0},{4,7},{5,6},{6,5},{7,4},{8,11},{9,10},{10,... | collective-permute-start | bytes 417800 | tf_op jit(solution)/shard_map/return_03/ppermute | solution.py:240
  64.7 6.5 %collective-permute-start.22 = (bf16[15,32,128]{2,1,0:T(8,128)(2,1)S(1)}, bf16[15,32,128]{2,1,0:T(8,128)(2,1)S(1)}, u32[]{:S(2)}, u32[]{:S(2)}) collective-permute-start(bf16[15,32,128]{2,1,0:T(8,128)(2,1)S(1)} %get-tuple-element.78), channel_id=1, source_target_pairs={{0,1},{1,0},{2,3},{3,2},{4,5},{5,4},{6,7},{7,6},{8,9},{9,8},{10,11... | collective-permute-start | bytes 368648 | tf_op jit(solution)/shard_map/return_11/ppermute | solution.py:240
  66.7 6.6 %collective-permute-start.23 = (bf16[15,32,128]{2,1,0:T(8,128)(2,1)S(1)}, bf16[15,32,128]{2,1,0:T(8,128)(2,1)S(1)}, u32[]{:S(2)}, u32[]{:S(2)}) collective-permute-start(bf16[15,32,128]{2,1,0:T(8,128)(2,1)S(1)} %get-tuple-element.79), channel_id=1, source_target_pairs={{0,2},{1,3},{2,0},{3,1},{4,6},{5,7},{6,4},{7,5},{8,10},{9,11},{10,... | collective-permute-start | bytes 368648 | tf_op jit(solution)/shard_map/return_12/ppermute | solution.py:240
  67.0 9.1 %collective-permute-start.24 = (bf16[15,32,128]{2,1,0:T(8,128)(2,1)S(1)}, bf16[15,32,128]{2,1,0:T(8,128)(2,1)S(1)}, u32[]{:S(2)}, u32[]{:S(2)}) collective-permute-start(bf16[15,32,128]{2,1,0:T(8,128)(2,1)S(1)} %get-tuple-element.80), channel_id=1, source_target_pairs={{0,3},{1,2},{2,1},{3,0},{4,7},{5,6},{6,5},{7,4},{8,11},{9,10},{10,... | collective-permute-start | bytes 368648 | tf_op jit(solution)/shard_map/return_13/ppermute | solution.py:240
